TPU v7x, 32 devices: a whole 2x2x4 slice. The times are simulated.
32 devices in a mesh: ctx: 4 (over y, x), tp: 8 (over z, core).
Axes of the slice: x: 2, y: 2, z: 4, core: 2. Of those that a mesh axis runs over, the one named last changes fastest.
Arguments:
- query_gate: bfloat16 [2048, 8192], P('ctx', 'tp'), may hold values from -6 to 6
- key_gate: bfloat16 [2048, 8192], P('ctx', 'tp'), may hold values from -6 to 6
- value_input: bfloat16 [2048, 8192], P('ctx', 'tp'), may hold values from -6 to 6
- filter_taps: float32 [2048, 512], P('ctx', 'tp'), may hold values from -6 to 6
- out_weight: bfloat16 [8192, 8192], P('tp'), may hold values from -0.09375 to 0.09375
- out_grad: bfloat16 [2048, 8192], P('ctx', 'tp'), may hold values from -6 to 6
Outputs:
- projected: bfloat16 [2048, 8192], P('ctx', 'tp')
- grad_query: bfloat16 [2048, 8192], P('ctx', 'tp')
- grad_key: bfloat16 [2048, 8192], P('ctx', 'tp')
- grad_value: bfloat16 [2048, 8192], P('ctx', 'tp')
- grad_filter: float32 [2048, 512], P('ctx', 'tp')
All inputs are finite; a program needn't handle non-finite values.
Results may differ from a plain program's by a relative error of at most 0.027.
Values may be sent and summed in bfloat16 or wider, within the bound.
No kernel may reach another device: no remote copies, remote signals or barrier semaphores. Data moves between devices by JAX's collectives and lax.ppermute only.
A program may use at most 192 MiB of HBM per device.

v0:
```python
import math

import jax
import jax.numpy as jnp
from jax import lax
from jax.sharding import PartitionSpec as P

PRECISE = lax.Precision.HIGHEST


def passed_along(array, axis, by):
    size = lax.axis_size(axis)
    pairs = [(i, i + by) for i in range(size) if 0 <= i + by < size]
    return lax.ppermute(array, axis, pairs)


def basis_tables(length):
    fft_len = 2 * length
    row_ids = jnp.arange(fft_len, dtype=jnp.int32)
    freq_ids = jnp.where(row_ids <= length, row_ids, row_ids - length)
    phase_ids = freq_ids[:, None] * row_ids[None, :] % fft_len
    angles = phase_ids.astype(jnp.float32) * jnp.float32(2.0 * math.pi / fft_len)
    basis = jnp.where((row_ids > length)[:, None], -jnp.sin(angles), jnp.cos(angles))
    inv_weight = jnp.where(
        (row_ids == 0) | (row_ids == length), 1.0 / fft_len, 2.0 / fft_len
    ).astype(jnp.float32)
    pad_basis = basis[:, :length]
    tail_basis = basis[:, length:]
    back_basis = inv_weight[:, None] * tail_basis
    return (pad_basis, tail_basis, back_basis)


def split_basis(basis):
    upper = basis.astype(jnp.bfloat16)
    rest = basis - upper.astype(jnp.float32)
    middle = rest.astype(jnp.bfloat16)
    lower = (rest - middle.astype(jnp.float32)).astype(jnp.bfloat16)
    return (upper, middle, lower)


def split_apply(parts, form, data):
    total = jnp.einsum(form, parts[0], data, preferred_element_type=jnp.float32)
    total = total + jnp.einsum(form, parts[1], data, preferred_element_type=jnp.float32)
    return total + jnp.einsum(form, parts[2], data, preferred_element_type=jnp.float32)


def first_mask(spectrum):
    half_len = spectrum.shape[0] // 2
    return (jnp.arange(half_len) == 0).reshape((half_len,) + (1,) * (spectrum.ndim - 1))


def spec_product(left_spec, right_spec):
    half_len = left_spec.shape[0] // 2
    at_first = first_mask(left_spec)
    left_re = left_spec[:half_len]
    left_im = left_spec[half_len:]
    right_re = right_spec[:half_len]
    right_im = right_spec[half_len:]
    im_product = left_im * right_im
    real_part = left_re * right_re - jnp.where(at_first, 0.0, im_product)
    imag_part = jnp.where(at_first, im_product, left_re * right_im + left_im * right_re)
    return jnp.concatenate([real_part, imag_part], axis=0)


def conjugate(spectrum):
    half_len = spectrum.shape[0] // 2
    imag_half = spectrum[half_len:]
    return jnp.concatenate(
        [spectrum[:half_len], jnp.where(first_mask(spectrum), imag_half, -imag_half)], axis=0
    )


def local(query_gate, key_gate, value_input, filter_taps, out_weight, out_grad):
    length, channels = query_gate.shape
    groups = filter_taps.shape[1]
    per_group = channels // groups
    members = lax.axis_size("ctx")
    position = lax.axis_index("ctx")
    fft_len = 2 * length
    tap_scale = 1.0 / math.sqrt(length * members)
    pad_basis, tail_basis, back_basis = basis_tables(length)
    pad_parts = split_basis(pad_basis)
    back_parts = split_basis(back_basis)
    tap_rows = filter_taps * tap_scale
    product_in = (key_gate.astype(jnp.float32) * value_input.astype(jnp.float32)).astype(
        jnp.bfloat16
    )
    dgated = jnp.einsum(
        "tk,ck->tc",
        lax.all_gather(out_grad, "tp", axis=1, tiled=True),
        out_weight,
        preferred_element_type=jnp.float32,
    ).astype(jnp.bfloat16)
    conv_grad = (dgated.astype(jnp.float32) * query_gate.astype(jnp.float32)).astype(jnp.bfloat16)
    all_taps = (
        lax.all_gather(tap_rows.astype(jnp.bfloat16), "ctx", axis=0, tiled=True)
        .astype(tap_rows.dtype)
        .reshape(members, length, groups)
    )
    own_part = jnp.einsum("nl,dlg->dng", tail_basis, all_taps, precision=PRECISE)
    early_part = jnp.einsum("nl,dlg->dng", pad_basis, all_taps, precision=PRECISE)
    early_part = jnp.concatenate(
        [jnp.zeros((1, fft_len, groups), jnp.float32), early_part[:-1]], axis=0
    )
    spectra = own_part + early_part
    full_spectra = jnp.repeat(spectra, per_group, axis=2)
    spec_in = split_apply(pad_parts, "nl,lc->nc", product_in)
    spec_grad = split_apply(back_parts, "nl,lc->nc", conv_grad)

    def group_total(spectrum):
        return spectrum.reshape(fft_len, groups, per_group).sum(axis=2)

    def visit(totals, spectrum, item_pos):
        fwd_acc, bwd_acc, grad_acc = totals
        distance = jnp.minimum(jnp.abs(position - item_pos), members - 1)
        earlier = (item_pos < position).astype(jnp.float32)
        later_side = (item_pos > position).astype(jnp.float32)
        filter_spec = lax.dynamic_index_in_dim(full_spectra, distance, 0, keepdims=False)
        fwd_acc = fwd_acc + earlier * spec_product(filter_spec, spectrum)
        bwd_acc = bwd_acc + later_side * spec_product(conjugate(filter_spec), spectrum)
        grad_term = earlier * group_total(spec_product(conjugate(spectrum), spec_grad))
        grad_row = lax.dynamic_index_in_dim(grad_acc, distance, 0, keepdims=False)
        grad_acc = lax.dynamic_update_index_in_dim(grad_acc, grad_row + grad_term, distance, 0)
        return (fwd_acc, bwd_acc, grad_acc)

    def from_tokens(forward_part, backward_part, earlier):
        item_parts = (
            jnp.where(earlier, pad_parts[0], back_parts[0]),
            jnp.where(earlier, pad_parts[1], back_parts[1]),
            jnp.where(earlier, pad_parts[2], back_parts[2]),
        )
        item_data = jnp.where(earlier, forward_part, backward_part)
        return split_apply(item_parts, "nl,lc->nc", item_data)

    start_totals = (
        jnp.zeros((fft_len, channels), jnp.float32),
        jnp.zeros((fft_len, channels), jnp.float32),
        jnp.zeros((members, fft_len, groups), jnp.float32),
    )
    received = (
        lax.all_gather(product_in, "ctx", axis=0, tiled=True),
        lax.all_gather(conv_grad, "ctx", axis=0, tiled=True),
    )
    item_count = received[0].shape[0] // length

    def visit_item(item_no, inner):
        forward_part = lax.dynamic_slice_in_dim(received[0], item_no * length, length, 0)
        backward_part = lax.dynamic_slice_in_dim(received[1], item_no * length, length, 0)
        return visit(inner, from_tokens(forward_part, backward_part, item_no < position), item_no)

    totals = lax.fori_loop(0, item_count, visit_item, start_totals)
    fwd_acc, bwd_acc, grad_acc = totals
    own_filter = full_spectra[0]
    fwd_acc = fwd_acc + spec_product(own_filter, spec_in)
    bwd_acc = bwd_acc + spec_product(conjugate(own_filter), spec_grad)
    own_grad = group_total(spec_product(conjugate(spec_in), spec_grad))
    grad_acc = grad_acc.at[0].add(own_grad)
    convolved = jnp.einsum("nl,nc->lc", back_basis, fwd_acc, precision=PRECISE)
    input_grad = jnp.einsum("nl,nc->lc", pad_basis, bwd_acc, precision=PRECISE)
    offset_grad = lax.psum_scatter(
        grad_acc.astype(jnp.bfloat16), "ctx", scatter_dimension=0, tiled=True
    ).astype(jnp.float32)[0]
    own_rows = jnp.einsum("nl,ng->lg", tail_basis, offset_grad, precision=PRECISE)
    early_rows = jnp.einsum("nl,ng->lg", pad_basis, offset_grad, precision=PRECISE)
    later_rows = passed_along(early_rows.astype(jnp.bfloat16), "ctx", -1).astype(early_rows.dtype)
    grad_filter = (own_rows + later_rows) * tap_scale
    gated_out = (query_gate.astype(jnp.float32) * convolved).astype(jnp.bfloat16)
    partial_value = jnp.dot(gated_out, out_weight, preferred_element_type=jnp.float32)
    projected = lax.psum_scatter(
        partial_value.astype(jnp.bfloat16), "tp", scatter_dimension=1, tiled=True
    )
    grad_query = (dgated.astype(jnp.float32) * convolved).astype(jnp.bfloat16)
    grad_key = (input_grad * value_input.astype(jnp.float32)).astype(jnp.bfloat16)
    grad_value = (input_grad * key_gate.astype(jnp.float32)).astype(jnp.bfloat16)
    return (projected, grad_query, grad_key, grad_value, grad_filter)


def solution(mesh):
    return jax.shard_map(
        local,
        mesh=mesh,
        in_specs=(
            P("ctx", "tp"),
            P("ctx", "tp"),
            P("ctx", "tp"),
            P("ctx", "tp"),
            P("tp", None),
            P("ctx", "tp"),
        ),
        out_specs=(P("ctx", "tp"), P("ctx", "tp"), P("ctx", "tp"), P("ctx", "tp"), P("ctx", "tp")),
        check_vma=False,
    )
```

profile of v0, /device:TPU:0, one launch (start us, length us, event | category | flops | bytes accessed | tf_op | source)
XLA Modules:
  0.0 539.3 jit_solution(6860860051522683110)
XLA Ops:
  11.1 83.3 %all-gather.6.cloned.1.call-done = bf16[512,8192]{1,0:T(8,128)(2,1)} async-done(((bf16[512,1024]{1,0:T(8,128)(2,1)}), bf16[512,8192]{1,0:T(8,128)(2,1)}) %all-gather.6.cloned.1.call-update) | async-done | bytes 8388624 | tf_op jit(solution)/shard_map/all_gather | solution.py:90
  94.4 15.8 %fusion.30 = (bf16[512,1024]{1,0:T(8,128)(2,1)}, bf16[512,1024]{1,0:T(8,128)(2,1)}) fusion(bf16[512,1024]{1,0:T(8,128)(2,1)S(1)} %copy-done.27, bf16[512,8192]{1,0:T(8,128)(2,1)} %all-gather.6.cloned.1.call-done, bf16[1024,8192]{1,0:T(8,128)(2,1)} %param.14), kind=kOutput, calls=%fused_computation.71 | convolution fusion | flops 8592556032 | bytes 28311552 | tf_op jit(solution)/shard_map/tk,ck->tc/dot_general | solution.py:88
  110.3 9.9 %all_gather.12 = bf16[2048,64]{0,1:T(8,128)(2,1)S(1)} all-gather(bf16[512,64]{0,1:T(8,128)(2,1)S(1)} %multiply_convert_fusion), channel_id=1, replica_groups=mesh['ctx'=4,'tp'=8] {'ctx'}, dimensions={0}, use_global_device_ids=true | all-gather | bytes 327680 | tf_op jit(solution)/shard_map/all_gather | solution.py:96
  120.2 17.3 %cosine_select_fusion = f32[1024,1024]{1,0:T(8,128)S(1)} fusion(s32[1024]{0:T(1024)S(1)} %compare_select_fusion, pred[1024]{0:T(1024)(128)(4,1)S(1)} %iota_compare_fusion.3), kind=kLoop, calls=%fused_computation.55 | loop fusion | flops 16777216 | bytes 4199424 | tf_op jit(solution)/shard_map/jit(_where)/select_n | solution.py:23
  165.7 5.4 copy.39
  174.9 29.9 %all-gather.8.cloned.1.call-done = bf16[2048,1024]{1,0:T(8,128)(2,1)} async-done(((bf16[512,1024]{1,0:T(8,128)(2,1)}), bf16[2048,1024]{1,0:T(8,128)(2,1)}) %all-gather.8.cloned.1.call-update) | async-done | bytes 4194320 | tf_op jit(solution)/shard_map/all_gather | solution.py:142
  204.8 9.2 %broadcast_in_dim.188 = f32[4,1024,64,16]{1,3,2,0:T(8,128)} broadcast(f32[4,1024,64]{1,2,0:T(8,128)} %copy-done.20), dimensions={0,1,2} | broadcast | bytes 17825792 | tf_op jit(solution)/shard_map/broadcast_in_dim | solution.py:106
  215.1 194.7 %while.19 = (s32[]{:T(128)}, f32[1024,1024]{1,0:T(8,128)}, f32[1024,1024]{1,0:T(8,128)}, f32[4,1024,64]{1,2,0:T(8,128)}, s32[]{:T(128)}, /*index=5*/f32[4,1024,1...) while((s32[]{:T(128)}, f32[1024,1024]{1,0:T(8,128)}, ...), condition=%wide.region_2.3_spmd.clone, body=%wide.region_0.2_spmd.clone.sunk | while | flops 3249603072 | bytes 160433792 | solution.py:151
  232.9 9.1 %select_subtract_fusion.7 = (f32[512,1024]{1,0:T(8,128)S(1)}, f32[512,1024]{1,0:T(8,128)}, f32[512,1024]{1,0:T(8,128)}, f32[512,1024]{1,0:T(8,128)}, f32[512,1024]{1,0:T(8,128)}, /*index=5*/f32[512,1024]{1,0:T(8,128)}) fusion(f32[1024,1024]{1,0:T(8,128)} %get-tuple-element.584, f32[1024,1024]{1,0:T(8,128)} %add_add_fusion.4, ...), kind=kLoop, calls=%fused_computation.16.clone.1 | loop fusion | flops 13631488 | bytes 25166336 | tf_op jit(solution)/shard_map/while/body/eval_jaxpr/sub | solution.py:60
  242.0 6.7 %fusion.116 = (f32[1024,1024]{1,0:T(8,128)}, f32[1024,1024]{1,0:T(8,128)}) fusion(f32[512,1024]{1,0:T(8,128)} %get-tuple-element.518, f32[512,1024]{1,0:T(8,128)} %get-tuple-element.519, f32[1024,1024]{1,0:T(8,128)} %get-tuple-element.549, f32[]{:T(128)S(6)} %convert_element_type.283, pred[]{:T(512)S(6)} %compare.11, ...), kind=kLoop, calls=%fused_computation.1.clone.1 | loop fusion | flops 8388608 | bytes 25165832 | tf_op jit(solution)/shard_map/while/body/eval_jaxpr/add | solution.py:119
  251.3 5.3 copy.57
  279.3 9.1 %select_subtract_fusion.7 = (f32[512,1024]{1,0:T(8,128)S(1)}, f32[512,1024]{1,0:T(8,128)}, f32[512,1024]{1,0:T(8,128)}, f32[512,1024]{1,0:T(8,128)}, f32[512,1024]{1,0:T(8,128)}, /*index=5*/f32[512,1024]{1,0:T(8,128)}) fusion(f32[1024,1024]{1,0:T(8,128)} %get-tuple-element.584, f32[1024,1024]{1,0:T(8,128)} %add_add_fusion.4, ...), kind=kLoop, calls=%fused_computation.16.clone.1 | loop fusion | flops 13631488 | bytes 25166336 | tf_op jit(solution)/shard_map/while/body/eval_jaxpr/sub | solution.py:60
  288.4 9.8 %fusion.116 = (f32[1024,1024]{1,0:T(8,128)}, f32[1024,1024]{1,0:T(8,128)}) fusion(f32[512,1024]{1,0:T(8,128)} %get-tuple-element.518, f32[512,1024]{1,0:T(8,128)} %get-tuple-element.519, f32[1024,1024]{1,0:T(8,128)} %get-tuple-element.549, f32[]{:T(128)S(6)} %convert_element_type.283, pred[]{:T(512)S(6)} %compare.11, ...), kind=kLoop, calls=%fused_computation.1.clone.1 | loop fusion | flops 8388608 | bytes 25165832 | tf_op jit(solution)/shard_map/while/body/eval_jaxpr/add | solution.py:119
  300.7 5.3 copy.57
  328.6 9.1 %select_subtract_fusion.7 = (f32[512,1024]{1,0:T(8,128)S(1)}, f32[512,1024]{1,0:T(8,128)}, f32[512,1024]{1,0:T(8,128)}, f32[512,1024]{1,0:T(8,128)}, f32[512,1024]{1,0:T(8,128)}, /*index=5*/f32[512,1024]{1,0:T(8,128)}) fusion(f32[1024,1024]{1,0:T(8,128)} %get-tuple-element.584, f32[1024,1024]{1,0:T(8,128)} %add_add_fusion.4, ...), kind=kLoop, calls=%fused_computation.16.clone.1 | loop fusion | flops 13631488 | bytes 25166336 | tf_op jit(solution)/shard_map/while/body/eval_jaxpr/sub | solution.py:60
  337.7 9.8 %fusion.116 = (f32[1024,1024]{1,0:T(8,128)}, f32[1024,1024]{1,0:T(8,128)}) fusion(f32[512,1024]{1,0:T(8,128)} %get-tuple-element.518, f32[512,1024]{1,0:T(8,128)} %get-tuple-element.519, f32[1024,1024]{1,0:T(8,128)} %get-tuple-element.549, f32[]{:T(128)S(6)} %convert_element_type.283, pred[]{:T(512)S(6)} %compare.11, ...), kind=kLoop, calls=%fused_computation.1.clone.1 | loop fusion | flops 8388608 | bytes 25165832 | tf_op jit(solution)/shard_map/while/body/eval_jaxpr/add | solution.py:119
  350.1 5.3 copy.57
  378.0 9.1 %select_subtract_fusion.7 = (f32[512,1024]{1,0:T(8,128)S(1)}, f32[512,1024]{1,0:T(8,128)}, f32[512,1024]{1,0:T(8,128)}, f32[512,1024]{1,0:T(8,128)}, f32[512,1024]{1,0:T(8,128)}, /*index=5*/f32[512,1024]{1,0:T(8,128)}) fusion(f32[1024,1024]{1,0:T(8,128)} %get-tuple-element.584, f32[1024,1024]{1,0:T(8,128)} %add_add_fusion.4, ...), kind=kLoop, calls=%fused_computation.16.clone.1 | loop fusion | flops 13631488 | bytes 25166336 | tf_op jit(solution)/shard_map/while/body/eval_jaxpr/sub | solution.py:60
  387.1 9.8 %fusion.116 = (f32[1024,1024]{1,0:T(8,128)}, f32[1024,1024]{1,0:T(8,128)}) fusion(f32[512,1024]{1,0:T(8,128)} %get-tuple-element.518, f32[512,1024]{1,0:T(8,128)} %get-tuple-element.519, f32[1024,1024]{1,0:T(8,128)} %get-tuple-element.549, f32[]{:T(128)S(6)} %convert_element_type.283, pred[]{:T(512)S(6)} %compare.11, ...), kind=kLoop, calls=%fused_computation.1.clone.1 | loop fusion | flops 8388608 | bytes 25165832 | tf_op jit(solution)/shard_map/while/body/eval_jaxpr/add | solution.py:119
  399.4 5.3 copy.57
  413.8 11.8 %fusion.31 = (bf16[512,1024]{1,0:T(8,128)(2,1)}, f32[512,1024]{1,0:T(8,128)S(1)}) fusion(bf16[512,1024]{1,0:T(8,128)(2,1)} %get-tuple-element.412, f32[1024,1024]{1,0:T(8,128)} %get-tuple-element.263, f32[512,1024]{1,0:T(8,128)S(1)} %copy-done.18, f32[512,1024]{1,0:T(8,128)} %get-tuple-element.401, f32[1024,1024]{1,0:T(8,128)} %copy-done.2, ...), kind=kOutput, calls=%fused_computation.72 | convolution fusion | flops 6446645248 | bytes 14684160 | tf_op jit(solution)/shard_map/nl,nc->lc/dot_general | solution.py:158
  425.6 16.9 %convolution_convert_fusion = bf16[512,8192]{1,0:T(8,128)(2,1)} fusion(bf16[1024,8192]{1,0:T(8,128)(2,1)} %param.14, f32[512,1024]{1,0:T(8,128)S(1)} %get-tuple-element.414, bf16[512,1024]{1,0:T(8,128)(2,1)S(1)} %copy-done.28), kind=kOutput, calls=%fused_computation.36 | convolution fusion | flops 8595701760 | bytes 28311552 | tf_op jit(solution)/shard_map/dot_general | solution.py:168
  446.6 13.0 %fusion.27 = (bf16[512,1024]{1,0:T(8,128)(2,1)}, bf16[512,1024]{1,0:T(8,128)(2,1)}) fusion(bf16[512,1024]{1,0:T(8,128)(2,1)} %param.11, bf16[512,1024]{1,0:T(8,128)(2,1)S(1)} %copy-done.19, f32[1024,1024]{1,0:T(8,128)} %get-tuple-element.264, f32[512,1024]{1,0:T(8,128)S(1)} %copy-done.15, f32[512,1024]{1,0:T(8,128)} %get-tuple-element.403, ...), kind=kOutput, calls=%fused_computation.68 | convolution fusion | flops 6447693824 | bytes 14680064 | tf_op jit(solution)/shard_map/nl,nc->lc/dot_general | solution.py:159
  461.2 71.1 %reduce-scatter.5.cloned.1.call-done = bf16[512,1024]{1,0:T(8,128)(2,1)} async-done(((bf16[512,8192]{1,0:T(8,128)(2,1)}), bf16[512,1024]{1,0:T(8,128)(2,1)}) %reduce-scatter.5.cloned.1.call-update) | async-done | bytes 1048592 | tf_op jit(solution)/shard_map/reduce_scatter | solution.py:169
  (195 shorter events, 146.4 us)
Async XLA Ops:
  7.2 87.2 %all-gather.6.cloned.1.call-start = ((), (), s32[]{:S(2)}) async-start(), calls=%async_computation.3 | async-start | bytes 9437184 | tf_op jit(solution)/shard_map/all_gather | solution.py:90
  7.9 86.5 %copy-start.27 = (bf16[512,1024]{1,0:T(8,128)(2,1)S(1)}, bf16[512,1024]{1,0:T(8,128)(2,1)}, u32[]{:S(2)}) copy-start(bf16[512,1024]{1,0:T(8,128)(2,1)} %param.10) | copy-start | bytes 3145732
  7.9 167.0 %all-gather.4.cloned.1.call-start = ((), (), s32[]{:S(2)}) async-start(), calls=%async_computation.2 | async-start | bytes 5242880 | tf_op jit(solution)/shard_map/all_gather | solution.py:141
  11.0 193.8 %all-gather.8.cloned.1.call-start = ((), (), s32[]{:S(2)}) async-start(), calls=%async_computation.4 | async-start | bytes 5242880 | tf_op jit(solution)/shard_map/all_gather | solution.py:142
  110.2 332.4 %reduce-scatter.7.cloned.1.call-start = ((), (), s32[]{:S(2)}) async-start(), calls=%async_computation.6 | async-start | bytes 655360
  150.0 6.4 %copy-start.10 = (bf16[1024,512]{1,0:T(8,128)(2,1)}, bf16[1024,512]{1,0:T(8,128)(2,1)S(1)}, u32[]{:S(2)}) copy-start(bf16[1024,512]{1,0:T(8,128)(2,1)S(1)} %get-tuple-element.539) | copy-start | bytes 3145732
  215.1 194.7 %copy-start.22 = (f32[1024,64]{0,1:T(8,128)S(1)}, f32[1024,64]{0,1:T(8,128)}, u32[]{:S(2)}) copy-start(f32[1024,64]{0,1:T(8,128)} %bitcast_reduce_fusion.1) | copy-start | bytes 786436
  242.0 6.8 %copy-start = (f32[512,1024]{1,0:T(8,128)S(1)}, f32[512,1024]{1,0:T(8,128)}, u32[]{:S(2)}) copy-start(f32[512,1024]{1,0:T(8,128)} %get-tuple-element.524) | copy-start | bytes 6291460 | tf_op jit(solution)/shard_map/while
  256.7 5.0 copy-start.5
  256.7 5.0 copy-start.7
  288.4 9.8 %copy-start = (f32[512,1024]{1,0:T(8,128)S(1)}, f32[512,1024]{1,0:T(8,128)}, u32[]{:S(2)}) copy-start(f32[512,1024]{1,0:T(8,128)} %get-tuple-element.524) | copy-start | bytes 6291460 | tf_op jit(solution)/shard_map/while
  306.0 5.0 copy-start.5
  306.0 5.0 copy-start.7
  337.7 9.8 %copy-start = (f32[512,1024]{1,0:T(8,128)S(1)}, f32[512,1024]{1,0:T(8,128)}, u32[]{:S(2)}) copy-start(f32[512,1024]{1,0:T(8,128)} %get-tuple-element.524) | copy-start | bytes 6291460 | tf_op jit(solution)/shard_map/while
  355.4 5.0 copy-start.5
  355.4 5.0 copy-start.7
  387.1 9.8 %copy-start = (f32[512,1024]{1,0:T(8,128)S(1)}, f32[512,1024]{1,0:T(8,128)}, u32[]{:S(2)}) copy-start(f32[512,1024]{1,0:T(8,128)} %get-tuple-element.524) | copy-start | bytes 6291460 | tf_op jit(solution)/shard_map/while
  404.8 5.0 copy-start.5
  404.8 5.0 copy-start.7
  413.7 118.6 %reduce-scatter.5.cloned.1.call-start = ((), (), s32[]{:S(2)}) async-start(), calls=%async_computation.5 | async-start | bytes 9437184 | tf_op jit(solution)/shard_map/reduce_scatter | solution.py:169
  413.8 11.8 %copy-start.28 = (bf16[512,1024]{1,0:T(8,128)(2,1)S(1)}, bf16[512,1024]{1,0:T(8,128)(2,1)}, u32[]{:S(2)}) copy-start(bf16[512,1024]{1,0:T(8,128)(2,1)} %param.10) | copy-start | bytes 3145732
  445.2 14.4 %collective-permute-start = (bf16[512,64]{0,1:T(8,128)(2,1)S(1)}, bf16[512,64]{0,1:T(8,128)(2,1)S(1)}, u32[]{:S(2)}, u32[]{:S(2)}) collective-permute-start(bf16[512,64]{0,1:T(8,128)(2,1)S(1)} %fusion.57), channel_id=1, source_target_pairs={{8,0},{16,8},{24,16},{9,1},{17,9},{25,17},{10,2},{18,10},{26,18},{... | collective-permute-start | bytes 196616 | tf_op jit(solution)/shard_map/ppermute | solution.py:14
  446.6 13.0 %copy-start.3 = (f32[1024,1024]{1,0:T(8,128)S(1)}, f32[1024,1024]{1,0:T(8,128)}, u32[]{:S(2)}) copy-start(f32[1024,1024]{1,0:T(8,128)} %copy-done.2) | copy-start | bytes 12582916
  446.6 13.0 %copy-start.23 = (bf16[1,1024,64]{1,2,0:T(8,128)(2,1)S(1)}, bf16[1,1024,64]{1,2,0:T(8,128)(2,1)}, u32[]{:S(2)}) copy-start(bf16[1,1024,64]{1,2,0:T(8,128)(2,1)} %reduce-scatter.7.cloned.1.call-done) | copy-start | bytes 393220
  (35 other events, 98.1 us)
Sparse Core Ops, SparseCore 0:
  9.6 84.7 all-gather.5
  96.2 53.3 all-gather.3
  152.0 52.6 all-gather.7
  413.8 24.7 reduce-scatter.6
  442.7 89.5 reduce-scatter.4
where the time goes:
time: 544 us; the launch traced here: 539 us
  waiting for transfers between devices  185 us (34%)
  other arithmetic  152 us (28%)
  matrix products  94.6 us (17%)
  local copies, waits for them, and re-layouts  80.6 us (15%)
  between operations  14.7 us (3%)
  blocking collectives  9.93 us (2%)
    all_gather x1, waiting for transfers between devices, local(): lax.all_gather(out_grad, 'tp', axis=1, tiled=True)  83.3 us
    reduce_scatter x1, waiting for transfers between devices, local(): lax.psum_scatter(partial_value.astype(jnp.bfloat16), 'tp', scatter_dimens...  71.1 us
    sub x5, other arithmetic, spec_product(): real_part = left_re * right_re - jnp.where(at_first, 0.0, im_product)  41 us
    add x4, other arithmetic, visit(): fwd_acc = fwd_acc + earlier * spec_product(filter_spec, spectrum)  36.1 us
    all_gather x1, waiting for transfers between devices, local(): lax.all_gather(conv_grad, 'ctx', axis=0, tiled=True)  29.9 us
    concatenate x5, local copies, waits for them, and re-layouts, spec_product(): return jnp.concatenate([real_part, imag_part], axis=0)  26.8 us
    while x72, local copies, waits for them, and re-layouts  20.2 us
    select_n x1, other arithmetic, basis_tables(): jnp.where((row_ids > length)[:, None], -jnp.sin(angles), jnp.cos(angles))  17.3 us
  transfers between devices with their start and end apart: 6, of which 3 were waited for; matrix products, arithmetic and copies ran while one was open for 22% of the time, Pallas kernels for 0%

commit v1 on v0

v1 whole, which is shorter than its diff:
```python
import functools
import math
import jax
import jax.numpy as jnp
from jax import lax
from jax.experimental import pallas as pl
from jax.experimental.pallas import tpu as pltpu
from jax.sharding import PartitionSpec as P

BLOCK = 128
NT = (((1,), (1,)), ((), ()))


def lag_matrix(row, length):
    lanes = lax.broadcasted_iota(jnp.int32, (BLOCK, length), 1)
    rows = lax.broadcasted_iota(jnp.int32, (BLOCK, length), 0)
    spread = pltpu.roll(
        jnp.broadcast_to(row, (BLOCK, length)), 0, axis=1, stride=1, stride_axis=0
    )
    return jnp.where(lanes >= rows, spread, 0.0).astype(jnp.bfloat16)


def stacked(ref, start, rows, members, width):
    pieces = []
    for member in range(members):
        part = ref[member, pl.ds(start, rows), :]
        for at in range(0, width, BLOCK):
            pieces.append(part[:, at : at + BLOCK])
    return jnp.concatenate(pieces, axis=0)


def spread_out(ref, start, rows, value, members, width):
    per_member = width // BLOCK
    for member in range(members):
        base = member * per_member * rows
        parts = [value[base + i * rows : base + (i + 1) * rows] for i in range(per_member)]
        ref[member, pl.ds(start, rows), :] = jnp.concatenate(parts, axis=1)


def forward_kernel(members, per_group, pos_ref, *refs):
    inputs, taps = refs[:members], refs[members : 2 * members]
    outputs = refs[2 * members : 3 * members]
    tap_scr, in_scr, out_scr = refs[3 * members :]
    position = pos_ref[0]
    width, channels = inputs[0].shape
    groups = taps[0].shape[0]
    length = members * width
    blocks = length // BLOCK
    for step in range(members):
        at = position ^ step
        in_scr[at] = inputs[step][...].T
        tap_scr[:, pl.ds(pl.multiple_of(at * width, width), width)] = taps[step][...]

    def one_group(group, carry):
        start = pl.multiple_of(group * per_group, per_group)
        lags = lag_matrix(tap_scr[pl.ds(group, 1), :], length)
        data = stacked(in_scr, start, per_group, members, width)
        total = [jnp.zeros((per_group, BLOCK), jnp.float32) for _ in range(blocks)]
        for offset in range(0, blocks, 2):
            rows = (blocks - offset) * per_group
            result = jnp.dot(
                data[:rows],
                lags[:, offset * BLOCK : (offset + 2) * BLOCK],
                preferred_element_type=jnp.float32,
            )
            for side in range(2):
                for source in range(blocks - offset - side):
                    total[source + offset + side] += result[
                        source * per_group : (source + 1) * per_group,
                        side * BLOCK : (side + 1) * BLOCK,
                    ]
        value = jnp.concatenate(total, axis=0).astype(jnp.bfloat16)
        spread_out(out_scr, start, per_group, value, members, width)
        return carry

    lax.fori_loop(0, groups, one_group, 0)
    for step in range(members):
        outputs[step][...] = out_scr[position ^ step].T


def backward_kernel(members, per_group, scale, pos_ref, *refs):
    inputs, cotangents, taps = (
        refs[:members],
        refs[members : 2 * members],
        refs[2 * members : 3 * members],
    )
    outputs = refs[3 * members : 4 * members]
    tap_grads = refs[4 * members : 5 * members]
    tap_scr, in_scr, cot_scr, out_scr, grad_scr, pad_scr = refs[5 * members :]
    position = pos_ref[0]
    width, channels = inputs[0].shape
    groups = taps[0].shape[0]
    length = members * width
    blocks = length // BLOCK
    depth = blocks * per_group
    for step in range(members):
        at = position ^ step
        in_scr[at] = inputs[step][...].T
        cot_scr[at] = cotangents[step][...].T
        tap_scr[:, pl.ds(pl.multiple_of(at * width, width), width)] = taps[step][...]
    pad_scr[...] = jnp.zeros_like(pad_scr)
    rows_of = lax.broadcasted_iota(jnp.int32, (BLOCK, BLOCK), 0)
    lanes_of = lax.broadcasted_iota(jnp.int32, (BLOCK, BLOCK), 1)
    mirror = (rows_of + lanes_of == BLOCK - 1).astype(jnp.bfloat16)

    def one_group(group, carry):
        start = pl.multiple_of(group * per_group, per_group)
        lags = lag_matrix(tap_scr[pl.ds(group, 1), :], length)
        data = stacked(in_scr, start, per_group, members, width)
        cot = stacked(cot_scr, start, per_group, members, width)
        pad_scr[:depth, :BLOCK] = cot
        pad_scr[: depth - per_group, BLOCK:] = cot[per_group:]
        flipped = lax.dot_general(
            mirror, data, NT, preferred_element_type=jnp.float32
        ).astype(jnp.bfloat16)
        total = jnp.zeros((depth, BLOCK), jnp.float32)
        products = []
        for offset in range(0, blocks, 2):
            rows = depth - offset * per_group
            pair = pad_scr[offset * per_group : offset * per_group + depth, :]
            result = lax.dot_general(
                pair[:rows],
                lags[:, offset * BLOCK : (offset + 2) * BLOCK],
                NT,
                preferred_element_type=jnp.float32,
            )
            if rows < depth:
                result = jnp.concatenate(
                    [result, jnp.zeros((depth - rows, BLOCK), jnp.float32)], axis=0
                )
            total = total + result
            products.append(jnp.dot(flipped, pair, preferred_element_type=jnp.float32))
        spread_out(
            out_scr, start, per_group, total.astype(jnp.bfloat16), members, width
        )
        product = jnp.concatenate(products, axis=1)
        lanes = lax.broadcasted_iota(jnp.int32, (BLOCK, length), 1)
        back = BLOCK - 1 - lax.broadcasted_iota(jnp.int32, (BLOCK, length), 0)
        product = jnp.where(lanes >= back, product, 0.0)
        product = pltpu.roll(
            product, length - (BLOCK - 1), axis=1, stride=1, stride_axis=0
        )
        grad_scr[pl.ds(group, 1), :] = jnp.sum(product, axis=0, keepdims=True) * scale
        return carry

    lax.fori_loop(0, groups, one_group, 0)
    for step in range(members):
        at = position ^ step
        outputs[step][...] = out_scr[at].T
        tap_grads[step][...] = grad_scr[:, pl.ds(pl.multiple_of(at * width, width), width)]


VMEM = pl.BlockSpec(memory_space=pltpu.VMEM)
SMEM = pl.BlockSpec(memory_space=pltpu.SMEM)


def convolve(position, inputs, taps, per_group):
    members = len(inputs)
    width, channels = inputs[0].shape
    groups = taps[0].shape[0]
    length = members * width
    flops = 4 * length * length * channels
    return pl.pallas_call(
        functools.partial(forward_kernel, members, per_group),
        out_shape=[jax.ShapeDtypeStruct((width, channels), jnp.bfloat16)] * members,
        in_specs=[SMEM] + [VMEM] * (2 * members),
        out_specs=[VMEM] * members,
        scratch_shapes=[
            pltpu.VMEM((groups, length), jnp.float32),
            pltpu.VMEM((members, channels, width), jnp.bfloat16),
            pltpu.VMEM((members, channels, width), jnp.bfloat16),
        ],
        compiler_params=pltpu.CompilerParams(vmem_limit_bytes=32 * 2**20),
        cost_estimate=pl.CostEstimate(
            flops=flops, bytes_accessed=4 * length * channels, transcendentals=0
        ),
        name="causal_conv",
    )(position, *inputs, *taps)


def correlate(position, inputs, cotangents, taps, per_group, scale):
    members = len(inputs)
    width, channels = inputs[0].shape
    groups = taps[0].shape[0]
    length = members * width
    flops = 8 * length * length * channels
    results = pl.pallas_call(
        functools.partial(backward_kernel, members, per_group, scale),
        out_shape=[jax.ShapeDtypeStruct((width, channels), jnp.bfloat16)] * members
        + [jax.ShapeDtypeStruct((groups, width), jnp.float32)] * members,
        in_specs=[SMEM] + [VMEM] * (3 * members),
        out_specs=[VMEM] * (2 * members),
        scratch_shapes=[
            pltpu.VMEM((groups, length), jnp.float32),
            pltpu.VMEM((members, channels, width), jnp.bfloat16),
            pltpu.VMEM((members, channels, width), jnp.bfloat16),
            pltpu.VMEM((members, channels, width), jnp.bfloat16),
            pltpu.VMEM((groups, length), jnp.float32),
            pltpu.VMEM((2 * length // BLOCK * per_group, 2 * BLOCK), jnp.bfloat16),
        ],
        compiler_params=pltpu.CompilerParams(vmem_limit_bytes=32 * 2**20),
        cost_estimate=pl.CostEstimate(
            flops=flops, bytes_accessed=6 * length * channels, transcendentals=0
        ),
        name="causal_conv_grads",
    )(position, *inputs, *cotangents, *taps)
    return results[:members], results[members:]


def swapped(array, axis, step):
    size = lax.axis_size(axis)
    return lax.ppermute(array, axis, [(i, i ^ step) for i in range(size)])


def traded(pieces, axis):
    return [pieces[0]] + [swapped(pieces[step], axis, step) for step in range(1, len(pieces))]


def cut(array, position, members, axis):
    width = array.shape[axis] // members
    return [
        lax.dynamic_slice_in_dim(array, (position ^ step) * width, width, axis)
        for step in range(members)
    ]


def joined(pieces, position, axis):
    members = len(pieces)
    width = pieces[0].shape[axis]
    shape = list(pieces[0].shape)
    shape[axis] = members * width
    whole = jnp.zeros(shape, pieces[0].dtype)
    for step in range(members):
        whole = lax.dynamic_update_slice_in_dim(
            whole, pieces[step], (position ^ step) * width, axis
        )
    return whole


def wide(array):
    return array.astype(jnp.float32)


def local(query_gate, key_gate, value_input, filter_taps, out_weight, out_grad):
    length, channels = query_gate.shape
    groups = filter_taps.shape[1]
    per_group = channels // groups
    members = lax.axis_size("ctx")
    position = lax.axis_index("ctx")
    at = position.reshape((1,)).astype(jnp.int32)
    tap_scale = 1.0 / math.sqrt(length * members)

    all_cotangents = lax.all_gather(out_grad, "tp", axis=1, tiled=True)
    tap_rows = (filter_taps * tap_scale).astype(jnp.bfloat16).T
    tap_parts = [wide(p) for p in traded(cut(tap_rows, position, members, 0), "ctx")]
    product_in = (wide(key_gate) * wide(value_input)).astype(jnp.bfloat16)
    input_parts = traded(cut(product_in, position, members, 1), "ctx")
    conv_parts = traded(convolve(at, input_parts, tap_parts, per_group), "ctx")
    convolved = joined(conv_parts, position, 1)
    gated_out = (wide(query_gate) * wide(convolved)).astype(jnp.bfloat16)
    partial_value = jnp.dot(gated_out, out_weight, preferred_element_type=jnp.float32)
    projected = lax.psum_scatter(
        partial_value.astype(jnp.bfloat16), "tp", scatter_dimension=1, tiled=True
    )
    dgated = jnp.einsum(
        "tk,ck->tc", all_cotangents, out_weight, preferred_element_type=jnp.float32
    ).astype(jnp.bfloat16)
    grad_query = (wide(dgated) * wide(convolved)).astype(jnp.bfloat16)
    conv_grad = (wide(dgated) * wide(query_gate)).astype(jnp.bfloat16)
    grad_parts = traded(cut(conv_grad, position, members, 1), "ctx")
    back_parts, filter_parts = correlate(
        at, input_parts, grad_parts, tap_parts, per_group, tap_scale
    )
    input_grad = wide(joined(traded(back_parts, "ctx"), position, 1))
    grad_filter = joined(traded(filter_parts, "ctx"), position, 0).T
    grad_key = (input_grad * wide(value_input)).astype(jnp.bfloat16)
    grad_value = (input_grad * wide(key_gate)).astype(jnp.bfloat16)
    return (projected, grad_query, grad_key, grad_value, grad_filter)


def solution(mesh):
    both = P("ctx", "tp")
    return jax.shard_map(
        local,
        mesh=mesh,
        in_specs=(both, both, both, both, P("tp", None), both),
        out_specs=(both,) * 5,
        check_vma=False,
    )
```

time: 544 us -> 192 us (0.35)
  other arithmetic: 152 us -> 4.11 us
  waiting for transfers between devices: 185 us -> 95.6 us
  local copies, waits for them, and re-layouts: 80.6 us -> 0.79 us
  matrix products: 94.6 us -> 32.6 us
  starting transfers between devices: 1.49 us -> 25 us
  Pallas kernels: 0 us -> 19.8 us
  blocking collectives: 9.93 us -> 0 us
    all_gather x3 -> x1, waiting for transfers between devices: 113 us -> 26.2 us  [local(): all_cotangents = lax.all_gather(out_grad, 'tp', axis=1, tiled=True)]
    dot_general x25 -> x1, matrix products: 77.7 us -> 15.7 us  [local(): jnp.einsum('tk,ck->tc', all_cotangents, out_weight, preferred_element_typ...]
    reduce_scatter x1, waiting for transfers between devices: 71.1 us -> 27.8 us  [local(): lax.psum_scatter(partial_value.astype(jnp.bfloat16), 'tp', scatter_dimens...]
    sub x5 -> x0, other arithmetic: 41 us -> none  [spec_product(): real_part = left_re * right_re - jnp.where(at_first, 0.0, im_product)]
    ppermute x1 -> x18, waiting for transfers between devices: 0.01 us -> 40.9 us  [swapped(): return lax.ppermute(array, axis, [(i, i ^ step) for i in range(size)])]
    add x4 -> x0, other arithmetic: 36.1 us -> none  [visit(): fwd_acc = fwd_acc + earlier * spec_product(filter_spec, spectrum)]
    select_n x7 -> x0, other arithmetic: 28.2 us -> none  [the longest x1 17.3 us: basis_tables(): jnp.where((row_ids > length)[:, None], -jnp.sin(angles), jnp.cos(angles))]
    concatenate x5 -> x0, local copies, waits for them, and re-layouts: 26.8 us -> none  [spec_product(): return jnp.concatenate([real_part, imag_part], axis=0)]
  transfers between devices with their start and end apart: 6 -> 20, of which waited for: 3 -> 11; matrix products, arithmetic and copies ran while one was open for 22% -> 20% of each run, Pallas kernels for 0% -> 10%
where the time goes in v1:
time: 192 us
  waiting for transfers between devices  95.6 us (50%)
  matrix products  32.6 us (17%)
  starting transfers between devices  25 us (13%)
  Pallas kernels  19.8 us (10%)
  between operations  14.3 us (7%)
  other arithmetic  4.11 us (2%)
    ppermute x18, waiting for transfers between devices, swapped(): return lax.ppermute(array, axis, [(i, i ^ step) for i in range(size)])  40.9 us
    reduce_scatter x1, waiting for transfers between devices, local(): lax.psum_scatter(partial_value.astype(jnp.bfloat16), 'tp', scatter_dimens...  27.8 us
    all_gather x1, waiting for transfers between devices, local(): all_cotangents = lax.all_gather(out_grad, 'tp', axis=1, tiled=True)  26.2 us
    ppermute x18, starting transfers between devices, swapped(): return lax.ppermute(array, axis, [(i, i ^ step) for i in range(size)])  24.9 us
    dot_general x1, matrix products, local(): jnp.dot(gated_out, out_weight, preferred_element_type=jnp.float32)  16.9 us
    dot_general x1, matrix products, local(): jnp.einsum('tk,ck->tc', all_cotangents, out_weight, preferred_element_typ...  15.7 us
    pallas_call x1, Pallas kernels, correlate(): pl.pallas_call(functools.partial(backward_kernel, members, per_group, sca...  12.4 us
    pallas_call x1, Pallas kernels, convolve(): pl.pallas_call(functools.partial(forward_kernel, members, per_group), out...  7.38 us
  transfers between devices with their start and end apart: 20, of which 11 were waited for; matrix products, arithmetic and copies ran while one was open for 20% of the time, Pallas kernels for 10%

profile of v1, /device:TPU:0, one launch (start us, length us, event | category | flops | bytes accessed | tf_op | source)
XLA Modules:
  0.0 192.3 jit_solution(6440064880448226605)
XLA Ops:
  8.0 2.0 %fusion = bf16[512,1024]{1,0:T(8,128)(2,1)S(1)} fusion(bf16[512,1024]{1,0:T(8,128)(2,1)} %param.8, bf16[512,1024]{1,0:T(8,128)(2,1)} %param.7), kind=kLoop, calls=%fused_computation.7 | loop fusion | flops 2097152 | bytes 3145728 | tf_op jit(solution)/shard_map/convert_element_type | solution.py:256
  10.1 3.0 %collective-permute-start = (bf16[512,256]{1,0:T(8,128)(2,1)S(1)}, bf16[512,256]{1,0:T(8,128)(2,1)S(1)}, u32[]{:S(2)}, u32[]{:S(2)}) collective-permute-start(bf16[512,256]{1,0:T(8,128)(2,1)S(1)} %get-tuple-element.39), channel_id=1, source_target_pairs={{0,8},{8,0},{16,24},{24,16},{1,9},{9,1},{17,25},{25,17},{2,10},{10... | collective-permute-start | bytes 786440 | tf_op jit(solution)/shard_map/ppermute | solution.py:212
  13.1 1.5 collective-permute-start.1
  14.7 2.0 %collective-permute-start.3 = (bf16[16,512]{1,0:T(8,128)(2,1)S(1)}, bf16[16,512]{1,0:T(8,128)(2,1)S(1)}, u32[]{:S(2)}, u32[]{:S(2)}) collective-permute-start(bf16[16,512]{1,0:T(8,128)(2,1)S(1)} %get-tuple-element.43), channel_id=1, source_target_pairs={{0,8},{8,0},{16,24},{24,16},{1,9},{9,1},{17,25},{25,17},{2,10},{10... | collective-permute-start | bytes 49160 | tf_op jit(solution)/shard_map/ppermute | solution.py:212
  16.7 1.5 collective-permute-start.4
  18.2 7.2 %collective-permute-done.3 = bf16[16,512]{1,0:T(8,128)(2,1)S(1)} collective-permute-done((bf16[16,512]{1,0:T(8,128)(2,1)S(1)}, bf16[16,512]{1,0:T(8,128)(2,1)S(1)}, u32[]{:S(2)}, u32[]{:S(2)}) %collective-permute-start.3) | collective-permute-done | bytes 16416 | tf_op jit(solution)/shard_map/ppermute | solution.py:212
  25.4 2.6 %collective-permute-start.5 = (bf16[16,512]{1,0:T(8,128)(2,1)S(1)}, bf16[16,512]{1,0:T(8,128)(2,1)S(1)}, u32[]{:S(2)}, u32[]{:S(2)}) collective-permute-start(bf16[16,512]{1,0:T(8,128)(2,1)S(1)} %get-tuple-element.41), channel_id=1, source_target_pairs={{0,24},{8,16},{16,8},{24,0},{1,25},{9,17},{17,9},{25,1},{2,26},{10... | collective-permute-start | bytes 49160 | tf_op jit(solution)/shard_map/ppermute | solution.py:212
  28.1 2.0 %collective-permute-done.5 = bf16[16,512]{1,0:T(8,128)(2,1)S(1)} collective-permute-done((bf16[16,512]{1,0:T(8,128)(2,1)S(1)}, bf16[16,512]{1,0:T(8,128)(2,1)S(1)}, u32[]{:S(2)}, u32[]{:S(2)}) %collective-permute-start.5) | collective-permute-done | bytes 16416 | tf_op jit(solution)/shard_map/ppermute | solution.py:212
  30.1 7.4 %causal_conv.1 = (bf16[512,256]{1,0:T(8,128)(2,1)S(1)}, bf16[512,256]{1,0:T(8,128)(2,1)S(1)}, bf16[512,256]{1,0:T(8,128)(2,1)S(1)}, bf16[512,256]{1,0:T(8,128)(2,1)S(1)}) custom-call(s32[1]{0:T(128)} %bitcast.pos_ref, bf16[512,256]{1,0:T(8,128)(2,1)S(1)} %get-tuple-element.40.refs_0_, bf16[512,256]{1,0:T(8,128)(2,1)S(1)} %collective-permute-done.refs_1_, ...), custom_call_target="tpu_custom_call" | custom-call | flops 4294967296 | bytes 2097152 | tf_op jit(solution)/shard_map/causal_conv/pallas_call | solution.py:163
  37.5 1.8 collective-permute-start.6
  41.2 5.6 %collective-permute-done.6 = bf16[512,256]{1,0:T(8,128)(2,1)S(1)} collective-permute-done((bf16[512,256]{1,0:T(8,128)(2,1)S(1)}, bf16[512,256]{1,0:T(8,128)(2,1)S(1)}, u32[]{:S(2)}, u32[]{:S(2)}) %collective-permute-start.6) | collective-permute-done | bytes 262176 | tf_op jit(solution)/shard_map/ppermute | solution.py:212
  46.9 4.3 %collective-permute-done.7 = bf16[512,256]{1,0:T(8,128)(2,1)S(1)} collective-permute-done((bf16[512,256]{1,0:T(8,128)(2,1)S(1)}, bf16[512,256]{1,0:T(8,128)(2,1)S(1)}, u32[]{:S(2)}, u32[]{:S(2)}) %collective-permute-start.7) | collective-permute-done | bytes 262176 | tf_op jit(solution)/shard_map/ppermute | solution.py:212
  51.3 16.9 %convolution_convert_fusion = bf16[512,8192]{1,0:T(8,128)(2,1)} fusion(bf16[1024,8192]{1,0:T(8,128)(2,1)} %param.10, bf16[512,1024]{1,0:T(8,128)(2,1)S(1)} %constant_dynamic-update-slice_fusion.8, bf16[512,1024]{1,0:T(8,128)(2,1)S(1)} %copy-done.4), kind=kOutput, calls=%fused_computation | convolution fusion | flops 8596226048 | bytes 27262976 | tf_op jit(solution)/shard_map/dot_general | solution.py:261
  68.2 26.2 %all-gather.2.cloned.1.call-done = bf16[512,8192]{1,0:T(8,128)(2,1)} async-done(((bf16[512,1024]{1,0:T(8,128)(2,1)}), bf16[512,8192]{1,0:T(8,128)(2,1)}) %all-gather.2.cloned.1.call-update) | async-done | bytes 8388624 | tf_op jit(solution)/shard_map/all_gather | solution.py:253
  94.4 15.7 %fusion.3 = (bf16[512,1024]{1,0:T(8,128)(2,1)S(1)}, bf16[512,1024]{1,0:T(8,128)(2,1)}) fusion(bf16[512,1024]{1,0:T(8,128)(2,1)S(1)} %copy-done.4, bf16[512,1024]{1,0:T(8,128)(2,1)S(1)} %constant_dynamic-update-slice_fusion.8, bf16[512,8192]{1,0:T(8,128)(2,1)} %all-gather.2.cloned.1.call-done, bf16[1024,8192]{1,0:T(8,128)(2,1)} %param.10), kind=kOutput, calls=%fused_computation.10 | convolution fusion | flops 8594128896 | bytes 29360128 | tf_op jit(solution)/shard_map/tk,ck->tc/dot_general | solution.py:265
  110.2 1.5 collective-permute-start.10
  113.8 10.6 %collective-permute-done.10.refs_6_ = bf16[512,256]{1,0:T(8,128)(2,1)S(1)} collective-permute-done((bf16[512,256]{1,0:T(8,128)(2,1)S(1)}, bf16[512,256]{1,0:T(8,128)(2,1)S(1)}, u32[]{:S(2)}, u32[]{:S(2)}) %collective-permute-start.10) | collective-permute-done | bytes 262176 | tf_op jit(solution)/shard_map/ppermute | solution.py:212
  125.6 12.4 %causal_conv_grads.1 = (bf16[512,256]{1,0:T(8,128)(2,1)S(1)}, bf16[512,256]{1,0:T(8,128)(2,1)S(1)}, bf16[512,256]{1,0:T(8,128)(2,1)S(1)}, bf16[512,256]{1,0:T(8,...) custom-call(s32[1]{0:T(128)} %bitcast.pos_ref, ...), custom_call_target="tpu_custom_call" | custom-call | flops 8589934592 | bytes 3145728 | tf_op jit(solution)/shard_map/causal_conv_grads/pallas_call | solution.py:187
  138.1 1.5 collective-permute-start.15
  139.6 1.5 collective-permute-start.16
  146.3 4.7 %collective-permute-done.12 = bf16[512,256]{1,0:T(8,128)(2,1)S(1)} collective-permute-done((bf16[512,256]{1,0:T(8,128)(2,1)S(1)}, bf16[512,256]{1,0:T(8,128)(2,1)S(1)}, u32[]{:S(2)}, u32[]{:S(2)}) %collective-permute-start.12) | collective-permute-done | bytes 262176 | tf_op jit(solution)/shard_map/ppermute | solution.py:212
  151.1 4.4 %collective-permute-done.13 = bf16[512,256]{1,0:T(8,128)(2,1)S(1)} collective-permute-done((bf16[512,256]{1,0:T(8,128)(2,1)S(1)}, bf16[512,256]{1,0:T(8,128)(2,1)S(1)}, u32[]{:S(2)}, u32[]{:S(2)}) %collective-permute-start.13) | collective-permute-done | bytes 262176 | tf_op jit(solution)/shard_map/ppermute | solution.py:212
  155.6 2.1 %fusion.5 = (bf16[512,1024]{1,0:T(8,128)(2,1)}, bf16[512,1024]{1,0:T(8,128)(2,1)}) fusion(bf16[512,1024]{1,0:T(8,128)(2,1)S(1)} %copy-done.1, bf16[512,1024]{1,0:T(8,128)(2,1)S(1)} %constant_dynamic-update-slice_fusion.4, bf16[512,1024]{1,0:T(8,128)(2,1)S(1)} %copy-done), kind=kLoop, calls=%fused_computation.12 | loop fusion | flops 3670016 | bytes 5242880 | tf_op jit(solution)/shard_map/convert_element_type | solution.py:277
  157.7 27.8 %reduce-scatter.2.cloned.1.call-done = bf16[512,1024]{1,0:T(8,128)(2,1)} async-done(((bf16[512,8192]{1,0:T(8,128)(2,1)}), bf16[512,1024]{1,0:T(8,128)(2,1)}) %reduce-scatter.2.cloned.1.call-update) | async-done | bytes 1048592 | tf_op jit(solution)/shard_map/reduce_scatter | solution.py:262
  (56 shorter events, 11.7 us)
Async XLA Ops:
  7.2 87.2 %all-gather.2.cloned.1.call-start = ((), (), s32[]{:S(2)}) async-start(), calls=%async_computation.2 | async-start | bytes 9437184 | tf_op jit(solution)/shard_map/all_gather | solution.py:253
  7.9 177.5 %reduce-scatter.2.cloned.1.call-start = ((), (), s32[]{:S(2)}) async-start(), calls=%async_computation.1 | async-start | bytes 9437184 | tf_op jit(solution)/shard_map/reduce_scatter | solution.py:262
  10.1 20.0 %collective-permute-start = (bf16[512,256]{1,0:T(8,128)(2,1)S(1)}, bf16[512,256]{1,0:T(8,128)(2,1)S(1)}, u32[]{:S(2)}, u32[]{:S(2)}) collective-permute-start(bf16[512,256]{1,0:T(8,128)(2,1)S(1)} %get-tuple-element.39), channel_id=1, source_target_pairs={{0,8},{8,0},{16,24},{24,16},{1,9},{9,1},{17,25},{25,17},{2,10},{10... | collective-permute-start | bytes 786440 | tf_op jit(solution)/shard_map/ppermute | solution.py:212
  13.1 17.0 %collective-permute-start.1 = (bf16[512,256]{1,0:T(8,128)(2,1)S(1)}, bf16[512,256]{1,0:T(8,128)(2,1)S(1)}, u32[]{:S(2)}, u32[]{:S(2)}) collective-permute-start(bf16[512,256]{1,0:T(8,128)(2,1)S(1)} %get-tuple-element.38), channel_id=1, source_target_pairs={{0,16},{8,24},{16,0},{24,8},{1,17},{9,25},{17,1},{25,9},{2,18},{10... | collective-permute-start | bytes 786440 | tf_op jit(solution)/shard_map/ppermute | solution.py:212
  14.6 15.5 %collective-permute-start.2 = (bf16[512,256]{1,0:T(8,128)(2,1)S(1)}, bf16[512,256]{1,0:T(8,128)(2,1)S(1)}, u32[]{:S(2)}, u32[]{:S(2)}) collective-permute-start(bf16[512,256]{1,0:T(8,128)(2,1)S(1)} %get-tuple-element.37), channel_id=1, source_target_pairs={{0,24},{8,16},{16,8},{24,0},{1,25},{9,17},{17,9},{25,1},{2,26},{10... | collective-permute-start | bytes 786440 | tf_op jit(solution)/shard_map/ppermute | solution.py:212
  14.7 10.7 %collective-permute-start.3 = (bf16[16,512]{1,0:T(8,128)(2,1)S(1)}, bf16[16,512]{1,0:T(8,128)(2,1)S(1)}, u32[]{:S(2)}, u32[]{:S(2)}) collective-permute-start(bf16[16,512]{1,0:T(8,128)(2,1)S(1)} %get-tuple-element.43), channel_id=1, source_target_pairs={{0,8},{8,0},{16,24},{24,16},{1,9},{9,1},{17,25},{25,17},{2,10},{10... | collective-permute-start | bytes 49160 | tf_op jit(solution)/shard_map/ppermute | solution.py:212
  16.7 11.4 %collective-permute-start.4 = (bf16[16,512]{1,0:T(8,128)(2,1)S(1)}, bf16[16,512]{1,0:T(8,128)(2,1)S(1)}, u32[]{:S(2)}, u32[]{:S(2)}) collective-permute-start(bf16[16,512]{1,0:T(8,128)(2,1)S(1)} %get-tuple-element.42), channel_id=1, source_target_pairs={{0,16},{8,24},{16,0},{24,8},{1,17},{9,25},{17,1},{25,9},{2,18},{10... | collective-permute-start | bytes 49160 | tf_op jit(solution)/shard_map/ppermute | solution.py:212
  25.4 4.6 %collective-permute-start.5 = (bf16[16,512]{1,0:T(8,128)(2,1)S(1)}, bf16[16,512]{1,0:T(8,128)(2,1)S(1)}, u32[]{:S(2)}, u32[]{:S(2)}) collective-permute-start(bf16[16,512]{1,0:T(8,128)(2,1)S(1)} %get-tuple-element.41), channel_id=1, source_target_pairs={{0,24},{8,16},{16,8},{24,0},{1,25},{9,17},{17,9},{25,1},{2,26},{10... | collective-permute-start | bytes 49160 | tf_op jit(solution)/shard_map/ppermute | solution.py:212
  37.5 13.8 %copy-start.4 = (bf16[512,1024]{1,0:T(8,128)(2,1)S(1)}, bf16[512,1024]{1,0:T(8,128)(2,1)}, u32[]{:S(2)}) copy-start(bf16[512,1024]{1,0:T(8,128)(2,1)} %param.6) | copy-start | bytes 3145732
  37.5 9.3 %collective-permute-start.6 = (bf16[512,256]{1,0:T(8,128)(2,1)S(1)}, bf16[512,256]{1,0:T(8,128)(2,1)S(1)}, u32[]{:S(2)}, u32[]{:S(2)}) collective-permute-start(bf16[512,256]{1,0:T(8,128)(2,1)S(1)} %get-tuple-element.18), channel_id=1, source_target_pairs={{0,8},{8,0},{16,24},{24,16},{1,9},{9,1},{17,25},{25,17},{2,10},{10... | collective-permute-start | bytes 786440 | tf_op jit(solution)/shard_map/ppermute | solution.py:212
  39.3 11.9 %collective-permute-start.7 = (bf16[512,256]{1,0:T(8,128)(2,1)S(1)}, bf16[512,256]{1,0:T(8,128)(2,1)S(1)}, u32[]{:S(2)}, u32[]{:S(2)}) collective-permute-start(bf16[512,256]{1,0:T(8,128)(2,1)S(1)} %get-tuple-element.19), channel_id=1, source_target_pairs={{0,16},{8,24},{16,0},{24,8},{1,17},{9,25},{17,1},{25,9},{2,18},{10... | collective-permute-start | bytes 786440 | tf_op jit(solution)/shard_map/ppermute | solution.py:212
  40.8 10.4 %collective-permute-start.8 = (bf16[512,256]{1,0:T(8,128)(2,1)S(1)}, bf16[512,256]{1,0:T(8,128)(2,1)S(1)}, u32[]{:S(2)}, u32[]{:S(2)}) collective-permute-start(bf16[512,256]{1,0:T(8,128)(2,1)S(1)} %get-tuple-element.20), channel_id=1, source_target_pairs={{0,24},{8,16},{16,8},{24,0},{1,25},{9,17},{17,9},{25,1},{2,26},{10... | collective-permute-start | bytes 786440 | tf_op jit(solution)/shard_map/ppermute | solution.py:212
  110.2 14.1 %collective-permute-start.10 = (bf16[512,256]{1,0:T(8,128)(2,1)S(1)}, bf16[512,256]{1,0:T(8,128)(2,1)S(1)}, u32[]{:S(2)}, u32[]{:S(2)}) collective-permute-start(bf16[512,256]{1,0:T(8,128)(2,1)S(1)} %get-tuple-element.32), channel_id=1, source_target_pairs={{0,16},{8,24},{16,0},{24,8},{1,17},{9,25},{17,1},{25,9},{2,18},{10... | collective-permute-start | bytes 786440 | tf_op jit(solution)/shard_map/ppermute | solution.py:212
  111.8 12.6 %collective-permute-start.11 = (bf16[512,256]{1,0:T(8,128)(2,1)S(1)}, bf16[512,256]{1,0:T(8,128)(2,1)S(1)}, u32[]{:S(2)}, u32[]{:S(2)}) collective-permute-start(bf16[512,256]{1,0:T(8,128)(2,1)S(1)} %get-tuple-element.31), channel_id=1, source_target_pairs={{0,24},{8,16},{16,8},{24,0},{1,25},{9,17},{17,9},{25,1},{2,26},{10... | collective-permute-start | bytes 786440 | tf_op jit(solution)/shard_map/ppermute | solution.py:212
  113.2 12.4 %collective-permute-start.9 = (bf16[512,256]{1,0:T(8,128)(2,1)S(1)}, bf16[512,256]{1,0:T(8,128)(2,1)S(1)}, u32[]{:S(2)}, u32[]{:S(2)}) collective-permute-start(bf16[512,256]{1,0:T(8,128)(2,1)S(1)} %get-tuple-element.33), channel_id=1, source_target_pairs={{0,8},{8,0},{16,24},{24,16},{1,9},{9,1},{17,25},{25,17},{2,10},{10... | collective-permute-start | bytes 786440 | tf_op jit(solution)/shard_map/ppermute | solution.py:212
  138.1 17.5 %copy-start = (bf16[512,1024]{1,0:T(8,128)(2,1)S(1)}, bf16[512,1024]{1,0:T(8,128)(2,1)}, u32[]{:S(2)}) copy-start(bf16[512,1024]{1,0:T(8,128)(2,1)} %param.8) | copy-start | bytes 3145732
  138.1 17.5 %copy-start.1 = (bf16[512,1024]{1,0:T(8,128)(2,1)S(1)}, bf16[512,1024]{1,0:T(8,128)(2,1)}, u32[]{:S(2)}) copy-start(bf16[512,1024]{1,0:T(8,128)(2,1)} %param.7) | copy-start | bytes 3145732
  138.1 6.7 %collective-permute-start.15 = (f32[16,512]{1,0:T(8,128)S(1)}, f32[16,512]{1,0:T(8,128)S(1)}, u32[]{:S(2)}, u32[]{:S(2)}) collective-permute-start(f32[16,512]{1,0:T(8,128)S(1)} %get-tuple-element.26), channel_id=1, source_target_pairs={{0,8},{8,0},{16,24},{24,16},{1,9},{9,1},{17,25},{25,17},{2,10},{10... | collective-permute-start | bytes 98312 | tf_op jit(solution)/shard_map/ppermute | solution.py:212
  139.6 5.8 %collective-permute-start.16 = (f32[16,512]{1,0:T(8,128)S(1)}, f32[16,512]{1,0:T(8,128)S(1)}, u32[]{:S(2)}, u32[]{:S(2)}) collective-permute-start(f32[16,512]{1,0:T(8,128)S(1)} %get-tuple-element.27), channel_id=1, source_target_pairs={{0,16},{8,24},{16,0},{24,8},{1,17},{9,25},{17,1},{25,9},{2,18},{10... | collective-permute-start | bytes 98312 | tf_op jit(solution)/shard_map/ppermute | solution.py:212
  141.1 5.2 %collective-permute-start.17 = (f32[16,512]{1,0:T(8,128)S(1)}, f32[16,512]{1,0:T(8,128)S(1)}, u32[]{:S(2)}, u32[]{:S(2)}) collective-permute-start(f32[16,512]{1,0:T(8,128)S(1)} %get-tuple-element.28), channel_id=1, source_target_pairs={{0,24},{8,16},{16,8},{24,0},{1,25},{9,17},{17,9},{25,1},{2,26},{10... | collective-permute-start | bytes 98312 | tf_op jit(solution)/shard_map/ppermute | solution.py:212
  141.6 9.4 %collective-permute-start.12 = (bf16[512,256]{1,0:T(8,128)(2,1)S(1)}, bf16[512,256]{1,0:T(8,128)(2,1)S(1)}, u32[]{:S(2)}, u32[]{:S(2)}) collective-permute-start(bf16[512,256]{1,0:T(8,128)(2,1)S(1)} %get-tuple-element.22), channel_id=1, source_target_pairs={{0,8},{8,0},{16,24},{24,16},{1,9},{9,1},{17,25},{25,17},{2,10},{10... | collective-permute-start | bytes 786440 | tf_op jit(solution)/shard_map/ppermute | solution.py:212
  143.1 12.4 %collective-permute-start.13 = (bf16[512,256]{1,0:T(8,128)(2,1)S(1)}, bf16[512,256]{1,0:T(8,128)(2,1)S(1)}, u32[]{:S(2)}, u32[]{:S(2)}) collective-permute-start(bf16[512,256]{1,0:T(8,128)(2,1)S(1)} %get-tuple-element.23), channel_id=1, source_target_pairs={{0,16},{8,24},{16,0},{24,8},{1,17},{9,25},{17,1},{25,9},{2,18},{10... | collective-permute-start | bytes 786440 | tf_op jit(solution)/shard_map/ppermute | solution.py:212
  144.8 10.7 %collective-permute-start.14 = (bf16[512,256]{1,0:T(8,128)(2,1)S(1)}, bf16[512,256]{1,0:T(8,128)(2,1)S(1)}, u32[]{:S(2)}, u32[]{:S(2)}) collective-permute-start(bf16[512,256]{1,0:T(8,128)(2,1)S(1)} %get-tuple-element.24), channel_id=1, source_target_pairs={{0,24},{8,16},{16,8},{24,0},{1,25},{9,17},{17,9},{25,1},{2,26},{10... | collective-permute-start | bytes 786440 | tf_op jit(solution)/shard_map/ppermute | solution.py:212
  146.3 11.3 %copy-start.3 = (f32[64,512]{1,0:T(8,128)}, f32[64,512]{1,0:T(8,128)S(1)}, u32[]{:S(2)}) copy-start(f32[64,512]{1,0:T(8,128)S(1)} %constant_dynamic-update-slice_fusion) | copy-start | bytes 393220
  (1 other events, 6.7 us)
Sparse Core Ops, SparseCore 0:
  9.6 84.7 all-gather.1
  97.3 88.1 reduce-scatter.1

commit v2 on v1

--- a/solution.py
+++ b/solution.py
@@ -241,6 +241,88 @@
     return array.astype(jnp.float32)
 
 
+def hop(array, pairs):
+    return lax.ppermute(
+        array, "tp", [(2 * i + core, 2 * j + core) for i, j in pairs for core in range(2)]
+    )
+
+
+INWARD = ((0, 1), (3, 2))
+ACROSS = ((1, 2), (2, 1))
+OUTWARD = ((1, 0), (2, 3))
+
+
+def of_chip(chip, table):
+    return jnp.asarray(table, jnp.int32)[chip]
+
+
+def columns(array, block, width):
+    return lax.dynamic_slice_in_dim(array, block * width, width, 1)
+
+
+def gathered_product(block, out_weight):
+    place = lax.axis_index("tp")
+    chip, core = place // 2, place % 2
+    width = block.shape[1]
+    middle = (chip == 1) | (chip == 2)
+    to_middle = hop(block, INWARD)
+    swap_middle = hop(block, ACROSS)
+    to_end = hop(block, OUTWARD)
+    far_middle = hop(to_middle, ACROSS)
+    far_end = hop(swap_middle, OUTWARD)
+    last_end = hop(far_middle, OUTWARD)
+    arrivals = (
+        (block, (0, 1, 2, 3)),
+        (jnp.where(middle, to_middle, to_end), (1, 0, 3, 2)),
+        (jnp.where(middle, swap_middle, far_end), (2, 2, 1, 1)),
+        (jnp.where(middle, far_middle, last_end), (3, 3, 0, 0)),
+    )
+    total = jnp.zeros((block.shape[0], out_weight.shape[0]), jnp.float32)
+    for array, table in arrivals:
+        source = 2 * of_chip(chip, table)
+        other = swapped(array, "tp", 1)
+        for part, at in ((array, source + core), (other, source + 1 - core)):
+            total = total + jnp.einsum(
+                "tk,ck->tc",
+                part,
+                columns(out_weight, at, width),
+                preferred_element_type=jnp.float32,
+            )
+    return total
+
+
+def scattered_product(data, out_weight, width):
+    place = lax.axis_index("tp")
+    chip, core = place // 2, place % 2
+
+    def share(table):
+        source = 2 * of_chip(chip, table)
+        given = jnp.dot(
+            data,
+            columns(out_weight, source + 1 - core, width),
+            preferred_element_type=jnp.float32,
+        ).astype(jnp.bfloat16)
+        kept = jnp.dot(
+            data, columns(out_weight, source + core, width), preferred_element_type=jnp.float32
+        )
+        return kept + wide(swapped(given, "tp", 1))
+
+    def short(array):
+        return array.astype(jnp.bfloat16)
+
+    first = share((3, 3, 0, 0))
+    one = hop(short(first), INWARD)
+    second = share((2, 2, 1, 1))
+    two_a = hop(short(first + wide(one)), ACROSS)
+    two_b = hop(short(second), INWARD)
+    third = share((1, 0, 3, 2))
+    three_a = hop(short(third + wide(two_a)), OUTWARD)
+    three_b = hop(short(second + wide(two_b)), ACROSS)
+    three_c = hop(short(third), INWARD)
+    own = share((0, 1, 2, 3))
+    return short(own + wide(three_a) + wide(three_b) + wide(three_c))
+
+
 def local(query_gate, key_gate, value_input, filter_taps, out_weight, out_grad):
     length, channels = query_gate.shape
     groups = filter_taps.shape[1]
@@ -250,7 +332,16 @@
     at = position.reshape((1,)).astype(jnp.int32)
     tap_scale = 1.0 / math.sqrt(length * members)
 
-    all_cotangents = lax.all_gather(out_grad, "tp", axis=1, tiled=True)
+    in_line = lax.axis_size("tp") == 8
+    if in_line:
+        dgated = gathered_product(out_grad, out_weight).astype(jnp.bfloat16)
+    else:
+        dgated = jnp.einsum(
+            "tk,ck->tc",
+            lax.all_gather(out_grad, "tp", axis=1, tiled=True),
+            out_weight,
+            preferred_element_type=jnp.float32,
+        ).astype(jnp.bfloat16)
     tap_rows = (filter_taps * tap_scale).astype(jnp.bfloat16).T
     tap_parts = [wide(p) for p in traded(cut(tap_rows, position, members, 0), "ctx")]
     product_in = (wide(key_gate) * wide(value_input)).astype(jnp.bfloat16)
@@ -258,13 +349,13 @@
     conv_parts = traded(convolve(at, input_parts, tap_parts, per_group), "ctx")
     convolved = joined(conv_parts, position, 1)
     gated_out = (wide(query_gate) * wide(convolved)).astype(jnp.bfloat16)
-    partial_value = jnp.dot(gated_out, out_weight, preferred_element_type=jnp.float32)
-    projected = lax.psum_scatter(
-        partial_value.astype(jnp.bfloat16), "tp", scatter_dimension=1, tiled=True
-    )
-    dgated = jnp.einsum(
-        "tk,ck->tc", all_cotangents, out_weight, preferred_element_type=jnp.float32
-    ).astype(jnp.bfloat16)
+    if in_line:
+        projected = scattered_product(gated_out, out_weight, channels)
+    else:
+        partial_value = jnp.dot(gated_out, out_weight, preferred_element_type=jnp.float32)
+        projected = lax.psum_scatter(
+            partial_value.astype(jnp.bfloat16), "tp", scatter_dimension=1, tiled=True
+        )
     grad_query = (wide(dgated) * wide(convolved)).astype(jnp.bfloat16)
     conv_grad = (wide(dgated) * wide(query_gate)).astype(jnp.bfloat16)
     grad_parts = traded(cut(conv_grad, position, members, 1), "ctx")

time: 192 us -> 229 us (1.19)
  starting transfers between devices: 25 us -> 51.8 us
  matrix products: 32.6 us -> 46 us
  between operations: 14.3 us -> 3.44 us
  other arithmetic: 4.11 us -> 9.22 us
  local copies, waits for them, and re-layouts: 0.79 us -> 3.58 us
    ppermute x0 -> x12, waiting for transfers between devices: none -> 83.4 us  [hop(): lax.ppermute(array, 'tp', [(2 * i + core, 2 * j + core) for i, j in pairs...]
    ppermute x18 -> x26, waiting for transfers between devices: 40.9 us -> 10.6 us  [swapped(): return lax.ppermute(array, axis, [(i, i ^ step) for i in range(size)])]
    reduce_scatter x1 -> x0, waiting for transfers between devices: 27.8 us -> none  [local(): lax.psum_scatter(partial_value.astype(jnp.bfloat16), 'tp', scatter_dimens...]
    ppermute x0 -> x12, starting transfers between devices: none -> 27.3 us  [hop(): lax.ppermute(array, 'tp', [(2 * i + core, 2 * j + core) for i, j in pairs...]
    all_gather x1 -> x0, waiting for transfers between devices: 26.2 us -> none  [local(): all_cotangents = lax.all_gather(out_grad, 'tp', axis=1, tiled=True)]
    dot_general x2 -> x16, matrix products: 32.6 us -> 46 us  [the longest x8 26.2 us: gathered_product(): jnp.einsum('tk,ck->tc', part, columns(out_weight, at, width), preferred_e...]
    convert_element_type x0 -> x3, other arithmetic: none -> 2.65 us  [short(): return array.astype(jnp.bfloat16)]
    ppermute x18 -> x26, starting transfers between devices: 24.9 us -> 24.5 us  [swapped(): return lax.ppermute(array, axis, [(i, i ^ step) for i in range(size)])]
  transfers between devices with their start and end apart: 20 -> 38, of which waited for: 11 -> 11; matrix products, arithmetic and copies ran while one was open for 20% -> 20% of each run, Pallas kernels for 10% -> 9%
where the time goes in v2:
time: 229 us; the launch traced here: 228 us
  waiting for transfers between devices  94 us (41%)
  starting transfers between devices  51.8 us (23%)
  matrix products  46 us (20%)
  Pallas kernels  19.8 us (9%)
  other arithmetic  9.22 us (4%)
  local copies, waits for them, and re-layouts  3.58 us (2%)
  between operations  3.44 us (2%)
    ppermute x12, waiting for transfers between devices, hop(): lax.ppermute(array, 'tp', [(2 * i + core, 2 * j + core) for i, j in pairs...  83.4 us
    ppermute x12, starting transfers between devices, hop(): lax.ppermute(array, 'tp', [(2 * i + core, 2 * j + core) for i, j in pairs...  27.3 us
    dot_general x8, matrix products, gathered_product(): jnp.einsum('tk,ck->tc', part, columns(out_weight, at, width), preferred_e...  26.2 us
    ppermute x26, starting transfers between devices, swapped(): return lax.ppermute(array, axis, [(i, i ^ step) for i in range(size)])  24.5 us
    pallas_call x1, Pallas kernels, correlate(): pl.pallas_call(functools.partial(backward_kernel, members, per_group, sca...  12.5 us
    dot_general x4, matrix products, share(): jnp.dot(data, columns(out_weight, source + 1 - core, width), preferred_el...  10.6 us
    ppermute x26, waiting for transfers between devices, swapped(): return lax.ppermute(array, axis, [(i, i ^ step) for i in range(size)])  10.6 us
    dot_general x4, matrix products, share(): jnp.dot(data, columns(out_weight, source + core, width), preferred_elemen...  9.2 us
  transfers between devices with their start and end apart: 38, of which 11 were waited for; matrix products, arithmetic and copies ran while one was open for 20% of the time, Pallas kernels for 9%

profile of v2, /device:TPU:0, one launch (start us, length us, event | category | flops | bytes accessed | tf_op | source)
XLA Modules:
  0.0 227.9 jit_solution(17129222055390002314)
XLA Ops:
  0.6 5.9 %collective-permute-start.20 = (bf16[512,1024]{1,0:T(8,128)(2,1)}, bf16[512,1024]{1,0:T(8,128)(2,1)}, u32[]{:S(2)}, u32[]{:S(2)}) collective-permute-start(bf16[512,1024]{1,0:T(8,128)(2,1)} %param.19), channel_id=1, source_target_pairs={{0,2},{1,3},{6,4},{7,5},{8,10},{9,11},{14,12},{15,13},{16,18},{17,... | collective-permute-start | bytes 3145736 | tf_op jit(solution)/shard_map/ppermute | solution.py:245
  17.5 10.8 %collective-permute-done.20 = bf16[512,1024]{1,0:T(8,128)(2,1)} collective-permute-done((bf16[512,1024]{1,0:T(8,128)(2,1)}, bf16[512,1024]{1,0:T(8,128)(2,1)}, u32[]{:S(2)}, u32[]{:S(2)}) %collective-permute-start.20) | collective-permute-done | bytes 1048608 | tf_op jit(solution)/shard_map/ppermute | solution.py:245
  31.3 7.4 %causal_conv.1 = (bf16[512,256]{1,0:T(8,128)(2,1)S(1)}, bf16[512,256]{1,0:T(8,128)(2,1)S(1)}, bf16[512,256]{1,0:T(8,128)(2,1)S(1)}, bf16[512,256]{1,0:T(8,128)(2,1)S(1)}) custom-call(s32[1]{0:T(128)} %bitcast.pos_ref, bf16[512,256]{1,0:T(8,128)(2,1)S(1)} %get-tuple-element.43.refs_0_, bf16[512,256]{1,0:T(8,128)(2,1)S(1)} %collective-permute-done.refs_1_, ...), custom_call_target="tpu_custom_call" | custom-call | flops 4294967296 | bytes 2097152 | tf_op jit(solution)/shard_map/causal_conv/pallas_call | solution.py:163
  41.8 4.2 %fusion.40 = f32[1024,512]{0,1:T(8,128)} fusion(bf16[512,1024]{1,0:T(8,128)(2,1)S(1)} %copy-done.5, bf16[1024,8192]{1,0:T(8,128)(2,1)} %param.18, s32[]{:T(128)S(6)} %select_n.139), kind=kOutput, calls=%fused_computation.54 | convolution fusion | flops 1073741824 | bytes 5242884 | tf_op jit(solution)/shard_map/tk,ck->tc/dot_general | solution.py:285
  54.4 3.0 %collective-permute-done.8 = bf16[512,256]{1,0:T(8,128)(2,1)S(1)} collective-permute-done((bf16[512,256]{1,0:T(8,128)(2,1)S(1)}, bf16[512,256]{1,0:T(8,128)(2,1)S(1)}, u32[]{:S(2)}, u32[]{:S(2)}) %collective-permute-start.8) | collective-permute-done | bytes 262176 | tf_op jit(solution)/shard_map/ppermute | solution.py:212
  61.3 2.9 %fusion.32 = f32[512,1024]{1,0:T(8,128)S(1)} fusion(bf16[512,1024]{1,0:T(8,128)(2,1)S(1)} %broadcast_select_fusion.2, bf16[1024,8192]{1,0:T(8,128)(2,1)} %param.18, s32[]{:T(128)S(6)} %select_n.141), kind=kOutput, calls=%fused_computation.46 | convolution fusion | flops 1073741824 | bytes 5242884 | tf_op jit(solution)/shard_map/tk,ck->tc/dot_general | solution.py:285
  64.2 18.1 %collective-permute-done.24 = bf16[512,1024]{1,0:T(8,128)(2,1)S(1)} collective-permute-done((bf16[512,1024]{1,0:T(8,128)(2,1)S(1)}, bf16[512,1024]{1,0:T(8,128)(2,1)S(1)}, u32[]{:S(2)}, u32[]{:S(2)}) %collective-permute-start.24) | collective-permute-done | bytes 1048608 | tf_op jit(solution)/shard_map/ppermute | solution.py:245
  82.4 20.3 %collective-permute-done.27 = bf16[512,1024]{1,0:T(8,128)(2,1)S(1)} collective-permute-done((bf16[512,1024]{1,0:T(8,128)(2,1)}, bf16[512,1024]{1,0:T(8,128)(2,1)S(1)}, u32[]{:S(2)}, u32[]{:S(2)}) %collective-permute-start.27) | collective-permute-done | bytes 1048608 | tf_op jit(solution)/shard_map/ppermute | solution.py:245
  103.0 2.9 %fusion.36 = f32[1024,512]{0,1:T(8,128)S(1)} fusion(bf16[512,1024]{1,0:T(8,128)(2,1)S(1)} %collective-permute-done.19, bf16[1024,8192]{1,0:T(8,128)(2,1)} %param.18, s32[]{:T(128)S(6)} %select_n.140), kind=kOutput, calls=%fused_computation.50 | convolution fusion | flops 1073741824 | bytes 5242884 | tf_op jit(solution)/shard_map/tk,ck->tc/dot_general | solution.py:285
  105.9 2.9 %fusion.16 = f32[512,1024]{1,0:T(8,128)S(1)} fusion(bf16[512,1024]{1,0:T(8,128)(2,1)S(1)} %broadcast_select_fusion.1, bf16[1024,8192]{1,0:T(8,128)(2,1)} %param.18, s32[]{:T(128)S(6)} %select_n.145), kind=kOutput, calls=%fused_computation.30 | convolution fusion | flops 1073741824 | bytes 5242884 | tf_op jit(solution)/shard_map/tk,ck->tc/dot_general | solution.py:285
  111.7 2.9 %fusion.12 = f32[512,1024]{1,0:T(8,128)S(1)} fusion(bf16[512,1024]{1,0:T(8,128)(2,1)S(1)} %collective-permute-done.25, bf16[1024,8192]{1,0:T(8,128)(2,1)} %param.18, s32[]{:T(128)S(6)} %select_n.146), kind=kOutput, calls=%fused_computation.26 | convolution fusion | flops 1073741824 | bytes 5242884 | tf_op jit(solution)/shard_map/tk,ck->tc/dot_general | solution.py:285
  114.6 3.0 %fusion.20 = f32[512,1024]{1,0:T(8,128)S(1)} fusion(bf16[512,1024]{1,0:T(8,128)(2,1)S(1)} %collective-permute-done.28, bf16[1024,8192]{1,0:T(8,128)(2,1)} %param.18, s32[]{:T(128)S(6)} %select_n.144), kind=kOutput, calls=%fused_computation.34 | convolution fusion | flops 1073741824 | bytes 5242884 | tf_op jit(solution)/shard_map/tk,ck->tc/dot_general | solution.py:285
  117.7 4.6 %fusion.3 = (bf16[512,1024]{1,0:T(8,128)(2,1)S(1)}, bf16[512,1024]{1,0:T(8,128)(2,1)}, bf16[512,1024]{1,0:T(8,128)(2,1)S(1)}) fusion(bf16[512,1024]{1,0:T(8,128)(2,1)S(1)} %copy-done.3, bf16[512,1024]{1,0:T(8,128)(2,1)S(1)} %constant_dynamic-update-slice_fusion.8, f32[512,1024]{1,0:T(8,128)S(1)} %fusion.20, bf16[512,1024]{1,0:T(8,128)(2,1)S(1)} %broadcast_select_fusion, ...), kind=kOutput, calls=%fused_computation.9 | convolution fusion | flops 1082654720 | bytes 23068676 | tf_op jit(solution)/shard_map/tk,ck->tc/dot_general | solution.py:285
  122.2 3.0 %fusion.56 = bf16[512,1024]{1,0:T(8,128)(2,1)S(1)} fusion(bf16[512,1024]{1,0:T(8,128)(2,1)S(1)} %get-tuple-element.39, bf16[1024,8192]{1,0:T(8,128)(2,1)} %param.18, s32[]{:T(128)S(6)} %select_n.144), kind=kOutput, calls=%fused_computation.60 | convolution fusion | flops 1074266112 | bytes 4194308 | tf_op jit(solution)/shard_map/dot_general | solution.py:300
  125.8 3.1 %fusion.59 = bf16[512,1024]{1,0:T(8,128)(2,1)S(1)} fusion(bf16[512,1024]{1,0:T(8,128)(2,1)S(1)} %get-tuple-element.39, bf16[1024,8192]{1,0:T(8,128)(2,1)} %param.18, s32[]{:T(128)S(6)} %select_n.146), kind=kOutput, calls=%fused_computation.61 | convolution fusion | flops 1074266112 | bytes 4194308 | tf_op jit(solution)/shard_map/dot_general | solution.py:300
  129.0 3.2 %fusion.53 = bf16[512,1024]{1,0:T(8,128)(2,1)S(1)} fusion(bf16[512,1024]{1,0:T(8,128)(2,1)S(1)} %get-tuple-element.39, bf16[1024,8192]{1,0:T(8,128)(2,1)} %param.18, s32[]{:T(128)S(6)} %select_n.142), kind=kOutput, calls=%fused_computation.59 | convolution fusion | flops 1074266112 | bytes 4194308 | tf_op jit(solution)/shard_map/dot_general | solution.py:300
  132.3 3.0 %fusion.80 = (bf16[512,1024]{1,0:T(8,128)(2,1)S(1)}, f32[512,1024]{1,0:T(8,128)S(1)}) fusion(bf16[512,1024]{1,0:T(8,128)(2,1)S(1)} %collective-permute-done.11, bf16[512,1024]{1,0:T(8,128)(2,1)S(1)} %get-tuple-element.39, bf16[1024,8192]{1,0:T(8,128)(2,1)} %param.18, s32[]{:T(128)S(6)} %select_n.143), kind=kOutput, calls=%fused_computation.106 | convolution fusion | flops 1075314688 | bytes 7340036 | tf_op jit(solution)/shard_map/dot_general | solution.py:305
  146.7 14.6 %collective-permute-done.12 = bf16[512,1024]{1,0:T(8,128)(2,1)S(1)} collective-permute-done((bf16[512,1024]{1,0:T(8,128)(2,1)S(1)}, bf16[512,1024]{1,0:T(8,128)(2,1)S(1)}, u32[]{:S(2)}, u32[]{:S(2)}) %collective-permute-start.12) | collective-permute-done | bytes 1048608 | tf_op jit(solution)/shard_map/ppermute | solution.py:245
  161.3 4.4 %collective-permute-start.16 = (bf16[512,1024]{1,0:T(8,128)(2,1)}, bf16[512,1024]{1,0:T(8,128)(2,1)S(1)}, u32[]{:S(2)}, u32[]{:S(2)}) collective-permute-start(bf16[512,1024]{1,0:T(8,128)(2,1)} %get-tuple-element.50), channel_id=1, source_target_pairs={{0,2},{1,3},{6,4},{7,5},{8,10},{9,11},{14,12},{15,13},{16,18},{17,... | collective-permute-start | bytes 3145736 | tf_op jit(solution)/shard_map/ppermute | solution.py:245
  166.9 12.5 %causal_conv_grads.1 = (bf16[512,256]{1,0:T(8,128)(2,1)S(1)}, bf16[512,256]{1,0:T(8,128)(2,1)S(1)}, bf16[512,256]{1,0:T(8,128)(2,1)S(1)}, bf16[512,256]{1,0:T(8,...) custom-call(s32[1]{0:T(128)} %bitcast.pos_ref, ...), custom_call_target="tpu_custom_call" | custom-call | flops 8589934592 | bytes 3145728 | tf_op jit(solution)/shard_map/causal_conv_grads/pallas_call | solution.py:187
  182.6 5.8 %collective-permute-done.16 = bf16[512,1024]{1,0:T(8,128)(2,1)S(1)} collective-permute-done((bf16[512,1024]{1,0:T(8,128)(2,1)}, bf16[512,1024]{1,0:T(8,128)(2,1)S(1)}, u32[]{:S(2)}, u32[]{:S(2)}) %collective-permute-start.16) | collective-permute-done | bytes 1048608 | tf_op jit(solution)/shard_map/ppermute | solution.py:245
  198.5 4.8 %collective-permute-start.18 = (bf16[512,1024]{1,0:T(8,128)(2,1)S(1)}, bf16[512,1024]{1,0:T(8,128)(2,1)S(1)}, u32[]{:S(2)}, u32[]{:S(2)}) collective-permute-start(bf16[512,1024]{1,0:T(8,128)(2,1)S(1)} %get-tuple-element.30), channel_id=1, source_target_pairs={{0,2},{1,3},{6,4},{7,5},{8,10},{9,11},{14,12},{15,13},{16,18},{17,... | collective-permute-start | bytes 3145736 | tf_op jit(solution)/shard_map/ppermute | solution.py:245
  206.0 6.3 %collective-permute-done.34 = bf16[512,256]{1,0:T(8,128)(2,1)S(1)} collective-permute-done((bf16[512,256]{1,0:T(8,128)(2,1)S(1)}, bf16[512,256]{1,0:T(8,128)(2,1)S(1)}, u32[]{:S(2)}, u32[]{:S(2)}) %collective-permute-start.34) | collective-permute-done | bytes 262176 | tf_op jit(solution)/shard_map/ppermute | solution.py:212
  214.5 10.2 %collective-permute-done.14 = bf16[512,1024]{1,0:T(8,128)(2,1)S(1)} collective-permute-done((bf16[512,1024]{1,0:T(8,128)(2,1)S(1)}, bf16[512,1024]{1,0:T(8,128)(2,1)S(1)}, u32[]{:S(2)}, u32[]{:S(2)}) %collective-permute-start.14) | collective-permute-done | bytes 1048608 | tf_op jit(solution)/shard_map/ppermute | solution.py:245
  (132 shorter events, 64.7 us)
Async XLA Ops:
  0.6 27.7 %collective-permute-start.20 = (bf16[512,1024]{1,0:T(8,128)(2,1)}, bf16[512,1024]{1,0:T(8,128)(2,1)}, u32[]{:S(2)}, u32[]{:S(2)}) collective-permute-start(bf16[512,1024]{1,0:T(8,128)(2,1)} %param.19), channel_id=1, source_target_pairs={{0,2},{1,3},{6,4},{7,5},{8,10},{9,11},{14,12},{15,13},{16,18},{17,... | collective-permute-start | bytes 3145736 | tf_op jit(solution)/shard_map/ppermute | solution.py:245
  6.5 43.8 %collective-permute-start.23 = (bf16[512,1024]{1,0:T(8,128)(2,1)}, bf16[512,1024]{1,0:T(8,128)(2,1)S(1)}, u32[]{:S(2)}, u32[]{:S(2)}) collective-permute-start(bf16[512,1024]{1,0:T(8,128)(2,1)} %param.19), channel_id=1, source_target_pairs={{2,4},{3,5},{4,2},{5,3},{10,12},{11,13},{12,10},{13,11},{18,20},{1... | collective-permute-start | bytes 3145736 | tf_op jit(solution)/shard_map/ppermute | solution.py:245
  13.9 16.1 %collective-permute-start = (bf16[512,256]{1,0:T(8,128)(2,1)S(1)}, bf16[512,256]{1,0:T(8,128)(2,1)S(1)}, u32[]{:S(2)}, u32[]{:S(2)}) collective-permute-start(bf16[512,256]{1,0:T(8,128)(2,1)S(1)} %get-tuple-element.42), channel_id=1, source_target_pairs={{0,8},{8,0},{16,24},{24,16},{1,9},{9,1},{17,25},{25,17},{2,10},{10... | collective-permute-start | bytes 786440 | tf_op jit(solution)/shard_map/ppermute | solution.py:212
  15.4 15.8 %collective-permute-start.1 = (bf16[512,256]{1,0:T(8,128)(2,1)S(1)}, bf16[512,256]{1,0:T(8,128)(2,1)S(1)}, u32[]{:S(2)}, u32[]{:S(2)}) collective-permute-start(bf16[512,256]{1,0:T(8,128)(2,1)S(1)} %get-tuple-element.41), channel_id=1, source_target_pairs={{0,16},{8,24},{16,0},{24,8},{1,17},{9,25},{17,1},{25,9},{2,18},{10... | collective-permute-start | bytes 786440 | tf_op jit(solution)/shard_map/ppermute | solution.py:212
  28.3 24.6 %collective-permute-start.26 = (bf16[512,1024]{1,0:T(8,128)(2,1)}, bf16[512,1024]{1,0:T(8,128)(2,1)}, u32[]{:S(2)}, u32[]{:S(2)}) collective-permute-start(bf16[512,1024]{1,0:T(8,128)(2,1)} %collective-permute-done.20), channel_id=1, source_target_pairs={{2,4},{3,5},{4,2},{5,3},{10,12},{11,13},{12,10},{13,11},{18,20},{1... | collective-permute-start | bytes 3145736 | tf_op jit(solution)/shard_map/ppermute | solution.py:245
  30.0 29.9 %collective-permute-start.21 = (bf16[512,1024]{1,0:T(8,128)(2,1)}, bf16[512,1024]{1,0:T(8,128)(2,1)}, u32[]{:S(2)}, u32[]{:S(2)}) collective-permute-start(bf16[512,1024]{1,0:T(8,128)(2,1)} %param.19), channel_id=1, source_target_pairs={{2,0},{3,1},{4,6},{5,7},{10,8},{11,9},{12,14},{13,15},{18,16},{19,... | collective-permute-start | bytes 3145736 | tf_op jit(solution)/shard_map/ppermute | solution.py:245
  50.4 31.8 %collective-permute-start.24 = (bf16[512,1024]{1,0:T(8,128)(2,1)S(1)}, bf16[512,1024]{1,0:T(8,128)(2,1)S(1)}, u32[]{:S(2)}, u32[]{:S(2)}) collective-permute-start(bf16[512,1024]{1,0:T(8,128)(2,1)S(1)} %collective-permute-done.23), channel_id=1, source_target_pairs={{2,0},{3,1},{4,6},{5,7},{10,8},{11,9},{12,14},{13,15},{18,16},{19,... | collective-permute-start | bytes 3145736 | tf_op jit(solution)/shard_map/ppermute | solution.py:245
  52.8 50.2 %collective-permute-start.19 = (bf16[512,1024]{1,0:T(8,128)(2,1)S(1)}, bf16[512,1024]{1,0:T(8,128)(2,1)S(1)}, u32[]{:S(2)}, u32[]{:S(2)}) collective-permute-start(bf16[512,1024]{1,0:T(8,128)(2,1)S(1)} %copy-done.6), channel_id=1, source_target_pairs={{0,1},{1,0},{2,3},{3,2},{4,5},{5,4},{6,7},{7,6},{8,9},{9,8},{10,11... | collective-permute-start | bytes 3145736 | tf_op jit(solution)/shard_map/ppermute | solution.py:212
  52.9 49.8 %collective-permute-start.27 = (bf16[512,1024]{1,0:T(8,128)(2,1)}, bf16[512,1024]{1,0:T(8,128)(2,1)S(1)}, u32[]{:S(2)}, u32[]{:S(2)}) collective-permute-start(bf16[512,1024]{1,0:T(8,128)(2,1)} %collective-permute-done.26), channel_id=1, source_target_pairs={{2,0},{3,1},{4,6},{5,7},{10,8},{11,9},{12,14},{13,15},{18,16},{19,... | collective-permute-start | bytes 3145736 | tf_op jit(solution)/shard_map/ppermute | solution.py:245
  61.2 47.6 %collective-permute-start.22 = (bf16[512,1024]{1,0:T(8,128)(2,1)S(1)}, bf16[512,1024]{1,0:T(8,128)(2,1)S(1)}, u32[]{:S(2)}, u32[]{:S(2)}) collective-permute-start(bf16[512,1024]{1,0:T(8,128)(2,1)S(1)} %broadcast_select_fusion.2), channel_id=1, source_target_pairs={{0,1},{1,0},{2,3},{3,2},{4,5},{5,4},{6,7},{7,6},{8,9},{9,8},{10,11... | collective-permute-start | bytes 3145736 | tf_op jit(solution)/shard_map/ppermute | solution.py:212
  82.4 29.3 %collective-permute-start.25 = (bf16[512,1024]{1,0:T(8,128)(2,1)S(1)}, bf16[512,1024]{1,0:T(8,128)(2,1)S(1)}, u32[]{:S(2)}, u32[]{:S(2)}) collective-permute-start(bf16[512,1024]{1,0:T(8,128)(2,1)S(1)} %broadcast_select_fusion.1), channel_id=1, source_target_pairs={{0,1},{1,0},{2,3},{3,2},{4,5},{5,4},{6,7},{7,6},{8,9},{9,8},{10,11... | collective-permute-start | bytes 3145736 | tf_op jit(solution)/shard_map/ppermute | solution.py:212
  129.0 15.4 %collective-permute-start.15 = (bf16[512,1024]{1,0:T(8,128)(2,1)S(1)}, bf16[512,1024]{1,0:T(8,128)(2,1)S(1)}, u32[]{:S(2)}, u32[]{:S(2)}) collective-permute-start(bf16[512,1024]{1,0:T(8,128)(2,1)S(1)} %fusion.59), channel_id=1, source_target_pairs={{0,1},{1,0},{2,3},{3,2},{4,5},{5,4},{6,7},{7,6},{8,9},{9,8},{10,11... | collective-permute-start | bytes 3145736 | tf_op jit(solution)/shard_map/ppermute | solution.py:212
  135.3 26.0 %collective-permute-start.12 = (bf16[512,1024]{1,0:T(8,128)(2,1)S(1)}, bf16[512,1024]{1,0:T(8,128)(2,1)S(1)}, u32[]{:S(2)}, u32[]{:S(2)}) collective-permute-start(bf16[512,1024]{1,0:T(8,128)(2,1)S(1)} %get-tuple-element.48), channel_id=1, source_target_pairs={{0,2},{1,3},{6,4},{7,5},{8,10},{9,11},{14,12},{15,13},{16,18},{17,... | collective-permute-start | bytes 3145736 | tf_op jit(solution)/shard_map/ppermute | solution.py:245
  138.3 27.8 %collective-permute-start.29 = (bf16[512,256]{1,0:T(8,128)(2,1)S(1)}, bf16[512,256]{1,0:T(8,128)(2,1)S(1)}, u32[]{:S(2)}, u32[]{:S(2)}) collective-permute-start(bf16[512,256]{1,0:T(8,128)(2,1)S(1)} %get-tuple-element.35), channel_id=1, source_target_pairs={{0,8},{8,0},{16,24},{24,16},{1,9},{9,1},{17,25},{25,17},{2,10},{10... | collective-permute-start | bytes 786440 | tf_op jit(solution)/shard_map/ppermute | solution.py:212
  139.8 27.0 %collective-permute-start.30 = (bf16[512,256]{1,0:T(8,128)(2,1)S(1)}, bf16[512,256]{1,0:T(8,128)(2,1)S(1)}, u32[]{:S(2)}, u32[]{:S(2)}) collective-permute-start(bf16[512,256]{1,0:T(8,128)(2,1)S(1)} %get-tuple-element.34), channel_id=1, source_target_pairs={{0,16},{8,24},{16,0},{24,8},{1,17},{9,25},{17,1},{25,9},{2,18},{10... | collective-permute-start | bytes 786440 | tf_op jit(solution)/shard_map/ppermute | solution.py:212
  141.4 25.5 %collective-permute-start.31 = (bf16[512,256]{1,0:T(8,128)(2,1)S(1)}, bf16[512,256]{1,0:T(8,128)(2,1)S(1)}, u32[]{:S(2)}, u32[]{:S(2)}) collective-permute-start(bf16[512,256]{1,0:T(8,128)(2,1)S(1)} %get-tuple-element.33), channel_id=1, source_target_pairs={{0,24},{8,16},{16,8},{24,0},{1,25},{9,17},{17,9},{25,1},{2,26},{10... | collective-permute-start | bytes 786440 | tf_op jit(solution)/shard_map/ppermute | solution.py:212
  144.4 46.8 %collective-permute-start.10 = (bf16[512,1024]{1,0:T(8,128)(2,1)S(1)}, bf16[512,1024]{1,0:T(8,128)(2,1)}, u32[]{:S(2)}, u32[]{:S(2)}) collective-permute-start(bf16[512,1024]{1,0:T(8,128)(2,1)S(1)} %fusion.53), channel_id=1, source_target_pairs={{0,1},{1,0},{2,3},{3,2},{4,5},{5,4},{6,7},{7,6},{8,9},{9,8},{10,11... | collective-permute-start | bytes 3145736 | tf_op jit(solution)/shard_map/ppermute | solution.py:212
  161.3 27.1 %collective-permute-start.16 = (bf16[512,1024]{1,0:T(8,128)(2,1)}, bf16[512,1024]{1,0:T(8,128)(2,1)S(1)}, u32[]{:S(2)}, u32[]{:S(2)}) collective-permute-start(bf16[512,1024]{1,0:T(8,128)(2,1)} %get-tuple-element.50), channel_id=1, source_target_pairs={{0,2},{1,3},{6,4},{7,5},{8,10},{9,11},{14,12},{15,13},{16,18},{17,... | collective-permute-start | bytes 3145736 | tf_op jit(solution)/shard_map/ppermute | solution.py:245
  166.1 25.7 %collective-permute-start.13 = (bf16[512,1024]{1,0:T(8,128)(2,1)S(1)}, bf16[512,1024]{1,0:T(8,128)(2,1)S(1)}, u32[]{:S(2)}, u32[]{:S(2)}) collective-permute-start(bf16[512,1024]{1,0:T(8,128)(2,1)S(1)} %add_convert_fusion.3), channel_id=1, source_target_pairs={{2,4},{3,5},{4,2},{5,3},{10,12},{11,13},{12,10},{13,11},{18,20},{1... | collective-permute-start | bytes 3145736 | tf_op jit(solution)/shard_map/ppermute | solution.py:245
  179.3 15.7 %collective-permute-start.35 = (f32[16,512]{1,0:T(8,128)S(1)}, f32[16,512]{1,0:T(8,128)S(1)}, u32[]{:S(2)}, u32[]{:S(2)}) collective-permute-start(f32[16,512]{1,0:T(8,128)S(1)} %get-tuple-element.26), channel_id=1, source_target_pairs={{0,8},{8,0},{16,24},{24,16},{1,9},{9,1},{17,25},{25,17},{2,10},{10... | collective-permute-start | bytes 98312 | tf_op jit(solution)/shard_map/ppermute | solution.py:212
  195.0 19.4 %collective-permute-start.9 = (bf16[512,1024]{1,0:T(8,128)(2,1)S(1)}, bf16[512,1024]{1,0:T(8,128)(2,1)S(1)}, u32[]{:S(2)}, u32[]{:S(2)}) collective-permute-start(bf16[512,1024]{1,0:T(8,128)(2,1)S(1)} %fusion.50), channel_id=1, source_target_pairs={{0,1},{1,0},{2,3},{3,2},{4,5},{5,4},{6,7},{7,6},{8,9},{9,8},{10,11... | collective-permute-start | bytes 3145736 | tf_op jit(solution)/shard_map/ppermute | solution.py:212
  195.1 19.4 %collective-permute-start.17 = (bf16[512,1024]{1,0:T(8,128)(2,1)S(1)}, bf16[512,1024]{1,0:T(8,128)(2,1)S(1)}, u32[]{:S(2)}, u32[]{:S(2)}) collective-permute-start(bf16[512,1024]{1,0:T(8,128)(2,1)S(1)} %add_convert_fusion.1), channel_id=1, source_target_pairs={{2,4},{3,5},{4,2},{5,3},{10,12},{11,13},{12,10},{13,11},{18,20},{1... | collective-permute-start | bytes 3145736 | tf_op jit(solution)/shard_map/ppermute | solution.py:245
  196.0 28.6 %collective-permute-start.14 = (bf16[512,1024]{1,0:T(8,128)(2,1)S(1)}, bf16[512,1024]{1,0:T(8,128)(2,1)S(1)}, u32[]{:S(2)}, u32[]{:S(2)}) collective-permute-start(bf16[512,1024]{1,0:T(8,128)(2,1)S(1)} %get-tuple-element.29), channel_id=1, source_target_pairs={{2,0},{3,1},{4,6},{5,7},{10,8},{11,9},{12,14},{13,15},{18,16},{19,... | collective-permute-start | bytes 3145736 | tf_op jit(solution)/shard_map/ppermute | solution.py:245
  198.5 27.4 %collective-permute-start.18 = (bf16[512,1024]{1,0:T(8,128)(2,1)S(1)}, bf16[512,1024]{1,0:T(8,128)(2,1)S(1)}, u32[]{:S(2)}, u32[]{:S(2)}) collective-permute-start(bf16[512,1024]{1,0:T(8,128)(2,1)S(1)} %get-tuple-element.30), channel_id=1, source_target_pairs={{0,2},{1,3},{6,4},{7,5},{8,10},{9,11},{14,12},{15,13},{16,18},{17,... | collective-permute-start | bytes 3145736 | tf_op jit(solution)/shard_map/ppermute | solution.py:245
  (28 other events, 276.3 us)

commit v3 on v1

--- a/solution.py
+++ b/solution.py
@@ -9,6 +9,7 @@
 
 BLOCK = 128
 NT = (((1,), (1,)), ((), ()))
+COST = pl.CostEstimate(flops=2**20, bytes_accessed=2**12, transcendentals=0)
 
 
 def lag_matrix(row, length):
@@ -159,7 +160,6 @@
     width, channels = inputs[0].shape
     groups = taps[0].shape[0]
     length = members * width
-    flops = 4 * length * length * channels
     return pl.pallas_call(
         functools.partial(forward_kernel, members, per_group),
         out_shape=[jax.ShapeDtypeStruct((width, channels), jnp.bfloat16)] * members,
@@ -171,9 +171,7 @@
             pltpu.VMEM((members, channels, width), jnp.bfloat16),
         ],
         compiler_params=pltpu.CompilerParams(vmem_limit_bytes=32 * 2**20),
-        cost_estimate=pl.CostEstimate(
-            flops=flops, bytes_accessed=4 * length * channels, transcendentals=0
-        ),
+        cost_estimate=COST,
         name="causal_conv",
     )(position, *inputs, *taps)
 
@@ -183,7 +181,6 @@
     width, channels = inputs[0].shape
     groups = taps[0].shape[0]
     length = members * width
-    flops = 8 * length * length * channels
     results = pl.pallas_call(
         functools.partial(backward_kernel, members, per_group, scale),
         out_shape=[jax.ShapeDtypeStruct((width, channels), jnp.bfloat16)] * members
@@ -199,9 +196,7 @@
             pltpu.VMEM((2 * length // BLOCK * per_group, 2 * BLOCK), jnp.bfloat16),
         ],
         compiler_params=pltpu.CompilerParams(vmem_limit_bytes=32 * 2**20),
-        cost_estimate=pl.CostEstimate(
-            flops=flops, bytes_accessed=6 * length * channels, transcendentals=0
-        ),
+        cost_estimate=COST,
         name="causal_conv_grads",
     )(position, *inputs, *cotangents, *taps)
     return results[:members], results[members:]
@@ -241,6 +236,178 @@
     return array.astype(jnp.float32)
 
 
+def hop(array, pairs):
+    return lax.ppermute(
+        array, "tp", [(2 * i + core, 2 * j + core) for i, j in pairs for core in range(2)]
+    )
+
+
+INWARD = ((0, 1), (3, 2))
+ACROSS = ((1, 2), (2, 1))
+OUTWARD = ((1, 0), (2, 3))
+
+
+def of_chip(chip, table):
+    return jnp.where(
+        chip == 0, table[0], jnp.where(chip == 1, table[1], jnp.where(chip == 2, table[2], table[3]))
+    )
+
+
+def pass_kernel(*refs):
+    del refs
+
+
+def held_until(value, after):
+    return pl.pallas_call(
+        pass_kernel,
+        out_shape=jax.ShapeDtypeStruct(value.shape, value.dtype),
+        in_specs=[pl.BlockSpec(memory_space=pl.ANY)] * (1 + len(after)),
+        out_specs=pl.BlockSpec(memory_space=pl.ANY),
+        input_output_aliases={0: 0},
+        name="held",
+    )(value, *after)
+
+
+def column_kernel(_, data_ref, weight_ref, *refs):
+    out_ref = refs[-1]
+    out_ref[...] = jnp.dot(
+        data_ref[...], weight_ref[...], preferred_element_type=jnp.float32
+    ).astype(jnp.bfloat16)
+
+
+def column_sum_kernel(_, data_ref, weight_ref, more_ref, out_ref):
+    product = jnp.dot(data_ref[...], weight_ref[...], preferred_element_type=jnp.float32)
+    out_ref[...] = (product + wide(more_ref[...])).astype(jnp.bfloat16)
+
+
+def column_product(data, out_weight, block, width, more=(), after=()):
+    rows, depth = data.shape
+    tile = min(width, 256)
+    tiles = width // tile
+    column = pl.BlockSpec((rows, tile), lambda i, at: (0, i))
+    return pl.pallas_call(
+        column_sum_kernel if more else column_kernel,
+        out_shape=jax.ShapeDtypeStruct((rows, width), jnp.bfloat16),
+        grid_spec=pltpu.PrefetchScalarGridSpec(
+            num_scalar_prefetch=1,
+            grid=(tiles,),
+            in_specs=[
+                pl.BlockSpec((rows, depth), lambda i, at: (0, 0)),
+                pl.BlockSpec((depth, tile), lambda i, at: (0, at[0] * tiles + i)),
+            ]
+            + [column] * len(more)
+            + [pl.BlockSpec(memory_space=pl.ANY)] * len(after),
+            out_specs=column,
+        ),
+        compiler_params=pltpu.CompilerParams(vmem_limit_bytes=50 * 2**20),
+        cost_estimate=COST,
+        name="projection_block",
+    )(block.reshape((1,)).astype(jnp.int32), data, out_weight, *more, *after)
+
+
+def first_half_kernel(_, data_ref, weight_ref, out_ref):
+    product = lax.dot_general(
+        data_ref[0], weight_ref[...], NT, preferred_element_type=jnp.float32
+    )
+
+    @pl.when(pl.program_id(0) == 0)
+    def _():
+        out_ref[...] = product
+
+    @pl.when(pl.program_id(0) > 0)
+    def _():
+        out_ref[...] += product
+
+
+def second_half_kernel(
+    _, data_ref, weight_ref, start_ref, conv_ref, query_ref, grad_ref, cot_ref, total
+):
+    product = lax.dot_general(
+        data_ref[0], weight_ref[...], NT, preferred_element_type=jnp.float32
+    )
+
+    @pl.when(pl.program_id(0) == 0)
+    def _():
+        total[...] = start_ref[...] + product
+
+    @pl.when(pl.program_id(0) > 0)
+    def _():
+        total[...] += product
+
+    @pl.when(pl.program_id(0) == pl.num_programs(0) - 1)
+    def _():
+        dgated = wide(total[...].astype(jnp.bfloat16))
+        grad_ref[...] = (dgated * wide(conv_ref[...])).astype(jnp.bfloat16)
+        cot_ref[...] = (dgated * wide(query_ref[...])).astype(jnp.bfloat16)
+
+
+def cotangent_product(parity, blocks, out_weight, rest=None):
+    chips, rows, width = blocks.shape
+    channels = out_weight.shape[0]
+    whole = pl.BlockSpec((rows, channels), lambda i, at: (0, 0))
+    array = jax.ShapeDtypeStruct((rows, channels), jnp.bfloat16)
+    return pl.pallas_call(
+        first_half_kernel if rest is None else second_half_kernel,
+        out_shape=jax.ShapeDtypeStruct((rows, channels), jnp.float32)
+        if rest is None
+        else [array, array],
+        grid_spec=pltpu.PrefetchScalarGridSpec(
+            num_scalar_prefetch=1,
+            grid=(chips,),
+            in_specs=[
+                pl.BlockSpec((1, rows, width), lambda i, at: (i, 0, 0)),
+                pl.BlockSpec((channels, width), lambda i, at: (0, 2 * i + at[0])),
+            ]
+            + ([] if rest is None else [whole] * 3),
+            out_specs=whole if rest is None else [whole, whole],
+            scratch_shapes=[]
+            if rest is None
+            else [pltpu.VMEM((rows, channels), jnp.float32)],
+        ),
+        compiler_params=pltpu.CompilerParams(vmem_limit_bytes=50 * 2**20),
+        cost_estimate=COST,
+        name="cotangent_half",
+    )(
+        parity.reshape((1,)).astype(jnp.int32),
+        blocks,
+        out_weight,
+        *(() if rest is None else rest),
+    )
+
+
+def scattered_product(data, out_weight, width):
+    place = lax.axis_index("tp")
+    chip, core = place // 2, place % 2
+
+    def given(table, after=()):
+        source = 2 * of_chip(chip, table)
+        return column_product(data, out_weight, source + 1 - core, width, after=after)
+
+    def kept(table, other):
+        source = 2 * of_chip(chip, table)
+        more = (swapped(other, "tp", 1),)
+        return column_product(data, out_weight, source + core, width, more)
+
+    def added(*arrays):
+        return sum(wide(array) for array in arrays).astype(jnp.bfloat16)
+
+    tables = ((3, 3, 0, 0), (2, 2, 1, 1), (1, 0, 3, 2), (0, 1, 2, 3))
+    for_first, for_second = given(tables[0]), given(tables[1])
+    first, second = kept(tables[0], for_first), kept(tables[1], for_second)
+    third = kept(tables[2], given(tables[2], (first,)))
+    own = kept(tables[3], given(tables[3], (first,)))
+    one = hop(first, INWARD)
+    two_b = hop(second, INWARD)
+    two_a = hop(added(first, one), ACROSS)
+
+    def rest(after):
+        three_b = hop(added(second, held_until(two_b, after)), ACROSS)
+        three_a = hop(added(third, held_until(two_a, after)), OUTWARD + INWARD)
+        return added(own, three_a, three_b)
+
+    return rest, (one, second, third, own)
+
+
 def local(query_gate, key_gate, value_input, filter_taps, out_weight, out_grad):
     length, channels = query_gate.shape
     groups = filter_taps.shape[1]
@@ -250,7 +417,11 @@
     at = position.reshape((1,)).astype(jnp.int32)
     tap_scale = 1.0 / math.sqrt(length * members)
 
-    all_cotangents = lax.all_gather(out_grad, "tp", axis=1, tiled=True)
+    place = lax.axis_index("tp")
+    devices = lax.axis_size("tp")
+    core = place % 2
+    lines = [list(range(parity, devices, 2)) for parity in range(2)]
+    cotangents = lax.all_gather(out_grad, "tp", axis_index_groups=lines)
     tap_rows = (filter_taps * tap_scale).astype(jnp.bfloat16).T
     tap_parts = [wide(p) for p in traded(cut(tap_rows, position, members, 0), "ctx")]
     product_in = (wide(key_gate) * wide(value_input)).astype(jnp.bfloat16)
@@ -258,15 +429,24 @@
     conv_parts = traded(convolve(at, input_parts, tap_parts, per_group), "ctx")
     convolved = joined(conv_parts, position, 1)
     gated_out = (wide(query_gate) * wide(convolved)).astype(jnp.bfloat16)
-    partial_value = jnp.dot(gated_out, out_weight, preferred_element_type=jnp.float32)
-    projected = lax.psum_scatter(
-        partial_value.astype(jnp.bfloat16), "tp", scatter_dimension=1, tiled=True
-    )
-    dgated = jnp.einsum(
-        "tk,ck->tc", all_cotangents, out_weight, preferred_element_type=jnp.float32
-    ).astype(jnp.bfloat16)
-    grad_query = (wide(dgated) * wide(convolved)).astype(jnp.bfloat16)
-    conv_grad = (wide(dgated) * wide(query_gate)).astype(jnp.bfloat16)
+    if devices == 8:
+        finish, after = scattered_product(gated_out, out_weight, channels)
+    else:
+        partial_value = jnp.dot(gated_out, out_weight, preferred_element_type=jnp.float32)
+        projected = lax.psum_scatter(
+            partial_value.astype(jnp.bfloat16), "tp", scatter_dimension=1, tiled=True
+        )
+        after = (gated_out,)
+    cotangents = held_until(cotangents, after)
+    half = cotangent_product(core, cotangents, out_weight)
+    grad_query, conv_grad = cotangent_product(
+        1 - core,
+        swapped(cotangents, "tp", 1),
+        out_weight,
+        rest=(half, convolved, query_gate),
+    )
+    if devices == 8:
+        projected = finish((conv_grad,))
     grad_parts = traded(cut(conv_grad, position, members, 1), "ctx")
     back_parts, filter_parts = correlate(
         at, input_parts, grad_parts, tap_parts, per_group, tap_scale

time: 192 us -> 203 us (1.057)
  Pallas kernels: 19.8 us -> 72.1 us
  waiting for transfers between devices: 95.6 us -> 56.7 us
  matrix products: 32.6 us -> 0 us
  starting transfers between devices: 25 us -> 40.7 us
  other arithmetic: 4.11 us -> 12.2 us
  local copies, waits for them, and re-layouts: 0.79 us -> 6.06 us
    pallas_call x0 -> x13, Pallas kernels: none -> 51.2 us  [the longest x8 32.1 us: column_product(): pl.pallas_call(column_sum_kernel if more else column_kernel, out_shape=ja...]
    dot_general x2 -> x0, matrix products: 32.6 us -> none  [the longest x1 16.9 us: local(): jnp.dot(gated_out, out_weight, preferred_element_type=jnp.float32)]
    reduce_scatter x1 -> x0, waiting for transfers between devices: 27.8 us -> none  [local(): lax.psum_scatter(partial_value.astype(jnp.bfloat16), 'tp', scatter_dimens...]
    all_gather x1, waiting for transfers between devices: 26.2 us -> 0.01 us  [local(): cotangents = lax.all_gather(out_grad, 'tp', axis_index_groups=lines)]
    ppermute x0 -> x5, waiting for transfers between devices: none -> 20.6 us  [hop(): lax.ppermute(array, 'tp', [(2 * i + core, 2 * j + core) for i, j in pairs...]
    ppermute x0 -> x5, starting transfers between devices: none -> 15 us  [hop(): lax.ppermute(array, 'tp', [(2 * i + core, 2 * j + core) for i, j in pairs...]
    convert_element_type x0 -> x5, other arithmetic: none -> 8.09 us  [the longest x4 7.69 us: added(): return sum((wide(array) for array in arrays)).astype(jnp.bfloat16)]
    ppermute x18 -> x23, waiting for transfers between devices: 40.9 us -> 35.5 us  [swapped(): return lax.ppermute(array, axis, [(i, i ^ step) for i in range(size)])]
  transfers between devices with their start and end apart: 20 -> 29, of which waited for: 11 -> 11; matrix products, arithmetic and copies ran while one was open for 20% -> 7% of each run, Pallas kernels for 10% -> 36%
where the time goes in v3:
time: 203 us
  Pallas kernels  72.1 us (36%)
  waiting for transfers between devices  56.7 us (28%)
  starting transfers between devices  40.7 us (20%)
  between operations  14.7 us (7%)
  other arithmetic  12.2 us (6%)
  local copies, waits for them, and re-layouts  6.06 us (3%)
    ppermute x23, waiting for transfers between devices, swapped(): return lax.ppermute(array, axis, [(i, i ^ step) for i in range(size)])  35.5 us
    pallas_call x8, Pallas kernels, column_product(): pl.pallas_call(column_sum_kernel if more else column_kernel, out_shape=ja...  32.1 us
    ppermute x23, starting transfers between devices, swapped(): return lax.ppermute(array, axis, [(i, i ^ step) for i in range(size)])  25.7 us
    ppermute x5, waiting for transfers between devices, hop(): lax.ppermute(array, 'tp', [(2 * i + core, 2 * j + core) for i, j in pairs...  20.6 us
    pallas_call x2, Pallas kernels, cotangent_product(): pl.pallas_call(first_half_kernel if rest is None else second_half_kernel,...  19.1 us
    ppermute x5, starting transfers between devices, hop(): lax.ppermute(array, 'tp', [(2 * i + core, 2 * j + core) for i, j in pairs...  15 us
    pallas_call x1, Pallas kernels, correlate(): pl.pallas_call(functools.partial(backward_kernel, members, per_group, sca...  13.6 us
    convert_element_type x4, other arithmetic, added(): return sum((wide(array) for array in arrays)).astype(jnp.bfloat16)  7.69 us
  transfers between devices with their start and end apart: 29, of which 11 were waited for; matrix products, arithmetic and copies ran while one was open for 7% of the time, Pallas kernels for 36%

profile of v3, /device:TPU:0, one launch (start us, length us, event | category | flops | bytes accessed | tf_op | source)
XLA Modules:
  0.0 202.5 jit_solution(16874844912959755168)
XLA Ops:
  10.1 3.0 %collective-permute-start = (bf16[512,256]{1,0:T(8,128)(2,1)S(1)}, bf16[512,256]{1,0:T(8,128)(2,1)S(1)}, u32[]{:S(2)}, u32[]{:S(2)}) collective-permute-start(bf16[512,256]{1,0:T(8,128)(2,1)S(1)} %get-tuple-element.41), channel_id=1, source_target_pairs={{0,8},{8,0},{16,24},{24,16},{1,9},{9,1},{17,25},{25,17},{2,10},{10... | collective-permute-start | bytes 786440 | tf_op jit(solution)/shard_map/ppermute | solution.py:207
  18.2 7.2 %collective-permute-done.3 = bf16[16,512]{1,0:T(8,128)(2,1)S(1)} collective-permute-done((bf16[16,512]{1,0:T(8,128)(2,1)S(1)}, bf16[16,512]{1,0:T(8,128)(2,1)S(1)}, u32[]{:S(2)}, u32[]{:S(2)}) %collective-permute-start.3) | collective-permute-done | bytes 16416 | tf_op jit(solution)/shard_map/ppermute | solution.py:207
  25.4 2.6 %collective-permute-start.5 = (bf16[16,512]{1,0:T(8,128)(2,1)S(1)}, bf16[16,512]{1,0:T(8,128)(2,1)S(1)}, u32[]{:S(2)}, u32[]{:S(2)}) collective-permute-start(bf16[16,512]{1,0:T(8,128)(2,1)S(1)} %get-tuple-element.43), channel_id=1, source_target_pairs={{0,24},{8,16},{16,8},{24,0},{1,25},{9,17},{17,9},{25,1},{2,26},{10... | collective-permute-start | bytes 49160 | tf_op jit(solution)/shard_map/ppermute | solution.py:207
  30.1 7.4 %causal_conv.1 = (bf16[512,256]{1,0:T(8,128)(2,1)S(1)}, bf16[512,256]{1,0:T(8,128)(2,1)S(1)}, bf16[512,256]{1,0:T(8,128)(2,1)S(1)}, bf16[512,256]{1,0:T(8,128)(2,1)S(1)}) custom-call(s32[1]{0:T(128)} %bitcast.1.pos_ref, bf16[512,256]{1,0:T(8,128)(2,1)S(1)} %get-tuple-element.42.refs_0_, bf16[512,256]{1,0:T(8,128)(2,1)S(1)} %collective-permute-done.refs_1_, ...), custom_call_target="tpu_custom_call" | custom-call | flops 1048576 | bytes 4096 | tf_op jit(solution)/shard_map/causal_conv/pallas_call | solution.py:163
  41.2 5.7 %collective-permute-done.6 = bf16[512,256]{1,0:T(8,128)(2,1)} collective-permute-done((bf16[512,256]{1,0:T(8,128)(2,1)S(1)}, bf16[512,256]{1,0:T(8,128)(2,1)}, u32[]{:S(2)}, u32[]{:S(2)}) %collective-permute-start.6) | collective-permute-done | bytes 262176 | tf_op jit(solution)/shard_map/ppermute | solution.py:207
  47.9 3.3 %collective-permute-done.7 = bf16[512,256]{1,0:T(8,128)(2,1)S(1)} collective-permute-done((bf16[512,256]{1,0:T(8,128)(2,1)S(1)}, bf16[512,256]{1,0:T(8,128)(2,1)S(1)}, u32[]{:S(2)}, u32[]{:S(2)}) %collective-permute-start.7) | collective-permute-done | bytes 262176 | tf_op jit(solution)/shard_map/ppermute | solution.py:207
  52.7 3.5 %projection_block.8 = bf16[512,1024]{1,0:T(8,128)(2,1)S(1)} custom-call(s32[1]{0:T(128)} %bitcast.8._, bf16[512,1024]{1,0:T(8,128)(2,1)S(1)} %multiply_convert_fusion.data_ref, bf16[1024,8192]{1,0:T(8,128)(2,1)} %weight_ref.19), custom_call_target="tpu_custom_call" | custom-call | flops 1048576 | bytes 4096 | tf_op jit(solution)/shard_map/projection_block/pallas_call | solution.py:288
  56.3 4.4 %projection_block.14 = bf16[512,1024]{1,0:T(8,128)(2,1)} custom-call(s32[1]{0:T(128)} %bitcast.14._, bf16[512,1024]{1,0:T(8,128)(2,1)S(1)} %multiply_convert_fusion.data_ref, bf16[1024,8192]{1,0:T(8,128)(2,1)} %weight_ref.19), custom_call_target="tpu_custom_call" | custom-call | flops 1048576 | bytes 4096 | tf_op jit(solution)/shard_map/projection_block/pallas_call | solution.py:288
  61.2 3.6 %projection_block.9.refs_0_ = bf16[512,1024]{1,0:T(8,128)(2,1)S(1)} custom-call(s32[1]{0:T(128)} %bitcast.7._, bf16[512,1024]{1,0:T(8,128)(2,1)S(1)} %multiply_convert_fusion.data_ref, bf16[1024,8192]{1,0:T(8,128)(2,1)} %weight_ref.19, bf16[512,1024]{1,0:T(8,128)(2,1)S(1)} %collective-permute-done.9.more_ref), custom_call_target="tpu_custom_call" | custom-call | flops 1048576 | bytes 4096 | tf_op jit(solution)/shard_map/projection_block/pallas_call | solution.py:288
  64.8 4.4 %projection_block.10 = bf16[512,1024]{1,0:T(8,128)(2,1)} custom-call(s32[1]{0:T(128)} %bitcast.6._, bf16[512,1024]{1,0:T(8,128)(2,1)S(1)} %multiply_convert_fusion.data_ref, bf16[1024,8192]{1,0:T(8,128)(2,1)} %weight_ref.19, bf16[512,1024]{1,0:T(8,128)(2,1)S(1)} %projection_block.9.refs_0_), custom_call_target="tpu_custom_call" | custom-call | flops 1048576 | bytes 4096 | tf_op jit(solution)/shard_map/projection_block/pallas_call | solution.py:288
  69.3 4.4 %projection_block.12 = bf16[512,1024]{1,0:T(8,128)(2,1)} custom-call(s32[1]{0:T(128)} %bitcast.10._, bf16[512,1024]{1,0:T(8,128)(2,1)S(1)} %multiply_convert_fusion.data_ref, bf16[1024,8192]{1,0:T(8,128)(2,1)} %weight_ref.19, bf16[512,1024]{1,0:T(8,128)(2,1)S(1)} %projection_block.9.refs_0_), custom_call_target="tpu_custom_call" | custom-call | flops 1048576 | bytes 4096 | tf_op jit(solution)/shard_map/projection_block/pallas_call | solution.py:288
  74.1 4.0 %collective-permute-start.12 = (bf16[512,1024]{1,0:T(8,128)(2,1)S(1)}, bf16[512,1024]{1,0:T(8,128)(2,1)}, u32[]{:S(2)}, u32[]{:S(2)}) collective-permute-start(bf16[512,1024]{1,0:T(8,128)(2,1)S(1)} %projection_block.9.refs_0_), channel_id=1, source_target_pairs={{0,2},{1,3},{6,4},{7,5},{8,10},{9,11},{14,12},{15,13},{16,18},{17,... | collective-permute-start | bytes 3145736 | tf_op jit(solution)/shard_map/ppermute | solution.py:240
  78.1 3.7 %projection_block.15.refs_2_ = bf16[512,1024]{1,0:T(8,128)(2,1)S(1)} custom-call(s32[1]{0:T(128)} %bitcast.13._, bf16[512,1024]{1,0:T(8,128)(2,1)S(1)} %multiply_convert_fusion.data_ref, bf16[1024,8192]{1,0:T(8,128)(2,1)} %weight_ref.19, bf16[512,1024]{1,0:T(8,128)(2,1)} %collective-permute-done.14.more_ref), custom_call_target="tpu_custom_call" | custom-call | flops 1048576 | bytes 4096 | tf_op jit(solution)/shard_map/projection_block/pallas_call | solution.py:288
  81.8 4.1 %projection_block.11.refs_4_ = bf16[512,1024]{1,0:T(8,128)(2,1)S(1)} custom-call(s32[1]{0:T(128)} %bitcast._, bf16[512,1024]{1,0:T(8,128)(2,1)S(1)} %multiply_convert_fusion.data_ref, bf16[1024,8192]{1,0:T(8,128)(2,1)} %weight_ref.19, bf16[512,1024]{1,0:T(8,128)(2,1)} %collective-permute-done.10.more_ref), custom_call_target="tpu_custom_call" | custom-call | flops 1048576 | bytes 4096 | tf_op jit(solution)/shard_map/projection_block/pallas_call | solution.py:288
  85.9 3.9 %projection_block.13.refs_3_ = bf16[512,1024]{1,0:T(8,128)(2,1)S(1)} custom-call(s32[1]{0:T(128)} %bitcast.9._, bf16[512,1024]{1,0:T(8,128)(2,1)S(1)} %multiply_convert_fusion.data_ref, bf16[1024,8192]{1,0:T(8,128)(2,1)} %weight_ref.19, bf16[512,1024]{1,0:T(8,128)(2,1)S(1)} %collective-permute-done.11.more_ref), custom_call_target="tpu_custom_call" | custom-call | flops 1048576 | bytes 4096 | tf_op jit(solution)/shard_map/projection_block/pallas_call | solution.py:288
  90.9 20.6 %collective-permute-done.12.refs_1_ = bf16[512,1024]{1,0:T(8,128)(2,1)} collective-permute-done((bf16[512,1024]{1,0:T(8,128)(2,1)S(1)}, bf16[512,1024]{1,0:T(8,128)(2,1)}, u32[]{:S(2)}, u32[]{:S(2)}) %collective-permute-start.12) | collective-permute-done | bytes 1048608 | tf_op jit(solution)/shard_map/ppermute | solution.py:240
  111.4 2.8 %add_convert_fusion.3 = bf16[512,1024]{1,0:T(8,128)(2,1)} fusion(bf16[512,1024]{1,0:T(8,128)(2,1)} %collective-permute-done.12.refs_1_, bf16[512,1024]{1,0:T(8,128)(2,1)S(1)} %projection_block.9.refs_0_), kind=kLoop, calls=%fused_computation.9 | loop fusion | flops 2097152 | bytes 3145728 | tf_op jit(solution)/shard_map/convert_element_type | solution.py:392
  115.8 8.4 %collective-permute-start.17 = (bf16[512,1024]{1,0:T(8,128)(2,1)S(1)}, bf16[512,1024]{1,0:T(8,128)(2,1)}, u32[]{:S(2)}, u32[]{:S(2)}) collective-permute-start(bf16[512,1024]{1,0:T(8,128)(2,1)S(1)} %copy-done.1), channel_id=1, source_target_pairs={{0,2},{1,3},{6,4},{7,5},{8,10},{9,11},{14,12},{15,13},{16,18},{17,... | collective-permute-start | bytes 3145736 | tf_op jit(solution)/shard_map/ppermute | solution.py:240
  124.3 8.5 %cotangent_half.2.start_ref = f32[512,1024]{1,0:T(8,128)S(1)} custom-call(s32[1]{0:T(128)} %bitcast.15._, bf16[4,512,1024]{2,1,0:T(8,128)(2,1)} %held.3.data_ref, bf16[1024,8192]{1,0:T(8,128)(2,1)} %weight_ref.19), custom_call_target="tpu_custom_call" | custom-call | flops 1048576 | bytes 4096 | tf_op jit(solution)/shard_map/cotangent_half/pallas_call | solution.py:349
  134.1 10.6 %cotangent_half.3 = (bf16[512,1024]{1,0:T(8,128)(2,1)}, bf16[512,1024]{1,0:T(8,128)(2,1)S(1)}) custom-call(s32[1]{0:T(128)} %bitcast.11._, bf16[4,512,1024]{2,1,0:T(8,128)(2,1)} %collective-permute-done.15.data_ref, bf16[1024,8192]{1,0:T(8,128)(2,1)} %weight_ref.19, f32[512,1024]{1,0:T(8,128)} %copy-done.9, bf16[512,1024]{1,0:T(8,128)(2,1)S(1)} %copy-done.6, ...), custom_call_target="tpu_custom_call" | custom-call | flops 1048576 | bytes 4096 | tf_op jit(solution)/shard_map/cotangent_half/pallas_call | solution.py:349
  155.3 5.7 %collective-permute-done.20.refs_6_ = bf16[512,256]{1,0:T(8,128)(2,1)} collective-permute-done((bf16[512,256]{1,0:T(8,128)(2,1)}, bf16[512,256]{1,0:T(8,128)(2,1)}, u32[]{:S(2)}, u32[]{:S(2)}) %collective-permute-start.20) | collective-permute-done | bytes 262176 | tf_op jit(solution)/shard_map/ppermute | solution.py:207
  161.1 13.6 %causal_conv_grads.1 = (bf16[512,256]{1,0:T(8,128)(2,1)S(1)}, bf16[512,256]{1,0:T(8,128)(2,1)S(1)}, bf16[512,256]{1,0:T(8,128)(2,1)S(1)}, bf16[512,256]{1,0:T(8,...) custom-call(s32[1]{0:T(128)} %bitcast.1.pos_ref, ...), custom_call_target="tpu_custom_call" | custom-call | flops 1048576 | bytes 4096 | tf_op jit(solution)/shard_map/causal_conv_grads/pallas_call | solution.py:184
  183.5 4.6 %collective-permute-done.22 = bf16[512,256]{1,0:T(8,128)(2,1)S(1)} collective-permute-done((bf16[512,256]{1,0:T(8,128)(2,1)S(1)}, bf16[512,256]{1,0:T(8,128)(2,1)S(1)}, u32[]{:S(2)}, u32[]{:S(2)}) %collective-permute-start.22) | collective-permute-done | bytes 262176 | tf_op jit(solution)/shard_map/ppermute | solution.py:207
  188.1 3.7 %collective-permute-done.23 = bf16[512,256]{1,0:T(8,128)(2,1)S(1)} collective-permute-done((bf16[512,256]{1,0:T(8,128)(2,1)S(1)}, bf16[512,256]{1,0:T(8,128)(2,1)S(1)}, u32[]{:S(2)}, u32[]{:S(2)}) %collective-permute-start.23) | collective-permute-done | bytes 262176 | tf_op jit(solution)/shard_map/ppermute | solution.py:207
  (125 shorter events, 44.2 us)
Async XLA Ops:
  7.2 104.3 %all-gather.3.cloned.1.call-start = ((), (), s32[]{:S(2)}) async-start(), calls=%async_computation | async-start | bytes 5242880 | tf_op jit(solution)/shard_map/all_gather | solution.py:424
  10.1 20.0 %collective-permute-start = (bf16[512,256]{1,0:T(8,128)(2,1)S(1)}, bf16[512,256]{1,0:T(8,128)(2,1)S(1)}, u32[]{:S(2)}, u32[]{:S(2)}) collective-permute-start(bf16[512,256]{1,0:T(8,128)(2,1)S(1)} %get-tuple-element.41), channel_id=1, source_target_pairs={{0,8},{8,0},{16,24},{24,16},{1,9},{9,1},{17,25},{25,17},{2,10},{10... | collective-permute-start | bytes 786440 | tf_op jit(solution)/shard_map/ppermute | solution.py:207
  13.1 17.0 %collective-permute-start.1 = (bf16[512,256]{1,0:T(8,128)(2,1)S(1)}, bf16[512,256]{1,0:T(8,128)(2,1)S(1)}, u32[]{:S(2)}, u32[]{:S(2)}) collective-permute-start(bf16[512,256]{1,0:T(8,128)(2,1)S(1)} %get-tuple-element.40), channel_id=1, source_target_pairs={{0,16},{8,24},{16,0},{24,8},{1,17},{9,25},{17,1},{25,9},{2,18},{10... | collective-permute-start | bytes 786440 | tf_op jit(solution)/shard_map/ppermute | solution.py:207
  14.6 15.5 %collective-permute-start.2 = (bf16[512,256]{1,0:T(8,128)(2,1)S(1)}, bf16[512,256]{1,0:T(8,128)(2,1)S(1)}, u32[]{:S(2)}, u32[]{:S(2)}) collective-permute-start(bf16[512,256]{1,0:T(8,128)(2,1)S(1)} %get-tuple-element.39), channel_id=1, source_target_pairs={{0,24},{8,16},{16,8},{24,0},{1,25},{9,17},{17,9},{25,1},{2,26},{10... | collective-permute-start | bytes 786440 | tf_op jit(solution)/shard_map/ppermute | solution.py:207
  14.7 10.7 %collective-permute-start.3 = (bf16[16,512]{1,0:T(8,128)(2,1)S(1)}, bf16[16,512]{1,0:T(8,128)(2,1)S(1)}, u32[]{:S(2)}, u32[]{:S(2)}) collective-permute-start(bf16[16,512]{1,0:T(8,128)(2,1)S(1)} %get-tuple-element.45), channel_id=1, source_target_pairs={{0,8},{8,0},{16,24},{24,16},{1,9},{9,1},{17,25},{25,17},{2,10},{10... | collective-permute-start | bytes 49160 | tf_op jit(solution)/shard_map/ppermute | solution.py:207
  16.7 11.4 %collective-permute-start.4 = (bf16[16,512]{1,0:T(8,128)(2,1)S(1)}, bf16[16,512]{1,0:T(8,128)(2,1)S(1)}, u32[]{:S(2)}, u32[]{:S(2)}) collective-permute-start(bf16[16,512]{1,0:T(8,128)(2,1)S(1)} %get-tuple-element.44), channel_id=1, source_target_pairs={{0,16},{8,24},{16,0},{24,8},{1,17},{9,25},{17,1},{25,9},{2,18},{10... | collective-permute-start | bytes 49160 | tf_op jit(solution)/shard_map/ppermute | solution.py:207
  37.5 9.4 %collective-permute-start.6 = (bf16[512,256]{1,0:T(8,128)(2,1)S(1)}, bf16[512,256]{1,0:T(8,128)(2,1)}, u32[]{:S(2)}, u32[]{:S(2)}) collective-permute-start(bf16[512,256]{1,0:T(8,128)(2,1)S(1)} %get-tuple-element.20), channel_id=1, source_target_pairs={{0,8},{8,0},{16,24},{24,16},{1,9},{9,1},{17,25},{25,17},{2,10},{10... | collective-permute-start | bytes 786440 | tf_op jit(solution)/shard_map/ppermute | solution.py:207
  39.3 11.9 %collective-permute-start.7 = (bf16[512,256]{1,0:T(8,128)(2,1)S(1)}, bf16[512,256]{1,0:T(8,128)(2,1)S(1)}, u32[]{:S(2)}, u32[]{:S(2)}) collective-permute-start(bf16[512,256]{1,0:T(8,128)(2,1)S(1)} %get-tuple-element.21), channel_id=1, source_target_pairs={{0,16},{8,24},{16,0},{24,8},{1,17},{9,25},{17,1},{25,9},{2,18},{10... | collective-permute-start | bytes 786440 | tf_op jit(solution)/shard_map/ppermute | solution.py:207
  40.8 10.4 %collective-permute-start.8 = (bf16[512,256]{1,0:T(8,128)(2,1)S(1)}, bf16[512,256]{1,0:T(8,128)(2,1)S(1)}, u32[]{:S(2)}, u32[]{:S(2)}) collective-permute-start(bf16[512,256]{1,0:T(8,128)(2,1)S(1)} %get-tuple-element.22), channel_id=1, source_target_pairs={{0,24},{8,16},{16,8},{24,0},{1,25},{9,17},{17,9},{25,1},{2,26},{10... | collective-permute-start | bytes 786440 | tf_op jit(solution)/shard_map/ppermute | solution.py:207
  60.7 17.3 %collective-permute-start.14 = (bf16[512,1024]{1,0:T(8,128)(2,1)}, bf16[512,1024]{1,0:T(8,128)(2,1)}, u32[]{:S(2)}, u32[]{:S(2)}) collective-permute-start(bf16[512,1024]{1,0:T(8,128)(2,1)} %projection_block.14), channel_id=1, source_target_pairs={{0,1},{1,0},{2,3},{3,2},{4,5},{5,4},{6,7},{7,6},{8,9},{9,8},{10,11... | collective-permute-start | bytes 3145736 | tf_op jit(solution)/shard_map/ppermute | solution.py:207
  69.2 12.6 %collective-permute-start.10 = (bf16[512,1024]{1,0:T(8,128)(2,1)}, bf16[512,1024]{1,0:T(8,128)(2,1)}, u32[]{:S(2)}, u32[]{:S(2)}) collective-permute-start(bf16[512,1024]{1,0:T(8,128)(2,1)} %projection_block.10), channel_id=1, source_target_pairs={{0,1},{1,0},{2,3},{3,2},{4,5},{5,4},{6,7},{7,6},{8,9},{9,8},{10,11... | collective-permute-start | bytes 3145736 | tf_op jit(solution)/shard_map/ppermute | solution.py:207
  73.7 12.3 %collective-permute-start.11 = (bf16[512,1024]{1,0:T(8,128)(2,1)}, bf16[512,1024]{1,0:T(8,128)(2,1)S(1)}, u32[]{:S(2)}, u32[]{:S(2)}) collective-permute-start(bf16[512,1024]{1,0:T(8,128)(2,1)} %projection_block.12), channel_id=1, source_target_pairs={{0,1},{1,0},{2,3},{3,2},{4,5},{5,4},{6,7},{7,6},{8,9},{9,8},{10,11... | collective-permute-start | bytes 3145736 | tf_op jit(solution)/shard_map/ppermute | solution.py:207
  74.1 37.3 %collective-permute-start.12 = (bf16[512,1024]{1,0:T(8,128)(2,1)S(1)}, bf16[512,1024]{1,0:T(8,128)(2,1)}, u32[]{:S(2)}, u32[]{:S(2)}) collective-permute-start(bf16[512,1024]{1,0:T(8,128)(2,1)S(1)} %projection_block.9.refs_0_), channel_id=1, source_target_pairs={{0,2},{1,3},{6,4},{7,5},{8,10},{9,11},{14,12},{15,13},{16,18},{17,... | collective-permute-start | bytes 3145736 | tf_op jit(solution)/shard_map/ppermute | solution.py:240
  111.4 22.7 %collective-permute-start.15 = (bf16[4,512,1024]{2,1,0:T(8,128)(2,1)}, bf16[4,512,1024]{2,1,0:T(8,128)(2,1)}, u32[]{:S(2)}, u32[]{:S(2)}) collective-permute-start(bf16[4,512,1024]{2,1,0:T(8,128)(2,1)} %held.3.data_ref), channel_id=1, source_target_pairs={{0,1},{1,0},{2,3},{3,2},{4,5},{5,4},{6,7},{7,6},{8,9},{9,8},{10,11... | collective-permute-start | bytes 12582920 | tf_op jit(solution)/shard_map/ppermute | solution.py:207
  114.2 35.1 %collective-permute-start.13 = (bf16[512,1024]{1,0:T(8,128)(2,1)}, bf16[512,1024]{1,0:T(8,128)(2,1)}, u32[]{:S(2)}, u32[]{:S(2)}) collective-permute-start(bf16[512,1024]{1,0:T(8,128)(2,1)} %add_convert_fusion.3), channel_id=1, source_target_pairs={{2,4},{3,5},{4,2},{5,3},{10,12},{11,13},{12,10},{13,11},{18,20},{1... | collective-permute-start | bytes 3145736 | tf_op jit(solution)/shard_map/ppermute | solution.py:240
  115.8 35.2 %collective-permute-start.17 = (bf16[512,1024]{1,0:T(8,128)(2,1)S(1)}, bf16[512,1024]{1,0:T(8,128)(2,1)}, u32[]{:S(2)}, u32[]{:S(2)}) collective-permute-start(bf16[512,1024]{1,0:T(8,128)(2,1)S(1)} %copy-done.1), channel_id=1, source_target_pairs={{0,2},{1,3},{6,4},{7,5},{8,10},{9,11},{14,12},{15,13},{16,18},{17,... | collective-permute-start | bytes 3145736 | tf_op jit(solution)/shard_map/ppermute | solution.py:240
  145.8 9.5 %collective-permute-start.19 = (bf16[512,256]{1,0:T(8,128)(2,1)}, bf16[512,256]{1,0:T(8,128)(2,1)}, u32[]{:S(2)}, u32[]{:S(2)}) collective-permute-start(bf16[512,256]{1,0:T(8,128)(2,1)} %get-tuple-element.37), channel_id=1, source_target_pairs={{0,8},{8,0},{16,24},{24,16},{1,9},{9,1},{17,25},{25,17},{2,10},{10... | collective-permute-start | bytes 786440 | tf_op jit(solution)/shard_map/ppermute | solution.py:207
  147.3 13.7 %collective-permute-start.20 = (bf16[512,256]{1,0:T(8,128)(2,1)}, bf16[512,256]{1,0:T(8,128)(2,1)}, u32[]{:S(2)}, u32[]{:S(2)}) collective-permute-start(bf16[512,256]{1,0:T(8,128)(2,1)} %get-tuple-element.36), channel_id=1, source_target_pairs={{0,16},{8,24},{16,0},{24,8},{1,17},{9,25},{17,1},{25,9},{2,18},{10... | collective-permute-start | bytes 786440 | tf_op jit(solution)/shard_map/ppermute | solution.py:207
  148.8 12.3 %collective-permute-start.21 = (bf16[512,256]{1,0:T(8,128)(2,1)}, bf16[512,256]{1,0:T(8,128)(2,1)}, u32[]{:S(2)}, u32[]{:S(2)}) collective-permute-start(bf16[512,256]{1,0:T(8,128)(2,1)} %get-tuple-element.35), channel_id=1, source_target_pairs={{0,24},{8,16},{16,8},{24,0},{1,25},{9,17},{17,9},{25,1},{2,26},{10... | collective-permute-start | bytes 786440 | tf_op jit(solution)/shard_map/ppermute | solution.py:207
  151.0 43.1 %collective-permute-start.16 = (bf16[512,1024]{1,0:T(8,128)(2,1)S(1)}, bf16[512,1024]{1,0:T(8,128)(2,1)S(1)}, u32[]{:S(2)}, u32[]{:S(2)}) collective-permute-start(bf16[512,1024]{1,0:T(8,128)(2,1)S(1)} %add_convert_fusion.2), channel_id=1, source_target_pairs={{2,0},{3,1},{4,6},{5,7},{0,2},{1,3},{6,4},{7,5},{10,8},{11,9},{12,... | collective-permute-start | bytes 3145736 | tf_op jit(solution)/shard_map/ppermute | solution.py:240
  152.8 41.2 %collective-permute-start.18 = (bf16[512,1024]{1,0:T(8,128)(2,1)S(1)}, bf16[512,1024]{1,0:T(8,128)(2,1)S(1)}, u32[]{:S(2)}, u32[]{:S(2)}) collective-permute-start(bf16[512,1024]{1,0:T(8,128)(2,1)S(1)} %add_convert_fusion.1), channel_id=1, source_target_pairs={{2,4},{3,5},{4,2},{5,3},{10,12},{11,13},{12,10},{13,11},{18,20},{1... | collective-permute-start | bytes 3145736 | tf_op jit(solution)/shard_map/ppermute | solution.py:240
  178.9 9.1 %collective-permute-start.22 = (bf16[512,256]{1,0:T(8,128)(2,1)S(1)}, bf16[512,256]{1,0:T(8,128)(2,1)S(1)}, u32[]{:S(2)}, u32[]{:S(2)}) collective-permute-start(bf16[512,256]{1,0:T(8,128)(2,1)S(1)} %get-tuple-element.26), channel_id=1, source_target_pairs={{0,8},{8,0},{16,24},{24,16},{1,9},{9,1},{17,25},{25,17},{2,10},{10... | collective-permute-start | bytes 786440 | tf_op jit(solution)/shard_map/ppermute | solution.py:207
  179.8 12.0 %collective-permute-start.23 = (bf16[512,256]{1,0:T(8,128)(2,1)S(1)}, bf16[512,256]{1,0:T(8,128)(2,1)S(1)}, u32[]{:S(2)}, u32[]{:S(2)}) collective-permute-start(bf16[512,256]{1,0:T(8,128)(2,1)S(1)} %get-tuple-element.27), channel_id=1, source_target_pairs={{0,16},{8,24},{16,0},{24,8},{1,17},{9,25},{17,1},{25,9},{2,18},{10... | collective-permute-start | bytes 786440 | tf_op jit(solution)/shard_map/ppermute | solution.py:207
  182.0 9.8 %collective-permute-start.24 = (bf16[512,256]{1,0:T(8,128)(2,1)S(1)}, bf16[512,256]{1,0:T(8,128)(2,1)S(1)}, u32[]{:S(2)}, u32[]{:S(2)}) collective-permute-start(bf16[512,256]{1,0:T(8,128)(2,1)S(1)} %get-tuple-element.28), channel_id=1, source_target_pairs={{0,24},{8,16},{16,8},{24,0},{1,25},{9,17},{17,9},{25,1},{2,26},{10... | collective-permute-start | bytes 786440 | tf_op jit(solution)/shard_map/ppermute | solution.py:207
  (28 other events, 245.1 us)
Sparse Core Ops, SparseCore 0:
  9.6 90.9 all-gather.2

commit v4 on v1

--- a/solution.py
+++ b/solution.py
@@ -9,6 +9,7 @@
 
 BLOCK = 128
 NT = (((1,), (1,)), ((), ()))
+COST = pl.CostEstimate(flops=2**20, bytes_accessed=2**12, transcendentals=0)
 
 
 def lag_matrix(row, length):
@@ -37,19 +38,33 @@
         ref[member, pl.ds(start, rows), :] = jnp.concatenate(parts, axis=1)
 
 
-def forward_kernel(members, per_group, pos_ref, *refs):
-    inputs, taps = refs[:members], refs[members : 2 * members]
-    outputs = refs[2 * members : 3 * members]
-    tap_scr, in_scr, out_scr = refs[3 * members :]
+def padded(groups):
+    return -(-groups // 16) * 16
+
+
+def load_taps(tap_scr, packed, at, width):
+    groups, channels = tap_scr.shape[0], packed.shape[1]
+    rows = padded(groups)
+    parts = [
+        packed[width + chunk * rows : width + (chunk + 1) * rows, :].astype(jnp.float32)
+        for chunk in range(width // channels)
+    ]
+    start = pl.multiple_of(at * width, width)
+    tap_scr[:, pl.ds(start, width)] = jnp.concatenate(parts, axis=1)[:groups]
+
+
+def forward_kernel(members, per_group, width, pos_ref, *refs):
+    inputs, outputs = refs[:members], refs[-members - 3 : -3]
+    tap_scr, in_scr, out_scr = refs[-3:]
     position = pos_ref[0]
-    width, channels = inputs[0].shape
-    groups = taps[0].shape[0]
+    channels = inputs[0].shape[1]
+    groups = channels // per_group
     length = members * width
     blocks = length // BLOCK
     for step in range(members):
         at = position ^ step
-        in_scr[at] = inputs[step][...].T
-        tap_scr[:, pl.ds(pl.multiple_of(at * width, width), width)] = taps[step][...]
+        in_scr[at] = inputs[step][:width].T
+        load_taps(tap_scr, inputs[step], at, width)
 
     def one_group(group, carry):
         start = pl.multiple_of(group * per_group, per_group)
@@ -78,26 +93,21 @@
         outputs[step][...] = out_scr[position ^ step].T
 
 
-def backward_kernel(members, per_group, scale, pos_ref, *refs):
-    inputs, cotangents, taps = (
-        refs[:members],
-        refs[members : 2 * members],
-        refs[2 * members : 3 * members],
-    )
-    outputs = refs[3 * members : 4 * members]
-    tap_grads = refs[4 * members : 5 * members]
-    tap_scr, in_scr, cot_scr, out_scr, grad_scr, pad_scr = refs[5 * members :]
+def backward_kernel(members, per_group, scale, width, pos_ref, *refs):
+    inputs, cotangents = refs[:members], refs[members : 2 * members]
+    outputs = refs[-members - 6 : -6]
+    tap_scr, in_scr, cot_scr, out_scr, grad_scr, pad_scr = refs[-6:]
     position = pos_ref[0]
-    width, channels = inputs[0].shape
-    groups = taps[0].shape[0]
+    channels = inputs[0].shape[1]
+    groups = channels // per_group
     length = members * width
     blocks = length // BLOCK
     depth = blocks * per_group
     for step in range(members):
         at = position ^ step
-        in_scr[at] = inputs[step][...].T
+        in_scr[at] = inputs[step][:width].T
         cot_scr[at] = cotangents[step][...].T
-        tap_scr[:, pl.ds(pl.multiple_of(at * width, width), width)] = taps[step][...]
+        load_taps(tap_scr, inputs[step], at, width)
     pad_scr[...] = jnp.zeros_like(pad_scr)
     rows_of = lax.broadcasted_iota(jnp.int32, (BLOCK, BLOCK), 0)
     lanes_of = lax.broadcasted_iota(jnp.int32, (BLOCK, BLOCK), 1)
@@ -146,50 +156,53 @@
     lax.fori_loop(0, groups, one_group, 0)
     for step in range(members):
         at = position ^ step
-        outputs[step][...] = out_scr[at].T
-        tap_grads[step][...] = grad_scr[:, pl.ds(pl.multiple_of(at * width, width), width)]
+        outputs[step][:width] = out_scr[at].T
+        rows = padded(groups)
+        whole = grad_scr[:, pl.ds(pl.multiple_of(at * width, width), width)].astype(jnp.bfloat16)
+        if rows > groups:
+            blank = jnp.zeros((rows - groups, width), jnp.bfloat16)
+            whole = jnp.concatenate([whole, blank], axis=0)
+        for chunk in range(width // channels):
+            outputs[step][width + chunk * rows : width + (chunk + 1) * rows, :] = whole[
+                :, chunk * channels : (chunk + 1) * channels
+            ]
 
 
 VMEM = pl.BlockSpec(memory_space=pltpu.VMEM)
+ANYWHERE = pl.BlockSpec(memory_space=pl.ANY)
 SMEM = pl.BlockSpec(memory_space=pltpu.SMEM)
 
 
-def convolve(position, inputs, taps, per_group):
+def convolve(position, inputs, width, per_group, after=()):
     members = len(inputs)
-    width, channels = inputs[0].shape
-    groups = taps[0].shape[0]
+    channels = inputs[0].shape[1]
     length = members * width
-    flops = 4 * length * length * channels
     return pl.pallas_call(
-        functools.partial(forward_kernel, members, per_group),
+        functools.partial(forward_kernel, members, per_group, width),
         out_shape=[jax.ShapeDtypeStruct((width, channels), jnp.bfloat16)] * members,
-        in_specs=[SMEM] + [VMEM] * (2 * members),
+        in_specs=[SMEM] + [VMEM] * members + [ANYWHERE] * len(after),
         out_specs=[VMEM] * members,
         scratch_shapes=[
-            pltpu.VMEM((groups, length), jnp.float32),
+            pltpu.VMEM((channels // per_group, length), jnp.float32),
             pltpu.VMEM((members, channels, width), jnp.bfloat16),
             pltpu.VMEM((members, channels, width), jnp.bfloat16),
         ],
-        compiler_params=pltpu.CompilerParams(vmem_limit_bytes=32 * 2**20),
-        cost_estimate=pl.CostEstimate(
-            flops=flops, bytes_accessed=4 * length * channels, transcendentals=0
-        ),
+        compiler_params=pltpu.CompilerParams(vmem_limit_bytes=24 * 2**20),
+        cost_estimate=COST,
         name="causal_conv",
-    )(position, *inputs, *taps)
-
-
-def correlate(position, inputs, cotangents, taps, per_group, scale):
+    )(position, *inputs, *after)
+
+
+def correlate(position, inputs, cotangents, per_group, scale, after=()):
     members = len(inputs)
-    width, channels = inputs[0].shape
-    groups = taps[0].shape[0]
+    width, channels = cotangents[0].shape
     length = members * width
-    flops = 8 * length * length * channels
-    results = pl.pallas_call(
-        functools.partial(backward_kernel, members, per_group, scale),
-        out_shape=[jax.ShapeDtypeStruct((width, channels), jnp.bfloat16)] * members
-        + [jax.ShapeDtypeStruct((groups, width), jnp.float32)] * members,
-        in_specs=[SMEM] + [VMEM] * (3 * members),
-        out_specs=[VMEM] * (2 * members),
+    groups = channels // per_group
+    return pl.pallas_call(
+        functools.partial(backward_kernel, members, per_group, scale, width),
+        out_shape=[jax.ShapeDtypeStruct(inputs[0].shape, jnp.bfloat16)] * members,
+        in_specs=[SMEM] + [VMEM] * (2 * members) + [ANYWHERE] * len(after),
+        out_specs=[VMEM] * members,
         scratch_shapes=[
             pltpu.VMEM((groups, length), jnp.float32),
             pltpu.VMEM((members, channels, width), jnp.bfloat16),
@@ -198,13 +211,88 @@
             pltpu.VMEM((groups, length), jnp.float32),
             pltpu.VMEM((2 * length // BLOCK * per_group, 2 * BLOCK), jnp.bfloat16),
         ],
-        compiler_params=pltpu.CompilerParams(vmem_limit_bytes=32 * 2**20),
-        cost_estimate=pl.CostEstimate(
-            flops=flops, bytes_accessed=6 * length * channels, transcendentals=0
-        ),
+        compiler_params=pltpu.CompilerParams(vmem_limit_bytes=24 * 2**20),
+        cost_estimate=COST,
         name="causal_conv_grads",
-    )(position, *inputs, *cotangents, *taps)
-    return results[:members], results[members:]
+    )(position, *inputs, *cotangents, *after)
+
+
+def prepare_kernel(members, scale, pos_ref, key_ref, value_ref, taps_ref, *refs):
+    outputs = refs
+    position = pos_ref[0]
+    width, channels = key_ref.shape
+    share = channels // members
+    groups = taps_ref.shape[0] // members
+    for step in range(members):
+        at = position ^ step
+        columns = pl.ds(pl.multiple_of(at * share, share), share)
+        product = key_ref[:, columns].astype(jnp.float32) * value_ref[:, columns].astype(
+            jnp.float32
+        )
+        outputs[step][:width] = product.astype(jnp.bfloat16)
+        taps = taps_ref[pl.ds(pl.multiple_of(at * groups, groups), groups), :]
+        taps = (taps * scale).astype(jnp.bfloat16)
+        for chunk in range(width // share):
+            outputs[step][width + chunk * groups : width + (chunk + 1) * groups, :] = taps[
+                :, chunk * share : (chunk + 1) * share
+            ]
+
+
+def prepare(position, key_gate, value_input, filter_taps, members, scale):
+    width, channels = key_gate.shape
+    share = channels // members
+    rows = width + filter_taps.size // members // share
+    return pl.pallas_call(
+        functools.partial(prepare_kernel, members, scale),
+        out_shape=[jax.ShapeDtypeStruct((rows, share), jnp.bfloat16)] * members,
+        in_specs=[SMEM] + [VMEM] * 3,
+        out_specs=[VMEM] * members,
+        compiler_params=pltpu.CompilerParams(vmem_limit_bytes=24 * 2**20),
+        cost_estimate=COST,
+        name="gated_input",
+    )(position, key_gate, value_input, filter_taps.T)
+
+
+def finish_kernel(members, pos_ref, *refs):
+    parts = refs[:members]
+    key_ref, value_ref, key_out, value_out, taps_out = refs[members:]
+    position = pos_ref[0]
+    width, channels = key_ref.shape
+    share = channels // members
+    groups = taps_out.shape[0] // members
+    for step in range(members):
+        at = position ^ step
+        columns = pl.ds(pl.multiple_of(at * share, share), share)
+        grad = parts[step][:width].astype(jnp.float32)
+        key_out[:, columns] = (grad * value_ref[:, columns].astype(jnp.float32)).astype(
+            jnp.bfloat16
+        )
+        value_out[:, columns] = (grad * key_ref[:, columns].astype(jnp.float32)).astype(
+            jnp.bfloat16
+        )
+        taps = [
+            parts[step][width + chunk * groups : width + (chunk + 1) * groups, :]
+            for chunk in range(width // share)
+        ]
+        taps_out[pl.ds(pl.multiple_of(at * groups, groups), groups), :] = jnp.concatenate(
+            taps, axis=1
+        ).astype(jnp.float32)
+
+
+def finished(position, parts, key_gate, value_input, groups):
+    members = len(parts)
+    width, channels = key_gate.shape
+    array = jax.ShapeDtypeStruct((width, channels), jnp.bfloat16)
+    grad_key, grad_value, taps = pl.pallas_call(
+        functools.partial(finish_kernel, members),
+        out_shape=[array, array, jax.ShapeDtypeStruct((groups, width), jnp.float32)],
+        in_specs=[SMEM] + [VMEM] * (members + 2),
+        out_specs=[VMEM] * 3,
+        compiler_params=pltpu.CompilerParams(vmem_limit_bytes=24 * 2**20),
+        cost_estimate=COST,
+        name="input_gradients",
+    )(position, *parts, key_gate, value_input)
+    return grad_key, grad_value, taps.T
 
 
 def swapped(array, axis, step):
@@ -241,6 +329,239 @@
     return array.astype(jnp.float32)
 
 
+def hop(array, pairs):
+    return lax.ppermute(
+        array, "tp", [(2 * i + core, 2 * j + core) for i, j in pairs for core in range(2)]
+    )
+
+
+INWARD = ((0, 1), (3, 2))
+ACROSS = ((1, 2), (2, 1))
+OUTWARD = ((1, 0), (2, 3))
+
+
+def of_chip(chip, table):
+    return jnp.where(
+        chip == 0, table[0], jnp.where(chip == 1, table[1], jnp.where(chip == 2, table[2], table[3]))
+    )
+
+
+def pass_kernel(*refs):
+    del refs
+
+
+def in_hbm(array):
+    return pltpu.with_memory_space_constraint(array, pltpu.HBM)
+
+
+def held_until(values, after):
+    return pl.pallas_call(
+        pass_kernel,
+        out_shape=[jax.ShapeDtypeStruct(value.shape, value.dtype) for value in values],
+        in_specs=[ANYWHERE] * (len(values) + len(after)),
+        out_specs=[ANYWHERE] * len(values),
+        input_output_aliases={number: number for number in range(len(values))},
+        cost_estimate=COST,
+        name="held",
+    )(*values, *after)
+
+
+def given_kernel(_, data_ref, weight_ref, *refs):
+    refs[-1][0] = jnp.dot(
+        data_ref[...], weight_ref[...], preferred_element_type=jnp.float32
+    ).astype(jnp.bfloat16)
+
+
+def kept_kernel(tiles, count, _, data_ref, weight_ref, more_ref, *refs):
+    product = jnp.dot(data_ref[...], weight_ref[...], preferred_element_type=jnp.float32)
+    result = (product + wide(more_ref[0])).astype(jnp.bfloat16)
+    for number, out_ref in enumerate(refs[-count:]):
+
+        @pl.when(pl.program_id(0) // tiles == number)
+        def _(out_ref=out_ref):
+            out_ref[...] = result
+
+
+def column_products(data, out_weight, blocks, width, more=None, after=()):
+    rows, depth = data.shape
+    tile = min(width, 512)
+    tiles = width // tile
+    count = len(blocks)
+    stack = pl.BlockSpec((1, rows, tile), lambda i, at: (i // tiles, 0, i % tiles))
+    array = jax.ShapeDtypeStruct((rows, width), jnp.bfloat16)
+
+    def column(number):
+        return pl.BlockSpec(
+            (rows, tile), lambda i, at: (0, jnp.clip(i - number * tiles, 0, tiles - 1))
+        )
+
+    return pl.pallas_call(
+        given_kernel if more is None else functools.partial(kept_kernel, tiles, count),
+        out_shape=jax.ShapeDtypeStruct((count, rows, width), jnp.bfloat16)
+        if more is None
+        else [array] * count,
+        grid_spec=pltpu.PrefetchScalarGridSpec(
+            num_scalar_prefetch=1,
+            grid=(count * tiles,),
+            in_specs=[
+                pl.BlockSpec((rows, depth), lambda i, at: (0, 0)),
+                pl.BlockSpec((depth, tile), lambda i, at: (0, at[i // tiles] * tiles + i % tiles)),
+            ]
+            + ([] if more is None else [stack])
+            + [ANYWHERE] * len(after),
+            out_specs=stack if more is None else [column(number) for number in range(count)],
+        ),
+        compiler_params=pltpu.CompilerParams(vmem_limit_bytes=24 * 2**20),
+        cost_estimate=COST,
+        name="projection_blocks",
+    )(
+        jnp.stack(blocks).astype(jnp.int32),
+        data,
+        in_hbm(out_weight),
+        *(() if more is None else (more,)),
+        *after,
+    )
+
+
+def cotangent_kernel(count, first, last, _, weight_ref, *refs):
+    blocks, refs = refs[:count], refs[count:]
+    step = pl.program_id(0)
+    total = refs[-1]
+
+    @pl.when(step == 0)
+    def _():
+        total[...] = jnp.zeros_like(total) if first else refs[0][...]
+
+    for number, block in enumerate(blocks):
+
+        @pl.when(step == number)
+        def _(block=block):
+            total[...] += lax.dot_general(
+                block[...], weight_ref[...], NT, preferred_element_type=jnp.float32
+            )
+
+    if last:
+        conv_ref, query_ref = refs[1:3]
+        grad_ref, cot_ref = refs[-3:-1]
+
+        @pl.when(step == count - 1)
+        def _():
+            dgated = wide(total[...].astype(jnp.bfloat16))
+            grad_ref[...] = (dgated * wide(conv_ref[...])).astype(jnp.bfloat16)
+            cot_ref[...] = (dgated * wide(query_ref[...])).astype(jnp.bfloat16)
+
+
+def cotangent_products(blocks, places, out_weight, start=None, gates=(), after=()):
+    rows, width = blocks[0].shape
+    channels = out_weight.shape[0]
+    count = len(blocks)
+    whole = pl.BlockSpec((rows, channels), lambda i, at: (0, 0))
+    part = pl.BlockSpec((rows, width), lambda i, at: (0, 0))
+    array = jax.ShapeDtypeStruct((rows, channels), jnp.bfloat16)
+    first, last = start is None, bool(gates)
+    extra = (() if first else (start,)) + tuple(gates)
+    return pl.pallas_call(
+        functools.partial(cotangent_kernel, count, first, last),
+        out_shape=[array, array] if last else jax.ShapeDtypeStruct((rows, channels), jnp.float32),
+        grid_spec=pltpu.PrefetchScalarGridSpec(
+            num_scalar_prefetch=1,
+            grid=(count,),
+            in_specs=[pl.BlockSpec((channels, width), lambda i, at: (0, at[i]))]
+            + [part] * count
+            + [whole] * len(extra)
+            + [ANYWHERE] * len(after),
+            out_specs=[whole, whole] if last else whole,
+            scratch_shapes=[pltpu.VMEM((rows, channels), jnp.float32)] if last else [],
+        ),
+        compiler_params=pltpu.CompilerParams(vmem_limit_bytes=24 * 2**20),
+        cost_estimate=COST,
+        name="cotangent_blocks",
+    )(jnp.stack(places).astype(jnp.int32), in_hbm(out_weight), *blocks, *extra, *after)
+
+
+OWN, NEAR, MIDDLE, FAR = (0, 1, 2, 3), (1, 0, 3, 2), (2, 2, 1, 1), (3, 3, 0, 0)
+
+
+def added(*arrays):
+    return sum(wide(array) for array in arrays).astype(jnp.bfloat16)
+
+
+def line_scatter(data, out_weight, width, before, later):
+    place = lax.axis_index("tp")
+    chip, core = place // 2, place % 2
+
+    def share(tables, before, later=()):
+        sources = [2 * of_chip(chip, table) for table in tables]
+        given = column_products(
+            data, out_weight, [at + 1 - core for at in sources], width, after=before
+        )
+        more = swapped(given, "tp", 1)
+        return column_products(
+            data, out_weight, [at + core for at in sources], width, more, after=later
+        )
+
+    (first,) = share((FAR,), before, later)
+    one = hop(first, INWARD)
+    second, third, own = share((MIDDLE, NEAR, OWN), (first,))
+    two_b = hop(second, INWARD)
+    through = added(first, one)
+    two_a = hop(through, ACROSS)
+
+    def ready(after):
+        across, inward = held_until([two_a, two_b], after)
+        return added(third, across), added(second, inward)
+
+    def rest(final, onward):
+        return added(own, hop(final, OUTWARD + INWARD), hop(onward, ACROSS))
+
+    return own, through, ready, rest
+
+
+def line_cotangents(block, table, out_weight, start=None, gates=(), after=()):
+    place = lax.axis_index("tp")
+    core = place % 2
+    source = 2 * of_chip(place // 2, table)
+    places = (source + core, source + 1 - core)
+    parts = (block, swapped(block, "tp", 1))
+    return cotangent_products(parts, places, out_weight, start, gates, after)
+
+
+def packed_parts(position, key_gate, value_input, filter_taps, members, scale):
+    length, channels = key_gate.shape
+    share = channels // members
+    product_in = (wide(key_gate) * wide(value_input)).astype(jnp.bfloat16)
+    tap_rows = (filter_taps * scale).astype(jnp.bfloat16).T
+    owned = filter_taps.shape[1] // members
+    chunks = length // share
+    packed = []
+    pieces = cut(product_in, position, members, 1)
+    for piece, taps in zip(pieces, cut(tap_rows, position, members, 0)):
+        taps = taps.reshape(owned, chunks, share).transpose(1, 0, 2)
+        taps = jnp.pad(taps, ((0, 0), (0, padded(owned) - owned), (0, 0)))
+        packed.append(jnp.concatenate([piece, taps.reshape(-1, share)], axis=0))
+    return packed
+
+
+def unpacked_parts(position, parts, key_gate, value_input, groups):
+    length, channels = key_gate.shape
+    members = len(parts)
+    share = channels // members
+    owned = groups // members
+    chunks = length // share
+    input_grad = wide(joined([part[:length] for part in parts], position, 1))
+    filter_parts = [
+        part[length:]
+        .reshape(chunks, padded(owned), share)[:, :owned]
+        .transpose(1, 0, 2)
+        .reshape(owned, length)
+        for part in parts
+    ]
+    grad_filter = wide(joined(filter_parts, position, 0)).T
+    grad_key = (input_grad * wide(value_input)).astype(jnp.bfloat16)
+    grad_value = (input_grad * wide(key_gate)).astype(jnp.bfloat16)
+    return grad_key, grad_value, grad_filter
+
+
 def local(query_gate, key_gate, value_input, filter_taps, out_weight, out_grad):
     length, channels = query_gate.shape
     groups = filter_taps.shape[1]
@@ -249,32 +570,57 @@
     position = lax.axis_index("ctx")
     at = position.reshape((1,)).astype(jnp.int32)
     tap_scale = 1.0 / math.sqrt(length * members)
-
-    all_cotangents = lax.all_gather(out_grad, "tp", axis=1, tiled=True)
-    tap_rows = (filter_taps * tap_scale).astype(jnp.bfloat16).T
-    tap_parts = [wide(p) for p in traded(cut(tap_rows, position, members, 0), "ctx")]
-    product_in = (wide(key_gate) * wide(value_input)).astype(jnp.bfloat16)
-    input_parts = traded(cut(product_in, position, members, 1), "ctx")
-    conv_parts = traded(convolve(at, input_parts, tap_parts, per_group), "ctx")
+    share = channels // members
+    in_line = lax.axis_size("tp") == 8
+
+    if in_line:
+        near, cross = hop(out_grad, INWARD + OUTWARD), hop(out_grad, ACROSS)
+        total = line_cotangents(out_grad, OWN, out_weight)
+    in_tiles = share % 128 == 0 and groups // members % 16 == 0
+    if in_tiles:
+        packed = prepare(at, key_gate, value_input, filter_taps, members, tap_scale)
+    else:
+        packed = packed_parts(position, key_gate, value_input, filter_taps, members, tap_scale)
+    input_parts = traded(packed, "ctx")
+    conv_parts = convolve(at, input_parts, length, per_group, (total,) if in_line else ())
+    if in_line:
+        *conv_parts, near, cross = held_until([*conv_parts, near, cross], ())
+    conv_parts = traded(conv_parts, "ctx")
     convolved = joined(conv_parts, position, 1)
     gated_out = (wide(query_gate) * wide(convolved)).astype(jnp.bfloat16)
-    partial_value = jnp.dot(gated_out, out_weight, preferred_element_type=jnp.float32)
-    projected = lax.psum_scatter(
-        partial_value.astype(jnp.bfloat16), "tp", scatter_dimension=1, tiled=True
-    )
-    dgated = jnp.einsum(
-        "tk,ck->tc", all_cotangents, out_weight, preferred_element_type=jnp.float32
-    ).astype(jnp.bfloat16)
-    grad_query = (wide(dgated) * wide(convolved)).astype(jnp.bfloat16)
-    conv_grad = (wide(dgated) * wide(query_gate)).astype(jnp.bfloat16)
+    if in_line:
+        far, skip = hop(near, ACROSS), hop(cross, OUTWARD)
+        total = line_cotangents(near, NEAR, out_weight, total)
+        own, through, ready, rest = line_scatter(
+            gated_out, out_weight, channels, (total,), (far, skip)
+        )
+        total = line_cotangents(added(cross, skip), MIDDLE, out_weight, total)
+        (last,) = held_until([hop(far, OUTWARD)], (own,))
+        grad_query, conv_grad = line_cotangents(
+            added(far, last), FAR, out_weight, total, (convolved, query_gate), (through,)
+        )
+    else:
+        partial_value = jnp.dot(gated_out, out_weight, preferred_element_type=jnp.float32)
+        projected = lax.psum_scatter(
+            partial_value.astype(jnp.bfloat16), "tp", scatter_dimension=1, tiled=True
+        )
+        dgated = jnp.einsum(
+            "tk,ck->tc",
+            lax.all_gather(out_grad, "tp", axis=1, tiled=True),
+            out_weight,
+            preferred_element_type=jnp.float32,
+        ).astype(jnp.bfloat16)
+        grad_query = (wide(dgated) * wide(convolved)).astype(jnp.bfloat16)
+        conv_grad = (wide(dgated) * wide(query_gate)).astype(jnp.bfloat16)
     grad_parts = traded(cut(conv_grad, position, members, 1), "ctx")
-    back_parts, filter_parts = correlate(
-        at, input_parts, grad_parts, tap_parts, per_group, tap_scale
-    )
-    input_grad = wide(joined(traded(back_parts, "ctx"), position, 1))
-    grad_filter = joined(traded(filter_parts, "ctx"), position, 0).T
-    grad_key = (input_grad * wide(value_input)).astype(jnp.bfloat16)
-    grad_value = (input_grad * wide(key_gate)).astype(jnp.bfloat16)
+    arrived = ready(tuple(grad_parts[1:])) if in_line else ()
+    back_parts = correlate(at, input_parts, grad_parts, per_group, tap_scale, arrived)
+    if in_line:
+        projected = rest(*arrived)
+    back_parts = traded(back_parts, "ctx")
+    unpack = finished if in_tiles else unpacked_parts
+    arguments = (at if in_tiles else position, back_parts, key_gate, value_input, groups)
+    grad_key, grad_value, grad_filter = unpack(*arguments)
     return (projected, grad_query, grad_key, grad_value, grad_filter)
 
 

time: 192 us -> 187 us (0.974)
  Pallas kernels: 19.8 us -> 68.1 us
  waiting for transfers between devices: 95.6 us -> 50.8 us
  matrix products: 32.6 us -> 0 us
  local copies, waits for them, and re-layouts: 0.79 us -> 16.3 us
  between operations: 14.3 us -> 1.11 us
  starting transfers between devices: 25 us -> 38.1 us
  other arithmetic: 4.11 us -> 11.4 us
    pallas_call x1 -> x14, Pallas kernels: 7.38 us -> 55.6 us  [the longest x4 24.2 us: column_products(): pl.pallas_call(given_kernel if more is None else functools.partial(kept_k...]
    dot_general x2 -> x0, matrix products: 32.6 us -> none  [the longest x1 16.9 us: local(): jnp.dot(gated_out, out_weight, preferred_element_type=jnp.float32)]
    reduce_scatter x1 -> x0, waiting for transfers between devices: 27.8 us -> none  [local(): lax.psum_scatter(partial_value.astype(jnp.bfloat16), 'tp', scatter_dimens...]
    all_gather x1 -> x0, waiting for transfers between devices: 26.2 us -> none  [local(): all_cotangents = lax.all_gather(out_grad, 'tp', axis=1, tiled=True)]
    ppermute x0 -> x10, starting transfers between devices: none -> 23.3 us  [hop(): lax.ppermute(array, 'tp', [(2 * i + core, 2 * j + core) for i, j in pairs...]
    ppermute x0 -> x10, waiting for transfers between devices: none -> 21.5 us  [hop(): lax.ppermute(array, 'tp', [(2 * i + core, 2 * j + core) for i, j in pairs...]
    unnamed x10 -> x82, local copies, waits for them, and re-layouts: 0.03 us -> 14.9 us
    ppermute x18, waiting for transfers between devices: 40.9 us -> 29.4 us  [swapped(): return lax.ppermute(array, axis, [(i, i ^ step) for i in range(size)])]
  transfers between devices with their start and end apart: 20 -> 28, of which waited for: 11 -> 13; matrix products, arithmetic and copies ran while one was open for 20% -> 5% of each run, Pallas kernels for 10% -> 30%
where the time goes in v4:
time: 187 us; the launch traced here: 186 us
  Pallas kernels  68.1 us (36%)
  waiting for transfers between devices  50.8 us (27%)
  starting transfers between devices  38.1 us (20%)
  local copies, waits for them, and re-layouts  16.3 us (9%)
  other arithmetic  11.4 us (6%)
    ppermute x18, waiting for transfers between devices, swapped(): return lax.ppermute(array, axis, [(i, i ^ step) for i in range(size)])  29.4 us
    pallas_call x4, Pallas kernels, column_products(): pl.pallas_call(given_kernel if more is None else functools.partial(kept_k...  24.2 us
    ppermute x10, starting transfers between devices, hop(): lax.ppermute(array, 'tp', [(2 * i + core, 2 * j + core) for i, j in pairs...  23.3 us
    ppermute x10, waiting for transfers between devices, hop(): lax.ppermute(array, 'tp', [(2 * i + core, 2 * j + core) for i, j in pairs...  21.5 us
    pallas_call x4, Pallas kernels, cotangent_products(): pl.pallas_call(functools.partial(cotangent_kernel, count, first, last), o...  21.3 us
    unnamed x82, local copies, waits for them, and re-layouts  14.9 us
    ppermute x18, starting transfers between devices, swapped(): return lax.ppermute(array, axis, [(i, i ^ step) for i in range(size)])  14.8 us
    pallas_call x1, Pallas kernels, correlate(): pl.pallas_call(functools.partial(backward_kernel, members, per_group, sca...  12.4 us
  transfers between devices with their start and end apart: 28, of which 13 were waited for; matrix products, arithmetic and copies ran while one was open for 5% of the time, Pallas kernels for 30%

profile of v4, /device:TPU:0, one launch (start us, length us, event | category | flops | bytes accessed | tf_op | source)
XLA Modules:
  0.0 185.8 jit_solution(7854781823938814623)
XLA Ops:
  1.1 2.7 %collective-permute-start.4 = (bf16[512,1024]{1,0:T(8,128)(2,1)}, bf16[512,1024]{1,0:T(8,128)(2,1)S(1)}, u32[]{:S(2)}, u32[]{:S(2)}) collective-permute-start(bf16[512,1024]{1,0:T(8,128)(2,1)} %refs_0_.1), channel_id=1, source_target_pairs={{0,2},{1,3},{6,4},{7,5},{2,0},{3,1},{4,6},{5,7},{8,10},{9,11},{14,... | collective-permute-start | bytes 3145736 | tf_op jit(solution)/shard_map/ppermute | solution.py:333
  13.4 5.0 %cotangent_blocks.4.refs_4_.refs_2_ = f32[512,1024]{1,0:T(8,128)S(1)} custom-call(s32[2]{0:T(128)S(1)} %pad_add_fusion.1._, bf16[1024,8192]{1,0:T(8,128)(2,1)} %weight_ref.15, bf16[512,1024]{1,0:T(8,128)(2,1)S(1)} %copy-done.20, bf16[512,1024]{1,0:T(8,128)(2,1)} %collective-permute-done.3.refs_1_), custom_call_target="tpu_custom_call" | custom-call | flops 1048576 | bytes 4096 | tf_op jit(solution)/shard_map/cotangent_blocks/pallas_call | solution.py:463
  19.5 6.4 %collective-permute-done.1.refs_2_ = bf16[544,256]{1,0:T(8,128)(2,1)S(1)} collective-permute-done((bf16[544,256]{1,0:T(8,128)(2,1)}, bf16[544,256]{1,0:T(8,128)(2,1)S(1)}, u32[]{:S(2)}, u32[]{:S(2)}) %collective-permute-start.1) | collective-permute-done | bytes 278560 | tf_op jit(solution)/shard_map/ppermute | solution.py:300
  26.0 7.4 %causal_conv.1 = (bf16[512,256]{1,0:T(8,128)(2,1)S(1)}, bf16[512,256]{1,0:T(8,128)(2,1)S(1)}, bf16[512,256]{1,0:T(8,128)(2,1)S(1)}, bf16[512,256]{1,0:T(8,128)(2,1)S(1)}) custom-call(s32[1]{0:T(128)} %bitcast.3.pos_ref, bf16[544,256]{1,0:T(8,128)(2,1)S(1)} %get-tuple-element.33.refs_0_, bf16[544,256]{1,0:T(8,128)(2,1)S(1)} %collective-permute-done.refs_1_, ...), custom_call_target="tpu_custom_call" | custom-call | flops 1048576 | bytes 4096 | tf_op jit(solution)/shard_map/causal_conv/pallas_call | solution.py:180
  45.0 2.9 %collective-permute-done.6 = bf16[512,256]{1,0:T(8,128)(2,1)S(1)} collective-permute-done((bf16[512,256]{1,0:T(8,128)(2,1)}, bf16[512,256]{1,0:T(8,128)(2,1)S(1)}, u32[]{:S(2)}, u32[]{:S(2)}) %collective-permute-start.6) | collective-permute-done | bytes 262176 | tf_op jit(solution)/shard_map/ppermute | solution.py:300
  49.3 3.3 %collective-permute-done.7 = bf16[512,256]{1,0:T(8,128)(2,1)S(1)} collective-permute-done((bf16[512,256]{1,0:T(8,128)(2,1)}, bf16[512,256]{1,0:T(8,128)(2,1)S(1)}, u32[]{:S(2)}, u32[]{:S(2)}) %collective-permute-start.7) | collective-permute-done | bytes 262176 | tf_op jit(solution)/shard_map/ppermute | solution.py:300
  57.3 4.8 %cotangent_blocks.5.refs_0_.refs_2_ = f32[512,1024]{1,0:T(8,128)S(1)} custom-call(s32[2]{0:T(128)S(1)} %pad_add_fusion.3._, bf16[1024,8192]{1,0:T(8,128)(2,1)} %weight_ref.15, bf16[512,1024]{1,0:T(8,128)(2,1)S(1)} %copy-done.5, bf16[512,1024]{1,0:T(8,128)(2,1)S(1)} %copy-done.22, f32[512,1024]{1,0:T(8,128)S(1)} %copy-done.1), custom_call_target="tpu_custom_call" | custom-call | flops 1048576 | bytes 4096 | tf_op jit(solution)/shard_map/cotangent_blocks/pallas_call | solution.py:463
  62.1 3.5 %projection_blocks.4 = bf16[1,512,1024]{2,1,0:T(8,128)(2,1)} custom-call(s32[1]{0:T(128)} %bitcast.9._, bf16[512,1024]{1,0:T(8,128)(2,1)S(1)} %multiply_convert_fusion.data_ref, bf16[1024,8192]{1,0:T(8,128)(2,1)} %weight_ref.15, f32[512,1024]{1,0:T(8,128)S(1)} %cotangent_blocks.5.refs_0_.refs_2_), custom_call_target="tpu_custom_call" | custom-call | flops 1048576 | bytes 4096 | tf_op jit(solution)/shard_map/projection_blocks/pallas_call | solution.py:398
  65.7 9.6 %collective-permute-done.12.refs_1_ = bf16[512,1024]{1,0:T(8,128)(2,1)} collective-permute-done((bf16[512,1024]{1,0:T(8,128)(2,1)}, bf16[512,1024]{1,0:T(8,128)(2,1)}, u32[]{:S(2)}, u32[]{:S(2)}) %collective-permute-start.12) | collective-permute-done | bytes 1048608 | tf_op jit(solution)/shard_map/ppermute | solution.py:333
  75.3 3.8 %projection_blocks.5.refs_0_ = bf16[512,1024]{1,0:T(8,128)(2,1)} custom-call(s32[1]{0:T(128)} %bitcast.8._, bf16[512,1024]{1,0:T(8,128)(2,1)S(1)} %multiply_convert_fusion.data_ref, bf16[1024,8192]{1,0:T(8,128)(2,1)} %weight_ref.15, bf16[1,512,1024]{2,1,0:T(8,128)(2,1)} %collective-permute-done.10.more_ref, ...), custom_call_target="tpu_custom_call" | custom-call | flops 1048576 | bytes 4096 | tf_op jit(solution)/shard_map/projection_blocks/pallas_call | solution.py:398
  79.1 8.5 %projection_blocks.6 = bf16[3,512,1024]{2,1,0:T(8,128)(2,1)} custom-call(s32[3]{0:T(128)S(1)} %pad_add_fusion.2._, bf16[512,1024]{1,0:T(8,128)(2,1)S(1)} %multiply_convert_fusion.data_ref, bf16[1024,8192]{1,0:T(8,128)(2,1)} %weight_ref.15, bf16[512,1024]{1,0:T(8,128)(2,1)} %projection_blocks.5.refs_0_), custom_call_target="tpu_custom_call" | custom-call | flops 1048576 | bytes 4096 | tf_op jit(solution)/shard_map/projection_blocks/pallas_call | solution.py:398
  88.9 6.6 %collective-permute-start.14 = (bf16[512,1024]{1,0:T(8,128)(2,1)}, bf16[512,1024]{1,0:T(8,128)(2,1)}, u32[]{:S(2)}, u32[]{:S(2)}) collective-permute-start(bf16[512,1024]{1,0:T(8,128)(2,1)} %projection_blocks.5.refs_0_), channel_id=1, source_target_pairs={{0,2},{1,3},{6,4},{7,5},{8,10},{9,11},{14,12},{15,13},{16,18},{17,... | collective-permute-start | bytes 3145736 | tf_op jit(solution)/shard_map/ppermute | solution.py:333
  95.5 2.9 %add_convert_fusion.3.refs_0_ = bf16[512,1024]{1,0:T(8,128)(2,1)} fusion(bf16[512,1024]{1,0:T(8,128)(2,1)} %collective-permute-done.12.refs_1_, bf16[512,1024]{1,0:T(8,128)(2,1)} %get-tuple-element.46), kind=kLoop, calls=%fused_computation.3 | loop fusion | flops 2097152 | bytes 3145728 | tf_op jit(solution)/shard_map/convert_element_type | solution.py:486
  98.5 8.4 %projection_blocks.7 = (bf16[512,1024]{1,0:T(8,128)(2,1)S(1)}, bf16[512,1024]{1,0:T(8,128)(2,1)S(1)}, bf16[512,1024]{1,0:T(8,128)(2,1)S(1)}) custom-call(s32[3]{0:T(128)S(1)} %pad_add_fusion._, bf16[512,1024]{1,0:T(8,128)(2,1)S(1)} %multiply_convert_fusion.data_ref, bf16[1024,8192]{1,0:T(8,128)(2,1)} %weight_ref.15, ...), custom_call_target="tpu_custom_call" | custom-call | flops 1048576 | bytes 4096 | tf_op jit(solution)/shard_map/projection_blocks/pallas_call | solution.py:398
  109.8 5.6 %collective-permute-done.17.refs_0_ = bf16[512,1024]{1,0:T(8,128)(2,1)} collective-permute-done((bf16[512,1024]{1,0:T(8,128)(2,1)}, bf16[512,1024]{1,0:T(8,128)(2,1)}, u32[]{:S(2)}, u32[]{:S(2)}) %collective-permute-start.17) | collective-permute-done | bytes 1048608 | tf_op jit(solution)/shard_map/ppermute | solution.py:333
  117.6 2.0 %add_convert_fusion.5.refs_5_ = bf16[512,1024]{1,0:T(8,128)(2,1)S(1)} fusion(bf16[512,1024]{1,0:T(8,128)(2,1)} %collective-permute-done.14, bf16[512,1024]{1,0:T(8,128)(2,1)} %projection_blocks.5.refs_0_), kind=kLoop, calls=%fused_computation.5 | loop fusion | flops 2097152 | bytes 3145728 | tf_op jit(solution)/shard_map/convert_element_type | solution.py:486
  120.3 6.5 %collective-permute-start.16 = (bf16[512,1024]{1,0:T(8,128)(2,1)S(1)}, bf16[512,1024]{1,0:T(8,128)(2,1)S(1)}, u32[]{:S(2)}, u32[]{:S(2)}) collective-permute-start(bf16[512,1024]{1,0:T(8,128)(2,1)S(1)} %copy-done.26), channel_id=1, source_target_pairs={{0,2},{1,3},{6,4},{7,5},{8,10},{9,11},{14,12},{15,13},{16,18},{17,... | collective-permute-start | bytes 3145736 | tf_op jit(solution)/shard_map/ppermute | solution.py:333
  127.0 5.4 %cotangent_blocks.6.refs_2_ = f32[512,1024]{1,0:T(8,128)S(1)} custom-call(s32[2]{0:T(128)S(1)} %pad_add_fusion.5._, bf16[1024,8192]{1,0:T(8,128)(2,1)} %weight_ref.15, bf16[512,1024]{1,0:T(8,128)(2,1)} %add_convert_fusion.3.refs_0_, bf16[512,1024]{1,0:T(8,128)(2,1)} %collective-permute-done.19.refs_1_, f32[512,1024]{1,0:T(8,128)S(1)} %cotangent_blocks.5.refs_0_.refs_2_), custom_call_target="tpu_custom_call" | custom-call | flops 1048576 | bytes 4096 | tf_op jit(solution)/shard_map/cotangent_blocks/pallas_call | solution.py:463
  132.4 6.0 %cotangent_blocks.7 = (bf16[512,1024]{1,0:T(8,128)(2,1)}, bf16[512,1024]{1,0:T(8,128)(2,1)S(1)}) custom-call(s32[2]{0:T(128)S(1)} %pad_add_fusion.4._, bf16[1024,8192]{1,0:T(8,128)(2,1)} %weight_ref.15, bf16[512,1024]{1,0:T(8,128)(2,1)S(1)} %add_convert_fusion.4.refs_0_, bf16[512,1024]{1,0:T(8,128)(2,1)S(1)} %collective-permute-done.18.refs_1_, ...), custom_call_target="tpu_custom_call" | custom-call | flops 1048576 | bytes 4096 | tf_op jit(solution)/shard_map/cotangent_blocks/pallas_call | solution.py:463
  142.2 6.1 %collective-permute-done.16.refs_1_ = bf16[512,1024]{1,0:T(8,128)(2,1)S(1)} collective-permute-done((bf16[512,1024]{1,0:T(8,128)(2,1)S(1)}, bf16[512,1024]{1,0:T(8,128)(2,1)S(1)}, u32[]{:S(2)}, u32[]{:S(2)}) %collective-permute-start.16) | collective-permute-done | bytes 1048608 | tf_op jit(solution)/shard_map/ppermute | solution.py:333
  148.2 2.4 %collective-permute-done.21.refs_3_.refs_6_ = bf16[512,256]{1,0:T(8,128)(2,1)S(1)} collective-permute-done((bf16[512,256]{1,0:T(8,128)(2,1)S(1)}, bf16[512,256]{1,0:T(8,128)(2,1)S(1)}, u32[]{:S(2)}, u32[]{:S(2)}) %collective-permute-start.21) | collective-permute-done | bytes 262176 | tf_op jit(solution)/shard_map/ppermute | solution.py:300
  156.2 12.4 %causal_conv_grads.1 = (bf16[544,256]{1,0:T(8,128)(2,1)S(1)}, bf16[544,256]{1,0:T(8,128)(2,1)S(1)}, bf16[544,256]{1,0:T(8,128)(2,1)S(1)}, bf16[544,256]{1,0:T(8,128)(2,1)S(1)}) custom-call(s32[1]{0:T(128)} %bitcast.3.pos_ref, bf16[544,256]{1,0:T(8,128)(2,1)S(1)} %get-tuple-element.33.refs_0_, bf16[544,256]{1,0:T(8,128)(2,1)S(1)} %copy-done.15, ...), custom_call_target="tpu_custom_call" | custom-call | flops 1048576 | bytes 4096 | tf_op jit(solution)/shard_map/causal_conv_grads/pallas_call | solution.py:201
  172.3 6.0 %collective-permute-done.25.refs_1_ = bf16[544,256]{1,0:T(8,128)(2,1)S(1)} collective-permute-done((bf16[544,256]{1,0:T(8,128)(2,1)S(1)}, bf16[544,256]{1,0:T(8,128)(2,1)S(1)}, u32[]{:S(2)}, u32[]{:S(2)}) %collective-permute-start.25) | collective-permute-done | bytes 278560 | tf_op jit(solution)/shard_map/ppermute | solution.py:300
  178.2 4.2 %collective-permute-done.26.refs_2_ = bf16[544,256]{1,0:T(8,128)(2,1)S(1)} collective-permute-done((bf16[544,256]{1,0:T(8,128)(2,1)S(1)}, bf16[544,256]{1,0:T(8,128)(2,1)S(1)}, u32[]{:S(2)}, u32[]{:S(2)}) %collective-permute-start.26) | collective-permute-done | bytes 278560 | tf_op jit(solution)/shard_map/ppermute | solution.py:300
  (148 shorter events, 52.4 us)
Async XLA Ops:
  0.6 12.2 %collective-permute-start.3 = (bf16[512,1024]{1,0:T(8,128)(2,1)}, bf16[512,1024]{1,0:T(8,128)(2,1)}, u32[]{:S(2)}, u32[]{:S(2)}) collective-permute-start(bf16[512,1024]{1,0:T(8,128)(2,1)} %refs_0_.1), channel_id=1, source_target_pairs={{0,1},{1,0},{2,3},{3,2},{4,5},{5,4},{6,7},{7,6},{8,9},{9,8},{10,11... | collective-permute-start | bytes 3145736 | tf_op jit(solution)/shard_map/ppermute | solution.py:300
  1.1 36.3 %collective-permute-start.4 = (bf16[512,1024]{1,0:T(8,128)(2,1)}, bf16[512,1024]{1,0:T(8,128)(2,1)S(1)}, u32[]{:S(2)}, u32[]{:S(2)}) collective-permute-start(bf16[512,1024]{1,0:T(8,128)(2,1)} %refs_0_.1), channel_id=1, source_target_pairs={{0,2},{1,3},{6,4},{7,5},{2,0},{3,1},{4,6},{5,7},{8,10},{9,11},{14,... | collective-permute-start | bytes 3145736 | tf_op jit(solution)/shard_map/ppermute | solution.py:333
  3.8 33.7 %collective-permute-start.5 = (bf16[512,1024]{1,0:T(8,128)(2,1)}, bf16[512,1024]{1,0:T(8,128)(2,1)}, u32[]{:S(2)}, u32[]{:S(2)}) collective-permute-start(bf16[512,1024]{1,0:T(8,128)(2,1)} %refs_0_.1), channel_id=1, source_target_pairs={{2,4},{3,5},{4,2},{5,3},{10,12},{11,13},{12,10},{13,11},{18,20},{1... | collective-permute-start | bytes 3145736 | tf_op jit(solution)/shard_map/ppermute | solution.py:333
  9.8 9.7 %collective-permute-start = (bf16[544,256]{1,0:T(8,128)(2,1)}, bf16[544,256]{1,0:T(8,128)(2,1)S(1)}, u32[]{:S(2)}, u32[]{:S(2)}) collective-permute-start(bf16[544,256]{1,0:T(8,128)(2,1)} %get-tuple-element.34), channel_id=1, source_target_pairs={{0,8},{8,0},{16,24},{24,16},{1,9},{9,1},{17,25},{25,17},{2,10},{10... | collective-permute-start | bytes 835592 | tf_op jit(solution)/shard_map/ppermute | solution.py:300
  11.3 14.6 %collective-permute-start.1 = (bf16[544,256]{1,0:T(8,128)(2,1)}, bf16[544,256]{1,0:T(8,128)(2,1)S(1)}, u32[]{:S(2)}, u32[]{:S(2)}) collective-permute-start(bf16[544,256]{1,0:T(8,128)(2,1)} %get-tuple-element.35), channel_id=1, source_target_pairs={{0,16},{8,24},{16,0},{24,8},{1,17},{9,25},{17,1},{25,9},{2,18},{10... | collective-permute-start | bytes 835592 | tf_op jit(solution)/shard_map/ppermute | solution.py:300
  12.8 13.1 %collective-permute-start.2 = (bf16[544,256]{1,0:T(8,128)(2,1)S(1)}, bf16[544,256]{1,0:T(8,128)(2,1)S(1)}, u32[]{:S(2)}, u32[]{:S(2)}) collective-permute-start(bf16[544,256]{1,0:T(8,128)(2,1)S(1)} %get-tuple-element.36), channel_id=1, source_target_pairs={{0,24},{8,16},{16,8},{24,0},{1,25},{9,17},{17,9},{25,1},{2,26},{10... | collective-permute-start | bytes 835592 | tf_op jit(solution)/shard_map/ppermute | solution.py:300
  38.5 16.6 %collective-permute-start.9 = (bf16[512,1024]{1,0:T(8,128)(2,1)}, bf16[512,1024]{1,0:T(8,128)(2,1)S(1)}, u32[]{:S(2)}, u32[]{:S(2)}) collective-permute-start(bf16[512,1024]{1,0:T(8,128)(2,1)} %get-tuple-element.45.refs_0_), channel_id=1, source_target_pairs={{0,1},{1,0},{2,3},{3,2},{4,5},{5,4},{6,7},{7,6},{8,9},{9,8},{10,11... | collective-permute-start | bytes 3145736 | tf_op jit(solution)/shard_map/ppermute | solution.py:300
  39.9 12.7 %collective-permute-start.7 = (bf16[512,256]{1,0:T(8,128)(2,1)}, bf16[512,256]{1,0:T(8,128)(2,1)S(1)}, u32[]{:S(2)}, u32[]{:S(2)}) collective-permute-start(bf16[512,256]{1,0:T(8,128)(2,1)} %get-tuple-element.43), channel_id=1, source_target_pairs={{0,16},{8,24},{16,0},{24,8},{1,17},{9,25},{17,1},{25,9},{2,18},{10... | collective-permute-start | bytes 786440 | tf_op jit(solution)/shard_map/ppermute | solution.py:300
  40.8 34.5 %collective-permute-start.11 = (bf16[512,1024]{1,0:T(8,128)(2,1)}, bf16[512,1024]{1,0:T(8,128)(2,1)}, u32[]{:S(2)}, u32[]{:S(2)}) collective-permute-start(bf16[512,1024]{1,0:T(8,128)(2,1)} %get-tuple-element.45.refs_0_), channel_id=1, source_target_pairs={{2,4},{3,5},{4,2},{5,3},{10,12},{11,13},{12,10},{13,11},{18,20},{1... | collective-permute-start | bytes 3145736 | tf_op jit(solution)/shard_map/ppermute | solution.py:333
  42.5 11.6 %collective-permute-start.8 = (bf16[512,256]{1,0:T(8,128)(2,1)}, bf16[512,256]{1,0:T(8,128)(2,1)S(1)}, u32[]{:S(2)}, u32[]{:S(2)}) collective-permute-start(bf16[512,256]{1,0:T(8,128)(2,1)} %get-tuple-element.44), channel_id=1, source_target_pairs={{0,24},{8,16},{16,8},{24,0},{1,25},{9,17},{17,9},{25,1},{2,26},{10... | collective-permute-start | bytes 786440 | tf_op jit(solution)/shard_map/ppermute | solution.py:300
  47.9 27.3 %collective-permute-start.12 = (bf16[512,1024]{1,0:T(8,128)(2,1)}, bf16[512,1024]{1,0:T(8,128)(2,1)}, u32[]{:S(2)}, u32[]{:S(2)}) collective-permute-start(bf16[512,1024]{1,0:T(8,128)(2,1)} %get-tuple-element.46), channel_id=1, source_target_pairs={{2,0},{3,1},{4,6},{5,7},{10,8},{11,9},{12,14},{13,15},{18,16},{19,... | collective-permute-start | bytes 3145736 | tf_op jit(solution)/shard_map/ppermute | solution.py:333
  87.6 10.9 %collective-permute-start.13 = (bf16[3,512,1024]{2,1,0:T(8,128)(2,1)}, bf16[3,512,1024]{2,1,0:T(8,128)(2,1)}, u32[]{:S(2)}, u32[]{:S(2)}) collective-permute-start(bf16[3,512,1024]{2,1,0:T(8,128)(2,1)} %projection_blocks.6), channel_id=1, source_target_pairs={{0,1},{1,0},{2,3},{3,2},{4,5},{5,4},{6,7},{7,6},{8,9},{9,8},{10,11... | collective-permute-start | bytes 9437192 | tf_op jit(solution)/shard_map/ppermute | solution.py:300
  87.6 27.8 %collective-permute-start.17 = (bf16[512,1024]{1,0:T(8,128)(2,1)}, bf16[512,1024]{1,0:T(8,128)(2,1)}, u32[]{:S(2)}, u32[]{:S(2)}) collective-permute-start(bf16[512,1024]{1,0:T(8,128)(2,1)} %collective-permute-done.11.refs_0_), channel_id=1, source_target_pairs={{2,0},{3,1},{4,6},{5,7},{10,8},{11,9},{12,14},{13,15},{18,16},{19,... | collective-permute-start | bytes 3145736 | tf_op jit(solution)/shard_map/ppermute | solution.py:333
  88.9 28.7 %collective-permute-start.14 = (bf16[512,1024]{1,0:T(8,128)(2,1)}, bf16[512,1024]{1,0:T(8,128)(2,1)}, u32[]{:S(2)}, u32[]{:S(2)}) collective-permute-start(bf16[512,1024]{1,0:T(8,128)(2,1)} %projection_blocks.5.refs_0_), channel_id=1, source_target_pairs={{0,2},{1,3},{6,4},{7,5},{8,10},{9,11},{14,12},{15,13},{16,18},{17,... | collective-permute-start | bytes 3145736 | tf_op jit(solution)/shard_map/ppermute | solution.py:333
  98.4 28.5 %collective-permute-start.19 = (bf16[512,1024]{1,0:T(8,128)(2,1)}, bf16[512,1024]{1,0:T(8,128)(2,1)}, u32[]{:S(2)}, u32[]{:S(2)}) collective-permute-start(bf16[512,1024]{1,0:T(8,128)(2,1)} %add_convert_fusion.3.refs_0_), channel_id=1, source_target_pairs={{0,1},{1,0},{2,3},{3,2},{4,5},{5,4},{6,7},{7,6},{8,9},{9,8},{10,11... | collective-permute-start | bytes 3145736 | tf_op jit(solution)/shard_map/ppermute | solution.py:300
  117.3 15.1 %collective-permute-start.18 = (bf16[512,1024]{1,0:T(8,128)(2,1)S(1)}, bf16[512,1024]{1,0:T(8,128)(2,1)S(1)}, u32[]{:S(2)}, u32[]{:S(2)}) collective-permute-start(bf16[512,1024]{1,0:T(8,128)(2,1)S(1)} %add_convert_fusion.4.refs_0_), channel_id=1, source_target_pairs={{0,1},{1,0},{2,3},{3,2},{4,5},{5,4},{6,7},{7,6},{8,9},{9,8},{10,11... | collective-permute-start | bytes 3145736 | tf_op jit(solution)/shard_map/ppermute | solution.py:300
  119.6 22.6 %collective-permute-start.15 = (bf16[512,1024]{1,0:T(8,128)(2,1)S(1)}, bf16[512,1024]{1,0:T(8,128)(2,1)S(1)}, u32[]{:S(2)}, u32[]{:S(2)}) collective-permute-start(bf16[512,1024]{1,0:T(8,128)(2,1)S(1)} %add_convert_fusion.5.refs_5_), channel_id=1, source_target_pairs={{2,4},{3,5},{4,2},{5,3},{10,12},{11,13},{12,10},{13,11},{18,20},{1... | collective-permute-start | bytes 3145736 | tf_op jit(solution)/shard_map/ppermute | solution.py:333
  120.3 27.9 %collective-permute-start.16 = (bf16[512,1024]{1,0:T(8,128)(2,1)S(1)}, bf16[512,1024]{1,0:T(8,128)(2,1)S(1)}, u32[]{:S(2)}, u32[]{:S(2)}) collective-permute-start(bf16[512,1024]{1,0:T(8,128)(2,1)S(1)} %copy-done.26), channel_id=1, source_target_pairs={{0,2},{1,3},{6,4},{7,5},{8,10},{9,11},{14,12},{15,13},{16,18},{17,... | collective-permute-start | bytes 3145736 | tf_op jit(solution)/shard_map/ppermute | solution.py:333
  139.9 10.8 %collective-permute-start.21 = (bf16[512,256]{1,0:T(8,128)(2,1)S(1)}, bf16[512,256]{1,0:T(8,128)(2,1)S(1)}, u32[]{:S(2)}, u32[]{:S(2)}) collective-permute-start(bf16[512,256]{1,0:T(8,128)(2,1)S(1)} %get-tuple-element.63), channel_id=1, source_target_pairs={{0,16},{8,24},{16,0},{24,8},{1,17},{9,25},{17,1},{25,9},{2,18},{10... | collective-permute-start | bytes 786440 | tf_op jit(solution)/shard_map/ppermute | solution.py:300
  140.7 11.6 %collective-permute-start.22 = (bf16[512,256]{1,0:T(8,128)(2,1)S(1)}, bf16[512,256]{1,0:T(8,128)(2,1)S(1)}, u32[]{:S(2)}, u32[]{:S(2)}) collective-permute-start(bf16[512,256]{1,0:T(8,128)(2,1)S(1)} %get-tuple-element.62), channel_id=1, source_target_pairs={{0,24},{8,16},{16,8},{24,0},{1,25},{9,17},{17,9},{25,1},{2,26},{10... | collective-permute-start | bytes 786440 | tf_op jit(solution)/shard_map/ppermute | solution.py:300
  155.3 28.9 %collective-permute-start.23 = (bf16[512,1024]{1,0:T(8,128)(2,1)S(1)}, bf16[512,1024]{1,0:T(8,128)(2,1)S(1)}, u32[]{:S(2)}, u32[]{:S(2)}) collective-permute-start(bf16[512,1024]{1,0:T(8,128)(2,1)S(1)} %add_convert_fusion.2.refs_8_), channel_id=1, source_target_pairs={{2,0},{3,1},{4,6},{5,7},{0,2},{1,3},{6,4},{7,5},{10,8},{11,9},{12,... | collective-permute-start | bytes 3145736 | tf_op jit(solution)/shard_map/ppermute | solution.py:333
  155.4 28.8 %collective-permute-start.24 = (bf16[512,1024]{1,0:T(8,128)(2,1)S(1)}, bf16[512,1024]{1,0:T(8,128)(2,1)S(1)}, u32[]{:S(2)}, u32[]{:S(2)}) collective-permute-start(bf16[512,1024]{1,0:T(8,128)(2,1)S(1)} %add_convert_fusion.1.refs_9_), channel_id=1, source_target_pairs={{2,4},{3,5},{4,2},{5,3},{10,12},{11,13},{12,10},{13,11},{18,20},{1... | collective-permute-start | bytes 3145736 | tf_op jit(solution)/shard_map/ppermute | solution.py:333
  170.2 12.2 %collective-permute-start.26 = (bf16[544,256]{1,0:T(8,128)(2,1)S(1)}, bf16[544,256]{1,0:T(8,128)(2,1)S(1)}, u32[]{:S(2)}, u32[]{:S(2)}) collective-permute-start(bf16[544,256]{1,0:T(8,128)(2,1)S(1)} %get-tuple-element.56), channel_id=1, source_target_pairs={{0,16},{8,24},{16,0},{24,8},{1,17},{9,25},{17,1},{25,9},{2,18},{10... | collective-permute-start | bytes 835592 | tf_op jit(solution)/shard_map/ppermute | solution.py:300
  171.7 10.7 %collective-permute-start.27 = (bf16[544,256]{1,0:T(8,128)(2,1)S(1)}, bf16[544,256]{1,0:T(8,128)(2,1)S(1)}, u32[]{:S(2)}, u32[]{:S(2)}) collective-permute-start(bf16[544,256]{1,0:T(8,128)(2,1)S(1)} %get-tuple-element.57), channel_id=1, source_target_pairs={{0,24},{8,16},{16,8},{24,0},{1,25},{9,17},{17,9},{25,1},{2,26},{10... | collective-permute-start | bytes 835592 | tf_op jit(solution)/shard_map/ppermute | solution.py:300
  (45 other events, 241.7 us)

commit v5 on v4

--- a/solution.py
+++ b/solution.py
@@ -217,40 +217,55 @@
     )(position, *inputs, *cotangents, *after)
 
 
-def prepare_kernel(members, scale, pos_ref, key_ref, value_ref, taps_ref, *refs):
-    outputs = refs
+def in_hbm(array):
+    return pltpu.with_memory_space_constraint(array, pltpu.HBM)
+
+
+def prepare_kernel(members, scale, pos_ref, key_ref, value_ref, taps_ref, *outputs):
     position = pos_ref[0]
-    width, channels = key_ref.shape
+    step_no = pl.program_id(0)
+    rows, channels = key_ref.shape
     share = channels // members
     groups = taps_ref.shape[0] // members
+    total_width = taps_ref.shape[1]
     for step in range(members):
         at = position ^ step
         columns = pl.ds(pl.multiple_of(at * share, share), share)
         product = key_ref[:, columns].astype(jnp.float32) * value_ref[:, columns].astype(
             jnp.float32
         )
-        outputs[step][:width] = product.astype(jnp.bfloat16)
-        taps = taps_ref[pl.ds(pl.multiple_of(at * groups, groups), groups), :]
-        taps = (taps * scale).astype(jnp.bfloat16)
-        for chunk in range(width // share):
-            outputs[step][width + chunk * groups : width + (chunk + 1) * groups, :] = taps[
-                :, chunk * share : (chunk + 1) * share
-            ]
+        here = pl.ds(pl.multiple_of(step_no * rows, rows), rows)
+        outputs[step][here, :] = product.astype(jnp.bfloat16)
+
+    @pl.when(step_no == 0)
+    def _():
+        for step in range(members):
+            at = position ^ step
+            taps = taps_ref[pl.ds(pl.multiple_of(at * groups, groups), groups), :]
+            taps = (taps * scale).astype(jnp.bfloat16)
+            for chunk in range(total_width // share):
+                start = total_width + chunk * groups
+                outputs[step][start : start + groups, :] = taps[
+                    :, chunk * share : (chunk + 1) * share
+                ]
 
 
 def prepare(position, key_gate, value_input, filter_taps, members, scale):
     width, channels = key_gate.shape
     share = channels // members
     rows = width + filter_taps.size // members // share
+    tile = width // 4
+    part = pl.BlockSpec((tile, channels), lambda i: (i, 0))
     return pl.pallas_call(
         functools.partial(prepare_kernel, members, scale),
         out_shape=[jax.ShapeDtypeStruct((rows, share), jnp.bfloat16)] * members,
-        in_specs=[SMEM] + [VMEM] * 3,
+        grid=(4,),
+        in_specs=[SMEM, part, part, pl.BlockSpec(filter_taps.shape[::-1], lambda i: (0, 0))],
         out_specs=[VMEM] * members,
         compiler_params=pltpu.CompilerParams(vmem_limit_bytes=24 * 2**20),
         cost_estimate=COST,
         name="gated_input",
-    )(position, key_gate, value_input, filter_taps.T)
+    )(position, in_hbm(key_gate), in_hbm(value_input), in_hbm(filter_taps.T))
 
 
 def finish_kernel(members, pos_ref, *refs):
@@ -350,10 +365,6 @@
     del refs
 
 
-def in_hbm(array):
-    return pltpu.with_memory_space_constraint(array, pltpu.HBM)
-
-
 def held_until(values, after):
     return pl.pallas_call(
         pass_kernel,
@@ -361,6 +372,7 @@
         in_specs=[ANYWHERE] * (len(values) + len(after)),
         out_specs=[ANYWHERE] * len(values),
         input_output_aliases={number: number for number in range(len(values))},
+        compiler_params=pltpu.CompilerParams(vmem_limit_bytes=2**20),
         cost_estimate=COST,
         name="held",
     )(*values, *after)
@@ -486,43 +498,46 @@
     return sum(wide(array) for array in arrays).astype(jnp.bfloat16)
 
 
-def line_scatter(data, out_weight, width, before, later):
+def line_scatter(data, out_weight, width, later):
     place = lax.axis_index("tp")
     chip, core = place // 2, place % 2
 
-    def share(tables, before, later=()):
-        sources = [2 * of_chip(chip, table) for table in tables]
-        given = column_products(
-            data, out_weight, [at + 1 - core for at in sources], width, after=before
-        )
-        more = swapped(given, "tp", 1)
-        return column_products(
-            data, out_weight, [at + core for at in sources], width, more, after=later
-        )
-
-    (first,) = share((FAR,), before, later)
+    def product(tables, other, more=None, after=()):
+        blocks = [2 * of_chip(chip, table) + other for table in tables]
+        return column_products(data, out_weight, blocks, width, more, after)
+
+    others = (MIDDLE, NEAR, OWN)
+    given = product((FAR,), 1 - core, after=later)
+    given_others = product(others, 1 - core, after=(given,))
+    (first,) = product((FAR,), core, swapped(given, "tp", 1), (given_others,))
     one = hop(first, INWARD)
-    second, third, own = share((MIDDLE, NEAR, OWN), (first,))
+    (given_others,) = held_until([given_others], (first,))
+    second, third, own = product(others, core, swapped(given_others, "tp", 1))
     two_b = hop(second, INWARD)
-    through = added(first, one)
-    two_a = hop(through, ACROSS)
-
-    def ready(after):
+
+    def passed(after):
+        (arrived,) = held_until([one], after)
+        through = added(first, arrived)
+        return through, hop(through, ACROSS)
+
+    def ready(two_a, after):
         across, inward = held_until([two_a, two_b], after)
         return added(third, across), added(second, inward)
 
     def rest(final, onward):
         return added(own, hop(final, OUTWARD + INWARD), hop(onward, ACROSS))
 
-    return own, through, ready, rest
-
-
-def line_cotangents(block, table, out_weight, start=None, gates=(), after=()):
+    return first, own, passed, ready, rest
+
+
+def line_cotangents(blocks, tables, out_weight, start=None, gates=(), after=()):
     place = lax.axis_index("tp")
     core = place % 2
-    source = 2 * of_chip(place // 2, table)
-    places = (source + core, source + 1 - core)
-    parts = (block, swapped(block, "tp", 1))
+    parts, places = [], []
+    for block, table in zip(blocks, tables):
+        source = 2 * of_chip(place // 2, table)
+        parts += [block, swapped(block, "tp", 1)]
+        places += [source + core, source + 1 - core]
     return cotangent_products(parts, places, out_weight, start, gates, after)
 
 
@@ -575,7 +590,7 @@
 
     if in_line:
         near, cross = hop(out_grad, INWARD + OUTWARD), hop(out_grad, ACROSS)
-        total = line_cotangents(out_grad, OWN, out_weight)
+        total = line_cotangents((out_grad,), (OWN,), out_weight)
     in_tiles = share % 128 == 0 and groups // members % 16 == 0
     if in_tiles:
         packed = prepare(at, key_gate, value_input, filter_taps, members, tap_scale)
@@ -590,14 +605,15 @@
     gated_out = (wide(query_gate) * wide(convolved)).astype(jnp.bfloat16)
     if in_line:
         far, skip = hop(near, ACROSS), hop(cross, OUTWARD)
-        total = line_cotangents(near, NEAR, out_weight, total)
-        own, through, ready, rest = line_scatter(
-            gated_out, out_weight, channels, (total,), (far, skip)
-        )
-        total = line_cotangents(added(cross, skip), MIDDLE, out_weight, total)
-        (last,) = held_until([hop(far, OUTWARD)], (own,))
+        first, own, passed, ready, rest = line_scatter(
+            gated_out, out_weight, channels, (far, skip)
+        )
+        blocks = (near, added(cross, skip))
+        total = line_cotangents(blocks, (NEAR, MIDDLE), out_weight, total, after=(first,))
+        through, two_a = passed((total,))
+        (last,) = held_until([hop(far, OUTWARD)], (own, total))
         grad_query, conv_grad = line_cotangents(
-            added(far, last), FAR, out_weight, total, (convolved, query_gate), (through,)
+            (added(far, last),), (FAR,), out_weight, total, (convolved, query_gate), (through,)
         )
     else:
         partial_value = jnp.dot(gated_out, out_weight, preferred_element_type=jnp.float32)
@@ -613,7 +629,7 @@
         grad_query = (wide(dgated) * wide(convolved)).astype(jnp.bfloat16)
         conv_grad = (wide(dgated) * wide(query_gate)).astype(jnp.bfloat16)
     grad_parts = traded(cut(conv_grad, position, members, 1), "ctx")
-    arrived = ready(tuple(grad_parts[1:])) if in_line else ()
+    arrived = ready(two_a, tuple(grad_parts[1:])) if in_line else ()
     back_parts = correlate(at, input_parts, grad_parts, per_group, tap_scale, arrived)
     if in_line:
         projected = rest(*arrived)

time: 187 us -> 184 us (0.984)
  local copies, waits for them, and re-layouts: 16.3 us -> 10.8 us
  waiting for transfers between devices: 50.8 us -> 45.6 us
  other arithmetic: 11.4 us -> 15.8 us
  starting transfers between devices: 38.1 us -> 40.1 us
    unnamed x82 -> x44, local copies, waits for them, and re-layouts: 14.9 us -> 8.58 us
    ppermute x10, waiting for transfers between devices: 21.5 us -> 16.4 us  [hop(): lax.ppermute(array, 'tp', [(2 * i + core, 2 * j + core) for i, j in pairs...]
    convert_element_type x6, other arithmetic: 10.6 us -> 13.8 us  [added(): return sum((wide(array) for array in arrays)).astype(jnp.bfloat16)]
    pallas_call x1, Pallas kernels: 1.01 us -> 3.35 us  [prepare(): pl.pallas_call(functools.partial(prepare_kernel, members, scale), out_sha...]
    pallas_call x4 -> x3, Pallas kernels: 21.3 us -> 20 us  [cotangent_products(): pl.pallas_call(functools.partial(cotangent_kernel, count, first, last), o...]
  transfers between devices with their start and end apart: 28 -> 28, of which waited for: 13 -> 9; matrix products, arithmetic and copies ran while one was open for 5% -> 7% of each run, Pallas kernels for 30% -> 34%
where the time goes in v5:
time: 184 us; the launch traced here: 183 us
  Pallas kernels  69.7 us (38%)
  waiting for transfers between devices  45.6 us (25%)
  starting transfers between devices  40.1 us (22%)
  other arithmetic  15.8 us (9%)
  local copies, waits for them, and re-layouts  10.8 us (6%)
    ppermute x18, waiting for transfers between devices, swapped(): return lax.ppermute(array, axis, [(i, i ^ step) for i in range(size)])  29.1 us
    pallas_call x4, Pallas kernels, column_products(): pl.pallas_call(given_kernel if more is None else functools.partial(kept_k...  24.7 us
    ppermute x10, starting transfers between devices, hop(): lax.ppermute(array, 'tp', [(2 * i + core, 2 * j + core) for i, j in pairs...  24.5 us
    pallas_call x3, Pallas kernels, cotangent_products(): pl.pallas_call(functools.partial(cotangent_kernel, count, first, last), o...  20 us
    ppermute x10, waiting for transfers between devices, hop(): lax.ppermute(array, 'tp', [(2 * i + core, 2 * j + core) for i, j in pairs...  16.4 us
    ppermute x18, starting transfers between devices, swapped(): return lax.ppermute(array, axis, [(i, i ^ step) for i in range(size)])  15.6 us
    convert_element_type x6, other arithmetic, added(): return sum((wide(array) for array in arrays)).astype(jnp.bfloat16)  13.8 us
    pallas_call x1, Pallas kernels, correlate(): pl.pallas_call(functools.partial(backward_kernel, members, per_group, sca...  12.5 us
  transfers between devices with their start and end apart: 28, of which 9 were waited for; matrix products, arithmetic and copies ran while one was open for 7% of the time, Pallas kernels for 34%

profile of v5, /device:TPU:0, one launch (start us, length us, event | category | flops | bytes accessed | tf_op | source)
XLA Modules:
  0.0 183.1 jit_solution(13464878513334010630)
XLA Ops:
  1.2 2.7 %collective-permute-start.4 = (bf16[512,1024]{1,0:T(8,128)(2,1)}, bf16[512,1024]{1,0:T(8,128)(2,1)S(1)}, u32[]{:S(2)}, u32[]{:S(2)}) collective-permute-start(bf16[512,1024]{1,0:T(8,128)(2,1)} %refs_0_.1), channel_id=1, source_target_pairs={{0,2},{1,3},{6,4},{7,5},{2,0},{3,1},{4,6},{5,7},{8,10},{9,11},{14,... | collective-permute-start | bytes 3145736 | tf_op jit(solution)/shard_map/ppermute | solution.py:348
  5.4 3.3 %gated_input.1 = (bf16[544,256]{1,0:T(8,128)(2,1)S(1)}, bf16[544,256]{1,0:T(8,128)(2,1)}, bf16[544,256]{1,0:T(8,128)(2,1)}, bf16[544,256]{1,0:T(8,128)(2,1)}) custom-call(s32[1]{0:T(128)} %bitcast.3.pos_ref, bf16[512,1024]{1,0:T(8,128)(2,1)} %refs_4_.3, bf16[512,1024]{1,0:T(8,128)(2,1)} %refs_5_.1, f32[64,512]{1,0:T(8,128)} %bitcast.15), custom_call_target="tpu_custom_call" | custom-call | flops 1048576 | bytes 4096 | tf_op jit(solution)/shard_map/gated_input/pallas_call | solution.py:259
  12.3 5.0 %cotangent_blocks.3.refs_4_ = f32[512,1024]{1,0:T(8,128)S(1)} custom-call(s32[2]{0:T(128)S(1)} %pad_add_fusion.1._, bf16[1024,8192]{1,0:T(8,128)(2,1)} %weight_ref.13, bf16[512,1024]{1,0:T(8,128)(2,1)S(1)} %copy-done.17, bf16[512,1024]{1,0:T(8,128)(2,1)} %collective-permute-done.3.refs_1_), custom_call_target="tpu_custom_call" | custom-call | flops 1048576 | bytes 4096 | tf_op jit(solution)/shard_map/cotangent_blocks/pallas_call | solution.py:475
  18.5 6.4 %collective-permute-done.1.refs_2_ = bf16[544,256]{1,0:T(8,128)(2,1)S(1)} collective-permute-done((bf16[544,256]{1,0:T(8,128)(2,1)}, bf16[544,256]{1,0:T(8,128)(2,1)S(1)}, u32[]{:S(2)}, u32[]{:S(2)}) %collective-permute-start.1) | collective-permute-done | bytes 278560 | tf_op jit(solution)/shard_map/ppermute | solution.py:315
  24.9 7.4 %causal_conv.1 = (bf16[512,256]{1,0:T(8,128)(2,1)S(1)}, bf16[512,256]{1,0:T(8,128)(2,1)S(1)}, bf16[512,256]{1,0:T(8,128)(2,1)S(1)}, bf16[512,256]{1,0:T(8,128)(2,1)S(1)}) custom-call(s32[1]{0:T(128)} %bitcast.3.pos_ref, bf16[544,256]{1,0:T(8,128)(2,1)S(1)} %get-tuple-element.33.refs_0_, bf16[544,256]{1,0:T(8,128)(2,1)S(1)} %collective-permute-done.refs_1_, ...), custom_call_target="tpu_custom_call" | custom-call | flops 1048576 | bytes 4096 | tf_op jit(solution)/shard_map/causal_conv/pallas_call | solution.py:180
  39.0 5.7 %collective-permute-done.6 = bf16[512,256]{1,0:T(8,128)(2,1)} collective-permute-done((bf16[512,256]{1,0:T(8,128)(2,1)S(1)}, bf16[512,256]{1,0:T(8,128)(2,1)}, u32[]{:S(2)}, u32[]{:S(2)}) %collective-permute-start.6) | collective-permute-done | bytes 262176 | tf_op jit(solution)/shard_map/ppermute | solution.py:315
  45.6 3.9 %collective-permute-done.7 = bf16[512,256]{1,0:T(8,128)(2,1)} collective-permute-done((bf16[512,256]{1,0:T(8,128)(2,1)S(1)}, bf16[512,256]{1,0:T(8,128)(2,1)}, u32[]{:S(2)}, u32[]{:S(2)}) %collective-permute-start.7) | collective-permute-done | bytes 262176 | tf_op jit(solution)/shard_map/ppermute | solution.py:315
  53.2 6.0 %collective-permute-done.10.refs_1_ = bf16[512,1024]{1,0:T(8,128)(2,1)S(1)} collective-permute-done((bf16[512,1024]{1,0:T(8,128)(2,1)}, bf16[512,1024]{1,0:T(8,128)(2,1)S(1)}, u32[]{:S(2)}, u32[]{:S(2)}) %collective-permute-start.10) | collective-permute-done | bytes 1048608 | tf_op jit(solution)/shard_map/ppermute | solution.py:348
  59.2 3.5 %projection_blocks.4.refs_0_ = bf16[1,512,1024]{2,1,0:T(8,128)(2,1)} custom-call(s32[1]{0:T(128)} %bitcast.9._, bf16[512,1024]{1,0:T(8,128)(2,1)S(1)} %multiply_convert_fusion.data_ref, bf16[1024,8192]{1,0:T(8,128)(2,1)} %weight_ref.13, bf16[512,1024]{1,0:T(8,128)(2,1)} %collective-permute-done.9.refs_0_, bf16[512,1024]{1,0:T(8,128)(2,1)S(1)} %collective-permute-done.10.refs_1_), custom_call_target="tpu_custom_call" | custom-call | flops 1048576 | bytes 4096 | tf_op jit(solution)/shard_map/projection_blocks/pallas_call | solution.py:410
  62.7 8.5 %projection_blocks.5.refs_0_ = bf16[3,512,1024]{2,1,0:T(8,128)(2,1)} custom-call(s32[3]{0:T(128)S(1)} %pad_add_fusion.2._, bf16[512,1024]{1,0:T(8,128)(2,1)S(1)} %multiply_convert_fusion.data_ref, bf16[1024,8192]{1,0:T(8,128)(2,1)} %weight_ref.13, bf16[1,512,1024]{2,1,0:T(8,128)(2,1)} %projection_blocks.4.refs_0_), custom_call_target="tpu_custom_call" | custom-call | flops 1048576 | bytes 4096 | tf_op jit(solution)/shard_map/projection_blocks/pallas_call | solution.py:410
  71.2 3.7 %projection_blocks.6.refs_1_.refs_5_ = bf16[512,1024]{1,0:T(8,128)(2,1)} custom-call(s32[1]{0:T(128)} %bitcast.10._, bf16[512,1024]{1,0:T(8,128)(2,1)S(1)} %multiply_convert_fusion.data_ref, bf16[1024,8192]{1,0:T(8,128)(2,1)} %weight_ref.13, bf16[1,512,1024]{2,1,0:T(8,128)(2,1)} %collective-permute-done.11.more_ref, ...), custom_call_target="tpu_custom_call" | custom-call | flops 1048576 | bytes 4096 | tf_op jit(solution)/shard_map/projection_blocks/pallas_call | solution.py:410
  75.6 2.6 %add_convert_fusion.5.refs_2_ = bf16[512,1024]{1,0:T(8,128)(2,1)} fusion(bf16[512,1024]{1,0:T(8,128)(2,1)S(1)} %collective-permute-done.10.refs_1_, bf16[512,1024]{1,0:T(8,128)(2,1)} %get-tuple-element.46), kind=kLoop, calls=%fused_computation.5 | loop fusion | flops 2097152 | bytes 3145728 | tf_op jit(solution)/shard_map/convert_element_type | solution.py:498
  79.9 7.5 %collective-permute-start.13 = (bf16[512,1024]{1,0:T(8,128)(2,1)}, bf16[512,1024]{1,0:T(8,128)(2,1)}, u32[]{:S(2)}, u32[]{:S(2)}) collective-permute-start(bf16[512,1024]{1,0:T(8,128)(2,1)} %projection_blocks.6.refs_1_.refs_5_), channel_id=1, source_target_pairs={{0,2},{1,3},{6,4},{7,5},{8,10},{9,11},{14,12},{15,13},{16,18},{17,... | collective-permute-start | bytes 3145736 | tf_op jit(solution)/shard_map/ppermute | solution.py:348
  92.6 8.3 %cotangent_blocks.4.refs_1_.refs_2_ = f32[512,1024]{1,0:T(8,128)S(1)} custom-call(s32[4]{0:T(128)S(1)} %pad_add_fusion.3._, bf16[1024,8192]{1,0:T(8,128)(2,1)} %weight_ref.13, bf16[512,1024]{1,0:T(8,128)(2,1)S(1)} %copy-done.5, bf16[512,1024]{1,0:T(8,128)(2,1)} %collective-permute-done.14.refs_1_, bf16[512,1024]{1,0:T(8,128)(2,1)} %add_convert_fusion.5.refs_2_, ...), custom_call_target="tpu_custom_call" | custom-call | flops 1048576 | bytes 4096 | tf_op jit(solution)/shard_map/cotangent_blocks/pallas_call | solution.py:475
  100.9 9.0 %projection_blocks.7 = (bf16[512,1024]{1,0:T(8,128)(2,1)}, bf16[512,1024]{1,0:T(8,128)(2,1)S(1)}, bf16[512,1024]{1,0:T(8,128)(2,1)S(1)}) custom-call(s32[3]{0:T(128)S(1)} %pad_add_fusion._, bf16[512,1024]{1,0:T(8,128)(2,1)S(1)} %multiply_convert_fusion.data_ref, bf16[1024,8192]{1,0:T(8,128)(2,1)} %weight_ref.13, ...), custom_call_target="tpu_custom_call" | custom-call | flops 1048576 | bytes 4096 | tf_op jit(solution)/shard_map/projection_blocks/pallas_call | solution.py:410
  111.3 2.9 %add_convert_fusion.3.refs_0_ = bf16[512,1024]{1,0:T(8,128)(2,1)} fusion(bf16[512,1024]{1,0:T(8,128)(2,1)} %held.8, bf16[512,1024]{1,0:T(8,128)(2,1)} %collective-permute-done.9.refs_0_), kind=kLoop, calls=%fused_computation.3 | loop fusion | flops 2097152 | bytes 3145728 | tf_op jit(solution)/shard_map/convert_element_type | solution.py:498
  114.2 3.0 %add_convert_fusion.4.refs_5_ = bf16[512,1024]{1,0:T(8,128)(2,1)} fusion(bf16[512,1024]{1,0:T(8,128)(2,1)} %held.7, bf16[512,1024]{1,0:T(8,128)(2,1)} %projection_blocks.6.refs_1_.refs_5_), kind=kLoop, calls=%fused_computation.4 | loop fusion | flops 2097152 | bytes 3145728 | tf_op jit(solution)/shard_map/convert_element_type | solution.py:498
  118.9 4.3 %collective-permute-start.17 = (bf16[512,1024]{1,0:T(8,128)(2,1)}, bf16[512,1024]{1,0:T(8,128)(2,1)}, u32[]{:S(2)}, u32[]{:S(2)}) collective-permute-start(bf16[512,1024]{1,0:T(8,128)(2,1)} %get-tuple-element.49), channel_id=1, source_target_pairs={{0,2},{1,3},{6,4},{7,5},{8,10},{9,11},{14,12},{15,13},{16,18},{17,... | collective-permute-start | bytes 3145736 | tf_op jit(solution)/shard_map/ppermute | solution.py:348
  124.4 6.6 %cotangent_blocks.5 = (bf16[512,1024]{1,0:T(8,128)(2,1)}, bf16[512,1024]{1,0:T(8,128)(2,1)S(1)}) custom-call(s32[2]{0:T(128)S(1)} %pad_add_fusion.4._, bf16[1024,8192]{1,0:T(8,128)(2,1)} %weight_ref.13, bf16[512,1024]{1,0:T(8,128)(2,1)} %add_convert_fusion.3.refs_0_, bf16[512,1024]{1,0:T(8,128)(2,1)} %collective-permute-done.19.refs_1_, ...), custom_call_target="tpu_custom_call" | custom-call | flops 1048576 | bytes 4096 | tf_op jit(solution)/shard_map/cotangent_blocks/pallas_call | solution.py:475
  134.7 10.4 %collective-permute-done.17.refs_1_ = bf16[512,1024]{1,0:T(8,128)(2,1)} collective-permute-done((bf16[512,1024]{1,0:T(8,128)(2,1)}, bf16[512,1024]{1,0:T(8,128)(2,1)}, u32[]{:S(2)}, u32[]{:S(2)}) %collective-permute-start.17) | collective-permute-done | bytes 1048608 | tf_op jit(solution)/shard_map/ppermute | solution.py:348
  146.0 2.0 %add_convert_fusion.1.refs_9_ = bf16[512,1024]{1,0:T(8,128)(2,1)S(1)} fusion(bf16[512,1024]{1,0:T(8,128)(2,1)} %get-tuple-element.52, bf16[512,1024]{1,0:T(8,128)(2,1)} %get-tuple-element.49), kind=kLoop, calls=%fused_computation.1 | loop fusion | flops 2097152 | bytes 3145728 | tf_op jit(solution)/shard_map/convert_element_type | solution.py:498
  152.5 12.5 %causal_conv_grads.1 = (bf16[544,256]{1,0:T(8,128)(2,1)S(1)}, bf16[544,256]{1,0:T(8,128)(2,1)S(1)}, bf16[544,256]{1,0:T(8,128)(2,1)S(1)}, bf16[544,256]{1,0:T(8,128)(2,1)S(1)}) custom-call(s32[1]{0:T(128)} %bitcast.3.pos_ref, bf16[544,256]{1,0:T(8,128)(2,1)S(1)} %get-tuple-element.33.refs_0_, bf16[544,256]{1,0:T(8,128)(2,1)S(1)} %copy-done.12, ...), custom_call_target="tpu_custom_call" | custom-call | flops 1048576 | bytes 4096 | tf_op jit(solution)/shard_map/causal_conv_grads/pallas_call | solution.py:201
  168.5 6.1 %collective-permute-done.25.refs_1_ = bf16[544,256]{1,0:T(8,128)(2,1)S(1)} collective-permute-done((bf16[544,256]{1,0:T(8,128)(2,1)S(1)}, bf16[544,256]{1,0:T(8,128)(2,1)S(1)}, u32[]{:S(2)}, u32[]{:S(2)}) %collective-permute-start.25) | collective-permute-done | bytes 278560 | tf_op jit(solution)/shard_map/ppermute | solution.py:315
  174.6 5.0 %collective-permute-done.26.refs_2_ = bf16[544,256]{1,0:T(8,128)(2,1)S(1)} collective-permute-done((bf16[544,256]{1,0:T(8,128)(2,1)S(1)}, bf16[544,256]{1,0:T(8,128)(2,1)S(1)}, u32[]{:S(2)}, u32[]{:S(2)}) %collective-permute-start.26) | collective-permute-done | bytes 278560 | tf_op jit(solution)/shard_map/ppermute | solution.py:315
  (110 shorter events, 45.7 us)
Async XLA Ops:
  0.6 11.1 %collective-permute-start.3 = (bf16[512,1024]{1,0:T(8,128)(2,1)}, bf16[512,1024]{1,0:T(8,128)(2,1)}, u32[]{:S(2)}, u32[]{:S(2)}) collective-permute-start(bf16[512,1024]{1,0:T(8,128)(2,1)} %refs_0_.1), channel_id=1, source_target_pairs={{0,1},{1,0},{2,3},{3,2},{4,5},{5,4},{6,7},{7,6},{8,9},{9,8},{10,11... | collective-permute-start | bytes 3145736 | tf_op jit(solution)/shard_map/ppermute | solution.py:315
  1.2 31.1 %collective-permute-start.4 = (bf16[512,1024]{1,0:T(8,128)(2,1)}, bf16[512,1024]{1,0:T(8,128)(2,1)S(1)}, u32[]{:S(2)}, u32[]{:S(2)}) collective-permute-start(bf16[512,1024]{1,0:T(8,128)(2,1)} %refs_0_.1), channel_id=1, source_target_pairs={{0,2},{1,3},{6,4},{7,5},{2,0},{3,1},{4,6},{5,7},{8,10},{9,11},{14,... | collective-permute-start | bytes 3145736 | tf_op jit(solution)/shard_map/ppermute | solution.py:348
  3.8 28.5 %collective-permute-start.5 = (bf16[512,1024]{1,0:T(8,128)(2,1)}, bf16[512,1024]{1,0:T(8,128)(2,1)}, u32[]{:S(2)}, u32[]{:S(2)}) collective-permute-start(bf16[512,1024]{1,0:T(8,128)(2,1)} %refs_0_.1), channel_id=1, source_target_pairs={{2,4},{3,5},{4,2},{5,3},{10,12},{11,13},{12,10},{13,11},{18,20},{1... | collective-permute-start | bytes 3145736 | tf_op jit(solution)/shard_map/ppermute | solution.py:348
  8.8 9.7 %collective-permute-start = (bf16[544,256]{1,0:T(8,128)(2,1)}, bf16[544,256]{1,0:T(8,128)(2,1)S(1)}, u32[]{:S(2)}, u32[]{:S(2)}) collective-permute-start(bf16[544,256]{1,0:T(8,128)(2,1)} %get-tuple-element.34), channel_id=1, source_target_pairs={{0,8},{8,0},{16,24},{24,16},{1,9},{9,1},{17,25},{25,17},{2,10},{10... | collective-permute-start | bytes 835592 | tf_op jit(solution)/shard_map/ppermute | solution.py:315
  10.3 14.6 %collective-permute-start.1 = (bf16[544,256]{1,0:T(8,128)(2,1)}, bf16[544,256]{1,0:T(8,128)(2,1)S(1)}, u32[]{:S(2)}, u32[]{:S(2)}) collective-permute-start(bf16[544,256]{1,0:T(8,128)(2,1)} %get-tuple-element.35), channel_id=1, source_target_pairs={{0,16},{8,24},{16,0},{24,8},{1,17},{9,25},{17,1},{25,9},{2,18},{10... | collective-permute-start | bytes 835592 | tf_op jit(solution)/shard_map/ppermute | solution.py:315
  11.8 13.1 %collective-permute-start.2 = (bf16[544,256]{1,0:T(8,128)(2,1)}, bf16[544,256]{1,0:T(8,128)(2,1)S(1)}, u32[]{:S(2)}, u32[]{:S(2)}) collective-permute-start(bf16[544,256]{1,0:T(8,128)(2,1)} %get-tuple-element.36), channel_id=1, source_target_pairs={{0,24},{8,16},{16,8},{24,0},{1,25},{9,17},{17,9},{25,1},{2,26},{10... | collective-permute-start | bytes 835592 | tf_op jit(solution)/shard_map/ppermute | solution.py:315
  32.4 26.8 %collective-permute-start.10 = (bf16[512,1024]{1,0:T(8,128)(2,1)}, bf16[512,1024]{1,0:T(8,128)(2,1)S(1)}, u32[]{:S(2)}, u32[]{:S(2)}) collective-permute-start(bf16[512,1024]{1,0:T(8,128)(2,1)} %get-tuple-element.46), channel_id=1, source_target_pairs={{2,0},{3,1},{4,6},{5,7},{10,8},{11,9},{12,14},{13,15},{18,16},{19,... | collective-permute-start | bytes 3145736 | tf_op jit(solution)/shard_map/ppermute | solution.py:348
  33.7 25.5 %collective-permute-start.9 = (bf16[512,1024]{1,0:T(8,128)(2,1)S(1)}, bf16[512,1024]{1,0:T(8,128)(2,1)}, u32[]{:S(2)}, u32[]{:S(2)}) collective-permute-start(bf16[512,1024]{1,0:T(8,128)(2,1)S(1)} %get-tuple-element.45.refs_0_), channel_id=1, source_target_pairs={{2,4},{3,5},{4,2},{5,3},{10,12},{11,13},{12,10},{13,11},{18,20},{1... | collective-permute-start | bytes 3145736 | tf_op jit(solution)/shard_map/ppermute | solution.py:348
  36.5 13.0 %collective-permute-start.7 = (bf16[512,256]{1,0:T(8,128)(2,1)S(1)}, bf16[512,256]{1,0:T(8,128)(2,1)}, u32[]{:S(2)}, u32[]{:S(2)}) collective-permute-start(bf16[512,256]{1,0:T(8,128)(2,1)S(1)} %get-tuple-element.43), channel_id=1, source_target_pairs={{0,16},{8,24},{16,0},{24,8},{1,17},{9,25},{17,1},{25,9},{2,18},{10... | collective-permute-start | bytes 786440 | tf_op jit(solution)/shard_map/ppermute | solution.py:315
  37.4 13.1 %collective-permute-start.8 = (bf16[512,256]{1,0:T(8,128)(2,1)S(1)}, bf16[512,256]{1,0:T(8,128)(2,1)S(1)}, u32[]{:S(2)}, u32[]{:S(2)}) collective-permute-start(bf16[512,256]{1,0:T(8,128)(2,1)S(1)} %get-tuple-element.44), channel_id=1, source_target_pairs={{0,24},{8,16},{16,8},{24,0},{1,25},{9,17},{17,9},{25,1},{2,26},{10... | collective-permute-start | bytes 786440 | tf_op jit(solution)/shard_map/ppermute | solution.py:315
  75.0 25.9 %collective-permute-start.12 = (bf16[3,512,1024]{2,1,0:T(8,128)(2,1)}, bf16[3,512,1024]{2,1,0:T(8,128)(2,1)}, u32[]{:S(2)}, u32[]{:S(2)}) collective-permute-start(bf16[3,512,1024]{2,1,0:T(8,128)(2,1)} %held.6), channel_id=1, source_target_pairs={{0,1},{1,0},{2,3},{3,2},{4,5},{5,4},{6,7},{7,6},{8,9},{9,8},{10,11... | collective-permute-start | bytes 9437192 | tf_op jit(solution)/shard_map/ppermute | solution.py:315
  75.5 12.1 %collective-permute-start.14 = (bf16[512,1024]{1,0:T(8,128)(2,1)S(1)}, bf16[512,1024]{1,0:T(8,128)(2,1)}, u32[]{:S(2)}, u32[]{:S(2)}) collective-permute-start(bf16[512,1024]{1,0:T(8,128)(2,1)S(1)} %get-tuple-element.45.refs_0_), channel_id=1, source_target_pairs={{0,1},{1,0},{2,3},{3,2},{4,5},{5,4},{6,7},{7,6},{8,9},{9,8},{10,11... | collective-permute-start | bytes 3145736 | tf_op jit(solution)/shard_map/ppermute | solution.py:315
  78.6 31.4 %collective-permute-start.18 = (bf16[512,1024]{1,0:T(8,128)(2,1)}, bf16[512,1024]{1,0:T(8,128)(2,1)}, u32[]{:S(2)}, u32[]{:S(2)}) collective-permute-start(bf16[512,1024]{1,0:T(8,128)(2,1)} %collective-permute-done.9.refs_0_), channel_id=1, source_target_pairs={{2,0},{3,1},{4,6},{5,7},{10,8},{11,9},{12,14},{13,15},{18,16},{19,... | collective-permute-start | bytes 3145736 | tf_op jit(solution)/shard_map/ppermute | solution.py:348
  79.9 34.3 %collective-permute-start.13 = (bf16[512,1024]{1,0:T(8,128)(2,1)}, bf16[512,1024]{1,0:T(8,128)(2,1)}, u32[]{:S(2)}, u32[]{:S(2)}) collective-permute-start(bf16[512,1024]{1,0:T(8,128)(2,1)} %projection_blocks.6.refs_1_.refs_5_), channel_id=1, source_target_pairs={{0,2},{1,3},{6,4},{7,5},{8,10},{9,11},{14,12},{15,13},{16,18},{17,... | collective-permute-start | bytes 3145736 | tf_op jit(solution)/shard_map/ppermute | solution.py:348
  117.2 17.5 %collective-permute-start.16 = (bf16[512,1024]{1,0:T(8,128)(2,1)}, bf16[512,1024]{1,0:T(8,128)(2,1)}, u32[]{:S(2)}, u32[]{:S(2)}) collective-permute-start(bf16[512,1024]{1,0:T(8,128)(2,1)} %add_convert_fusion.4.refs_5_), channel_id=1, source_target_pairs={{2,4},{3,5},{4,2},{5,3},{10,12},{11,13},{12,10},{13,11},{18,20},{1... | collective-permute-start | bytes 3145736 | tf_op jit(solution)/shard_map/ppermute | solution.py:348
  118.9 26.3 %collective-permute-start.17 = (bf16[512,1024]{1,0:T(8,128)(2,1)}, bf16[512,1024]{1,0:T(8,128)(2,1)}, u32[]{:S(2)}, u32[]{:S(2)}) collective-permute-start(bf16[512,1024]{1,0:T(8,128)(2,1)} %get-tuple-element.49), channel_id=1, source_target_pairs={{0,2},{1,3},{6,4},{7,5},{8,10},{9,11},{14,12},{15,13},{16,18},{17,... | collective-permute-start | bytes 3145736 | tf_op jit(solution)/shard_map/ppermute | solution.py:348
  131.2 14.0 %collective-permute-start.20 = (bf16[512,256]{1,0:T(8,128)(2,1)S(1)}, bf16[512,256]{1,0:T(8,128)(2,1)S(1)}, u32[]{:S(2)}, u32[]{:S(2)}) collective-permute-start(bf16[512,256]{1,0:T(8,128)(2,1)S(1)} %get-tuple-element.64), channel_id=1, source_target_pairs={{0,8},{8,0},{16,24},{24,16},{1,9},{9,1},{17,25},{25,17},{2,10},{10... | collective-permute-start | bytes 786440 | tf_op jit(solution)/shard_map/ppermute | solution.py:315
  132.7 13.3 %collective-permute-start.21 = (bf16[512,256]{1,0:T(8,128)(2,1)S(1)}, bf16[512,256]{1,0:T(8,128)(2,1)S(1)}, u32[]{:S(2)}, u32[]{:S(2)}) collective-permute-start(bf16[512,256]{1,0:T(8,128)(2,1)S(1)} %get-tuple-element.63), channel_id=1, source_target_pairs={{0,16},{8,24},{16,0},{24,8},{1,17},{9,25},{17,1},{25,9},{2,18},{10... | collective-permute-start | bytes 786440 | tf_op jit(solution)/shard_map/ppermute | solution.py:315
  133.2 12.8 %collective-permute-start.22 = (bf16[512,256]{1,0:T(8,128)(2,1)S(1)}, bf16[512,256]{1,0:T(8,128)(2,1)S(1)}, u32[]{:S(2)}, u32[]{:S(2)}) collective-permute-start(bf16[512,256]{1,0:T(8,128)(2,1)S(1)} %get-tuple-element.62), channel_id=1, source_target_pairs={{0,24},{8,16},{16,8},{24,0},{1,25},{9,17},{17,9},{25,1},{2,26},{10... | collective-permute-start | bytes 786440 | tf_op jit(solution)/shard_map/ppermute | solution.py:315
  149.8 31.7 %collective-permute-start.23 = (bf16[512,1024]{1,0:T(8,128)(2,1)S(1)}, bf16[512,1024]{1,0:T(8,128)(2,1)S(1)}, u32[]{:S(2)}, u32[]{:S(2)}) collective-permute-start(bf16[512,1024]{1,0:T(8,128)(2,1)S(1)} %add_convert_fusion.2.refs_8_), channel_id=1, source_target_pairs={{2,0},{3,1},{4,6},{5,7},{0,2},{1,3},{6,4},{7,5},{10,8},{11,9},{12,... | collective-permute-start | bytes 3145736 | tf_op jit(solution)/shard_map/ppermute | solution.py:348
  151.5 30.0 %collective-permute-start.24 = (bf16[512,1024]{1,0:T(8,128)(2,1)S(1)}, bf16[512,1024]{1,0:T(8,128)(2,1)S(1)}, u32[]{:S(2)}, u32[]{:S(2)}) collective-permute-start(bf16[512,1024]{1,0:T(8,128)(2,1)S(1)} %add_convert_fusion.1.refs_9_), channel_id=1, source_target_pairs={{2,4},{3,5},{4,2},{5,3},{10,12},{11,13},{12,10},{13,11},{18,20},{1... | collective-permute-start | bytes 3145736 | tf_op jit(solution)/shard_map/ppermute | solution.py:348
  164.9 9.7 %collective-permute-start.25 = (bf16[544,256]{1,0:T(8,128)(2,1)S(1)}, bf16[544,256]{1,0:T(8,128)(2,1)S(1)}, u32[]{:S(2)}, u32[]{:S(2)}) collective-permute-start(bf16[544,256]{1,0:T(8,128)(2,1)S(1)} %get-tuple-element.55), channel_id=1, source_target_pairs={{0,8},{8,0},{16,24},{24,16},{1,9},{9,1},{17,25},{25,17},{2,10},{10... | collective-permute-start | bytes 835592 | tf_op jit(solution)/shard_map/ppermute | solution.py:315
  166.4 13.2 %collective-permute-start.26 = (bf16[544,256]{1,0:T(8,128)(2,1)S(1)}, bf16[544,256]{1,0:T(8,128)(2,1)S(1)}, u32[]{:S(2)}, u32[]{:S(2)}) collective-permute-start(bf16[544,256]{1,0:T(8,128)(2,1)S(1)} %get-tuple-element.56), channel_id=1, source_target_pairs={{0,16},{8,24},{16,0},{24,8},{1,17},{9,25},{17,1},{25,9},{2,18},{10... | collective-permute-start | bytes 835592 | tf_op jit(solution)/shard_map/ppermute | solution.py:315
  167.0 12.6 %collective-permute-start.27 = (bf16[544,256]{1,0:T(8,128)(2,1)S(1)}, bf16[544,256]{1,0:T(8,128)(2,1)S(1)}, u32[]{:S(2)}, u32[]{:S(2)}) collective-permute-start(bf16[544,256]{1,0:T(8,128)(2,1)S(1)} %get-tuple-element.57), channel_id=1, source_target_pairs={{0,24},{8,16},{16,8},{24,0},{1,25},{9,17},{17,9},{25,1},{2,26},{10... | collective-permute-start | bytes 835592 | tf_op jit(solution)/shard_map/ppermute | solution.py:315
  (26 other events, 239.5 us)

commit v6 on v5

--- a/solution.py
+++ b/solution.py
@@ -8,6 +8,7 @@
 from jax.sharding import PartitionSpec as P
 
 BLOCK = 128
+POSITION = 8
 NT = (((1,), (1,)), ((), ()))
 COST = pl.CostEstimate(flops=2**20, bytes_accessed=2**12, transcendentals=0)
 
@@ -53,10 +54,10 @@
     tap_scr[:, pl.ds(start, width)] = jnp.concatenate(parts, axis=1)[:groups]
 
 
-def forward_kernel(members, per_group, width, pos_ref, *refs):
+def forward_kernel(members, per_group, width, plan_ref, *refs):
     inputs, outputs = refs[:members], refs[-members - 3 : -3]
     tap_scr, in_scr, out_scr = refs[-3:]
-    position = pos_ref[0]
+    position = plan_ref[POSITION]
     channels = inputs[0].shape[1]
     groups = channels // per_group
     length = members * width
@@ -93,11 +94,11 @@
         outputs[step][...] = out_scr[position ^ step].T
 
 
-def backward_kernel(members, per_group, scale, width, pos_ref, *refs):
+def backward_kernel(members, per_group, scale, width, plan_ref, *refs):
     inputs, cotangents = refs[:members], refs[members : 2 * members]
     outputs = refs[-members - 6 : -6]
     tap_scr, in_scr, cot_scr, out_scr, grad_scr, pad_scr = refs[-6:]
-    position = pos_ref[0]
+    position = plan_ref[POSITION]
     channels = inputs[0].shape[1]
     groups = channels // per_group
     length = members * width
@@ -173,7 +174,7 @@
 SMEM = pl.BlockSpec(memory_space=pltpu.SMEM)
 
 
-def convolve(position, inputs, width, per_group, after=()):
+def convolve(plan, inputs, width, per_group, after=()):
     members = len(inputs)
     channels = inputs[0].shape[1]
     length = members * width
@@ -190,10 +191,10 @@
         compiler_params=pltpu.CompilerParams(vmem_limit_bytes=24 * 2**20),
         cost_estimate=COST,
         name="causal_conv",
-    )(position, *inputs, *after)
-
-
-def correlate(position, inputs, cotangents, per_group, scale, after=()):
+    )(plan, *inputs, *after)
+
+
+def correlate(plan, inputs, cotangents, per_group, scale, after=()):
     members = len(inputs)
     width, channels = cotangents[0].shape
     length = members * width
@@ -214,15 +215,15 @@
         compiler_params=pltpu.CompilerParams(vmem_limit_bytes=24 * 2**20),
         cost_estimate=COST,
         name="causal_conv_grads",
-    )(position, *inputs, *cotangents, *after)
+    )(plan, *inputs, *cotangents, *after)
 
 
 def in_hbm(array):
     return pltpu.with_memory_space_constraint(array, pltpu.HBM)
 
 
-def prepare_kernel(members, scale, pos_ref, key_ref, value_ref, taps_ref, *outputs):
-    position = pos_ref[0]
+def prepare_kernel(members, scale, plan_ref, key_ref, value_ref, taps_ref, *outputs):
+    position = plan_ref[POSITION]
     step_no = pl.program_id(0)
     rows, channels = key_ref.shape
     share = channels // members
@@ -250,7 +251,7 @@
                 ]
 
 
-def prepare(position, key_gate, value_input, filter_taps, members, scale):
+def prepare(plan, key_gate, value_input, filter_taps, members, scale):
     width, channels = key_gate.shape
     share = channels // members
     rows = width + filter_taps.size // members // share
@@ -265,13 +266,13 @@
         compiler_params=pltpu.CompilerParams(vmem_limit_bytes=24 * 2**20),
         cost_estimate=COST,
         name="gated_input",
-    )(position, in_hbm(key_gate), in_hbm(value_input), in_hbm(filter_taps.T))
-
-
-def finish_kernel(members, pos_ref, *refs):
+    )(plan, in_hbm(key_gate), in_hbm(value_input), in_hbm(filter_taps.T))
+
+
+def finish_kernel(members, plan_ref, *refs):
     parts = refs[:members]
     key_ref, value_ref, key_out, value_out, taps_out = refs[members:]
-    position = pos_ref[0]
+    position = plan_ref[POSITION]
     width, channels = key_ref.shape
     share = channels // members
     groups = taps_out.shape[0] // members
@@ -294,7 +295,7 @@
         ).astype(jnp.float32)
 
 
-def finished(position, parts, key_gate, value_input, groups):
+def finished(plan, parts, key_gate, value_input, groups):
     members = len(parts)
     width, channels = key_gate.shape
     array = jax.ShapeDtypeStruct((width, channels), jnp.bfloat16)
@@ -306,7 +307,7 @@
         compiler_params=pltpu.CompilerParams(vmem_limit_bytes=24 * 2**20),
         cost_estimate=COST,
         name="input_gradients",
-    )(position, *parts, key_gate, value_input)
+    )(plan, *parts, key_gate, value_input)
     return grad_key, grad_value, taps.T
 
 
@@ -353,12 +354,35 @@
 INWARD = ((0, 1), (3, 2))
 ACROSS = ((1, 2), (2, 1))
 OUTWARD = ((1, 0), (2, 3))
-
-
-def of_chip(chip, table):
-    return jnp.where(
-        chip == 0, table[0], jnp.where(chip == 1, table[1], jnp.where(chip == 2, table[2], table[3]))
-    )
+OWN, NEAR, MIDDLE, FAR = range(4)
+CHIPS = ((0, 1, 2, 3), (1, 0, 3, 2), (2, 2, 1, 1), (3, 3, 0, 0))
+
+
+def plan_kernel(who_ref, plan_ref):
+    place = who_ref[1]
+    chip, core = place // 2, place % 2
+    for number, table in enumerate(CHIPS):
+        source = jnp.where(
+            chip < 2,
+            jnp.where(chip == 0, table[0], table[1]),
+            jnp.where(chip == 2, table[2], table[3]),
+        )
+        plan_ref[2 * number] = 2 * source + core
+        plan_ref[2 * number + 1] = 2 * source + 1 - core
+    plan_ref[POSITION] = who_ref[0]
+
+
+def planned():
+    who = jnp.stack([lax.axis_index("ctx"), lax.axis_index("tp")]).astype(jnp.int32)
+    return pl.pallas_call(
+        plan_kernel,
+        out_shape=jax.ShapeDtypeStruct((POSITION + 1,), jnp.int32),
+        in_specs=[SMEM],
+        out_specs=SMEM,
+        compiler_params=pltpu.CompilerParams(vmem_limit_bytes=2**20),
+        cost_estimate=COST,
+        name="plan",
+    )(who)
 
 
 def pass_kernel(*refs):
@@ -378,71 +402,104 @@
     )(*values, *after)
 
 
-def given_kernel(_, data_ref, weight_ref, *refs):
-    refs[-1][0] = jnp.dot(
-        data_ref[...], weight_ref[...], preferred_element_type=jnp.float32
-    ).astype(jnp.bfloat16)
-
-
-def kept_kernel(tiles, count, _, data_ref, weight_ref, more_ref, *refs):
+def add_kernel(*refs):
+    refs[-1][...] = sum(wide(ref[...]) for ref in refs[:-1]).astype(jnp.bfloat16)
+
+
+def added(*arrays):
+    rows, width = arrays[0].shape
+    part = pl.BlockSpec((rows // 4, width), lambda i: (i, 0))
+    return pl.pallas_call(
+        add_kernel,
+        out_shape=jax.ShapeDtypeStruct((rows, width), jnp.bfloat16),
+        grid=(4,),
+        in_specs=[part] * len(arrays),
+        out_specs=part,
+        compiler_params=pltpu.CompilerParams(vmem_limit_bytes=8 * 2**20),
+        cost_estimate=COST,
+        name="added",
+    )(*arrays)
+
+
+def gate_kernel(members, plan_ref, *refs):
+    parts = refs[:members]
+    query_ref, gated_ref, conv_ref = refs[members:]
+    position = plan_ref[POSITION]
+    share = parts[0].shape[1]
+    for step in range(members):
+        columns = pl.ds(pl.multiple_of((position ^ step) * share, share), share)
+        conv = parts[step][...]
+        conv_ref[:, columns] = conv
+        gated_ref[:, columns] = (wide(conv) * wide(query_ref[:, columns])).astype(jnp.bfloat16)
+
+
+def gated(plan, parts, query_gate):
+    array = jax.ShapeDtypeStruct(query_gate.shape, jnp.bfloat16)
+    return pl.pallas_call(
+        functools.partial(gate_kernel, len(parts)),
+        out_shape=[array, array],
+        in_specs=[SMEM] + [VMEM] * (len(parts) + 1),
+        out_specs=[VMEM] * 2,
+        compiler_params=pltpu.CompilerParams(vmem_limit_bytes=8 * 2**20),
+        cost_estimate=COST,
+        name="gated_output",
+    )(plan, *parts, query_gate)
+
+
+def product_kernel(tiles, count, extra, _, data_ref, weight_ref, *refs):
+    more, outputs = refs[:extra], refs[-count:]
     product = jnp.dot(data_ref[...], weight_ref[...], preferred_element_type=jnp.float32)
-    result = (product + wide(more_ref[0])).astype(jnp.bfloat16)
-    for number, out_ref in enumerate(refs[-count:]):
+    for number, out_ref in enumerate(outputs):
 
         @pl.when(pl.program_id(0) // tiles == number)
-        def _(out_ref=out_ref):
-            out_ref[...] = result
-
-
-def column_products(data, out_weight, blocks, width, more=None, after=()):
+        def _(number=number, out_ref=out_ref):
+            total = product + wide(more[number][...]) if more else product
+            out_ref[...] = total.astype(jnp.bfloat16)
+
+
+def column_products(plan, data, out_weight, first, count, other, more=(), after=()):
     rows, depth = data.shape
+    width = data.shape[1]
     tile = min(width, 512)
     tiles = width // tile
-    count = len(blocks)
-    stack = pl.BlockSpec((1, rows, tile), lambda i, at: (i // tiles, 0, i % tiles))
-    array = jax.ShapeDtypeStruct((rows, width), jnp.bfloat16)
 
     def column(number):
         return pl.BlockSpec(
             (rows, tile), lambda i, at: (0, jnp.clip(i - number * tiles, 0, tiles - 1))
         )
 
-    return pl.pallas_call(
-        given_kernel if more is None else functools.partial(kept_kernel, tiles, count),
-        out_shape=jax.ShapeDtypeStruct((count, rows, width), jnp.bfloat16)
-        if more is None
-        else [array] * count,
+    def weights(i, at):
+        return 0, at[2 * (first - i // tiles) + other] * tiles + i % tiles
+
+    columns = [column(number) for number in range(count)]
+    return pl.pallas_call(
+        functools.partial(product_kernel, tiles, count, len(more)),
+        out_shape=[jax.ShapeDtypeStruct((rows, width), jnp.bfloat16)] * count,
         grid_spec=pltpu.PrefetchScalarGridSpec(
             num_scalar_prefetch=1,
             grid=(count * tiles,),
             in_specs=[
                 pl.BlockSpec((rows, depth), lambda i, at: (0, 0)),
-                pl.BlockSpec((depth, tile), lambda i, at: (0, at[i // tiles] * tiles + i % tiles)),
+                pl.BlockSpec((depth, tile), weights),
             ]
-            + ([] if more is None else [stack])
+            + columns[: len(more)]
             + [ANYWHERE] * len(after),
-            out_specs=stack if more is None else [column(number) for number in range(count)],
+            out_specs=columns,
         ),
         compiler_params=pltpu.CompilerParams(vmem_limit_bytes=24 * 2**20),
         cost_estimate=COST,
         name="projection_blocks",
-    )(
-        jnp.stack(blocks).astype(jnp.int32),
-        data,
-        in_hbm(out_weight),
-        *(() if more is None else (more,)),
-        *after,
-    )
-
-
-def cotangent_kernel(count, first, last, _, weight_ref, *refs):
+    )(plan, data, in_hbm(out_weight), *more, *after)
+
+
+def cotangent_kernel(count, begin, last, members, plan_ref, weight_ref, *refs):
     blocks, refs = refs[:count], refs[count:]
     step = pl.program_id(0)
     total = refs[-1]
 
     @pl.when(step == 0)
     def _():
-        total[...] = jnp.zeros_like(total) if first else refs[0][...]
+        total[...] = jnp.zeros_like(total) if begin else refs[0][...]
 
     for number, block in enumerate(blocks):
 
@@ -454,91 +511,53 @@
 
     if last:
         conv_ref, query_ref = refs[1:3]
-        grad_ref, cot_ref = refs[-3:-1]
+        grad_ref, parts = refs[-2 - members], refs[-1 - members : -1]
 
         @pl.when(step == count - 1)
         def _():
             dgated = wide(total[...].astype(jnp.bfloat16))
             grad_ref[...] = (dgated * wide(conv_ref[...])).astype(jnp.bfloat16)
-            cot_ref[...] = (dgated * wide(query_ref[...])).astype(jnp.bfloat16)
-
-
-def cotangent_products(blocks, places, out_weight, start=None, gates=(), after=()):
+            share = parts[0].shape[1]
+            for step in range(members):
+                start = pl.multiple_of((plan_ref[POSITION] ^ step) * share, share)
+                columns = pl.ds(start, share)
+                dgated = wide(total[:, columns].astype(jnp.bfloat16))
+                parts[step][...] = (dgated * wide(query_ref[:, columns])).astype(jnp.bfloat16)
+
+
+def cotangent_products(
+    plan, first, blocks, out_weight, start=None, gates=(), after=(), members=0
+):
+    parts = [part for block in blocks for part in (block, swapped(block, "tp", 1))]
     rows, width = blocks[0].shape
     channels = out_weight.shape[0]
-    count = len(blocks)
+    count = len(parts)
     whole = pl.BlockSpec((rows, channels), lambda i, at: (0, 0))
     part = pl.BlockSpec((rows, width), lambda i, at: (0, 0))
+    piece = pl.BlockSpec((rows, channels // max(members, 1)), lambda i, at: (0, 0))
     array = jax.ShapeDtypeStruct((rows, channels), jnp.bfloat16)
-    first, last = start is None, bool(gates)
-    extra = (() if first else (start,)) + tuple(gates)
-    return pl.pallas_call(
-        functools.partial(cotangent_kernel, count, first, last),
-        out_shape=[array, array] if last else jax.ShapeDtypeStruct((rows, channels), jnp.float32),
+    cut_array = jax.ShapeDtypeStruct((rows, channels // max(members, 1)), jnp.bfloat16)
+    begin, last = start is None, bool(gates)
+    extra = (() if begin else (start,)) + tuple(gates)
+    return pl.pallas_call(
+        functools.partial(cotangent_kernel, count, begin, last, members),
+        out_shape=[array] + [cut_array] * members
+        if last
+        else jax.ShapeDtypeStruct((rows, channels), jnp.float32),
         grid_spec=pltpu.PrefetchScalarGridSpec(
             num_scalar_prefetch=1,
             grid=(count,),
-            in_specs=[pl.BlockSpec((channels, width), lambda i, at: (0, at[i]))]
+            in_specs=[pl.BlockSpec((channels, width), lambda i, at: (0, at[2 * first + i]))]
             + [part] * count
             + [whole] * len(extra)
             + [ANYWHERE] * len(after),
-            out_specs=[whole, whole] if last else whole,
+            out_specs=[whole] + [piece] * members if last else whole,
             scratch_shapes=[pltpu.VMEM((rows, channels), jnp.float32)] if last else [],
         ),
         compiler_params=pltpu.CompilerParams(vmem_limit_bytes=24 * 2**20),
         cost_estimate=COST,
         name="cotangent_blocks",
-    )(jnp.stack(places).astype(jnp.int32), in_hbm(out_weight), *blocks, *extra, *after)
-
-
-OWN, NEAR, MIDDLE, FAR = (0, 1, 2, 3), (1, 0, 3, 2), (2, 2, 1, 1), (3, 3, 0, 0)
-
-
-def added(*arrays):
-    return sum(wide(array) for array in arrays).astype(jnp.bfloat16)
-
-
-def line_scatter(data, out_weight, width, later):
-    place = lax.axis_index("tp")
-    chip, core = place // 2, place % 2
-
-    def product(tables, other, more=None, after=()):
-        blocks = [2 * of_chip(chip, table) + other for table in tables]
-        return column_products(data, out_weight, blocks, width, more, after)
-
-    others = (MIDDLE, NEAR, OWN)
-    given = product((FAR,), 1 - core, after=later)
-    given_others = product(others, 1 - core, after=(given,))
-    (first,) = product((FAR,), core, swapped(given, "tp", 1), (given_others,))
-    one = hop(first, INWARD)
-    (given_others,) = held_until([given_others], (first,))
-    second, third, own = product(others, core, swapped(given_others, "tp", 1))
-    two_b = hop(second, INWARD)
-
-    def passed(after):
-        (arrived,) = held_until([one], after)
-        through = added(first, arrived)
-        return through, hop(through, ACROSS)
-
-    def ready(two_a, after):
-        across, inward = held_until([two_a, two_b], after)
-        return added(third, across), added(second, inward)
-
-    def rest(final, onward):
-        return added(own, hop(final, OUTWARD + INWARD), hop(onward, ACROSS))
-
-    return first, own, passed, ready, rest
-
-
-def line_cotangents(blocks, tables, out_weight, start=None, gates=(), after=()):
-    place = lax.axis_index("tp")
-    core = place % 2
-    parts, places = [], []
-    for block, table in zip(blocks, tables):
-        source = 2 * of_chip(place // 2, table)
-        parts += [block, swapped(block, "tp", 1)]
-        places += [source + core, source + 1 - core]
-    return cotangent_products(parts, places, out_weight, start, gates, after)
+    )(plan, in_hbm(out_weight), *parts, *extra, *after)
 
 
 def packed_parts(position, key_gate, value_input, filter_taps, members, scale):
@@ -577,67 +596,110 @@
     return grad_key, grad_value, grad_filter
 
 
+def in_line(
+    query_gate, key_gate, value_input, filter_taps, out_weight, out_grad, members, scale
+):
+    length, channels = query_gate.shape
+    groups = filter_taps.shape[1]
+    per_group = channels // groups
+    plan = planned()
+    near, cross = hop(out_grad, INWARD + OUTWARD), hop(out_grad, ACROSS)
+    total = cotangent_products(plan, OWN, (out_grad,), out_weight)
+
+    packed = prepare(plan, key_gate, value_input, filter_taps, members, scale)
+    input_parts = traded(packed, "ctx")
+    conv_parts = convolve(plan, input_parts, length, per_group, (total,))
+    *conv_parts, near, cross = held_until([*conv_parts, near, cross], ())
+    far, skip = hop(near, ACROSS), hop(cross, OUTWARD)
+    gated_out, convolved = gated(plan, traded(conv_parts, "ctx"), query_gate)
+
+    def product(first, count, other, more=(), after=()):
+        return column_products(plan, gated_out, out_weight, first, count, other, more, after)
+
+    given_far, given_middle = product(FAR, 2, 1)
+    far, skip = held_until([far, skip], (given_far,))
+    last = hop(far, OUTWARD)
+    middle_block = added(cross, skip)
+    (first,) = product(FAR, 1, 0, (swapped(given_far, "tp", 1),))
+    one = hop(first, INWARD)
+    (second,) = product(MIDDLE, 1, 0, (swapped(given_middle, "tp", 1),), (first,))
+    near, middle_block = held_until([near, middle_block], (first,))
+    total = cotangent_products(plan, NEAR, (near, middle_block), out_weight, total)
+    given_near, given_own = product(NEAR, 2, 1, (), (second,))
+    (one,) = held_until([one], (total, given_near))
+    through = added(first, one)
+    two_a = hop(through, ACROSS)
+    (second,) = held_until([second], (one,))
+    two_b = hop(second, INWARD)
+
+    (last,) = held_until([last], (total, given_near))
+    grad_query, *grad_parts = cotangent_products(
+        plan,
+        FAR,
+        (added(far, last),),
+        out_weight,
+        total,
+        (convolved, query_gate),
+        (through,),
+        members,
+    )
+    received = (swapped(given_near, "tp", 1), swapped(given_own, "tp", 1))
+    third, own = product(NEAR, 2, 0, received, (grad_parts[0],))
+    grad_parts = traded(grad_parts, "ctx")
+
+    two_a, two_b = held_until([two_a, two_b], tuple(grad_parts[1:]))
+    third, second = added(third, two_a), added(second, two_b)
+    back_parts = correlate(plan, input_parts, grad_parts, per_group, scale, (third, second))
+    projected = added(own, hop(third, OUTWARD + INWARD), hop(second, ACROSS))
+    back_parts = traded(back_parts, "ctx")
+    return projected, grad_query, *finished(plan, back_parts, key_gate, value_input, groups)
+
+
+def anywhere(
+    query_gate, key_gate, value_input, filter_taps, out_weight, out_grad, members, scale
+):
+    length, channels = query_gate.shape
+    groups = filter_taps.shape[1]
+    per_group = channels // groups
+    position = lax.axis_index("ctx")
+    plan = jnp.full((POSITION + 1,), position, jnp.int32)
+    packed = packed_parts(position, key_gate, value_input, filter_taps, members, scale)
+    input_parts = traded(packed, "ctx")
+    conv_parts = traded(convolve(plan, input_parts, length, per_group), "ctx")
+    convolved = joined(conv_parts, position, 1)
+    gated_out = (wide(query_gate) * wide(convolved)).astype(jnp.bfloat16)
+    partial_value = jnp.dot(gated_out, out_weight, preferred_element_type=jnp.float32)
+    projected = lax.psum_scatter(
+        partial_value.astype(jnp.bfloat16), "tp", scatter_dimension=1, tiled=True
+    )
+    dgated = jnp.einsum(
+        "tk,ck->tc",
+        lax.all_gather(out_grad, "tp", axis=1, tiled=True),
+        out_weight,
+        preferred_element_type=jnp.float32,
+    ).astype(jnp.bfloat16)
+    grad_query = (wide(dgated) * wide(convolved)).astype(jnp.bfloat16)
+    conv_grad = (wide(dgated) * wide(query_gate)).astype(jnp.bfloat16)
+    grad_parts = traded(cut(conv_grad, position, members, 1), "ctx")
+    back_parts = correlate(plan, input_parts, grad_parts, per_group, scale)
+    back_parts = traded(back_parts, "ctx")
+    return (
+        projected,
+        grad_query,
+        *unpacked_parts(position, back_parts, key_gate, value_input, groups),
+    )
+
+
 def local(query_gate, key_gate, value_input, filter_taps, out_weight, out_grad):
     length, channels = query_gate.shape
     groups = filter_taps.shape[1]
-    per_group = channels // groups
     members = lax.axis_size("ctx")
-    position = lax.axis_index("ctx")
-    at = position.reshape((1,)).astype(jnp.int32)
-    tap_scale = 1.0 / math.sqrt(length * members)
-    share = channels // members
-    in_line = lax.axis_size("tp") == 8
-
-    if in_line:
-        near, cross = hop(out_grad, INWARD + OUTWARD), hop(out_grad, ACROSS)
-        total = line_cotangents((out_grad,), (OWN,), out_weight)
-    in_tiles = share % 128 == 0 and groups // members % 16 == 0
-    if in_tiles:
-        packed = prepare(at, key_gate, value_input, filter_taps, members, tap_scale)
-    else:
-        packed = packed_parts(position, key_gate, value_input, filter_taps, members, tap_scale)
-    input_parts = traded(packed, "ctx")
-    conv_parts = convolve(at, input_parts, length, per_group, (total,) if in_line else ())
-    if in_line:
-        *conv_parts, near, cross = held_until([*conv_parts, near, cross], ())
-    conv_parts = traded(conv_parts, "ctx")
-    convolved = joined(conv_parts, position, 1)
-    gated_out = (wide(query_gate) * wide(convolved)).astype(jnp.bfloat16)
-    if in_line:
-        far, skip = hop(near, ACROSS), hop(cross, OUTWARD)
-        first, own, passed, ready, rest = line_scatter(
-            gated_out, out_weight, channels, (far, skip)
-        )
-        blocks = (near, added(cross, skip))
-        total = line_cotangents(blocks, (NEAR, MIDDLE), out_weight, total, after=(first,))
-        through, two_a = passed((total,))
-        (last,) = held_until([hop(far, OUTWARD)], (own, total))
-        grad_query, conv_grad = line_cotangents(
-            (added(far, last),), (FAR,), out_weight, total, (convolved, query_gate), (through,)
-        )
-    else:
-        partial_value = jnp.dot(gated_out, out_weight, preferred_element_type=jnp.float32)
-        projected = lax.psum_scatter(
-            partial_value.astype(jnp.bfloat16), "tp", scatter_dimension=1, tiled=True
-        )
-        dgated = jnp.einsum(
-            "tk,ck->tc",
-            lax.all_gather(out_grad, "tp", axis=1, tiled=True),
-            out_weight,
-            preferred_element_type=jnp.float32,
-        ).astype(jnp.bfloat16)
-        grad_query = (wide(dgated) * wide(convolved)).astype(jnp.bfloat16)
-        conv_grad = (wide(dgated) * wide(query_gate)).astype(jnp.bfloat16)
-    grad_parts = traded(cut(conv_grad, position, members, 1), "ctx")
-    arrived = ready(two_a, tuple(grad_parts[1:])) if in_line else ()
-    back_parts = correlate(at, input_parts, grad_parts, per_group, tap_scale, arrived)
-    if in_line:
-        projected = rest(*arrived)
-    back_parts = traded(back_parts, "ctx")
-    unpack = finished if in_tiles else unpacked_parts
-    arguments = (at if in_tiles else position, back_parts, key_gate, value_input, groups)
-    grad_key, grad_value, grad_filter = unpack(*arguments)
-    return (projected, grad_query, grad_key, grad_value, grad_filter)
+    scale = 1.0 / math.sqrt(length * members)
+    fits = channels // members % 128 == 0 and groups // members % 16 == 0
+    body = in_line if lax.axis_size("tp") == 8 and fits else anywhere
+    return body(
+        query_gate, key_gate, value_input, filter_taps, out_weight, out_grad, members, scale
+    )
 
 
 def solution(mesh):

time: 184 us -> 163 us (0.89)
  other arithmetic: 15.8 us -> 0.08 us
  local copies, waits for them, and re-layouts: 10.8 us -> 0.02 us
  Pallas kernels: 69.7 us -> 74.8 us
    convert_element_type x7 -> x0, other arithmetic: 15.5 us -> none  [the longest x6 13.8 us: added(): return sum((wide(array) for array in arrays)).astype(jnp.bfloat16)]
    unnamed x44 -> x8, local copies, waits for them, and re-layouts: 8.58 us -> 0.02 us
    pallas_call x7 -> x16, Pallas kernels: 44.7 us -> 49 us  [the longest x5 24.5 us: column_products(): pl.pallas_call(functools.partial(product_kernel, tiles, count, len(more))...]
    ppermute x10, waiting for transfers between devices: 16.4 us -> 20 us  [hop(): lax.ppermute(array, 'tp', [(2 * i + core, 2 * j + core) for i, j in pairs...]
    ppermute x18 -> x20, waiting for transfers between devices: 29.1 us -> 25.7 us  [swapped(): return lax.ppermute(array, axis, [(i, i ^ step) for i in range(size)])]
    dynamic_update_slice x4 -> x0, local copies, waits for them, and re-layouts: 2 us -> none  [joined(): lax.dynamic_update_slice_in_dim(whole, pieces[step], (position ^ step) *...]
    ppermute x18 -> x20, starting transfers between devices: 15.6 us -> 16.4 us  [swapped(): return lax.ppermute(array, axis, [(i, i ^ step) for i in range(size)])]
  transfers between devices with their start and end apart: 28 -> 30, of which waited for: 9 -> 10; matrix products, arithmetic and copies ran while one was open for 7% -> 0% of each run, Pallas kernels for 34% -> 45%
where the time goes in v6:
time: 163 us; the launch traced here: 162 us
  Pallas kernels  74.8 us (46%)
  waiting for transfers between devices  45.7 us (28%)
  starting transfers between devices  40.5 us (25%)
    ppermute x20, waiting for transfers between devices, swapped(): return lax.ppermute(array, axis, [(i, i ^ step) for i in range(size)])  25.7 us
    pallas_call x5, Pallas kernels, column_products(): pl.pallas_call(functools.partial(product_kernel, tiles, count, len(more))...  24.5 us
    ppermute x10, starting transfers between devices, hop(): lax.ppermute(array, 'tp', [(2 * i + core, 2 * j + core) for i, j in pairs...  24.1 us
    ppermute x10, waiting for transfers between devices, hop(): lax.ppermute(array, 'tp', [(2 * i + core, 2 * j + core) for i, j in pairs...  20 us
    pallas_call x3, Pallas kernels, cotangent_products(): pl.pallas_call(functools.partial(cotangent_kernel, count, begin, last, me...  19.3 us
    ppermute x20, starting transfers between devices, swapped(): return lax.ppermute(array, axis, [(i, i ^ step) for i in range(size)])  16.4 us
    pallas_call x1, Pallas kernels, correlate(): pl.pallas_call(functools.partial(backward_kernel, members, per_group, sca...  13 us
    pallas_call x1, Pallas kernels, convolve(): pl.pallas_call(functools.partial(forward_kernel, members, per_group, widt...  7.92 us
  transfers between devices with their start and end apart: 30, of which 10 were waited for; matrix products, arithmetic and copies ran while one was open for 0% of the time, Pallas kernels for 45%

profile of v6, /device:TPU:0, one launch (start us, length us, event | category | flops | bytes accessed | tf_op | source)
XLA Modules:
  0.0 162.1 jit_solution(8873536664350472774)
XLA Ops:
  1.2 2.7 %collective-permute-start.4 = (bf16[512,1024]{1,0:T(8,128)(2,1)}, bf16[512,1024]{1,0:T(8,128)(2,1)S(1)}, u32[]{:S(2)}, u32[]{:S(2)}) collective-permute-start(bf16[512,1024]{1,0:T(8,128)(2,1)} %refs_0_.1), channel_id=1, source_target_pairs={{0,2},{1,3},{6,4},{7,5},{2,0},{3,1},{4,6},{5,7},{8,10},{9,11},{14,... | collective-permute-start | bytes 3145736 | tf_op jit(solution)/shard_map/ppermute | solution.py:349
  5.8 2.6 %gated_input.1 = (bf16[544,256]{1,0:T(8,128)(2,1)S(1)}, bf16[544,256]{1,0:T(8,128)(2,1)S(1)}, bf16[544,256]{1,0:T(8,128)(2,1)S(1)}, bf16[544,256]{1,0:T(8,128)(2,1)S(1)}) custom-call(s32[9]{0:T(128)S(1)} %plan.1.plan_ref._, bf16[512,1024]{1,0:T(8,128)(2,1)} %refs_4_.5, bf16[512,1024]{1,0:T(8,128)(2,1)} %refs_5_.1, f32[64,512]{1,0:T(8,128)} %bitcast.4), custom_call_target="tpu_custom_call" | custom-call | flops 1048576 | bytes 4096 | tf_op jit(solution)/shard_map/gated_input/pallas_call | solution.py:260
  12.0 5.0 %cotangent_blocks.3.refs_4_ = f32[512,1024]{1,0:T(8,128)S(1)} custom-call(s32[9]{0:T(128)S(1)} %plan.1.plan_ref._, bf16[1024,8192]{1,0:T(8,128)(2,1)} %weight_ref.15, bf16[512,1024]{1,0:T(8,128)(2,1)S(1)} %copy-done.3, bf16[512,1024]{1,0:T(8,128)(2,1)} %collective-permute-done.3.refs_1_), custom_call_target="tpu_custom_call" | custom-call | flops 1048576 | bytes 4096 | tf_op jit(solution)/shard_map/cotangent_blocks/pallas_call | solution.py:542
  18.0 6.4 %collective-permute-done.1.refs_2_ = bf16[544,256]{1,0:T(8,128)(2,1)S(1)} collective-permute-done((bf16[544,256]{1,0:T(8,128)(2,1)S(1)}, bf16[544,256]{1,0:T(8,128)(2,1)S(1)}, u32[]{:S(2)}, u32[]{:S(2)}) %collective-permute-start.1) | collective-permute-done | bytes 278560 | tf_op jit(solution)/shard_map/ppermute | solution.py:316
  24.4 7.9 %causal_conv.1 = (bf16[512,256]{1,0:T(8,128)(2,1)S(1)}, bf16[512,256]{1,0:T(8,128)(2,1)S(1)}, bf16[512,256]{1,0:T(8,128)(2,1)S(1)}, bf16[512,256]{1,0:T(8,128)(2,1)S(1)}) custom-call(s32[9]{0:T(128)S(1)} %plan.1.plan_ref._, bf16[544,256]{1,0:T(8,128)(2,1)S(1)} %get-tuple-element.45.refs_0_, bf16[544,256]{1,0:T(8,128)(2,1)S(1)} %collective-permute-done.refs_1_, ...), custom_call_target="tpu_custom_call" | custom-call | flops 1048576 | bytes 4096 | tf_op jit(solution)/shard_map/causal_conv/pallas_call | solution.py:181
  37.9 3.7 %collective-permute-done.6.refs_1_ = bf16[512,256]{1,0:T(8,128)(2,1)S(1)} collective-permute-done((bf16[512,256]{1,0:T(8,128)(2,1)S(1)}, bf16[512,256]{1,0:T(8,128)(2,1)S(1)}, u32[]{:S(2)}, u32[]{:S(2)}) %collective-permute-start.6) | collective-permute-done | bytes 262176 | tf_op jit(solution)/shard_map/ppermute | solution.py:316
  41.7 4.9 %collective-permute-done.7.refs_2_ = bf16[512,256]{1,0:T(8,128)(2,1)S(1)} collective-permute-done((bf16[512,256]{1,0:T(8,128)(2,1)S(1)}, bf16[512,256]{1,0:T(8,128)(2,1)S(1)}, u32[]{:S(2)}, u32[]{:S(2)}) %collective-permute-start.7) | collective-permute-done | bytes 262176 | tf_op jit(solution)/shard_map/ppermute | solution.py:316
  47.4 5.7 %projection_blocks.5 = (bf16[512,1024]{1,0:T(8,128)(2,1)S(1)}, bf16[512,1024]{1,0:T(8,128)(2,1)S(1)}) custom-call(s32[9]{0:T(128)S(1)} %plan.1.plan_ref._, bf16[512,1024]{1,0:T(8,128)(2,1)S(1)} %get-tuple-element.57.data_ref, bf16[1024,8192]{1,0:T(8,128)(2,1)} %weight_ref.15), custom_call_target="tpu_custom_call" | custom-call | flops 1048576 | bytes 4096 | tf_op jit(solution)/shard_map/projection_blocks/pallas_call | solution.py:475
  53.7 11.1 %collective-permute-done.14.refs_1_ = bf16[512,1024]{1,0:T(8,128)(2,1)S(1)} collective-permute-done((bf16[512,1024]{1,0:T(8,128)(2,1)S(1)}, bf16[512,1024]{1,0:T(8,128)(2,1)S(1)}, u32[]{:S(2)}, u32[]{:S(2)}) %collective-permute-start.14) | collective-permute-done | bytes 1048608 | tf_op jit(solution)/shard_map/ppermute | solution.py:349
  65.1 3.6 %projection_blocks.6.refs_1_.refs_2_.refs_0_ = bf16[512,1024]{1,0:T(8,128)(2,1)S(1)} custom-call(s32[9]{0:T(128)S(1)} %plan.1.plan_ref._, bf16[512,1024]{1,0:T(8,128)(2,1)S(1)} %get-tuple-element.57.data_ref, bf16[1024,8192]{1,0:T(8,128)(2,1)} %weight_ref.15, bf16[512,1024]{1,0:T(8,128)(2,1)S(1)} %collective-permute-done.10.refs_0_), custom_call_target="tpu_custom_call" | custom-call | flops 1048576 | bytes 4096 | tf_op jit(solution)/shard_map/projection_blocks/pallas_call | solution.py:475
  70.6 4.9 %collective-permute-start.19 = (bf16[512,1024]{1,0:T(8,128)(2,1)S(1)}, bf16[512,1024]{1,0:T(8,128)(2,1)S(1)}, u32[]{:S(2)}, u32[]{:S(2)}) collective-permute-start(bf16[512,1024]{1,0:T(8,128)(2,1)S(1)} %projection_blocks.6.refs_1_.refs_2_.refs_0_), channel_id=1, source_target_pairs={{0,2},{1,3},{6,4},{7,5},{8,10},{9,11},{14,12},{15,13},{16,18},{17,... | collective-permute-start | bytes 3145736 | tf_op jit(solution)/shard_map/ppermute | solution.py:349
  75.5 3.6 %projection_blocks.7.refs_0_ = bf16[512,1024]{1,0:T(8,128)(2,1)S(1)} custom-call(s32[9]{0:T(128)S(1)} %plan.1.plan_ref._, bf16[512,1024]{1,0:T(8,128)(2,1)S(1)} %get-tuple-element.57.data_ref, bf16[1024,8192]{1,0:T(8,128)(2,1)} %weight_ref.15, bf16[512,1024]{1,0:T(8,128)(2,1)S(1)} %collective-permute-done.9.refs_0_, ...), custom_call_target="tpu_custom_call" | custom-call | flops 1048576 | bytes 4096 | tf_op jit(solution)/shard_map/projection_blocks/pallas_call | solution.py:475
  79.2 5.7 %projection_blocks.8 = (bf16[512,1024]{1,0:T(8,128)(2,1)S(1)}, bf16[512,1024]{1,0:T(8,128)(2,1)S(1)}) custom-call(s32[9]{0:T(128)S(1)} %plan.1.plan_ref._, bf16[512,1024]{1,0:T(8,128)(2,1)S(1)} %get-tuple-element.57.data_ref, bf16[1024,8192]{1,0:T(8,128)(2,1)} %weight_ref.15, bf16[512,1024]{1,0:T(8,128)(2,1)S(1)} %projection_blocks.7.refs_0_), custom_call_target="tpu_custom_call" | custom-call | flops 1048576 | bytes 4096 | tf_op jit(solution)/shard_map/projection_blocks/pallas_call | solution.py:475
  84.9 7.8 %cotangent_blocks.4.refs_1_.refs_2_ = f32[512,1024]{1,0:T(8,128)S(1)} custom-call(s32[9]{0:T(128)S(1)} %plan.1.plan_ref._, bf16[1024,8192]{1,0:T(8,128)(2,1)} %weight_ref.15, bf16[512,1024]{1,0:T(8,128)(2,1)S(1)} %get-tuple-element.66.refs_0_, bf16[512,1024]{1,0:T(8,128)(2,1)S(1)} %collective-permute-done.16.refs_1_, ...), custom_call_target="tpu_custom_call" | custom-call | flops 1048576 | bytes 4096 | tf_op jit(solution)/shard_map/cotangent_blocks/pallas_call | solution.py:542
  92.6 3.7 %collective-permute-done.15.refs_0_ = bf16[512,1024]{1,0:T(8,128)(2,1)S(1)} collective-permute-done((bf16[512,1024]{1,0:T(8,128)(2,1)S(1)}, bf16[512,1024]{1,0:T(8,128)(2,1)S(1)}, u32[]{:S(2)}, u32[]{:S(2)}) %collective-permute-start.15) | collective-permute-done | bytes 1048608 | tf_op jit(solution)/shard_map/ppermute | solution.py:349
  97.9 4.5 %collective-permute-start.21 = (bf16[512,1024]{1,0:T(8,128)(2,1)S(1)}, bf16[512,1024]{1,0:T(8,128)(2,1)S(1)}, u32[]{:S(2)}, u32[]{:S(2)}) collective-permute-start(bf16[512,1024]{1,0:T(8,128)(2,1)S(1)} %held.12.refs_0_), channel_id=1, source_target_pairs={{0,2},{1,3},{6,4},{7,5},{8,10},{9,11},{14,12},{15,13},{16,18},{17,... | collective-permute-start | bytes 3145736 | tf_op jit(solution)/shard_map/ppermute | solution.py:349
  103.1 6.5 %cotangent_blocks.5 = (bf16[512,1024]{1,0:T(8,128)(2,1)}, bf16[512,256]{1,0:T(8,128)(2,1)S(1)}, bf16[512,256]{1,0:T(8,128)(2,1)S(1)}, bf16[512,256]{1,0:T(8,128)(2,1)S(1)}, bf16[512,256]{1,0:T(8,128)(2,1)S(1)}) custom-call(s32[9]{0:T(128)S(1)} %plan.1.plan_ref._, bf16[1024,8192]{1,0:T(8,128)(2,1)} %weight_ref.15, bf16[512,1024]{1,0:T(8,128)(2,1)S(1)} %added.7.refs_0_, ...), custom_call_target="tpu_custom_call" | custom-call | flops 1048576 | bytes 4096 | tf_op jit(solution)/shard_map/cotangent_blocks/pallas_call | solution.py:542
  113.1 5.8 %projection_blocks.9 = (bf16[512,1024]{1,0:T(8,128)(2,1)S(1)}, bf16[512,1024]{1,0:T(8,128)(2,1)S(1)}) custom-call(s32[9]{0:T(128)S(1)} %plan.1.plan_ref._, bf16[512,1024]{1,0:T(8,128)(2,1)S(1)} %get-tuple-element.57.data_ref, bf16[1024,8192]{1,0:T(8,128)(2,1)} %weight_ref.15, bf16[512,1024]{1,0:T(8,128)(2,1)S(1)} %collective-permute-done.11.refs_0_, ...), custom_call_target="tpu_custom_call" | custom-call | flops 1048576 | bytes 4096 | tf_op jit(solution)/shard_map/projection_blocks/pallas_call | solution.py:475
  118.9 4.9 %collective-permute-done.21.refs_1_ = bf16[512,1024]{1,0:T(8,128)(2,1)S(1)} collective-permute-done((bf16[512,1024]{1,0:T(8,128)(2,1)S(1)}, bf16[512,1024]{1,0:T(8,128)(2,1)S(1)}, u32[]{:S(2)}, u32[]{:S(2)}) %collective-permute-start.21) | collective-permute-done | bytes 1048608 | tf_op jit(solution)/shard_map/ppermute | solution.py:349
  125.4 6.4 %collective-permute-start.25 = (bf16[512,1024]{1,0:T(8,128)(2,1)S(1)}, bf16[512,1024]{1,0:T(8,128)(2,1)S(1)}, u32[]{:S(2)}, u32[]{:S(2)}) collective-permute-start(bf16[512,1024]{1,0:T(8,128)(2,1)S(1)} %added.9.refs_8_), channel_id=1, source_target_pairs={{2,0},{3,1},{4,6},{5,7},{0,2},{1,3},{6,4},{7,5},{10,8},{11,9},{12,... | collective-permute-start | bytes 3145736 | tf_op jit(solution)/shard_map/ppermute | solution.py:349
  131.9 13.0 %causal_conv_grads.1 = (bf16[544,256]{1,0:T(8,128)(2,1)S(1)}, bf16[544,256]{1,0:T(8,128)(2,1)S(1)}, bf16[544,256]{1,0:T(8,128)(2,1)S(1)}, bf16[544,256]{1,0:T(8,128)(2,1)S(1)}) custom-call(s32[9]{0:T(128)S(1)} %plan.1.plan_ref._, bf16[544,256]{1,0:T(8,128)(2,1)S(1)} %get-tuple-element.45.refs_0_, bf16[544,256]{1,0:T(8,128)(2,1)S(1)} %collective-permute-done.refs_1_, ...), custom_call_target="tpu_custom_call" | custom-call | flops 1048576 | bytes 4096 | tf_op jit(solution)/shard_map/causal_conv_grads/pallas_call | solution.py:202
  148.4 5.5 %collective-permute-done.27.refs_1_ = bf16[544,256]{1,0:T(8,128)(2,1)S(1)} collective-permute-done((bf16[544,256]{1,0:T(8,128)(2,1)S(1)}, bf16[544,256]{1,0:T(8,128)(2,1)S(1)}, u32[]{:S(2)}, u32[]{:S(2)}) %collective-permute-start.27) | collective-permute-done | bytes 278560 | tf_op jit(solution)/shard_map/ppermute | solution.py:316
  153.9 4.2 %collective-permute-done.28.refs_2_ = bf16[544,256]{1,0:T(8,128)(2,1)S(1)} collective-permute-done((bf16[544,256]{1,0:T(8,128)(2,1)S(1)}, bf16[544,256]{1,0:T(8,128)(2,1)S(1)}, u32[]{:S(2)}, u32[]{:S(2)}) %collective-permute-start.28) | collective-permute-done | bytes 278560 | tf_op jit(solution)/shard_map/ppermute | solution.py:316
  158.1 2.3 %input_gradients.1 = (bf16[512,1024]{1,0:T(8,128)(2,1)}, bf16[512,1024]{1,0:T(8,128)(2,1)}, f32[64,512]{1,0:T(8,128)}) custom-call(s32[9]{0:T(128)S(1)} %plan.1.plan_ref._, bf16[544,256]{1,0:T(8,128)(2,1)S(1)} %get-tuple-element.78.refs_0_, bf16[544,256]{1,0:T(8,128)(2,1)S(1)} %collective-permute-done.27.refs_1_, ...), custom_call_target="tpu_custom_call" | custom-call | flops 1048576 | bytes 4096 | tf_op jit(solution)/shard_map/input_gradients/pallas_call | solution.py:302
  (72 shorter events, 28.8 us)
Async XLA Ops:
  1.2 31.2 %collective-permute-start.4 = (bf16[512,1024]{1,0:T(8,128)(2,1)}, bf16[512,1024]{1,0:T(8,128)(2,1)S(1)}, u32[]{:S(2)}, u32[]{:S(2)}) collective-permute-start(bf16[512,1024]{1,0:T(8,128)(2,1)} %refs_0_.1), channel_id=1, source_target_pairs={{0,2},{1,3},{6,4},{7,5},{2,0},{3,1},{4,6},{5,7},{8,10},{9,11},{14,... | collective-permute-start | bytes 3145736 | tf_op jit(solution)/shard_map/ppermute | solution.py:349
  3.8 28.5 %collective-permute-start.5 = (bf16[512,1024]{1,0:T(8,128)(2,1)}, bf16[512,1024]{1,0:T(8,128)(2,1)S(1)}, u32[]{:S(2)}, u32[]{:S(2)}) collective-permute-start(bf16[512,1024]{1,0:T(8,128)(2,1)} %refs_0_.1), channel_id=1, source_target_pairs={{2,4},{3,5},{4,2},{5,3},{10,12},{11,13},{12,10},{13,11},{18,20},{1... | collective-permute-start | bytes 3145736 | tf_op jit(solution)/shard_map/ppermute | solution.py:349
  10.0 14.4 %collective-permute-start.1 = (bf16[544,256]{1,0:T(8,128)(2,1)S(1)}, bf16[544,256]{1,0:T(8,128)(2,1)S(1)}, u32[]{:S(2)}, u32[]{:S(2)}) collective-permute-start(bf16[544,256]{1,0:T(8,128)(2,1)S(1)} %get-tuple-element.47), channel_id=1, source_target_pairs={{0,16},{8,24},{16,0},{24,8},{1,17},{9,25},{17,1},{25,9},{2,18},{10... | collective-permute-start | bytes 835592 | tf_op jit(solution)/shard_map/ppermute | solution.py:316
  11.5 12.9 %collective-permute-start.2 = (bf16[544,256]{1,0:T(8,128)(2,1)S(1)}, bf16[544,256]{1,0:T(8,128)(2,1)S(1)}, u32[]{:S(2)}, u32[]{:S(2)}) collective-permute-start(bf16[544,256]{1,0:T(8,128)(2,1)S(1)} %get-tuple-element.48), channel_id=1, source_target_pairs={{0,24},{8,16},{16,8},{24,0},{1,25},{9,17},{17,9},{25,1},{2,26},{10... | collective-permute-start | bytes 835592 | tf_op jit(solution)/shard_map/ppermute | solution.py:316
  33.7 12.9 %collective-permute-start.7 = (bf16[512,256]{1,0:T(8,128)(2,1)S(1)}, bf16[512,256]{1,0:T(8,128)(2,1)S(1)}, u32[]{:S(2)}, u32[]{:S(2)}) collective-permute-start(bf16[512,256]{1,0:T(8,128)(2,1)S(1)} %get-tuple-element.55), channel_id=1, source_target_pairs={{0,16},{8,24},{16,0},{24,8},{1,17},{9,25},{17,1},{25,9},{2,18},{10... | collective-permute-start | bytes 786440 | tf_op jit(solution)/shard_map/ppermute | solution.py:316
  34.5 12.1 %collective-permute-start.8 = (bf16[512,256]{1,0:T(8,128)(2,1)S(1)}, bf16[512,256]{1,0:T(8,128)(2,1)S(1)}, u32[]{:S(2)}, u32[]{:S(2)}) collective-permute-start(bf16[512,256]{1,0:T(8,128)(2,1)S(1)} %get-tuple-element.56), channel_id=1, source_target_pairs={{0,24},{8,16},{16,8},{24,0},{1,25},{9,17},{17,9},{25,1},{2,26},{10... | collective-permute-start | bytes 786440 | tf_op jit(solution)/shard_map/ppermute | solution.py:316
  35.9 17.8 %collective-permute-start.13 = (bf16[512,1024]{1,0:T(8,128)(2,1)S(1)}, bf16[512,1024]{1,0:T(8,128)(2,1)S(1)}, u32[]{:S(2)}, u32[]{:S(2)}) collective-permute-start(bf16[512,1024]{1,0:T(8,128)(2,1)S(1)} %get-tuple-element.62.refs_0_), channel_id=1, source_target_pairs={{2,4},{3,5},{4,2},{5,3},{10,12},{11,13},{12,10},{13,11},{18,20},{1... | collective-permute-start | bytes 3145736 | tf_op jit(solution)/shard_map/ppermute | solution.py:349
  36.6 28.1 %collective-permute-start.14 = (bf16[512,1024]{1,0:T(8,128)(2,1)S(1)}, bf16[512,1024]{1,0:T(8,128)(2,1)S(1)}, u32[]{:S(2)}, u32[]{:S(2)}) collective-permute-start(bf16[512,1024]{1,0:T(8,128)(2,1)S(1)} %get-tuple-element.63.refs_0_), channel_id=1, source_target_pairs={{2,0},{3,1},{4,6},{5,7},{10,8},{11,9},{12,14},{13,15},{18,16},{19,... | collective-permute-start | bytes 3145736 | tf_op jit(solution)/shard_map/ppermute | solution.py:349
  53.1 12.0 %collective-permute-start.10 = (bf16[512,1024]{1,0:T(8,128)(2,1)S(1)}, bf16[512,1024]{1,0:T(8,128)(2,1)S(1)}, u32[]{:S(2)}, u32[]{:S(2)}) collective-permute-start(bf16[512,1024]{1,0:T(8,128)(2,1)S(1)} %get-tuple-element.59.refs_2_), channel_id=1, source_target_pairs={{0,1},{1,0},{2,3},{3,2},{4,5},{5,4},{6,7},{7,6},{8,9},{9,8},{10,11... | collective-permute-start | bytes 3145736 | tf_op jit(solution)/shard_map/ppermute | solution.py:316
  53.2 22.3 %collective-permute-start.9 = (bf16[512,1024]{1,0:T(8,128)(2,1)S(1)}, bf16[512,1024]{1,0:T(8,128)(2,1)S(1)}, u32[]{:S(2)}, u32[]{:S(2)}) collective-permute-start(bf16[512,1024]{1,0:T(8,128)(2,1)S(1)} %get-tuple-element.58), channel_id=1, source_target_pairs={{0,1},{1,0},{2,3},{3,2},{4,5},{5,4},{6,7},{7,6},{8,9},{9,8},{10,11... | collective-permute-start | bytes 3145736 | tf_op jit(solution)/shard_map/ppermute | solution.py:316
  68.8 16.1 %collective-permute-start.16 = (bf16[512,1024]{1,0:T(8,128)(2,1)S(1)}, bf16[512,1024]{1,0:T(8,128)(2,1)S(1)}, u32[]{:S(2)}, u32[]{:S(2)}) collective-permute-start(bf16[512,1024]{1,0:T(8,128)(2,1)S(1)} %get-tuple-element.66.refs_0_), channel_id=1, source_target_pairs={{0,1},{1,0},{2,3},{3,2},{4,5},{5,4},{6,7},{7,6},{8,9},{9,8},{10,11... | collective-permute-start | bytes 3145736 | tf_op jit(solution)/shard_map/ppermute | solution.py:316
  68.8 16.0 %collective-permute-start.17 = (bf16[512,1024]{1,0:T(8,128)(2,1)S(1)}, bf16[512,1024]{1,0:T(8,128)(2,1)S(1)}, u32[]{:S(2)}, u32[]{:S(2)}) collective-permute-start(bf16[512,1024]{1,0:T(8,128)(2,1)S(1)} %get-tuple-element.67.refs_2_), channel_id=1, source_target_pairs={{0,1},{1,0},{2,3},{3,2},{4,5},{5,4},{6,7},{7,6},{8,9},{9,8},{10,11... | collective-permute-start | bytes 3145736 | tf_op jit(solution)/shard_map/ppermute | solution.py:316
  69.3 27.0 %collective-permute-start.15 = (bf16[512,1024]{1,0:T(8,128)(2,1)S(1)}, bf16[512,1024]{1,0:T(8,128)(2,1)S(1)}, u32[]{:S(2)}, u32[]{:S(2)}) collective-permute-start(bf16[512,1024]{1,0:T(8,128)(2,1)S(1)} %get-tuple-element.64.refs_0_), channel_id=1, source_target_pairs={{2,0},{3,1},{4,6},{5,7},{10,8},{11,9},{12,14},{13,15},{18,16},{19,... | collective-permute-start | bytes 3145736 | tf_op jit(solution)/shard_map/ppermute | solution.py:349
  70.6 27.0 %collective-permute-start.19 = (bf16[512,1024]{1,0:T(8,128)(2,1)S(1)}, bf16[512,1024]{1,0:T(8,128)(2,1)S(1)}, u32[]{:S(2)}, u32[]{:S(2)}) collective-permute-start(bf16[512,1024]{1,0:T(8,128)(2,1)S(1)} %projection_blocks.6.refs_1_.refs_2_.refs_0_), channel_id=1, source_target_pairs={{0,2},{1,3},{6,4},{7,5},{8,10},{9,11},{14,12},{15,13},{16,18},{17,... | collective-permute-start | bytes 3145736 | tf_op jit(solution)/shard_map/ppermute | solution.py:349
  96.7 14.3 %collective-permute-start.11 = (bf16[512,1024]{1,0:T(8,128)(2,1)S(1)}, bf16[512,1024]{1,0:T(8,128)(2,1)S(1)}, u32[]{:S(2)}, u32[]{:S(2)}) collective-permute-start(bf16[512,1024]{1,0:T(8,128)(2,1)S(1)} %get-tuple-element.60.refs_2_), channel_id=1, source_target_pairs={{0,1},{1,0},{2,3},{3,2},{4,5},{5,4},{6,7},{7,6},{8,9},{9,8},{10,11... | collective-permute-start | bytes 3145736 | tf_op jit(solution)/shard_map/ppermute | solution.py:316
  97.2 14.4 %collective-permute-start.12 = (bf16[512,1024]{1,0:T(8,128)(2,1)S(1)}, bf16[512,1024]{1,0:T(8,128)(2,1)S(1)}, u32[]{:S(2)}, u32[]{:S(2)}) collective-permute-start(bf16[512,1024]{1,0:T(8,128)(2,1)S(1)} %get-tuple-element.61), channel_id=1, source_target_pairs={{0,1},{1,0},{2,3},{3,2},{4,5},{5,4},{6,7},{7,6},{8,9},{9,8},{10,11... | collective-permute-start | bytes 3145736 | tf_op jit(solution)/shard_map/ppermute | solution.py:316
  97.9 25.9 %collective-permute-start.21 = (bf16[512,1024]{1,0:T(8,128)(2,1)S(1)}, bf16[512,1024]{1,0:T(8,128)(2,1)S(1)}, u32[]{:S(2)}, u32[]{:S(2)}) collective-permute-start(bf16[512,1024]{1,0:T(8,128)(2,1)S(1)} %held.12.refs_0_), channel_id=1, source_target_pairs={{0,2},{1,3},{6,4},{7,5},{8,10},{9,11},{14,12},{15,13},{16,18},{17,... | collective-permute-start | bytes 3145736 | tf_op jit(solution)/shard_map/ppermute | solution.py:349
  102.4 21.4 %collective-permute-start.20 = (bf16[512,1024]{1,0:T(8,128)(2,1)S(1)}, bf16[512,1024]{1,0:T(8,128)(2,1)S(1)}, u32[]{:S(2)}, u32[]{:S(2)}) collective-permute-start(bf16[512,1024]{1,0:T(8,128)(2,1)S(1)} %added.8.refs_5_), channel_id=1, source_target_pairs={{2,4},{3,5},{4,2},{5,3},{10,12},{11,13},{12,10},{13,11},{18,20},{1... | collective-permute-start | bytes 3145736 | tf_op jit(solution)/shard_map/ppermute | solution.py:349
  109.6 14.2 %collective-permute-start.22 = (bf16[512,256]{1,0:T(8,128)(2,1)S(1)}, bf16[512,256]{1,0:T(8,128)(2,1)S(1)}, u32[]{:S(2)}, u32[]{:S(2)}) collective-permute-start(bf16[512,256]{1,0:T(8,128)(2,1)S(1)} %get-tuple-element.72), channel_id=1, source_target_pairs={{0,8},{8,0},{16,24},{24,16},{1,9},{9,1},{17,25},{25,17},{2,10},{10... | collective-permute-start | bytes 786440 | tf_op jit(solution)/shard_map/ppermute | solution.py:316
  111.0 12.8 %collective-permute-start.23 = (bf16[512,256]{1,0:T(8,128)(2,1)S(1)}, bf16[512,256]{1,0:T(8,128)(2,1)S(1)}, u32[]{:S(2)}, u32[]{:S(2)}) collective-permute-start(bf16[512,256]{1,0:T(8,128)(2,1)S(1)} %get-tuple-element.73), channel_id=1, source_target_pairs={{0,16},{8,24},{16,0},{24,8},{1,17},{9,25},{17,1},{25,9},{2,18},{10... | collective-permute-start | bytes 786440 | tf_op jit(solution)/shard_map/ppermute | solution.py:316
  111.6 12.2 %collective-permute-start.24 = (bf16[512,256]{1,0:T(8,128)(2,1)S(1)}, bf16[512,256]{1,0:T(8,128)(2,1)S(1)}, u32[]{:S(2)}, u32[]{:S(2)}) collective-permute-start(bf16[512,256]{1,0:T(8,128)(2,1)S(1)} %get-tuple-element.74), channel_id=1, source_target_pairs={{0,24},{8,16},{16,8},{24,0},{1,25},{9,17},{17,9},{25,1},{2,26},{10... | collective-permute-start | bytes 786440 | tf_op jit(solution)/shard_map/ppermute | solution.py:316
  124.1 36.3 %collective-permute-start.26 = (bf16[512,1024]{1,0:T(8,128)(2,1)S(1)}, bf16[512,1024]{1,0:T(8,128)(2,1)S(1)}, u32[]{:S(2)}, u32[]{:S(2)}) collective-permute-start(bf16[512,1024]{1,0:T(8,128)(2,1)S(1)} %added.10.refs_9_), channel_id=1, source_target_pairs={{2,4},{3,5},{4,2},{5,3},{10,12},{11,13},{12,10},{13,11},{18,20},{1... | collective-permute-start | bytes 3145736 | tf_op jit(solution)/shard_map/ppermute | solution.py:349
  125.4 35.0 %collective-permute-start.25 = (bf16[512,1024]{1,0:T(8,128)(2,1)S(1)}, bf16[512,1024]{1,0:T(8,128)(2,1)S(1)}, u32[]{:S(2)}, u32[]{:S(2)}) collective-permute-start(bf16[512,1024]{1,0:T(8,128)(2,1)S(1)} %added.9.refs_8_), channel_id=1, source_target_pairs={{2,0},{3,1},{4,6},{5,7},{0,2},{1,3},{6,4},{7,5},{10,8},{11,9},{12,... | collective-permute-start | bytes 3145736 | tf_op jit(solution)/shard_map/ppermute | solution.py:349
  146.4 11.7 %collective-permute-start.28 = (bf16[544,256]{1,0:T(8,128)(2,1)S(1)}, bf16[544,256]{1,0:T(8,128)(2,1)S(1)}, u32[]{:S(2)}, u32[]{:S(2)}) collective-permute-start(bf16[544,256]{1,0:T(8,128)(2,1)S(1)} %get-tuple-element.80), channel_id=1, source_target_pairs={{0,16},{8,24},{16,0},{24,8},{1,17},{9,25},{17,1},{25,9},{2,18},{10... | collective-permute-start | bytes 835592 | tf_op jit(solution)/shard_map/ppermute | solution.py:316
  (10 other events, 147.3 us)

commit v7 on v6

--- a/solution.py
+++ b/solution.py
@@ -14,12 +14,15 @@
 
 
 def lag_matrix(row, length):
-    lanes = lax.broadcasted_iota(jnp.int32, (BLOCK, length), 1)
-    rows = lax.broadcasted_iota(jnp.int32, (BLOCK, length), 0)
+    lanes = lax.broadcasted_iota(jnp.int32, (BLOCK, BLOCK), 1)
+    rows = lax.broadcasted_iota(jnp.int32, (BLOCK, BLOCK), 0)
     spread = pltpu.roll(
         jnp.broadcast_to(row, (BLOCK, length)), 0, axis=1, stride=1, stride_axis=0
     )
-    return jnp.where(lanes >= rows, spread, 0.0).astype(jnp.bfloat16)
+    first = jnp.where(lanes >= rows, spread[:, :BLOCK], 0.0)
+    return jnp.concatenate(
+        [first.astype(jnp.bfloat16), spread[:, BLOCK:].astype(jnp.bfloat16)], axis=1
+    )
 
 
 def stacked(ref, start, rows, members, width):
@@ -89,7 +92,7 @@
         spread_out(out_scr, start, per_group, value, members, width)
         return carry
 
-    lax.fori_loop(0, groups, one_group, 0)
+    lax.fori_loop(0, groups, one_group, 0, unroll=2)
     for step in range(members):
         outputs[step][...] = out_scr[position ^ step].T
 
@@ -144,17 +147,15 @@
         spread_out(
             out_scr, start, per_group, total.astype(jnp.bfloat16), members, width
         )
-        product = jnp.concatenate(products, axis=1)
-        lanes = lax.broadcasted_iota(jnp.int32, (BLOCK, length), 1)
-        back = BLOCK - 1 - lax.broadcasted_iota(jnp.int32, (BLOCK, length), 0)
-        product = jnp.where(lanes >= back, product, 0.0)
+        kept = jnp.where(rows_of + lanes_of >= BLOCK - 1, products[0][:, :BLOCK], 0.0)
+        product = jnp.concatenate([kept, products[0][:, BLOCK:], *products[1:]], axis=1)
         product = pltpu.roll(
             product, length - (BLOCK - 1), axis=1, stride=1, stride_axis=0
         )
         grad_scr[pl.ds(group, 1), :] = jnp.sum(product, axis=0, keepdims=True) * scale
         return carry
 
-    lax.fori_loop(0, groups, one_group, 0)
+    lax.fori_loop(0, groups, one_group, 0, unroll=2)
     for step in range(members):
         at = position ^ step
         outputs[step][:width] = out_scr[at].T
@@ -222,8 +223,8 @@
     return pltpu.with_memory_space_constraint(array, pltpu.HBM)
 
 
-def prepare_kernel(members, scale, plan_ref, key_ref, value_ref, taps_ref, *outputs):
-    position = plan_ref[POSITION]
+def prepare_kernel(members, scale, who_ref, key_ref, value_ref, taps_ref, *outputs):
+    position = who_ref[0]
     step_no = pl.program_id(0)
     rows, channels = key_ref.shape
     share = channels // members
@@ -251,7 +252,7 @@
                 ]
 
 
-def prepare(plan, key_gate, value_input, filter_taps, members, scale):
+def prepare(who, key_gate, value_input, filter_taps, members, scale):
     width, channels = key_gate.shape
     share = channels // members
     rows = width + filter_taps.size // members // share
@@ -266,48 +267,59 @@
         compiler_params=pltpu.CompilerParams(vmem_limit_bytes=24 * 2**20),
         cost_estimate=COST,
         name="gated_input",
-    )(plan, in_hbm(key_gate), in_hbm(value_input), in_hbm(filter_taps.T))
+    )(who, in_hbm(key_gate), in_hbm(value_input), in_hbm(filter_taps.T))
 
 
 def finish_kernel(members, plan_ref, *refs):
     parts = refs[:members]
-    key_ref, value_ref, key_out, value_out, taps_out = refs[members:]
+    key_ref, value_ref = refs[members : members + 2]
+    key_out, value_out, taps_out = refs[-3:]
     position = plan_ref[POSITION]
-    width, channels = key_ref.shape
+    step_no = pl.program_id(0)
+    rows, channels = key_ref.shape
     share = channels // members
-    groups = taps_out.shape[0] // members
+    groups, width = taps_out.shape
+    groups = groups // members
+    here = pl.ds(pl.multiple_of(step_no * rows, rows), rows)
     for step in range(members):
         at = position ^ step
         columns = pl.ds(pl.multiple_of(at * share, share), share)
-        grad = parts[step][:width].astype(jnp.float32)
+        grad = parts[step][here, :].astype(jnp.float32)
         key_out[:, columns] = (grad * value_ref[:, columns].astype(jnp.float32)).astype(
             jnp.bfloat16
         )
         value_out[:, columns] = (grad * key_ref[:, columns].astype(jnp.float32)).astype(
             jnp.bfloat16
         )
-        taps = [
-            parts[step][width + chunk * groups : width + (chunk + 1) * groups, :]
-            for chunk in range(width // share)
-        ]
-        taps_out[pl.ds(pl.multiple_of(at * groups, groups), groups), :] = jnp.concatenate(
-            taps, axis=1
-        ).astype(jnp.float32)
-
-
-def finished(plan, parts, key_gate, value_input, groups):
+
+    @pl.when(step_no == 0)
+    def _():
+        for step in range(members):
+            at = position ^ step
+            taps = [
+                parts[step][width + chunk * groups : width + (chunk + 1) * groups, :]
+                for chunk in range(width // share)
+            ]
+            taps_out[pl.ds(pl.multiple_of(at * groups, groups), groups), :] = jnp.concatenate(
+                taps, axis=1
+            ).astype(jnp.float32)
+
+
+def finished(plan, parts, key_gate, value_input, groups, after=()):
     members = len(parts)
     width, channels = key_gate.shape
     array = jax.ShapeDtypeStruct((width, channels), jnp.bfloat16)
+    part = pl.BlockSpec((width // 4, channels), lambda i: (i, 0))
     grad_key, grad_value, taps = pl.pallas_call(
         functools.partial(finish_kernel, members),
         out_shape=[array, array, jax.ShapeDtypeStruct((groups, width), jnp.float32)],
-        in_specs=[SMEM] + [VMEM] * (members + 2),
-        out_specs=[VMEM] * 3,
+        grid=(4,),
+        in_specs=[SMEM] + [VMEM] * members + [part] * 2 + [ANYWHERE] * len(after),
+        out_specs=[part, part, pl.BlockSpec((groups, width), lambda i: (0, 0))],
         compiler_params=pltpu.CompilerParams(vmem_limit_bytes=24 * 2**20),
         cost_estimate=COST,
         name="input_gradients",
-    )(plan, *parts, key_gate, value_input)
+    )(plan, *parts, in_hbm(key_gate), in_hbm(value_input), *after)
     return grad_key, grad_value, taps.T
 
 
@@ -372,8 +384,7 @@
     plan_ref[POSITION] = who_ref[0]
 
 
-def planned():
-    who = jnp.stack([lax.axis_index("ctx"), lax.axis_index("tp")]).astype(jnp.int32)
+def planned(who):
     return pl.pallas_call(
         plan_kernel,
         out_shape=jax.ShapeDtypeStruct((POSITION + 1,), jnp.int32),
@@ -446,45 +457,48 @@
     )(plan, *parts, query_gate)
 
 
-def product_kernel(tiles, count, extra, _, data_ref, weight_ref, *refs):
-    more, outputs = refs[:extra], refs[-count:]
+def product_kernel(steps, joins, extra, _, data_ref, weight_ref, *refs):
+    more, outputs = refs[:extra], refs[-(steps // joins) :]
     product = jnp.dot(data_ref[...], weight_ref[...], preferred_element_type=jnp.float32)
-    for number, out_ref in enumerate(outputs):
-
-        @pl.when(pl.program_id(0) // tiles == number)
-        def _(number=number, out_ref=out_ref):
+    for number in range(steps):
+        out_ref = outputs[number // joins]
+        wide_out = out_ref.shape[1] > product.shape[1]
+
+        @pl.when(pl.program_id(0) == number)
+        def _(number=number, out_ref=out_ref, wide_out=wide_out):
             total = product + wide(more[number][...]) if more else product
-            out_ref[...] = total.astype(jnp.bfloat16)
-
-
-def column_products(plan, data, out_weight, first, count, other, more=(), after=()):
+            if wide_out:
+                width = product.shape[1]
+                at = number % joins * width
+                out_ref[:, at : at + width] = total.astype(jnp.bfloat16)
+            else:
+                out_ref[...] = total.astype(jnp.bfloat16)
+
+
+def column_products(
+    plan, data, out_weight, first, count, other, more=(), after=(), tiles=1, joins=1
+):
     rows, depth = data.shape
     width = data.shape[1]
-    tile = min(width, 512)
-    tiles = width // tile
-
-    def column(number):
-        return pl.BlockSpec(
-            (rows, tile), lambda i, at: (0, jnp.clip(i - number * tiles, 0, tiles - 1))
-        )
+    tile = width // tiles
+    steps = count * tiles
 
     def weights(i, at):
         return 0, at[2 * (first - i // tiles) + other] * tiles + i % tiles
 
-    columns = [column(number) for number in range(count)]
-    return pl.pallas_call(
-        functools.partial(product_kernel, tiles, count, len(more)),
-        out_shape=[jax.ShapeDtypeStruct((rows, width), jnp.bfloat16)] * count,
+    def whole(array_width):
+        return pl.BlockSpec((rows, array_width), lambda i, at: (0, 0))
+
+    return pl.pallas_call(
+        functools.partial(product_kernel, steps, joins, len(more)),
+        out_shape=[jax.ShapeDtypeStruct((rows, tile * joins), jnp.bfloat16)] * (steps // joins),
         grid_spec=pltpu.PrefetchScalarGridSpec(
             num_scalar_prefetch=1,
-            grid=(count * tiles,),
-            in_specs=[
-                pl.BlockSpec((rows, depth), lambda i, at: (0, 0)),
-                pl.BlockSpec((depth, tile), weights),
-            ]
-            + columns[: len(more)]
+            grid=(steps,),
+            in_specs=[whole(depth), pl.BlockSpec((depth, tile), weights)]
+            + [whole(tile)] * len(more)
             + [ANYWHERE] * len(after),
-            out_specs=columns,
+            out_specs=[whole(tile * joins)] * (steps // joins),
         ),
         compiler_params=pltpu.CompilerParams(vmem_limit_bytes=24 * 2**20),
         cost_estimate=COST,
@@ -525,11 +539,14 @@
                 parts[step][...] = (dgated * wide(query_ref[:, columns])).astype(jnp.bfloat16)
 
 
+def both(blocks):
+    return [part for block in blocks for part in (block, swapped(block, "tp", 1))]
+
+
 def cotangent_products(
-    plan, first, blocks, out_weight, start=None, gates=(), after=(), members=0
+    plan, first, parts, out_weight, start=None, gates=(), after=(), members=0
 ):
-    parts = [part for block in blocks for part in (block, swapped(block, "tp", 1))]
-    rows, width = blocks[0].shape
+    rows, width = parts[0].shape
     channels = out_weight.shape[0]
     count = len(parts)
     whole = pl.BlockSpec((rows, channels), lambda i, at: (0, 0))
@@ -547,7 +564,7 @@
         grid_spec=pltpu.PrefetchScalarGridSpec(
             num_scalar_prefetch=1,
             grid=(count,),
-            in_specs=[pl.BlockSpec((channels, width), lambda i, at: (0, at[2 * first + i]))]
+            in_specs=[pl.BlockSpec((channels, width), lambda i, at: (0, at[first + i]))]
             + [part] * count
             + [whole] * len(extra)
             + [ANYWHERE] * len(after),
@@ -602,57 +619,62 @@
     length, channels = query_gate.shape
     groups = filter_taps.shape[1]
     per_group = channels // groups
-    plan = planned()
+    who = jnp.stack([lax.axis_index("ctx"), lax.axis_index("tp")]).astype(jnp.int32)
+    plan = planned(who)
     near, cross = hop(out_grad, INWARD + OUTWARD), hop(out_grad, ACROSS)
-    total = cotangent_products(plan, OWN, (out_grad,), out_weight)
-
-    packed = prepare(plan, key_gate, value_input, filter_taps, members, scale)
+    total = cotangent_products(plan, 2 * OWN, both([out_grad]), out_weight)
+
+    packed = prepare(who, key_gate, value_input, filter_taps, members, scale)
     input_parts = traded(packed, "ctx")
     conv_parts = convolve(plan, input_parts, length, per_group, (total,))
     *conv_parts, near, cross = held_until([*conv_parts, near, cross], ())
     far, skip = hop(near, ACROSS), hop(cross, OUTWARD)
     gated_out, convolved = gated(plan, traded(conv_parts, "ctx"), query_gate)
 
-    def product(first, count, other, more=(), after=()):
-        return column_products(plan, gated_out, out_weight, first, count, other, more, after)
+    def product(first, count, other, more=(), after=(), tiles=1, joins=1):
+        return column_products(
+            plan, gated_out, out_weight, first, count, other, more, after, tiles, joins
+        )
 
     given_far, given_middle = product(FAR, 2, 1)
     far, skip = held_until([far, skip], (given_far,))
     last = hop(far, OUTWARD)
-    middle_block = added(cross, skip)
     (first,) = product(FAR, 1, 0, (swapped(given_far, "tp", 1),))
     one = hop(first, INWARD)
     (second,) = product(MIDDLE, 1, 0, (swapped(given_middle, "tp", 1),), (first,))
-    near, middle_block = held_until([near, middle_block], (first,))
-    total = cotangent_products(plan, NEAR, (near, middle_block), out_weight, total)
+    beside = hop(second, ACROSS)
+    near, cross = held_until([near, cross], (second,))
+    total = cotangent_products(
+        plan, 2 * NEAR, both([near, added(cross, skip)]), out_weight, total
+    )
     given_near, given_own = product(NEAR, 2, 1, (), (second,))
     (one,) = held_until([one], (total, given_near))
     through = added(first, one)
-    two_a = hop(through, ACROSS)
+    over_two = hop(through, ((1, 3), (2, 0)))
     (second,) = held_until([second], (one,))
-    two_b = hop(second, INWARD)
-
-    (last,) = held_until([last], (total, given_near))
+    to_middle = hop(second, ((0, 2), (3, 1)))
+
+    last, beside = held_until([last, beside], (total, given_near))
+    far_block, far_other = both([added(far, last)])
+    total = cotangent_products(plan, 2 * FAR, [far_block], out_weight, total, after=(through,))
     grad_query, *grad_parts = cotangent_products(
         plan,
-        FAR,
-        (added(far, last),),
+        2 * FAR + 1,
+        [far_other],
         out_weight,
         total,
         (convolved, query_gate),
-        (through,),
-        members,
+        members=members,
     )
     received = (swapped(given_near, "tp", 1), swapped(given_own, "tp", 1))
     third, own = product(NEAR, 2, 0, received, (grad_parts[0],))
     grad_parts = traded(grad_parts, "ctx")
-
-    two_a, two_b = held_until([two_a, two_b], tuple(grad_parts[1:]))
-    third, second = added(third, two_a), added(second, two_b)
-    back_parts = correlate(plan, input_parts, grad_parts, per_group, scale, (third, second))
-    projected = added(own, hop(third, OUTWARD + INWARD), hop(second, ACROSS))
+    (third,) = held_until([third], tuple(grad_parts[1:]))
+    beside_near = hop(third, INWARD + OUTWARD)
+    back_parts = correlate(plan, input_parts, grad_parts, per_group, scale, (third,))
+    projected = added(own, beside, over_two, to_middle, beside_near)
     back_parts = traded(back_parts, "ctx")
-    return projected, grad_query, *finished(plan, back_parts, key_gate, value_input, groups)
+    return projected, grad_query, *finished(plan, back_parts, key_gate, value_input, groups, (projected,))
 
 
 def anywhere(

time: 163 us -> 180 us (1.10)
  waiting for transfers between devices: 45.7 us -> 66.8 us
  Pallas kernels: 74.8 us -> 70.3 us
    ppermute x10, waiting for transfers between devices: 20 us -> 49 us  [hop(): lax.ppermute(array, 'tp', [(2 * i + core, 2 * j + core) for i, j in pairs...]
    ppermute x20, waiting for transfers between devices: 25.7 us -> 17.9 us  [swapped(): return lax.ppermute(array, axis, [(i, i ^ step) for i in range(size)])]
    pallas_call x1, Pallas kernels: 13 us -> 9.99 us  [correlate(): pl.pallas_call(functools.partial(backward_kernel, members, per_group, sca...]
    pallas_call x5, Pallas kernels: 24.5 us -> 21.7 us  [column_products(): pl.pallas_call(functools.partial(product_kernel, steps, joins, len(more))...]
    pallas_call x3 -> x4, Pallas kernels: 19.3 us -> 20.8 us  [cotangent_products(): pl.pallas_call(functools.partial(cotangent_kernel, count, begin, last, me...]
  transfers between devices with their start and end apart: 30 -> 30, of which waited for: 10 -> 9; matrix products, arithmetic and copies ran while one was open for 0% -> 0% of each run, Pallas kernels for 45% -> 35%
where the time goes in v7:
time: 180 us
  Pallas kernels  70.3 us (39%)
  waiting for transfers between devices  66.8 us (37%)
  starting transfers between devices  40.2 us (22%)
    ppermute x10, waiting for transfers between devices, hop(): lax.ppermute(array, 'tp', [(2 * i + core, 2 * j + core) for i, j in pairs...  49 us
    ppermute x10, starting transfers between devices, hop(): lax.ppermute(array, 'tp', [(2 * i + core, 2 * j + core) for i, j in pairs...  23.7 us
    pallas_call x5, Pallas kernels, column_products(): pl.pallas_call(functools.partial(product_kernel, steps, joins, len(more))...  21.7 us
    pallas_call x4, Pallas kernels, cotangent_products(): pl.pallas_call(functools.partial(cotangent_kernel, count, begin, last, me...  20.8 us
    ppermute x20, waiting for transfers between devices, swapped(): return lax.ppermute(array, axis, [(i, i ^ step) for i in range(size)])  17.9 us
    ppermute x20, starting transfers between devices, swapped(): return lax.ppermute(array, axis, [(i, i ^ step) for i in range(size)])  16.4 us
    pallas_call x1, Pallas kernels, correlate(): pl.pallas_call(functools.partial(backward_kernel, members, per_group, sca...  9.99 us
    pallas_call x1, Pallas kernels, convolve(): pl.pallas_call(functools.partial(forward_kernel, members, per_group, widt...  6.19 us
  transfers between devices with their start and end apart: 30, of which 9 were waited for; matrix products, arithmetic and copies ran while one was open for 0% of the time, Pallas kernels for 35%

profile of v7, /device:TPU:0, one launch (start us, length us, event | category | flops | bytes accessed | tf_op | source)
XLA Modules:
  0.0 179.8 jit_solution(575963921197736440)
XLA Ops:
  1.9 5.6 %collective-permute-start.4 = (bf16[512,1024]{1,0:T(8,128)(2,1)}, bf16[512,1024]{1,0:T(8,128)(2,1)S(1)}, u32[]{:S(2)}, u32[]{:S(2)}) collective-permute-start(bf16[512,1024]{1,0:T(8,128)(2,1)} %refs_0_.1), channel_id=1, source_target_pairs={{0,2},{1,3},{6,4},{7,5},{2,0},{3,1},{4,6},{5,7},{8,10},{9,11},{14,... | collective-permute-start | bytes 3145736 | tf_op jit(solution)/shard_map/ppermute | solution.py:361
  14.9 5.0 %cotangent_blocks.4.refs_4_ = f32[512,1024]{1,0:T(8,128)S(1)} custom-call(s32[9]{0:T(128)S(1)} %plan.1.plan_ref._, bf16[1024,8192]{1,0:T(8,128)(2,1)} %weight_ref.17, bf16[512,1024]{1,0:T(8,128)(2,1)S(1)} %copy-done.2, bf16[512,1024]{1,0:T(8,128)(2,1)} %collective-permute-done.3.refs_1_), custom_call_target="tpu_custom_call" | custom-call | flops 1048576 | bytes 4096 | tf_op jit(solution)/shard_map/cotangent_blocks/pallas_call | solution.py:559
  19.9 5.8 %collective-permute-done.1.refs_2_ = bf16[544,256]{1,0:T(8,128)(2,1)S(1)} collective-permute-done((bf16[544,256]{1,0:T(8,128)(2,1)S(1)}, bf16[544,256]{1,0:T(8,128)(2,1)S(1)}, u32[]{:S(2)}, u32[]{:S(2)}) %collective-permute-start.1) | collective-permute-done | bytes 278560 | tf_op jit(solution)/shard_map/ppermute | solution.py:328
  25.7 6.2 %causal_conv.1 = (bf16[512,256]{1,0:T(8,128)(2,1)S(1)}, bf16[512,256]{1,0:T(8,128)(2,1)S(1)}, bf16[512,256]{1,0:T(8,128)(2,1)S(1)}, bf16[512,256]{1,0:T(8,128)(2,1)S(1)}) custom-call(s32[9]{0:T(128)S(1)} %plan.1.plan_ref._, bf16[544,256]{1,0:T(8,128)(2,1)S(1)} %get-tuple-element.45.refs_0_, bf16[544,256]{1,0:T(8,128)(2,1)S(1)} %collective-permute-done.refs_1_, ...), custom_call_target="tpu_custom_call" | custom-call | flops 1048576 | bytes 4096 | tf_op jit(solution)/shard_map/causal_conv/pallas_call | solution.py:182
  37.6 3.7 %collective-permute-done.6.refs_1_ = bf16[512,256]{1,0:T(8,128)(2,1)S(1)} collective-permute-done((bf16[512,256]{1,0:T(8,128)(2,1)S(1)}, bf16[512,256]{1,0:T(8,128)(2,1)S(1)}, u32[]{:S(2)}, u32[]{:S(2)}) %collective-permute-start.6) | collective-permute-done | bytes 262176 | tf_op jit(solution)/shard_map/ppermute | solution.py:328
  41.3 4.5 %collective-permute-done.7.refs_2_ = bf16[512,256]{1,0:T(8,128)(2,1)S(1)} collective-permute-done((bf16[512,256]{1,0:T(8,128)(2,1)S(1)}, bf16[512,256]{1,0:T(8,128)(2,1)S(1)}, u32[]{:S(2)}, u32[]{:S(2)}) %collective-permute-start.7) | collective-permute-done | bytes 262176 | tf_op jit(solution)/shard_map/ppermute | solution.py:328
  46.6 4.9 %projection_blocks.5 = (bf16[512,1024]{1,0:T(8,128)(2,1)S(1)}, bf16[512,1024]{1,0:T(8,128)(2,1)S(1)}) custom-call(s32[9]{0:T(128)S(1)} %plan.1.plan_ref._, bf16[512,1024]{1,0:T(8,128)(2,1)S(1)} %get-tuple-element.57.data_ref, bf16[1024,8192]{1,0:T(8,128)(2,1)} %weight_ref.17), custom_call_target="tpu_custom_call" | custom-call | flops 1048576 | bytes 4096 | tf_op jit(solution)/shard_map/projection_blocks/pallas_call | solution.py:492
  52.1 9.3 %collective-permute-done.14.refs_1_ = bf16[512,1024]{1,0:T(8,128)(2,1)S(1)} collective-permute-done((bf16[512,1024]{1,0:T(8,128)(2,1)S(1)}, bf16[512,1024]{1,0:T(8,128)(2,1)S(1)}, u32[]{:S(2)}, u32[]{:S(2)}) %collective-permute-start.14) | collective-permute-done | bytes 1048608 | tf_op jit(solution)/shard_map/ppermute | solution.py:361
  61.4 3.4 %projection_blocks.6.refs_1_.refs_0_ = bf16[512,1024]{1,0:T(8,128)(2,1)S(1)} custom-call(s32[9]{0:T(128)S(1)} %plan.1.plan_ref._, bf16[512,1024]{1,0:T(8,128)(2,1)S(1)} %get-tuple-element.57.data_ref, bf16[1024,8192]{1,0:T(8,128)(2,1)} %weight_ref.17, bf16[512,1024]{1,0:T(8,128)(2,1)S(1)} %collective-permute-done.10.refs_0_), custom_call_target="tpu_custom_call" | custom-call | flops 1048576 | bytes 4096 | tf_op jit(solution)/shard_map/projection_blocks/pallas_call | solution.py:492
  64.8 3.4 %projection_blocks.7.refs_0_.refs_2_ = bf16[512,1024]{1,0:T(8,128)(2,1)S(1)} custom-call(s32[9]{0:T(128)S(1)} %plan.1.plan_ref._, bf16[512,1024]{1,0:T(8,128)(2,1)S(1)} %get-tuple-element.57.data_ref, bf16[1024,8192]{1,0:T(8,128)(2,1)} %weight_ref.17, bf16[512,1024]{1,0:T(8,128)(2,1)S(1)} %collective-permute-done.9.refs_0_, ...), custom_call_target="tpu_custom_call" | custom-call | flops 1048576 | bytes 4096 | tf_op jit(solution)/shard_map/projection_blocks/pallas_call | solution.py:492
  71.2 7.5 %collective-permute-start.20 = (bf16[512,1024]{1,0:T(8,128)(2,1)S(1)}, bf16[512,1024]{1,0:T(8,128)(2,1)S(1)}, u32[]{:S(2)}, u32[]{:S(2)}) collective-permute-start(bf16[512,1024]{1,0:T(8,128)(2,1)S(1)} %projection_blocks.6.refs_1_.refs_0_), channel_id=1, source_target_pairs={{0,2},{1,3},{6,4},{7,5},{8,10},{9,11},{14,12},{15,13},{16,18},{17,... | collective-permute-start | bytes 3145736 | tf_op jit(solution)/shard_map/ppermute | solution.py:361
  78.7 4.9 %projection_blocks.8 = (bf16[512,1024]{1,0:T(8,128)(2,1)S(1)}, bf16[512,1024]{1,0:T(8,128)(2,1)S(1)}) custom-call(s32[9]{0:T(128)S(1)} %plan.1.plan_ref._, bf16[512,1024]{1,0:T(8,128)(2,1)S(1)} %get-tuple-element.57.data_ref, bf16[1024,8192]{1,0:T(8,128)(2,1)} %weight_ref.17, bf16[512,1024]{1,0:T(8,128)(2,1)S(1)} %projection_blocks.7.refs_0_.refs_2_), custom_call_target="tpu_custom_call" | custom-call | flops 1048576 | bytes 4096 | tf_op jit(solution)/shard_map/projection_blocks/pallas_call | solution.py:492
  83.7 7.8 %cotangent_blocks.5.refs_2_.refs_1_ = f32[512,1024]{1,0:T(8,128)S(1)} custom-call(s32[9]{0:T(128)S(1)} %plan.1.plan_ref._, bf16[1024,8192]{1,0:T(8,128)(2,1)} %weight_ref.17, bf16[512,1024]{1,0:T(8,128)(2,1)S(1)} %get-tuple-element.65.refs_0_, bf16[512,1024]{1,0:T(8,128)(2,1)S(1)} %collective-permute-done.17.refs_1_, bf16[512,1024]{1,0:T(8,128)(2,1)S(1)} %added.4.refs_2_, ...), custom_call_target="tpu_custom_call" | custom-call | flops 1048576 | bytes 4096 | tf_op jit(solution)/shard_map/cotangent_blocks/pallas_call | solution.py:559
  91.4 4.7 %collective-permute-done.15.refs_0_ = bf16[512,1024]{1,0:T(8,128)(2,1)S(1)} collective-permute-done((bf16[512,1024]{1,0:T(8,128)(2,1)S(1)}, bf16[512,1024]{1,0:T(8,128)(2,1)S(1)}, u32[]{:S(2)}, u32[]{:S(2)}) %collective-permute-start.15) | collective-permute-done | bytes 1048608 | tf_op jit(solution)/shard_map/ppermute | solution.py:361
  97.1 3.4 %collective-permute-done.20.refs_0_ = bf16[512,1024]{1,0:T(8,128)(2,1)S(1)} collective-permute-done((bf16[512,1024]{1,0:T(8,128)(2,1)S(1)}, bf16[512,1024]{1,0:T(8,128)(2,1)S(1)}, u32[]{:S(2)}, u32[]{:S(2)}) %collective-permute-start.20) | collective-permute-done | bytes 1048608 | tf_op jit(solution)/shard_map/ppermute | solution.py:361
  100.6 4.4 %collective-permute-start.22 = (bf16[512,1024]{1,0:T(8,128)(2,1)S(1)}, bf16[512,1024]{1,0:T(8,128)(2,1)S(1)}, u32[]{:S(2)}, u32[]{:S(2)}) collective-permute-start(bf16[512,1024]{1,0:T(8,128)(2,1)S(1)} %held.12), channel_id=1, source_target_pairs={{0,4},{1,5},{6,2},{7,3},{8,12},{9,13},{14,10},{15,11},{16,20},{17,... | collective-permute-start | bytes 3145736 | tf_op jit(solution)/shard_map/ppermute | solution.py:361
  105.3 3.4 %cotangent_blocks.6.refs_1_ = f32[512,1024]{1,0:T(8,128)S(1)} custom-call(s32[9]{0:T(128)S(1)} %plan.1.plan_ref._, bf16[1024,8192]{1,0:T(8,128)(2,1)} %weight_ref.17, bf16[512,1024]{1,0:T(8,128)(2,1)S(1)} %added.5.refs_0_, f32[512,1024]{1,0:T(8,128)S(1)} %cotangent_blocks.5.refs_2_.refs_1_, bf16[512,1024]{1,0:T(8,128)(2,1)S(1)} %added.6.refs_2_), custom_call_target="tpu_custom_call" | custom-call | flops 1048576 | bytes 4096 | tf_op jit(solution)/shard_map/cotangent_blocks/pallas_call | solution.py:559
  108.7 4.6 %cotangent_blocks.7 = (bf16[512,1024]{1,0:T(8,128)(2,1)}, bf16[512,256]{1,0:T(8,128)(2,1)S(1)}, bf16[512,256]{1,0:T(8,128)(2,1)S(1)}, bf16[512,256]{1,0:T(8,128)(2,1)S(1)}, bf16[512,256]{1,0:T(8,128)(2,1)S(1)}) custom-call(s32[9]{0:T(128)S(1)} %plan.1.plan_ref._, bf16[1024,8192]{1,0:T(8,128)(2,1)} %weight_ref.17, ...), custom_call_target="tpu_custom_call" | custom-call | flops 1048576 | bytes 4096 | tf_op jit(solution)/shard_map/cotangent_blocks/pallas_call | solution.py:559
  118.3 5.1 %projection_blocks.9 = (bf16[512,1024]{1,0:T(8,128)(2,1)S(1)}, bf16[512,1024]{1,0:T(8,128)(2,1)S(1)}) custom-call(s32[9]{0:T(128)S(1)} %plan.1.plan_ref._, bf16[512,1024]{1,0:T(8,128)(2,1)S(1)} %get-tuple-element.57.data_ref, bf16[1024,8192]{1,0:T(8,128)(2,1)} %weight_ref.17, bf16[512,1024]{1,0:T(8,128)(2,1)S(1)} %collective-permute-done.11.refs_0_, ...), custom_call_target="tpu_custom_call" | custom-call | flops 1048576 | bytes 4096 | tf_op jit(solution)/shard_map/projection_blocks/pallas_call | solution.py:492
  123.5 3.8 %collective-permute-done.24.refs_2_.refs_6_ = bf16[512,256]{1,0:T(8,128)(2,1)S(1)} collective-permute-done((bf16[512,256]{1,0:T(8,128)(2,1)S(1)}, bf16[512,256]{1,0:T(8,128)(2,1)S(1)}, u32[]{:S(2)}, u32[]{:S(2)}) %collective-permute-start.24) | collective-permute-done | bytes 262176 | tf_op jit(solution)/shard_map/ppermute | solution.py:328
  127.3 10.0 %causal_conv_grads.1 = (bf16[544,256]{1,0:T(8,128)(2,1)S(1)}, bf16[544,256]{1,0:T(8,128)(2,1)S(1)}, bf16[544,256]{1,0:T(8,128)(2,1)S(1)}, bf16[544,256]{1,0:T(8,128)(2,1)S(1)}) custom-call(s32[9]{0:T(128)S(1)} %plan.1.plan_ref._, bf16[544,256]{1,0:T(8,128)(2,1)S(1)} %get-tuple-element.45.refs_0_, bf16[544,256]{1,0:T(8,128)(2,1)S(1)} %collective-permute-done.refs_1_, ...), custom_call_target="tpu_custom_call" | custom-call | flops 1048576 | bytes 4096 | tf_op jit(solution)/shard_map/causal_conv_grads/pallas_call | solution.py:203
  140.9 10.6 %collective-permute-done.21.refs_2_ = bf16[512,1024]{1,0:T(8,128)(2,1)S(1)} collective-permute-done((bf16[512,1024]{1,0:T(8,128)(2,1)S(1)}, bf16[512,1024]{1,0:T(8,128)(2,1)S(1)}, u32[]{:S(2)}, u32[]{:S(2)}) %collective-permute-start.21) | collective-permute-done | bytes 1048608 | tf_op jit(solution)/shard_map/ppermute | solution.py:361
  151.5 20.9 %collective-permute-done.26.refs_4_ = bf16[512,1024]{1,0:T(8,128)(2,1)S(1)} collective-permute-done((bf16[512,1024]{1,0:T(8,128)(2,1)S(1)}, bf16[512,1024]{1,0:T(8,128)(2,1)S(1)}, u32[]{:S(2)}, u32[]{:S(2)}) %collective-permute-start.26) | collective-permute-done | bytes 1048608 | tf_op jit(solution)/shard_map/ppermute | solution.py:361
  175.5 4.1 %input_gradients.1 = (bf16[512,1024]{1,0:T(8,128)(2,1)}, bf16[512,1024]{1,0:T(8,128)(2,1)}, f32[64,512]{1,0:T(8,128)}) custom-call(s32[9]{0:T(128)S(1)} %plan.1.plan_ref._, bf16[544,256]{1,0:T(8,128)(2,1)S(1)} %get-tuple-element.78.refs_0_, bf16[544,256]{1,0:T(8,128)(2,1)S(1)} %collective-permute-done.27.refs_1_, ...), custom_call_target="tpu_custom_call" | custom-call | flops 1048576 | bytes 4096 | tf_op jit(solution)/shard_map/input_gradients/pallas_call | solution.py:313
  (69 shorter events, 31.5 us)
Async XLA Ops:
  0.6 12.6 %collective-permute-start.3 = (bf16[512,1024]{1,0:T(8,128)(2,1)}, bf16[512,1024]{1,0:T(8,128)(2,1)}, u32[]{:S(2)}, u32[]{:S(2)}) collective-permute-start(bf16[512,1024]{1,0:T(8,128)(2,1)} %refs_0_.1), channel_id=1, source_target_pairs={{0,1},{1,0},{2,3},{3,2},{4,5},{5,4},{6,7},{7,6},{8,9},{9,8},{10,11... | collective-permute-start | bytes 3145736 | tf_op jit(solution)/shard_map/ppermute | solution.py:328
  1.2 30.8 %collective-permute-start.5 = (bf16[512,1024]{1,0:T(8,128)(2,1)}, bf16[512,1024]{1,0:T(8,128)(2,1)S(1)}, u32[]{:S(2)}, u32[]{:S(2)}) collective-permute-start(bf16[512,1024]{1,0:T(8,128)(2,1)} %refs_0_.1), channel_id=1, source_target_pairs={{2,4},{3,5},{4,2},{5,3},{10,12},{11,13},{12,10},{13,11},{18,20},{1... | collective-permute-start | bytes 3145736 | tf_op jit(solution)/shard_map/ppermute | solution.py:361
  1.9 30.1 %collective-permute-start.4 = (bf16[512,1024]{1,0:T(8,128)(2,1)}, bf16[512,1024]{1,0:T(8,128)(2,1)S(1)}, u32[]{:S(2)}, u32[]{:S(2)}) collective-permute-start(bf16[512,1024]{1,0:T(8,128)(2,1)} %refs_0_.1), channel_id=1, source_target_pairs={{0,2},{1,3},{6,4},{7,5},{2,0},{3,1},{4,6},{5,7},{8,10},{9,11},{14,... | collective-permute-start | bytes 3145736 | tf_op jit(solution)/shard_map/ppermute | solution.py:361
  11.7 14.0 %collective-permute-start.1 = (bf16[544,256]{1,0:T(8,128)(2,1)S(1)}, bf16[544,256]{1,0:T(8,128)(2,1)S(1)}, u32[]{:S(2)}, u32[]{:S(2)}) collective-permute-start(bf16[544,256]{1,0:T(8,128)(2,1)S(1)} %get-tuple-element.47), channel_id=1, source_target_pairs={{0,16},{8,24},{16,0},{24,8},{1,17},{9,25},{17,1},{25,9},{2,18},{10... | collective-permute-start | bytes 835592 | tf_op jit(solution)/shard_map/ppermute | solution.py:328
  13.2 12.5 %collective-permute-start.2 = (bf16[544,256]{1,0:T(8,128)(2,1)S(1)}, bf16[544,256]{1,0:T(8,128)(2,1)S(1)}, u32[]{:S(2)}, u32[]{:S(2)}) collective-permute-start(bf16[544,256]{1,0:T(8,128)(2,1)S(1)} %get-tuple-element.48), channel_id=1, source_target_pairs={{0,24},{8,16},{16,8},{24,0},{1,25},{9,17},{17,9},{25,1},{2,26},{10... | collective-permute-start | bytes 835592 | tf_op jit(solution)/shard_map/ppermute | solution.py:328
  33.3 12.5 %collective-permute-start.7 = (bf16[512,256]{1,0:T(8,128)(2,1)S(1)}, bf16[512,256]{1,0:T(8,128)(2,1)S(1)}, u32[]{:S(2)}, u32[]{:S(2)}) collective-permute-start(bf16[512,256]{1,0:T(8,128)(2,1)S(1)} %get-tuple-element.55), channel_id=1, source_target_pairs={{0,16},{8,24},{16,0},{24,8},{1,17},{9,25},{17,1},{25,9},{2,18},{10... | collective-permute-start | bytes 786440 | tf_op jit(solution)/shard_map/ppermute | solution.py:328
  35.5 16.5 %collective-permute-start.13 = (bf16[512,1024]{1,0:T(8,128)(2,1)S(1)}, bf16[512,1024]{1,0:T(8,128)(2,1)S(1)}, u32[]{:S(2)}, u32[]{:S(2)}) collective-permute-start(bf16[512,1024]{1,0:T(8,128)(2,1)S(1)} %get-tuple-element.62.refs_0_), channel_id=1, source_target_pairs={{2,4},{3,5},{4,2},{5,3},{10,12},{11,13},{12,10},{13,11},{18,20},{1... | collective-permute-start | bytes 3145736 | tf_op jit(solution)/shard_map/ppermute | solution.py:361
  36.3 25.1 %collective-permute-start.14 = (bf16[512,1024]{1,0:T(8,128)(2,1)S(1)}, bf16[512,1024]{1,0:T(8,128)(2,1)S(1)}, u32[]{:S(2)}, u32[]{:S(2)}) collective-permute-start(bf16[512,1024]{1,0:T(8,128)(2,1)S(1)} %get-tuple-element.63.refs_1_), channel_id=1, source_target_pairs={{2,0},{3,1},{4,6},{5,7},{10,8},{11,9},{12,14},{13,15},{18,16},{19,... | collective-permute-start | bytes 3145736 | tf_op jit(solution)/shard_map/ppermute | solution.py:361
  51.6 13.2 %collective-permute-start.9 = (bf16[512,1024]{1,0:T(8,128)(2,1)S(1)}, bf16[512,1024]{1,0:T(8,128)(2,1)S(1)}, u32[]{:S(2)}, u32[]{:S(2)}) collective-permute-start(bf16[512,1024]{1,0:T(8,128)(2,1)S(1)} %get-tuple-element.58), channel_id=1, source_target_pairs={{0,1},{1,0},{2,3},{3,2},{4,5},{5,4},{6,7},{7,6},{8,9},{9,8},{10,11... | collective-permute-start | bytes 3145736 | tf_op jit(solution)/shard_map/ppermute | solution.py:328
  68.6 15.1 %collective-permute-start.18 = (bf16[512,1024]{1,0:T(8,128)(2,1)S(1)}, bf16[512,1024]{1,0:T(8,128)(2,1)S(1)}, u32[]{:S(2)}, u32[]{:S(2)}) collective-permute-start(bf16[512,1024]{1,0:T(8,128)(2,1)S(1)} %added.4.refs_2_), channel_id=1, source_target_pairs={{0,1},{1,0},{2,3},{3,2},{4,5},{5,4},{6,7},{7,6},{8,9},{9,8},{10,11... | collective-permute-start | bytes 3145736 | tf_op jit(solution)/shard_map/ppermute | solution.py:328
  68.7 15.0 %collective-permute-start.17 = (bf16[512,1024]{1,0:T(8,128)(2,1)S(1)}, bf16[512,1024]{1,0:T(8,128)(2,1)S(1)}, u32[]{:S(2)}, u32[]{:S(2)}) collective-permute-start(bf16[512,1024]{1,0:T(8,128)(2,1)S(1)} %get-tuple-element.65.refs_0_), channel_id=1, source_target_pairs={{0,1},{1,0},{2,3},{3,2},{4,5},{5,4},{6,7},{7,6},{8,9},{9,8},{10,11... | collective-permute-start | bytes 3145736 | tf_op jit(solution)/shard_map/ppermute | solution.py:328
  69.1 27.0 %collective-permute-start.15 = (bf16[512,1024]{1,0:T(8,128)(2,1)S(1)}, bf16[512,1024]{1,0:T(8,128)(2,1)S(1)}, u32[]{:S(2)}, u32[]{:S(2)}) collective-permute-start(bf16[512,1024]{1,0:T(8,128)(2,1)S(1)} %get-tuple-element.64.refs_0_), channel_id=1, source_target_pairs={{2,0},{3,1},{4,6},{5,7},{10,8},{11,9},{12,14},{13,15},{18,16},{19,... | collective-permute-start | bytes 3145736 | tf_op jit(solution)/shard_map/ppermute | solution.py:361
  70.4 25.7 %collective-permute-start.16 = (bf16[512,1024]{1,0:T(8,128)(2,1)S(1)}, bf16[512,1024]{1,0:T(8,128)(2,1)S(1)}, u32[]{:S(2)}, u32[]{:S(2)}) collective-permute-start(bf16[512,1024]{1,0:T(8,128)(2,1)S(1)} %projection_blocks.7.refs_0_.refs_2_), channel_id=1, source_target_pairs={{2,4},{3,5},{4,2},{5,3},{10,12},{11,13},{12,10},{13,11},{18,20},{1... | collective-permute-start | bytes 3145736 | tf_op jit(solution)/shard_map/ppermute | solution.py:361
  71.2 29.4 %collective-permute-start.20 = (bf16[512,1024]{1,0:T(8,128)(2,1)S(1)}, bf16[512,1024]{1,0:T(8,128)(2,1)S(1)}, u32[]{:S(2)}, u32[]{:S(2)}) collective-permute-start(bf16[512,1024]{1,0:T(8,128)(2,1)S(1)} %projection_blocks.6.refs_1_.refs_0_), channel_id=1, source_target_pairs={{0,2},{1,3},{6,4},{7,5},{8,10},{9,11},{14,12},{15,13},{16,18},{17,... | collective-permute-start | bytes 3145736 | tf_op jit(solution)/shard_map/ppermute | solution.py:361
  96.5 12.3 %collective-permute-start.19 = (bf16[512,1024]{1,0:T(8,128)(2,1)S(1)}, bf16[512,1024]{1,0:T(8,128)(2,1)S(1)}, u32[]{:S(2)}, u32[]{:S(2)}) collective-permute-start(bf16[512,1024]{1,0:T(8,128)(2,1)S(1)} %added.5.refs_0_), channel_id=1, source_target_pairs={{0,1},{1,0},{2,3},{3,2},{4,5},{5,4},{6,7},{7,6},{8,9},{9,8},{10,11... | collective-permute-start | bytes 3145736 | tf_op jit(solution)/shard_map/ppermute | solution.py:328
  96.6 19.8 %collective-permute-start.12 = (bf16[512,1024]{1,0:T(8,128)(2,1)S(1)}, bf16[512,1024]{1,0:T(8,128)(2,1)S(1)}, u32[]{:S(2)}, u32[]{:S(2)}) collective-permute-start(bf16[512,1024]{1,0:T(8,128)(2,1)S(1)} %get-tuple-element.61), channel_id=1, source_target_pairs={{0,1},{1,0},{2,3},{3,2},{4,5},{5,4},{6,7},{7,6},{8,9},{9,8},{10,11... | collective-permute-start | bytes 3145736 | tf_op jit(solution)/shard_map/ppermute | solution.py:328
  97.1 19.8 %collective-permute-start.11 = (bf16[512,1024]{1,0:T(8,128)(2,1)S(1)}, bf16[512,1024]{1,0:T(8,128)(2,1)S(1)}, u32[]{:S(2)}, u32[]{:S(2)}) collective-permute-start(bf16[512,1024]{1,0:T(8,128)(2,1)S(1)} %get-tuple-element.60.refs_3_.refs_2_), channel_id=1, source_target_pairs={{0,1},{1,0},{2,3},{3,2},{4,5},{5,4},{6,7},{7,6},{8,9},{9,8},{10,11... | collective-permute-start | bytes 3145736 | tf_op jit(solution)/shard_map/ppermute | solution.py:328
  100.6 39.8 %collective-permute-start.22 = (bf16[512,1024]{1,0:T(8,128)(2,1)S(1)}, bf16[512,1024]{1,0:T(8,128)(2,1)S(1)}, u32[]{:S(2)}, u32[]{:S(2)}) collective-permute-start(bf16[512,1024]{1,0:T(8,128)(2,1)S(1)} %held.12), channel_id=1, source_target_pairs={{0,4},{1,5},{6,2},{7,3},{8,12},{9,13},{14,10},{15,11},{16,20},{17,... | collective-permute-start | bytes 3145736 | tf_op jit(solution)/shard_map/ppermute | solution.py:361
  114.8 12.5 %collective-permute-start.24 = (bf16[512,256]{1,0:T(8,128)(2,1)S(1)}, bf16[512,256]{1,0:T(8,128)(2,1)S(1)}, u32[]{:S(2)}, u32[]{:S(2)}) collective-permute-start(bf16[512,256]{1,0:T(8,128)(2,1)S(1)} %get-tuple-element.75), channel_id=1, source_target_pairs={{0,16},{8,24},{16,0},{24,8},{1,17},{9,25},{17,1},{25,9},{2,18},{10... | collective-permute-start | bytes 786440 | tf_op jit(solution)/shard_map/ppermute | solution.py:328
  116.8 34.7 %collective-permute-start.21 = (bf16[512,1024]{1,0:T(8,128)(2,1)S(1)}, bf16[512,1024]{1,0:T(8,128)(2,1)S(1)}, u32[]{:S(2)}, u32[]{:S(2)}) collective-permute-start(bf16[512,1024]{1,0:T(8,128)(2,1)S(1)} %added.6.refs_2_), channel_id=1, source_target_pairs={{2,6},{3,7},{4,0},{5,1},{10,14},{11,15},{12,8},{13,9},{18,22},{19,... | collective-permute-start | bytes 3145736 | tf_op jit(solution)/shard_map/ppermute | solution.py:361
  127.3 45.0 %collective-permute-start.26 = (bf16[512,1024]{1,0:T(8,128)(2,1)S(1)}, bf16[512,1024]{1,0:T(8,128)(2,1)S(1)}, u32[]{:S(2)}, u32[]{:S(2)}) collective-permute-start(bf16[512,1024]{1,0:T(8,128)(2,1)S(1)} %held.13.refs_8_), channel_id=1, source_target_pairs={{0,2},{1,3},{6,4},{7,5},{2,0},{3,1},{4,6},{5,7},{8,10},{9,11},{14,... | collective-permute-start | bytes 3145736 | tf_op jit(solution)/shard_map/ppermute | solution.py:361
  137.3 36.9 %collective-permute-start.27 = (bf16[544,256]{1,0:T(8,128)(2,1)S(1)}, bf16[544,256]{1,0:T(8,128)(2,1)S(1)}, u32[]{:S(2)}, u32[]{:S(2)}) collective-permute-start(bf16[544,256]{1,0:T(8,128)(2,1)S(1)} %get-tuple-element.79), channel_id=1, source_target_pairs={{0,8},{8,0},{16,24},{24,16},{1,9},{9,1},{17,25},{25,17},{2,10},{10... | collective-permute-start | bytes 835592 | tf_op jit(solution)/shard_map/ppermute | solution.py:328
  138.8 35.5 %collective-permute-start.28 = (bf16[544,256]{1,0:T(8,128)(2,1)S(1)}, bf16[544,256]{1,0:T(8,128)(2,1)S(1)}, u32[]{:S(2)}, u32[]{:S(2)}) collective-permute-start(bf16[544,256]{1,0:T(8,128)(2,1)S(1)} %get-tuple-element.80), channel_id=1, source_target_pairs={{0,16},{8,24},{16,0},{24,8},{1,17},{9,25},{17,1},{25,9},{2,18},{10... | collective-permute-start | bytes 835592 | tf_op jit(solution)/shard_map/ppermute | solution.py:328
  140.3 33.9 %collective-permute-start.29 = (bf16[544,256]{1,0:T(8,128)(2,1)S(1)}, bf16[544,256]{1,0:T(8,128)(2,1)S(1)}, u32[]{:S(2)}, u32[]{:S(2)}) collective-permute-start(bf16[544,256]{1,0:T(8,128)(2,1)S(1)} %get-tuple-element.81), channel_id=1, source_target_pairs={{0,24},{8,16},{16,8},{24,0},{1,25},{9,17},{17,9},{25,1},{2,26},{10... | collective-permute-start | bytes 835592 | tf_op jit(solution)/shard_map/ppermute | solution.py:328
  (9 other events, 91.0 us)

commit v8 on v7

--- a/solution.py
+++ b/solution.py
@@ -92,7 +92,7 @@
         spread_out(out_scr, start, per_group, value, members, width)
         return carry
 
-    lax.fori_loop(0, groups, one_group, 0, unroll=2)
+    lax.fori_loop(0, groups, one_group, 0, unroll=4)
     for step in range(members):
         outputs[step][...] = out_scr[position ^ step].T
 
@@ -155,7 +155,7 @@
         grad_scr[pl.ds(group, 1), :] = jnp.sum(product, axis=0, keepdims=True) * scale
         return carry
 
-    lax.fori_loop(0, groups, one_group, 0, unroll=2)
+    lax.fori_loop(0, groups, one_group, 0, unroll=4)
     for step in range(members):
         at = position ^ step
         outputs[step][:width] = out_scr[at].T
@@ -275,51 +275,41 @@
     key_ref, value_ref = refs[members : members + 2]
     key_out, value_out, taps_out = refs[-3:]
     position = plan_ref[POSITION]
-    step_no = pl.program_id(0)
-    rows, channels = key_ref.shape
+    width, channels = key_ref.shape
     share = channels // members
-    groups, width = taps_out.shape
-    groups = groups // members
-    here = pl.ds(pl.multiple_of(step_no * rows, rows), rows)
+    groups = taps_out.shape[0] // members
     for step in range(members):
         at = position ^ step
         columns = pl.ds(pl.multiple_of(at * share, share), share)
-        grad = parts[step][here, :].astype(jnp.float32)
+        grad = parts[step][:width].astype(jnp.float32)
         key_out[:, columns] = (grad * value_ref[:, columns].astype(jnp.float32)).astype(
             jnp.bfloat16
         )
         value_out[:, columns] = (grad * key_ref[:, columns].astype(jnp.float32)).astype(
             jnp.bfloat16
         )
-
-    @pl.when(step_no == 0)
-    def _():
-        for step in range(members):
-            at = position ^ step
-            taps = [
-                parts[step][width + chunk * groups : width + (chunk + 1) * groups, :]
-                for chunk in range(width // share)
-            ]
-            taps_out[pl.ds(pl.multiple_of(at * groups, groups), groups), :] = jnp.concatenate(
-                taps, axis=1
-            ).astype(jnp.float32)
+        taps = [
+            parts[step][width + chunk * groups : width + (chunk + 1) * groups, :]
+            for chunk in range(width // share)
+        ]
+        taps_out[pl.ds(pl.multiple_of(at * groups, groups), groups), :] = jnp.concatenate(
+            taps, axis=1
+        ).astype(jnp.float32)
 
 
 def finished(plan, parts, key_gate, value_input, groups, after=()):
     members = len(parts)
     width, channels = key_gate.shape
     array = jax.ShapeDtypeStruct((width, channels), jnp.bfloat16)
-    part = pl.BlockSpec((width // 4, channels), lambda i: (i, 0))
     grad_key, grad_value, taps = pl.pallas_call(
         functools.partial(finish_kernel, members),
         out_shape=[array, array, jax.ShapeDtypeStruct((groups, width), jnp.float32)],
-        grid=(4,),
-        in_specs=[SMEM] + [VMEM] * members + [part] * 2 + [ANYWHERE] * len(after),
-        out_specs=[part, part, pl.BlockSpec((groups, width), lambda i: (0, 0))],
+        in_specs=[SMEM] + [VMEM] * (members + 2) + [ANYWHERE] * len(after),
+        out_specs=[VMEM] * 3,
         compiler_params=pltpu.CompilerParams(vmem_limit_bytes=24 * 2**20),
         cost_estimate=COST,
         name="input_gradients",
-    )(plan, *parts, in_hbm(key_gate), in_hbm(value_input), *after)
+    )(plan, *parts, key_gate, value_input, *after)
     return grad_key, grad_value, taps.T
 
 
@@ -636,27 +626,31 @@
             plan, gated_out, out_weight, first, count, other, more, after, tiles, joins
         )
 
-    given_far, given_middle = product(FAR, 2, 1)
-    far, skip = held_until([far, skip], (given_far,))
+    given_far = product(FAR, 1, 1, tiles=2)
+    received = [swapped(part, "tp", 1) for part in given_far]
+    (first,) = product(FAR, 1, 0, received, tiles=2, joins=2)
+    one = hop(first, INWARD)
+    far, skip = held_until([far, skip], (first,))
     last = hop(far, OUTWARD)
-    (first,) = product(FAR, 1, 0, (swapped(given_far, "tp", 1),))
-    one = hop(first, INWARD)
-    (second,) = product(MIDDLE, 1, 0, (swapped(given_middle, "tp", 1),), (first,))
-    beside = hop(second, ACROSS)
-    near, cross = held_until([near, cross], (second,))
-    total = cotangent_products(
-        plan, 2 * NEAR, both([near, added(cross, skip)]), out_weight, total
-    )
+    given_middle = product(MIDDLE, 1, 1, (), (far,), tiles=2)
+    received = [swapped(part, "tp", 1) for part in given_middle]
+    (second,) = product(MIDDLE, 1, 0, received, tiles=2, joins=2)
+    middle_block = added(cross, skip)
+    blocks = [near, swapped(near, "tp", 1), middle_block]
+    total = cotangent_products(plan, 2 * NEAR, blocks, out_weight, total, after=(second,))
     given_near, given_own = product(NEAR, 2, 1, (), (second,))
     (one,) = held_until([one], (total, given_near))
     through = added(first, one)
-    over_two = hop(through, ((1, 3), (2, 0)))
+    two_a = hop(through, ACROSS)
     (second,) = held_until([second], (one,))
-    to_middle = hop(second, ((0, 2), (3, 1)))
-
-    last, beside = held_until([last, beside], (total, given_near))
+    two_b = hop(second, INWARD)
+
+    (last,) = held_until([last], (total, given_near))
     far_block, far_other = both([added(far, last)])
-    total = cotangent_products(plan, 2 * FAR, [far_block], out_weight, total, after=(through,))
+    blocks = [swapped(middle_block, "tp", 1), far_block]
+    total = cotangent_products(
+        plan, 2 * MIDDLE + 1, blocks, out_weight, total, after=(through,)
+    )
     grad_query, *grad_parts = cotangent_products(
         plan,
         2 * FAR + 1,
@@ -669,10 +663,11 @@
     received = (swapped(given_near, "tp", 1), swapped(given_own, "tp", 1))
     third, own = product(NEAR, 2, 0, received, (grad_parts[0],))
     grad_parts = traded(grad_parts, "ctx")
-    (third,) = held_until([third], tuple(grad_parts[1:]))
-    beside_near = hop(third, INWARD + OUTWARD)
-    back_parts = correlate(plan, input_parts, grad_parts, per_group, scale, (third,))
-    projected = added(own, beside, over_two, to_middle, beside_near)
+
+    two_a, two_b = held_until([two_a, two_b], tuple(grad_parts[1:]))
+    third, second = added(third, two_a), added(second, two_b)
+    back_parts = correlate(plan, input_parts, grad_parts, per_group, scale, (third, second))
+    projected = added(own, hop(third, OUTWARD + INWARD), hop(second, ACROSS))
     back_parts = traded(back_parts, "ctx")
     return projected, grad_query, *finished(plan, back_parts, key_gate, value_input, groups, (projected,))
 

time: 180 us -> 155 us (0.86)
  waiting for transfers between devices: 66.8 us -> 37.3 us
  starting transfers between devices: 40.2 us -> 44.4 us
    ppermute x10, waiting for transfers between devices: 49 us -> 14.2 us  [hop(): lax.ppermute(array, 'tp', [(2 * i + core, 2 * j + core) for i, j in pairs...]
    ppermute x20 -> x22, waiting for transfers between devices: 17.9 us -> 23.1 us  [swapped(): return lax.ppermute(array, axis, [(i, i ^ step) for i in range(size)])]
    ppermute x10, starting transfers between devices: 23.7 us -> 27.4 us  [hop(): lax.ppermute(array, 'tp', [(2 * i + core, 2 * j + core) for i, j in pairs...]
    pallas_call x5 -> x6, Pallas kernels: 21.7 us -> 23.7 us  [column_products(): pl.pallas_call(functools.partial(product_kernel, steps, joins, len(more))...]
    ppermute x20 -> x22, starting transfers between devices: 16.4 us -> 17 us  [swapped(): return lax.ppermute(array, axis, [(i, i ^ step) for i in range(size)])]
  transfers between devices with their start and end apart: 30 -> 32, of which waited for: 9 -> 12; matrix products, arithmetic and copies ran while one was open for 0% -> 0% of each run, Pallas kernels for 35% -> 42%
where the time goes in v8:
time: 155 us; the launch traced here: 154 us
  Pallas kernels  70 us (45%)
  starting transfers between devices  44.4 us (29%)
  waiting for transfers between devices  37.3 us (24%)
    ppermute x10, starting transfers between devices, hop(): lax.ppermute(array, 'tp', [(2 * i + core, 2 * j + core) for i, j in pairs...  27.4 us
    pallas_call x6, Pallas kernels, column_products(): pl.pallas_call(functools.partial(product_kernel, steps, joins, len(more))...  23.7 us
    ppermute x22, waiting for transfers between devices, swapped(): return lax.ppermute(array, axis, [(i, i ^ step) for i in range(size)])  23.1 us
    pallas_call x4, Pallas kernels, cotangent_products(): pl.pallas_call(functools.partial(cotangent_kernel, count, begin, last, me...  20.8 us
    ppermute x22, starting transfers between devices, swapped(): return lax.ppermute(array, axis, [(i, i ^ step) for i in range(size)])  17 us
    ppermute x10, waiting for transfers between devices, hop(): lax.ppermute(array, 'tp', [(2 * i + core, 2 * j + core) for i, j in pairs...  14.2 us
    pallas_call x1, Pallas kernels, correlate(): pl.pallas_call(functools.partial(backward_kernel, members, per_group, sca...  9.78 us
    pallas_call x1, Pallas kernels, convolve(): pl.pallas_call(functools.partial(forward_kernel, members, per_group, widt...  5.54 us
  transfers between devices with their start and end apart: 32, of which 12 were waited for; matrix products, arithmetic and copies ran while one was open for 0% of the time, Pallas kernels for 42%

profile of v8, /device:TPU:0, one launch (start us, length us, event | category | flops | bytes accessed | tf_op | source)
XLA Modules:
  0.0 154.1 jit_solution(17380969063465804556)
XLA Ops:
  1.9 5.6 %collective-permute-start.4 = (bf16[512,1024]{1,0:T(8,128)(2,1)}, bf16[512,1024]{1,0:T(8,128)(2,1)S(1)}, u32[]{:S(2)}, u32[]{:S(2)}) collective-permute-start(bf16[512,1024]{1,0:T(8,128)(2,1)} %refs_0_.1), channel_id=1, source_target_pairs={{0,2},{1,3},{6,4},{7,5},{2,0},{3,1},{4,6},{5,7},{8,10},{9,11},{14,... | collective-permute-start | bytes 3145736 | tf_op jit(solution)/shard_map/ppermute | solution.py:351
  7.5 2.6 %gated_input.1 = (bf16[544,256]{1,0:T(8,128)(2,1)S(1)}, bf16[544,256]{1,0:T(8,128)(2,1)S(1)}, bf16[544,256]{1,0:T(8,128)(2,1)S(1)}, bf16[544,256]{1,0:T(8,128)(2,1)S(1)}) custom-call(s32[2]{0:T(128)S(1)} %pad_add_fusion.who_ref, bf16[512,1024]{1,0:T(8,128)(2,1)} %refs_4_.3, bf16[512,1024]{1,0:T(8,128)(2,1)} %refs_5_.1, f32[64,512]{1,0:T(8,128)} %bitcast.4), custom_call_target="tpu_custom_call" | custom-call | flops 1048576 | bytes 4096 | tf_op jit(solution)/shard_map/gated_input/pallas_call | solution.py:261
  14.9 5.0 %cotangent_blocks.4.refs_4_.refs_3_ = f32[512,1024]{1,0:T(8,128)S(1)} custom-call(s32[9]{0:T(128)S(1)} %plan.1.plan_ref._, bf16[1024,8192]{1,0:T(8,128)(2,1)} %weight_ref.19, bf16[512,1024]{1,0:T(8,128)(2,1)S(1)} %copy-done.4, bf16[512,1024]{1,0:T(8,128)(2,1)} %collective-permute-done.3.refs_1_), custom_call_target="tpu_custom_call" | custom-call | flops 1048576 | bytes 4096 | tf_op jit(solution)/shard_map/cotangent_blocks/pallas_call | solution.py:549
  19.9 5.8 %collective-permute-done.1.refs_2_ = bf16[544,256]{1,0:T(8,128)(2,1)S(1)} collective-permute-done((bf16[544,256]{1,0:T(8,128)(2,1)S(1)}, bf16[544,256]{1,0:T(8,128)(2,1)S(1)}, u32[]{:S(2)}, u32[]{:S(2)}) %collective-permute-start.1) | collective-permute-done | bytes 278560 | tf_op jit(solution)/shard_map/ppermute | solution.py:318
  25.7 5.5 %causal_conv.1 = (bf16[512,256]{1,0:T(8,128)(2,1)S(1)}, bf16[512,256]{1,0:T(8,128)(2,1)S(1)}, bf16[512,256]{1,0:T(8,128)(2,1)S(1)}, bf16[512,256]{1,0:T(8,128)(2,1)S(1)}) custom-call(s32[9]{0:T(128)S(1)} %plan.1.plan_ref._, bf16[544,256]{1,0:T(8,128)(2,1)S(1)} %get-tuple-element.45.refs_0_, bf16[544,256]{1,0:T(8,128)(2,1)S(1)} %collective-permute-done.refs_1_, ...), custom_call_target="tpu_custom_call" | custom-call | flops 1048576 | bytes 4096 | tf_op jit(solution)/shard_map/causal_conv/pallas_call | solution.py:182
  37.1 5.8 %collective-permute-done.6.refs_1_ = bf16[512,256]{1,0:T(8,128)(2,1)S(1)} collective-permute-done((bf16[512,256]{1,0:T(8,128)(2,1)S(1)}, bf16[512,256]{1,0:T(8,128)(2,1)S(1)}, u32[]{:S(2)}, u32[]{:S(2)}) %collective-permute-start.6) | collective-permute-done | bytes 262176 | tf_op jit(solution)/shard_map/ppermute | solution.py:318
  42.8 4.9 %collective-permute-done.7.refs_2_ = bf16[512,256]{1,0:T(8,128)(2,1)S(1)} collective-permute-done((bf16[512,256]{1,0:T(8,128)(2,1)S(1)}, bf16[512,256]{1,0:T(8,128)(2,1)S(1)}, u32[]{:S(2)}, u32[]{:S(2)}) %collective-permute-start.7) | collective-permute-done | bytes 262176 | tf_op jit(solution)/shard_map/ppermute | solution.py:318
  48.6 3.4 %projection_blocks.6 = (bf16[512,512]{1,0:T(8,128)(2,1)S(1)}, bf16[512,512]{1,0:T(8,128)(2,1)S(1)}) custom-call(s32[9]{0:T(128)S(1)} %plan.1.plan_ref._, bf16[512,1024]{1,0:T(8,128)(2,1)S(1)} %get-tuple-element.57.data_ref, bf16[1024,8192]{1,0:T(8,128)(2,1)} %weight_ref.19), custom_call_target="tpu_custom_call" | custom-call | flops 1048576 | bytes 4096 | tf_op jit(solution)/shard_map/projection_blocks/pallas_call | solution.py:482
  54.7 3.5 %projection_blocks.7.refs_2_.refs_0_ = bf16[512,1024]{1,0:T(8,128)(2,1)S(1)} custom-call(s32[9]{0:T(128)S(1)} %plan.1.plan_ref._, bf16[512,1024]{1,0:T(8,128)(2,1)S(1)} %get-tuple-element.57.data_ref, bf16[1024,8192]{1,0:T(8,128)(2,1)} %weight_ref.19, bf16[512,512]{1,0:T(8,128)(2,1)S(1)} %collective-permute-done.11.refs_0_, ...), custom_call_target="tpu_custom_call" | custom-call | flops 1048576 | bytes 4096 | tf_op jit(solution)/shard_map/projection_blocks/pallas_call | solution.py:482
  58.2 3.4 %projection_blocks.8 = (bf16[512,512]{1,0:T(8,128)(2,1)S(1)}, bf16[512,512]{1,0:T(8,128)(2,1)S(1)}) custom-call(s32[9]{0:T(128)S(1)} %plan.1.plan_ref._, bf16[512,1024]{1,0:T(8,128)(2,1)S(1)} %get-tuple-element.57.data_ref, bf16[1024,8192]{1,0:T(8,128)(2,1)} %weight_ref.19, bf16[512,1024]{1,0:T(8,128)(2,1)S(1)} %get-tuple-element.62.refs_0_), custom_call_target="tpu_custom_call" | custom-call | flops 1048576 | bytes 4096 | tf_op jit(solution)/shard_map/projection_blocks/pallas_call | solution.py:482
  63.5 6.0 %collective-permute-start.21 = (bf16[512,1024]{1,0:T(8,128)(2,1)S(1)}, bf16[512,1024]{1,0:T(8,128)(2,1)S(1)}, u32[]{:S(2)}, u32[]{:S(2)}) collective-permute-start(bf16[512,1024]{1,0:T(8,128)(2,1)S(1)} %projection_blocks.7.refs_2_.refs_0_), channel_id=1, source_target_pairs={{0,2},{1,3},{6,4},{7,5},{8,10},{9,11},{14,12},{15,13},{16,18},{17,... | collective-permute-start | bytes 3145736 | tf_op jit(solution)/shard_map/ppermute | solution.py:351
  70.4 2.9 %collective-permute-done.14.refs_1_ = bf16[512,512]{1,0:T(8,128)(2,1)S(1)} collective-permute-done((bf16[512,512]{1,0:T(8,128)(2,1)S(1)}, bf16[512,512]{1,0:T(8,128)(2,1)S(1)}, u32[]{:S(2)}, u32[]{:S(2)}) %collective-permute-start.14) | collective-permute-done | bytes 524320 | tf_op jit(solution)/shard_map/ppermute | solution.py:318
  73.3 3.5 %projection_blocks.9.refs_0_.refs_4_ = bf16[512,1024]{1,0:T(8,128)(2,1)S(1)} custom-call(s32[9]{0:T(128)S(1)} %plan.1.plan_ref._, bf16[512,1024]{1,0:T(8,128)(2,1)S(1)} %get-tuple-element.57.data_ref, bf16[1024,8192]{1,0:T(8,128)(2,1)} %weight_ref.19, bf16[512,512]{1,0:T(8,128)(2,1)S(1)} %collective-permute-done.13.refs_0_, ...), custom_call_target="tpu_custom_call" | custom-call | flops 1048576 | bytes 4096 | tf_op jit(solution)/shard_map/projection_blocks/pallas_call | solution.py:482
  76.7 4.9 %projection_blocks.10 = (bf16[512,1024]{1,0:T(8,128)(2,1)S(1)}, bf16[512,1024]{1,0:T(8,128)(2,1)S(1)}) custom-call(s32[9]{0:T(128)S(1)} %plan.1.plan_ref._, bf16[512,1024]{1,0:T(8,128)(2,1)S(1)} %get-tuple-element.57.data_ref, bf16[1024,8192]{1,0:T(8,128)(2,1)} %weight_ref.19, bf16[512,1024]{1,0:T(8,128)(2,1)S(1)} %projection_blocks.9.refs_0_.refs_4_), custom_call_target="tpu_custom_call" | custom-call | flops 1048576 | bytes 4096 | tf_op jit(solution)/shard_map/projection_blocks/pallas_call | solution.py:482
  81.7 6.4 %cotangent_blocks.5.refs_1_.refs_2_ = f32[512,1024]{1,0:T(8,128)S(1)} custom-call(s32[9]{0:T(128)S(1)} %plan.1.plan_ref._, bf16[1024,8192]{1,0:T(8,128)(2,1)} %weight_ref.19, bf16[512,1024]{1,0:T(8,128)(2,1)S(1)} %get-tuple-element.58.refs_0_, bf16[512,1024]{1,0:T(8,128)(2,1)S(1)} %collective-permute-done.18.refs_1_, bf16[512,1024]{1,0:T(8,128)(2,1)S(1)} %added.6.refs_2_, ...), custom_call_target="tpu_custom_call" | custom-call | flops 1048576 | bytes 4096 | tf_op jit(solution)/shard_map/cotangent_blocks/pallas_call | solution.py:549
  88.0 2.6 %collective-permute-done.17.refs_0_ = bf16[512,1024]{1,0:T(8,128)(2,1)S(1)} collective-permute-done((bf16[512,1024]{1,0:T(8,128)(2,1)S(1)}, bf16[512,1024]{1,0:T(8,128)(2,1)S(1)}, u32[]{:S(2)}, u32[]{:S(2)}) %collective-permute-start.17) | collective-permute-done | bytes 1048608 | tf_op jit(solution)/shard_map/ppermute | solution.py:351
  93.0 7.2 %collective-permute-start.23 = (bf16[512,1024]{1,0:T(8,128)(2,1)S(1)}, bf16[512,1024]{1,0:T(8,128)(2,1)S(1)}, u32[]{:S(2)}, u32[]{:S(2)}) collective-permute-start(bf16[512,1024]{1,0:T(8,128)(2,1)S(1)} %held.10.refs_0_), channel_id=1, source_target_pairs={{0,2},{1,3},{6,4},{7,5},{8,10},{9,11},{14,12},{15,13},{16,18},{17,... | collective-permute-start | bytes 3145736 | tf_op jit(solution)/shard_map/ppermute | solution.py:351
  100.2 4.8 %cotangent_blocks.6.refs_1_ = f32[512,1024]{1,0:T(8,128)S(1)} custom-call(s32[9]{0:T(128)S(1)} %plan.1.plan_ref._, bf16[1024,8192]{1,0:T(8,128)(2,1)} %weight_ref.19, bf16[512,1024]{1,0:T(8,128)(2,1)S(1)} %collective-permute-done.20.refs_0_, bf16[512,1024]{1,0:T(8,128)(2,1)S(1)} %added.7.refs_1_, f32[512,1024]{1,0:T(8,128)S(1)} %cotangent_blocks.5.refs_1_.refs_2_, ...), custom_call_target="tpu_custom_call" | custom-call | flops 1048576 | bytes 4096 | tf_op jit(solution)/shard_map/cotangent_blocks/pallas_call | solution.py:549
  105.0 4.6 %cotangent_blocks.7 = (bf16[512,1024]{1,0:T(8,128)(2,1)}, bf16[512,256]{1,0:T(8,128)(2,1)S(1)}, bf16[512,256]{1,0:T(8,128)(2,1)S(1)}, bf16[512,256]{1,0:T(8,128)(2,1)S(1)}, bf16[512,256]{1,0:T(8,128)(2,1)S(1)}) custom-call(s32[9]{0:T(128)S(1)} %plan.1.plan_ref._, bf16[1024,8192]{1,0:T(8,128)(2,1)} %weight_ref.19, ...), custom_call_target="tpu_custom_call" | custom-call | flops 1048576 | bytes 4096 | tf_op jit(solution)/shard_map/cotangent_blocks/pallas_call | solution.py:549
  113.1 5.1 %projection_blocks.11 = (bf16[512,1024]{1,0:T(8,128)(2,1)S(1)}, bf16[512,1024]{1,0:T(8,128)(2,1)S(1)}) custom-call(s32[9]{0:T(128)S(1)} %plan.1.plan_ref._, bf16[512,1024]{1,0:T(8,128)(2,1)S(1)} %get-tuple-element.57.data_ref, bf16[1024,8192]{1,0:T(8,128)(2,1)} %weight_ref.19, bf16[512,1024]{1,0:T(8,128)(2,1)S(1)} %collective-permute-done.15.refs_0_, ...), custom_call_target="tpu_custom_call" | custom-call | flops 1048576 | bytes 4096 | tf_op jit(solution)/shard_map/projection_blocks/pallas_call | solution.py:482
  118.2 3.5 %collective-permute-done.23.refs_1_ = bf16[512,1024]{1,0:T(8,128)(2,1)S(1)} collective-permute-done((bf16[512,1024]{1,0:T(8,128)(2,1)S(1)}, bf16[512,1024]{1,0:T(8,128)(2,1)S(1)}, u32[]{:S(2)}, u32[]{:S(2)}) %collective-permute-start.23) | collective-permute-done | bytes 1048608 | tf_op jit(solution)/shard_map/ppermute | solution.py:351
  124.7 2.8 %collective-permute-start.27 = (bf16[512,1024]{1,0:T(8,128)(2,1)S(1)}, bf16[512,1024]{1,0:T(8,128)(2,1)S(1)}, u32[]{:S(2)}, u32[]{:S(2)}) collective-permute-start(bf16[512,1024]{1,0:T(8,128)(2,1)S(1)} %added.9.refs_8_), channel_id=1, source_target_pairs={{2,0},{3,1},{4,6},{5,7},{0,2},{1,3},{6,4},{7,5},{10,8},{11,9},{12,... | collective-permute-start | bytes 3145736 | tf_op jit(solution)/shard_map/ppermute | solution.py:351
  127.5 9.8 %causal_conv_grads.1 = (bf16[544,256]{1,0:T(8,128)(2,1)S(1)}, bf16[544,256]{1,0:T(8,128)(2,1)S(1)}, bf16[544,256]{1,0:T(8,128)(2,1)S(1)}, bf16[544,256]{1,0:T(8,128)(2,1)S(1)}) custom-call(s32[9]{0:T(128)S(1)} %plan.1.plan_ref._, bf16[544,256]{1,0:T(8,128)(2,1)S(1)} %get-tuple-element.45.refs_0_, bf16[544,256]{1,0:T(8,128)(2,1)S(1)} %collective-permute-done.refs_1_, ...), custom_call_target="tpu_custom_call" | custom-call | flops 1048576 | bytes 4096 | tf_op jit(solution)/shard_map/causal_conv_grads/pallas_call | solution.py:203
  140.9 7.8 %collective-permute-done.27.refs_1_ = bf16[512,1024]{1,0:T(8,128)(2,1)S(1)} collective-permute-done((bf16[512,1024]{1,0:T(8,128)(2,1)S(1)}, bf16[512,1024]{1,0:T(8,128)(2,1)S(1)}, u32[]{:S(2)}, u32[]{:S(2)}) %collective-permute-start.27) | collective-permute-done | bytes 1048608 | tf_op jit(solution)/shard_map/ppermute | solution.py:351
  (79 shorter events, 35.7 us)
Async XLA Ops:
  0.6 12.6 %collective-permute-start.3 = (bf16[512,1024]{1,0:T(8,128)(2,1)}, bf16[512,1024]{1,0:T(8,128)(2,1)}, u32[]{:S(2)}, u32[]{:S(2)}) collective-permute-start(bf16[512,1024]{1,0:T(8,128)(2,1)} %refs_0_.1), channel_id=1, source_target_pairs={{0,1},{1,0},{2,3},{3,2},{4,5},{5,4},{6,7},{7,6},{8,9},{9,8},{10,11... | collective-permute-start | bytes 3145736 | tf_op jit(solution)/shard_map/ppermute | solution.py:318
  1.2 30.2 %collective-permute-start.5 = (bf16[512,1024]{1,0:T(8,128)(2,1)}, bf16[512,1024]{1,0:T(8,128)(2,1)S(1)}, u32[]{:S(2)}, u32[]{:S(2)}) collective-permute-start(bf16[512,1024]{1,0:T(8,128)(2,1)} %refs_0_.1), channel_id=1, source_target_pairs={{2,4},{3,5},{4,2},{5,3},{10,12},{11,13},{12,10},{13,11},{18,20},{1... | collective-permute-start | bytes 3145736 | tf_op jit(solution)/shard_map/ppermute | solution.py:351
  1.9 29.4 %collective-permute-start.4 = (bf16[512,1024]{1,0:T(8,128)(2,1)}, bf16[512,1024]{1,0:T(8,128)(2,1)S(1)}, u32[]{:S(2)}, u32[]{:S(2)}) collective-permute-start(bf16[512,1024]{1,0:T(8,128)(2,1)} %refs_0_.1), channel_id=1, source_target_pairs={{0,2},{1,3},{6,4},{7,5},{2,0},{3,1},{4,6},{5,7},{8,10},{9,11},{14,... | collective-permute-start | bytes 3145736 | tf_op jit(solution)/shard_map/ppermute | solution.py:351
  11.7 14.0 %collective-permute-start.1 = (bf16[544,256]{1,0:T(8,128)(2,1)S(1)}, bf16[544,256]{1,0:T(8,128)(2,1)S(1)}, u32[]{:S(2)}, u32[]{:S(2)}) collective-permute-start(bf16[544,256]{1,0:T(8,128)(2,1)S(1)} %get-tuple-element.47), channel_id=1, source_target_pairs={{0,16},{8,24},{16,0},{24,8},{1,17},{9,25},{17,1},{25,9},{2,18},{10... | collective-permute-start | bytes 835592 | tf_op jit(solution)/shard_map/ppermute | solution.py:318
  13.2 12.5 %collective-permute-start.2 = (bf16[544,256]{1,0:T(8,128)(2,1)S(1)}, bf16[544,256]{1,0:T(8,128)(2,1)S(1)}, u32[]{:S(2)}, u32[]{:S(2)}) collective-permute-start(bf16[544,256]{1,0:T(8,128)(2,1)S(1)} %get-tuple-element.48), channel_id=1, source_target_pairs={{0,24},{8,16},{16,8},{24,0},{1,25},{9,17},{17,9},{25,1},{2,26},{10... | collective-permute-start | bytes 835592 | tf_op jit(solution)/shard_map/ppermute | solution.py:318
  31.3 26.8 %collective-permute-start.10 = (bf16[512,1024]{1,0:T(8,128)(2,1)S(1)}, bf16[512,1024]{1,0:T(8,128)(2,1)S(1)}, u32[]{:S(2)}, u32[]{:S(2)}) collective-permute-start(bf16[512,1024]{1,0:T(8,128)(2,1)S(1)} %get-tuple-element.59.refs_0_), channel_id=1, source_target_pairs={{2,0},{3,1},{4,6},{5,7},{10,8},{11,9},{12,14},{13,15},{18,16},{19,... | collective-permute-start | bytes 3145736 | tf_op jit(solution)/shard_map/ppermute | solution.py:351
  32.8 25.4 %collective-permute-start.9 = (bf16[512,1024]{1,0:T(8,128)(2,1)S(1)}, bf16[512,1024]{1,0:T(8,128)(2,1)S(1)}, u32[]{:S(2)}, u32[]{:S(2)}) collective-permute-start(bf16[512,1024]{1,0:T(8,128)(2,1)S(1)} %get-tuple-element.58.refs_0_), channel_id=1, source_target_pairs={{2,4},{3,5},{4,2},{5,3},{10,12},{11,13},{12,10},{13,11},{18,20},{1... | collective-permute-start | bytes 3145736 | tf_op jit(solution)/shard_map/ppermute | solution.py:351
  34.8 12.9 %collective-permute-start.7 = (bf16[512,256]{1,0:T(8,128)(2,1)S(1)}, bf16[512,256]{1,0:T(8,128)(2,1)S(1)}, u32[]{:S(2)}, u32[]{:S(2)}) collective-permute-start(bf16[512,256]{1,0:T(8,128)(2,1)S(1)} %get-tuple-element.55), channel_id=1, source_target_pairs={{0,16},{8,24},{16,0},{24,8},{1,17},{9,25},{17,1},{25,9},{2,18},{10... | collective-permute-start | bytes 786440 | tf_op jit(solution)/shard_map/ppermute | solution.py:318
  36.1 11.6 %collective-permute-start.8 = (bf16[512,256]{1,0:T(8,128)(2,1)S(1)}, bf16[512,256]{1,0:T(8,128)(2,1)S(1)}, u32[]{:S(2)}, u32[]{:S(2)}) collective-permute-start(bf16[512,256]{1,0:T(8,128)(2,1)S(1)} %get-tuple-element.56), channel_id=1, source_target_pairs={{0,24},{8,16},{16,8},{24,0},{1,25},{9,17},{17,9},{25,1},{2,26},{10... | collective-permute-start | bytes 786440 | tf_op jit(solution)/shard_map/ppermute | solution.py:318
  61.8 19.8 %collective-permute-start.18 = (bf16[512,1024]{1,0:T(8,128)(2,1)S(1)}, bf16[512,1024]{1,0:T(8,128)(2,1)S(1)}, u32[]{:S(2)}, u32[]{:S(2)}) collective-permute-start(bf16[512,1024]{1,0:T(8,128)(2,1)S(1)} %get-tuple-element.58.refs_0_), channel_id=1, source_target_pairs={{0,1},{1,0},{2,3},{3,2},{4,5},{5,4},{6,7},{7,6},{8,9},{9,8},{10,11... | collective-permute-start | bytes 3145736 | tf_op jit(solution)/shard_map/ppermute | solution.py:318
  62.2 28.5 %collective-permute-start.17 = (bf16[512,1024]{1,0:T(8,128)(2,1)S(1)}, bf16[512,1024]{1,0:T(8,128)(2,1)S(1)}, u32[]{:S(2)}, u32[]{:S(2)}) collective-permute-start(bf16[512,1024]{1,0:T(8,128)(2,1)S(1)} %get-tuple-element.62.refs_0_), channel_id=1, source_target_pairs={{2,0},{3,1},{4,6},{5,7},{10,8},{11,9},{12,14},{13,15},{18,16},{19,... | collective-permute-start | bytes 3145736 | tf_op jit(solution)/shard_map/ppermute | solution.py:351
  63.5 28.5 %collective-permute-start.21 = (bf16[512,1024]{1,0:T(8,128)(2,1)S(1)}, bf16[512,1024]{1,0:T(8,128)(2,1)S(1)}, u32[]{:S(2)}, u32[]{:S(2)}) collective-permute-start(bf16[512,1024]{1,0:T(8,128)(2,1)S(1)} %projection_blocks.7.refs_2_.refs_0_), channel_id=1, source_target_pairs={{0,2},{1,3},{6,4},{7,5},{8,10},{9,11},{14,12},{15,13},{16,18},{17,... | collective-permute-start | bytes 3145736 | tf_op jit(solution)/shard_map/ppermute | solution.py:351
  69.8 23.2 %collective-permute-start.20 = (bf16[512,1024]{1,0:T(8,128)(2,1)S(1)}, bf16[512,1024]{1,0:T(8,128)(2,1)S(1)}, u32[]{:S(2)}, u32[]{:S(2)}) collective-permute-start(bf16[512,1024]{1,0:T(8,128)(2,1)S(1)} %added.6.refs_2_), channel_id=1, source_target_pairs={{0,1},{1,0},{2,3},{3,2},{4,5},{5,4},{6,7},{7,6},{8,9},{9,8},{10,11... | collective-permute-start | bytes 3145736 | tf_op jit(solution)/shard_map/ppermute | solution.py:318
  91.0 14.0 %collective-permute-start.19 = (bf16[512,1024]{1,0:T(8,128)(2,1)S(1)}, bf16[512,1024]{1,0:T(8,128)(2,1)S(1)}, u32[]{:S(2)}, u32[]{:S(2)}) collective-permute-start(bf16[512,1024]{1,0:T(8,128)(2,1)S(1)} %added.7.refs_1_), channel_id=1, source_target_pairs={{0,1},{1,0},{2,3},{3,2},{4,5},{5,4},{6,7},{7,6},{8,9},{9,8},{10,11... | collective-permute-start | bytes 3145736 | tf_op jit(solution)/shard_map/ppermute | solution.py:318
  91.0 19.8 %collective-permute-start.16 = (bf16[512,1024]{1,0:T(8,128)(2,1)S(1)}, bf16[512,1024]{1,0:T(8,128)(2,1)S(1)}, u32[]{:S(2)}, u32[]{:S(2)}) collective-permute-start(bf16[512,1024]{1,0:T(8,128)(2,1)S(1)} %get-tuple-element.66), channel_id=1, source_target_pairs={{0,1},{1,0},{2,3},{3,2},{4,5},{5,4},{6,7},{7,6},{8,9},{9,8},{10,11... | collective-permute-start | bytes 3145736 | tf_op jit(solution)/shard_map/ppermute | solution.py:318
  91.5 20.1 %collective-permute-start.15 = (bf16[512,1024]{1,0:T(8,128)(2,1)S(1)}, bf16[512,1024]{1,0:T(8,128)(2,1)S(1)}, u32[]{:S(2)}, u32[]{:S(2)}) collective-permute-start(bf16[512,1024]{1,0:T(8,128)(2,1)S(1)} %get-tuple-element.65.refs_2_), channel_id=1, source_target_pairs={{0,1},{1,0},{2,3},{3,2},{4,5},{5,4},{6,7},{7,6},{8,9},{9,8},{10,11... | collective-permute-start | bytes 3145736 | tf_op jit(solution)/shard_map/ppermute | solution.py:318
  92.2 26.0 %collective-permute-start.22 = (bf16[512,1024]{1,0:T(8,128)(2,1)S(1)}, bf16[512,1024]{1,0:T(8,128)(2,1)S(1)}, u32[]{:S(2)}, u32[]{:S(2)}) collective-permute-start(bf16[512,1024]{1,0:T(8,128)(2,1)S(1)} %added.8.refs_3_), channel_id=1, source_target_pairs={{2,4},{3,5},{4,2},{5,3},{10,12},{11,13},{12,10},{13,11},{18,20},{1... | collective-permute-start | bytes 3145736 | tf_op jit(solution)/shard_map/ppermute | solution.py:351
  93.0 28.7 %collective-permute-start.23 = (bf16[512,1024]{1,0:T(8,128)(2,1)S(1)}, bf16[512,1024]{1,0:T(8,128)(2,1)S(1)}, u32[]{:S(2)}, u32[]{:S(2)}) collective-permute-start(bf16[512,1024]{1,0:T(8,128)(2,1)S(1)} %held.10.refs_0_), channel_id=1, source_target_pairs={{0,2},{1,3},{6,4},{7,5},{8,10},{9,11},{14,12},{15,13},{16,18},{17,... | collective-permute-start | bytes 3145736 | tf_op jit(solution)/shard_map/ppermute | solution.py:351
  109.6 12.1 %collective-permute-start.24 = (bf16[512,256]{1,0:T(8,128)(2,1)S(1)}, bf16[512,256]{1,0:T(8,128)(2,1)S(1)}, u32[]{:S(2)}, u32[]{:S(2)}) collective-permute-start(bf16[512,256]{1,0:T(8,128)(2,1)S(1)} %get-tuple-element.72), channel_id=1, source_target_pairs={{0,8},{8,0},{16,24},{24,16},{1,9},{9,1},{17,25},{25,17},{2,10},{10... | collective-permute-start | bytes 786440 | tf_op jit(solution)/shard_map/ppermute | solution.py:318
  111.6 11.5 %collective-permute-start.26 = (bf16[512,256]{1,0:T(8,128)(2,1)S(1)}, bf16[512,256]{1,0:T(8,128)(2,1)S(1)}, u32[]{:S(2)}, u32[]{:S(2)}) collective-permute-start(bf16[512,256]{1,0:T(8,128)(2,1)S(1)} %get-tuple-element.74), channel_id=1, source_target_pairs={{0,24},{8,16},{16,8},{24,0},{1,25},{9,17},{17,9},{25,1},{2,26},{10... | collective-permute-start | bytes 786440 | tf_op jit(solution)/shard_map/ppermute | solution.py:318
  123.4 17.4 %collective-permute-start.28 = (bf16[512,1024]{1,0:T(8,128)(2,1)S(1)}, bf16[512,1024]{1,0:T(8,128)(2,1)S(1)}, u32[]{:S(2)}, u32[]{:S(2)}) collective-permute-start(bf16[512,1024]{1,0:T(8,128)(2,1)S(1)} %added.10.refs_9_), channel_id=1, source_target_pairs={{2,4},{3,5},{4,2},{5,3},{10,12},{11,13},{12,10},{13,11},{18,20},{1... | collective-permute-start | bytes 3145736 | tf_op jit(solution)/shard_map/ppermute | solution.py:351
  124.7 24.0 %collective-permute-start.27 = (bf16[512,1024]{1,0:T(8,128)(2,1)S(1)}, bf16[512,1024]{1,0:T(8,128)(2,1)S(1)}, u32[]{:S(2)}, u32[]{:S(2)}) collective-permute-start(bf16[512,1024]{1,0:T(8,128)(2,1)S(1)} %added.9.refs_8_), channel_id=1, source_target_pairs={{2,0},{3,1},{4,6},{5,7},{0,2},{1,3},{6,4},{7,5},{10,8},{11,9},{12,... | collective-permute-start | bytes 3145736 | tf_op jit(solution)/shard_map/ppermute | solution.py:351
  137.3 13.1 %collective-permute-start.29 = (bf16[544,256]{1,0:T(8,128)(2,1)S(1)}, bf16[544,256]{1,0:T(8,128)(2,1)S(1)}, u32[]{:S(2)}, u32[]{:S(2)}) collective-permute-start(bf16[544,256]{1,0:T(8,128)(2,1)S(1)} %get-tuple-element.79), channel_id=1, source_target_pairs={{0,8},{8,0},{16,24},{24,16},{1,9},{9,1},{17,25},{25,17},{2,10},{10... | collective-permute-start | bytes 835592 | tf_op jit(solution)/shard_map/ppermute | solution.py:318
  138.6 11.9 %collective-permute-start.30 = (bf16[544,256]{1,0:T(8,128)(2,1)S(1)}, bf16[544,256]{1,0:T(8,128)(2,1)S(1)}, u32[]{:S(2)}, u32[]{:S(2)}) collective-permute-start(bf16[544,256]{1,0:T(8,128)(2,1)S(1)} %get-tuple-element.80), channel_id=1, source_target_pairs={{0,16},{8,24},{16,0},{24,8},{1,17},{9,25},{17,1},{25,9},{2,18},{10... | collective-permute-start | bytes 835592 | tf_op jit(solution)/shard_map/ppermute | solution.py:318
  (13 other events, 92.8 us)

commit v9 on v8

--- a/solution.py
+++ b/solution.py
@@ -357,6 +357,7 @@
 ACROSS = ((1, 2), (2, 1))
 OUTWARD = ((1, 0), (2, 3))
 OWN, NEAR, MIDDLE, FAR = range(4)
+IN_MIDDLE = POSITION + 1
 CHIPS = ((0, 1, 2, 3), (1, 0, 3, 2), (2, 2, 1, 1), (3, 3, 0, 0))
 
 
@@ -372,12 +373,13 @@
         plan_ref[2 * number] = 2 * source + core
         plan_ref[2 * number + 1] = 2 * source + 1 - core
     plan_ref[POSITION] = who_ref[0]
+    plan_ref[IN_MIDDLE] = ((chip == 1) | (chip == 2)).astype(jnp.int32)
 
 
 def planned(who):
     return pl.pallas_call(
         plan_kernel,
-        out_shape=jax.ShapeDtypeStruct((POSITION + 1,), jnp.int32),
+        out_shape=jax.ShapeDtypeStruct((IN_MIDDLE + 1,), jnp.int32),
         in_specs=[SMEM],
         out_specs=SMEM,
         compiler_params=pltpu.CompilerParams(vmem_limit_bytes=2**20),
@@ -420,6 +422,31 @@
         cost_estimate=COST,
         name="added",
     )(*arrays)
+
+
+def choice_kernel(plan_ref, middle_ref, end_ref, *refs):
+    out_ref = refs[-1]
+    in_middle = plan_ref[IN_MIDDLE] == 1
+
+    @pl.when(in_middle)
+    def _():
+        out_ref[...] = middle_ref[...]
+
+    @pl.when(jnp.logical_not(in_middle))
+    def _():
+        out_ref[...] = end_ref[...]
+
+
+def chosen(plan, in_middle, at_end, after=()):
+    return pl.pallas_call(
+        choice_kernel,
+        out_shape=jax.ShapeDtypeStruct(at_end.shape, at_end.dtype),
+        in_specs=[SMEM, VMEM, VMEM] + [ANYWHERE] * len(after),
+        out_specs=VMEM,
+        compiler_params=pltpu.CompilerParams(vmem_limit_bytes=2**20),
+        cost_estimate=COST,
+        name="chosen",
+    )(plan, in_middle, at_end, *after)
 
 
 def gate_kernel(members, plan_ref, *refs):
@@ -476,92 +503,108 @@
     def weights(i, at):
         return 0, at[2 * (first - i // tiles) + other] * tiles + i % tiles
 
-    def whole(array_width):
-        return pl.BlockSpec((rows, array_width), lambda i, at: (0, 0))
-
     return pl.pallas_call(
         functools.partial(product_kernel, steps, joins, len(more)),
         out_shape=[jax.ShapeDtypeStruct((rows, tile * joins), jnp.bfloat16)] * (steps // joins),
         grid_spec=pltpu.PrefetchScalarGridSpec(
             num_scalar_prefetch=1,
             grid=(steps,),
-            in_specs=[whole(depth), pl.BlockSpec((depth, tile), weights)]
-            + [whole(tile)] * len(more)
+            in_specs=[VMEM, pl.BlockSpec((depth, tile), weights)]
+            + [VMEM] * len(more)
             + [ANYWHERE] * len(after),
-            out_specs=[whole(tile * joins)] * (steps // joins),
+            out_specs=[VMEM] * (steps // joins),
         ),
-        compiler_params=pltpu.CompilerParams(vmem_limit_bytes=24 * 2**20),
+        compiler_params=pltpu.CompilerParams(vmem_limit_bytes=16 * 2**20),
         cost_estimate=COST,
         name="projection_blocks",
     )(plan, data, in_hbm(out_weight), *more, *after)
 
 
-def cotangent_kernel(count, begin, last, members, plan_ref, weight_ref, *refs):
+def cotangent_kernel(count, begin, _, weight_ref, *refs):
     blocks, refs = refs[:count], refs[count:]
     step = pl.program_id(0)
     total = refs[-1]
 
-    @pl.when(step == 0)
-    def _():
-        total[...] = jnp.zeros_like(total) if begin else refs[0][...]
-
     for number, block in enumerate(blocks):
 
         @pl.when(step == number)
-        def _(block=block):
-            total[...] += lax.dot_general(
+        def _(number=number, block=block):
+            product = lax.dot_general(
                 block[...], weight_ref[...], NT, preferred_element_type=jnp.float32
             )
-
-    if last:
-        conv_ref, query_ref = refs[1:3]
-        grad_ref, parts = refs[-2 - members], refs[-1 - members : -1]
-
-        @pl.when(step == count - 1)
-        def _():
-            dgated = wide(total[...].astype(jnp.bfloat16))
-            grad_ref[...] = (dgated * wide(conv_ref[...])).astype(jnp.bfloat16)
-            share = parts[0].shape[1]
-            for step in range(members):
-                start = pl.multiple_of((plan_ref[POSITION] ^ step) * share, share)
-                columns = pl.ds(start, share)
-                dgated = wide(total[:, columns].astype(jnp.bfloat16))
-                parts[step][...] = (dgated * wide(query_ref[:, columns])).astype(jnp.bfloat16)
+            if number == 0:
+                total[...] = product if begin else refs[0][...] + product
+            else:
+                total[...] += product
+
+
+def last_cotangent_kernel(
+    members, _, weight_ref, block_ref, start_ref, conv_ref, query_ref, grad_ref, *parts
+):
+    product = lax.dot_general(
+        block_ref[...], weight_ref[...], NT, preferred_element_type=jnp.float32
+    )
+    dgated = wide((start_ref[...] + product).astype(jnp.bfloat16))
+    grad_ref[...] = (dgated * wide(conv_ref[...])).astype(jnp.bfloat16)
+    cotangent = (dgated * wide(query_ref[...])).astype(jnp.bfloat16)
+    for step in range(members):
+
+        @pl.when(pl.program_id(0) == step)
+        def _(step=step):
+            parts[step][...] = cotangent
+
+
+def last_cotangents(plan, first, block, out_weight, start, convolved, query_gate, members):
+    rows, width = block.shape
+    channels = out_weight.shape[0]
+    share = channels // members
+    piece = pl.BlockSpec((rows, share), lambda i, at: (0, at[POSITION] ^ i))
+    whole = pl.BlockSpec((rows, width), lambda i, at: (0, 0))
+    part = pl.BlockSpec((rows, share), lambda i, at: (0, 0))
+    return pl.pallas_call(
+        functools.partial(last_cotangent_kernel, members),
+        out_shape=[jax.ShapeDtypeStruct((rows, channels), jnp.bfloat16)]
+        + [jax.ShapeDtypeStruct((rows, share), jnp.bfloat16)] * members,
+        grid_spec=pltpu.PrefetchScalarGridSpec(
+            num_scalar_prefetch=1,
+            grid=(members,),
+            in_specs=[
+                pl.BlockSpec((share, width), lambda i, at: (at[POSITION] ^ i, at[first])),
+                whole,
+                piece,
+                piece,
+                piece,
+            ],
+            out_specs=[piece] + [part] * members,
+        ),
+        compiler_params=pltpu.CompilerParams(vmem_limit_bytes=16 * 2**20),
+        cost_estimate=COST,
+        name="cotangent_last",
+    )(plan, in_hbm(out_weight), block, start, convolved, query_gate)
 
 
 def both(blocks):
     return [part for block in blocks for part in (block, swapped(block, "tp", 1))]
 
 
-def cotangent_products(
-    plan, first, parts, out_weight, start=None, gates=(), after=(), members=0
-):
+def cotangent_products(plan, first, parts, out_weight, start=None, after=()):
     rows, width = parts[0].shape
     channels = out_weight.shape[0]
     count = len(parts)
-    whole = pl.BlockSpec((rows, channels), lambda i, at: (0, 0))
-    part = pl.BlockSpec((rows, width), lambda i, at: (0, 0))
-    piece = pl.BlockSpec((rows, channels // max(members, 1)), lambda i, at: (0, 0))
-    array = jax.ShapeDtypeStruct((rows, channels), jnp.bfloat16)
-    cut_array = jax.ShapeDtypeStruct((rows, channels // max(members, 1)), jnp.bfloat16)
-    begin, last = start is None, bool(gates)
-    extra = (() if begin else (start,)) + tuple(gates)
-    return pl.pallas_call(
-        functools.partial(cotangent_kernel, count, begin, last, members),
-        out_shape=[array] + [cut_array] * members
-        if last
-        else jax.ShapeDtypeStruct((rows, channels), jnp.float32),
+    begin = start is None
+    extra = () if begin else (start,)
+    return pl.pallas_call(
+        functools.partial(cotangent_kernel, count, begin),
+        out_shape=jax.ShapeDtypeStruct((rows, channels), jnp.float32),
         grid_spec=pltpu.PrefetchScalarGridSpec(
             num_scalar_prefetch=1,
             grid=(count,),
             in_specs=[pl.BlockSpec((channels, width), lambda i, at: (0, at[first + i]))]
-            + [part] * count
-            + [whole] * len(extra)
+            + [VMEM] * (count + len(extra))
             + [ANYWHERE] * len(after),
-            out_specs=[whole] + [piece] * members if last else whole,
-            scratch_shapes=[pltpu.VMEM((rows, channels), jnp.float32)] if last else [],
+            out_specs=VMEM,
         ),
-        compiler_params=pltpu.CompilerParams(vmem_limit_bytes=24 * 2**20),
+        compiler_params=pltpu.CompilerParams(vmem_limit_bytes=16 * 2**20),
         cost_estimate=COST,
         name="cotangent_blocks",
     )(plan, in_hbm(out_weight), *parts, *extra, *after)
@@ -629,36 +672,29 @@
     given_far = product(FAR, 1, 1, tiles=2)
     received = [swapped(part, "tp", 1) for part in given_far]
     (first,) = product(FAR, 1, 0, received, tiles=2, joins=2)
-    one = hop(first, INWARD)
-    far, skip = held_until([far, skip], (first,))
-    last = hop(far, OUTWARD)
-    given_middle = product(MIDDLE, 1, 1, (), (far,), tiles=2)
+    far, skip, near = held_until([far, skip, near], (first,))
+    mixed = chosen(plan, far, first)
+    arrived = hop(mixed, OUTWARD + INWARD)
+    given_middle = product(MIDDLE, 1, 1, (), (mixed,), tiles=2)
     received = [swapped(part, "tp", 1) for part in given_middle]
     (second,) = product(MIDDLE, 1, 0, received, tiles=2, joins=2)
     middle_block = added(cross, skip)
     blocks = [near, swapped(near, "tp", 1), middle_block]
     total = cotangent_products(plan, 2 * NEAR, blocks, out_weight, total, after=(second,))
     given_near, given_own = product(NEAR, 2, 1, (), (second,))
-    (one,) = held_until([one], (total, given_near))
-    through = added(first, one)
+    (arrived,) = held_until([arrived], (total, given_near))
+    through = added(first, arrived)
     two_a = hop(through, ACROSS)
-    (second,) = held_until([second], (one,))
+    (second,) = held_until([second], (arrived,))
     two_b = hop(second, INWARD)
 
-    (last,) = held_until([last], (total, given_near))
-    far_block, far_other = both([added(far, last)])
+    far_block, far_other = both([chosen(plan, far, arrived, (through,))])
     blocks = [swapped(middle_block, "tp", 1), far_block]
     total = cotangent_products(
         plan, 2 * MIDDLE + 1, blocks, out_weight, total, after=(through,)
     )
-    grad_query, *grad_parts = cotangent_products(
-        plan,
-        2 * FAR + 1,
-        [far_other],
-        out_weight,
-        total,
-        (convolved, query_gate),
-        members=members,
+    grad_query, *grad_parts = last_cotangents(
+        plan, 2 * FAR + 1, far_other, out_weight, total, convolved, query_gate, members
     )
     received = (swapped(given_near, "tp", 1), swapped(given_own, "tp", 1))
     third, own = product(NEAR, 2, 0, received, (grad_parts[0],))

time: 155 us -> 152 us (0.981)
  starting transfers between devices: 44.4 us -> 36.9 us
  waiting for transfers between devices: 37.3 us -> 40 us
  Pallas kernels: 70 us -> 71.8 us
    ppermute x10 -> x9, starting transfers between devices: 27.4 us -> 20.3 us  [hop(): lax.ppermute(array, 'tp', [(2 * i + core, 2 * j + core) for i, j in pairs...]
    pallas_call x5 -> x7, Pallas kernels: 21.9 us -> 24 us  [the longest x3 16.2 us: cotangent_products(): pl.pallas_call(functools.partial(cotangent_kernel, count, begin), out_sha...]
    ppermute x10 -> x9, waiting for transfers between devices: 14.2 us -> 16 us  [hop(): lax.ppermute(array, 'tp', [(2 * i + core, 2 * j + core) for i, j in pairs...]
    pallas_call x6 -> x5, Pallas kernels: 3.21 us -> 2.9 us  [added(): pl.pallas_call(add_kernel, out_shape=jax.ShapeDtypeStruct((rows, width),...]
  transfers between devices with their start and end apart: 32 -> 31, of which waited for: 12 -> 13; matrix products, arithmetic and copies ran while one was open for 0% -> 0% of each run, Pallas kernels for 42% -> 46%
where the time goes in v9:
time: 152 us; the launch traced here: 151 us
  Pallas kernels  71.8 us (47%)
  waiting for transfers between devices  40 us (26%)
  starting transfers between devices  36.9 us (24%)
    ppermute x22, waiting for transfers between devices, swapped(): return lax.ppermute(array, axis, [(i, i ^ step) for i in range(size)])  24 us
    pallas_call x6, Pallas kernels, column_products(): pl.pallas_call(functools.partial(product_kernel, steps, joins, len(more))...  23.7 us
    ppermute x9, starting transfers between devices, hop(): lax.ppermute(array, 'tp', [(2 * i + core, 2 * j + core) for i, j in pairs...  20.3 us
    ppermute x22, starting transfers between devices, swapped(): return lax.ppermute(array, axis, [(i, i ^ step) for i in range(size)])  16.6 us
    pallas_call x3, Pallas kernels, cotangent_products(): pl.pallas_call(functools.partial(cotangent_kernel, count, begin), out_sha...  16.2 us
    ppermute x9, waiting for transfers between devices, hop(): lax.ppermute(array, 'tp', [(2 * i + core, 2 * j + core) for i, j in pairs...  16 us
    pallas_call x1, Pallas kernels, correlate(): pl.pallas_call(functools.partial(backward_kernel, members, per_group, sca...  9.77 us
    pallas_call x1, Pallas kernels, convolve(): pl.pallas_call(functools.partial(forward_kernel, members, per_group, widt...  5.55 us
  transfers between devices with their start and end apart: 31, of which 13 were waited for; matrix products, arithmetic and copies ran while one was open for 0% of the time, Pallas kernels for 46%

profile of v9, /device:TPU:0, one launch (start us, length us, event | category | flops | bytes accessed | tf_op | source)
XLA Modules:
  0.0 151.0 jit_solution(6583730088110577624)
XLA Ops:
  1.2 2.7 %collective-permute-start.4 = (bf16[512,1024]{1,0:T(8,128)(2,1)}, bf16[512,1024]{1,0:T(8,128)(2,1)S(1)}, u32[]{:S(2)}, u32[]{:S(2)}) collective-permute-start(bf16[512,1024]{1,0:T(8,128)(2,1)} %refs_0_.1), channel_id=1, source_target_pairs={{0,2},{1,3},{6,4},{7,5},{2,0},{3,1},{4,6},{5,7},{8,10},{9,11},{14,... | collective-permute-start | bytes 3145736 | tf_op jit(solution)/shard_map/ppermute | solution.py:351
  4.6 2.6 %gated_input.1 = (bf16[544,256]{1,0:T(8,128)(2,1)S(1)}, bf16[544,256]{1,0:T(8,128)(2,1)S(1)}, bf16[544,256]{1,0:T(8,128)(2,1)S(1)}, bf16[544,256]{1,0:T(8,128)(2,1)S(1)}) custom-call(s32[2]{0:T(128)S(1)} %pad_add_fusion.who_ref, bf16[512,1024]{1,0:T(8,128)(2,1)} %refs_4_.3, bf16[512,1024]{1,0:T(8,128)(2,1)} %refs_5_.1, f32[64,512]{1,0:T(8,128)} %bitcast.4), custom_call_target="tpu_custom_call" | custom-call | flops 1048576 | bytes 4096 | tf_op jit(solution)/shard_map/gated_input/pallas_call | solution.py:261
  12.0 5.0 %cotangent_blocks.3.refs_4_.refs_3_ = f32[512,1024]{1,0:T(8,128)S(1)} custom-call(s32[10]{0:T(128)S(1)} %plan.1._.plan_ref, bf16[1024,8192]{1,0:T(8,128)(2,1)} %weight_ref.19, bf16[512,1024]{1,0:T(8,128)(2,1)S(1)} %copy-done.4, bf16[512,1024]{1,0:T(8,128)(2,1)} %collective-permute-done.3.refs_1_), custom_call_target="tpu_custom_call" | custom-call | flops 1048576 | bytes 4096 | tf_op jit(solution)/shard_map/cotangent_blocks/pallas_call | solution.py:596
  17.0 6.2 %collective-permute-done.1.refs_2_ = bf16[544,256]{1,0:T(8,128)(2,1)S(1)} collective-permute-done((bf16[544,256]{1,0:T(8,128)(2,1)S(1)}, bf16[544,256]{1,0:T(8,128)(2,1)S(1)}, u32[]{:S(2)}, u32[]{:S(2)}) %collective-permute-start.1) | collective-permute-done | bytes 278560 | tf_op jit(solution)/shard_map/ppermute | solution.py:318
  23.2 5.5 %causal_conv.1 = (bf16[512,256]{1,0:T(8,128)(2,1)S(1)}, bf16[512,256]{1,0:T(8,128)(2,1)S(1)}, bf16[512,256]{1,0:T(8,128)(2,1)S(1)}, bf16[512,256]{1,0:T(8,128)(2,1)S(1)}) custom-call(s32[10]{0:T(128)S(1)} %plan.1._.plan_ref, bf16[544,256]{1,0:T(8,128)(2,1)S(1)} %get-tuple-element.46.refs_0_, bf16[544,256]{1,0:T(8,128)(2,1)S(1)} %collective-permute-done.refs_1_, ...), custom_call_target="tpu_custom_call" | custom-call | flops 1048576 | bytes 4096 | tf_op jit(solution)/shard_map/causal_conv/pallas_call | solution.py:182
  34.5 5.8 %collective-permute-done.6.refs_1_ = bf16[512,256]{1,0:T(8,128)(2,1)S(1)} collective-permute-done((bf16[512,256]{1,0:T(8,128)(2,1)S(1)}, bf16[512,256]{1,0:T(8,128)(2,1)S(1)}, u32[]{:S(2)}, u32[]{:S(2)}) %collective-permute-start.6) | collective-permute-done | bytes 262176 | tf_op jit(solution)/shard_map/ppermute | solution.py:318
  40.3 4.9 %collective-permute-done.7.refs_2_ = bf16[512,256]{1,0:T(8,128)(2,1)S(1)} collective-permute-done((bf16[512,256]{1,0:T(8,128)(2,1)S(1)}, bf16[512,256]{1,0:T(8,128)(2,1)S(1)}, u32[]{:S(2)}, u32[]{:S(2)}) %collective-permute-start.7) | collective-permute-done | bytes 262176 | tf_op jit(solution)/shard_map/ppermute | solution.py:318
  46.0 3.4 %projection_blocks.6 = (bf16[512,512]{1,0:T(8,128)(2,1)S(1)}, bf16[512,512]{1,0:T(8,128)(2,1)S(1)}) custom-call(s32[10]{0:T(128)S(1)} %plan.1._.plan_ref, bf16[512,1024]{1,0:T(8,128)(2,1)S(1)} %get-tuple-element.58.data_ref, bf16[1024,8192]{1,0:T(8,128)(2,1)} %weight_ref.19), custom_call_target="tpu_custom_call" | custom-call | flops 1048576 | bytes 4096 | tf_op jit(solution)/shard_map/projection_blocks/pallas_call | solution.py:506
  52.1 3.5 %projection_blocks.7.refs_3_.end_ref.refs_0_ = bf16[512,1024]{1,0:T(8,128)(2,1)S(1)} custom-call(s32[10]{0:T(128)S(1)} %plan.1._.plan_ref, bf16[512,1024]{1,0:T(8,128)(2,1)S(1)} %get-tuple-element.58.data_ref, bf16[1024,8192]{1,0:T(8,128)(2,1)} %weight_ref.19, bf16[512,512]{1,0:T(8,128)(2,1)S(1)} %collective-permute-done.11.refs_0_, ...), custom_call_target="tpu_custom_call" | custom-call | flops 1048576 | bytes 4096 | tf_op jit(solution)/shard_map/projection_blocks/pallas_call | solution.py:506
  57.6 5.7 %collective-permute-start.17 = (bf16[512,1024]{1,0:T(8,128)(2,1)S(1)}, bf16[512,1024]{1,0:T(8,128)(2,1)S(1)}, u32[]{:S(2)}, u32[]{:S(2)}) collective-permute-start(bf16[512,1024]{1,0:T(8,128)(2,1)S(1)} %chosen.2.refs_0_), channel_id=1, source_target_pairs={{2,0},{3,1},{4,6},{5,7},{0,2},{1,3},{6,4},{7,5},{10,8},{11,9},{12,... | collective-permute-start | bytes 3145736 | tf_op jit(solution)/shard_map/ppermute | solution.py:351
  63.7 3.4 %projection_blocks.8 = (bf16[512,512]{1,0:T(8,128)(2,1)S(1)}, bf16[512,512]{1,0:T(8,128)(2,1)S(1)}) custom-call(s32[10]{0:T(128)S(1)} %plan.1._.plan_ref, bf16[512,1024]{1,0:T(8,128)(2,1)S(1)} %get-tuple-element.58.data_ref, bf16[1024,8192]{1,0:T(8,128)(2,1)} %weight_ref.19, bf16[512,1024]{1,0:T(8,128)(2,1)S(1)} %chosen.2.refs_0_), custom_call_target="tpu_custom_call" | custom-call | flops 1048576 | bytes 4096 | tf_op jit(solution)/shard_map/projection_blocks/pallas_call | solution.py:506
  69.9 3.5 %projection_blocks.9.refs_0_.refs_4_ = bf16[512,1024]{1,0:T(8,128)(2,1)S(1)} custom-call(s32[10]{0:T(128)S(1)} %plan.1._.plan_ref, bf16[512,1024]{1,0:T(8,128)(2,1)S(1)} %get-tuple-element.58.data_ref, bf16[1024,8192]{1,0:T(8,128)(2,1)} %weight_ref.19, bf16[512,512]{1,0:T(8,128)(2,1)S(1)} %collective-permute-done.13.refs_0_, ...), custom_call_target="tpu_custom_call" | custom-call | flops 1048576 | bytes 4096 | tf_op jit(solution)/shard_map/projection_blocks/pallas_call | solution.py:506
  73.4 4.9 %projection_blocks.10 = (bf16[512,1024]{1,0:T(8,128)(2,1)S(1)}, bf16[512,1024]{1,0:T(8,128)(2,1)S(1)}) custom-call(s32[10]{0:T(128)S(1)} %plan.1._.plan_ref, bf16[512,1024]{1,0:T(8,128)(2,1)S(1)} %get-tuple-element.58.data_ref, bf16[1024,8192]{1,0:T(8,128)(2,1)} %weight_ref.19, bf16[512,1024]{1,0:T(8,128)(2,1)S(1)} %projection_blocks.9.refs_0_.refs_4_), custom_call_target="tpu_custom_call" | custom-call | flops 1048576 | bytes 4096 | tf_op jit(solution)/shard_map/projection_blocks/pallas_call | solution.py:506
  78.3 6.4 %cotangent_blocks.4.refs_1_.refs_2_ = f32[512,1024]{1,0:T(8,128)S(1)} custom-call(s32[10]{0:T(128)S(1)} %plan.1._.plan_ref, bf16[1024,8192]{1,0:T(8,128)(2,1)} %weight_ref.19, bf16[512,1024]{1,0:T(8,128)(2,1)S(1)} %get-tuple-element.68.refs_0_, bf16[512,1024]{1,0:T(8,128)(2,1)S(1)} %collective-permute-done.18.refs_1_, bf16[512,1024]{1,0:T(8,128)(2,1)S(1)} %added.5.refs_2_, ...), custom_call_target="tpu_custom_call" | custom-call | flops 1048576 | bytes 4096 | tf_op jit(solution)/shard_map/cotangent_blocks/pallas_call | solution.py:596
  84.7 2.3 %collective-permute-done.17.refs_0_ = bf16[512,1024]{1,0:T(8,128)(2,1)S(1)} collective-permute-done((bf16[512,1024]{1,0:T(8,128)(2,1)S(1)}, bf16[512,1024]{1,0:T(8,128)(2,1)S(1)}, u32[]{:S(2)}, u32[]{:S(2)}) %collective-permute-start.17) | collective-permute-done | bytes 1048608 | tf_op jit(solution)/shard_map/ppermute | solution.py:351
  88.6 3.7 %collective-permute-start.22 = (bf16[512,1024]{1,0:T(8,128)(2,1)S(1)}, bf16[512,1024]{1,0:T(8,128)(2,1)S(1)}, u32[]{:S(2)}, u32[]{:S(2)}) collective-permute-start(bf16[512,1024]{1,0:T(8,128)(2,1)S(1)} %held.8.refs_0_), channel_id=1, source_target_pairs={{0,2},{1,3},{6,4},{7,5},{8,10},{9,11},{14,12},{15,13},{16,18},{17,... | collective-permute-start | bytes 3145736 | tf_op jit(solution)/shard_map/ppermute | solution.py:351
  93.0 4.8 %cotangent_blocks.5.start_ref = f32[512,1024]{1,0:T(8,128)S(1)} custom-call(s32[10]{0:T(128)S(1)} %plan.1._.plan_ref, bf16[1024,8192]{1,0:T(8,128)(2,1)} %weight_ref.19, bf16[512,1024]{1,0:T(8,128)(2,1)S(1)} %collective-permute-done.20.refs_0_, bf16[512,1024]{1,0:T(8,128)(2,1)S(1)} %chosen.3.refs_1_, f32[512,1024]{1,0:T(8,128)S(1)} %cotangent_blocks.4.refs_1_.refs_2_, ...), custom_call_target="tpu_custom_call" | custom-call | flops 1048576 | bytes 4096 | tf_op jit(solution)/shard_map/cotangent_blocks/pallas_call | solution.py:596
  97.8 5.2 %cotangent_last.1 = (bf16[512,1024]{1,0:T(8,128)(2,1)}, bf16[512,256]{1,0:T(8,128)(2,1)S(1)}, bf16[512,256]{1,0:T(8,128)(2,1)S(1)}, bf16[512,256]{1,0:T(8,128)(2,1)S(1)}, bf16[512,256]{1,0:T(8,128)(2,1)S(1)}) custom-call(s32[10]{0:T(128)S(1)} %plan.1._.plan_ref, bf16[1024,8192]{1,0:T(8,128)(2,1)} %weight_ref.19, ...), custom_call_target="tpu_custom_call" | custom-call | flops 1048576 | bytes 4096 | tf_op jit(solution)/shard_map/cotangent_last/pallas_call | solution.py:564
  106.6 5.1 %projection_blocks.11 = (bf16[512,1024]{1,0:T(8,128)(2,1)S(1)}, bf16[512,1024]{1,0:T(8,128)(2,1)S(1)}) custom-call(s32[10]{0:T(128)S(1)} %plan.1._.plan_ref, bf16[512,1024]{1,0:T(8,128)(2,1)S(1)} %get-tuple-element.58.data_ref, bf16[1024,8192]{1,0:T(8,128)(2,1)} %weight_ref.19, bf16[512,1024]{1,0:T(8,128)(2,1)S(1)} %collective-permute-done.15.refs_0_, ...), custom_call_target="tpu_custom_call" | custom-call | flops 1048576 | bytes 4096 | tf_op jit(solution)/shard_map/projection_blocks/pallas_call | solution.py:506
  111.7 3.5 %collective-permute-done.22.refs_1_ = bf16[512,1024]{1,0:T(8,128)(2,1)S(1)} collective-permute-done((bf16[512,1024]{1,0:T(8,128)(2,1)S(1)}, bf16[512,1024]{1,0:T(8,128)(2,1)S(1)}, u32[]{:S(2)}, u32[]{:S(2)}) %collective-permute-start.22) | collective-permute-done | bytes 1048608 | tf_op jit(solution)/shard_map/ppermute | solution.py:351
  119.6 3.8 %collective-permute-start.26 = (bf16[512,1024]{1,0:T(8,128)(2,1)S(1)}, bf16[512,1024]{1,0:T(8,128)(2,1)S(1)}, u32[]{:S(2)}, u32[]{:S(2)}) collective-permute-start(bf16[512,1024]{1,0:T(8,128)(2,1)S(1)} %added.7.refs_8_), channel_id=1, source_target_pairs={{2,0},{3,1},{4,6},{5,7},{0,2},{1,3},{6,4},{7,5},{10,8},{11,9},{12,... | collective-permute-start | bytes 3145736 | tf_op jit(solution)/shard_map/ppermute | solution.py:351
  123.3 9.8 %causal_conv_grads.1 = (bf16[544,256]{1,0:T(8,128)(2,1)S(1)}, bf16[544,256]{1,0:T(8,128)(2,1)S(1)}, bf16[544,256]{1,0:T(8,128)(2,1)S(1)}, bf16[544,256]{1,0:T(8,128)(2,1)S(1)}) custom-call(s32[10]{0:T(128)S(1)} %plan.1._.plan_ref, bf16[544,256]{1,0:T(8,128)(2,1)S(1)} %get-tuple-element.46.refs_0_, bf16[544,256]{1,0:T(8,128)(2,1)S(1)} %collective-permute-done.refs_1_, ...), custom_call_target="tpu_custom_call" | custom-call | flops 1048576 | bytes 4096 | tf_op jit(solution)/shard_map/causal_conv_grads/pallas_call | solution.py:203
  136.7 9.0 %collective-permute-done.26.refs_1_ = bf16[512,1024]{1,0:T(8,128)(2,1)S(1)} collective-permute-done((bf16[512,1024]{1,0:T(8,128)(2,1)S(1)}, bf16[512,1024]{1,0:T(8,128)(2,1)S(1)}, u32[]{:S(2)}, u32[]{:S(2)}) %collective-permute-start.26) | collective-permute-done | bytes 1048608 | tf_op jit(solution)/shard_map/ppermute | solution.py:351
  148.7 2.3 %input_gradients.1 = (bf16[512,1024]{1,0:T(8,128)(2,1)}, bf16[512,1024]{1,0:T(8,128)(2,1)}, f32[64,512]{1,0:T(8,128)}) custom-call(s32[10]{0:T(128)S(1)} %plan.1._.plan_ref, bf16[544,256]{1,0:T(8,128)(2,1)S(1)} %get-tuple-element.80.refs_0_, bf16[544,256]{1,0:T(8,128)(2,1)S(1)} %collective-permute-done.28.refs_1_, ...), custom_call_target="tpu_custom_call" | custom-call | flops 1048576 | bytes 4096 | tf_op jit(solution)/shard_map/input_gradients/pallas_call | solution.py:304
  (77 shorter events, 37.2 us)
Async XLA Ops:
  1.2 27.6 %collective-permute-start.4 = (bf16[512,1024]{1,0:T(8,128)(2,1)}, bf16[512,1024]{1,0:T(8,128)(2,1)S(1)}, u32[]{:S(2)}, u32[]{:S(2)}) collective-permute-start(bf16[512,1024]{1,0:T(8,128)(2,1)} %refs_0_.1), channel_id=1, source_target_pairs={{0,2},{1,3},{6,4},{7,5},{2,0},{3,1},{4,6},{5,7},{8,10},{9,11},{14,... | collective-permute-start | bytes 3145736 | tf_op jit(solution)/shard_map/ppermute | solution.py:351
  3.8 25.0 %collective-permute-start.5 = (bf16[512,1024]{1,0:T(8,128)(2,1)}, bf16[512,1024]{1,0:T(8,128)(2,1)S(1)}, u32[]{:S(2)}, u32[]{:S(2)}) collective-permute-start(bf16[512,1024]{1,0:T(8,128)(2,1)} %refs_0_.1), channel_id=1, source_target_pairs={{2,4},{3,5},{4,2},{5,3},{10,12},{11,13},{12,10},{13,11},{18,20},{1... | collective-permute-start | bytes 3145736 | tf_op jit(solution)/shard_map/ppermute | solution.py:351
  8.8 14.4 %collective-permute-start.1 = (bf16[544,256]{1,0:T(8,128)(2,1)S(1)}, bf16[544,256]{1,0:T(8,128)(2,1)S(1)}, u32[]{:S(2)}, u32[]{:S(2)}) collective-permute-start(bf16[544,256]{1,0:T(8,128)(2,1)S(1)} %get-tuple-element.48), channel_id=1, source_target_pairs={{0,16},{8,24},{16,0},{24,8},{1,17},{9,25},{17,1},{25,9},{2,18},{10... | collective-permute-start | bytes 835592 | tf_op jit(solution)/shard_map/ppermute | solution.py:318
  10.3 12.9 %collective-permute-start.2 = (bf16[544,256]{1,0:T(8,128)(2,1)S(1)}, bf16[544,256]{1,0:T(8,128)(2,1)S(1)}, u32[]{:S(2)}, u32[]{:S(2)}) collective-permute-start(bf16[544,256]{1,0:T(8,128)(2,1)S(1)} %get-tuple-element.49), channel_id=1, source_target_pairs={{0,24},{8,16},{16,8},{24,0},{1,25},{9,17},{17,9},{25,1},{2,26},{10... | collective-permute-start | bytes 835592 | tf_op jit(solution)/shard_map/ppermute | solution.py:318
  28.8 28.0 %collective-permute-start.10 = (bf16[512,1024]{1,0:T(8,128)(2,1)S(1)}, bf16[512,1024]{1,0:T(8,128)(2,1)S(1)}, u32[]{:S(2)}, u32[]{:S(2)}) collective-permute-start(bf16[512,1024]{1,0:T(8,128)(2,1)S(1)} %get-tuple-element.60.refs_0_), channel_id=1, source_target_pairs={{2,0},{3,1},{4,6},{5,7},{10,8},{11,9},{12,14},{13,15},{18,16},{19,... | collective-permute-start | bytes 3145736 | tf_op jit(solution)/shard_map/ppermute | solution.py:351
  30.3 26.5 %collective-permute-start.9 = (bf16[512,1024]{1,0:T(8,128)(2,1)S(1)}, bf16[512,1024]{1,0:T(8,128)(2,1)S(1)}, u32[]{:S(2)}, u32[]{:S(2)}) collective-permute-start(bf16[512,1024]{1,0:T(8,128)(2,1)S(1)} %get-tuple-element.59.refs_2_), channel_id=1, source_target_pairs={{2,4},{3,5},{4,2},{5,3},{10,12},{11,13},{12,10},{13,11},{18,20},{1... | collective-permute-start | bytes 3145736 | tf_op jit(solution)/shard_map/ppermute | solution.py:351
  32.3 12.9 %collective-permute-start.7 = (bf16[512,256]{1,0:T(8,128)(2,1)S(1)}, bf16[512,256]{1,0:T(8,128)(2,1)S(1)}, u32[]{:S(2)}, u32[]{:S(2)}) collective-permute-start(bf16[512,256]{1,0:T(8,128)(2,1)S(1)} %get-tuple-element.56), channel_id=1, source_target_pairs={{0,16},{8,24},{16,0},{24,8},{1,17},{9,25},{17,1},{25,9},{2,18},{10... | collective-permute-start | bytes 786440 | tf_op jit(solution)/shard_map/ppermute | solution.py:318
  33.2 12.0 %collective-permute-start.8 = (bf16[512,256]{1,0:T(8,128)(2,1)S(1)}, bf16[512,256]{1,0:T(8,128)(2,1)S(1)}, u32[]{:S(2)}, u32[]{:S(2)}) collective-permute-start(bf16[512,256]{1,0:T(8,128)(2,1)S(1)} %get-tuple-element.57), channel_id=1, source_target_pairs={{0,24},{8,16},{16,8},{24,0},{1,25},{9,17},{17,9},{25,1},{2,26},{10... | collective-permute-start | bytes 786440 | tf_op jit(solution)/shard_map/ppermute | solution.py:318
  56.8 21.5 %collective-permute-start.18 = (bf16[512,1024]{1,0:T(8,128)(2,1)S(1)}, bf16[512,1024]{1,0:T(8,128)(2,1)S(1)}, u32[]{:S(2)}, u32[]{:S(2)}) collective-permute-start(bf16[512,1024]{1,0:T(8,128)(2,1)S(1)} %get-tuple-element.68.refs_0_), channel_id=1, source_target_pairs={{0,1},{1,0},{2,3},{3,2},{4,5},{5,4},{6,7},{7,6},{8,9},{9,8},{10,11... | collective-permute-start | bytes 3145736 | tf_op jit(solution)/shard_map/ppermute | solution.py:318
  57.6 29.4 %collective-permute-start.17 = (bf16[512,1024]{1,0:T(8,128)(2,1)S(1)}, bf16[512,1024]{1,0:T(8,128)(2,1)S(1)}, u32[]{:S(2)}, u32[]{:S(2)}) collective-permute-start(bf16[512,1024]{1,0:T(8,128)(2,1)S(1)} %chosen.2.refs_0_), channel_id=1, source_target_pairs={{2,0},{3,1},{4,6},{5,7},{0,2},{1,3},{6,4},{7,5},{10,8},{11,9},{12,... | collective-permute-start | bytes 3145736 | tf_op jit(solution)/shard_map/ppermute | solution.py:351
  63.6 28.7 %collective-permute-start.20 = (bf16[512,1024]{1,0:T(8,128)(2,1)S(1)}, bf16[512,1024]{1,0:T(8,128)(2,1)S(1)}, u32[]{:S(2)}, u32[]{:S(2)}) collective-permute-start(bf16[512,1024]{1,0:T(8,128)(2,1)S(1)} %added.5.refs_2_), channel_id=1, source_target_pairs={{0,1},{1,0},{2,3},{3,2},{4,5},{5,4},{6,7},{7,6},{8,9},{9,8},{10,11... | collective-permute-start | bytes 3145736 | tf_op jit(solution)/shard_map/ppermute | solution.py:318
  87.9 9.9 %collective-permute-start.19 = (bf16[512,1024]{1,0:T(8,128)(2,1)S(1)}, bf16[512,1024]{1,0:T(8,128)(2,1)S(1)}, u32[]{:S(2)}, u32[]{:S(2)}) collective-permute-start(bf16[512,1024]{1,0:T(8,128)(2,1)S(1)} %chosen.3.refs_1_), channel_id=1, source_target_pairs={{0,1},{1,0},{2,3},{3,2},{4,5},{5,4},{6,7},{7,6},{8,9},{9,8},{10,11... | collective-permute-start | bytes 3145736 | tf_op jit(solution)/shard_map/ppermute | solution.py:318
  88.0 16.3 %collective-permute-start.15 = (bf16[512,1024]{1,0:T(8,128)(2,1)S(1)}, bf16[512,1024]{1,0:T(8,128)(2,1)S(1)}, u32[]{:S(2)}, u32[]{:S(2)}) collective-permute-start(bf16[512,1024]{1,0:T(8,128)(2,1)S(1)} %get-tuple-element.66.refs_2_), channel_id=1, source_target_pairs={{0,1},{1,0},{2,3},{3,2},{4,5},{5,4},{6,7},{7,6},{8,9},{9,8},{10,11... | collective-permute-start | bytes 3145736 | tf_op jit(solution)/shard_map/ppermute | solution.py:318
  88.5 16.7 %collective-permute-start.16 = (bf16[512,1024]{1,0:T(8,128)(2,1)S(1)}, bf16[512,1024]{1,0:T(8,128)(2,1)S(1)}, u32[]{:S(2)}, u32[]{:S(2)}) collective-permute-start(bf16[512,1024]{1,0:T(8,128)(2,1)S(1)} %get-tuple-element.67), channel_id=1, source_target_pairs={{0,1},{1,0},{2,3},{3,2},{4,5},{5,4},{6,7},{7,6},{8,9},{9,8},{10,11... | collective-permute-start | bytes 3145736 | tf_op jit(solution)/shard_map/ppermute | solution.py:318
  88.6 26.7 %collective-permute-start.22 = (bf16[512,1024]{1,0:T(8,128)(2,1)S(1)}, bf16[512,1024]{1,0:T(8,128)(2,1)S(1)}, u32[]{:S(2)}, u32[]{:S(2)}) collective-permute-start(bf16[512,1024]{1,0:T(8,128)(2,1)S(1)} %held.8.refs_0_), channel_id=1, source_target_pairs={{0,2},{1,3},{6,4},{7,5},{8,10},{9,11},{14,12},{15,13},{16,18},{17,... | collective-permute-start | bytes 3145736 | tf_op jit(solution)/shard_map/ppermute | solution.py:351
  92.3 22.9 %collective-permute-start.21 = (bf16[512,1024]{1,0:T(8,128)(2,1)S(1)}, bf16[512,1024]{1,0:T(8,128)(2,1)S(1)}, u32[]{:S(2)}, u32[]{:S(2)}) collective-permute-start(bf16[512,1024]{1,0:T(8,128)(2,1)S(1)} %added.6.refs_0_.refs_3_), channel_id=1, source_target_pairs={{2,4},{3,5},{4,2},{5,3},{10,12},{11,13},{12,10},{13,11},{18,20},{1... | collective-permute-start | bytes 3145736 | tf_op jit(solution)/shard_map/ppermute | solution.py:351
  103.1 12.2 %collective-permute-start.23 = (bf16[512,256]{1,0:T(8,128)(2,1)S(1)}, bf16[512,256]{1,0:T(8,128)(2,1)S(1)}, u32[]{:S(2)}, u32[]{:S(2)}) collective-permute-start(bf16[512,256]{1,0:T(8,128)(2,1)S(1)} %get-tuple-element.74), channel_id=1, source_target_pairs={{0,8},{8,0},{16,24},{24,16},{1,9},{9,1},{17,25},{25,17},{2,10},{10... | collective-permute-start | bytes 786440 | tf_op jit(solution)/shard_map/ppermute | solution.py:318
  104.3 12.1 %collective-permute-start.24 = (bf16[512,256]{1,0:T(8,128)(2,1)S(1)}, bf16[512,256]{1,0:T(8,128)(2,1)S(1)}, u32[]{:S(2)}, u32[]{:S(2)}) collective-permute-start(bf16[512,256]{1,0:T(8,128)(2,1)S(1)} %get-tuple-element.75), channel_id=1, source_target_pairs={{0,16},{8,24},{16,0},{24,8},{1,17},{9,25},{17,1},{25,9},{2,18},{10... | collective-permute-start | bytes 786440 | tf_op jit(solution)/shard_map/ppermute | solution.py:318
  105.1 12.9 %collective-permute-start.25 = (bf16[512,256]{1,0:T(8,128)(2,1)S(1)}, bf16[512,256]{1,0:T(8,128)(2,1)S(1)}, u32[]{:S(2)}, u32[]{:S(2)}) collective-permute-start(bf16[512,256]{1,0:T(8,128)(2,1)S(1)} %get-tuple-element.76), channel_id=1, source_target_pairs={{0,24},{8,16},{16,8},{24,0},{1,25},{9,17},{17,9},{25,1},{2,26},{10... | collective-permute-start | bytes 786440 | tf_op jit(solution)/shard_map/ppermute | solution.py:318
  118.3 18.4 %collective-permute-start.27 = (bf16[512,1024]{1,0:T(8,128)(2,1)S(1)}, bf16[512,1024]{1,0:T(8,128)(2,1)S(1)}, u32[]{:S(2)}, u32[]{:S(2)}) collective-permute-start(bf16[512,1024]{1,0:T(8,128)(2,1)S(1)} %added.8.refs_9_), channel_id=1, source_target_pairs={{2,4},{3,5},{4,2},{5,3},{10,12},{11,13},{12,10},{13,11},{18,20},{1... | collective-permute-start | bytes 3145736 | tf_op jit(solution)/shard_map/ppermute | solution.py:351
  119.6 26.1 %collective-permute-start.26 = (bf16[512,1024]{1,0:T(8,128)(2,1)S(1)}, bf16[512,1024]{1,0:T(8,128)(2,1)S(1)}, u32[]{:S(2)}, u32[]{:S(2)}) collective-permute-start(bf16[512,1024]{1,0:T(8,128)(2,1)S(1)} %added.7.refs_8_), channel_id=1, source_target_pairs={{2,0},{3,1},{4,6},{5,7},{0,2},{1,3},{6,4},{7,5},{10,8},{11,9},{12,... | collective-permute-start | bytes 3145736 | tf_op jit(solution)/shard_map/ppermute | solution.py:351
  133.1 14.3 %collective-permute-start.28 = (bf16[544,256]{1,0:T(8,128)(2,1)S(1)}, bf16[544,256]{1,0:T(8,128)(2,1)S(1)}, u32[]{:S(2)}, u32[]{:S(2)}) collective-permute-start(bf16[544,256]{1,0:T(8,128)(2,1)S(1)} %get-tuple-element.81), channel_id=1, source_target_pairs={{0,8},{8,0},{16,24},{24,16},{1,9},{9,1},{17,25},{25,17},{2,10},{10... | collective-permute-start | bytes 835592 | tf_op jit(solution)/shard_map/ppermute | solution.py:318
  134.0 13.4 %collective-permute-start.29 = (bf16[544,256]{1,0:T(8,128)(2,1)S(1)}, bf16[544,256]{1,0:T(8,128)(2,1)S(1)}, u32[]{:S(2)}, u32[]{:S(2)}) collective-permute-start(bf16[544,256]{1,0:T(8,128)(2,1)S(1)} %get-tuple-element.82), channel_id=1, source_target_pairs={{0,16},{8,24},{16,0},{24,8},{1,17},{9,25},{17,1},{25,9},{2,18},{10... | collective-permute-start | bytes 835592 | tf_op jit(solution)/shard_map/ppermute | solution.py:318
  135.5 11.9 %collective-permute-start.30 = (bf16[544,256]{1,0:T(8,128)(2,1)S(1)}, bf16[544,256]{1,0:T(8,128)(2,1)S(1)}, u32[]{:S(2)}, u32[]{:S(2)}) collective-permute-start(bf16[544,256]{1,0:T(8,128)(2,1)S(1)} %get-tuple-element.83), channel_id=1, source_target_pairs={{0,24},{8,16},{16,8},{24,0},{1,25},{9,17},{17,9},{25,1},{2,26},{10... | collective-permute-start | bytes 835592 | tf_op jit(solution)/shard_map/ppermute | solution.py:318
  (12 other events, 70.2 us)

commit v10 on v9

--- a/solution.py
+++ b/solution.py
@@ -405,23 +405,53 @@
     )(*values, *after)
 
 
-def add_kernel(*refs):
-    refs[-1][...] = sum(wide(ref[...]) for ref in refs[:-1]).astype(jnp.bfloat16)
-
-
-def added(*arrays):
+def add_kernel(count, *refs):
+    total = sum(wide(ref[...]) for ref in refs[:count])
+    if len(refs) > count + 1:
+        halves = [wide(ref[...]) for ref in refs[count:-1]]
+        total = total + jnp.concatenate(halves, axis=1)
+    refs[-1][...] = total.astype(jnp.bfloat16)
+
+
+def added(*arrays, halves=()):
     rows, width = arrays[0].shape
     part = pl.BlockSpec((rows // 4, width), lambda i: (i, 0))
-    return pl.pallas_call(
-        add_kernel,
+    half = pl.BlockSpec((rows // 4, width // 2), lambda i: (i, 0))
+    return pl.pallas_call(
+        functools.partial(add_kernel, len(arrays)),
         out_shape=jax.ShapeDtypeStruct((rows, width), jnp.bfloat16),
         grid=(4,),
-        in_specs=[part] * len(arrays),
+        in_specs=[part] * len(arrays) + [half] * len(halves),
         out_specs=part,
         compiler_params=pltpu.CompilerParams(vmem_limit_bytes=8 * 2**20),
         cost_estimate=COST,
         name="added",
-    )(*arrays)
+    )(*arrays, *halves)
+
+
+def passing_kernel(plan_ref, first_ref, arrived_ref, second_ref, *refs):
+    out_ref = refs[-1]
+    in_middle = plan_ref[IN_MIDDLE] == 1
+
+    @pl.when(in_middle)
+    def _():
+        out_ref[...] = (wide(first_ref[...]) + wide(arrived_ref[...])).astype(jnp.bfloat16)
+
+    @pl.when(jnp.logical_not(in_middle))
+    def _():
+        out_ref[...] = second_ref[...]
+
+
+def passing(plan, first, arrived, second, after):
+    return pl.pallas_call(
+        passing_kernel,
+        out_shape=jax.ShapeDtypeStruct(first.shape, first.dtype),
+        in_specs=[SMEM] + [VMEM] * 3 + [ANYWHERE] * len(after),
+        out_specs=VMEM,
+        compiler_params=pltpu.CompilerParams(vmem_limit_bytes=4 * 2**20),
+        cost_estimate=COST,
+        name="passing",
+    )(plan, first, arrived, second, *after)
 
 
 def choice_kernel(plan_ref, middle_ref, end_ref, *refs):
@@ -474,45 +504,56 @@
     )(plan, *parts, query_gate)
 
 
-def product_kernel(steps, joins, extra, _, data_ref, weight_ref, *refs):
-    more, outputs = refs[:extra], refs[-(steps // joins) :]
+def spans(widths, start, stop):
+    found, begin = [], 0
+    for number, width in enumerate(widths):
+        low, high = max(start, begin), min(stop, begin + width)
+        if low < high:
+            found.append((number, slice(low - begin, high - begin), slice(low - start, high - start)))
+        begin += width
+    return found
+
+
+def product_kernel(steps, more_widths, out_widths, _, data_ref, weight_ref, *refs):
+    more, outputs = refs[: len(more_widths)], refs[-len(out_widths) :]
     product = jnp.dot(data_ref[...], weight_ref[...], preferred_element_type=jnp.float32)
-    for number in range(steps):
-        out_ref = outputs[number // joins]
-        wide_out = out_ref.shape[1] > product.shape[1]
-
-        @pl.when(pl.program_id(0) == number)
-        def _(number=number, out_ref=out_ref, wide_out=wide_out):
-            total = product + wide(more[number][...]) if more else product
-            if wide_out:
-                width = product.shape[1]
-                at = number % joins * width
-                out_ref[:, at : at + width] = total.astype(jnp.bfloat16)
-            else:
-                out_ref[...] = total.astype(jnp.bfloat16)
+    width = product.shape[1]
+    for step in range(steps):
+        start, stop = step * width, (step + 1) * width
+
+        @pl.when(pl.program_id(0) == step)
+        def _(start=start, stop=stop):
+            total = product
+            if more:
+                parts = [wide(more[n][:, there]) for n, there, _ in spans(more_widths, start, stop)]
+                total = total + jnp.concatenate(parts, axis=1)
+            total = total.astype(jnp.bfloat16)
+            for n, there, here in spans(out_widths, start, stop):
+                outputs[n][:, there] = total[:, here]
 
 
 def column_products(
-    plan, data, out_weight, first, count, other, more=(), after=(), tiles=1, joins=1
+    plan, data, out_weight, first, count, other, more=(), after=(), tiles=1, widths=()
 ):
     rows, depth = data.shape
     width = data.shape[1]
     tile = width // tiles
     steps = count * tiles
+    widths = tuple(widths) or (width,) * count
 
     def weights(i, at):
         return 0, at[2 * (first - i // tiles) + other] * tiles + i % tiles
 
     return pl.pallas_call(
-        functools.partial(product_kernel, steps, joins, len(more)),
-        out_shape=[jax.ShapeDtypeStruct((rows, tile * joins), jnp.bfloat16)] * (steps // joins),
+        functools.partial(product_kernel, steps, [part.shape[1] for part in more], widths),
+        out_shape=[jax.ShapeDtypeStruct((rows, part), jnp.bfloat16) for part in widths],
         grid_spec=pltpu.PrefetchScalarGridSpec(
             num_scalar_prefetch=1,
             grid=(steps,),
             in_specs=[VMEM, pl.BlockSpec((depth, tile), weights)]
             + [VMEM] * len(more)
             + [ANYWHERE] * len(after),
-            out_specs=[VMEM] * (steps // joins),
+            out_specs=[VMEM] * len(widths),
         ),
         compiler_params=pltpu.CompilerParams(vmem_limit_bytes=16 * 2**20),
         cost_estimate=COST,
@@ -539,48 +580,57 @@
 
 
 def last_cotangent_kernel(
-    members, _, weight_ref, block_ref, start_ref, conv_ref, query_ref, grad_ref, *parts
+    members, plan_ref, weight_ref, block_ref, start_ref, conv_ref, query_ref, *refs
 ):
+    parts, cot_scr = refs[-1 - members : -1], refs[-1]
+    grad_ref = refs[-2 - members]
     product = lax.dot_general(
         block_ref[...], weight_ref[...], NT, preferred_element_type=jnp.float32
     )
     dgated = wide((start_ref[...] + product).astype(jnp.bfloat16))
     grad_ref[...] = (dgated * wide(conv_ref[...])).astype(jnp.bfloat16)
-    cotangent = (dgated * wide(query_ref[...])).astype(jnp.bfloat16)
-    for step in range(members):
-
-        @pl.when(pl.program_id(0) == step)
+    cot_scr[...] = (dgated * wide(query_ref[...])).astype(jnp.bfloat16)
+    share = parts[0].shape[1]
+    odd = plan_ref[POSITION] % 2
+    for step in range(0, members, 2):
+
+        @pl.when(pl.program_id(0) == step // 2)
         def _(step=step):
-            parts[step][...] = cotangent
-
-
-def last_cotangents(plan, first, block, out_weight, start, convolved, query_gate, members):
+            parts[step][...] = cot_scr[:, pl.ds(pl.multiple_of(odd * share, share), share)]
+            parts[step + 1][...] = cot_scr[
+                :, pl.ds(pl.multiple_of((1 - odd) * share, share), share)
+            ]
+
+
+def last_cotangents(
+    plan, first, block, out_weight, start, convolved, query_gate, members, after
+):
     rows, width = block.shape
     channels = out_weight.shape[0]
     share = channels // members
-    piece = pl.BlockSpec((rows, share), lambda i, at: (0, at[POSITION] ^ i))
-    whole = pl.BlockSpec((rows, width), lambda i, at: (0, 0))
-    part = pl.BlockSpec((rows, share), lambda i, at: (0, 0))
+    pair = pl.BlockSpec((rows, 2 * share), lambda i, at: (0, at[POSITION] // 2 ^ i))
     return pl.pallas_call(
         functools.partial(last_cotangent_kernel, members),
         out_shape=[jax.ShapeDtypeStruct((rows, channels), jnp.bfloat16)]
         + [jax.ShapeDtypeStruct((rows, share), jnp.bfloat16)] * members,
         grid_spec=pltpu.PrefetchScalarGridSpec(
             num_scalar_prefetch=1,
-            grid=(members,),
+            grid=(members // 2,),
             in_specs=[
-                pl.BlockSpec((share, width), lambda i, at: (at[POSITION] ^ i, at[first])),
-                whole,
-                piece,
-                piece,
-                piece,
-            ],
-            out_specs=[piece] + [part] * members,
+                pl.BlockSpec((2 * share, width), lambda i, at: (at[POSITION] // 2 ^ i, at[first])),
+                VMEM,
+                pair,
+                pair,
+                pair,
+            ]
+            + [ANYWHERE] * len(after),
+            out_specs=[pair] + [VMEM] * members,
+            scratch_shapes=[pltpu.VMEM((rows, 2 * share), jnp.bfloat16)],
         ),
-        compiler_params=pltpu.CompilerParams(vmem_limit_bytes=16 * 2**20),
+        compiler_params=pltpu.CompilerParams(vmem_limit_bytes=24 * 2**20),
         cost_estimate=COST,
         name="cotangent_last",
-    )(plan, in_hbm(out_weight), block, start, convolved, query_gate)
+    )(plan, in_hbm(out_weight), block, start, convolved, query_gate, *after)
 
 
 def both(blocks):
@@ -664,46 +714,44 @@
     far, skip = hop(near, ACROSS), hop(cross, OUTWARD)
     gated_out, convolved = gated(plan, traded(conv_parts, "ctx"), query_gate)
 
-    def product(first, count, other, more=(), after=(), tiles=1, joins=1):
+    def product(first, count, other, more=(), after=(), tiles=1, widths=()):
         return column_products(
-            plan, gated_out, out_weight, first, count, other, more, after, tiles, joins
+            plan, gated_out, out_weight, first, count, other, more, after, tiles, widths
         )
 
-    given_far = product(FAR, 1, 1, tiles=2)
-    received = [swapped(part, "tp", 1) for part in given_far]
-    (first,) = product(FAR, 1, 0, received, tiles=2, joins=2)
+    third_part = 2 * channels // 3 // 128 * 128
+    widths = (2 * channels - 2 * third_part, third_part, third_part)
+    given = product(FAR, 2, 1, tiles=2, widths=widths)
+    received = [swapped(part, "tp", 1) for part in given]
+    first, second = product(FAR, 2, 0, received, tiles=2)
     far, skip, near = held_until([far, skip, near], (first,))
     mixed = chosen(plan, far, first)
     arrived = hop(mixed, OUTWARD + INWARD)
-    given_middle = product(MIDDLE, 1, 1, (), (mixed,), tiles=2)
-    received = [swapped(part, "tp", 1) for part in given_middle]
-    (second,) = product(MIDDLE, 1, 0, received, tiles=2, joins=2)
+    beside = hop(second, ACROSS)
     middle_block = added(cross, skip)
     blocks = [near, swapped(near, "tp", 1), middle_block]
-    total = cotangent_products(plan, 2 * NEAR, blocks, out_weight, total, after=(second,))
-    given_near, given_own = product(NEAR, 2, 1, (), (second,))
-    (arrived,) = held_until([arrived], (total, given_near))
-    through = added(first, arrived)
-    two_a = hop(through, ACROSS)
-    (second,) = held_until([second], (arrived,))
-    two_b = hop(second, INWARD)
-
-    far_block, far_other = both([chosen(plan, far, arrived, (through,))])
+    total = cotangent_products(plan, 2 * NEAR, blocks, out_weight, total, after=(mixed,))
+    given = product(NEAR, 2, 1, (), (mixed,))
+    (arrived,) = held_until([arrived], (total, given[0]))
+    passed = passing(plan, first, arrived, second, (beside,))
+    jumped = hop(passed, ((0, 2), (1, 3), (2, 0), (3, 1)))
+
+    far_block, far_other = both([chosen(plan, far, arrived, (passed,))])
     blocks = [swapped(middle_block, "tp", 1), far_block]
     total = cotangent_products(
-        plan, 2 * MIDDLE + 1, blocks, out_weight, total, after=(through,)
-    )
+        plan, 2 * MIDDLE + 1, blocks, out_weight, total, after=(passed,)
+    )
+    received = [swapped(part, "tp", 1) for part in given]
     grad_query, *grad_parts = last_cotangents(
-        plan, 2 * FAR + 1, far_other, out_weight, total, convolved, query_gate, members
-    )
-    received = (swapped(given_near, "tp", 1), swapped(given_own, "tp", 1))
-    third, own = product(NEAR, 2, 0, received, (grad_parts[0],))
+        plan, 2 * FAR + 1, far_other, out_weight, total, convolved, query_gate, members, received
+    )
+    widths = (channels // 2, channels // 2, channels)
+    *halves, own = product(NEAR, 2, 0, received, (grad_parts[0],), widths=widths)
+    halves_near = [hop(half, INWARD + OUTWARD) for half in halves]
     grad_parts = traded(grad_parts, "ctx")
-
-    two_a, two_b = held_until([two_a, two_b], tuple(grad_parts[1:]))
-    third, second = added(third, two_a), added(second, two_b)
-    back_parts = correlate(plan, input_parts, grad_parts, per_group, scale, (third, second))
-    projected = added(own, hop(third, OUTWARD + INWARD), hop(second, ACROSS))
+    back_parts = correlate(plan, input_parts, grad_parts, per_group, scale, (own,))
+    back_parts = held_until(back_parts, (halves_near[0],))
+    projected = added(own, beside, jumped, halves=halves_near)
     back_parts = traded(back_parts, "ctx")
     return projected, grad_query, *finished(plan, back_parts, key_gate, value_input, groups, (projected,))
 

time: 152 us -> 163 us (1.072)
  waiting for transfers between devices: 40 us -> 58.4 us
  Pallas kernels: 71.8 us -> 68.3 us
  starting transfers between devices: 36.9 us -> 33.4 us
    ppermute x9, waiting for transfers between devices: 16 us -> 28.8 us  [hop(): lax.ppermute(array, 'tp', [(2 * i + core, 2 * j + core) for i, j in pairs...]
    ppermute x22 -> x21, waiting for transfers between devices: 24 us -> 29.6 us  [swapped(): return lax.ppermute(array, axis, [(i, i ^ step) for i in range(size)])]
    ppermute x9, starting transfers between devices: 20.3 us -> 17.2 us  [hop(): lax.ppermute(array, 'tp', [(2 * i + core, 2 * j + core) for i, j in pairs...]
    pallas_call x11 -> x7, Pallas kernels: 26.6 us -> 24.1 us  [the longest x4 21.2 us: column_products(): pl.pallas_call(functools.partial(product_kernel, steps, [part.shape[1] fo...]
    ppermute x22 -> x21, starting transfers between devices: 16.6 us -> 16.2 us  [swapped(): return lax.ppermute(array, axis, [(i, i ^ step) for i in range(size)])]
  transfers between devices with their start and end apart: 31 -> 30, of which waited for: 13 -> 14; matrix products, arithmetic and copies ran while one was open for 0% -> 0% of each run, Pallas kernels for 46% -> 41%
where the time goes in v10:
time: 163 us; the launch traced here: 162 us
  Pallas kernels  68.3 us (42%)
  waiting for transfers between devices  58.4 us (36%)
  starting transfers between devices  33.4 us (20%)
    ppermute x21, waiting for transfers between devices, swapped(): return lax.ppermute(array, axis, [(i, i ^ step) for i in range(size)])  29.6 us
    ppermute x9, waiting for transfers between devices, hop(): lax.ppermute(array, 'tp', [(2 * i + core, 2 * j + core) for i, j in pairs...  28.8 us
    pallas_call x4, Pallas kernels, column_products(): pl.pallas_call(functools.partial(product_kernel, steps, [part.shape[1] fo...  21.2 us
    ppermute x9, starting transfers between devices, hop(): lax.ppermute(array, 'tp', [(2 * i + core, 2 * j + core) for i, j in pairs...  17.2 us
    ppermute x21, starting transfers between devices, swapped(): return lax.ppermute(array, axis, [(i, i ^ step) for i in range(size)])  16.2 us
    pallas_call x3, Pallas kernels, cotangent_products(): pl.pallas_call(functools.partial(cotangent_kernel, count, begin), out_sha...  16.2 us
    pallas_call x1, Pallas kernels, correlate(): pl.pallas_call(functools.partial(backward_kernel, members, per_group, sca...  9.78 us
    pallas_call x1, Pallas kernels, convolve(): pl.pallas_call(functools.partial(forward_kernel, members, per_group, widt...  5.55 us
  transfers between devices with their start and end apart: 30, of which 14 were waited for; matrix products, arithmetic and copies ran while one was open for 0% of the time, Pallas kernels for 41%

profile of v10, /device:TPU:0, one launch (start us, length us, event | category | flops | bytes accessed | tf_op | source)
XLA Modules:
  0.0 162.4 jit_solution(16675304642824385035)
XLA Ops:
  1.2 2.7 %collective-permute-start.4 = (bf16[512,1024]{1,0:T(8,128)(2,1)}, bf16[512,1024]{1,0:T(8,128)(2,1)S(1)}, u32[]{:S(2)}, u32[]{:S(2)}) collective-permute-start(bf16[512,1024]{1,0:T(8,128)(2,1)} %refs_0_.1), channel_id=1, source_target_pairs={{0,2},{1,3},{6,4},{7,5},{2,0},{3,1},{4,6},{5,7},{8,10},{9,11},{14,... | collective-permute-start | bytes 3145736 | tf_op jit(solution)/shard_map/ppermute | solution.py:351
  4.6 2.6 %gated_input.1 = (bf16[544,256]{1,0:T(8,128)(2,1)S(1)}, bf16[544,256]{1,0:T(8,128)(2,1)S(1)}, bf16[544,256]{1,0:T(8,128)(2,1)S(1)}, bf16[544,256]{1,0:T(8,128)(2,1)S(1)}) custom-call(s32[2]{0:T(128)S(1)} %pad_add_fusion.who_ref, bf16[512,1024]{1,0:T(8,128)(2,1)} %refs_4_.3, bf16[512,1024]{1,0:T(8,128)(2,1)} %refs_5_.1, f32[64,512]{1,0:T(8,128)} %bitcast.4), custom_call_target="tpu_custom_call" | custom-call | flops 1048576 | bytes 4096 | tf_op jit(solution)/shard_map/gated_input/pallas_call | solution.py:261
  12.0 5.0 %cotangent_blocks.3.refs_4_.refs_3_ = f32[512,1024]{1,0:T(8,128)S(1)} custom-call(s32[10]{0:T(128)S(1)} %plan.1._.plan_ref, bf16[1024,8192]{1,0:T(8,128)(2,1)} %weight_ref.15, bf16[512,1024]{1,0:T(8,128)(2,1)S(1)} %copy-done.4, bf16[512,1024]{1,0:T(8,128)(2,1)} %collective-permute-done.3.refs_1_), custom_call_target="tpu_custom_call" | custom-call | flops 1048576 | bytes 4096 | tf_op jit(solution)/shard_map/cotangent_blocks/pallas_call | solution.py:646
  17.0 6.2 %collective-permute-done.1.refs_2_ = bf16[544,256]{1,0:T(8,128)(2,1)S(1)} collective-permute-done((bf16[544,256]{1,0:T(8,128)(2,1)S(1)}, bf16[544,256]{1,0:T(8,128)(2,1)S(1)}, u32[]{:S(2)}, u32[]{:S(2)}) %collective-permute-start.1) | collective-permute-done | bytes 278560 | tf_op jit(solution)/shard_map/ppermute | solution.py:318
  23.2 5.5 %causal_conv.1 = (bf16[512,256]{1,0:T(8,128)(2,1)S(1)}, bf16[512,256]{1,0:T(8,128)(2,1)S(1)}, bf16[512,256]{1,0:T(8,128)(2,1)S(1)}, bf16[512,256]{1,0:T(8,128)(2,1)S(1)}) custom-call(s32[10]{0:T(128)S(1)} %plan.1._.plan_ref, bf16[544,256]{1,0:T(8,128)(2,1)S(1)} %get-tuple-element.50.refs_0_, bf16[544,256]{1,0:T(8,128)(2,1)S(1)} %collective-permute-done.refs_1_, ...), custom_call_target="tpu_custom_call" | custom-call | flops 1048576 | bytes 4096 | tf_op jit(solution)/shard_map/causal_conv/pallas_call | solution.py:182
  34.4 3.7 %collective-permute-done.6.refs_1_ = bf16[512,256]{1,0:T(8,128)(2,1)S(1)} collective-permute-done((bf16[512,256]{1,0:T(8,128)(2,1)S(1)}, bf16[512,256]{1,0:T(8,128)(2,1)S(1)}, u32[]{:S(2)}, u32[]{:S(2)}) %collective-permute-start.6) | collective-permute-done | bytes 262176 | tf_op jit(solution)/shard_map/ppermute | solution.py:318
  38.1 4.9 %collective-permute-done.7.refs_2_ = bf16[512,256]{1,0:T(8,128)(2,1)S(1)} collective-permute-done((bf16[512,256]{1,0:T(8,128)(2,1)S(1)}, bf16[512,256]{1,0:T(8,128)(2,1)S(1)}, u32[]{:S(2)}, u32[]{:S(2)}) %collective-permute-start.7) | collective-permute-done | bytes 262176 | tf_op jit(solution)/shard_map/ppermute | solution.py:318
  43.9 5.5 %projection_blocks.4 = (bf16[512,768]{1,0:T(8,128)(2,1)S(1)}, bf16[512,640]{1,0:T(8,128)(2,1)S(1)}, bf16[512,640]{1,0:T(8,128)(2,1)S(1)}) custom-call(s32[10]{0:T(128)S(1)} %plan.1._.plan_ref, bf16[512,1024]{1,0:T(8,128)(2,1)S(1)} %get-tuple-element.62.data_ref, bf16[1024,8192]{1,0:T(8,128)(2,1)} %weight_ref.15), custom_call_target="tpu_custom_call" | custom-call | flops 1048576 | bytes 4096 | tf_op jit(solution)/shard_map/projection_blocks/pallas_call | solution.py:547
  50.0 2.6 %collective-permute-done.12.refs_1_ = bf16[512,640]{1,0:T(8,128)(2,1)S(1)} collective-permute-done((bf16[512,640]{1,0:T(8,128)(2,1)S(1)}, bf16[512,640]{1,0:T(8,128)(2,1)S(1)}, u32[]{:S(2)}, u32[]{:S(2)}) %collective-permute-start.12) | collective-permute-done | bytes 655392 | tf_op jit(solution)/shard_map/ppermute | solution.py:318
  53.6 5.7 %projection_blocks.5 = (bf16[512,1024]{1,0:T(8,128)(2,1)S(1)}, bf16[512,1024]{1,0:T(8,128)(2,1)S(1)}) custom-call(s32[10]{0:T(128)S(1)} %plan.1._.plan_ref, bf16[512,1024]{1,0:T(8,128)(2,1)S(1)} %get-tuple-element.62.data_ref, bf16[1024,8192]{1,0:T(8,128)(2,1)} %weight_ref.15, bf16[512,768]{1,0:T(8,128)(2,1)S(1)} %collective-permute-done.11.refs_0_, ...), custom_call_target="tpu_custom_call" | custom-call | flops 1048576 | bytes 4096 | tf_op jit(solution)/shard_map/projection_blocks/pallas_call | solution.py:547
  60.2 4.3 %collective-permute-start.16 = (bf16[512,1024]{1,0:T(8,128)(2,1)S(1)}, bf16[512,1024]{1,0:T(8,128)(2,1)S(1)}, u32[]{:S(2)}, u32[]{:S(2)}) collective-permute-start(bf16[512,1024]{1,0:T(8,128)(2,1)S(1)} %chosen.2.refs_0_.refs_4_), channel_id=1, source_target_pairs={{2,0},{3,1},{4,6},{5,7},{0,2},{1,3},{6,4},{7,5},{10,8},{11,9},{12,... | collective-permute-start | bytes 3145736 | tf_op jit(solution)/shard_map/ppermute | solution.py:351
  65.7 4.9 %projection_blocks.6 = (bf16[512,1024]{1,0:T(8,128)(2,1)S(1)}, bf16[512,1024]{1,0:T(8,128)(2,1)S(1)}) custom-call(s32[10]{0:T(128)S(1)} %plan.1._.plan_ref, bf16[512,1024]{1,0:T(8,128)(2,1)S(1)} %get-tuple-element.62.data_ref, bf16[1024,8192]{1,0:T(8,128)(2,1)} %weight_ref.15, bf16[512,1024]{1,0:T(8,128)(2,1)S(1)} %chosen.2.refs_0_.refs_4_), custom_call_target="tpu_custom_call" | custom-call | flops 1048576 | bytes 4096 | tf_op jit(solution)/shard_map/projection_blocks/pallas_call | solution.py:547
  71.2 6.4 %cotangent_blocks.4.refs_1_.refs_2_ = f32[512,1024]{1,0:T(8,128)S(1)} custom-call(s32[10]{0:T(128)S(1)} %plan.1._.plan_ref, bf16[1024,8192]{1,0:T(8,128)(2,1)} %weight_ref.15, bf16[512,1024]{1,0:T(8,128)(2,1)S(1)} %get-tuple-element.72.refs_0_, bf16[512,1024]{1,0:T(8,128)(2,1)S(1)} %collective-permute-done.17.refs_1_, bf16[512,1024]{1,0:T(8,128)(2,1)S(1)} %added.2.refs_2_, ...), custom_call_target="tpu_custom_call" | custom-call | flops 1048576 | bytes 4096 | tf_op jit(solution)/shard_map/cotangent_blocks/pallas_call | solution.py:646
  77.6 10.6 %collective-permute-done.16.refs_0_ = bf16[512,1024]{1,0:T(8,128)(2,1)S(1)} collective-permute-done((bf16[512,1024]{1,0:T(8,128)(2,1)S(1)}, bf16[512,1024]{1,0:T(8,128)(2,1)S(1)}, u32[]{:S(2)}, u32[]{:S(2)}) %collective-permute-start.16) | collective-permute-done | bytes 1048608 | tf_op jit(solution)/shard_map/ppermute | solution.py:351
  89.7 4.7 %collective-permute-start.21 = (bf16[512,1024]{1,0:T(8,128)(2,1)S(1)}, bf16[512,1024]{1,0:T(8,128)(2,1)S(1)}, u32[]{:S(2)}, u32[]{:S(2)}) collective-permute-start(bf16[512,1024]{1,0:T(8,128)(2,1)S(1)} %passing.1.refs_0_.refs_3_), channel_id=1, source_target_pairs={{0,4},{1,5},{2,6},{3,7},{4,0},{5,1},{6,2},{7,3},{8,12},{9,13},{10,... | collective-permute-start | bytes 3145736 | tf_op jit(solution)/shard_map/ppermute | solution.py:351
  94.4 4.8 %cotangent_blocks.5.start_ref = f32[512,1024]{1,0:T(8,128)S(1)} custom-call(s32[10]{0:T(128)S(1)} %plan.1._.plan_ref, bf16[1024,8192]{1,0:T(8,128)(2,1)} %weight_ref.15, bf16[512,1024]{1,0:T(8,128)(2,1)S(1)} %collective-permute-done.20.refs_0_, bf16[512,1024]{1,0:T(8,128)(2,1)S(1)} %chosen.3.refs_1_, f32[512,1024]{1,0:T(8,128)S(1)} %cotangent_blocks.4.refs_1_.refs_2_, ...), custom_call_target="tpu_custom_call" | custom-call | flops 1048576 | bytes 4096 | tf_op jit(solution)/shard_map/cotangent_blocks/pallas_call | solution.py:646
  99.2 4.5 %cotangent_last.1 = (bf16[512,1024]{1,0:T(8,128)(2,1)}, bf16[512,256]{1,0:T(8,128)(2,1)S(1)}, bf16[512,256]{1,0:T(8,128)(2,1)S(1)}, bf16[512,256]{1,0:T(8,128)(2,1)S(1)}, bf16[512,256]{1,0:T(8,128)(2,1)S(1)}) custom-call(s32[10]{0:T(128)S(1)} %plan.1._.plan_ref, bf16[1024,8192]{1,0:T(8,128)(2,1)} %weight_ref.15, ...), custom_call_target="tpu_custom_call" | custom-call | flops 1048576 | bytes 4096 | tf_op jit(solution)/shard_map/cotangent_last/pallas_call | solution.py:612
  103.7 5.1 %projection_blocks.7 = (bf16[512,512]{1,0:T(8,128)(2,1)S(1)}, bf16[512,512]{1,0:T(8,128)(2,1)S(1)}, bf16[512,1024]{1,0:T(8,128)(2,1)S(1)}) custom-call(s32[10]{0:T(128)S(1)} %plan.1._.plan_ref, bf16[512,1024]{1,0:T(8,128)(2,1)S(1)} %get-tuple-element.62.data_ref, bf16[1024,8192]{1,0:T(8,128)(2,1)} %weight_ref.15, ...), custom_call_target="tpu_custom_call" | custom-call | flops 1048576 | bytes 4096 | tf_op jit(solution)/shard_map/projection_blocks/pallas_call | solution.py:547
  112.5 5.7 %collective-permute-done.24.refs_5_ = bf16[512,256]{1,0:T(8,128)(2,1)S(1)} collective-permute-done((bf16[512,256]{1,0:T(8,128)(2,1)S(1)}, bf16[512,256]{1,0:T(8,128)(2,1)S(1)}, u32[]{:S(2)}, u32[]{:S(2)}) %collective-permute-start.24) | collective-permute-done | bytes 262176 | tf_op jit(solution)/shard_map/ppermute | solution.py:318
  120.1 2.6 %collective-permute-done.25.refs_6_ = bf16[512,256]{1,0:T(8,128)(2,1)S(1)} collective-permute-done((bf16[512,256]{1,0:T(8,128)(2,1)S(1)}, bf16[512,256]{1,0:T(8,128)(2,1)S(1)}, u32[]{:S(2)}, u32[]{:S(2)}) %collective-permute-start.25) | collective-permute-done | bytes 262176 | tf_op jit(solution)/shard_map/ppermute | solution.py:318
  124.0 9.8 %causal_conv_grads.1 = (bf16[544,256]{1,0:T(8,128)(2,1)S(1)}, bf16[544,256]{1,0:T(8,128)(2,1)S(1)}, bf16[544,256]{1,0:T(8,128)(2,1)S(1)}, bf16[544,256]{1,0:T(8,128)(2,1)S(1)}) custom-call(s32[10]{0:T(128)S(1)} %plan.1._.plan_ref, bf16[544,256]{1,0:T(8,128)(2,1)S(1)} %get-tuple-element.50.refs_0_, bf16[544,256]{1,0:T(8,128)(2,1)S(1)} %collective-permute-done.refs_1_, ...), custom_call_target="tpu_custom_call" | custom-call | flops 1048576 | bytes 4096 | tf_op jit(solution)/shard_map/causal_conv_grads/pallas_call | solution.py:203
  133.7 11.1 %collective-permute-done.22.refs_3_.refs_4_ = bf16[512,512]{1,0:T(8,128)(2,1)S(1)} collective-permute-done((bf16[512,512]{1,0:T(8,128)(2,1)S(1)}, bf16[512,512]{1,0:T(8,128)(2,1)S(1)}, u32[]{:S(2)}, u32[]{:S(2)}) %collective-permute-start.22) | collective-permute-done | bytes 524320 | tf_op jit(solution)/shard_map/ppermute | solution.py:351
  148.3 7.0 %collective-permute-done.23.refs_4_ = bf16[512,512]{1,0:T(8,128)(2,1)S(1)} collective-permute-done((bf16[512,512]{1,0:T(8,128)(2,1)S(1)}, bf16[512,512]{1,0:T(8,128)(2,1)S(1)}, u32[]{:S(2)}, u32[]{:S(2)}) %collective-permute-start.23) | collective-permute-done | bytes 524320 | tf_op jit(solution)/shard_map/ppermute | solution.py:351
  160.1 2.3 %input_gradients.1 = (bf16[512,1024]{1,0:T(8,128)(2,1)}, bf16[512,1024]{1,0:T(8,128)(2,1)}, f32[64,512]{1,0:T(8,128)}) custom-call(s32[10]{0:T(128)S(1)} %plan.1._.plan_ref, bf16[544,256]{1,0:T(8,128)(2,1)S(1)} %get-tuple-element.88.refs_0_, bf16[544,256]{1,0:T(8,128)(2,1)S(1)} %collective-permute-done.27.refs_1_, ...), custom_call_target="tpu_custom_call" | custom-call | flops 1048576 | bytes 4096 | tf_op jit(solution)/shard_map/input_gradients/pallas_call | solution.py:304
  (70 shorter events, 33.3 us)
Async XLA Ops:
  0.6 9.7 %collective-permute-start.3 = (bf16[512,1024]{1,0:T(8,128)(2,1)}, bf16[512,1024]{1,0:T(8,128)(2,1)}, u32[]{:S(2)}, u32[]{:S(2)}) collective-permute-start(bf16[512,1024]{1,0:T(8,128)(2,1)} %refs_0_.1), channel_id=1, source_target_pairs={{0,1},{1,0},{2,3},{3,2},{4,5},{5,4},{6,7},{7,6},{8,9},{9,8},{10,11... | collective-permute-start | bytes 3145736 | tf_op jit(solution)/shard_map/ppermute | solution.py:318
  1.2 27.6 %collective-permute-start.4 = (bf16[512,1024]{1,0:T(8,128)(2,1)}, bf16[512,1024]{1,0:T(8,128)(2,1)S(1)}, u32[]{:S(2)}, u32[]{:S(2)}) collective-permute-start(bf16[512,1024]{1,0:T(8,128)(2,1)} %refs_0_.1), channel_id=1, source_target_pairs={{0,2},{1,3},{6,4},{7,5},{2,0},{3,1},{4,6},{5,7},{8,10},{9,11},{14,... | collective-permute-start | bytes 3145736 | tf_op jit(solution)/shard_map/ppermute | solution.py:351
  3.8 25.0 %collective-permute-start.5 = (bf16[512,1024]{1,0:T(8,128)(2,1)}, bf16[512,1024]{1,0:T(8,128)(2,1)S(1)}, u32[]{:S(2)}, u32[]{:S(2)}) collective-permute-start(bf16[512,1024]{1,0:T(8,128)(2,1)} %refs_0_.1), channel_id=1, source_target_pairs={{2,4},{3,5},{4,2},{5,3},{10,12},{11,13},{12,10},{13,11},{18,20},{1... | collective-permute-start | bytes 3145736 | tf_op jit(solution)/shard_map/ppermute | solution.py:351
  7.2 9.8 %collective-permute-start = (bf16[544,256]{1,0:T(8,128)(2,1)S(1)}, bf16[544,256]{1,0:T(8,128)(2,1)S(1)}, u32[]{:S(2)}, u32[]{:S(2)}) collective-permute-start(bf16[544,256]{1,0:T(8,128)(2,1)S(1)} %get-tuple-element.51), channel_id=1, source_target_pairs={{0,8},{8,0},{16,24},{24,16},{1,9},{9,1},{17,25},{25,17},{2,10},{10... | collective-permute-start | bytes 835592 | tf_op jit(solution)/shard_map/ppermute | solution.py:318
  8.8 14.4 %collective-permute-start.1 = (bf16[544,256]{1,0:T(8,128)(2,1)S(1)}, bf16[544,256]{1,0:T(8,128)(2,1)S(1)}, u32[]{:S(2)}, u32[]{:S(2)}) collective-permute-start(bf16[544,256]{1,0:T(8,128)(2,1)S(1)} %get-tuple-element.52), channel_id=1, source_target_pairs={{0,16},{8,24},{16,0},{24,8},{1,17},{9,25},{17,1},{25,9},{2,18},{10... | collective-permute-start | bytes 835592 | tf_op jit(solution)/shard_map/ppermute | solution.py:318
  10.3 12.9 %collective-permute-start.2 = (bf16[544,256]{1,0:T(8,128)(2,1)S(1)}, bf16[544,256]{1,0:T(8,128)(2,1)S(1)}, u32[]{:S(2)}, u32[]{:S(2)}) collective-permute-start(bf16[544,256]{1,0:T(8,128)(2,1)S(1)} %get-tuple-element.53), channel_id=1, source_target_pairs={{0,24},{8,16},{16,8},{24,0},{1,25},{9,17},{17,9},{25,1},{2,26},{10... | collective-permute-start | bytes 835592 | tf_op jit(solution)/shard_map/ppermute | solution.py:318
  30.1 12.9 %collective-permute-start.7 = (bf16[512,256]{1,0:T(8,128)(2,1)S(1)}, bf16[512,256]{1,0:T(8,128)(2,1)S(1)}, u32[]{:S(2)}, u32[]{:S(2)}) collective-permute-start(bf16[512,256]{1,0:T(8,128)(2,1)S(1)} %get-tuple-element.60), channel_id=1, source_target_pairs={{0,16},{8,24},{16,0},{24,8},{1,17},{9,25},{17,1},{25,9},{2,18},{10... | collective-permute-start | bytes 786440 | tf_op jit(solution)/shard_map/ppermute | solution.py:318
  31.0 12.0 %collective-permute-start.8 = (bf16[512,256]{1,0:T(8,128)(2,1)S(1)}, bf16[512,256]{1,0:T(8,128)(2,1)S(1)}, u32[]{:S(2)}, u32[]{:S(2)}) collective-permute-start(bf16[512,256]{1,0:T(8,128)(2,1)S(1)} %get-tuple-element.61), channel_id=1, source_target_pairs={{0,24},{8,16},{16,8},{24,0},{1,25},{9,17},{17,9},{25,1},{2,26},{10... | collective-permute-start | bytes 786440 | tf_op jit(solution)/shard_map/ppermute | solution.py:318
  32.4 27.1 %collective-permute-start.10 = (bf16[512,1024]{1,0:T(8,128)(2,1)S(1)}, bf16[512,1024]{1,0:T(8,128)(2,1)S(1)}, u32[]{:S(2)}, u32[]{:S(2)}) collective-permute-start(bf16[512,1024]{1,0:T(8,128)(2,1)S(1)} %get-tuple-element.64.refs_0_), channel_id=1, source_target_pairs={{2,0},{3,1},{4,6},{5,7},{10,8},{11,9},{12,14},{13,15},{18,16},{19,... | collective-permute-start | bytes 3145736 | tf_op jit(solution)/shard_map/ppermute | solution.py:351
  33.7 25.8 %collective-permute-start.9 = (bf16[512,1024]{1,0:T(8,128)(2,1)S(1)}, bf16[512,1024]{1,0:T(8,128)(2,1)S(1)}, u32[]{:S(2)}, u32[]{:S(2)}) collective-permute-start(bf16[512,1024]{1,0:T(8,128)(2,1)S(1)} %get-tuple-element.63.refs_2_), channel_id=1, source_target_pairs={{2,4},{3,5},{4,2},{5,3},{10,12},{11,13},{12,10},{13,11},{18,20},{1... | collective-permute-start | bytes 3145736 | tf_op jit(solution)/shard_map/ppermute | solution.py:351
  59.5 11.6 %collective-permute-start.17 = (bf16[512,1024]{1,0:T(8,128)(2,1)S(1)}, bf16[512,1024]{1,0:T(8,128)(2,1)S(1)}, u32[]{:S(2)}, u32[]{:S(2)}) collective-permute-start(bf16[512,1024]{1,0:T(8,128)(2,1)S(1)} %get-tuple-element.72.refs_0_), channel_id=1, source_target_pairs={{0,1},{1,0},{2,3},{3,2},{4,5},{5,4},{6,7},{7,6},{8,9},{9,8},{10,11... | collective-permute-start | bytes 3145736 | tf_op jit(solution)/shard_map/ppermute | solution.py:318
  60.2 28.0 %collective-permute-start.16 = (bf16[512,1024]{1,0:T(8,128)(2,1)S(1)}, bf16[512,1024]{1,0:T(8,128)(2,1)S(1)}, u32[]{:S(2)}, u32[]{:S(2)}) collective-permute-start(bf16[512,1024]{1,0:T(8,128)(2,1)S(1)} %chosen.2.refs_0_.refs_4_), channel_id=1, source_target_pairs={{2,0},{3,1},{4,6},{5,7},{0,2},{1,3},{6,4},{7,5},{10,8},{11,9},{12,... | collective-permute-start | bytes 3145736 | tf_op jit(solution)/shard_map/ppermute | solution.py:351
  64.5 23.7 %collective-permute-start.18 = (bf16[512,1024]{1,0:T(8,128)(2,1)S(1)}, bf16[512,1024]{1,0:T(8,128)(2,1)S(1)}, u32[]{:S(2)}, u32[]{:S(2)}) collective-permute-start(bf16[512,1024]{1,0:T(8,128)(2,1)S(1)} %get-tuple-element.74.second_ref), channel_id=1, source_target_pairs={{2,4},{3,5},{4,2},{5,3},{10,12},{11,13},{12,10},{13,11},{18,20},{1... | collective-permute-start | bytes 3145736 | tf_op jit(solution)/shard_map/ppermute | solution.py:351
  65.5 28.9 %collective-permute-start.20 = (bf16[512,1024]{1,0:T(8,128)(2,1)S(1)}, bf16[512,1024]{1,0:T(8,128)(2,1)S(1)}, u32[]{:S(2)}, u32[]{:S(2)}) collective-permute-start(bf16[512,1024]{1,0:T(8,128)(2,1)S(1)} %added.2.refs_2_), channel_id=1, source_target_pairs={{0,1},{1,0},{2,3},{3,2},{4,5},{5,4},{6,7},{7,6},{8,9},{9,8},{10,11... | collective-permute-start | bytes 3145736 | tf_op jit(solution)/shard_map/ppermute | solution.py:318
  70.6 28.6 %collective-permute-start.14 = (bf16[512,1024]{1,0:T(8,128)(2,1)S(1)}, bf16[512,1024]{1,0:T(8,128)(2,1)S(1)}, u32[]{:S(2)}, u32[]{:S(2)}) collective-permute-start(bf16[512,1024]{1,0:T(8,128)(2,1)S(1)} %get-tuple-element.70.refs_2_), channel_id=1, source_target_pairs={{0,1},{1,0},{2,3},{3,2},{4,5},{5,4},{6,7},{7,6},{8,9},{9,8},{10,11... | collective-permute-start | bytes 3145736 | tf_op jit(solution)/shard_map/ppermute | solution.py:318
  71.1 28.1 %collective-permute-start.15 = (bf16[512,1024]{1,0:T(8,128)(2,1)S(1)}, bf16[512,1024]{1,0:T(8,128)(2,1)S(1)}, u32[]{:S(2)}, u32[]{:S(2)}) collective-permute-start(bf16[512,1024]{1,0:T(8,128)(2,1)S(1)} %get-tuple-element.71), channel_id=1, source_target_pairs={{0,1},{1,0},{2,3},{3,2},{4,5},{5,4},{6,7},{7,6},{8,9},{9,8},{10,11... | collective-permute-start | bytes 3145736 | tf_op jit(solution)/shard_map/ppermute | solution.py:318
  89.7 58.6 %collective-permute-start.21 = (bf16[512,1024]{1,0:T(8,128)(2,1)S(1)}, bf16[512,1024]{1,0:T(8,128)(2,1)S(1)}, u32[]{:S(2)}, u32[]{:S(2)}) collective-permute-start(bf16[512,1024]{1,0:T(8,128)(2,1)S(1)} %passing.1.refs_0_.refs_3_), channel_id=1, source_target_pairs={{0,4},{1,5},{2,6},{3,7},{4,0},{5,1},{6,2},{7,3},{8,12},{9,13},{10,... | collective-permute-start | bytes 3145736 | tf_op jit(solution)/shard_map/ppermute | solution.py:351
  108.9 35.9 %collective-permute-start.22 = (bf16[512,512]{1,0:T(8,128)(2,1)S(1)}, bf16[512,512]{1,0:T(8,128)(2,1)S(1)}, u32[]{:S(2)}, u32[]{:S(2)}) collective-permute-start(bf16[512,512]{1,0:T(8,128)(2,1)S(1)} %get-tuple-element.78), channel_id=1, source_target_pairs={{0,2},{1,3},{6,4},{7,5},{2,0},{3,1},{4,6},{5,7},{8,10},{9,11},{14,... | collective-permute-start | bytes 1572872 | tf_op jit(solution)/shard_map/ppermute | solution.py:351
  110.2 12.5 %collective-permute-start.25 = (bf16[512,256]{1,0:T(8,128)(2,1)S(1)}, bf16[512,256]{1,0:T(8,128)(2,1)S(1)}, u32[]{:S(2)}, u32[]{:S(2)}) collective-permute-start(bf16[512,256]{1,0:T(8,128)(2,1)S(1)} %get-tuple-element.82), channel_id=1, source_target_pairs={{0,16},{8,24},{16,0},{24,8},{1,17},{9,25},{17,1},{25,9},{2,18},{10... | collective-permute-start | bytes 786440 | tf_op jit(solution)/shard_map/ppermute | solution.py:318
  111.5 12.4 %collective-permute-start.26 = (bf16[512,256]{1,0:T(8,128)(2,1)S(1)}, bf16[512,256]{1,0:T(8,128)(2,1)S(1)}, u32[]{:S(2)}, u32[]{:S(2)}) collective-permute-start(bf16[512,256]{1,0:T(8,128)(2,1)S(1)} %get-tuple-element.83), channel_id=1, source_target_pairs={{0,24},{8,16},{16,8},{24,0},{1,25},{9,17},{17,9},{25,1},{2,26},{10... | collective-permute-start | bytes 786440 | tf_op jit(solution)/shard_map/ppermute | solution.py:318
  118.2 37.1 %collective-permute-start.23 = (bf16[512,512]{1,0:T(8,128)(2,1)S(1)}, bf16[512,512]{1,0:T(8,128)(2,1)S(1)}, u32[]{:S(2)}, u32[]{:S(2)}) collective-permute-start(bf16[512,512]{1,0:T(8,128)(2,1)S(1)} %get-tuple-element.79), channel_id=1, source_target_pairs={{0,2},{1,3},{6,4},{7,5},{2,0},{3,1},{4,6},{5,7},{8,10},{9,11},{14,... | collective-permute-start | bytes 1572872 | tf_op jit(solution)/shard_map/ppermute | solution.py:351
  144.8 12.3 %collective-permute-start.27 = (bf16[544,256]{1,0:T(8,128)(2,1)S(1)}, bf16[544,256]{1,0:T(8,128)(2,1)S(1)}, u32[]{:S(2)}, u32[]{:S(2)}) collective-permute-start(bf16[544,256]{1,0:T(8,128)(2,1)S(1)} %get-tuple-element.89), channel_id=1, source_target_pairs={{0,8},{8,0},{16,24},{24,16},{1,9},{9,1},{17,25},{25,17},{2,10},{10... | collective-permute-start | bytes 835592 | tf_op jit(solution)/shard_map/ppermute | solution.py:318
  146.1 11.6 %collective-permute-start.28 = (bf16[544,256]{1,0:T(8,128)(2,1)S(1)}, bf16[544,256]{1,0:T(8,128)(2,1)S(1)}, u32[]{:S(2)}, u32[]{:S(2)}) collective-permute-start(bf16[544,256]{1,0:T(8,128)(2,1)S(1)} %get-tuple-element.90), channel_id=1, source_target_pairs={{0,16},{8,24},{16,0},{24,8},{1,17},{9,25},{17,1},{25,9},{2,18},{10... | collective-permute-start | bytes 835592 | tf_op jit(solution)/shard_map/ppermute | solution.py:318
  147.4 11.5 %collective-permute-start.29 = (bf16[544,256]{1,0:T(8,128)(2,1)S(1)}, bf16[544,256]{1,0:T(8,128)(2,1)S(1)}, u32[]{:S(2)}, u32[]{:S(2)}) collective-permute-start(bf16[544,256]{1,0:T(8,128)(2,1)S(1)} %get-tuple-element.91), channel_id=1, source_target_pairs={{0,24},{8,16},{16,8},{24,0},{1,25},{9,17},{17,9},{25,1},{2,26},{10... | collective-permute-start | bytes 835592 | tf_op jit(solution)/shard_map/ppermute | solution.py:318
  (11 other events, 89.0 us)

commit v11 on v10

--- a/solution.py
+++ b/solution.py
@@ -59,7 +59,7 @@
 
 def forward_kernel(members, per_group, width, plan_ref, *refs):
     inputs, outputs = refs[:members], refs[-members - 3 : -3]
-    tap_scr, in_scr, out_scr = refs[-3:]
+    in_scr, tap_scr, out_scr = refs[-3:]
     position = plan_ref[POSITION]
     channels = inputs[0].shape[1]
     groups = channels // per_group
@@ -97,21 +97,19 @@
         outputs[step][...] = out_scr[position ^ step].T
 
 
-def backward_kernel(members, per_group, scale, width, plan_ref, *refs):
-    inputs, cotangents = refs[:members], refs[members : 2 * members]
-    outputs = refs[-members - 6 : -6]
-    tap_scr, in_scr, cot_scr, out_scr, grad_scr, pad_scr = refs[-6:]
+def backward_kernel(members, per_group, scale, width, plan_ref, in_scr, tap_scr, *refs):
+    cotangents = refs[:members]
+    outputs = refs[-members - 4 : -4]
+    cot_scr, out_scr, grad_scr, pad_scr = refs[-4:]
     position = plan_ref[POSITION]
-    channels = inputs[0].shape[1]
+    channels = cotangents[0].shape[1]
     groups = channels // per_group
     length = members * width
     blocks = length // BLOCK
     depth = blocks * per_group
     for step in range(members):
         at = position ^ step
-        in_scr[at] = inputs[step][:width].T
         cot_scr[at] = cotangents[step][...].T
-        load_taps(tap_scr, inputs[step], at, width)
     pad_scr[...] = jnp.zeros_like(pad_scr)
     rows_of = lax.broadcasted_iota(jnp.int32, (BLOCK, BLOCK), 0)
     lanes_of = lax.broadcasted_iota(jnp.int32, (BLOCK, BLOCK), 1)
@@ -179,35 +177,35 @@
     members = len(inputs)
     channels = inputs[0].shape[1]
     length = members * width
-    return pl.pallas_call(
+    *parts, turned, taps = pl.pallas_call(
         functools.partial(forward_kernel, members, per_group, width),
-        out_shape=[jax.ShapeDtypeStruct((width, channels), jnp.bfloat16)] * members,
+        out_shape=[jax.ShapeDtypeStruct((width, channels), jnp.bfloat16)] * members
+        + [
+            jax.ShapeDtypeStruct((members, channels, width), jnp.bfloat16),
+            jax.ShapeDtypeStruct((channels // per_group, length), jnp.float32),
+        ],
         in_specs=[SMEM] + [VMEM] * members + [ANYWHERE] * len(after),
-        out_specs=[VMEM] * members,
-        scratch_shapes=[
-            pltpu.VMEM((channels // per_group, length), jnp.float32),
-            pltpu.VMEM((members, channels, width), jnp.bfloat16),
-            pltpu.VMEM((members, channels, width), jnp.bfloat16),
-        ],
+        out_specs=[VMEM] * (members + 2),
+        scratch_shapes=[pltpu.VMEM((members, channels, width), jnp.bfloat16)],
         compiler_params=pltpu.CompilerParams(vmem_limit_bytes=24 * 2**20),
         cost_estimate=COST,
         name="causal_conv",
     )(plan, *inputs, *after)
-
-
-def correlate(plan, inputs, cotangents, per_group, scale, after=()):
-    members = len(inputs)
+    return parts, turned, taps
+
+
+def correlate(plan, turned, taps, cotangents, per_group, scale, after=()):
+    members = len(cotangents)
     width, channels = cotangents[0].shape
     length = members * width
     groups = channels // per_group
+    rows = width + padded(groups) * width // channels
     return pl.pallas_call(
         functools.partial(backward_kernel, members, per_group, scale, width),
-        out_shape=[jax.ShapeDtypeStruct(inputs[0].shape, jnp.bfloat16)] * members,
-        in_specs=[SMEM] + [VMEM] * (2 * members) + [ANYWHERE] * len(after),
+        out_shape=[jax.ShapeDtypeStruct((rows, channels), jnp.bfloat16)] * members,
+        in_specs=[SMEM] + [VMEM] * (members + 2) + [ANYWHERE] * len(after),
         out_specs=[VMEM] * members,
         scratch_shapes=[
-            pltpu.VMEM((groups, length), jnp.float32),
-            pltpu.VMEM((members, channels, width), jnp.bfloat16),
             pltpu.VMEM((members, channels, width), jnp.bfloat16),
             pltpu.VMEM((members, channels, width), jnp.bfloat16),
             pltpu.VMEM((groups, length), jnp.float32),
@@ -216,7 +214,7 @@
         compiler_params=pltpu.CompilerParams(vmem_limit_bytes=24 * 2**20),
         cost_estimate=COST,
         name="causal_conv_grads",
-    )(plan, *inputs, *cotangents, *after)
+    )(plan, turned, taps, *cotangents, *after)
 
 
 def in_hbm(array):
@@ -405,53 +403,23 @@
     )(*values, *after)
 
 
-def add_kernel(count, *refs):
-    total = sum(wide(ref[...]) for ref in refs[:count])
-    if len(refs) > count + 1:
-        halves = [wide(ref[...]) for ref in refs[count:-1]]
-        total = total + jnp.concatenate(halves, axis=1)
-    refs[-1][...] = total.astype(jnp.bfloat16)
-
-
-def added(*arrays, halves=()):
+def add_kernel(*refs):
+    refs[-1][...] = sum(wide(ref[...]) for ref in refs[:-1]).astype(jnp.bfloat16)
+
+
+def added(*arrays):
     rows, width = arrays[0].shape
     part = pl.BlockSpec((rows // 4, width), lambda i: (i, 0))
-    half = pl.BlockSpec((rows // 4, width // 2), lambda i: (i, 0))
-    return pl.pallas_call(
-        functools.partial(add_kernel, len(arrays)),
+    return pl.pallas_call(
+        add_kernel,
         out_shape=jax.ShapeDtypeStruct((rows, width), jnp.bfloat16),
         grid=(4,),
-        in_specs=[part] * len(arrays) + [half] * len(halves),
+        in_specs=[part] * len(arrays),
         out_specs=part,
         compiler_params=pltpu.CompilerParams(vmem_limit_bytes=8 * 2**20),
         cost_estimate=COST,
         name="added",
-    )(*arrays, *halves)
-
-
-def passing_kernel(plan_ref, first_ref, arrived_ref, second_ref, *refs):
-    out_ref = refs[-1]
-    in_middle = plan_ref[IN_MIDDLE] == 1
-
-    @pl.when(in_middle)
-    def _():
-        out_ref[...] = (wide(first_ref[...]) + wide(arrived_ref[...])).astype(jnp.bfloat16)
-
-    @pl.when(jnp.logical_not(in_middle))
-    def _():
-        out_ref[...] = second_ref[...]
-
-
-def passing(plan, first, arrived, second, after):
-    return pl.pallas_call(
-        passing_kernel,
-        out_shape=jax.ShapeDtypeStruct(first.shape, first.dtype),
-        in_specs=[SMEM] + [VMEM] * 3 + [ANYWHERE] * len(after),
-        out_specs=VMEM,
-        compiler_params=pltpu.CompilerParams(vmem_limit_bytes=4 * 2**20),
-        cost_estimate=COST,
-        name="passing",
-    )(plan, first, arrived, second, *after)
+    )(*arrays)
 
 
 def choice_kernel(plan_ref, middle_ref, end_ref, *refs):
@@ -709,7 +677,7 @@
 
     packed = prepare(who, key_gate, value_input, filter_taps, members, scale)
     input_parts = traded(packed, "ctx")
-    conv_parts = convolve(plan, input_parts, length, per_group, (total,))
+    conv_parts, turned, taps = convolve(plan, input_parts, length, per_group, (total,))
     *conv_parts, near, cross = held_until([*conv_parts, near, cross], ())
     far, skip = hop(near, ACROSS), hop(cross, OUTWARD)
     gated_out, convolved = gated(plan, traded(conv_parts, "ctx"), query_gate)
@@ -719,41 +687,44 @@
             plan, gated_out, out_weight, first, count, other, more, after, tiles, widths
         )
 
-    third_part = 2 * channels // 3 // 128 * 128
-    widths = (2 * channels - 2 * third_part, third_part, third_part)
-    given = product(FAR, 2, 1, tiles=2, widths=widths)
-    received = [swapped(part, "tp", 1) for part in given]
-    first, second = product(FAR, 2, 0, received, tiles=2)
+    quarter, half = channels // 4, channels // 2
+    given_far = product(FAR, 1, 1, tiles=2, widths=(3 * quarter, quarter))
+    received = [swapped(part, "tp", 1) for part in given_far]
+    (first,) = product(FAR, 1, 0, received, tiles=2)
     far, skip, near = held_until([far, skip, near], (first,))
     mixed = chosen(plan, far, first)
     arrived = hop(mixed, OUTWARD + INWARD)
-    beside = hop(second, ACROSS)
+    given_middle = product(MIDDLE, 1, 1, (), (mixed,), tiles=2, widths=(half, half))
+    received = [swapped(part, "tp", 1) for part in given_middle]
+    (second,) = product(MIDDLE, 1, 0, received, tiles=2)
     middle_block = added(cross, skip)
     blocks = [near, swapped(near, "tp", 1), middle_block]
-    total = cotangent_products(plan, 2 * NEAR, blocks, out_weight, total, after=(mixed,))
-    given = product(NEAR, 2, 1, (), (mixed,))
-    (arrived,) = held_until([arrived], (total, given[0]))
-    passed = passing(plan, first, arrived, second, (beside,))
-    jumped = hop(passed, ((0, 2), (1, 3), (2, 0), (3, 1)))
-
-    far_block, far_other = both([chosen(plan, far, arrived, (passed,))])
+    total = cotangent_products(plan, 2 * NEAR, blocks, out_weight, total, after=(second,))
+    given_near, given_own = product(NEAR, 2, 1, (), (second,))
+    (arrived,) = held_until([arrived], (total, given_near))
+    through = added(first, arrived)
+    two_a = hop(through, ACROSS)
+    (second,) = held_until([second], (arrived,))
+    two_b = hop(second, INWARD)
+
+    far_block, far_other = both([chosen(plan, far, arrived, (through,))])
     blocks = [swapped(middle_block, "tp", 1), far_block]
     total = cotangent_products(
-        plan, 2 * MIDDLE + 1, blocks, out_weight, total, after=(passed,)
-    )
-    received = [swapped(part, "tp", 1) for part in given]
+        plan, 2 * MIDDLE + 1, blocks, out_weight, total, after=(through,)
+    )
     grad_query, *grad_parts = last_cotangents(
-        plan, 2 * FAR + 1, far_other, out_weight, total, convolved, query_gate, members, received
-    )
-    widths = (channels // 2, channels // 2, channels)
-    *halves, own = product(NEAR, 2, 0, received, (grad_parts[0],), widths=widths)
-    halves_near = [hop(half, INWARD + OUTWARD) for half in halves]
+        plan, 2 * FAR + 1, far_other, out_weight, total, convolved, query_gate, members, ()
+    )
+    received = (swapped(given_near, "tp", 1), swapped(given_own, "tp", 1))
+    third, own = product(NEAR, 2, 0, received, (grad_parts[0],))
     grad_parts = traded(grad_parts, "ctx")
-    back_parts = correlate(plan, input_parts, grad_parts, per_group, scale, (own,))
-    back_parts = held_until(back_parts, (halves_near[0],))
-    projected = added(own, beside, jumped, halves=halves_near)
+
+    two_a, two_b = held_until([two_a, two_b], tuple(grad_parts[1:]))
+    third, second = added(third, two_a), added(second, two_b)
+    back_parts = correlate(plan, turned, taps, grad_parts, per_group, scale, (third, second))
+    projected = added(own, hop(third, OUTWARD + INWARD), hop(second, ACROSS))
     back_parts = traded(back_parts, "ctx")
-    return projected, grad_query, *finished(plan, back_parts, key_gate, value_input, groups, (projected,))
+    return projected, grad_query, *finished(plan, back_parts, key_gate, value_input, groups, (in_hbm(projected),))
 
 
 def anywhere(
@@ -766,7 +737,8 @@
     plan = jnp.full((POSITION + 1,), position, jnp.int32)
     packed = packed_parts(position, key_gate, value_input, filter_taps, members, scale)
     input_parts = traded(packed, "ctx")
-    conv_parts = traded(convolve(plan, input_parts, length, per_group), "ctx")
+    conv_parts, turned, taps = convolve(plan, input_parts, length, per_group)
+    conv_parts = traded(conv_parts, "ctx")
     convolved = joined(conv_parts, position, 1)
     gated_out = (wide(query_gate) * wide(convolved)).astype(jnp.bfloat16)
     partial_value = jnp.dot(gated_out, out_weight, preferred_element_type=jnp.float32)
@@ -782,7 +754,7 @@
     grad_query = (wide(dgated) * wide(convolved)).astype(jnp.bfloat16)
     conv_grad = (wide(dgated) * wide(query_gate)).astype(jnp.bfloat16)
     grad_parts = traded(cut(conv_grad, position, members, 1), "ctx")
-    back_parts = correlate(plan, input_parts, grad_parts, per_group, scale)
+    back_parts = correlate(plan, turned, taps, grad_parts, per_group, scale)
     back_parts = traded(back_parts, "ctx")
     return (
         projected,

time: 163 us -> 151 us (0.926)
  waiting for transfers between devices: 58.4 us -> 43.5 us
  Pallas kernels: 68.3 us -> 70.9 us
  starting transfers between devices: 33.4 us -> 35.5 us
    ppermute x21 -> x22, waiting for transfers between devices: 29.6 us -> 21.5 us  [swapped(): return lax.ppermute(array, axis, [(i, i ^ step) for i in range(size)])]
    ppermute x9, waiting for transfers between devices: 28.8 us -> 22.1 us  [hop(): lax.ppermute(array, 'tp', [(2 * i + core, 2 * j + core) for i, j in pairs...]
    pallas_call x4 -> x6, Pallas kernels: 21.2 us -> 23.8 us  [column_products(): pl.pallas_call(functools.partial(product_kernel, steps, [part.shape[1] fo...]
    ppermute x21 -> x22, starting transfers between devices: 16.2 us -> 16.8 us  [swapped(): return lax.ppermute(array, axis, [(i, i ^ step) for i in range(size)])]
  transfers between devices with their start and end apart: 30 -> 31, of which waited for: 14 -> 11; matrix products, arithmetic and copies ran while one was open for 0% -> 0% of each run, Pallas kernels for 41% -> 45%
where the time goes in v11:
time: 151 us
  Pallas kernels  70.9 us (47%)
  waiting for transfers between devices  43.5 us (29%)
  starting transfers between devices  35.5 us (24%)
    pallas_call x6, Pallas kernels, column_products(): pl.pallas_call(functools.partial(product_kernel, steps, [part.shape[1] fo...  23.8 us
    ppermute x9, waiting for transfers between devices, hop(): lax.ppermute(array, 'tp', [(2 * i + core, 2 * j + core) for i, j in pairs...  22.1 us
    ppermute x22, waiting for transfers between devices, swapped(): return lax.ppermute(array, axis, [(i, i ^ step) for i in range(size)])  21.5 us
    ppermute x9, starting transfers between devices, hop(): lax.ppermute(array, 'tp', [(2 * i + core, 2 * j + core) for i, j in pairs...  18.7 us
    ppermute x22, starting transfers between devices, swapped(): return lax.ppermute(array, axis, [(i, i ^ step) for i in range(size)])  16.8 us
    pallas_call x3, Pallas kernels, cotangent_products(): pl.pallas_call(functools.partial(cotangent_kernel, count, begin), out_sha...  16.2 us
    pallas_call x1, Pallas kernels, correlate(): pl.pallas_call(functools.partial(backward_kernel, members, per_group, sca...  9.53 us
    pallas_call x1, Pallas kernels, convolve(): pl.pallas_call(functools.partial(forward_kernel, members, per_group, widt...  5.65 us
  transfers between devices with their start and end apart: 31, of which 11 were waited for; matrix products, arithmetic and copies ran while one was open for 0% of the time, Pallas kernels for 45%

profile of v11, /device:TPU:0, one launch (start us, length us, event | category | flops | bytes accessed | tf_op | source)
XLA Modules:
  0.0 151.0 jit_solution(6080221376786271118)
XLA Ops:
  1.2 2.7 %collective-permute-start.4 = (bf16[512,1024]{1,0:T(8,128)(2,1)}, bf16[512,1024]{1,0:T(8,128)(2,1)S(1)}, u32[]{:S(2)}, u32[]{:S(2)}) collective-permute-start(bf16[512,1024]{1,0:T(8,128)(2,1)} %refs_0_.1), channel_id=1, source_target_pairs={{0,2},{1,3},{6,4},{7,5},{2,0},{3,1},{4,6},{5,7},{8,10},{9,11},{14,... | collective-permute-start | bytes 3145736 | tf_op jit(solution)/shard_map/ppermute | solution.py:349
  4.6 2.6 %gated_input.1 = (bf16[544,256]{1,0:T(8,128)(2,1)S(1)}, bf16[544,256]{1,0:T(8,128)(2,1)S(1)}, bf16[544,256]{1,0:T(8,128)(2,1)S(1)}, bf16[544,256]{1,0:T(8,128)(2,1)S(1)}) custom-call(s32[2]{0:T(128)S(1)} %pad_add_fusion.who_ref, bf16[512,1024]{1,0:T(8,128)(2,1)} %refs_4_.3, bf16[512,1024]{1,0:T(8,128)(2,1)} %refs_5_.1, f32[64,512]{1,0:T(8,128)} %bitcast.4), custom_call_target="tpu_custom_call" | custom-call | flops 1048576 | bytes 4096 | tf_op jit(solution)/shard_map/gated_input/pallas_call | solution.py:259
  12.0 5.0 %cotangent_blocks.3.refs_4_.refs_3_ = f32[512,1024]{1,0:T(8,128)S(1)} custom-call(s32[10]{0:T(128)S(1)} %plan.1._.plan_ref, bf16[1024,8192]{1,0:T(8,128)(2,1)} %weight_ref.19, bf16[512,1024]{1,0:T(8,128)(2,1)S(1)} %copy-done.3, bf16[512,1024]{1,0:T(8,128)(2,1)} %collective-permute-done.3.refs_1_), custom_call_target="tpu_custom_call" | custom-call | flops 1048576 | bytes 4096 | tf_op jit(solution)/shard_map/cotangent_blocks/pallas_call | solution.py:614
  17.0 6.2 %collective-permute-done.1.refs_2_ = bf16[544,256]{1,0:T(8,128)(2,1)S(1)} collective-permute-done((bf16[544,256]{1,0:T(8,128)(2,1)S(1)}, bf16[544,256]{1,0:T(8,128)(2,1)S(1)}, u32[]{:S(2)}, u32[]{:S(2)}) %collective-permute-start.1) | collective-permute-done | bytes 278560 | tf_op jit(solution)/shard_map/ppermute | solution.py:316
  23.2 5.6 %causal_conv.1 = (bf16[512,256]{1,0:T(8,128)(2,1)S(1)}, bf16[512,256]{1,0:T(8,128)(2,1)S(1)}, bf16[512,256]{1,0:T(8,128)(2,1)S(1)}, bf16[512,256]{1,0:T(8,128)(2...) custom-call(s32[10]{0:T(128)S(1)} %plan.1._.plan_ref, bf16[544,256]{1,0:T(8,128)(2,1)S(1)} %get-tuple-element.48.refs_0_, ...), custom_call_target="tpu_custom_call" | custom-call | flops 1048576 | bytes 4096 | tf_op jit(solution)/shard_map/causal_conv/pallas_call | solution.py:180
  34.5 3.7 %collective-permute-done.6.refs_1_ = bf16[512,256]{1,0:T(8,128)(2,1)S(1)} collective-permute-done((bf16[512,256]{1,0:T(8,128)(2,1)S(1)}, bf16[512,256]{1,0:T(8,128)(2,1)S(1)}, u32[]{:S(2)}, u32[]{:S(2)}) %collective-permute-start.6) | collective-permute-done | bytes 262176 | tf_op jit(solution)/shard_map/ppermute | solution.py:316
  38.2 4.9 %collective-permute-done.7.refs_2_ = bf16[512,256]{1,0:T(8,128)(2,1)S(1)} collective-permute-done((bf16[512,256]{1,0:T(8,128)(2,1)S(1)}, bf16[512,256]{1,0:T(8,128)(2,1)S(1)}, u32[]{:S(2)}, u32[]{:S(2)}) %collective-permute-start.7) | collective-permute-done | bytes 262176 | tf_op jit(solution)/shard_map/ppermute | solution.py:316
  44.0 3.4 %projection_blocks.6 = (bf16[512,768]{1,0:T(8,128)(2,1)S(1)}, bf16[512,256]{1,0:T(8,128)(2,1)S(1)}) custom-call(s32[10]{0:T(128)S(1)} %plan.1._.plan_ref, bf16[512,1024]{1,0:T(8,128)(2,1)S(1)} %get-tuple-element.60.data_ref, bf16[1024,8192]{1,0:T(8,128)(2,1)} %weight_ref.19), custom_call_target="tpu_custom_call" | custom-call | flops 1048576 | bytes 4096 | tf_op jit(solution)/shard_map/projection_blocks/pallas_call | solution.py:515
  50.1 3.5 %projection_blocks.7.refs_3_.end_ref.refs_0_ = bf16[512,1024]{1,0:T(8,128)(2,1)S(1)} custom-call(s32[10]{0:T(128)S(1)} %plan.1._.plan_ref, bf16[512,1024]{1,0:T(8,128)(2,1)S(1)} %get-tuple-element.60.data_ref, bf16[1024,8192]{1,0:T(8,128)(2,1)} %weight_ref.19, bf16[512,768]{1,0:T(8,128)(2,1)S(1)} %collective-permute-done.11.refs_0_, ...), custom_call_target="tpu_custom_call" | custom-call | flops 1048576 | bytes 4096 | tf_op jit(solution)/shard_map/projection_blocks/pallas_call | solution.py:515
  53.6 5.9 %collective-permute-done.10.refs_1_ = bf16[512,1024]{1,0:T(8,128)(2,1)S(1)} collective-permute-done((bf16[512,1024]{1,0:T(8,128)(2,1)S(1)}, bf16[512,1024]{1,0:T(8,128)(2,1)S(1)}, u32[]{:S(2)}, u32[]{:S(2)}) %collective-permute-start.10) | collective-permute-done | bytes 1048608 | tf_op jit(solution)/shard_map/ppermute | solution.py:349
  60.3 3.8 %collective-permute-start.17 = (bf16[512,1024]{1,0:T(8,128)(2,1)S(1)}, bf16[512,1024]{1,0:T(8,128)(2,1)S(1)}, u32[]{:S(2)}, u32[]{:S(2)}) collective-permute-start(bf16[512,1024]{1,0:T(8,128)(2,1)S(1)} %chosen.2.refs_0_), channel_id=1, source_target_pairs={{2,0},{3,1},{4,6},{5,7},{0,2},{1,3},{6,4},{7,5},{10,8},{11,9},{12,... | collective-permute-start | bytes 3145736 | tf_op jit(solution)/shard_map/ppermute | solution.py:349
  64.7 3.4 %projection_blocks.8 = (bf16[512,512]{1,0:T(8,128)(2,1)S(1)}, bf16[512,512]{1,0:T(8,128)(2,1)S(1)}) custom-call(s32[10]{0:T(128)S(1)} %plan.1._.plan_ref, bf16[512,1024]{1,0:T(8,128)(2,1)S(1)} %get-tuple-element.60.data_ref, bf16[1024,8192]{1,0:T(8,128)(2,1)} %weight_ref.19, bf16[512,1024]{1,0:T(8,128)(2,1)S(1)} %chosen.2.refs_0_), custom_call_target="tpu_custom_call" | custom-call | flops 1048576 | bytes 4096 | tf_op jit(solution)/shard_map/projection_blocks/pallas_call | solution.py:515
  70.8 3.5 %projection_blocks.9.refs_0_.refs_4_ = bf16[512,1024]{1,0:T(8,128)(2,1)S(1)} custom-call(s32[10]{0:T(128)S(1)} %plan.1._.plan_ref, bf16[512,1024]{1,0:T(8,128)(2,1)S(1)} %get-tuple-element.60.data_ref, bf16[1024,8192]{1,0:T(8,128)(2,1)} %weight_ref.19, bf16[512,512]{1,0:T(8,128)(2,1)S(1)} %collective-permute-done.13.refs_0_, ...), custom_call_target="tpu_custom_call" | custom-call | flops 1048576 | bytes 4096 | tf_op jit(solution)/shard_map/projection_blocks/pallas_call | solution.py:515
  74.2 4.9 %projection_blocks.10 = (bf16[512,1024]{1,0:T(8,128)(2,1)S(1)}, bf16[512,1024]{1,0:T(8,128)(2,1)S(1)}) custom-call(s32[10]{0:T(128)S(1)} %plan.1._.plan_ref, bf16[512,1024]{1,0:T(8,128)(2,1)S(1)} %get-tuple-element.60.data_ref, bf16[1024,8192]{1,0:T(8,128)(2,1)} %weight_ref.19, bf16[512,1024]{1,0:T(8,128)(2,1)S(1)} %projection_blocks.9.refs_0_.refs_4_), custom_call_target="tpu_custom_call" | custom-call | flops 1048576 | bytes 4096 | tf_op jit(solution)/shard_map/projection_blocks/pallas_call | solution.py:515
  79.2 6.4 %cotangent_blocks.4.refs_1_.refs_2_ = f32[512,1024]{1,0:T(8,128)S(1)} custom-call(s32[10]{0:T(128)S(1)} %plan.1._.plan_ref, bf16[1024,8192]{1,0:T(8,128)(2,1)} %weight_ref.19, bf16[512,1024]{1,0:T(8,128)(2,1)S(1)} %get-tuple-element.70.refs_0_, bf16[512,1024]{1,0:T(8,128)(2,1)S(1)} %collective-permute-done.18.refs_1_, bf16[512,1024]{1,0:T(8,128)(2,1)S(1)} %added.5.refs_2_, ...), custom_call_target="tpu_custom_call" | custom-call | flops 1048576 | bytes 4096 | tf_op jit(solution)/shard_map/cotangent_blocks/pallas_call | solution.py:614
  85.5 2.4 %collective-permute-done.17.refs_0_ = bf16[512,1024]{1,0:T(8,128)(2,1)S(1)} collective-permute-done((bf16[512,1024]{1,0:T(8,128)(2,1)S(1)}, bf16[512,1024]{1,0:T(8,128)(2,1)S(1)}, u32[]{:S(2)}, u32[]{:S(2)}) %collective-permute-start.17) | collective-permute-done | bytes 1048608 | tf_op jit(solution)/shard_map/ppermute | solution.py:349
  89.5 3.7 %collective-permute-start.22 = (bf16[512,1024]{1,0:T(8,128)(2,1)S(1)}, bf16[512,1024]{1,0:T(8,128)(2,1)S(1)}, u32[]{:S(2)}, u32[]{:S(2)}) collective-permute-start(bf16[512,1024]{1,0:T(8,128)(2,1)S(1)} %held.8.refs_0_), channel_id=1, source_target_pairs={{0,2},{1,3},{6,4},{7,5},{8,10},{9,11},{14,12},{15,13},{16,18},{17,... | collective-permute-start | bytes 3145736 | tf_op jit(solution)/shard_map/ppermute | solution.py:349
  93.9 4.8 %cotangent_blocks.5.start_ref = f32[512,1024]{1,0:T(8,128)S(1)} custom-call(s32[10]{0:T(128)S(1)} %plan.1._.plan_ref, bf16[1024,8192]{1,0:T(8,128)(2,1)} %weight_ref.19, bf16[512,1024]{1,0:T(8,128)(2,1)S(1)} %collective-permute-done.20.refs_0_, bf16[512,1024]{1,0:T(8,128)(2,1)S(1)} %chosen.3.refs_1_, f32[512,1024]{1,0:T(8,128)S(1)} %cotangent_blocks.4.refs_1_.refs_2_, ...), custom_call_target="tpu_custom_call" | custom-call | flops 1048576 | bytes 4096 | tf_op jit(solution)/shard_map/cotangent_blocks/pallas_call | solution.py:614
  98.7 4.5 %cotangent_last.1 = (bf16[512,1024]{1,0:T(8,128)(2,1)}, bf16[512,256]{1,0:T(8,128)(2,1)S(1)}, bf16[512,256]{1,0:T(8,128)(2,1)S(1)}, bf16[512,256]{1,0:T(8,128)(2,1)S(1)}, bf16[512,256]{1,0:T(8,128)(2,1)S(1)}) custom-call(s32[10]{0:T(128)S(1)} %plan.1._.plan_ref, bf16[1024,8192]{1,0:T(8,128)(2,1)} %weight_ref.19, ...), custom_call_target="tpu_custom_call" | custom-call | flops 1048576 | bytes 4096 | tf_op jit(solution)/shard_map/cotangent_last/pallas_call | solution.py:580
  106.7 5.1 %projection_blocks.11 = (bf16[512,1024]{1,0:T(8,128)(2,1)S(1)}, bf16[512,1024]{1,0:T(8,128)(2,1)S(1)}) custom-call(s32[10]{0:T(128)S(1)} %plan.1._.plan_ref, bf16[512,1024]{1,0:T(8,128)(2,1)S(1)} %get-tuple-element.60.data_ref, bf16[1024,8192]{1,0:T(8,128)(2,1)} %weight_ref.19, bf16[512,1024]{1,0:T(8,128)(2,1)S(1)} %collective-permute-done.15.refs_0_, ...), custom_call_target="tpu_custom_call" | custom-call | flops 1048576 | bytes 4096 | tf_op jit(solution)/shard_map/projection_blocks/pallas_call | solution.py:515
  111.9 4.2 %collective-permute-done.22.refs_1_ = bf16[512,1024]{1,0:T(8,128)(2,1)S(1)} collective-permute-done((bf16[512,1024]{1,0:T(8,128)(2,1)S(1)}, bf16[512,1024]{1,0:T(8,128)(2,1)S(1)}, u32[]{:S(2)}, u32[]{:S(2)}) %collective-permute-start.22) | collective-permute-done | bytes 1048608 | tf_op jit(solution)/shard_map/ppermute | solution.py:349
  120.0 4.2 %collective-permute-start.26 = (bf16[512,1024]{1,0:T(8,128)(2,1)S(1)}, bf16[512,1024]{1,0:T(8,128)(2,1)S(1)}, u32[]{:S(2)}, u32[]{:S(2)}) collective-permute-start(bf16[512,1024]{1,0:T(8,128)(2,1)S(1)} %added.7.refs_4_), channel_id=1, source_target_pairs={{2,0},{3,1},{4,6},{5,7},{0,2},{1,3},{6,4},{7,5},{10,8},{11,9},{12,... | collective-permute-start | bytes 3145736 | tf_op jit(solution)/shard_map/ppermute | solution.py:349
  124.2 9.5 %causal_conv_grads.1 = (bf16[544,256]{1,0:T(8,128)(2,1)S(1)}, bf16[544,256]{1,0:T(8,128)(2,1)S(1)}, bf16[544,256]{1,0:T(8,128)(2,1)S(1)}, bf16[544,256]{1,0:T(8,128)(2,1)S(1)}) custom-call(s32[10]{0:T(128)S(1)} %plan.1._.plan_ref, bf16[4,256,512]{2,1,0:T(8,128)(2,1)S(1)} %get-tuple-element.82.in_scr, f32[16,2048]{1,0:T(8,128)S(1)} %get-tuple-element.83.tap_scr, ...), custom_call_target="tpu_custom_call" | custom-call | flops 1048576 | bytes 4096 | tf_op jit(solution)/shard_map/causal_conv_grads/pallas_call | solution.py:203
  137.3 9.6 %collective-permute-done.26.refs_1_ = bf16[512,1024]{1,0:T(8,128)(2,1)S(1)} collective-permute-done((bf16[512,1024]{1,0:T(8,128)(2,1)S(1)}, bf16[512,1024]{1,0:T(8,128)(2,1)S(1)}, u32[]{:S(2)}, u32[]{:S(2)}) %collective-permute-start.26) | collective-permute-done | bytes 1048608 | tf_op jit(solution)/shard_map/ppermute | solution.py:349
  (75 shorter events, 36.6 us)
Async XLA Ops:
  1.2 27.7 %collective-permute-start.4 = (bf16[512,1024]{1,0:T(8,128)(2,1)}, bf16[512,1024]{1,0:T(8,128)(2,1)S(1)}, u32[]{:S(2)}, u32[]{:S(2)}) collective-permute-start(bf16[512,1024]{1,0:T(8,128)(2,1)} %refs_0_.1), channel_id=1, source_target_pairs={{0,2},{1,3},{6,4},{7,5},{2,0},{3,1},{4,6},{5,7},{8,10},{9,11},{14,... | collective-permute-start | bytes 3145736 | tf_op jit(solution)/shard_map/ppermute | solution.py:349
  3.8 25.1 %collective-permute-start.5 = (bf16[512,1024]{1,0:T(8,128)(2,1)}, bf16[512,1024]{1,0:T(8,128)(2,1)S(1)}, u32[]{:S(2)}, u32[]{:S(2)}) collective-permute-start(bf16[512,1024]{1,0:T(8,128)(2,1)} %refs_0_.1), channel_id=1, source_target_pairs={{2,4},{3,5},{4,2},{5,3},{10,12},{11,13},{12,10},{13,11},{18,20},{1... | collective-permute-start | bytes 3145736 | tf_op jit(solution)/shard_map/ppermute | solution.py:349
  8.8 14.4 %collective-permute-start.1 = (bf16[544,256]{1,0:T(8,128)(2,1)S(1)}, bf16[544,256]{1,0:T(8,128)(2,1)S(1)}, u32[]{:S(2)}, u32[]{:S(2)}) collective-permute-start(bf16[544,256]{1,0:T(8,128)(2,1)S(1)} %get-tuple-element.50), channel_id=1, source_target_pairs={{0,16},{8,24},{16,0},{24,8},{1,17},{9,25},{17,1},{25,9},{2,18},{10... | collective-permute-start | bytes 835592 | tf_op jit(solution)/shard_map/ppermute | solution.py:316
  10.3 12.9 %collective-permute-start.2 = (bf16[544,256]{1,0:T(8,128)(2,1)S(1)}, bf16[544,256]{1,0:T(8,128)(2,1)S(1)}, u32[]{:S(2)}, u32[]{:S(2)}) collective-permute-start(bf16[544,256]{1,0:T(8,128)(2,1)S(1)} %get-tuple-element.51), channel_id=1, source_target_pairs={{0,24},{8,16},{16,8},{24,0},{1,25},{9,17},{17,9},{25,1},{2,26},{10... | collective-permute-start | bytes 835592 | tf_op jit(solution)/shard_map/ppermute | solution.py:316
  30.2 12.9 %collective-permute-start.7 = (bf16[512,256]{1,0:T(8,128)(2,1)S(1)}, bf16[512,256]{1,0:T(8,128)(2,1)S(1)}, u32[]{:S(2)}, u32[]{:S(2)}) collective-permute-start(bf16[512,256]{1,0:T(8,128)(2,1)S(1)} %get-tuple-element.58), channel_id=1, source_target_pairs={{0,16},{8,24},{16,0},{24,8},{1,17},{9,25},{17,1},{25,9},{2,18},{10... | collective-permute-start | bytes 786440 | tf_op jit(solution)/shard_map/ppermute | solution.py:316
  31.0 12.1 %collective-permute-start.8 = (bf16[512,256]{1,0:T(8,128)(2,1)S(1)}, bf16[512,256]{1,0:T(8,128)(2,1)S(1)}, u32[]{:S(2)}, u32[]{:S(2)}) collective-permute-start(bf16[512,256]{1,0:T(8,128)(2,1)S(1)} %get-tuple-element.59), channel_id=1, source_target_pairs={{0,24},{8,16},{16,8},{24,0},{1,25},{9,17},{17,9},{25,1},{2,26},{10... | collective-permute-start | bytes 786440 | tf_op jit(solution)/shard_map/ppermute | solution.py:316
  32.5 27.0 %collective-permute-start.10 = (bf16[512,1024]{1,0:T(8,128)(2,1)S(1)}, bf16[512,1024]{1,0:T(8,128)(2,1)S(1)}, u32[]{:S(2)}, u32[]{:S(2)}) collective-permute-start(bf16[512,1024]{1,0:T(8,128)(2,1)S(1)} %get-tuple-element.62.refs_0_), channel_id=1, source_target_pairs={{2,0},{3,1},{4,6},{5,7},{10,8},{11,9},{12,14},{13,15},{18,16},{19,... | collective-permute-start | bytes 3145736 | tf_op jit(solution)/shard_map/ppermute | solution.py:349
  33.8 25.7 %collective-permute-start.9 = (bf16[512,1024]{1,0:T(8,128)(2,1)S(1)}, bf16[512,1024]{1,0:T(8,128)(2,1)S(1)}, u32[]{:S(2)}, u32[]{:S(2)}) collective-permute-start(bf16[512,1024]{1,0:T(8,128)(2,1)S(1)} %get-tuple-element.61.refs_2_), channel_id=1, source_target_pairs={{2,4},{3,5},{4,2},{5,3},{10,12},{11,13},{12,10},{13,11},{18,20},{1... | collective-permute-start | bytes 3145736 | tf_op jit(solution)/shard_map/ppermute | solution.py:349
  59.5 19.7 %collective-permute-start.18 = (bf16[512,1024]{1,0:T(8,128)(2,1)S(1)}, bf16[512,1024]{1,0:T(8,128)(2,1)S(1)}, u32[]{:S(2)}, u32[]{:S(2)}) collective-permute-start(bf16[512,1024]{1,0:T(8,128)(2,1)S(1)} %get-tuple-element.70.refs_0_), channel_id=1, source_target_pairs={{0,1},{1,0},{2,3},{3,2},{4,5},{5,4},{6,7},{7,6},{8,9},{9,8},{10,11... | collective-permute-start | bytes 3145736 | tf_op jit(solution)/shard_map/ppermute | solution.py:316
  60.3 27.6 %collective-permute-start.17 = (bf16[512,1024]{1,0:T(8,128)(2,1)S(1)}, bf16[512,1024]{1,0:T(8,128)(2,1)S(1)}, u32[]{:S(2)}, u32[]{:S(2)}) collective-permute-start(bf16[512,1024]{1,0:T(8,128)(2,1)S(1)} %chosen.2.refs_0_), channel_id=1, source_target_pairs={{2,0},{3,1},{4,6},{5,7},{0,2},{1,3},{6,4},{7,5},{10,8},{11,9},{12,... | collective-permute-start | bytes 3145736 | tf_op jit(solution)/shard_map/ppermute | solution.py:349
  64.4 28.8 %collective-permute-start.20 = (bf16[512,1024]{1,0:T(8,128)(2,1)S(1)}, bf16[512,1024]{1,0:T(8,128)(2,1)S(1)}, u32[]{:S(2)}, u32[]{:S(2)}) collective-permute-start(bf16[512,1024]{1,0:T(8,128)(2,1)S(1)} %added.5.refs_2_), channel_id=1, source_target_pairs={{0,1},{1,0},{2,3},{3,2},{4,5},{5,4},{6,7},{7,6},{8,9},{9,8},{10,11... | collective-permute-start | bytes 3145736 | tf_op jit(solution)/shard_map/ppermute | solution.py:316
  88.8 9.9 %collective-permute-start.19 = (bf16[512,1024]{1,0:T(8,128)(2,1)S(1)}, bf16[512,1024]{1,0:T(8,128)(2,1)S(1)}, u32[]{:S(2)}, u32[]{:S(2)}) collective-permute-start(bf16[512,1024]{1,0:T(8,128)(2,1)S(1)} %chosen.3.refs_1_), channel_id=1, source_target_pairs={{0,1},{1,0},{2,3},{3,2},{4,5},{5,4},{6,7},{7,6},{8,9},{9,8},{10,11... | collective-permute-start | bytes 3145736 | tf_op jit(solution)/shard_map/ppermute | solution.py:316
  88.9 15.8 %collective-permute-start.15 = (bf16[512,1024]{1,0:T(8,128)(2,1)S(1)}, bf16[512,1024]{1,0:T(8,128)(2,1)S(1)}, u32[]{:S(2)}, u32[]{:S(2)}) collective-permute-start(bf16[512,1024]{1,0:T(8,128)(2,1)S(1)} %get-tuple-element.68.refs_2_), channel_id=1, source_target_pairs={{0,1},{1,0},{2,3},{3,2},{4,5},{5,4},{6,7},{7,6},{8,9},{9,8},{10,11... | collective-permute-start | bytes 3145736 | tf_op jit(solution)/shard_map/ppermute | solution.py:316
  89.4 16.9 %collective-permute-start.16 = (bf16[512,1024]{1,0:T(8,128)(2,1)S(1)}, bf16[512,1024]{1,0:T(8,128)(2,1)S(1)}, u32[]{:S(2)}, u32[]{:S(2)}) collective-permute-start(bf16[512,1024]{1,0:T(8,128)(2,1)S(1)} %get-tuple-element.69), channel_id=1, source_target_pairs={{0,1},{1,0},{2,3},{3,2},{4,5},{5,4},{6,7},{7,6},{8,9},{9,8},{10,11... | collective-permute-start | bytes 3145736 | tf_op jit(solution)/shard_map/ppermute | solution.py:316
  89.5 26.7 %collective-permute-start.22 = (bf16[512,1024]{1,0:T(8,128)(2,1)S(1)}, bf16[512,1024]{1,0:T(8,128)(2,1)S(1)}, u32[]{:S(2)}, u32[]{:S(2)}) collective-permute-start(bf16[512,1024]{1,0:T(8,128)(2,1)S(1)} %held.8.refs_0_), channel_id=1, source_target_pairs={{0,2},{1,3},{6,4},{7,5},{8,10},{9,11},{14,12},{15,13},{16,18},{17,... | collective-permute-start | bytes 3145736 | tf_op jit(solution)/shard_map/ppermute | solution.py:349
  93.2 22.9 %collective-permute-start.21 = (bf16[512,1024]{1,0:T(8,128)(2,1)S(1)}, bf16[512,1024]{1,0:T(8,128)(2,1)S(1)}, u32[]{:S(2)}, u32[]{:S(2)}) collective-permute-start(bf16[512,1024]{1,0:T(8,128)(2,1)S(1)} %added.6.refs_0_.refs_3_), channel_id=1, source_target_pairs={{2,4},{3,5},{4,2},{5,3},{10,12},{11,13},{12,10},{13,11},{18,20},{1... | collective-permute-start | bytes 3145736 | tf_op jit(solution)/shard_map/ppermute | solution.py:349
  103.2 12.9 %collective-permute-start.23 = (bf16[512,256]{1,0:T(8,128)(2,1)S(1)}, bf16[512,256]{1,0:T(8,128)(2,1)S(1)}, u32[]{:S(2)}, u32[]{:S(2)}) collective-permute-start(bf16[512,256]{1,0:T(8,128)(2,1)S(1)} %get-tuple-element.76), channel_id=1, source_target_pairs={{0,8},{8,0},{16,24},{24,16},{1,9},{9,1},{17,25},{25,17},{2,10},{10... | collective-permute-start | bytes 786440 | tf_op jit(solution)/shard_map/ppermute | solution.py:316
  104.7 13.7 %collective-permute-start.24 = (bf16[512,256]{1,0:T(8,128)(2,1)S(1)}, bf16[512,256]{1,0:T(8,128)(2,1)S(1)}, u32[]{:S(2)}, u32[]{:S(2)}) collective-permute-start(bf16[512,256]{1,0:T(8,128)(2,1)S(1)} %get-tuple-element.77), channel_id=1, source_target_pairs={{0,16},{8,24},{16,0},{24,8},{1,17},{9,25},{17,1},{25,9},{2,18},{10... | collective-permute-start | bytes 786440 | tf_op jit(solution)/shard_map/ppermute | solution.py:316
  106.2 12.2 %collective-permute-start.25 = (bf16[512,256]{1,0:T(8,128)(2,1)S(1)}, bf16[512,256]{1,0:T(8,128)(2,1)S(1)}, u32[]{:S(2)}, u32[]{:S(2)}) collective-permute-start(bf16[512,256]{1,0:T(8,128)(2,1)S(1)} %get-tuple-element.78), channel_id=1, source_target_pairs={{0,24},{8,16},{16,8},{24,0},{1,25},{9,17},{17,9},{25,1},{2,26},{10... | collective-permute-start | bytes 786440 | tf_op jit(solution)/shard_map/ppermute | solution.py:316
  118.7 18.5 %collective-permute-start.27 = (bf16[512,1024]{1,0:T(8,128)(2,1)S(1)}, bf16[512,1024]{1,0:T(8,128)(2,1)S(1)}, u32[]{:S(2)}, u32[]{:S(2)}) collective-permute-start(bf16[512,1024]{1,0:T(8,128)(2,1)S(1)} %added.8.refs_5_), channel_id=1, source_target_pairs={{2,4},{3,5},{4,2},{5,3},{10,12},{11,13},{12,10},{13,11},{18,20},{1... | collective-permute-start | bytes 3145736 | tf_op jit(solution)/shard_map/ppermute | solution.py:349
  120.0 26.9 %collective-permute-start.26 = (bf16[512,1024]{1,0:T(8,128)(2,1)S(1)}, bf16[512,1024]{1,0:T(8,128)(2,1)S(1)}, u32[]{:S(2)}, u32[]{:S(2)}) collective-permute-start(bf16[512,1024]{1,0:T(8,128)(2,1)S(1)} %added.7.refs_4_), channel_id=1, source_target_pairs={{2,0},{3,1},{4,6},{5,7},{0,2},{1,3},{6,4},{7,5},{10,8},{11,9},{12,... | collective-permute-start | bytes 3145736 | tf_op jit(solution)/shard_map/ppermute | solution.py:349
  133.7 14.9 %collective-permute-start.28 = (bf16[544,256]{1,0:T(8,128)(2,1)S(1)}, bf16[544,256]{1,0:T(8,128)(2,1)S(1)}, u32[]{:S(2)}, u32[]{:S(2)}) collective-permute-start(bf16[544,256]{1,0:T(8,128)(2,1)S(1)} %get-tuple-element.85), channel_id=1, source_target_pairs={{0,8},{8,0},{16,24},{24,16},{1,9},{9,1},{17,25},{25,17},{2,10},{10... | collective-permute-start | bytes 835592 | tf_op jit(solution)/shard_map/ppermute | solution.py:316
  135.3 13.3 %collective-permute-start.29 = (bf16[544,256]{1,0:T(8,128)(2,1)S(1)}, bf16[544,256]{1,0:T(8,128)(2,1)S(1)}, u32[]{:S(2)}, u32[]{:S(2)}) collective-permute-start(bf16[544,256]{1,0:T(8,128)(2,1)S(1)} %get-tuple-element.86), channel_id=1, source_target_pairs={{0,16},{8,24},{16,0},{24,8},{1,17},{9,25},{17,1},{25,9},{2,18},{10... | collective-permute-start | bytes 835592 | tf_op jit(solution)/shard_map/ppermute | solution.py:316
  136.8 11.8 %collective-permute-start.30 = (bf16[544,256]{1,0:T(8,128)(2,1)S(1)}, bf16[544,256]{1,0:T(8,128)(2,1)S(1)}, u32[]{:S(2)}, u32[]{:S(2)}) collective-permute-start(bf16[544,256]{1,0:T(8,128)(2,1)S(1)} %get-tuple-element.87), channel_id=1, source_target_pairs={{0,24},{8,16},{16,8},{24,0},{1,25},{9,17},{17,9},{25,1},{2,26},{10... | collective-permute-start | bytes 835592 | tf_op jit(solution)/shard_map/ppermute | solution.py:316
  (11 other events, 67.6 us)

commit v12 on v11

--- a/solution.py
+++ b/solution.py
@@ -97,8 +97,8 @@
         outputs[step][...] = out_scr[position ^ step].T
 
 
-def backward_kernel(members, per_group, scale, width, plan_ref, in_scr, tap_scr, *refs):
-    cotangents = refs[:members]
+def backward_kernel(members, pieces, per_group, scale, width, plan_ref, in_scr, tap_scr, *refs):
+    cotangents = refs[:pieces]
     outputs = refs[-members - 4 : -4]
     cot_scr, out_scr, grad_scr, pad_scr = refs[-4:]
     position = plan_ref[POSITION]
@@ -109,7 +109,11 @@
     depth = blocks * per_group
     for step in range(members):
         at = position ^ step
-        cot_scr[at] = cotangents[step][...].T
+        rows = cotangents[step].shape[0]
+        for part in range(pieces // members):
+            cot_scr[at, :, part * rows : (part + 1) * rows] = cotangents[
+                part * members + step
+            ][...].T
     pad_scr[...] = jnp.zeros_like(pad_scr)
     rows_of = lax.broadcasted_iota(jnp.int32, (BLOCK, BLOCK), 0)
     lanes_of = lax.broadcasted_iota(jnp.int32, (BLOCK, BLOCK), 1)
@@ -195,15 +199,14 @@
 
 
 def correlate(plan, turned, taps, cotangents, per_group, scale, after=()):
-    members = len(cotangents)
-    width, channels = cotangents[0].shape
+    members, channels, width = turned.shape
     length = members * width
     groups = channels // per_group
     rows = width + padded(groups) * width // channels
     return pl.pallas_call(
-        functools.partial(backward_kernel, members, per_group, scale, width),
+        functools.partial(backward_kernel, members, len(cotangents), per_group, scale, width),
         out_shape=[jax.ShapeDtypeStruct((rows, channels), jnp.bfloat16)] * members,
-        in_specs=[SMEM] + [VMEM] * (members + 2) + [ANYWHERE] * len(after),
+        in_specs=[SMEM] + [VMEM] * (len(cotangents) + 2) + [ANYWHERE] * len(after),
         out_specs=[VMEM] * members,
         scratch_shapes=[
             pltpu.VMEM((members, channels, width), jnp.bfloat16),
@@ -529,103 +532,64 @@
     )(plan, data, in_hbm(out_weight), *more, *after)
 
 
-def cotangent_kernel(count, begin, _, weight_ref, *refs):
-    blocks, refs = refs[:count], refs[count:]
+def cotangent_kernel(members, plan_ref, data_ref, weight_ref, conv_ref, query_ref, *refs):
+    grad_ref, parts = refs[-3 - members], refs[-2 - members : -2]
+    total, cot_scr = refs[-2:]
     step = pl.program_id(0)
-    total = refs[-1]
-
-    for number, block in enumerate(blocks):
-
-        @pl.when(step == number)
-        def _(number=number, block=block):
-            product = lax.dot_general(
-                block[...], weight_ref[...], NT, preferred_element_type=jnp.float32
-            )
-            if number == 0:
-                total[...] = product if begin else refs[0][...] + product
-            else:
-                total[...] += product
-
-
-def last_cotangent_kernel(
-    members, plan_ref, weight_ref, block_ref, start_ref, conv_ref, query_ref, *refs
-):
-    parts, cot_scr = refs[-1 - members : -1], refs[-1]
-    grad_ref = refs[-2 - members]
     product = lax.dot_general(
-        block_ref[...], weight_ref[...], NT, preferred_element_type=jnp.float32
+        data_ref[...], weight_ref[...], NT, preferred_element_type=jnp.float32
     )
-    dgated = wide((start_ref[...] + product).astype(jnp.bfloat16))
-    grad_ref[...] = (dgated * wide(conv_ref[...])).astype(jnp.bfloat16)
-    cot_scr[...] = (dgated * wide(query_ref[...])).astype(jnp.bfloat16)
-    share = parts[0].shape[1]
-    odd = plan_ref[POSITION] % 2
-    for step in range(0, members, 2):
-
-        @pl.when(pl.program_id(0) == step // 2)
-        def _(step=step):
-            parts[step][...] = cot_scr[:, pl.ds(pl.multiple_of(odd * share, share), share)]
-            parts[step + 1][...] = cot_scr[
-                :, pl.ds(pl.multiple_of((1 - odd) * share, share), share)
-            ]
-
-
-def last_cotangents(
-    plan, first, block, out_weight, start, convolved, query_gate, members, after
-):
-    rows, width = block.shape
-    channels = out_weight.shape[0]
+
+    @pl.when(step == 0)
+    def _():
+        total[...] = product
+
+    @pl.when(step > 0)
+    def _():
+        total[...] += product
+
+    @pl.when(step == pl.num_programs(0) - 1)
+    def _():
+        dgated = wide(total[...].astype(jnp.bfloat16))
+        grad_ref[...] = (dgated * wide(conv_ref[...])).astype(jnp.bfloat16)
+        cot_scr[...] = (dgated * wide(query_ref[...])).astype(jnp.bfloat16)
+        share = parts[0].shape[1]
+        for number in range(members):
+            start = pl.multiple_of((plan_ref[POSITION] ^ number) * share, share)
+            parts[number][...] = cot_scr[:, pl.ds(start, share)]
+
+
+def cotangents(plan, number, gathered, out_weight, convolved, query_gate, members, begun, after):
+    rows, depth = gathered.shape
+    length, channels = convolved.shape
     share = channels // members
-    pair = pl.BlockSpec((rows, 2 * share), lambda i, at: (0, at[POSITION] // 2 ^ i))
-    return pl.pallas_call(
-        functools.partial(last_cotangent_kernel, members),
-        out_shape=[jax.ShapeDtypeStruct((rows, channels), jnp.bfloat16)]
+    tile = min(depth, 1024)
+    place = pl.BlockSpec((rows, channels), lambda i, at: (number, 0))
+    return pl.pallas_call(
+        functools.partial(cotangent_kernel, members),
+        out_shape=[jax.ShapeDtypeStruct((length, channels), jnp.bfloat16)]
         + [jax.ShapeDtypeStruct((rows, share), jnp.bfloat16)] * members,
         grid_spec=pltpu.PrefetchScalarGridSpec(
             num_scalar_prefetch=1,
-            grid=(members // 2,),
+            grid=(depth // tile,),
             in_specs=[
-                pl.BlockSpec((2 * share, width), lambda i, at: (at[POSITION] // 2 ^ i, at[first])),
-                VMEM,
-                pair,
-                pair,
-                pair,
+                pl.BlockSpec((rows, tile), lambda i, at: (0, i)),
+                pl.BlockSpec((channels, tile), lambda i, at: (0, i)),
+                place,
+                place,
             ]
-            + [ANYWHERE] * len(after),
-            out_specs=[pair] + [VMEM] * members,
-            scratch_shapes=[pltpu.VMEM((rows, 2 * share), jnp.bfloat16)],
+            + [ANYWHERE] * (len(begun) + len(after)),
+            out_specs=[place] + [VMEM] * members,
+            scratch_shapes=[
+                pltpu.VMEM((rows, channels), jnp.float32),
+                pltpu.VMEM((rows, channels), jnp.bfloat16),
+            ],
         ),
+        input_output_aliases={5: 0} if begun else {},
         compiler_params=pltpu.CompilerParams(vmem_limit_bytes=24 * 2**20),
         cost_estimate=COST,
-        name="cotangent_last",
-    )(plan, in_hbm(out_weight), block, start, convolved, query_gate, *after)
-
-
-def both(blocks):
-    return [part for block in blocks for part in (block, swapped(block, "tp", 1))]
-
-
-def cotangent_products(plan, first, parts, out_weight, start=None, after=()):
-    rows, width = parts[0].shape
-    channels = out_weight.shape[0]
-    count = len(parts)
-    begin = start is None
-    extra = () if begin else (start,)
-    return pl.pallas_call(
-        functools.partial(cotangent_kernel, count, begin),
-        out_shape=jax.ShapeDtypeStruct((rows, channels), jnp.float32),
-        grid_spec=pltpu.PrefetchScalarGridSpec(
-            num_scalar_prefetch=1,
-            grid=(count,),
-            in_specs=[pl.BlockSpec((channels, width), lambda i, at: (0, at[first + i]))]
-            + [VMEM] * (count + len(extra))
-            + [ANYWHERE] * len(after),
-            out_specs=VMEM,
-        ),
-        compiler_params=pltpu.CompilerParams(vmem_limit_bytes=16 * 2**20),
-        cost_estimate=COST,
-        name="cotangent_blocks",
-    )(plan, in_hbm(out_weight), *parts, *extra, *after)
+        name="cotangents",
+    )(plan, in_hbm(gathered), in_hbm(out_weight), convolved, query_gate, *begun, *after)
 
 
 def packed_parts(position, key_gate, value_input, filter_taps, members, scale):
@@ -672,14 +636,15 @@
     per_group = channels // groups
     who = jnp.stack([lax.axis_index("ctx"), lax.axis_index("tp")]).astype(jnp.int32)
     plan = planned(who)
-    near, cross = hop(out_grad, INWARD + OUTWARD), hop(out_grad, ACROSS)
-    total = cotangent_products(plan, 2 * OWN, both([out_grad]), out_weight)
-
+    count = 2
+    rows = length // count
+    gathered = [
+        lax.all_gather(out_grad[part * rows : (part + 1) * rows], "tp", axis=1, tiled=True)
+        for part in range(count)
+    ]
     packed = prepare(who, key_gate, value_input, filter_taps, members, scale)
     input_parts = traded(packed, "ctx")
-    conv_parts, turned, taps = convolve(plan, input_parts, length, per_group, (total,))
-    *conv_parts, near, cross = held_until([*conv_parts, near, cross], ())
-    far, skip = hop(near, ACROSS), hop(cross, OUTWARD)
+    conv_parts, turned, taps = convolve(plan, input_parts, length, per_group)
     gated_out, convolved = gated(plan, traded(conv_parts, "ctx"), query_gate)
 
     def product(first, count, other, more=(), after=(), tiles=1, widths=()):
@@ -687,39 +652,39 @@
             plan, gated_out, out_weight, first, count, other, more, after, tiles, widths
         )
 
-    quarter, half = channels // 4, channels // 2
-    given_far = product(FAR, 1, 1, tiles=2, widths=(3 * quarter, quarter))
-    received = [swapped(part, "tp", 1) for part in given_far]
-    (first,) = product(FAR, 1, 0, received, tiles=2)
-    far, skip, near = held_until([far, skip, near], (first,))
-    mixed = chosen(plan, far, first)
-    arrived = hop(mixed, OUTWARD + INWARD)
-    given_middle = product(MIDDLE, 1, 1, (), (mixed,), tiles=2, widths=(half, half))
-    received = [swapped(part, "tp", 1) for part in given_middle]
-    (second,) = product(MIDDLE, 1, 0, received, tiles=2)
-    middle_block = added(cross, skip)
-    blocks = [near, swapped(near, "tp", 1), middle_block]
-    total = cotangent_products(plan, 2 * NEAR, blocks, out_weight, total, after=(second,))
-    given_near, given_own = product(NEAR, 2, 1, (), (second,))
-    (arrived,) = held_until([arrived], (total, given_near))
-    through = added(first, arrived)
-    two_a = hop(through, ACROSS)
-    (second,) = held_until([second], (arrived,))
-    two_b = hop(second, INWARD)
-
-    far_block, far_other = both([chosen(plan, far, arrived, (through,))])
-    blocks = [swapped(middle_block, "tp", 1), far_block]
-    total = cotangent_products(
-        plan, 2 * MIDDLE + 1, blocks, out_weight, total, after=(through,)
-    )
-    grad_query, *grad_parts = last_cotangents(
-        plan, 2 * FAR + 1, far_other, out_weight, total, convolved, query_gate, members, ()
-    )
-    received = (swapped(given_near, "tp", 1), swapped(given_own, "tp", 1))
-    third, own = product(NEAR, 2, 0, received, (grad_parts[0],))
-    grad_parts = traded(grad_parts, "ctx")
-
-    two_a, two_b = held_until([two_a, two_b], tuple(grad_parts[1:]))
+    (given,) = product(FAR, 1, 1, tiles=2)
+    (first,) = product(FAR, 1, 0, [swapped(given, "tp", 1)], tiles=2)
+    one = hop(first, INWARD)
+    given = product(MIDDLE, 3, 1, (), (first,), widths=(3 * channels // 4,) * 4)
+    received = [swapped(part, "tp", 1) for part in given]
+    second, third, own = product(MIDDLE, 3, 0, received)
+    grad_query, grad_parts = (), []
+    after = own
+    for part in range(count):
+        if part == count - 1:
+            (one,) = held_until([one], (after,))
+            through = added(first, one)
+            two_a = hop(through, ACROSS)
+            (second,) = held_until([second], (one,))
+            two_b = hop(second, INWARD)
+            after = through
+        received = grad_parts[1:]
+        results = cotangents(
+            plan,
+            part,
+            gathered[part],
+            out_weight,
+            convolved,
+            query_gate,
+            members,
+            grad_query,
+            (after, *received),
+        )
+        grad_query, pieces = results[:1], results[1:]
+        after = pieces[0]
+        grad_parts += traded(pieces, "ctx")
+    (grad_query,) = grad_query
+    two_a, two_b = held_until([two_a, two_b], tuple(grad_parts[1 - members :]))
     third, second = added(third, two_a), added(second, two_b)
     back_parts = correlate(plan, turned, taps, grad_parts, per_group, scale, (third, second))
     projected = added(own, hop(third, OUTWARD + INWARD), hop(second, ACROSS))

time: 151 us -> 200 us (1.32)
  waiting for transfers between devices: 43.5 us -> 61.8 us
  between operations: 0.97 us -> 14.3 us
  local copies, waits for them, and re-layouts: 0.02 us -> 8.96 us
  Pallas kernels: 70.9 us -> 76.8 us
  starting transfers between devices: 35.5 us -> 37.5 us
    ppermute x22 -> x20, waiting for transfers between devices: 21.5 us -> 35.5 us  [swapped(): return lax.ppermute(array, axis, [(i, i ^ step) for i in range(size)])]
    all_gather x0 -> x2, waiting for transfers between devices: none -> 13.2 us  [in_line(): lax.all_gather(out_grad[part * rows:(part + 1) * rows], 'tp', axis=1, til...]
    ppermute x9 -> x5, waiting for transfers between devices: 22.1 us -> 12.3 us  [hop(): lax.ppermute(array, 'tp', [(2 * i + core, 2 * j + core) for i, j in pairs...]
    unnamed x8 -> x34, local copies, waits for them, and re-layouts: 0.02 us -> 6.64 us
    pallas_call x7 -> x3, Pallas kernels: 31.6 us -> 37 us  [the longest x2 27.5 us: cotangents(): pl.pallas_call(functools.partial(cotangent_kernel, members), out_shape=[j...]
    ppermute x22 -> x20, starting transfers between devices: 16.8 us -> 19.8 us  [swapped(): return lax.ppermute(array, axis, [(i, i ^ step) for i in range(size)])]
    pallas_call x5 -> x4, Pallas kernels: 2.9 us -> 5.82 us  [added(): pl.pallas_call(add_kernel, out_shape=jax.ShapeDtypeStruct((rows, width),...]
    pallas_call x6 -> x4, Pallas kernels: 23.8 us -> 21.3 us  [column_products(): pl.pallas_call(functools.partial(product_kernel, steps, [part.shape[1] fo...]
  transfers between devices with their start and end apart: 31 -> 27, of which waited for: 11 -> 15; matrix products, arithmetic and copies ran while one was open for 0% -> 0% of each run, Pallas kernels for 45% -> 36%
where the time goes in v12:
time: 200 us; the launch traced here: 199 us
  Pallas kernels  76.8 us (38%)
  waiting for transfers between devices  61.8 us (31%)
  starting transfers between devices  37.5 us (19%)
  between operations  14.3 us (7%)
  local copies, waits for them, and re-layouts  8.96 us (4%)
    ppermute x20, waiting for transfers between devices, swapped(): return lax.ppermute(array, axis, [(i, i ^ step) for i in range(size)])  35.5 us
    pallas_call x2, Pallas kernels, cotangents(): pl.pallas_call(functools.partial(cotangent_kernel, members), out_shape=[j...  27.5 us
    pallas_call x4, Pallas kernels, column_products(): pl.pallas_call(functools.partial(product_kernel, steps, [part.shape[1] fo...  21.3 us
    ppermute x20, starting transfers between devices, swapped(): return lax.ppermute(array, axis, [(i, i ^ step) for i in range(size)])  19.8 us
    ppermute x5, starting transfers between devices, hop(): lax.ppermute(array, 'tp', [(2 * i + core, 2 * j + core) for i, j in pairs...  17.6 us
    all_gather x2, waiting for transfers between devices, in_line(): lax.all_gather(out_grad[part * rows:(part + 1) * rows], 'tp', axis=1, til...  13.2 us
    ppermute x5, waiting for transfers between devices, hop(): lax.ppermute(array, 'tp', [(2 * i + core, 2 * j + core) for i, j in pairs...  12.3 us
    pallas_call x1, Pallas kernels, correlate(): pl.pallas_call(functools.partial(backward_kernel, members, len(cotangents...  9.54 us
  transfers between devices with their start and end apart: 27, of which 15 were waited for; matrix products, arithmetic and copies ran while one was open for 0% of the time, Pallas kernels for 36%

profile of v12, /device:TPU:0, one launch (start us, length us, event | category | flops | bytes accessed | tf_op | source)
XLA Modules:
  0.0 199.4 jit_solution(16036200070455273308)
XLA Ops:
  10.4 2.6 %gated_input.1 = (bf16[544,256]{1,0:T(8,128)(2,1)S(1)}, bf16[544,256]{1,0:T(8,128)(2,1)S(1)}, bf16[544,256]{1,0:T(8,128)(2,1)S(1)}, bf16[544,256]{1,0:T(8,128)(2,1)S(1)}) custom-call(s32[2]{0:T(128)S(1)} %pad_add_fusion.who_ref, bf16[512,1024]{1,0:T(8,128)(2,1)} %refs_4_.3, bf16[512,1024]{1,0:T(8,128)(2,1)} %refs_5_.1, f32[64,512]{1,0:T(8,128)} %bitcast.4), custom_call_target="tpu_custom_call" | custom-call | flops 1048576 | bytes 4096 | tf_op jit(solution)/shard_map/gated_input/pallas_call | solution.py:262
  13.0 3.0 %collective-permute-start = (bf16[544,256]{1,0:T(8,128)(2,1)S(1)}, bf16[544,256]{1,0:T(8,128)(2,1)S(1)}, u32[]{:S(2)}, u32[]{:S(2)}) collective-permute-start(bf16[544,256]{1,0:T(8,128)(2,1)S(1)} %get-tuple-element.44), channel_id=1, source_target_pairs={{0,8},{8,0},{16,24},{24,16},{1,9},{9,1},{17,25},{25,17},{2,10},{10... | collective-permute-start | bytes 835592 | tf_op jit(solution)/shard_map/ppermute | solution.py:319
  18.7 4.8 %collective-permute-done.refs_1_ = bf16[544,256]{1,0:T(8,128)(2,1)S(1)} collective-permute-done((bf16[544,256]{1,0:T(8,128)(2,1)S(1)}, bf16[544,256]{1,0:T(8,128)(2,1)S(1)}, u32[]{:S(2)}, u32[]{:S(2)}) %collective-permute-start) | collective-permute-done | bytes 278560 | tf_op jit(solution)/shard_map/ppermute | solution.py:319
  23.5 6.6 %collective-permute-done.1.refs_2_ = bf16[544,256]{1,0:T(8,128)(2,1)S(1)} collective-permute-done((bf16[544,256]{1,0:T(8,128)(2,1)S(1)}, bf16[544,256]{1,0:T(8,128)(2,1)S(1)}, u32[]{:S(2)}, u32[]{:S(2)}) %collective-permute-start.1) | collective-permute-done | bytes 278560 | tf_op jit(solution)/shard_map/ppermute | solution.py:319
  30.1 5.6 %causal_conv.1 = (bf16[512,256]{1,0:T(8,128)(2,1)S(1)}, bf16[512,256]{1,0:T(8,128)(2,1)S(1)}, bf16[512,256]{1,0:T(8,128)(2,1)S(1)}, bf16[512,256]{1,0:T(8,128)(2...) custom-call(s32[10]{0:T(128)S(1)} %plan.1.plan_ref._, bf16[544,256]{1,0:T(8,128)(2,1)S(1)} %get-tuple-element.43.refs_0_, ...), custom_call_target="tpu_custom_call" | custom-call | flops 1048576 | bytes 4096 | tf_op jit(solution)/shard_map/causal_conv/pallas_call | solution.py:184
  39.3 5.8 %collective-permute-done.3.refs_1_ = bf16[512,256]{1,0:T(8,128)(2,1)S(1)} collective-permute-done((bf16[512,256]{1,0:T(8,128)(2,1)S(1)}, bf16[512,256]{1,0:T(8,128)(2,1)S(1)}, u32[]{:S(2)}, u32[]{:S(2)}) %collective-permute-start.3) | collective-permute-done | bytes 262176 | tf_op jit(solution)/shard_map/ppermute | solution.py:319
  45.1 4.6 %collective-permute-done.4.refs_2_ = bf16[512,256]{1,0:T(8,128)(2,1)S(1)} collective-permute-done((bf16[512,256]{1,0:T(8,128)(2,1)S(1)}, bf16[512,256]{1,0:T(8,128)(2,1)S(1)}, u32[]{:S(2)}, u32[]{:S(2)}) %collective-permute-start.4) | collective-permute-done | bytes 262176 | tf_op jit(solution)/shard_map/ppermute | solution.py:319
  51.5 3.4 %projection_blocks.4 = bf16[512,1024]{1,0:T(8,128)(2,1)S(1)} custom-call(s32[10]{0:T(128)S(1)} %plan.1.plan_ref._, bf16[512,1024]{1,0:T(8,128)(2,1)S(1)} %get-tuple-element.51.data_ref, bf16[1024,8192]{1,0:T(8,128)(2,1)} %weight_ref.11), custom_call_target="tpu_custom_call" | custom-call | flops 1048576 | bytes 4096 | tf_op jit(solution)/shard_map/projection_blocks/pallas_call | solution.py:518
  55.0 2.6 %collective-permute-done.6.refs_0_ = bf16[512,1024]{1,0:T(8,128)(2,1)S(1)} collective-permute-done((bf16[512,1024]{1,0:T(8,128)(2,1)S(1)}, bf16[512,1024]{1,0:T(8,128)(2,1)S(1)}, u32[]{:S(2)}, u32[]{:S(2)}) %collective-permute-start.6) | collective-permute-done | bytes 1048608 | tf_op jit(solution)/shard_map/ppermute | solution.py:319
  57.7 3.5 %projection_blocks.5.refs_0_ = bf16[512,1024]{1,0:T(8,128)(2,1)S(1)} custom-call(s32[10]{0:T(128)S(1)} %plan.1.plan_ref._, bf16[512,1024]{1,0:T(8,128)(2,1)S(1)} %get-tuple-element.51.data_ref, bf16[1024,8192]{1,0:T(8,128)(2,1)} %weight_ref.11, bf16[512,1024]{1,0:T(8,128)(2,1)S(1)} %collective-permute-done.6.refs_0_), custom_call_target="tpu_custom_call" | custom-call | flops 1048576 | bytes 4096 | tf_op jit(solution)/shard_map/projection_blocks/pallas_call | solution.py:518
  61.2 3.5 %collective-permute-start.11 = (bf16[512,1024]{1,0:T(8,128)(2,1)S(1)}, bf16[512,1024]{1,0:T(8,128)(2,1)S(1)}, u32[]{:S(2)}, u32[]{:S(2)}) collective-permute-start(bf16[512,1024]{1,0:T(8,128)(2,1)S(1)} %projection_blocks.5.refs_0_), channel_id=1, source_target_pairs={{0,2},{1,3},{6,4},{7,5},{8,10},{9,11},{14,12},{15,13},{16,18},{17,... | collective-permute-start | bytes 3145736 | tf_op jit(solution)/shard_map/ppermute | solution.py:352
  64.7 6.8 %projection_blocks.6 = (bf16[512,768]{1,0:T(8,128)(2,1)S(1)}, bf16[512,768]{1,0:T(8,128)(2,1)S(1)}, bf16[512,768]{1,0:T(8,128)(2,1)S(1)}, bf16[512,768]{1,0:T(8,128)(2,1)S(1)}) custom-call(s32[10]{0:T(128)S(1)} %plan.1.plan_ref._, bf16[512,1024]{1,0:T(8,128)(2,1)S(1)} %get-tuple-element.51.data_ref, bf16[1024,8192]{1,0:T(8,128)(2,1)} %weight_ref.11, ...), custom_call_target="tpu_custom_call" | custom-call | flops 1048576 | bytes 4096 | tf_op jit(solution)/shard_map/projection_blocks/pallas_call | solution.py:518
  77.4 7.7 %projection_blocks.7 = (bf16[512,1024]{1,0:T(8,128)(2,1)}, bf16[512,1024]{1,0:T(8,128)(2,1)S(1)}, bf16[512,1024]{1,0:T(8,128)(2,1)S(1)}) custom-call(s32[10]{0:T(128)S(1)} %plan.1.plan_ref._, bf16[512,1024]{1,0:T(8,128)(2,1)S(1)} %get-tuple-element.51.data_ref, bf16[1024,8192]{1,0:T(8,128)(2,1)} %weight_ref.11, ...), custom_call_target="tpu_custom_call" | custom-call | flops 1048576 | bytes 4096 | tf_op jit(solution)/shard_map/projection_blocks/pallas_call | solution.py:518
  89.5 13.9 %cotangents.2 = (bf16[512,1024]{1,0:T(8,128)(2,1)}, bf16[256,256]{1,0:T(8,128)(2,1)S(1)}, bf16[256,256]{1,0:T(8,128)(2,1)}, bf16[256,256]{1,0:T(8,128)(2,1)}, bf16[256,256]{1,0:T(8,128)(2,1)}) custom-call(s32[10]{0:T(128)S(1)} %plan.1.plan_ref._, bf16[256,8192]{1,0:T(8,128)(2,1)} %all-gather.3.cloned.1.call-done.data_ref, bf16[1024,8192]{1,0:T(8,128)(2,1)} %weight_ref.11, ...), custom_call_target="tpu_custom_call" | custom-call | flops 1048576 | bytes 4096 | tf_op jit(solution)/shard_map/cotangents/pallas_call | solution.py:568
  103.4 3.4 %collective-permute-done.11.refs_0_ = bf16[512,1024]{1,0:T(8,128)(2,1)S(1)} collective-permute-done((bf16[512,1024]{1,0:T(8,128)(2,1)S(1)}, bf16[512,1024]{1,0:T(8,128)(2,1)S(1)}, u32[]{:S(2)}, u32[]{:S(2)}) %collective-permute-start.11) | collective-permute-done | bytes 1048608 | tf_op jit(solution)/shard_map/ppermute | solution.py:352
  108.5 4.4 %collective-permute-start.13 = (bf16[512,1024]{1,0:T(8,128)(2,1)}, bf16[512,1024]{1,0:T(8,128)(2,1)S(1)}, u32[]{:S(2)}, u32[]{:S(2)}) collective-permute-start(bf16[512,1024]{1,0:T(8,128)(2,1)} %held.4.refs_0_), channel_id=1, source_target_pairs={{0,2},{1,3},{6,4},{7,5},{8,10},{9,11},{14,12},{15,13},{16,18},{17,... | collective-permute-start | bytes 3145736 | tf_op jit(solution)/shard_map/ppermute | solution.py:352
  114.0 3.2 %collective-permute-start.16 = (bf16[256,256]{1,0:T(8,128)(2,1)}, bf16[256,256]{1,0:T(8,128)(2,1)S(1)}, u32[]{:S(2)}, u32[]{:S(2)}) collective-permute-start(bf16[256,256]{1,0:T(8,128)(2,1)} %get-tuple-element.64), channel_id=1, source_target_pairs={{0,24},{8,16},{16,8},{24,0},{1,25},{9,17},{17,9},{25,1},{2,26},{10... | collective-permute-start | bytes 393224 | tf_op jit(solution)/shard_map/ppermute | solution.py:319
  117.2 13.2 %all-gather.5.cloned.1.call-done.data_ref = bf16[256,8192]{1,0:T(8,128)(2,1)} async-done(((bf16[256,1024]{1,0:T(8,128)(2,1)}), bf16[256,8192]{1,0:T(8,128)(2,1)}) %all-gather.5.cloned.1.call-update) | async-done | bytes 4194320 | tf_op jit(solution)/shard_map/all_gather | solution.py:642
  131.7 13.6 %cotangents.3 = (bf16[512,1024]{1,0:T(8,128)(2,1)}, bf16[256,256]{1,0:T(8,128)(2,1)S(1)}, bf16[256,256]{1,0:T(8,128)(2,1)S(1)}, bf16[256,256]{1,0:T(8,128)(2,1)S(1)}, bf16[256,256]{1,0:T(8,128)(2,1)S(1)}) custom-call(s32[10]{0:T(128)S(1)} %plan.1.plan_ref._, ...), custom_call_target="tpu_custom_call", output_to_operand_aliasing={{0}: (5, {})} | custom-call | flops 1048576 | bytes 4096 | tf_op jit(solution)/shard_map/cotangents/pallas_call | solution.py:568
  151.0 3.9 %collective-permute-done.18.refs_3_.refs_6_ = bf16[256,256]{1,0:T(8,128)(2,1)S(1)} collective-permute-done((bf16[256,256]{1,0:T(8,128)(2,1)S(1)}, bf16[256,256]{1,0:T(8,128)(2,1)S(1)}, u32[]{:S(2)}, u32[]{:S(2)}) %collective-permute-start.18) | collective-permute-done | bytes 131104 | tf_op jit(solution)/shard_map/ppermute | solution.py:319
  158.4 7.8 %collective-permute-start.20 = (bf16[512,1024]{1,0:T(8,128)(2,1)S(1)}, bf16[512,1024]{1,0:T(8,128)(2,1)S(1)}, u32[]{:S(2)}, u32[]{:S(2)}) collective-permute-start(bf16[512,1024]{1,0:T(8,128)(2,1)S(1)} %added.5.refs_8_), channel_id=1, source_target_pairs={{2,0},{3,1},{4,6},{5,7},{0,2},{1,3},{6,4},{7,5},{10,8},{11,9},{12,... | collective-permute-start | bytes 3145736 | tf_op jit(solution)/shard_map/ppermute | solution.py:352
  166.3 9.5 %causal_conv_grads.1 = (bf16[544,256]{1,0:T(8,128)(2,1)S(1)}, bf16[544,256]{1,0:T(8,128)(2,1)S(1)}, bf16[544,256]{1,0:T(8,128)(2,1)S(1)}, bf16[544,256]{1,0:T(8,128)(2,1)S(1)}) custom-call(s32[10]{0:T(128)S(1)} %plan.1.plan_ref._, bf16[4,256,512]{2,1,0:T(8,128)(2,1)S(1)} %copy-done.10, f32[16,2048]{1,0:T(8,128)S(1)} %copy-done.16, ...), custom_call_target="tpu_custom_call" | custom-call | flops 1048576 | bytes 4096 | tf_op jit(solution)/shard_map/causal_conv_grads/pallas_call | solution.py:206
  179.4 8.9 %collective-permute-done.20.refs_1_ = bf16[512,1024]{1,0:T(8,128)(2,1)S(1)} collective-permute-done((bf16[512,1024]{1,0:T(8,128)(2,1)S(1)}, bf16[512,1024]{1,0:T(8,128)(2,1)S(1)}, u32[]{:S(2)}, u32[]{:S(2)}) %collective-permute-start.20) | collective-permute-done | bytes 1048608 | tf_op jit(solution)/shard_map/ppermute | solution.py:352
  190.2 2.3 %input_gradients.1 = (bf16[512,1024]{1,0:T(8,128)(2,1)}, bf16[512,1024]{1,0:T(8,128)(2,1)}, f32[64,512]{1,0:T(8,128)}) custom-call(s32[10]{0:T(128)S(1)} %plan.1.plan_ref._, bf16[544,256]{1,0:T(8,128)(2,1)S(1)} %get-tuple-element.74.refs_0_, bf16[544,256]{1,0:T(8,128)(2,1)S(1)} %collective-permute-done.22.refs_1_, ...), custom_call_target="tpu_custom_call" | custom-call | flops 1048576 | bytes 4096 | tf_op jit(solution)/shard_map/input_gradients/pallas_call | solution.py:305
  (87 shorter events, 40.3 us)
Async XLA Ops:
  7.2 79.9 %all-gather.3.cloned.1.call-start = ((), (), s32[]{:S(2)}) async-start(), calls=%async_computation | async-start | bytes 4718592 | tf_op jit(solution)/shard_map/all_gather | solution.py:642
  9.6 120.9 %all-gather.5.cloned.1.call-start = ((), (), s32[]{:S(2)}) async-start(), calls=%async_computation.1 | async-start | bytes 4718592 | tf_op jit(solution)/shard_map/all_gather | solution.py:642
  13.0 10.5 %collective-permute-start = (bf16[544,256]{1,0:T(8,128)(2,1)S(1)}, bf16[544,256]{1,0:T(8,128)(2,1)S(1)}, u32[]{:S(2)}, u32[]{:S(2)}) collective-permute-start(bf16[544,256]{1,0:T(8,128)(2,1)S(1)} %get-tuple-element.44), channel_id=1, source_target_pairs={{0,8},{8,0},{16,24},{24,16},{1,9},{9,1},{17,25},{25,17},{2,10},{10... | collective-permute-start | bytes 835592 | tf_op jit(solution)/shard_map/ppermute | solution.py:319
  16.0 14.1 %collective-permute-start.1 = (bf16[544,256]{1,0:T(8,128)(2,1)S(1)}, bf16[544,256]{1,0:T(8,128)(2,1)S(1)}, u32[]{:S(2)}, u32[]{:S(2)}) collective-permute-start(bf16[544,256]{1,0:T(8,128)(2,1)S(1)} %get-tuple-element.45), channel_id=1, source_target_pairs={{0,16},{8,24},{16,0},{24,8},{1,17},{9,25},{17,1},{25,9},{2,18},{10... | collective-permute-start | bytes 835592 | tf_op jit(solution)/shard_map/ppermute | solution.py:319
  17.5 12.6 %collective-permute-start.2 = (bf16[544,256]{1,0:T(8,128)(2,1)S(1)}, bf16[544,256]{1,0:T(8,128)(2,1)S(1)}, u32[]{:S(2)}, u32[]{:S(2)}) collective-permute-start(bf16[544,256]{1,0:T(8,128)(2,1)S(1)} %get-tuple-element.46), channel_id=1, source_target_pairs={{0,24},{8,16},{16,8},{24,0},{1,25},{9,17},{17,9},{25,1},{2,26},{10... | collective-permute-start | bytes 835592 | tf_op jit(solution)/shard_map/ppermute | solution.py:319
  35.8 9.3 %collective-permute-start.3 = (bf16[512,256]{1,0:T(8,128)(2,1)S(1)}, bf16[512,256]{1,0:T(8,128)(2,1)S(1)}, u32[]{:S(2)}, u32[]{:S(2)}) collective-permute-start(bf16[512,256]{1,0:T(8,128)(2,1)S(1)} %get-tuple-element.48), channel_id=1, source_target_pairs={{0,8},{8,0},{16,24},{24,16},{1,9},{9,1},{17,25},{25,17},{2,10},{10... | collective-permute-start | bytes 786440 | tf_op jit(solution)/shard_map/ppermute | solution.py:319
  37.1 12.6 %collective-permute-start.4 = (bf16[512,256]{1,0:T(8,128)(2,1)S(1)}, bf16[512,256]{1,0:T(8,128)(2,1)S(1)}, u32[]{:S(2)}, u32[]{:S(2)}) collective-permute-start(bf16[512,256]{1,0:T(8,128)(2,1)S(1)} %get-tuple-element.49), channel_id=1, source_target_pairs={{0,16},{8,24},{16,0},{24,8},{1,17},{9,25},{17,1},{25,9},{2,18},{10... | collective-permute-start | bytes 786440 | tf_op jit(solution)/shard_map/ppermute | solution.py:319
  37.9 11.8 %collective-permute-start.5 = (bf16[512,256]{1,0:T(8,128)(2,1)S(1)}, bf16[512,256]{1,0:T(8,128)(2,1)S(1)}, u32[]{:S(2)}, u32[]{:S(2)}) collective-permute-start(bf16[512,256]{1,0:T(8,128)(2,1)S(1)} %get-tuple-element.50), channel_id=1, source_target_pairs={{0,24},{8,16},{16,8},{24,0},{1,25},{9,17},{17,9},{25,1},{2,26},{10... | collective-permute-start | bytes 786440 | tf_op jit(solution)/shard_map/ppermute | solution.py:319
  61.2 45.6 %collective-permute-start.11 = (bf16[512,1024]{1,0:T(8,128)(2,1)S(1)}, bf16[512,1024]{1,0:T(8,128)(2,1)S(1)}, u32[]{:S(2)}, u32[]{:S(2)}) collective-permute-start(bf16[512,1024]{1,0:T(8,128)(2,1)S(1)} %projection_blocks.5.refs_0_), channel_id=1, source_target_pairs={{0,2},{1,3},{6,4},{7,5},{8,10},{9,11},{14,12},{15,13},{16,18},{17,... | collective-permute-start | bytes 3145736 | tf_op jit(solution)/shard_map/ppermute | solution.py:352
  72.1 4.2 %collective-permute-start.8 = (bf16[512,768]{1,0:T(8,128)(2,1)S(1)}, bf16[512,768]{1,0:T(8,128)(2,1)S(1)}, u32[]{:S(2)}, u32[]{:S(2)}) collective-permute-start(bf16[512,768]{1,0:T(8,128)(2,1)S(1)} %get-tuple-element.53), channel_id=1, source_target_pairs={{0,1},{1,0},{2,3},{3,2},{4,5},{5,4},{6,7},{7,6},{8,9},{9,8},{10,11... | collective-permute-start | bytes 2359304 | tf_op jit(solution)/shard_map/ppermute | solution.py:319
  72.2 5.3 %collective-permute-start.9 = (bf16[512,768]{1,0:T(8,128)(2,1)S(1)}, bf16[512,768]{1,0:T(8,128)(2,1)S(1)}, u32[]{:S(2)}, u32[]{:S(2)}) collective-permute-start(bf16[512,768]{1,0:T(8,128)(2,1)S(1)} %get-tuple-element.54), channel_id=1, source_target_pairs={{0,1},{1,0},{2,3},{3,2},{4,5},{5,4},{6,7},{7,6},{8,9},{9,8},{10,11... | collective-permute-start | bytes 2359304 | tf_op jit(solution)/shard_map/ppermute | solution.py:319
  108.5 46.4 %collective-permute-start.13 = (bf16[512,1024]{1,0:T(8,128)(2,1)}, bf16[512,1024]{1,0:T(8,128)(2,1)S(1)}, u32[]{:S(2)}, u32[]{:S(2)}) collective-permute-start(bf16[512,1024]{1,0:T(8,128)(2,1)} %held.4.refs_0_), channel_id=1, source_target_pairs={{0,2},{1,3},{6,4},{7,5},{8,10},{9,11},{14,12},{15,13},{16,18},{17,... | collective-permute-start | bytes 3145736 | tf_op jit(solution)/shard_map/ppermute | solution.py:352
  112.9 42.0 %collective-permute-start.12 = (bf16[512,1024]{1,0:T(8,128)(2,1)}, bf16[512,1024]{1,0:T(8,128)(2,1)S(1)}, u32[]{:S(2)}, u32[]{:S(2)}) collective-permute-start(bf16[512,1024]{1,0:T(8,128)(2,1)} %added.4.refs_1_), channel_id=1, source_target_pairs={{2,4},{3,5},{4,2},{5,3},{10,12},{11,13},{12,10},{13,11},{18,20},{1... | collective-permute-start | bytes 3145736 | tf_op jit(solution)/shard_map/ppermute | solution.py:352
  113.7 16.8 %collective-permute-start.14 = (bf16[256,256]{1,0:T(8,128)(2,1)}, bf16[256,256]{1,0:T(8,128)(2,1)S(1)}, u32[]{:S(2)}, u32[]{:S(2)}) collective-permute-start(bf16[256,256]{1,0:T(8,128)(2,1)} %get-tuple-element.62), channel_id=1, source_target_pairs={{0,8},{8,0},{16,24},{24,16},{1,9},{9,1},{17,25},{25,17},{2,10},{10... | collective-permute-start | bytes 393224 | tf_op jit(solution)/shard_map/ppermute | solution.py:319
  113.7 16.7 %collective-permute-start.15 = (bf16[256,256]{1,0:T(8,128)(2,1)}, bf16[256,256]{1,0:T(8,128)(2,1)S(1)}, u32[]{:S(2)}, u32[]{:S(2)}) collective-permute-start(bf16[256,256]{1,0:T(8,128)(2,1)} %get-tuple-element.63), channel_id=1, source_target_pairs={{0,16},{8,24},{16,0},{24,8},{1,17},{9,25},{17,1},{25,9},{2,18},{10... | collective-permute-start | bytes 393224 | tf_op jit(solution)/shard_map/ppermute | solution.py:319
  114.0 16.4 %collective-permute-start.16 = (bf16[256,256]{1,0:T(8,128)(2,1)}, bf16[256,256]{1,0:T(8,128)(2,1)S(1)}, u32[]{:S(2)}, u32[]{:S(2)}) collective-permute-start(bf16[256,256]{1,0:T(8,128)(2,1)} %get-tuple-element.64), channel_id=1, source_target_pairs={{0,24},{8,16},{16,8},{24,0},{1,25},{9,17},{17,9},{25,1},{2,26},{10... | collective-permute-start | bytes 393224 | tf_op jit(solution)/shard_map/ppermute | solution.py:319
  145.3 5.7 %collective-permute-start.17 = (bf16[256,256]{1,0:T(8,128)(2,1)S(1)}, bf16[256,256]{1,0:T(8,128)(2,1)S(1)}, u32[]{:S(2)}, u32[]{:S(2)}) collective-permute-start(bf16[256,256]{1,0:T(8,128)(2,1)S(1)} %get-tuple-element.65), channel_id=1, source_target_pairs={{0,8},{8,0},{16,24},{24,16},{1,9},{9,1},{17,25},{25,17},{2,10},{10... | collective-permute-start | bytes 393224 | tf_op jit(solution)/shard_map/ppermute | solution.py:319
  146.9 8.0 %collective-permute-start.18 = (bf16[256,256]{1,0:T(8,128)(2,1)S(1)}, bf16[256,256]{1,0:T(8,128)(2,1)S(1)}, u32[]{:S(2)}, u32[]{:S(2)}) collective-permute-start(bf16[256,256]{1,0:T(8,128)(2,1)S(1)} %get-tuple-element.66), channel_id=1, source_target_pairs={{0,16},{8,24},{16,0},{24,8},{1,17},{9,25},{17,1},{25,9},{2,18},{10... | collective-permute-start | bytes 393224 | tf_op jit(solution)/shard_map/ppermute | solution.py:319
  148.4 6.5 %collective-permute-start.19 = (bf16[256,256]{1,0:T(8,128)(2,1)S(1)}, bf16[256,256]{1,0:T(8,128)(2,1)S(1)}, u32[]{:S(2)}, u32[]{:S(2)}) collective-permute-start(bf16[256,256]{1,0:T(8,128)(2,1)S(1)} %get-tuple-element.67), channel_id=1, source_target_pairs={{0,24},{8,16},{16,8},{24,0},{1,25},{9,17},{17,9},{25,1},{2,26},{10... | collective-permute-start | bytes 393224 | tf_op jit(solution)/shard_map/ppermute | solution.py:319
  157.1 22.3 %collective-permute-start.21 = (bf16[512,1024]{1,0:T(8,128)(2,1)S(1)}, bf16[512,1024]{1,0:T(8,128)(2,1)S(1)}, u32[]{:S(2)}, u32[]{:S(2)}) collective-permute-start(bf16[512,1024]{1,0:T(8,128)(2,1)S(1)} %added.6.refs_9_), channel_id=1, source_target_pairs={{2,4},{3,5},{4,2},{5,3},{10,12},{11,13},{12,10},{13,11},{18,20},{1... | collective-permute-start | bytes 3145736 | tf_op jit(solution)/shard_map/ppermute | solution.py:352
  158.4 29.9 %collective-permute-start.20 = (bf16[512,1024]{1,0:T(8,128)(2,1)S(1)}, bf16[512,1024]{1,0:T(8,128)(2,1)S(1)}, u32[]{:S(2)}, u32[]{:S(2)}) collective-permute-start(bf16[512,1024]{1,0:T(8,128)(2,1)S(1)} %added.5.refs_8_), channel_id=1, source_target_pairs={{2,0},{3,1},{4,6},{5,7},{0,2},{1,3},{6,4},{7,5},{10,8},{11,9},{12,... | collective-permute-start | bytes 3145736 | tf_op jit(solution)/shard_map/ppermute | solution.py:352
  175.8 14.2 %collective-permute-start.22 = (bf16[544,256]{1,0:T(8,128)(2,1)S(1)}, bf16[544,256]{1,0:T(8,128)(2,1)S(1)}, u32[]{:S(2)}, u32[]{:S(2)}) collective-permute-start(bf16[544,256]{1,0:T(8,128)(2,1)S(1)} %get-tuple-element.75), channel_id=1, source_target_pairs={{0,8},{8,0},{16,24},{24,16},{1,9},{9,1},{17,25},{25,17},{2,10},{10... | collective-permute-start | bytes 835592 | tf_op jit(solution)/shard_map/ppermute | solution.py:319
  177.1 13.1 %collective-permute-start.23 = (bf16[544,256]{1,0:T(8,128)(2,1)S(1)}, bf16[544,256]{1,0:T(8,128)(2,1)S(1)}, u32[]{:S(2)}, u32[]{:S(2)}) collective-permute-start(bf16[544,256]{1,0:T(8,128)(2,1)S(1)} %get-tuple-element.76), channel_id=1, source_target_pairs={{0,16},{8,24},{16,0},{24,8},{1,17},{9,25},{17,1},{25,9},{2,18},{10... | collective-permute-start | bytes 835592 | tf_op jit(solution)/shard_map/ppermute | solution.py:319
  178.0 12.2 %collective-permute-start.24 = (bf16[544,256]{1,0:T(8,128)(2,1)S(1)}, bf16[544,256]{1,0:T(8,128)(2,1)S(1)}, u32[]{:S(2)}, u32[]{:S(2)}) collective-permute-start(bf16[544,256]{1,0:T(8,128)(2,1)S(1)} %get-tuple-element.77), channel_id=1, source_target_pairs={{0,24},{8,16},{16,8},{24,0},{1,25},{9,17},{17,9},{25,1},{2,26},{10... | collective-permute-start | bytes 835592 | tf_op jit(solution)/shard_map/ppermute | solution.py:319
  (20 other events, 246.8 us)
Sparse Core Ops, SparseCore 0:
  10.2 49.8 all-gather.2
  61.7 68.6 all-gather.4

commit v13 on v11

--- a/solution.py
+++ b/solution.py
@@ -97,7 +97,7 @@
         outputs[step][...] = out_scr[position ^ step].T
 
 
-def backward_kernel(members, per_group, scale, width, plan_ref, in_scr, tap_scr, *refs):
+def backward_kernel(members, batch, per_group, scale, width, plan_ref, in_scr, lag_ref, *refs):
     cotangents = refs[:members]
     outputs = refs[-members - 4 : -4]
     cot_scr, out_scr, grad_scr, pad_scr = refs[-4:]
@@ -107,21 +107,25 @@
     length = members * width
     blocks = length // BLOCK
     depth = blocks * per_group
-    for step in range(members):
-        at = position ^ step
-        cot_scr[at] = cotangents[step][...].T
-    pad_scr[...] = jnp.zeros_like(pad_scr)
     rows_of = lax.broadcasted_iota(jnp.int32, (BLOCK, BLOCK), 0)
     lanes_of = lax.broadcasted_iota(jnp.int32, (BLOCK, BLOCK), 1)
     mirror = (rows_of + lanes_of == BLOCK - 1).astype(jnp.bfloat16)
 
-    def one_group(group, carry):
+    @pl.when(pl.program_id(0) == 0)
+    def _():
+        for step in range(members):
+            cot_scr[position ^ step] = cotangents[step][...].T
+        pad_scr[...] = jnp.zeros_like(pad_scr)
+
+    for local_group in range(batch):
+        group = pl.program_id(0) * batch + local_group
         start = pl.multiple_of(group * per_group, per_group)
-        lags = lag_matrix(tap_scr[pl.ds(group, 1), :], length)
+        lags = lag_ref[local_group]
+        padded_cot = pad_scr.at[local_group]
         data = stacked(in_scr, start, per_group, members, width)
         cot = stacked(cot_scr, start, per_group, members, width)
-        pad_scr[:depth, :BLOCK] = cot
-        pad_scr[: depth - per_group, BLOCK:] = cot[per_group:]
+        padded_cot[:depth, :BLOCK] = cot
+        padded_cot[: depth - per_group, BLOCK:] = cot[per_group:]
         flipped = lax.dot_general(
             mirror, data, NT, preferred_element_type=jnp.float32
         ).astype(jnp.bfloat16)
@@ -129,7 +133,7 @@
         products = []
         for offset in range(0, blocks, 2):
             rows = depth - offset * per_group
-            pair = pad_scr[offset * per_group : offset * per_group + depth, :]
+            pair = padded_cot[offset * per_group : offset * per_group + depth, :]
             result = lax.dot_general(
                 pair[:rows],
                 lags[:, offset * BLOCK : (offset + 2) * BLOCK],
@@ -142,30 +146,34 @@
                 )
             total = total + result
             products.append(jnp.dot(flipped, pair, preferred_element_type=jnp.float32))
-        spread_out(
-            out_scr, start, per_group, total.astype(jnp.bfloat16), members, width
-        )
+        spread_out(out_scr, start, per_group, total.astype(jnp.bfloat16), members, width)
         kept = jnp.where(rows_of + lanes_of >= BLOCK - 1, products[0][:, :BLOCK], 0.0)
         product = jnp.concatenate([kept, products[0][:, BLOCK:], *products[1:]], axis=1)
         product = pltpu.roll(
             product, length - (BLOCK - 1), axis=1, stride=1, stride_axis=0
         )
         grad_scr[pl.ds(group, 1), :] = jnp.sum(product, axis=0, keepdims=True) * scale
-        return carry
-
-    lax.fori_loop(0, groups, one_group, 0, unroll=4)
-    for step in range(members):
-        at = position ^ step
-        outputs[step][:width] = out_scr[at].T
-        rows = padded(groups)
-        whole = grad_scr[:, pl.ds(pl.multiple_of(at * width, width), width)].astype(jnp.bfloat16)
-        if rows > groups:
-            blank = jnp.zeros((rows - groups, width), jnp.bfloat16)
-            whole = jnp.concatenate([whole, blank], axis=0)
-        for chunk in range(width // channels):
-            outputs[step][width + chunk * rows : width + (chunk + 1) * rows, :] = whole[
-                :, chunk * channels : (chunk + 1) * channels
-            ]
+
+    @pl.when(pl.program_id(0) == pl.num_programs(0) - 1)
+    def _():
+        for step in range(members):
+            at = position ^ step
+            outputs[step][:width] = out_scr[at].T
+            rows = padded(groups)
+            whole = grad_scr[:, pl.ds(pl.multiple_of(at * width, width), width)]
+            whole = whole.astype(jnp.bfloat16)
+            if rows > groups:
+                blank = jnp.zeros((rows - groups, width), jnp.bfloat16)
+                whole = jnp.concatenate([whole, blank], axis=0)
+            for chunk in range(width // channels):
+                outputs[step][width + chunk * rows : width + (chunk + 1) * rows, :] = whole[
+                    :, chunk * channels : (chunk + 1) * channels
+                ]
+
+
+def lag_kernel(taps_ref, out_ref):
+    row = taps_ref[pl.ds(pl.program_id(0), 1), :]
+    out_ref[0] = lag_matrix(row, taps_ref.shape[1])
 
 
 VMEM = pl.BlockSpec(memory_space=pltpu.VMEM)
@@ -194,27 +202,45 @@
     return parts, turned, taps
 
 
-def correlate(plan, turned, taps, cotangents, per_group, scale, after=()):
+def lag_matrices(taps):
+    groups, length = taps.shape
+    return pl.pallas_call(
+        lag_kernel,
+        out_shape=jax.ShapeDtypeStruct((groups, BLOCK, length), jnp.bfloat16),
+        grid=(groups,),
+        in_specs=[VMEM],
+        out_specs=pl.BlockSpec((1, BLOCK, length), lambda i: (i, 0, 0)),
+        compiler_params=pltpu.CompilerParams(vmem_limit_bytes=12 * 2**20),
+        cost_estimate=COST,
+        name="lag_matrices",
+    )(taps)
+
+
+def correlate(plan, turned, lags, cotangents, per_group, scale, after=()):
     members = len(cotangents)
     width, channels = cotangents[0].shape
     length = members * width
     groups = channels // per_group
+    batch = 4 if groups % 4 == 0 else 1
     rows = width + padded(groups) * width // channels
     return pl.pallas_call(
-        functools.partial(backward_kernel, members, per_group, scale, width),
+        functools.partial(backward_kernel, members, batch, per_group, scale, width),
         out_shape=[jax.ShapeDtypeStruct((rows, channels), jnp.bfloat16)] * members,
-        in_specs=[SMEM] + [VMEM] * (members + 2) + [ANYWHERE] * len(after),
+        grid=(groups // batch,),
+        in_specs=[SMEM, VMEM, pl.BlockSpec((batch, BLOCK, length), lambda i: (i, 0, 0))]
+        + [VMEM] * members
+        + [ANYWHERE] * len(after),
         out_specs=[VMEM] * members,
         scratch_shapes=[
             pltpu.VMEM((members, channels, width), jnp.bfloat16),
             pltpu.VMEM((members, channels, width), jnp.bfloat16),
             pltpu.VMEM((groups, length), jnp.float32),
-            pltpu.VMEM((2 * length // BLOCK * per_group, 2 * BLOCK), jnp.bfloat16),
+            pltpu.VMEM((batch, 2 * length // BLOCK * per_group, 2 * BLOCK), jnp.bfloat16),
         ],
         compiler_params=pltpu.CompilerParams(vmem_limit_bytes=24 * 2**20),
         cost_estimate=COST,
         name="causal_conv_grads",
-    )(plan, turned, taps, *cotangents, *after)
+    )(plan, turned, lags, *cotangents, *after)
 
 
 def in_hbm(array):
@@ -449,7 +475,7 @@
 
 def gate_kernel(members, plan_ref, *refs):
     parts = refs[:members]
-    query_ref, gated_ref, conv_ref = refs[members:]
+    query_ref, gated_ref, conv_ref = refs[members], *refs[-2:]
     position = plan_ref[POSITION]
     share = parts[0].shape[1]
     for step in range(members):
@@ -459,17 +485,17 @@
         gated_ref[:, columns] = (wide(conv) * wide(query_ref[:, columns])).astype(jnp.bfloat16)
 
 
-def gated(plan, parts, query_gate):
+def gated(plan, parts, query_gate, after):
     array = jax.ShapeDtypeStruct(query_gate.shape, jnp.bfloat16)
     return pl.pallas_call(
         functools.partial(gate_kernel, len(parts)),
         out_shape=[array, array],
-        in_specs=[SMEM] + [VMEM] * (len(parts) + 1),
+        in_specs=[SMEM] + [VMEM] * (len(parts) + 1) + [ANYWHERE] * len(after),
         out_specs=[VMEM] * 2,
         compiler_params=pltpu.CompilerParams(vmem_limit_bytes=8 * 2**20),
         cost_estimate=COST,
         name="gated_output",
-    )(plan, *parts, query_gate)
+    )(plan, *parts, query_gate, *after)
 
 
 def spans(widths, start, stop):
@@ -680,7 +706,8 @@
     conv_parts, turned, taps = convolve(plan, input_parts, length, per_group, (total,))
     *conv_parts, near, cross = held_until([*conv_parts, near, cross], ())
     far, skip = hop(near, ACROSS), hop(cross, OUTWARD)
-    gated_out, convolved = gated(plan, traded(conv_parts, "ctx"), query_gate)
+    lags = lag_matrices(taps)
+    gated_out, convolved = gated(plan, traded(conv_parts, "ctx"), query_gate, (lags,))
 
     def product(first, count, other, more=(), after=(), tiles=1, widths=()):
         return column_products(
@@ -691,7 +718,7 @@
     given_far = product(FAR, 1, 1, tiles=2, widths=(3 * quarter, quarter))
     received = [swapped(part, "tp", 1) for part in given_far]
     (first,) = product(FAR, 1, 0, received, tiles=2)
-    far, skip, near = held_until([far, skip, near], (first,))
+    far, skip = held_until([far, skip], (first,))
     mixed = chosen(plan, far, first)
     arrived = hop(mixed, OUTWARD + INWARD)
     given_middle = product(MIDDLE, 1, 1, (), (mixed,), tiles=2, widths=(half, half))
@@ -721,7 +748,7 @@
 
     two_a, two_b = held_until([two_a, two_b], tuple(grad_parts[1:]))
     third, second = added(third, two_a), added(second, two_b)
-    back_parts = correlate(plan, turned, taps, grad_parts, per_group, scale, (third, second))
+    back_parts = correlate(plan, turned, lags, grad_parts, per_group, scale, (third, second))
     projected = added(own, hop(third, OUTWARD + INWARD), hop(second, ACROSS))
     back_parts = traded(back_parts, "ctx")
     return projected, grad_query, *finished(plan, back_parts, key_gate, value_input, groups, (in_hbm(projected),))
@@ -754,7 +781,7 @@
     grad_query = (wide(dgated) * wide(convolved)).astype(jnp.bfloat16)
     conv_grad = (wide(dgated) * wide(query_gate)).astype(jnp.bfloat16)
     grad_parts = traded(cut(conv_grad, position, members, 1), "ctx")
-    back_parts = correlate(plan, turned, taps, grad_parts, per_group, scale)
+    back_parts = correlate(plan, turned, lag_matrices(taps), grad_parts, per_group, scale)
     back_parts = traded(back_parts, "ctx")
     return (
         projected,

time: 151 us -> 148 us (0.980)
  waiting for transfers between devices: 43.5 us -> 36.1 us
  Pallas kernels: 70.9 us -> 73.7 us
    ppermute x9, waiting for transfers between devices: 22.1 us -> 18.2 us  [hop(): lax.ppermute(array, 'tp', [(2 * i + core, 2 * j + core) for i, j in pairs...]
    ppermute x22, waiting for transfers between devices: 21.5 us -> 17.9 us  [swapped(): return lax.ppermute(array, axis, [(i, i ^ step) for i in range(size)])]
    pallas_call x1 -> x2, Pallas kernels: 9.53 us -> 12.3 us  [the longest x1 8.87 us: correlate(): pl.pallas_call(functools.partial(backward_kernel, members, batch, per_gro...]
  transfers between devices with their start and end apart: 31 -> 31, of which waited for: 11 -> 10; matrix products, arithmetic and copies ran while one was open for 0% -> 0% of each run, Pallas kernels for 45% -> 48%
where the time goes in v13:
time: 148 us
  Pallas kernels  73.7 us (50%)
  starting transfers between devices  36.8 us (25%)
  waiting for transfers between devices  36.1 us (24%)
    pallas_call x6, Pallas kernels, column_products(): pl.pallas_call(functools.partial(product_kernel, steps, [part.shape[1] fo...  23.8 us
    ppermute x9, starting transfers between devices, hop(): lax.ppermute(array, 'tp', [(2 * i + core, 2 * j + core) for i, j in pairs...  19.9 us
    ppermute x9, waiting for transfers between devices, hop(): lax.ppermute(array, 'tp', [(2 * i + core, 2 * j + core) for i, j in pairs...  18.2 us
    ppermute x22, waiting for transfers between devices, swapped(): return lax.ppermute(array, axis, [(i, i ^ step) for i in range(size)])  17.9 us
    ppermute x22, starting transfers between devices, swapped(): return lax.ppermute(array, axis, [(i, i ^ step) for i in range(size)])  17 us
    pallas_call x3, Pallas kernels, cotangent_products(): pl.pallas_call(functools.partial(cotangent_kernel, count, begin), out_sha...  16.2 us
    pallas_call x1, Pallas kernels, correlate(): pl.pallas_call(functools.partial(backward_kernel, members, batch, per_gro...  8.87 us
    pallas_call x1, Pallas kernels, convolve(): pl.pallas_call(functools.partial(forward_kernel, members, per_group, widt...  5.65 us
  transfers between devices with their start and end apart: 31, of which 10 were waited for; matrix products, arithmetic and copies ran while one was open for 0% of the time, Pallas kernels for 48%

profile of v13, /device:TPU:0, one launch (start us, length us, event | category | flops | bytes accessed | tf_op | source)
XLA Modules:
  0.0 147.7 jit_solution(17813308728470339239)
XLA Ops:
  1.9 5.6 %collective-permute-start.4 = (bf16[512,1024]{1,0:T(8,128)(2,1)}, bf16[512,1024]{1,0:T(8,128)(2,1)S(1)}, u32[]{:S(2)}, u32[]{:S(2)}) collective-permute-start(bf16[512,1024]{1,0:T(8,128)(2,1)} %refs_0_.1), channel_id=1, source_target_pairs={{0,2},{1,3},{6,4},{7,5},{2,0},{3,1},{4,6},{5,7},{8,10},{9,11},{14,... | collective-permute-start | bytes 3145736 | tf_op jit(solution)/shard_map/ppermute | solution.py:375
  7.5 2.6 %gated_input.1 = (bf16[544,256]{1,0:T(8,128)(2,1)S(1)}, bf16[544,256]{1,0:T(8,128)(2,1)S(1)}, bf16[544,256]{1,0:T(8,128)(2,1)S(1)}, bf16[544,256]{1,0:T(8,128)(2,1)S(1)}) custom-call(s32[2]{0:T(128)S(1)} %pad_add_fusion.who_ref, bf16[512,1024]{1,0:T(8,128)(2,1)} %refs_4_.3, bf16[512,1024]{1,0:T(8,128)(2,1)} %refs_5_.1, f32[64,512]{1,0:T(8,128)} %bitcast.4), custom_call_target="tpu_custom_call" | custom-call | flops 1048576 | bytes 4096 | tf_op jit(solution)/shard_map/gated_input/pallas_call | solution.py:285
  14.9 5.0 %cotangent_blocks.3.refs_4_.refs_3_ = f32[512,1024]{1,0:T(8,128)S(1)} custom-call(s32[10]{0:T(128)S(1)} %plan.1._.plan_ref, bf16[1024,8192]{1,0:T(8,128)(2,1)} %weight_ref.19, bf16[512,1024]{1,0:T(8,128)(2,1)S(1)} %copy-done.3, bf16[512,1024]{1,0:T(8,128)(2,1)} %collective-permute-done.3.refs_1_), custom_call_target="tpu_custom_call" | custom-call | flops 1048576 | bytes 4096 | tf_op jit(solution)/shard_map/cotangent_blocks/pallas_call | solution.py:640
  19.9 5.8 %collective-permute-done.1.refs_2_ = bf16[544,256]{1,0:T(8,128)(2,1)S(1)} collective-permute-done((bf16[544,256]{1,0:T(8,128)(2,1)S(1)}, bf16[544,256]{1,0:T(8,128)(2,1)S(1)}, u32[]{:S(2)}, u32[]{:S(2)}) %collective-permute-start.1) | collective-permute-done | bytes 278560 | tf_op jit(solution)/shard_map/ppermute | solution.py:342
  25.7 5.7 %causal_conv.1 = (bf16[512,256]{1,0:T(8,128)(2,1)S(1)}, bf16[512,256]{1,0:T(8,128)(2,1)S(1)}, bf16[512,256]{1,0:T(8,128)(2,1)S(1)}, bf16[512,256]{1,0:T(8,128)(2...) custom-call(s32[10]{0:T(128)S(1)} %plan.1._.plan_ref, bf16[544,256]{1,0:T(8,128)(2,1)S(1)} %get-tuple-element.47.refs_0_, ...), custom_call_target="tpu_custom_call" | custom-call | flops 1048576 | bytes 4096 | tf_op jit(solution)/shard_map/causal_conv/pallas_call | solution.py:188
  37.0 3.4 %lag_matrices.1.refs_5_.lag_ref = bf16[16,128,2048]{2,1,0:T(8,128)(2,1)S(1)} custom-call(f32[16,2048]{1,0:T(8,128)S(1)} %get-tuple-element.59.taps_ref), custom_call_target="tpu_custom_call" | custom-call | flops 1048576 | bytes 4096 | tf_op jit(solution)/shard_map/lag_matrices/pallas_call | solution.py:207
  40.7 4.9 %collective-permute-done.7.refs_2_ = bf16[512,256]{1,0:T(8,128)(2,1)S(1)} collective-permute-done((bf16[512,256]{1,0:T(8,128)(2,1)S(1)}, bf16[512,256]{1,0:T(8,128)(2,1)S(1)}, u32[]{:S(2)}, u32[]{:S(2)}) %collective-permute-start.7) | collective-permute-done | bytes 262176 | tf_op jit(solution)/shard_map/ppermute | solution.py:342
  46.5 3.4 %projection_blocks.6 = (bf16[512,768]{1,0:T(8,128)(2,1)S(1)}, bf16[512,256]{1,0:T(8,128)(2,1)S(1)}) custom-call(s32[10]{0:T(128)S(1)} %plan.1._.plan_ref, bf16[512,1024]{1,0:T(8,128)(2,1)S(1)} %get-tuple-element.60.data_ref, bf16[1024,8192]{1,0:T(8,128)(2,1)} %weight_ref.19), custom_call_target="tpu_custom_call" | custom-call | flops 1048576 | bytes 4096 | tf_op jit(solution)/shard_map/projection_blocks/pallas_call | solution.py:541
  52.6 3.5 %projection_blocks.7.refs_2_.end_ref.refs_0_ = bf16[512,1024]{1,0:T(8,128)(2,1)S(1)} custom-call(s32[10]{0:T(128)S(1)} %plan.1._.plan_ref, bf16[512,1024]{1,0:T(8,128)(2,1)S(1)} %get-tuple-element.60.data_ref, bf16[1024,8192]{1,0:T(8,128)(2,1)} %weight_ref.19, bf16[512,768]{1,0:T(8,128)(2,1)S(1)} %collective-permute-done.11.refs_0_, ...), custom_call_target="tpu_custom_call" | custom-call | flops 1048576 | bytes 4096 | tf_op jit(solution)/shard_map/projection_blocks/pallas_call | solution.py:541
  56.1 4.1 %collective-permute-done.10.refs_1_ = bf16[512,1024]{1,0:T(8,128)(2,1)S(1)} collective-permute-done((bf16[512,1024]{1,0:T(8,128)(2,1)S(1)}, bf16[512,1024]{1,0:T(8,128)(2,1)S(1)}, u32[]{:S(2)}, u32[]{:S(2)}) %collective-permute-start.10) | collective-permute-done | bytes 1048608 | tf_op jit(solution)/shard_map/ppermute | solution.py:375
  61.0 3.8 %collective-permute-start.17 = (bf16[512,1024]{1,0:T(8,128)(2,1)S(1)}, bf16[512,1024]{1,0:T(8,128)(2,1)S(1)}, u32[]{:S(2)}, u32[]{:S(2)}) collective-permute-start(bf16[512,1024]{1,0:T(8,128)(2,1)S(1)} %chosen.2.refs_0_), channel_id=1, source_target_pairs={{2,0},{3,1},{4,6},{5,7},{0,2},{1,3},{6,4},{7,5},{10,8},{11,9},{12,... | collective-permute-start | bytes 3145736 | tf_op jit(solution)/shard_map/ppermute | solution.py:375
  65.2 3.4 %projection_blocks.8 = (bf16[512,512]{1,0:T(8,128)(2,1)S(1)}, bf16[512,512]{1,0:T(8,128)(2,1)S(1)}) custom-call(s32[10]{0:T(128)S(1)} %plan.1._.plan_ref, bf16[512,1024]{1,0:T(8,128)(2,1)S(1)} %get-tuple-element.60.data_ref, bf16[1024,8192]{1,0:T(8,128)(2,1)} %weight_ref.19, bf16[512,1024]{1,0:T(8,128)(2,1)S(1)} %chosen.2.refs_0_), custom_call_target="tpu_custom_call" | custom-call | flops 1048576 | bytes 4096 | tf_op jit(solution)/shard_map/projection_blocks/pallas_call | solution.py:541
  71.4 3.5 %projection_blocks.9.refs_0_.refs_4_ = bf16[512,1024]{1,0:T(8,128)(2,1)S(1)} custom-call(s32[10]{0:T(128)S(1)} %plan.1._.plan_ref, bf16[512,1024]{1,0:T(8,128)(2,1)S(1)} %get-tuple-element.60.data_ref, bf16[1024,8192]{1,0:T(8,128)(2,1)} %weight_ref.19, bf16[512,512]{1,0:T(8,128)(2,1)S(1)} %collective-permute-done.13.refs_0_, ...), custom_call_target="tpu_custom_call" | custom-call | flops 1048576 | bytes 4096 | tf_op jit(solution)/shard_map/projection_blocks/pallas_call | solution.py:541
  74.9 4.9 %projection_blocks.10 = (bf16[512,1024]{1,0:T(8,128)(2,1)S(1)}, bf16[512,1024]{1,0:T(8,128)(2,1)S(1)}) custom-call(s32[10]{0:T(128)S(1)} %plan.1._.plan_ref, bf16[512,1024]{1,0:T(8,128)(2,1)S(1)} %get-tuple-element.60.data_ref, bf16[1024,8192]{1,0:T(8,128)(2,1)} %weight_ref.19, bf16[512,1024]{1,0:T(8,128)(2,1)S(1)} %projection_blocks.9.refs_0_.refs_4_), custom_call_target="tpu_custom_call" | custom-call | flops 1048576 | bytes 4096 | tf_op jit(solution)/shard_map/projection_blocks/pallas_call | solution.py:541
  79.8 6.4 %cotangent_blocks.4.refs_1_.refs_2_ = f32[512,1024]{1,0:T(8,128)S(1)} custom-call(s32[10]{0:T(128)S(1)} %plan.1._.plan_ref, bf16[1024,8192]{1,0:T(8,128)(2,1)} %weight_ref.19, bf16[512,1024]{1,0:T(8,128)(2,1)S(1)} %get-tuple-element.61.refs_0_, bf16[512,1024]{1,0:T(8,128)(2,1)S(1)} %collective-permute-done.18.refs_1_, bf16[512,1024]{1,0:T(8,128)(2,1)S(1)} %added.5.refs_2_, ...), custom_call_target="tpu_custom_call" | custom-call | flops 1048576 | bytes 4096 | tf_op jit(solution)/shard_map/cotangent_blocks/pallas_call | solution.py:640
  88.1 2.3 %collective-permute-start.22 = (bf16[512,1024]{1,0:T(8,128)(2,1)S(1)}, bf16[512,1024]{1,0:T(8,128)(2,1)S(1)}, u32[]{:S(2)}, u32[]{:S(2)}) collective-permute-start(bf16[512,1024]{1,0:T(8,128)(2,1)S(1)} %held.8.refs_0_), channel_id=1, source_target_pairs={{0,2},{1,3},{6,4},{7,5},{8,10},{9,11},{14,12},{15,13},{16,18},{17,... | collective-permute-start | bytes 3145736 | tf_op jit(solution)/shard_map/ppermute | solution.py:375
  91.2 4.8 %cotangent_blocks.5.start_ref = f32[512,1024]{1,0:T(8,128)S(1)} custom-call(s32[10]{0:T(128)S(1)} %plan.1._.plan_ref, bf16[1024,8192]{1,0:T(8,128)(2,1)} %weight_ref.19, bf16[512,1024]{1,0:T(8,128)(2,1)S(1)} %collective-permute-done.20.refs_0_, bf16[512,1024]{1,0:T(8,128)(2,1)S(1)} %chosen.3.refs_1_, f32[512,1024]{1,0:T(8,128)S(1)} %cotangent_blocks.4.refs_1_.refs_2_, ...), custom_call_target="tpu_custom_call" | custom-call | flops 1048576 | bytes 4096 | tf_op jit(solution)/shard_map/cotangent_blocks/pallas_call | solution.py:640
  96.0 4.5 %cotangent_last.1 = (bf16[512,1024]{1,0:T(8,128)(2,1)}, bf16[512,256]{1,0:T(8,128)(2,1)S(1)}, bf16[512,256]{1,0:T(8,128)(2,1)S(1)}, bf16[512,256]{1,0:T(8,128)(2,1)S(1)}, bf16[512,256]{1,0:T(8,128)(2,1)S(1)}) custom-call(s32[10]{0:T(128)S(1)} %plan.1._.plan_ref, bf16[1024,8192]{1,0:T(8,128)(2,1)} %weight_ref.19, ...), custom_call_target="tpu_custom_call" | custom-call | flops 1048576 | bytes 4096 | tf_op jit(solution)/shard_map/cotangent_last/pallas_call | solution.py:606
  104.0 5.1 %projection_blocks.11 = (bf16[512,1024]{1,0:T(8,128)(2,1)S(1)}, bf16[512,1024]{1,0:T(8,128)(2,1)S(1)}) custom-call(s32[10]{0:T(128)S(1)} %plan.1._.plan_ref, bf16[512,1024]{1,0:T(8,128)(2,1)S(1)} %get-tuple-element.60.data_ref, bf16[1024,8192]{1,0:T(8,128)(2,1)} %weight_ref.19, bf16[512,1024]{1,0:T(8,128)(2,1)S(1)} %collective-permute-done.15.refs_0_, ...), custom_call_target="tpu_custom_call" | custom-call | flops 1048576 | bytes 4096 | tf_op jit(solution)/shard_map/projection_blocks/pallas_call | solution.py:541
  109.1 4.3 %collective-permute-done.22.refs_1_ = bf16[512,1024]{1,0:T(8,128)(2,1)S(1)} collective-permute-done((bf16[512,1024]{1,0:T(8,128)(2,1)S(1)}, bf16[512,1024]{1,0:T(8,128)(2,1)S(1)}, u32[]{:S(2)}, u32[]{:S(2)}) %collective-permute-start.22) | collective-permute-done | bytes 1048608 | tf_op jit(solution)/shard_map/ppermute | solution.py:375
  113.4 2.6 %collective-permute-done.24.refs_3_.refs_2_ = bf16[512,256]{1,0:T(8,128)(2,1)S(1)} collective-permute-done((bf16[512,256]{1,0:T(8,128)(2,1)S(1)}, bf16[512,256]{1,0:T(8,128)(2,1)S(1)}, u32[]{:S(2)}, u32[]{:S(2)}) %collective-permute-start.24) | collective-permute-done | bytes 262176 | tf_op jit(solution)/shard_map/ppermute | solution.py:342
  117.5 3.8 %collective-permute-start.26 = (bf16[512,1024]{1,0:T(8,128)(2,1)S(1)}, bf16[512,1024]{1,0:T(8,128)(2,1)S(1)}, u32[]{:S(2)}, u32[]{:S(2)}) collective-permute-start(bf16[512,1024]{1,0:T(8,128)(2,1)S(1)} %added.7.refs_4_), channel_id=1, source_target_pairs={{2,0},{3,1},{4,6},{5,7},{0,2},{1,3},{6,4},{7,5},{10,8},{11,9},{12,... | collective-permute-start | bytes 3145736 | tf_op jit(solution)/shard_map/ppermute | solution.py:375
  121.3 8.9 %causal_conv_grads.1 = (bf16[544,256]{1,0:T(8,128)(2,1)S(1)}, bf16[544,256]{1,0:T(8,128)(2,1)S(1)}, bf16[544,256]{1,0:T(8,128)(2,1)S(1)}, bf16[544,256]{1,0:T(8,128)(2,1)S(1)}) custom-call(s32[10]{0:T(128)S(1)} %plan.1._.plan_ref, bf16[4,256,512]{2,1,0:T(8,128)(2,1)S(1)} %get-tuple-element.81.in_scr, bf16[16,128,2048]{2,1,0:T(8,128)(2,1)S(1)} %lag_matrices.1.refs_5_.lag_ref, ...), custom_call_target="tpu_custom_call" | custom-call | flops 1048576 | bytes 4096 | tf_op jit(solution)/shard_map/causal_conv_grads/pallas_call | solution.py:226
  133.8 9.9 %collective-permute-done.26.refs_1_ = bf16[512,1024]{1,0:T(8,128)(2,1)S(1)} collective-permute-done((bf16[512,1024]{1,0:T(8,128)(2,1)S(1)}, bf16[512,1024]{1,0:T(8,128)(2,1)S(1)}, u32[]{:S(2)}, u32[]{:S(2)}) %collective-permute-start.26) | collective-permute-done | bytes 1048608 | tf_op jit(solution)/shard_map/ppermute | solution.py:375
  (76 shorter events, 34.7 us)
Async XLA Ops:
  0.6 12.6 %collective-permute-start.3 = (bf16[512,1024]{1,0:T(8,128)(2,1)}, bf16[512,1024]{1,0:T(8,128)(2,1)}, u32[]{:S(2)}, u32[]{:S(2)}) collective-permute-start(bf16[512,1024]{1,0:T(8,128)(2,1)} %refs_0_.1), channel_id=1, source_target_pairs={{0,1},{1,0},{2,3},{3,2},{4,5},{5,4},{6,7},{7,6},{8,9},{9,8},{10,11... | collective-permute-start | bytes 3145736 | tf_op jit(solution)/shard_map/ppermute | solution.py:342
  1.2 30.2 %collective-permute-start.5 = (bf16[512,1024]{1,0:T(8,128)(2,1)}, bf16[512,1024]{1,0:T(8,128)(2,1)S(1)}, u32[]{:S(2)}, u32[]{:S(2)}) collective-permute-start(bf16[512,1024]{1,0:T(8,128)(2,1)} %refs_0_.1), channel_id=1, source_target_pairs={{2,4},{3,5},{4,2},{5,3},{10,12},{11,13},{12,10},{13,11},{18,20},{1... | collective-permute-start | bytes 3145736 | tf_op jit(solution)/shard_map/ppermute | solution.py:375
  1.9 29.5 %collective-permute-start.4 = (bf16[512,1024]{1,0:T(8,128)(2,1)}, bf16[512,1024]{1,0:T(8,128)(2,1)S(1)}, u32[]{:S(2)}, u32[]{:S(2)}) collective-permute-start(bf16[512,1024]{1,0:T(8,128)(2,1)} %refs_0_.1), channel_id=1, source_target_pairs={{0,2},{1,3},{6,4},{7,5},{2,0},{3,1},{4,6},{5,7},{8,10},{9,11},{14,... | collective-permute-start | bytes 3145736 | tf_op jit(solution)/shard_map/ppermute | solution.py:375
  11.7 14.0 %collective-permute-start.1 = (bf16[544,256]{1,0:T(8,128)(2,1)S(1)}, bf16[544,256]{1,0:T(8,128)(2,1)S(1)}, u32[]{:S(2)}, u32[]{:S(2)}) collective-permute-start(bf16[544,256]{1,0:T(8,128)(2,1)S(1)} %get-tuple-element.49), channel_id=1, source_target_pairs={{0,16},{8,24},{16,0},{24,8},{1,17},{9,25},{17,1},{25,9},{2,18},{10... | collective-permute-start | bytes 835592 | tf_op jit(solution)/shard_map/ppermute | solution.py:342
  13.2 12.5 %collective-permute-start.2 = (bf16[544,256]{1,0:T(8,128)(2,1)S(1)}, bf16[544,256]{1,0:T(8,128)(2,1)S(1)}, u32[]{:S(2)}, u32[]{:S(2)}) collective-permute-start(bf16[544,256]{1,0:T(8,128)(2,1)S(1)} %get-tuple-element.50), channel_id=1, source_target_pairs={{0,24},{8,16},{16,8},{24,0},{1,25},{9,17},{17,9},{25,1},{2,26},{10... | collective-permute-start | bytes 835592 | tf_op jit(solution)/shard_map/ppermute | solution.py:342
  32.7 12.9 %collective-permute-start.7 = (bf16[512,256]{1,0:T(8,128)(2,1)S(1)}, bf16[512,256]{1,0:T(8,128)(2,1)S(1)}, u32[]{:S(2)}, u32[]{:S(2)}) collective-permute-start(bf16[512,256]{1,0:T(8,128)(2,1)S(1)} %get-tuple-element.57), channel_id=1, source_target_pairs={{0,16},{8,24},{16,0},{24,8},{1,17},{9,25},{17,1},{25,9},{2,18},{10... | collective-permute-start | bytes 786440 | tf_op jit(solution)/shard_map/ppermute | solution.py:342
  34.1 11.6 %collective-permute-start.8 = (bf16[512,256]{1,0:T(8,128)(2,1)S(1)}, bf16[512,256]{1,0:T(8,128)(2,1)S(1)}, u32[]{:S(2)}, u32[]{:S(2)}) collective-permute-start(bf16[512,256]{1,0:T(8,128)(2,1)S(1)} %get-tuple-element.58), channel_id=1, source_target_pairs={{0,24},{8,16},{16,8},{24,0},{1,25},{9,17},{17,9},{25,1},{2,26},{10... | collective-permute-start | bytes 786440 | tf_op jit(solution)/shard_map/ppermute | solution.py:342
  35.0 25.2 %collective-permute-start.10 = (bf16[512,1024]{1,0:T(8,128)(2,1)S(1)}, bf16[512,1024]{1,0:T(8,128)(2,1)S(1)}, u32[]{:S(2)}, u32[]{:S(2)}) collective-permute-start(bf16[512,1024]{1,0:T(8,128)(2,1)S(1)} %get-tuple-element.62.refs_0_), channel_id=1, source_target_pairs={{2,0},{3,1},{4,6},{5,7},{10,8},{11,9},{12,14},{13,15},{18,16},{19,... | collective-permute-start | bytes 3145736 | tf_op jit(solution)/shard_map/ppermute | solution.py:375
  36.3 23.9 %collective-permute-start.9 = (bf16[512,1024]{1,0:T(8,128)(2,1)S(1)}, bf16[512,1024]{1,0:T(8,128)(2,1)S(1)}, u32[]{:S(2)}, u32[]{:S(2)}) collective-permute-start(bf16[512,1024]{1,0:T(8,128)(2,1)S(1)} %get-tuple-element.61.refs_0_), channel_id=1, source_target_pairs={{2,4},{3,5},{4,2},{5,3},{10,12},{11,13},{12,10},{13,11},{18,20},{1... | collective-permute-start | bytes 3145736 | tf_op jit(solution)/shard_map/ppermute | solution.py:375
  50.5 29.3 %collective-permute-start.18 = (bf16[512,1024]{1,0:T(8,128)(2,1)S(1)}, bf16[512,1024]{1,0:T(8,128)(2,1)S(1)}, u32[]{:S(2)}, u32[]{:S(2)}) collective-permute-start(bf16[512,1024]{1,0:T(8,128)(2,1)S(1)} %get-tuple-element.61.refs_0_), channel_id=1, source_target_pairs={{0,1},{1,0},{2,3},{3,2},{4,5},{5,4},{6,7},{7,6},{8,9},{9,8},{10,11... | collective-permute-start | bytes 3145736 | tf_op jit(solution)/shard_map/ppermute | solution.py:342
  61.0 25.2 %collective-permute-start.17 = (bf16[512,1024]{1,0:T(8,128)(2,1)S(1)}, bf16[512,1024]{1,0:T(8,128)(2,1)S(1)}, u32[]{:S(2)}, u32[]{:S(2)}) collective-permute-start(bf16[512,1024]{1,0:T(8,128)(2,1)S(1)} %chosen.2.refs_0_), channel_id=1, source_target_pairs={{2,0},{3,1},{4,6},{5,7},{0,2},{1,3},{6,4},{7,5},{10,8},{11,9},{12,... | collective-permute-start | bytes 3145736 | tf_op jit(solution)/shard_map/ppermute | solution.py:375
  65.1 25.4 %collective-permute-start.20 = (bf16[512,1024]{1,0:T(8,128)(2,1)S(1)}, bf16[512,1024]{1,0:T(8,128)(2,1)S(1)}, u32[]{:S(2)}, u32[]{:S(2)}) collective-permute-start(bf16[512,1024]{1,0:T(8,128)(2,1)S(1)} %added.5.refs_2_), channel_id=1, source_target_pairs={{0,1},{1,0},{2,3},{3,2},{4,5},{5,4},{6,7},{7,6},{8,9},{9,8},{10,11... | collective-permute-start | bytes 3145736 | tf_op jit(solution)/shard_map/ppermute | solution.py:342
  87.6 14.7 %collective-permute-start.16 = (bf16[512,1024]{1,0:T(8,128)(2,1)S(1)}, bf16[512,1024]{1,0:T(8,128)(2,1)S(1)}, u32[]{:S(2)}, u32[]{:S(2)}) collective-permute-start(bf16[512,1024]{1,0:T(8,128)(2,1)S(1)} %get-tuple-element.69), channel_id=1, source_target_pairs={{0,1},{1,0},{2,3},{3,2},{4,5},{5,4},{6,7},{7,6},{8,9},{9,8},{10,11... | collective-permute-start | bytes 3145736 | tf_op jit(solution)/shard_map/ppermute | solution.py:342
  87.7 16.3 %collective-permute-start.15 = (bf16[512,1024]{1,0:T(8,128)(2,1)S(1)}, bf16[512,1024]{1,0:T(8,128)(2,1)S(1)}, u32[]{:S(2)}, u32[]{:S(2)}) collective-permute-start(bf16[512,1024]{1,0:T(8,128)(2,1)S(1)} %get-tuple-element.68.refs_2_), channel_id=1, source_target_pairs={{0,1},{1,0},{2,3},{3,2},{4,5},{5,4},{6,7},{7,6},{8,9},{9,8},{10,11... | collective-permute-start | bytes 3145736 | tf_op jit(solution)/shard_map/ppermute | solution.py:342
  88.1 25.3 %collective-permute-start.22 = (bf16[512,1024]{1,0:T(8,128)(2,1)S(1)}, bf16[512,1024]{1,0:T(8,128)(2,1)S(1)}, u32[]{:S(2)}, u32[]{:S(2)}) collective-permute-start(bf16[512,1024]{1,0:T(8,128)(2,1)S(1)} %held.8.refs_0_), channel_id=1, source_target_pairs={{0,2},{1,3},{6,4},{7,5},{8,10},{9,11},{14,12},{15,13},{16,18},{17,... | collective-permute-start | bytes 3145736 | tf_op jit(solution)/shard_map/ppermute | solution.py:375
  90.5 22.9 %collective-permute-start.21 = (bf16[512,1024]{1,0:T(8,128)(2,1)S(1)}, bf16[512,1024]{1,0:T(8,128)(2,1)S(1)}, u32[]{:S(2)}, u32[]{:S(2)}) collective-permute-start(bf16[512,1024]{1,0:T(8,128)(2,1)S(1)} %added.6.refs_0_.refs_3_), channel_id=1, source_target_pairs={{2,4},{3,5},{4,2},{5,3},{10,12},{11,13},{12,10},{13,11},{18,20},{1... | collective-permute-start | bytes 3145736 | tf_op jit(solution)/shard_map/ppermute | solution.py:375
  100.5 12.9 %collective-permute-start.23 = (bf16[512,256]{1,0:T(8,128)(2,1)S(1)}, bf16[512,256]{1,0:T(8,128)(2,1)S(1)}, u32[]{:S(2)}, u32[]{:S(2)}) collective-permute-start(bf16[512,256]{1,0:T(8,128)(2,1)S(1)} %get-tuple-element.75), channel_id=1, source_target_pairs={{0,8},{8,0},{16,24},{24,16},{1,9},{9,1},{17,25},{25,17},{2,10},{10... | collective-permute-start | bytes 786440 | tf_op jit(solution)/shard_map/ppermute | solution.py:342
  102.2 13.7 %collective-permute-start.24 = (bf16[512,256]{1,0:T(8,128)(2,1)S(1)}, bf16[512,256]{1,0:T(8,128)(2,1)S(1)}, u32[]{:S(2)}, u32[]{:S(2)}) collective-permute-start(bf16[512,256]{1,0:T(8,128)(2,1)S(1)} %get-tuple-element.76), channel_id=1, source_target_pairs={{0,16},{8,24},{16,0},{24,8},{1,17},{9,25},{17,1},{25,9},{2,18},{10... | collective-permute-start | bytes 786440 | tf_op jit(solution)/shard_map/ppermute | solution.py:342
  104.0 12.0 %collective-permute-start.25 = (bf16[512,256]{1,0:T(8,128)(2,1)S(1)}, bf16[512,256]{1,0:T(8,128)(2,1)S(1)}, u32[]{:S(2)}, u32[]{:S(2)}) collective-permute-start(bf16[512,256]{1,0:T(8,128)(2,1)S(1)} %get-tuple-element.77), channel_id=1, source_target_pairs={{0,24},{8,16},{16,8},{24,0},{1,25},{9,17},{17,9},{25,1},{2,26},{10... | collective-permute-start | bytes 786440 | tf_op jit(solution)/shard_map/ppermute | solution.py:342
  116.3 17.5 %collective-permute-start.27 = (bf16[512,1024]{1,0:T(8,128)(2,1)S(1)}, bf16[512,1024]{1,0:T(8,128)(2,1)S(1)}, u32[]{:S(2)}, u32[]{:S(2)}) collective-permute-start(bf16[512,1024]{1,0:T(8,128)(2,1)S(1)} %added.8.refs_5_), channel_id=1, source_target_pairs={{2,4},{3,5},{4,2},{5,3},{10,12},{11,13},{12,10},{13,11},{18,20},{1... | collective-permute-start | bytes 3145736 | tf_op jit(solution)/shard_map/ppermute | solution.py:375
  117.5 26.1 %collective-permute-start.26 = (bf16[512,1024]{1,0:T(8,128)(2,1)S(1)}, bf16[512,1024]{1,0:T(8,128)(2,1)S(1)}, u32[]{:S(2)}, u32[]{:S(2)}) collective-permute-start(bf16[512,1024]{1,0:T(8,128)(2,1)S(1)} %added.7.refs_4_), channel_id=1, source_target_pairs={{2,0},{3,1},{4,6},{5,7},{0,2},{1,3},{6,4},{7,5},{10,8},{11,9},{12,... | collective-permute-start | bytes 3145736 | tf_op jit(solution)/shard_map/ppermute | solution.py:375
  130.2 15.2 %collective-permute-start.28 = (bf16[544,256]{1,0:T(8,128)(2,1)S(1)}, bf16[544,256]{1,0:T(8,128)(2,1)S(1)}, u32[]{:S(2)}, u32[]{:S(2)}) collective-permute-start(bf16[544,256]{1,0:T(8,128)(2,1)S(1)} %get-tuple-element.83), channel_id=1, source_target_pairs={{0,8},{8,0},{16,24},{24,16},{1,9},{9,1},{17,25},{25,17},{2,10},{10... | collective-permute-start | bytes 835592 | tf_op jit(solution)/shard_map/ppermute | solution.py:342
  131.7 13.7 %collective-permute-start.29 = (bf16[544,256]{1,0:T(8,128)(2,1)S(1)}, bf16[544,256]{1,0:T(8,128)(2,1)S(1)}, u32[]{:S(2)}, u32[]{:S(2)}) collective-permute-start(bf16[544,256]{1,0:T(8,128)(2,1)S(1)} %get-tuple-element.84), channel_id=1, source_target_pairs={{0,16},{8,24},{16,0},{24,8},{1,17},{9,25},{17,1},{25,9},{2,18},{10... | collective-permute-start | bytes 835592 | tf_op jit(solution)/shard_map/ppermute | solution.py:342
  132.9 12.5 %collective-permute-start.30 = (bf16[544,256]{1,0:T(8,128)(2,1)S(1)}, bf16[544,256]{1,0:T(8,128)(2,1)S(1)}, u32[]{:S(2)}, u32[]{:S(2)}) collective-permute-start(bf16[544,256]{1,0:T(8,128)(2,1)S(1)} %get-tuple-element.85), channel_id=1, source_target_pairs={{0,24},{8,16},{16,8},{24,0},{1,25},{9,17},{17,9},{25,1},{2,26},{10... | collective-permute-start | bytes 835592 | tf_op jit(solution)/shard_map/ppermute | solution.py:342
  (11 other events, 64.0 us)

commit v14 on v13

--- a/solution.py
+++ b/solution.py
@@ -247,13 +247,16 @@
     return pltpu.with_memory_space_constraint(array, pltpu.HBM)
 
 
-def prepare_kernel(members, scale, who_ref, key_ref, value_ref, taps_ref, *outputs):
+def prepare_kernel(
+    members, scale, who_ref, key_ref, value_ref, taps_ref, passed_ref, *outputs
+):
     position = who_ref[0]
     step_no = pl.program_id(0)
     rows, channels = key_ref.shape
     share = channels // members
     groups = taps_ref.shape[0] // members
     total_width = taps_ref.shape[1]
+    outputs[members][pl.ds(pl.multiple_of(step_no * rows, rows), rows), :] = passed_ref[...]
     for step in range(members):
         at = position ^ step
         columns = pl.ds(pl.multiple_of(at * share, share), share)
@@ -276,7 +279,7 @@
                 ]
 
 
-def prepare(who, key_gate, value_input, filter_taps, members, scale):
+def prepare(who, key_gate, value_input, filter_taps, passed, members, scale):
     width, channels = key_gate.shape
     share = channels // members
     rows = width + filter_taps.size // members // share
@@ -284,14 +287,15 @@
     part = pl.BlockSpec((tile, channels), lambda i: (i, 0))
     return pl.pallas_call(
         functools.partial(prepare_kernel, members, scale),
-        out_shape=[jax.ShapeDtypeStruct((rows, share), jnp.bfloat16)] * members,
+        out_shape=[jax.ShapeDtypeStruct((rows, share), jnp.bfloat16)] * members
+        + [jax.ShapeDtypeStruct(passed.shape, passed.dtype)],
         grid=(4,),
-        in_specs=[SMEM, part, part, pl.BlockSpec(filter_taps.shape[::-1], lambda i: (0, 0))],
-        out_specs=[VMEM] * members,
+        in_specs=[SMEM, part, part, pl.BlockSpec(filter_taps.shape[::-1], lambda i: (0, 0)), part],
+        out_specs=[VMEM] * (members + 1),
         compiler_params=pltpu.CompilerParams(vmem_limit_bytes=24 * 2**20),
         cost_estimate=COST,
         name="gated_input",
-    )(who, in_hbm(key_gate), in_hbm(value_input), in_hbm(filter_taps.T))
+    )(who, in_hbm(key_gate), in_hbm(value_input), in_hbm(filter_taps.T), in_hbm(passed))
 
 
 def finish_kernel(members, plan_ref, *refs):
@@ -698,10 +702,12 @@
     per_group = channels // groups
     who = jnp.stack([lax.axis_index("ctx"), lax.axis_index("tp")]).astype(jnp.int32)
     plan = planned(who)
+    *packed, out_grad = prepare(
+        who, key_gate, value_input, filter_taps, out_grad, members, scale
+    )
     near, cross = hop(out_grad, INWARD + OUTWARD), hop(out_grad, ACROSS)
     total = cotangent_products(plan, 2 * OWN, both([out_grad]), out_weight)
 
-    packed = prepare(who, key_gate, value_input, filter_taps, members, scale)
     input_parts = traded(packed, "ctx")
     conv_parts, turned, taps = convolve(plan, input_parts, length, per_group, (total,))
     *conv_parts, near, cross = held_until([*conv_parts, near, cross], ())
@@ -714,8 +720,8 @@
             plan, gated_out, out_weight, first, count, other, more, after, tiles, widths
         )
 
-    quarter, half = channels // 4, channels // 2
-    given_far = product(FAR, 1, 1, tiles=2, widths=(3 * quarter, quarter))
+    half = channels // 2
+    given_far = product(FAR, 1, 1, tiles=2, widths=(half, half))
     received = [swapped(part, "tp", 1) for part in given_far]
     (first,) = product(FAR, 1, 0, received, tiles=2)
     far, skip = held_until([far, skip], (first,))

time: 148 us -> 153 us (1.034)
  waiting for transfers between devices: 36.1 us -> 39.2 us
  starting transfers between devices: 36.8 us -> 38.6 us
    ppermute x22, waiting for transfers between devices: 17.9 us -> 20.4 us  [swapped(): return lax.ppermute(array, axis, [(i, i ^ step) for i in range(size)])]
    ppermute x9, starting transfers between devices: 19.9 us -> 21.9 us  [hop(): lax.ppermute(array, 'tp', [(2 * i + core, 2 * j + core) for i, j in pairs...]
  transfers between devices with their start and end apart: 31 -> 31, of which waited for: 10 -> 14; matrix products, arithmetic and copies ran while one was open for 0% -> 0% of each run, Pallas kernels for 48% -> 45%
where the time goes in v14:
time: 153 us; the launch traced here: 152 us
  Pallas kernels  73.6 us (48%)
  waiting for transfers between devices  39.2 us (26%)
  starting transfers between devices  38.6 us (25%)
    pallas_call x6, Pallas kernels, column_products(): pl.pallas_call(functools.partial(product_kernel, steps, [part.shape[1] fo...  23.7 us
    ppermute x9, starting transfers between devices, hop(): lax.ppermute(array, 'tp', [(2 * i + core, 2 * j + core) for i, j in pairs...  21.9 us
    ppermute x22, waiting for transfers between devices, swapped(): return lax.ppermute(array, axis, [(i, i ^ step) for i in range(size)])  20.4 us
    ppermute x9, waiting for transfers between devices, hop(): lax.ppermute(array, 'tp', [(2 * i + core, 2 * j + core) for i, j in pairs...  18.8 us
    ppermute x22, starting transfers between devices, swapped(): return lax.ppermute(array, axis, [(i, i ^ step) for i in range(size)])  16.6 us
    pallas_call x3, Pallas kernels, cotangent_products(): pl.pallas_call(functools.partial(cotangent_kernel, count, begin), out_sha...  15.9 us
    pallas_call x1, Pallas kernels, correlate(): pl.pallas_call(functools.partial(backward_kernel, members, batch, per_gro...  8.89 us
    pallas_call x1, Pallas kernels, convolve(): pl.pallas_call(functools.partial(forward_kernel, members, per_group, widt...  5.65 us
  transfers between devices with their start and end apart: 31, of which 14 were waited for; matrix products, arithmetic and copies ran while one was open for 0% of the time, Pallas kernels for 45%

profile of v14, /device:TPU:0, one launch (start us, length us, event | category | flops | bytes accessed | tf_op | source)
XLA Modules:
  0.0 152.4 jit_solution(6299315673205135199)
XLA Ops:
  0.7 2.8 %gated_input.1 = (bf16[544,256]{1,0:T(8,128)(2,1)S(1)}, bf16[544,256]{1,0:T(8,128)(2,1)S(1)}, bf16[544,256]{1,0:T(8,128)(2,1)S(1)}, bf16[544,256]{1,0:T(8,128)(2,1)S(1)}, bf16[512,1024]{1,0:T(8,128)(2,1)S(1)}) custom-call(s32[2]{0:T(128)S(1)} %pad_add_fusion.who_ref, bf16[512,1024]{1,0:T(8,128)(2,1)} %refs_4_.3, bf16[512,1024]{1,0:T(8,128)(2,1)} %refs_5_.1, ...), custom_call_target="tpu_custom_call" | custom-call | flops 1048576 | bytes 4096 | tf_op jit(solution)/shard_map/gated_input/pallas_call | solution.py:288
  4.8 5.4 %collective-permute-start.4 = (bf16[512,1024]{1,0:T(8,128)(2,1)S(1)}, bf16[512,1024]{1,0:T(8,128)(2,1)S(1)}, u32[]{:S(2)}, u32[]{:S(2)}) collective-permute-start(bf16[512,1024]{1,0:T(8,128)(2,1)S(1)} %get-tuple-element.52.refs_0_), channel_id=1, source_target_pairs={{0,2},{1,3},{6,4},{7,5},{2,0},{3,1},{4,6},{5,7},{8,10},{9,11},{14,... | collective-permute-start | bytes 3145736 | tf_op jit(solution)/shard_map/ppermute | solution.py:379
  14.9 4.8 %cotangent_blocks.3.refs_4_.refs_3_ = f32[512,1024]{1,0:T(8,128)S(1)} custom-call(s32[10]{0:T(128)S(1)} %plan.1._.plan_ref, bf16[1024,8192]{1,0:T(8,128)(2,1)} %weight_ref.19, bf16[512,1024]{1,0:T(8,128)(2,1)S(1)} %get-tuple-element.52.refs_0_, bf16[512,1024]{1,0:T(8,128)(2,1)S(1)} %collective-permute-done.3.refs_1_), custom_call_target="tpu_custom_call" | custom-call | flops 1048576 | bytes 4096 | tf_op jit(solution)/shard_map/cotangent_blocks/pallas_call | solution.py:644
  19.8 6.1 %collective-permute-done.1.refs_2_ = bf16[544,256]{1,0:T(8,128)(2,1)S(1)} collective-permute-done((bf16[544,256]{1,0:T(8,128)(2,1)S(1)}, bf16[544,256]{1,0:T(8,128)(2,1)S(1)}, u32[]{:S(2)}, u32[]{:S(2)}) %collective-permute-start.1) | collective-permute-done | bytes 278560 | tf_op jit(solution)/shard_map/ppermute | solution.py:346
  25.9 5.6 %causal_conv.1 = (bf16[512,256]{1,0:T(8,128)(2,1)S(1)}, bf16[512,256]{1,0:T(8,128)(2,1)S(1)}, bf16[512,256]{1,0:T(8,128)(2,1)S(1)}, bf16[512,256]{1,0:T(8,128)(2...) custom-call(s32[10]{0:T(128)S(1)} %plan.1._.plan_ref, bf16[544,256]{1,0:T(8,128)(2,1)S(1)} %get-tuple-element.48.refs_0_, ...), custom_call_target="tpu_custom_call" | custom-call | flops 1048576 | bytes 4096 | tf_op jit(solution)/shard_map/causal_conv/pallas_call | solution.py:188
  39.3 3.4 %lag_matrices.1.refs_5_.lag_ref = bf16[16,128,2048]{2,1,0:T(8,128)(2,1)S(1)} custom-call(f32[16,2048]{1,0:T(8,128)S(1)} %get-tuple-element.61.taps_ref), custom_call_target="tpu_custom_call" | custom-call | flops 1048576 | bytes 4096 | tf_op jit(solution)/shard_map/lag_matrices/pallas_call | solution.py:207
  42.8 2.3 %collective-permute-done.6.refs_1_ = bf16[512,256]{1,0:T(8,128)(2,1)S(1)} collective-permute-done((bf16[512,256]{1,0:T(8,128)(2,1)S(1)}, bf16[512,256]{1,0:T(8,128)(2,1)S(1)}, u32[]{:S(2)}, u32[]{:S(2)}) %collective-permute-start.6) | collective-permute-done | bytes 262176 | tf_op jit(solution)/shard_map/ppermute | solution.py:346
  45.1 5.5 %collective-permute-done.7.refs_2_ = bf16[512,256]{1,0:T(8,128)(2,1)S(1)} collective-permute-done((bf16[512,256]{1,0:T(8,128)(2,1)S(1)}, bf16[512,256]{1,0:T(8,128)(2,1)S(1)}, u32[]{:S(2)}, u32[]{:S(2)}) %collective-permute-start.7) | collective-permute-done | bytes 262176 | tf_op jit(solution)/shard_map/ppermute | solution.py:346
  51.5 3.4 %projection_blocks.6 = (bf16[512,512]{1,0:T(8,128)(2,1)S(1)}, bf16[512,512]{1,0:T(8,128)(2,1)S(1)}) custom-call(s32[10]{0:T(128)S(1)} %plan.1._.plan_ref, bf16[512,1024]{1,0:T(8,128)(2,1)S(1)} %get-tuple-element.62.data_ref, bf16[1024,8192]{1,0:T(8,128)(2,1)} %weight_ref.19), custom_call_target="tpu_custom_call" | custom-call | flops 1048576 | bytes 4096 | tf_op jit(solution)/shard_map/projection_blocks/pallas_call | solution.py:545
  57.6 3.5 %projection_blocks.7.refs_2_.end_ref.refs_0_ = bf16[512,1024]{1,0:T(8,128)(2,1)S(1)} custom-call(s32[10]{0:T(128)S(1)} %plan.1._.plan_ref, bf16[512,1024]{1,0:T(8,128)(2,1)S(1)} %get-tuple-element.62.data_ref, bf16[1024,8192]{1,0:T(8,128)(2,1)} %weight_ref.19, bf16[512,512]{1,0:T(8,128)(2,1)S(1)} %collective-permute-done.11.refs_0_, ...), custom_call_target="tpu_custom_call" | custom-call | flops 1048576 | bytes 4096 | tf_op jit(solution)/shard_map/projection_blocks/pallas_call | solution.py:545
  61.9 3.8 %collective-permute-start.17 = (bf16[512,1024]{1,0:T(8,128)(2,1)S(1)}, bf16[512,1024]{1,0:T(8,128)(2,1)S(1)}, u32[]{:S(2)}, u32[]{:S(2)}) collective-permute-start(bf16[512,1024]{1,0:T(8,128)(2,1)S(1)} %chosen.2.refs_0_), channel_id=1, source_target_pairs={{2,0},{3,1},{4,6},{5,7},{0,2},{1,3},{6,4},{7,5},{10,8},{11,9},{12,... | collective-permute-start | bytes 3145736 | tf_op jit(solution)/shard_map/ppermute | solution.py:379
  66.1 3.4 %projection_blocks.8 = (bf16[512,512]{1,0:T(8,128)(2,1)S(1)}, bf16[512,512]{1,0:T(8,128)(2,1)S(1)}) custom-call(s32[10]{0:T(128)S(1)} %plan.1._.plan_ref, bf16[512,1024]{1,0:T(8,128)(2,1)S(1)} %get-tuple-element.62.data_ref, bf16[1024,8192]{1,0:T(8,128)(2,1)} %weight_ref.19, bf16[512,1024]{1,0:T(8,128)(2,1)S(1)} %chosen.2.refs_0_), custom_call_target="tpu_custom_call" | custom-call | flops 1048576 | bytes 4096 | tf_op jit(solution)/shard_map/projection_blocks/pallas_call | solution.py:545
  72.3 3.5 %projection_blocks.9.refs_0_.refs_4_ = bf16[512,1024]{1,0:T(8,128)(2,1)S(1)} custom-call(s32[10]{0:T(128)S(1)} %plan.1._.plan_ref, bf16[512,1024]{1,0:T(8,128)(2,1)S(1)} %get-tuple-element.62.data_ref, bf16[1024,8192]{1,0:T(8,128)(2,1)} %weight_ref.19, bf16[512,512]{1,0:T(8,128)(2,1)S(1)} %collective-permute-done.13.refs_0_, ...), custom_call_target="tpu_custom_call" | custom-call | flops 1048576 | bytes 4096 | tf_op jit(solution)/shard_map/projection_blocks/pallas_call | solution.py:545
  75.8 4.9 %projection_blocks.10 = (bf16[512,1024]{1,0:T(8,128)(2,1)S(1)}, bf16[512,1024]{1,0:T(8,128)(2,1)S(1)}) custom-call(s32[10]{0:T(128)S(1)} %plan.1._.plan_ref, bf16[512,1024]{1,0:T(8,128)(2,1)S(1)} %get-tuple-element.62.data_ref, bf16[1024,8192]{1,0:T(8,128)(2,1)} %weight_ref.19, bf16[512,1024]{1,0:T(8,128)(2,1)S(1)} %projection_blocks.9.refs_0_.refs_4_), custom_call_target="tpu_custom_call" | custom-call | flops 1048576 | bytes 4096 | tf_op jit(solution)/shard_map/projection_blocks/pallas_call | solution.py:545
  80.7 6.4 %cotangent_blocks.4.refs_1_.refs_2_ = f32[512,1024]{1,0:T(8,128)S(1)} custom-call(s32[10]{0:T(128)S(1)} %plan.1._.plan_ref, bf16[1024,8192]{1,0:T(8,128)(2,1)} %weight_ref.19, bf16[512,1024]{1,0:T(8,128)(2,1)S(1)} %get-tuple-element.63.refs_0_, bf16[512,1024]{1,0:T(8,128)(2,1)S(1)} %collective-permute-done.18.refs_1_, bf16[512,1024]{1,0:T(8,128)(2,1)S(1)} %added.5.refs_2_, ...), custom_call_target="tpu_custom_call" | custom-call | flops 1048576 | bytes 4096 | tf_op jit(solution)/shard_map/cotangent_blocks/pallas_call | solution.py:644
  90.8 3.7 %collective-permute-start.22 = (bf16[512,1024]{1,0:T(8,128)(2,1)S(1)}, bf16[512,1024]{1,0:T(8,128)(2,1)S(1)}, u32[]{:S(2)}, u32[]{:S(2)}) collective-permute-start(bf16[512,1024]{1,0:T(8,128)(2,1)S(1)} %held.8.refs_0_), channel_id=1, source_target_pairs={{0,2},{1,3},{6,4},{7,5},{8,10},{9,11},{14,12},{15,13},{16,18},{17,... | collective-permute-start | bytes 3145736 | tf_op jit(solution)/shard_map/ppermute | solution.py:379
  95.2 4.8 %cotangent_blocks.5.start_ref = f32[512,1024]{1,0:T(8,128)S(1)} custom-call(s32[10]{0:T(128)S(1)} %plan.1._.plan_ref, bf16[1024,8192]{1,0:T(8,128)(2,1)} %weight_ref.19, bf16[512,1024]{1,0:T(8,128)(2,1)S(1)} %collective-permute-done.20.refs_0_, bf16[512,1024]{1,0:T(8,128)(2,1)S(1)} %chosen.3.refs_1_, f32[512,1024]{1,0:T(8,128)S(1)} %cotangent_blocks.4.refs_1_.refs_2_, ...), custom_call_target="tpu_custom_call" | custom-call | flops 1048576 | bytes 4096 | tf_op jit(solution)/shard_map/cotangent_blocks/pallas_call | solution.py:644
  100.0 4.5 %cotangent_last.1 = (bf16[512,1024]{1,0:T(8,128)(2,1)}, bf16[512,256]{1,0:T(8,128)(2,1)S(1)}, bf16[512,256]{1,0:T(8,128)(2,1)S(1)}, bf16[512,256]{1,0:T(8,128)(2,1)S(1)}, bf16[512,256]{1,0:T(8,128)(2,1)S(1)}) custom-call(s32[10]{0:T(128)S(1)} %plan.1._.plan_ref, bf16[1024,8192]{1,0:T(8,128)(2,1)} %weight_ref.19, ...), custom_call_target="tpu_custom_call" | custom-call | flops 1048576 | bytes 4096 | tf_op jit(solution)/shard_map/cotangent_last/pallas_call | solution.py:610
  108.0 5.1 %projection_blocks.11 = (bf16[512,1024]{1,0:T(8,128)(2,1)S(1)}, bf16[512,1024]{1,0:T(8,128)(2,1)S(1)}) custom-call(s32[10]{0:T(128)S(1)} %plan.1._.plan_ref, bf16[512,1024]{1,0:T(8,128)(2,1)S(1)} %get-tuple-element.62.data_ref, bf16[1024,8192]{1,0:T(8,128)(2,1)} %weight_ref.19, bf16[512,1024]{1,0:T(8,128)(2,1)S(1)} %collective-permute-done.15.refs_0_, ...), custom_call_target="tpu_custom_call" | custom-call | flops 1048576 | bytes 4096 | tf_op jit(solution)/shard_map/projection_blocks/pallas_call | solution.py:545
  113.2 4.2 %collective-permute-done.22.refs_1_ = bf16[512,1024]{1,0:T(8,128)(2,1)S(1)} collective-permute-done((bf16[512,1024]{1,0:T(8,128)(2,1)S(1)}, bf16[512,1024]{1,0:T(8,128)(2,1)S(1)}, u32[]{:S(2)}, u32[]{:S(2)}) %collective-permute-start.22) | collective-permute-done | bytes 1048608 | tf_op jit(solution)/shard_map/ppermute | solution.py:379
  121.0 4.6 %collective-permute-start.26 = (bf16[512,1024]{1,0:T(8,128)(2,1)S(1)}, bf16[512,1024]{1,0:T(8,128)(2,1)S(1)}, u32[]{:S(2)}, u32[]{:S(2)}) collective-permute-start(bf16[512,1024]{1,0:T(8,128)(2,1)S(1)} %added.7.refs_4_), channel_id=1, source_target_pairs={{2,0},{3,1},{4,6},{5,7},{0,2},{1,3},{6,4},{7,5},{10,8},{11,9},{12,... | collective-permute-start | bytes 3145736 | tf_op jit(solution)/shard_map/ppermute | solution.py:379
  125.6 8.9 %causal_conv_grads.1 = (bf16[544,256]{1,0:T(8,128)(2,1)S(1)}, bf16[544,256]{1,0:T(8,128)(2,1)S(1)}, bf16[544,256]{1,0:T(8,128)(2,1)S(1)}, bf16[544,256]{1,0:T(8,128)(2,1)S(1)}) custom-call(s32[10]{0:T(128)S(1)} %plan.1._.plan_ref, bf16[4,256,512]{2,1,0:T(8,128)(2,1)S(1)} %get-tuple-element.83.in_scr, bf16[16,128,2048]{2,1,0:T(8,128)(2,1)S(1)} %lag_matrices.1.refs_5_.lag_ref, ...), custom_call_target="tpu_custom_call" | custom-call | flops 1048576 | bytes 4096 | tf_op jit(solution)/shard_map/causal_conv_grads/pallas_call | solution.py:226
  138.1 10.3 %collective-permute-done.26.refs_1_ = bf16[512,1024]{1,0:T(8,128)(2,1)S(1)} collective-permute-done((bf16[512,1024]{1,0:T(8,128)(2,1)S(1)}, bf16[512,1024]{1,0:T(8,128)(2,1)S(1)}, u32[]{:S(2)}, u32[]{:S(2)}) %collective-permute-start.26) | collective-permute-done | bytes 1048608 | tf_op jit(solution)/shard_map/ppermute | solution.py:379
  150.1 2.3 %input_gradients.1 = (bf16[512,1024]{1,0:T(8,128)(2,1)}, bf16[512,1024]{1,0:T(8,128)(2,1)}, f32[64,512]{1,0:T(8,128)}) custom-call(s32[10]{0:T(128)S(1)} %plan.1._.plan_ref, bf16[544,256]{1,0:T(8,128)(2,1)S(1)} %get-tuple-element.84.refs_0_, bf16[544,256]{1,0:T(8,128)(2,1)S(1)} %collective-permute-done.28.refs_1_, ...), custom_call_target="tpu_custom_call" | custom-call | flops 1048576 | bytes 4096 | tf_op jit(solution)/shard_map/input_gradients/pallas_call | solution.py:332
  (74 shorter events, 38.1 us)
Async XLA Ops:
  4.1 27.5 %collective-permute-start.5 = (bf16[512,1024]{1,0:T(8,128)(2,1)S(1)}, bf16[512,1024]{1,0:T(8,128)(2,1)S(1)}, u32[]{:S(2)}, u32[]{:S(2)}) collective-permute-start(bf16[512,1024]{1,0:T(8,128)(2,1)S(1)} %get-tuple-element.52.refs_0_), channel_id=1, source_target_pairs={{2,4},{3,5},{4,2},{5,3},{10,12},{11,13},{12,10},{13,11},{18,20},{1... | collective-permute-start | bytes 3145736 | tf_op jit(solution)/shard_map/ppermute | solution.py:379
  4.8 28.9 %collective-permute-start.4 = (bf16[512,1024]{1,0:T(8,128)(2,1)S(1)}, bf16[512,1024]{1,0:T(8,128)(2,1)S(1)}, u32[]{:S(2)}, u32[]{:S(2)}) collective-permute-start(bf16[512,1024]{1,0:T(8,128)(2,1)S(1)} %get-tuple-element.52.refs_0_), channel_id=1, source_target_pairs={{0,2},{1,3},{6,4},{7,5},{2,0},{3,1},{4,6},{5,7},{8,10},{9,11},{14,... | collective-permute-start | bytes 3145736 | tf_op jit(solution)/shard_map/ppermute | solution.py:379
  11.7 14.2 %collective-permute-start.1 = (bf16[544,256]{1,0:T(8,128)(2,1)S(1)}, bf16[544,256]{1,0:T(8,128)(2,1)S(1)}, u32[]{:S(2)}, u32[]{:S(2)}) collective-permute-start(bf16[544,256]{1,0:T(8,128)(2,1)S(1)} %get-tuple-element.50), channel_id=1, source_target_pairs={{0,16},{8,24},{16,0},{24,8},{1,17},{9,25},{17,1},{25,9},{2,18},{10... | collective-permute-start | bytes 835592 | tf_op jit(solution)/shard_map/ppermute | solution.py:346
  13.2 12.7 %collective-permute-start.2 = (bf16[544,256]{1,0:T(8,128)(2,1)S(1)}, bf16[544,256]{1,0:T(8,128)(2,1)S(1)}, u32[]{:S(2)}, u32[]{:S(2)}) collective-permute-start(bf16[544,256]{1,0:T(8,128)(2,1)S(1)} %get-tuple-element.51), channel_id=1, source_target_pairs={{0,24},{8,16},{16,8},{24,0},{1,25},{9,17},{17,9},{25,1},{2,26},{10... | collective-permute-start | bytes 835592 | tf_op jit(solution)/shard_map/ppermute | solution.py:346
  33.8 27.3 %collective-permute-start.10 = (bf16[512,1024]{1,0:T(8,128)(2,1)S(1)}, bf16[512,1024]{1,0:T(8,128)(2,1)S(1)}, u32[]{:S(2)}, u32[]{:S(2)}) collective-permute-start(bf16[512,1024]{1,0:T(8,128)(2,1)S(1)} %get-tuple-element.64.refs_0_), channel_id=1, source_target_pairs={{2,0},{3,1},{4,6},{5,7},{10,8},{11,9},{12,14},{13,15},{18,16},{19,... | collective-permute-start | bytes 3145736 | tf_op jit(solution)/shard_map/ppermute | solution.py:379
  35.0 26.0 %collective-permute-start.9 = (bf16[512,1024]{1,0:T(8,128)(2,1)S(1)}, bf16[512,1024]{1,0:T(8,128)(2,1)S(1)}, u32[]{:S(2)}, u32[]{:S(2)}) collective-permute-start(bf16[512,1024]{1,0:T(8,128)(2,1)S(1)} %get-tuple-element.63.refs_0_), channel_id=1, source_target_pairs={{2,4},{3,5},{4,2},{5,3},{10,12},{11,13},{12,10},{13,11},{18,20},{1... | collective-permute-start | bytes 3145736 | tf_op jit(solution)/shard_map/ppermute | solution.py:379
  37.3 13.3 %collective-permute-start.7 = (bf16[512,256]{1,0:T(8,128)(2,1)S(1)}, bf16[512,256]{1,0:T(8,128)(2,1)S(1)}, u32[]{:S(2)}, u32[]{:S(2)}) collective-permute-start(bf16[512,256]{1,0:T(8,128)(2,1)S(1)} %get-tuple-element.59), channel_id=1, source_target_pairs={{0,16},{8,24},{16,0},{24,8},{1,17},{9,25},{17,1},{25,9},{2,18},{10... | collective-permute-start | bytes 786440 | tf_op jit(solution)/shard_map/ppermute | solution.py:346
  38.9 11.7 %collective-permute-start.8 = (bf16[512,256]{1,0:T(8,128)(2,1)S(1)}, bf16[512,256]{1,0:T(8,128)(2,1)S(1)}, u32[]{:S(2)}, u32[]{:S(2)}) collective-permute-start(bf16[512,256]{1,0:T(8,128)(2,1)S(1)} %get-tuple-element.60), channel_id=1, source_target_pairs={{0,24},{8,16},{16,8},{24,0},{1,25},{9,17},{17,9},{25,1},{2,26},{10... | collective-permute-start | bytes 786440 | tf_op jit(solution)/shard_map/ppermute | solution.py:346
  55.4 25.3 %collective-permute-start.18 = (bf16[512,1024]{1,0:T(8,128)(2,1)S(1)}, bf16[512,1024]{1,0:T(8,128)(2,1)S(1)}, u32[]{:S(2)}, u32[]{:S(2)}) collective-permute-start(bf16[512,1024]{1,0:T(8,128)(2,1)S(1)} %get-tuple-element.63.refs_0_), channel_id=1, source_target_pairs={{0,1},{1,0},{2,3},{3,2},{4,5},{5,4},{6,7},{7,6},{8,9},{9,8},{10,11... | collective-permute-start | bytes 3145736 | tf_op jit(solution)/shard_map/ppermute | solution.py:346
  61.9 27.3 %collective-permute-start.17 = (bf16[512,1024]{1,0:T(8,128)(2,1)S(1)}, bf16[512,1024]{1,0:T(8,128)(2,1)S(1)}, u32[]{:S(2)}, u32[]{:S(2)}) collective-permute-start(bf16[512,1024]{1,0:T(8,128)(2,1)S(1)} %chosen.2.refs_0_), channel_id=1, source_target_pairs={{2,0},{3,1},{4,6},{5,7},{0,2},{1,3},{6,4},{7,5},{10,8},{11,9},{12,... | collective-permute-start | bytes 3145736 | tf_op jit(solution)/shard_map/ppermute | solution.py:379
  66.0 28.5 %collective-permute-start.20 = (bf16[512,1024]{1,0:T(8,128)(2,1)S(1)}, bf16[512,1024]{1,0:T(8,128)(2,1)S(1)}, u32[]{:S(2)}, u32[]{:S(2)}) collective-permute-start(bf16[512,1024]{1,0:T(8,128)(2,1)S(1)} %added.5.refs_2_), channel_id=1, source_target_pairs={{0,1},{1,0},{2,3},{3,2},{4,5},{5,4},{6,7},{7,6},{8,9},{9,8},{10,11... | collective-permute-start | bytes 3145736 | tf_op jit(solution)/shard_map/ppermute | solution.py:346
  90.1 9.9 %collective-permute-start.19 = (bf16[512,1024]{1,0:T(8,128)(2,1)S(1)}, bf16[512,1024]{1,0:T(8,128)(2,1)S(1)}, u32[]{:S(2)}, u32[]{:S(2)}) collective-permute-start(bf16[512,1024]{1,0:T(8,128)(2,1)S(1)} %chosen.3.refs_1_), channel_id=1, source_target_pairs={{0,1},{1,0},{2,3},{3,2},{4,5},{5,4},{6,7},{7,6},{8,9},{9,8},{10,11... | collective-permute-start | bytes 3145736 | tf_op jit(solution)/shard_map/ppermute | solution.py:346
  90.2 15.6 %collective-permute-start.16 = (bf16[512,1024]{1,0:T(8,128)(2,1)S(1)}, bf16[512,1024]{1,0:T(8,128)(2,1)S(1)}, u32[]{:S(2)}, u32[]{:S(2)}) collective-permute-start(bf16[512,1024]{1,0:T(8,128)(2,1)S(1)} %get-tuple-element.71), channel_id=1, source_target_pairs={{0,1},{1,0},{2,3},{3,2},{4,5},{5,4},{6,7},{7,6},{8,9},{9,8},{10,11... | collective-permute-start | bytes 3145736 | tf_op jit(solution)/shard_map/ppermute | solution.py:346
  90.7 15.9 %collective-permute-start.15 = (bf16[512,1024]{1,0:T(8,128)(2,1)S(1)}, bf16[512,1024]{1,0:T(8,128)(2,1)S(1)}, u32[]{:S(2)}, u32[]{:S(2)}) collective-permute-start(bf16[512,1024]{1,0:T(8,128)(2,1)S(1)} %get-tuple-element.70.refs_2_), channel_id=1, source_target_pairs={{0,1},{1,0},{2,3},{3,2},{4,5},{5,4},{6,7},{7,6},{8,9},{9,8},{10,11... | collective-permute-start | bytes 3145736 | tf_op jit(solution)/shard_map/ppermute | solution.py:346
  90.8 26.7 %collective-permute-start.22 = (bf16[512,1024]{1,0:T(8,128)(2,1)S(1)}, bf16[512,1024]{1,0:T(8,128)(2,1)S(1)}, u32[]{:S(2)}, u32[]{:S(2)}) collective-permute-start(bf16[512,1024]{1,0:T(8,128)(2,1)S(1)} %held.8.refs_0_), channel_id=1, source_target_pairs={{0,2},{1,3},{6,4},{7,5},{8,10},{9,11},{14,12},{15,13},{16,18},{17,... | collective-permute-start | bytes 3145736 | tf_op jit(solution)/shard_map/ppermute | solution.py:379
  94.5 22.9 %collective-permute-start.21 = (bf16[512,1024]{1,0:T(8,128)(2,1)S(1)}, bf16[512,1024]{1,0:T(8,128)(2,1)S(1)}, u32[]{:S(2)}, u32[]{:S(2)}) collective-permute-start(bf16[512,1024]{1,0:T(8,128)(2,1)S(1)} %added.6.refs_0_.refs_3_), channel_id=1, source_target_pairs={{2,4},{3,5},{4,2},{5,3},{10,12},{11,13},{12,10},{13,11},{18,20},{1... | collective-permute-start | bytes 3145736 | tf_op jit(solution)/shard_map/ppermute | solution.py:379
  104.5 12.9 %collective-permute-start.23 = (bf16[512,256]{1,0:T(8,128)(2,1)S(1)}, bf16[512,256]{1,0:T(8,128)(2,1)S(1)}, u32[]{:S(2)}, u32[]{:S(2)}) collective-permute-start(bf16[512,256]{1,0:T(8,128)(2,1)S(1)} %get-tuple-element.77), channel_id=1, source_target_pairs={{0,8},{8,0},{16,24},{24,16},{1,9},{9,1},{17,25},{25,17},{2,10},{10... | collective-permute-start | bytes 786440 | tf_op jit(solution)/shard_map/ppermute | solution.py:346
  105.7 12.1 %collective-permute-start.24 = (bf16[512,256]{1,0:T(8,128)(2,1)S(1)}, bf16[512,256]{1,0:T(8,128)(2,1)S(1)}, u32[]{:S(2)}, u32[]{:S(2)}) collective-permute-start(bf16[512,256]{1,0:T(8,128)(2,1)S(1)} %get-tuple-element.78), channel_id=1, source_target_pairs={{0,16},{8,24},{16,0},{24,8},{1,17},{9,25},{17,1},{25,9},{2,18},{10... | collective-permute-start | bytes 786440 | tf_op jit(solution)/shard_map/ppermute | solution.py:346
  106.6 12.9 %collective-permute-start.25 = (bf16[512,256]{1,0:T(8,128)(2,1)S(1)}, bf16[512,256]{1,0:T(8,128)(2,1)S(1)}, u32[]{:S(2)}, u32[]{:S(2)}) collective-permute-start(bf16[512,256]{1,0:T(8,128)(2,1)S(1)} %get-tuple-element.79), channel_id=1, source_target_pairs={{0,24},{8,16},{16,8},{24,0},{1,25},{9,17},{17,9},{25,1},{2,26},{10... | collective-permute-start | bytes 786440 | tf_op jit(solution)/shard_map/ppermute | solution.py:346
  119.8 18.3 %collective-permute-start.27 = (bf16[512,1024]{1,0:T(8,128)(2,1)S(1)}, bf16[512,1024]{1,0:T(8,128)(2,1)S(1)}, u32[]{:S(2)}, u32[]{:S(2)}) collective-permute-start(bf16[512,1024]{1,0:T(8,128)(2,1)S(1)} %added.8.refs_5_), channel_id=1, source_target_pairs={{2,4},{3,5},{4,2},{5,3},{10,12},{11,13},{12,10},{13,11},{18,20},{1... | collective-permute-start | bytes 3145736 | tf_op jit(solution)/shard_map/ppermute | solution.py:379
  121.0 27.3 %collective-permute-start.26 = (bf16[512,1024]{1,0:T(8,128)(2,1)S(1)}, bf16[512,1024]{1,0:T(8,128)(2,1)S(1)}, u32[]{:S(2)}, u32[]{:S(2)}) collective-permute-start(bf16[512,1024]{1,0:T(8,128)(2,1)S(1)} %added.7.refs_4_), channel_id=1, source_target_pairs={{2,0},{3,1},{4,6},{5,7},{0,2},{1,3},{6,4},{7,5},{10,8},{11,9},{12,... | collective-permute-start | bytes 3145736 | tf_op jit(solution)/shard_map/ppermute | solution.py:379
  134.5 15.5 %collective-permute-start.28 = (bf16[544,256]{1,0:T(8,128)(2,1)S(1)}, bf16[544,256]{1,0:T(8,128)(2,1)S(1)}, u32[]{:S(2)}, u32[]{:S(2)}) collective-permute-start(bf16[544,256]{1,0:T(8,128)(2,1)S(1)} %get-tuple-element.85), channel_id=1, source_target_pairs={{0,8},{8,0},{16,24},{24,16},{1,9},{9,1},{17,25},{25,17},{2,10},{10... | collective-permute-start | bytes 835592 | tf_op jit(solution)/shard_map/ppermute | solution.py:346
  135.8 14.2 %collective-permute-start.29 = (bf16[544,256]{1,0:T(8,128)(2,1)S(1)}, bf16[544,256]{1,0:T(8,128)(2,1)S(1)}, u32[]{:S(2)}, u32[]{:S(2)}) collective-permute-start(bf16[544,256]{1,0:T(8,128)(2,1)S(1)} %get-tuple-element.86), channel_id=1, source_target_pairs={{0,16},{8,24},{16,0},{24,8},{1,17},{9,25},{17,1},{25,9},{2,18},{10... | collective-permute-start | bytes 835592 | tf_op jit(solution)/shard_map/ppermute | solution.py:346
  136.7 13.4 %collective-permute-start.30 = (bf16[544,256]{1,0:T(8,128)(2,1)S(1)}, bf16[544,256]{1,0:T(8,128)(2,1)S(1)}, u32[]{:S(2)}, u32[]{:S(2)}) collective-permute-start(bf16[544,256]{1,0:T(8,128)(2,1)S(1)} %get-tuple-element.87), channel_id=1, source_target_pairs={{0,24},{8,16},{16,8},{24,0},{1,25},{9,17},{17,9},{25,1},{2,26},{10... | collective-permute-start | bytes 835592 | tf_op jit(solution)/shard_map/ppermute | solution.py:346
  (10 other events, 52.2 us)

commit v15 on v13

--- a/solution.py
+++ b/solution.py
@@ -704,7 +704,8 @@
     packed = prepare(who, key_gate, value_input, filter_taps, members, scale)
     input_parts = traded(packed, "ctx")
     conv_parts, turned, taps = convolve(plan, input_parts, length, per_group, (total,))
-    *conv_parts, near, cross = held_until([*conv_parts, near, cross], ())
+    *conv_parts, near = held_until([*conv_parts, near], ())
+    (cross,) = held_until([cross], (near,))
     far, skip = hop(near, ACROSS), hop(cross, OUTWARD)
     lags = lag_matrices(taps)
     gated_out, convolved = gated(plan, traded(conv_parts, "ctx"), query_gate, (lags,))
@@ -714,8 +715,8 @@
             plan, gated_out, out_weight, first, count, other, more, after, tiles, widths
         )
 
-    quarter, half = channels // 4, channels // 2
-    given_far = product(FAR, 1, 1, tiles=2, widths=(3 * quarter, quarter))
+    half = channels // 2
+    given_far = product(FAR, 1, 1, tiles=2, widths=(half, half))
     received = [swapped(part, "tp", 1) for part in given_far]
     (first,) = product(FAR, 1, 0, received, tiles=2)
     far, skip = held_until([far, skip], (first,))

time: 148 us -> 149 us (level)
    ppermute x22, waiting for transfers between devices: 17.9 us -> 19.7 us  [swapped(): return lax.ppermute(array, axis, [(i, i ^ step) for i in range(size)])]
  transfers between devices with their start and end apart: 31 -> 31, of which waited for: 10 -> 13; matrix products, arithmetic and copies ran while one was open for 0% -> 0% of each run, Pallas kernels for 48% -> 48%
where the time goes in v15:
time: 149 us
  Pallas kernels  73.7 us (49%)
  waiting for transfers between devices  37.4 us (25%)
  starting transfers between devices  36.7 us (25%)
    pallas_call x6, Pallas kernels, column_products(): pl.pallas_call(functools.partial(product_kernel, steps, [part.shape[1] fo...  23.7 us
    ppermute x9, starting transfers between devices, hop(): lax.ppermute(array, 'tp', [(2 * i + core, 2 * j + core) for i, j in pairs...  20 us
    ppermute x22, waiting for transfers between devices, swapped(): return lax.ppermute(array, axis, [(i, i ^ step) for i in range(size)])  19.7 us
    ppermute x9, waiting for transfers between devices, hop(): lax.ppermute(array, 'tp', [(2 * i + core, 2 * j + core) for i, j in pairs...  17.7 us
    ppermute x22, starting transfers between devices, swapped(): return lax.ppermute(array, axis, [(i, i ^ step) for i in range(size)])  16.7 us
    pallas_call x3, Pallas kernels, cotangent_products(): pl.pallas_call(functools.partial(cotangent_kernel, count, begin), out_sha...  16.2 us
    pallas_call x1, Pallas kernels, correlate(): pl.pallas_call(functools.partial(backward_kernel, members, batch, per_gro...  8.88 us
    pallas_call x1, Pallas kernels, convolve(): pl.pallas_call(functools.partial(forward_kernel, members, per_group, widt...  5.65 us
  transfers between devices with their start and end apart: 31, of which 13 were waited for; matrix products, arithmetic and copies ran while one was open for 0% of the time, Pallas kernels for 48%

profile of v15, /device:TPU:0, one launch (start us, length us, event | category | flops | bytes accessed | tf_op | source)
XLA Modules:
  0.0 148.8 jit_solution(6929049904354908923)
XLA Ops:
  1.2 2.7 %collective-permute-start.4 = (bf16[512,1024]{1,0:T(8,128)(2,1)}, bf16[512,1024]{1,0:T(8,128)(2,1)S(1)}, u32[]{:S(2)}, u32[]{:S(2)}) collective-permute-start(bf16[512,1024]{1,0:T(8,128)(2,1)} %refs_0_.1), channel_id=1, source_target_pairs={{0,2},{1,3},{6,4},{7,5},{2,0},{3,1},{4,6},{5,7},{8,10},{9,11},{14,... | collective-permute-start | bytes 3145736 | tf_op jit(solution)/shard_map/ppermute | solution.py:375
  4.6 2.6 %gated_input.1 = (bf16[544,256]{1,0:T(8,128)(2,1)S(1)}, bf16[544,256]{1,0:T(8,128)(2,1)S(1)}, bf16[544,256]{1,0:T(8,128)(2,1)S(1)}, bf16[544,256]{1,0:T(8,128)(2,1)S(1)}) custom-call(s32[2]{0:T(128)S(1)} %pad_add_fusion.who_ref, bf16[512,1024]{1,0:T(8,128)(2,1)} %refs_4_.3, bf16[512,1024]{1,0:T(8,128)(2,1)} %refs_5_.1, f32[64,512]{1,0:T(8,128)} %bitcast.4), custom_call_target="tpu_custom_call" | custom-call | flops 1048576 | bytes 4096 | tf_op jit(solution)/shard_map/gated_input/pallas_call | solution.py:285
  12.0 5.0 %cotangent_blocks.3.refs_4_.refs_3_ = f32[512,1024]{1,0:T(8,128)S(1)} custom-call(s32[10]{0:T(128)S(1)} %plan.1._.plan_ref, bf16[1024,8192]{1,0:T(8,128)(2,1)} %weight_ref.19, bf16[512,1024]{1,0:T(8,128)(2,1)S(1)} %copy-done.3, bf16[512,1024]{1,0:T(8,128)(2,1)} %collective-permute-done.3.refs_1_), custom_call_target="tpu_custom_call" | custom-call | flops 1048576 | bytes 4096 | tf_op jit(solution)/shard_map/cotangent_blocks/pallas_call | solution.py:640
  17.0 6.2 %collective-permute-done.1.refs_2_ = bf16[544,256]{1,0:T(8,128)(2,1)S(1)} collective-permute-done((bf16[544,256]{1,0:T(8,128)(2,1)S(1)}, bf16[544,256]{1,0:T(8,128)(2,1)S(1)}, u32[]{:S(2)}, u32[]{:S(2)}) %collective-permute-start.1) | collective-permute-done | bytes 278560 | tf_op jit(solution)/shard_map/ppermute | solution.py:342
  23.2 5.6 %causal_conv.1 = (bf16[512,256]{1,0:T(8,128)(2,1)S(1)}, bf16[512,256]{1,0:T(8,128)(2,1)S(1)}, bf16[512,256]{1,0:T(8,128)(2,1)S(1)}, bf16[512,256]{1,0:T(8,128)(2...) custom-call(s32[10]{0:T(128)S(1)} %plan.1._.plan_ref, bf16[544,256]{1,0:T(8,128)(2,1)S(1)} %get-tuple-element.46.refs_0_, ...), custom_call_target="tpu_custom_call" | custom-call | flops 1048576 | bytes 4096 | tf_op jit(solution)/shard_map/causal_conv/pallas_call | solution.py:188
  34.5 3.4 %lag_matrices.1.refs_5_.lag_ref = bf16[16,128,2048]{2,1,0:T(8,128)(2,1)S(1)} custom-call(f32[16,2048]{1,0:T(8,128)S(1)} %get-tuple-element.58.taps_ref), custom_call_target="tpu_custom_call" | custom-call | flops 1048576 | bytes 4096 | tf_op jit(solution)/shard_map/lag_matrices/pallas_call | solution.py:207
  37.9 2.3 %collective-permute-done.5.refs_1_ = bf16[512,256]{1,0:T(8,128)(2,1)S(1)} collective-permute-done((bf16[512,256]{1,0:T(8,128)(2,1)S(1)}, bf16[512,256]{1,0:T(8,128)(2,1)S(1)}, u32[]{:S(2)}, u32[]{:S(2)}) %collective-permute-start.5) | collective-permute-done | bytes 262176 | tf_op jit(solution)/shard_map/ppermute | solution.py:342
  40.3 4.9 %collective-permute-done.6.refs_2_ = bf16[512,256]{1,0:T(8,128)(2,1)S(1)} collective-permute-done((bf16[512,256]{1,0:T(8,128)(2,1)S(1)}, bf16[512,256]{1,0:T(8,128)(2,1)S(1)}, u32[]{:S(2)}, u32[]{:S(2)}) %collective-permute-start.6) | collective-permute-done | bytes 262176 | tf_op jit(solution)/shard_map/ppermute | solution.py:342
  46.0 3.4 %projection_blocks.6 = (bf16[512,512]{1,0:T(8,128)(2,1)S(1)}, bf16[512,512]{1,0:T(8,128)(2,1)S(1)}) custom-call(s32[10]{0:T(128)S(1)} %plan.1._.plan_ref, bf16[512,1024]{1,0:T(8,128)(2,1)S(1)} %get-tuple-element.59.data_ref, bf16[1024,8192]{1,0:T(8,128)(2,1)} %weight_ref.19), custom_call_target="tpu_custom_call" | custom-call | flops 1048576 | bytes 4096 | tf_op jit(solution)/shard_map/projection_blocks/pallas_call | solution.py:541
  52.1 3.5 %projection_blocks.7.refs_2_.end_ref.refs_0_ = bf16[512,1024]{1,0:T(8,128)(2,1)S(1)} custom-call(s32[10]{0:T(128)S(1)} %plan.1._.plan_ref, bf16[512,1024]{1,0:T(8,128)(2,1)S(1)} %get-tuple-element.59.data_ref, bf16[1024,8192]{1,0:T(8,128)(2,1)} %weight_ref.19, bf16[512,512]{1,0:T(8,128)(2,1)S(1)} %collective-permute-done.11.refs_0_, ...), custom_call_target="tpu_custom_call" | custom-call | flops 1048576 | bytes 4096 | tf_op jit(solution)/shard_map/projection_blocks/pallas_call | solution.py:541
  57.6 5.5 %collective-permute-start.17 = (bf16[512,1024]{1,0:T(8,128)(2,1)S(1)}, bf16[512,1024]{1,0:T(8,128)(2,1)S(1)}, u32[]{:S(2)}, u32[]{:S(2)}) collective-permute-start(bf16[512,1024]{1,0:T(8,128)(2,1)S(1)} %chosen.2.refs_0_), channel_id=1, source_target_pairs={{2,0},{3,1},{4,6},{5,7},{0,2},{1,3},{6,4},{7,5},{10,8},{11,9},{12,... | collective-permute-start | bytes 3145736 | tf_op jit(solution)/shard_map/ppermute | solution.py:375
  63.5 3.4 %projection_blocks.8 = (bf16[512,512]{1,0:T(8,128)(2,1)S(1)}, bf16[512,512]{1,0:T(8,128)(2,1)S(1)}) custom-call(s32[10]{0:T(128)S(1)} %plan.1._.plan_ref, bf16[512,1024]{1,0:T(8,128)(2,1)S(1)} %get-tuple-element.59.data_ref, bf16[1024,8192]{1,0:T(8,128)(2,1)} %weight_ref.19, bf16[512,1024]{1,0:T(8,128)(2,1)S(1)} %chosen.2.refs_0_), custom_call_target="tpu_custom_call" | custom-call | flops 1048576 | bytes 4096 | tf_op jit(solution)/shard_map/projection_blocks/pallas_call | solution.py:541
  69.7 3.5 %projection_blocks.9.refs_0_.refs_4_ = bf16[512,1024]{1,0:T(8,128)(2,1)S(1)} custom-call(s32[10]{0:T(128)S(1)} %plan.1._.plan_ref, bf16[512,1024]{1,0:T(8,128)(2,1)S(1)} %get-tuple-element.59.data_ref, bf16[1024,8192]{1,0:T(8,128)(2,1)} %weight_ref.19, bf16[512,512]{1,0:T(8,128)(2,1)S(1)} %collective-permute-done.13.refs_0_, ...), custom_call_target="tpu_custom_call" | custom-call | flops 1048576 | bytes 4096 | tf_op jit(solution)/shard_map/projection_blocks/pallas_call | solution.py:541
  73.2 4.9 %projection_blocks.10 = (bf16[512,1024]{1,0:T(8,128)(2,1)S(1)}, bf16[512,1024]{1,0:T(8,128)(2,1)S(1)}) custom-call(s32[10]{0:T(128)S(1)} %plan.1._.plan_ref, bf16[512,1024]{1,0:T(8,128)(2,1)S(1)} %get-tuple-element.59.data_ref, bf16[1024,8192]{1,0:T(8,128)(2,1)} %weight_ref.19, bf16[512,1024]{1,0:T(8,128)(2,1)S(1)} %projection_blocks.9.refs_0_.refs_4_), custom_call_target="tpu_custom_call" | custom-call | flops 1048576 | bytes 4096 | tf_op jit(solution)/shard_map/projection_blocks/pallas_call | solution.py:541
  78.1 6.4 %cotangent_blocks.4.refs_1_.refs_2_ = f32[512,1024]{1,0:T(8,128)S(1)} custom-call(s32[10]{0:T(128)S(1)} %plan.1._.plan_ref, bf16[1024,8192]{1,0:T(8,128)(2,1)} %weight_ref.19, bf16[512,1024]{1,0:T(8,128)(2,1)S(1)} %get-tuple-element.60.refs_1_.refs_0_, bf16[512,1024]{1,0:T(8,128)(2,1)S(1)} %collective-permute-done.18.refs_1_, ...), custom_call_target="tpu_custom_call" | custom-call | flops 1048576 | bytes 4096 | tf_op jit(solution)/shard_map/cotangent_blocks/pallas_call | solution.py:640
  88.1 3.7 %collective-permute-start.22 = (bf16[512,1024]{1,0:T(8,128)(2,1)S(1)}, bf16[512,1024]{1,0:T(8,128)(2,1)S(1)}, u32[]{:S(2)}, u32[]{:S(2)}) collective-permute-start(bf16[512,1024]{1,0:T(8,128)(2,1)S(1)} %held.10.refs_0_), channel_id=1, source_target_pairs={{0,2},{1,3},{6,4},{7,5},{8,10},{9,11},{14,12},{15,13},{16,18},{17,... | collective-permute-start | bytes 3145736 | tf_op jit(solution)/shard_map/ppermute | solution.py:375
  92.6 4.8 %cotangent_blocks.5.start_ref = f32[512,1024]{1,0:T(8,128)S(1)} custom-call(s32[10]{0:T(128)S(1)} %plan.1._.plan_ref, bf16[1024,8192]{1,0:T(8,128)(2,1)} %weight_ref.19, bf16[512,1024]{1,0:T(8,128)(2,1)S(1)} %collective-permute-done.20.refs_0_, bf16[512,1024]{1,0:T(8,128)(2,1)S(1)} %chosen.3.refs_1_, f32[512,1024]{1,0:T(8,128)S(1)} %cotangent_blocks.4.refs_1_.refs_2_, ...), custom_call_target="tpu_custom_call" | custom-call | flops 1048576 | bytes 4096 | tf_op jit(solution)/shard_map/cotangent_blocks/pallas_call | solution.py:640
  97.4 4.5 %cotangent_last.1 = (bf16[512,1024]{1,0:T(8,128)(2,1)}, bf16[512,256]{1,0:T(8,128)(2,1)S(1)}, bf16[512,256]{1,0:T(8,128)(2,1)S(1)}, bf16[512,256]{1,0:T(8,128)(2,1)S(1)}, bf16[512,256]{1,0:T(8,128)(2,1)S(1)}) custom-call(s32[10]{0:T(128)S(1)} %plan.1._.plan_ref, bf16[1024,8192]{1,0:T(8,128)(2,1)} %weight_ref.19, ...), custom_call_target="tpu_custom_call" | custom-call | flops 1048576 | bytes 4096 | tf_op jit(solution)/shard_map/cotangent_last/pallas_call | solution.py:606
  105.4 5.1 %projection_blocks.11 = (bf16[512,1024]{1,0:T(8,128)(2,1)S(1)}, bf16[512,1024]{1,0:T(8,128)(2,1)S(1)}) custom-call(s32[10]{0:T(128)S(1)} %plan.1._.plan_ref, bf16[512,1024]{1,0:T(8,128)(2,1)S(1)} %get-tuple-element.59.data_ref, bf16[1024,8192]{1,0:T(8,128)(2,1)} %weight_ref.19, bf16[512,1024]{1,0:T(8,128)(2,1)S(1)} %collective-permute-done.15.refs_0_, ...), custom_call_target="tpu_custom_call" | custom-call | flops 1048576 | bytes 4096 | tf_op jit(solution)/shard_map/projection_blocks/pallas_call | solution.py:541
  110.5 4.2 %collective-permute-done.22.refs_1_ = bf16[512,1024]{1,0:T(8,128)(2,1)S(1)} collective-permute-done((bf16[512,1024]{1,0:T(8,128)(2,1)S(1)}, bf16[512,1024]{1,0:T(8,128)(2,1)S(1)}, u32[]{:S(2)}, u32[]{:S(2)}) %collective-permute-start.22) | collective-permute-done | bytes 1048608 | tf_op jit(solution)/shard_map/ppermute | solution.py:375
  118.4 3.8 %collective-permute-start.26 = (bf16[512,1024]{1,0:T(8,128)(2,1)S(1)}, bf16[512,1024]{1,0:T(8,128)(2,1)S(1)}, u32[]{:S(2)}, u32[]{:S(2)}) collective-permute-start(bf16[512,1024]{1,0:T(8,128)(2,1)S(1)} %added.7.refs_4_), channel_id=1, source_target_pairs={{2,0},{3,1},{4,6},{5,7},{0,2},{1,3},{6,4},{7,5},{10,8},{11,9},{12,... | collective-permute-start | bytes 3145736 | tf_op jit(solution)/shard_map/ppermute | solution.py:375
  122.2 8.9 %causal_conv_grads.1 = (bf16[544,256]{1,0:T(8,128)(2,1)S(1)}, bf16[544,256]{1,0:T(8,128)(2,1)S(1)}, bf16[544,256]{1,0:T(8,128)(2,1)S(1)}, bf16[544,256]{1,0:T(8,128)(2,1)S(1)}) custom-call(s32[10]{0:T(128)S(1)} %plan.1._.plan_ref, bf16[4,256,512]{2,1,0:T(8,128)(2,1)S(1)} %get-tuple-element.79.in_scr, bf16[16,128,2048]{2,1,0:T(8,128)(2,1)S(1)} %lag_matrices.1.refs_5_.lag_ref, ...), custom_call_target="tpu_custom_call" | custom-call | flops 1048576 | bytes 4096 | tf_op jit(solution)/shard_map/causal_conv_grads/pallas_call | solution.py:226
  134.6 10.1 %collective-permute-done.26.refs_1_ = bf16[512,1024]{1,0:T(8,128)(2,1)S(1)} collective-permute-done((bf16[512,1024]{1,0:T(8,128)(2,1)S(1)}, bf16[512,1024]{1,0:T(8,128)(2,1)S(1)}, u32[]{:S(2)}, u32[]{:S(2)}) %collective-permute-start.26) | collective-permute-done | bytes 1048608 | tf_op jit(solution)/shard_map/ppermute | solution.py:375
  146.5 2.3 %input_gradients.1 = (bf16[512,1024]{1,0:T(8,128)(2,1)}, bf16[512,1024]{1,0:T(8,128)(2,1)}, f32[64,512]{1,0:T(8,128)}) custom-call(s32[10]{0:T(128)S(1)} %plan.1._.plan_ref, bf16[544,256]{1,0:T(8,128)(2,1)S(1)} %get-tuple-element.80.refs_0_, bf16[544,256]{1,0:T(8,128)(2,1)S(1)} %collective-permute-done.28.refs_1_, ...), custom_call_target="tpu_custom_call" | custom-call | flops 1048576 | bytes 4096 | tf_op jit(solution)/shard_map/input_gradients/pallas_call | solution.py:328
  (77 shorter events, 37.1 us)
Async XLA Ops:
  1.2 27.7 %collective-permute-start.4 = (bf16[512,1024]{1,0:T(8,128)(2,1)}, bf16[512,1024]{1,0:T(8,128)(2,1)S(1)}, u32[]{:S(2)}, u32[]{:S(2)}) collective-permute-start(bf16[512,1024]{1,0:T(8,128)(2,1)} %refs_0_.1), channel_id=1, source_target_pairs={{0,2},{1,3},{6,4},{7,5},{2,0},{3,1},{4,6},{5,7},{8,10},{9,11},{14,... | collective-permute-start | bytes 3145736 | tf_op jit(solution)/shard_map/ppermute | solution.py:375
  3.8 25.1 %collective-permute-start.9 = (bf16[512,1024]{1,0:T(8,128)(2,1)}, bf16[512,1024]{1,0:T(8,128)(2,1)S(1)}, u32[]{:S(2)}, u32[]{:S(2)}) collective-permute-start(bf16[512,1024]{1,0:T(8,128)(2,1)} %refs_0_.1), channel_id=1, source_target_pairs={{2,4},{3,5},{4,2},{5,3},{10,12},{11,13},{12,10},{13,11},{18,20},{1... | collective-permute-start | bytes 3145736 | tf_op jit(solution)/shard_map/ppermute | solution.py:375
  8.8 14.4 %collective-permute-start.1 = (bf16[544,256]{1,0:T(8,128)(2,1)S(1)}, bf16[544,256]{1,0:T(8,128)(2,1)S(1)}, u32[]{:S(2)}, u32[]{:S(2)}) collective-permute-start(bf16[544,256]{1,0:T(8,128)(2,1)S(1)} %get-tuple-element.48), channel_id=1, source_target_pairs={{0,16},{8,24},{16,0},{24,8},{1,17},{9,25},{17,1},{25,9},{2,18},{10... | collective-permute-start | bytes 835592 | tf_op jit(solution)/shard_map/ppermute | solution.py:342
  10.3 12.9 %collective-permute-start.2 = (bf16[544,256]{1,0:T(8,128)(2,1)S(1)}, bf16[544,256]{1,0:T(8,128)(2,1)S(1)}, u32[]{:S(2)}, u32[]{:S(2)}) collective-permute-start(bf16[544,256]{1,0:T(8,128)(2,1)S(1)} %get-tuple-element.49), channel_id=1, source_target_pairs={{0,24},{8,16},{16,8},{24,0},{1,25},{9,17},{17,9},{25,1},{2,26},{10... | collective-permute-start | bytes 835592 | tf_op jit(solution)/shard_map/ppermute | solution.py:342
  28.9 27.9 %collective-permute-start.10 = (bf16[512,1024]{1,0:T(8,128)(2,1)S(1)}, bf16[512,1024]{1,0:T(8,128)(2,1)S(1)}, u32[]{:S(2)}, u32[]{:S(2)}) collective-permute-start(bf16[512,1024]{1,0:T(8,128)(2,1)S(1)} %held.7.refs_0_), channel_id=1, source_target_pairs={{2,0},{3,1},{4,6},{5,7},{10,8},{11,9},{12,14},{13,15},{18,16},{19,... | collective-permute-start | bytes 3145736 | tf_op jit(solution)/shard_map/ppermute | solution.py:375
  30.2 26.6 %collective-permute-start.8 = (bf16[512,1024]{1,0:T(8,128)(2,1)S(1)}, bf16[512,1024]{1,0:T(8,128)(2,1)S(1)}, u32[]{:S(2)}, u32[]{:S(2)}) collective-permute-start(bf16[512,1024]{1,0:T(8,128)(2,1)S(1)} %get-tuple-element.60.refs_1_.refs_0_), channel_id=1, source_target_pairs={{2,4},{3,5},{4,2},{5,3},{10,12},{11,13},{12,10},{13,11},{18,20},{1... | collective-permute-start | bytes 3145736 | tf_op jit(solution)/shard_map/ppermute | solution.py:375
  32.3 12.9 %collective-permute-start.6 = (bf16[512,256]{1,0:T(8,128)(2,1)S(1)}, bf16[512,256]{1,0:T(8,128)(2,1)S(1)}, u32[]{:S(2)}, u32[]{:S(2)}) collective-permute-start(bf16[512,256]{1,0:T(8,128)(2,1)S(1)} %get-tuple-element.56), channel_id=1, source_target_pairs={{0,16},{8,24},{16,0},{24,8},{1,17},{9,25},{17,1},{25,9},{2,18},{10... | collective-permute-start | bytes 786440 | tf_op jit(solution)/shard_map/ppermute | solution.py:342
  33.1 12.1 %collective-permute-start.7 = (bf16[512,256]{1,0:T(8,128)(2,1)S(1)}, bf16[512,256]{1,0:T(8,128)(2,1)S(1)}, u32[]{:S(2)}, u32[]{:S(2)}) collective-permute-start(bf16[512,256]{1,0:T(8,128)(2,1)S(1)} %get-tuple-element.57), channel_id=1, source_target_pairs={{0,24},{8,16},{16,8},{24,0},{1,25},{9,17},{17,9},{25,1},{2,26},{10... | collective-permute-start | bytes 786440 | tf_op jit(solution)/shard_map/ppermute | solution.py:342
  50.0 28.1 %collective-permute-start.18 = (bf16[512,1024]{1,0:T(8,128)(2,1)S(1)}, bf16[512,1024]{1,0:T(8,128)(2,1)S(1)}, u32[]{:S(2)}, u32[]{:S(2)}) collective-permute-start(bf16[512,1024]{1,0:T(8,128)(2,1)S(1)} %get-tuple-element.60.refs_1_.refs_0_), channel_id=1, source_target_pairs={{0,1},{1,0},{2,3},{3,2},{4,5},{5,4},{6,7},{7,6},{8,9},{9,8},{10,11... | collective-permute-start | bytes 3145736 | tf_op jit(solution)/shard_map/ppermute | solution.py:342
  57.6 28.9 %collective-permute-start.17 = (bf16[512,1024]{1,0:T(8,128)(2,1)S(1)}, bf16[512,1024]{1,0:T(8,128)(2,1)S(1)}, u32[]{:S(2)}, u32[]{:S(2)}) collective-permute-start(bf16[512,1024]{1,0:T(8,128)(2,1)S(1)} %chosen.2.refs_0_), channel_id=1, source_target_pairs={{2,0},{3,1},{4,6},{5,7},{0,2},{1,3},{6,4},{7,5},{10,8},{11,9},{12,... | collective-permute-start | bytes 3145736 | tf_op jit(solution)/shard_map/ppermute | solution.py:375
  63.4 28.4 %collective-permute-start.20 = (bf16[512,1024]{1,0:T(8,128)(2,1)S(1)}, bf16[512,1024]{1,0:T(8,128)(2,1)S(1)}, u32[]{:S(2)}, u32[]{:S(2)}) collective-permute-start(bf16[512,1024]{1,0:T(8,128)(2,1)S(1)} %added.5.refs_2_), channel_id=1, source_target_pairs={{0,1},{1,0},{2,3},{3,2},{4,5},{5,4},{6,7},{7,6},{8,9},{9,8},{10,11... | collective-permute-start | bytes 3145736 | tf_op jit(solution)/shard_map/ppermute | solution.py:342
  87.5 9.9 %collective-permute-start.19 = (bf16[512,1024]{1,0:T(8,128)(2,1)S(1)}, bf16[512,1024]{1,0:T(8,128)(2,1)S(1)}, u32[]{:S(2)}, u32[]{:S(2)}) collective-permute-start(bf16[512,1024]{1,0:T(8,128)(2,1)S(1)} %chosen.3.refs_1_), channel_id=1, source_target_pairs={{0,1},{1,0},{2,3},{3,2},{4,5},{5,4},{6,7},{7,6},{8,9},{9,8},{10,11... | collective-permute-start | bytes 3145736 | tf_op jit(solution)/shard_map/ppermute | solution.py:342
  87.5 15.6 %collective-permute-start.16 = (bf16[512,1024]{1,0:T(8,128)(2,1)S(1)}, bf16[512,1024]{1,0:T(8,128)(2,1)S(1)}, u32[]{:S(2)}, u32[]{:S(2)}) collective-permute-start(bf16[512,1024]{1,0:T(8,128)(2,1)S(1)} %get-tuple-element.67), channel_id=1, source_target_pairs={{0,1},{1,0},{2,3},{3,2},{4,5},{5,4},{6,7},{7,6},{8,9},{9,8},{10,11... | collective-permute-start | bytes 3145736 | tf_op jit(solution)/shard_map/ppermute | solution.py:342
  88.0 15.9 %collective-permute-start.15 = (bf16[512,1024]{1,0:T(8,128)(2,1)S(1)}, bf16[512,1024]{1,0:T(8,128)(2,1)S(1)}, u32[]{:S(2)}, u32[]{:S(2)}) collective-permute-start(bf16[512,1024]{1,0:T(8,128)(2,1)S(1)} %get-tuple-element.66.refs_2_), channel_id=1, source_target_pairs={{0,1},{1,0},{2,3},{3,2},{4,5},{5,4},{6,7},{7,6},{8,9},{9,8},{10,11... | collective-permute-start | bytes 3145736 | tf_op jit(solution)/shard_map/ppermute | solution.py:342
  88.1 26.7 %collective-permute-start.22 = (bf16[512,1024]{1,0:T(8,128)(2,1)S(1)}, bf16[512,1024]{1,0:T(8,128)(2,1)S(1)}, u32[]{:S(2)}, u32[]{:S(2)}) collective-permute-start(bf16[512,1024]{1,0:T(8,128)(2,1)S(1)} %held.10.refs_0_), channel_id=1, source_target_pairs={{0,2},{1,3},{6,4},{7,5},{8,10},{9,11},{14,12},{15,13},{16,18},{17,... | collective-permute-start | bytes 3145736 | tf_op jit(solution)/shard_map/ppermute | solution.py:375
  91.8 22.9 %collective-permute-start.21 = (bf16[512,1024]{1,0:T(8,128)(2,1)S(1)}, bf16[512,1024]{1,0:T(8,128)(2,1)S(1)}, u32[]{:S(2)}, u32[]{:S(2)}) collective-permute-start(bf16[512,1024]{1,0:T(8,128)(2,1)S(1)} %added.6.refs_0_.refs_3_), channel_id=1, source_target_pairs={{2,4},{3,5},{4,2},{5,3},{10,12},{11,13},{12,10},{13,11},{18,20},{1... | collective-permute-start | bytes 3145736 | tf_op jit(solution)/shard_map/ppermute | solution.py:375
  101.9 12.9 %collective-permute-start.23 = (bf16[512,256]{1,0:T(8,128)(2,1)S(1)}, bf16[512,256]{1,0:T(8,128)(2,1)S(1)}, u32[]{:S(2)}, u32[]{:S(2)}) collective-permute-start(bf16[512,256]{1,0:T(8,128)(2,1)S(1)} %get-tuple-element.73), channel_id=1, source_target_pairs={{0,8},{8,0},{16,24},{24,16},{1,9},{9,1},{17,25},{25,17},{2,10},{10... | collective-permute-start | bytes 786440 | tf_op jit(solution)/shard_map/ppermute | solution.py:342
  103.1 12.1 %collective-permute-start.24 = (bf16[512,256]{1,0:T(8,128)(2,1)S(1)}, bf16[512,256]{1,0:T(8,128)(2,1)S(1)}, u32[]{:S(2)}, u32[]{:S(2)}) collective-permute-start(bf16[512,256]{1,0:T(8,128)(2,1)S(1)} %get-tuple-element.74), channel_id=1, source_target_pairs={{0,16},{8,24},{16,0},{24,8},{1,17},{9,25},{17,1},{25,9},{2,18},{10... | collective-permute-start | bytes 786440 | tf_op jit(solution)/shard_map/ppermute | solution.py:342
  103.9 12.9 %collective-permute-start.25 = (bf16[512,256]{1,0:T(8,128)(2,1)S(1)}, bf16[512,256]{1,0:T(8,128)(2,1)S(1)}, u32[]{:S(2)}, u32[]{:S(2)}) collective-permute-start(bf16[512,256]{1,0:T(8,128)(2,1)S(1)} %get-tuple-element.75), channel_id=1, source_target_pairs={{0,24},{8,16},{16,8},{24,0},{1,25},{9,17},{17,9},{25,1},{2,26},{10... | collective-permute-start | bytes 786440 | tf_op jit(solution)/shard_map/ppermute | solution.py:342
  117.1 17.5 %collective-permute-start.27 = (bf16[512,1024]{1,0:T(8,128)(2,1)S(1)}, bf16[512,1024]{1,0:T(8,128)(2,1)S(1)}, u32[]{:S(2)}, u32[]{:S(2)}) collective-permute-start(bf16[512,1024]{1,0:T(8,128)(2,1)S(1)} %added.8.refs_5_), channel_id=1, source_target_pairs={{2,4},{3,5},{4,2},{5,3},{10,12},{11,13},{12,10},{13,11},{18,20},{1... | collective-permute-start | bytes 3145736 | tf_op jit(solution)/shard_map/ppermute | solution.py:375
  118.4 26.4 %collective-permute-start.26 = (bf16[512,1024]{1,0:T(8,128)(2,1)S(1)}, bf16[512,1024]{1,0:T(8,128)(2,1)S(1)}, u32[]{:S(2)}, u32[]{:S(2)}) collective-permute-start(bf16[512,1024]{1,0:T(8,128)(2,1)S(1)} %added.7.refs_4_), channel_id=1, source_target_pairs={{2,0},{3,1},{4,6},{5,7},{0,2},{1,3},{6,4},{7,5},{10,8},{11,9},{12,... | collective-permute-start | bytes 3145736 | tf_op jit(solution)/shard_map/ppermute | solution.py:375
  131.1 15.4 %collective-permute-start.28 = (bf16[544,256]{1,0:T(8,128)(2,1)S(1)}, bf16[544,256]{1,0:T(8,128)(2,1)S(1)}, u32[]{:S(2)}, u32[]{:S(2)}) collective-permute-start(bf16[544,256]{1,0:T(8,128)(2,1)S(1)} %get-tuple-element.81), channel_id=1, source_target_pairs={{0,8},{8,0},{16,24},{24,16},{1,9},{9,1},{17,25},{25,17},{2,10},{10... | collective-permute-start | bytes 835592 | tf_op jit(solution)/shard_map/ppermute | solution.py:342
  132.2 14.2 %collective-permute-start.29 = (bf16[544,256]{1,0:T(8,128)(2,1)S(1)}, bf16[544,256]{1,0:T(8,128)(2,1)S(1)}, u32[]{:S(2)}, u32[]{:S(2)}) collective-permute-start(bf16[544,256]{1,0:T(8,128)(2,1)S(1)} %get-tuple-element.82), channel_id=1, source_target_pairs={{0,16},{8,24},{16,0},{24,8},{1,17},{9,25},{17,1},{25,9},{2,18},{10... | collective-permute-start | bytes 835592 | tf_op jit(solution)/shard_map/ppermute | solution.py:342
  133.4 13.0 %collective-permute-start.30 = (bf16[544,256]{1,0:T(8,128)(2,1)S(1)}, bf16[544,256]{1,0:T(8,128)(2,1)S(1)}, u32[]{:S(2)}, u32[]{:S(2)}) collective-permute-start(bf16[544,256]{1,0:T(8,128)(2,1)S(1)} %get-tuple-element.83), channel_id=1, source_target_pairs={{0,24},{8,16},{16,8},{24,0},{1,25},{9,17},{17,9},{25,1},{2,26},{10... | collective-permute-start | bytes 835592 | tf_op jit(solution)/shard_map/ppermute | solution.py:342
  (11 other events, 63.2 us)

commit v16 on v13

--- a/solution.py
+++ b/solution.py
@@ -92,7 +92,7 @@
         spread_out(out_scr, start, per_group, value, members, width)
         return carry
 
-    lax.fori_loop(0, groups, one_group, 0, unroll=4)
+    lax.fori_loop(0, groups, one_group, 0, unroll=8)
     for step in range(members):
         outputs[step][...] = out_scr[position ^ step].T
 
@@ -297,44 +297,54 @@
 def finish_kernel(members, plan_ref, *refs):
     parts = refs[:members]
     key_ref, value_ref = refs[members : members + 2]
-    key_out, value_out, taps_out = refs[-3:]
+    summands = refs[members + 2 : -4]
+    key_out, value_out, projected_out, taps_out = refs[-4:]
     position = plan_ref[POSITION]
-    width, channels = key_ref.shape
-    share = channels // members
+    width = key_ref.shape[0]
+    share = key_out.shape[1]
     groups = taps_out.shape[0] // members
+    here = pl.ds(pl.multiple_of(pl.program_id(0) * share, share), share)
+    projected = sum(ref[:, here].astype(jnp.float32) for ref in summands)
+    projected_out[...] = projected.astype(jnp.bfloat16)
     for step in range(members):
-        at = position ^ step
-        columns = pl.ds(pl.multiple_of(at * share, share), share)
-        grad = parts[step][:width].astype(jnp.float32)
-        key_out[:, columns] = (grad * value_ref[:, columns].astype(jnp.float32)).astype(
-            jnp.bfloat16
-        )
-        value_out[:, columns] = (grad * key_ref[:, columns].astype(jnp.float32)).astype(
-            jnp.bfloat16
-        )
-        taps = [
-            parts[step][width + chunk * groups : width + (chunk + 1) * groups, :]
-            for chunk in range(width // share)
-        ]
-        taps_out[pl.ds(pl.multiple_of(at * groups, groups), groups), :] = jnp.concatenate(
-            taps, axis=1
-        ).astype(jnp.float32)
-
-
-def finished(plan, parts, key_gate, value_input, groups, after=()):
+
+        @pl.when(pl.program_id(0) == step)
+        def _(step=step):
+            at = position ^ step
+            columns = pl.ds(pl.multiple_of(at * share, share), share)
+            grad = parts[step][:width].astype(jnp.float32)
+            key_out[...] = (grad * value_ref[:, columns].astype(jnp.float32)).astype(jnp.bfloat16)
+            value_out[...] = (grad * key_ref[:, columns].astype(jnp.float32)).astype(jnp.bfloat16)
+            taps = [
+                parts[step][width + chunk * groups : width + (chunk + 1) * groups, :]
+                for chunk in range(width // share)
+            ]
+            taps_out[pl.ds(pl.multiple_of(at * groups, groups), groups), :] = jnp.concatenate(
+                taps, axis=1
+            ).astype(jnp.float32)
+
+
+def finished(plan, parts, key_gate, value_input, summands, groups):
     members = len(parts)
     width, channels = key_gate.shape
+    share = channels // members
     array = jax.ShapeDtypeStruct((width, channels), jnp.bfloat16)
-    grad_key, grad_value, taps = pl.pallas_call(
+    swapped_piece = pl.BlockSpec((width, share), lambda i, at: (0, at[POSITION] ^ i))
+    piece = pl.BlockSpec((width, share), lambda i, at: (0, i))
+    grad_key, grad_value, projected, taps = pl.pallas_call(
         functools.partial(finish_kernel, members),
-        out_shape=[array, array, jax.ShapeDtypeStruct((groups, width), jnp.float32)],
-        in_specs=[SMEM] + [VMEM] * (members + 2) + [ANYWHERE] * len(after),
-        out_specs=[VMEM] * 3,
+        out_shape=[array] * 3 + [jax.ShapeDtypeStruct((groups, width), jnp.float32)],
+        grid_spec=pltpu.PrefetchScalarGridSpec(
+            num_scalar_prefetch=1,
+            grid=(members,),
+            in_specs=[VMEM] * (members + 2 + len(summands)),
+            out_specs=[swapped_piece, swapped_piece, piece, VMEM],
+        ),
         compiler_params=pltpu.CompilerParams(vmem_limit_bytes=24 * 2**20),
         cost_estimate=COST,
         name="input_gradients",
-    )(plan, *parts, key_gate, value_input, *after)
-    return grad_key, grad_value, taps.T
+    )(plan, *parts, key_gate, value_input, *summands)
+    return projected, grad_key, grad_value, taps.T
 
 
 def swapped(array, axis, step):
@@ -749,9 +759,12 @@
     two_a, two_b = held_until([two_a, two_b], tuple(grad_parts[1:]))
     third, second = added(third, two_a), added(second, two_b)
     back_parts = correlate(plan, turned, lags, grad_parts, per_group, scale, (third, second))
-    projected = added(own, hop(third, OUTWARD + INWARD), hop(second, ACROSS))
+    summands = (own, hop(third, OUTWARD + INWARD), hop(second, ACROSS))
     back_parts = traded(back_parts, "ctx")
-    return projected, grad_query, *finished(plan, back_parts, key_gate, value_input, groups, (in_hbm(projected),))
+    projected, *gradients = finished(
+        plan, back_parts, key_gate, value_input, summands, groups
+    )
+    return projected, grad_query, *gradients
 
 
 def anywhere(

time: 148 us -> 149 us (level)
  Pallas kernels: 73.7 us -> 72.2 us
    ppermute x22, waiting for transfers between devices: 17.9 us -> 28.8 us  [swapped(): return lax.ppermute(array, axis, [(i, i ^ step) for i in range(size)])]
    ppermute x9, waiting for transfers between devices: 18.2 us -> 8.6 us  [hop(): lax.ppermute(array, 'tp', [(2 * i + core, 2 * j + core) for i, j in pairs...]
    pallas_call x5 -> x4, Pallas kernels: 2.92 us -> 1.22 us  [added(): pl.pallas_call(add_kernel, out_shape=jax.ShapeDtypeStruct((rows, width),...]
  transfers between devices with their start and end apart: 31 -> 31, of which waited for: 10 -> 12; matrix products, arithmetic and copies ran while one was open for 0% -> 0% of each run, Pallas kernels for 48% -> 46%
where the time goes in v16:
time: 149 us; the launch traced here: 148 us
  Pallas kernels  72.2 us (48%)
  waiting for transfers between devices  37.4 us (25%)
  starting transfers between devices  37.2 us (25%)
    ppermute x22, waiting for transfers between devices, swapped(): return lax.ppermute(array, axis, [(i, i ^ step) for i in range(size)])  28.8 us
    pallas_call x6, Pallas kernels, column_products(): pl.pallas_call(functools.partial(product_kernel, steps, [part.shape[1] fo...  23.8 us
    ppermute x9, starting transfers between devices, hop(): lax.ppermute(array, 'tp', [(2 * i + core, 2 * j + core) for i, j in pairs...  20.3 us
    ppermute x22, starting transfers between devices, swapped(): return lax.ppermute(array, axis, [(i, i ^ step) for i in range(size)])  16.9 us
    pallas_call x3, Pallas kernels, cotangent_products(): pl.pallas_call(functools.partial(cotangent_kernel, count, begin), out_sha...  16.2 us
    pallas_call x1, Pallas kernels, correlate(): pl.pallas_call(functools.partial(backward_kernel, members, batch, per_gro...  8.88 us
    ppermute x9, waiting for transfers between devices, hop(): lax.ppermute(array, 'tp', [(2 * i + core, 2 * j + core) for i, j in pairs...  8.6 us
    pallas_call x1, Pallas kernels, convolve(): pl.pallas_call(functools.partial(forward_kernel, members, per_group, widt...  5.02 us
  transfers between devices with their start and end apart: 31, of which 12 were waited for; matrix products, arithmetic and copies ran while one was open for 0% of the time, Pallas kernels for 46%

profile of v16, /device:TPU:0, one launch (start us, length us, event | category | flops | bytes accessed | tf_op | source)
XLA Modules:
  0.0 148.1 jit_solution(4447897224515780772)
XLA Ops:
  1.9 5.6 %collective-permute-start.4 = (bf16[512,1024]{1,0:T(8,128)(2,1)}, bf16[512,1024]{1,0:T(8,128)(2,1)S(1)}, u32[]{:S(2)}, u32[]{:S(2)}) collective-permute-start(bf16[512,1024]{1,0:T(8,128)(2,1)} %refs_0_.1), channel_id=1, source_target_pairs={{0,2},{1,3},{6,4},{7,5},{2,0},{3,1},{4,6},{5,7},{8,10},{9,11},{14,... | collective-permute-start | bytes 3145736 | tf_op jit(solution)/shard_map/ppermute | solution.py:385
  14.9 5.0 %cotangent_blocks.3.refs_4_.refs_3_ = f32[512,1024]{1,0:T(8,128)S(1)} custom-call(s32[10]{0:T(128)S(1)} %plan.1._.plan_ref, bf16[1024,8192]{1,0:T(8,128)(2,1)} %weight_ref.19, bf16[512,1024]{1,0:T(8,128)(2,1)S(1)} %copy-done.3, bf16[512,1024]{1,0:T(8,128)(2,1)} %collective-permute-done.3.refs_1_), custom_call_target="tpu_custom_call" | custom-call | flops 1048576 | bytes 4096 | tf_op jit(solution)/shard_map/cotangent_blocks/pallas_call | solution.py:650
  19.9 5.8 %collective-permute-done.1.refs_2_ = bf16[544,256]{1,0:T(8,128)(2,1)S(1)} collective-permute-done((bf16[544,256]{1,0:T(8,128)(2,1)S(1)}, bf16[544,256]{1,0:T(8,128)(2,1)S(1)}, u32[]{:S(2)}, u32[]{:S(2)}) %collective-permute-start.1) | collective-permute-done | bytes 278560 | tf_op jit(solution)/shard_map/ppermute | solution.py:352
  25.7 5.0 %causal_conv.1 = (bf16[512,256]{1,0:T(8,128)(2,1)S(1)}, bf16[512,256]{1,0:T(8,128)(2,1)S(1)}, bf16[512,256]{1,0:T(8,128)(2,1)S(1)}, bf16[512,256]{1,0:T(8,128)(2...) custom-call(s32[10]{0:T(128)S(1)} %plan.1._.plan_ref, bf16[544,256]{1,0:T(8,128)(2,1)S(1)} %get-tuple-element.48.refs_0_, ...), custom_call_target="tpu_custom_call" | custom-call | flops 1048576 | bytes 4096 | tf_op jit(solution)/shard_map/causal_conv/pallas_call | solution.py:188
  36.6 3.4 %lag_matrices.1.refs_5_.lag_ref = bf16[16,128,2048]{2,1,0:T(8,128)(2,1)S(1)} custom-call(f32[16,2048]{1,0:T(8,128)S(1)} %get-tuple-element.53.taps_ref), custom_call_target="tpu_custom_call" | custom-call | flops 1048576 | bytes 4096 | tf_op jit(solution)/shard_map/lag_matrices/pallas_call | solution.py:207
  40.3 5.4 %collective-permute-done.9.refs_2_ = bf16[512,256]{1,0:T(8,128)(2,1)S(1)} collective-permute-done((bf16[512,256]{1,0:T(8,128)(2,1)S(1)}, bf16[512,256]{1,0:T(8,128)(2,1)S(1)}, u32[]{:S(2)}, u32[]{:S(2)}) %collective-permute-start.9) | collective-permute-done | bytes 262176 | tf_op jit(solution)/shard_map/ppermute | solution.py:352
  46.5 3.4 %projection_blocks.6 = (bf16[512,768]{1,0:T(8,128)(2,1)S(1)}, bf16[512,256]{1,0:T(8,128)(2,1)S(1)}) custom-call(s32[10]{0:T(128)S(1)} %plan.1._.plan_ref, bf16[512,1024]{1,0:T(8,128)(2,1)S(1)} %get-tuple-element.64.data_ref, bf16[1024,8192]{1,0:T(8,128)(2,1)} %weight_ref.19), custom_call_target="tpu_custom_call" | custom-call | flops 1048576 | bytes 4096 | tf_op jit(solution)/shard_map/projection_blocks/pallas_call | solution.py:551
  52.6 3.5 %projection_blocks.7.refs_2_.end_ref.refs_0_ = bf16[512,1024]{1,0:T(8,128)(2,1)S(1)} custom-call(s32[10]{0:T(128)S(1)} %plan.1._.plan_ref, bf16[512,1024]{1,0:T(8,128)(2,1)S(1)} %get-tuple-element.64.data_ref, bf16[1024,8192]{1,0:T(8,128)(2,1)} %weight_ref.19, bf16[512,768]{1,0:T(8,128)(2,1)S(1)} %collective-permute-done.11.refs_0_, ...), custom_call_target="tpu_custom_call" | custom-call | flops 1048576 | bytes 4096 | tf_op jit(solution)/shard_map/projection_blocks/pallas_call | solution.py:551
  56.1 4.1 %collective-permute-done.7.refs_1_ = bf16[512,1024]{1,0:T(8,128)(2,1)S(1)} collective-permute-done((bf16[512,1024]{1,0:T(8,128)(2,1)S(1)}, bf16[512,1024]{1,0:T(8,128)(2,1)S(1)}, u32[]{:S(2)}, u32[]{:S(2)}) %collective-permute-start.7) | collective-permute-done | bytes 1048608 | tf_op jit(solution)/shard_map/ppermute | solution.py:385
  61.0 3.8 %collective-permute-start.13 = (bf16[512,1024]{1,0:T(8,128)(2,1)S(1)}, bf16[512,1024]{1,0:T(8,128)(2,1)S(1)}, u32[]{:S(2)}, u32[]{:S(2)}) collective-permute-start(bf16[512,1024]{1,0:T(8,128)(2,1)S(1)} %chosen.2.refs_0_), channel_id=1, source_target_pairs={{2,0},{3,1},{4,6},{5,7},{0,2},{1,3},{6,4},{7,5},{10,8},{11,9},{12,... | collective-permute-start | bytes 3145736 | tf_op jit(solution)/shard_map/ppermute | solution.py:385
  65.2 3.4 %projection_blocks.8 = (bf16[512,512]{1,0:T(8,128)(2,1)S(1)}, bf16[512,512]{1,0:T(8,128)(2,1)S(1)}) custom-call(s32[10]{0:T(128)S(1)} %plan.1._.plan_ref, bf16[512,1024]{1,0:T(8,128)(2,1)S(1)} %get-tuple-element.64.data_ref, bf16[1024,8192]{1,0:T(8,128)(2,1)} %weight_ref.19, bf16[512,1024]{1,0:T(8,128)(2,1)S(1)} %chosen.2.refs_0_), custom_call_target="tpu_custom_call" | custom-call | flops 1048576 | bytes 4096 | tf_op jit(solution)/shard_map/projection_blocks/pallas_call | solution.py:551
  71.4 3.5 %projection_blocks.9.refs_4_.refs_0_ = bf16[512,1024]{1,0:T(8,128)(2,1)S(1)} custom-call(s32[10]{0:T(128)S(1)} %plan.1._.plan_ref, bf16[512,1024]{1,0:T(8,128)(2,1)S(1)} %get-tuple-element.64.data_ref, bf16[1024,8192]{1,0:T(8,128)(2,1)} %weight_ref.19, bf16[512,512]{1,0:T(8,128)(2,1)S(1)} %collective-permute-done.15.refs_0_, ...), custom_call_target="tpu_custom_call" | custom-call | flops 1048576 | bytes 4096 | tf_op jit(solution)/shard_map/projection_blocks/pallas_call | solution.py:551
  74.9 4.9 %projection_blocks.10 = (bf16[512,1024]{1,0:T(8,128)(2,1)S(1)}, bf16[512,1024]{1,0:T(8,128)(2,1)S(1)}) custom-call(s32[10]{0:T(128)S(1)} %plan.1._.plan_ref, bf16[512,1024]{1,0:T(8,128)(2,1)S(1)} %get-tuple-element.64.data_ref, bf16[1024,8192]{1,0:T(8,128)(2,1)} %weight_ref.19, bf16[512,1024]{1,0:T(8,128)(2,1)S(1)} %projection_blocks.9.refs_4_.refs_0_), custom_call_target="tpu_custom_call" | custom-call | flops 1048576 | bytes 4096 | tf_op jit(solution)/shard_map/projection_blocks/pallas_call | solution.py:551
  79.8 6.4 %cotangent_blocks.4.refs_1_.refs_2_ = f32[512,1024]{1,0:T(8,128)S(1)} custom-call(s32[10]{0:T(128)S(1)} %plan.1._.plan_ref, bf16[1024,8192]{1,0:T(8,128)(2,1)} %weight_ref.19, bf16[512,1024]{1,0:T(8,128)(2,1)S(1)} %get-tuple-element.58.refs_0_, bf16[512,1024]{1,0:T(8,128)(2,1)S(1)} %collective-permute-done.14.refs_1_, bf16[512,1024]{1,0:T(8,128)(2,1)S(1)} %added.4.refs_2_, ...), custom_call_target="tpu_custom_call" | custom-call | flops 1048576 | bytes 4096 | tf_op jit(solution)/shard_map/cotangent_blocks/pallas_call | solution.py:650
  88.1 2.8 %collective-permute-start.25 = (bf16[512,1024]{1,0:T(8,128)(2,1)S(1)}, bf16[512,1024]{1,0:T(8,128)(2,1)S(1)}, u32[]{:S(2)}, u32[]{:S(2)}) collective-permute-start(bf16[512,1024]{1,0:T(8,128)(2,1)S(1)} %held.8.refs_0_), channel_id=1, source_target_pairs={{0,2},{1,3},{6,4},{7,5},{8,10},{9,11},{14,12},{15,13},{16,18},{17,... | collective-permute-start | bytes 3145736 | tf_op jit(solution)/shard_map/ppermute | solution.py:385
  91.7 4.8 %cotangent_blocks.5.start_ref = f32[512,1024]{1,0:T(8,128)S(1)} custom-call(s32[10]{0:T(128)S(1)} %plan.1._.plan_ref, bf16[1024,8192]{1,0:T(8,128)(2,1)} %weight_ref.19, bf16[512,1024]{1,0:T(8,128)(2,1)S(1)} %collective-permute-done.18.refs_0_, bf16[512,1024]{1,0:T(8,128)(2,1)S(1)} %chosen.3.refs_1_, f32[512,1024]{1,0:T(8,128)S(1)} %cotangent_blocks.4.refs_1_.refs_2_, ...), custom_call_target="tpu_custom_call" | custom-call | flops 1048576 | bytes 4096 | tf_op jit(solution)/shard_map/cotangent_blocks/pallas_call | solution.py:650
  96.5 4.5 %cotangent_last.1 = (bf16[512,1024]{1,0:T(8,128)(2,1)}, bf16[512,256]{1,0:T(8,128)(2,1)S(1)}, bf16[512,256]{1,0:T(8,128)(2,1)S(1)}, bf16[512,256]{1,0:T(8,128)(2,1)S(1)}, bf16[512,256]{1,0:T(8,128)(2,1)S(1)}) custom-call(s32[10]{0:T(128)S(1)} %plan.1._.plan_ref, bf16[1024,8192]{1,0:T(8,128)(2,1)} %weight_ref.19, ...), custom_call_target="tpu_custom_call" | custom-call | flops 1048576 | bytes 4096 | tf_op jit(solution)/shard_map/cotangent_last/pallas_call | solution.py:616
  104.4 5.1 %projection_blocks.11 = (bf16[512,1024]{1,0:T(8,128)(2,1)S(1)}, bf16[512,1024]{1,0:T(8,128)(2,1)S(1)}) custom-call(s32[10]{0:T(128)S(1)} %plan.1._.plan_ref, bf16[512,1024]{1,0:T(8,128)(2,1)S(1)} %get-tuple-element.64.data_ref, bf16[1024,8192]{1,0:T(8,128)(2,1)} %weight_ref.19, bf16[512,1024]{1,0:T(8,128)(2,1)S(1)} %collective-permute-done.22.refs_0_, ...), custom_call_target="tpu_custom_call" | custom-call | flops 1048576 | bytes 4096 | tf_op jit(solution)/shard_map/projection_blocks/pallas_call | solution.py:551
  109.6 4.3 %collective-permute-done.25.refs_1_ = bf16[512,1024]{1,0:T(8,128)(2,1)S(1)} collective-permute-done((bf16[512,1024]{1,0:T(8,128)(2,1)S(1)}, bf16[512,1024]{1,0:T(8,128)(2,1)S(1)}, u32[]{:S(2)}, u32[]{:S(2)}) %collective-permute-start.25) | collective-permute-done | bytes 1048608 | tf_op jit(solution)/shard_map/ppermute | solution.py:385
  117.7 3.8 %collective-permute-start.29 = (bf16[512,1024]{1,0:T(8,128)(2,1)S(1)}, bf16[512,1024]{1,0:T(8,128)(2,1)S(1)}, u32[]{:S(2)}, u32[]{:S(2)}) collective-permute-start(bf16[512,1024]{1,0:T(8,128)(2,1)S(1)} %added.6.refs_4_), channel_id=1, source_target_pairs={{2,0},{3,1},{4,6},{5,7},{0,2},{1,3},{6,4},{7,5},{10,8},{11,9},{12,... | collective-permute-start | bytes 3145736 | tf_op jit(solution)/shard_map/ppermute | solution.py:385
  121.5 8.9 %causal_conv_grads.1 = (bf16[544,256]{1,0:T(8,128)(2,1)S(1)}, bf16[544,256]{1,0:T(8,128)(2,1)S(1)}, bf16[544,256]{1,0:T(8,128)(2,1)S(1)}, bf16[544,256]{1,0:T(8,128)(2,1)S(1)}) custom-call(s32[10]{0:T(128)S(1)} %plan.1._.plan_ref, bf16[4,256,512]{2,1,0:T(8,128)(2,1)S(1)} %get-tuple-element.52.in_scr, bf16[16,128,2048]{2,1,0:T(8,128)(2,1)S(1)} %lag_matrices.1.refs_5_.lag_ref, ...), custom_call_target="tpu_custom_call" | custom-call | flops 1048576 | bytes 4096 | tf_op jit(solution)/shard_map/causal_conv_grads/pallas_call | solution.py:226
  134.0 6.1 %collective-permute-done.26.refs_1_ = bf16[544,256]{1,0:T(8,128)(2,1)S(1)} collective-permute-done((bf16[544,256]{1,0:T(8,128)(2,1)S(1)}, bf16[544,256]{1,0:T(8,128)(2,1)S(1)}, u32[]{:S(2)}, u32[]{:S(2)}) %collective-permute-start.26) | collective-permute-done | bytes 278560 | tf_op jit(solution)/shard_map/ppermute | solution.py:352
  140.1 4.7 %collective-permute-done.27.refs_2_ = bf16[544,256]{1,0:T(8,128)(2,1)S(1)} collective-permute-done((bf16[544,256]{1,0:T(8,128)(2,1)S(1)}, bf16[544,256]{1,0:T(8,128)(2,1)S(1)}, u32[]{:S(2)}, u32[]{:S(2)}) %collective-permute-start.27) | collective-permute-done | bytes 278560 | tf_op jit(solution)/shard_map/ppermute | solution.py:352
  144.8 3.2 %input_gradients.1 = (bf16[512,1024]{1,0:T(8,128)(2,1)}, bf16[512,1024]{1,0:T(8,128)(2,1)}, bf16[512,1024]{1,0:T(8,128)(2,1)}, f32[64,512]{1,0:T(8,128)}) custom-call(s32[10]{0:T(128)S(1)} %plan.1._.plan_ref, bf16[544,256]{1,0:T(8,128)(2,1)S(1)} %get-tuple-element.81.refs_0_, bf16[544,256]{1,0:T(8,128)(2,1)S(1)} %collective-permute-done.26.refs_1_, ...), custom_call_target="tpu_custom_call" | custom-call | flops 1048576 | bytes 4096 | tf_op jit(solution)/shard_map/input_gradients/pallas_call | solution.py:334
  (75 shorter events, 35.8 us)
Async XLA Ops:
  0.6 12.6 %collective-permute-start.3 = (bf16[512,1024]{1,0:T(8,128)(2,1)}, bf16[512,1024]{1,0:T(8,128)(2,1)}, u32[]{:S(2)}, u32[]{:S(2)}) collective-permute-start(bf16[512,1024]{1,0:T(8,128)(2,1)} %refs_0_.1), channel_id=1, source_target_pairs={{0,1},{1,0},{2,3},{3,2},{4,5},{5,4},{6,7},{7,6},{8,9},{9,8},{10,11... | collective-permute-start | bytes 3145736 | tf_op jit(solution)/shard_map/ppermute | solution.py:352
  1.2 29.6 %collective-permute-start.5 = (bf16[512,1024]{1,0:T(8,128)(2,1)}, bf16[512,1024]{1,0:T(8,128)(2,1)S(1)}, u32[]{:S(2)}, u32[]{:S(2)}) collective-permute-start(bf16[512,1024]{1,0:T(8,128)(2,1)} %refs_0_.1), channel_id=1, source_target_pairs={{2,4},{3,5},{4,2},{5,3},{10,12},{11,13},{12,10},{13,11},{18,20},{1... | collective-permute-start | bytes 3145736 | tf_op jit(solution)/shard_map/ppermute | solution.py:385
  1.9 29.2 %collective-permute-start.4 = (bf16[512,1024]{1,0:T(8,128)(2,1)}, bf16[512,1024]{1,0:T(8,128)(2,1)S(1)}, u32[]{:S(2)}, u32[]{:S(2)}) collective-permute-start(bf16[512,1024]{1,0:T(8,128)(2,1)} %refs_0_.1), channel_id=1, source_target_pairs={{0,2},{1,3},{6,4},{7,5},{2,0},{3,1},{4,6},{5,7},{8,10},{9,11},{14,... | collective-permute-start | bytes 3145736 | tf_op jit(solution)/shard_map/ppermute | solution.py:385
  10.1 9.8 %collective-permute-start = (bf16[544,256]{1,0:T(8,128)(2,1)S(1)}, bf16[544,256]{1,0:T(8,128)(2,1)S(1)}, u32[]{:S(2)}, u32[]{:S(2)}) collective-permute-start(bf16[544,256]{1,0:T(8,128)(2,1)S(1)} %get-tuple-element.49), channel_id=1, source_target_pairs={{0,8},{8,0},{16,24},{24,16},{1,9},{9,1},{17,25},{25,17},{2,10},{10... | collective-permute-start | bytes 835592 | tf_op jit(solution)/shard_map/ppermute | solution.py:352
  11.7 14.0 %collective-permute-start.1 = (bf16[544,256]{1,0:T(8,128)(2,1)S(1)}, bf16[544,256]{1,0:T(8,128)(2,1)S(1)}, u32[]{:S(2)}, u32[]{:S(2)}) collective-permute-start(bf16[544,256]{1,0:T(8,128)(2,1)S(1)} %get-tuple-element.50), channel_id=1, source_target_pairs={{0,16},{8,24},{16,0},{24,8},{1,17},{9,25},{17,1},{25,9},{2,18},{10... | collective-permute-start | bytes 835592 | tf_op jit(solution)/shard_map/ppermute | solution.py:352
  13.2 12.5 %collective-permute-start.2 = (bf16[544,256]{1,0:T(8,128)(2,1)S(1)}, bf16[544,256]{1,0:T(8,128)(2,1)S(1)}, u32[]{:S(2)}, u32[]{:S(2)}) collective-permute-start(bf16[544,256]{1,0:T(8,128)(2,1)S(1)} %get-tuple-element.51), channel_id=1, source_target_pairs={{0,24},{8,16},{16,8},{24,0},{1,25},{9,17},{17,9},{25,1},{2,26},{10... | collective-permute-start | bytes 835592 | tf_op jit(solution)/shard_map/ppermute | solution.py:352
  32.5 13.1 %collective-permute-start.9 = (bf16[512,256]{1,0:T(8,128)(2,1)S(1)}, bf16[512,256]{1,0:T(8,128)(2,1)S(1)}, u32[]{:S(2)}, u32[]{:S(2)}) collective-permute-start(bf16[512,256]{1,0:T(8,128)(2,1)S(1)} %get-tuple-element.62), channel_id=1, source_target_pairs={{0,16},{8,24},{16,0},{24,8},{1,17},{9,25},{17,1},{25,9},{2,18},{10... | collective-permute-start | bytes 786440 | tf_op jit(solution)/shard_map/ppermute | solution.py:352
  34.1 11.6 %collective-permute-start.10 = (bf16[512,256]{1,0:T(8,128)(2,1)S(1)}, bf16[512,256]{1,0:T(8,128)(2,1)S(1)}, u32[]{:S(2)}, u32[]{:S(2)}) collective-permute-start(bf16[512,256]{1,0:T(8,128)(2,1)S(1)} %get-tuple-element.63), channel_id=1, source_target_pairs={{0,24},{8,16},{16,8},{24,0},{1,25},{9,17},{17,9},{25,1},{2,26},{10... | collective-permute-start | bytes 786440 | tf_op jit(solution)/shard_map/ppermute | solution.py:352
  34.5 25.7 %collective-permute-start.7 = (bf16[512,1024]{1,0:T(8,128)(2,1)S(1)}, bf16[512,1024]{1,0:T(8,128)(2,1)S(1)}, u32[]{:S(2)}, u32[]{:S(2)}) collective-permute-start(bf16[512,1024]{1,0:T(8,128)(2,1)S(1)} %get-tuple-element.59.refs_0_), channel_id=1, source_target_pairs={{2,0},{3,1},{4,6},{5,7},{10,8},{11,9},{12,14},{13,15},{18,16},{19,... | collective-permute-start | bytes 3145736 | tf_op jit(solution)/shard_map/ppermute | solution.py:385
  35.8 24.4 %collective-permute-start.6 = (bf16[512,1024]{1,0:T(8,128)(2,1)S(1)}, bf16[512,1024]{1,0:T(8,128)(2,1)S(1)}, u32[]{:S(2)}, u32[]{:S(2)}) collective-permute-start(bf16[512,1024]{1,0:T(8,128)(2,1)S(1)} %get-tuple-element.58.refs_0_), channel_id=1, source_target_pairs={{2,4},{3,5},{4,2},{5,3},{10,12},{11,13},{12,10},{13,11},{18,20},{1... | collective-permute-start | bytes 3145736 | tf_op jit(solution)/shard_map/ppermute | solution.py:385
  50.5 29.3 %collective-permute-start.14 = (bf16[512,1024]{1,0:T(8,128)(2,1)S(1)}, bf16[512,1024]{1,0:T(8,128)(2,1)S(1)}, u32[]{:S(2)}, u32[]{:S(2)}) collective-permute-start(bf16[512,1024]{1,0:T(8,128)(2,1)S(1)} %get-tuple-element.58.refs_0_), channel_id=1, source_target_pairs={{0,1},{1,0},{2,3},{3,2},{4,5},{5,4},{6,7},{7,6},{8,9},{9,8},{10,11... | collective-permute-start | bytes 3145736 | tf_op jit(solution)/shard_map/ppermute | solution.py:352
  61.0 25.2 %collective-permute-start.13 = (bf16[512,1024]{1,0:T(8,128)(2,1)S(1)}, bf16[512,1024]{1,0:T(8,128)(2,1)S(1)}, u32[]{:S(2)}, u32[]{:S(2)}) collective-permute-start(bf16[512,1024]{1,0:T(8,128)(2,1)S(1)} %chosen.2.refs_0_), channel_id=1, source_target_pairs={{2,0},{3,1},{4,6},{5,7},{0,2},{1,3},{6,4},{7,5},{10,8},{11,9},{12,... | collective-permute-start | bytes 3145736 | tf_op jit(solution)/shard_map/ppermute | solution.py:385
  65.1 25.8 %collective-permute-start.18 = (bf16[512,1024]{1,0:T(8,128)(2,1)S(1)}, bf16[512,1024]{1,0:T(8,128)(2,1)S(1)}, u32[]{:S(2)}, u32[]{:S(2)}) collective-permute-start(bf16[512,1024]{1,0:T(8,128)(2,1)S(1)} %added.4.refs_2_), channel_id=1, source_target_pairs={{0,1},{1,0},{2,3},{3,2},{4,5},{5,4},{6,7},{7,6},{8,9},{9,8},{10,11... | collective-permute-start | bytes 3145736 | tf_op jit(solution)/shard_map/ppermute | solution.py:352
  87.6 14.9 %collective-permute-start.23 = (bf16[512,1024]{1,0:T(8,128)(2,1)S(1)}, bf16[512,1024]{1,0:T(8,128)(2,1)S(1)}, u32[]{:S(2)}, u32[]{:S(2)}) collective-permute-start(bf16[512,1024]{1,0:T(8,128)(2,1)S(1)} %get-tuple-element.77), channel_id=1, source_target_pairs={{0,1},{1,0},{2,3},{3,2},{4,5},{5,4},{6,7},{7,6},{8,9},{9,8},{10,11... | collective-permute-start | bytes 3145736 | tf_op jit(solution)/shard_map/ppermute | solution.py:352
  87.7 16.3 %collective-permute-start.22 = (bf16[512,1024]{1,0:T(8,128)(2,1)S(1)}, bf16[512,1024]{1,0:T(8,128)(2,1)S(1)}, u32[]{:S(2)}, u32[]{:S(2)}) collective-permute-start(bf16[512,1024]{1,0:T(8,128)(2,1)S(1)} %get-tuple-element.71.refs_2_), channel_id=1, source_target_pairs={{0,1},{1,0},{2,3},{3,2},{4,5},{5,4},{6,7},{7,6},{8,9},{9,8},{10,11... | collective-permute-start | bytes 3145736 | tf_op jit(solution)/shard_map/ppermute | solution.py:352
  88.1 25.8 %collective-permute-start.25 = (bf16[512,1024]{1,0:T(8,128)(2,1)S(1)}, bf16[512,1024]{1,0:T(8,128)(2,1)S(1)}, u32[]{:S(2)}, u32[]{:S(2)}) collective-permute-start(bf16[512,1024]{1,0:T(8,128)(2,1)S(1)} %held.8.refs_0_), channel_id=1, source_target_pairs={{0,2},{1,3},{6,4},{7,5},{8,10},{9,11},{14,12},{15,13},{16,18},{17,... | collective-permute-start | bytes 3145736 | tf_op jit(solution)/shard_map/ppermute | solution.py:385
  90.9 22.9 %collective-permute-start.24 = (bf16[512,1024]{1,0:T(8,128)(2,1)S(1)}, bf16[512,1024]{1,0:T(8,128)(2,1)S(1)}, u32[]{:S(2)}, u32[]{:S(2)}) collective-permute-start(bf16[512,1024]{1,0:T(8,128)(2,1)S(1)} %added.5.refs_0_.refs_3_), channel_id=1, source_target_pairs={{2,4},{3,5},{4,2},{5,3},{10,12},{11,13},{12,10},{13,11},{18,20},{1... | collective-permute-start | bytes 3145736 | tf_op jit(solution)/shard_map/ppermute | solution.py:385
  101.0 12.9 %collective-permute-start.19 = (bf16[512,256]{1,0:T(8,128)(2,1)S(1)}, bf16[512,256]{1,0:T(8,128)(2,1)S(1)}, u32[]{:S(2)}, u32[]{:S(2)}) collective-permute-start(bf16[512,256]{1,0:T(8,128)(2,1)S(1)} %get-tuple-element.74), channel_id=1, source_target_pairs={{0,8},{8,0},{16,24},{24,16},{1,9},{9,1},{17,25},{25,17},{2,10},{10... | collective-permute-start | bytes 786440 | tf_op jit(solution)/shard_map/ppermute | solution.py:352
  102.4 13.7 %collective-permute-start.20 = (bf16[512,256]{1,0:T(8,128)(2,1)S(1)}, bf16[512,256]{1,0:T(8,128)(2,1)S(1)}, u32[]{:S(2)}, u32[]{:S(2)}) collective-permute-start(bf16[512,256]{1,0:T(8,128)(2,1)S(1)} %get-tuple-element.75), channel_id=1, source_target_pairs={{0,16},{8,24},{16,0},{24,8},{1,17},{9,25},{17,1},{25,9},{2,18},{10... | collective-permute-start | bytes 786440 | tf_op jit(solution)/shard_map/ppermute | solution.py:352
  104.0 12.2 %collective-permute-start.21 = (bf16[512,256]{1,0:T(8,128)(2,1)S(1)}, bf16[512,256]{1,0:T(8,128)(2,1)S(1)}, u32[]{:S(2)}, u32[]{:S(2)}) collective-permute-start(bf16[512,256]{1,0:T(8,128)(2,1)S(1)} %get-tuple-element.76), channel_id=1, source_target_pairs={{0,24},{8,16},{16,8},{24,0},{1,25},{9,17},{17,9},{25,1},{2,26},{10... | collective-permute-start | bytes 786440 | tf_op jit(solution)/shard_map/ppermute | solution.py:352
  116.5 28.3 %collective-permute-start.30 = (bf16[512,1024]{1,0:T(8,128)(2,1)S(1)}, bf16[512,1024]{1,0:T(8,128)(2,1)S(1)}, u32[]{:S(2)}, u32[]{:S(2)}) collective-permute-start(bf16[512,1024]{1,0:T(8,128)(2,1)S(1)} %added.7.refs_5_), channel_id=1, source_target_pairs={{2,4},{3,5},{4,2},{5,3},{10,12},{11,13},{12,10},{13,11},{18,20},{1... | collective-permute-start | bytes 3145736 | tf_op jit(solution)/shard_map/ppermute | solution.py:385
  117.7 27.0 %collective-permute-start.29 = (bf16[512,1024]{1,0:T(8,128)(2,1)S(1)}, bf16[512,1024]{1,0:T(8,128)(2,1)S(1)}, u32[]{:S(2)}, u32[]{:S(2)}) collective-permute-start(bf16[512,1024]{1,0:T(8,128)(2,1)S(1)} %added.6.refs_4_), channel_id=1, source_target_pairs={{2,0},{3,1},{4,6},{5,7},{0,2},{1,3},{6,4},{7,5},{10,8},{11,9},{12,... | collective-permute-start | bytes 3145736 | tf_op jit(solution)/shard_map/ppermute | solution.py:385
  131.7 13.1 %collective-permute-start.27 = (bf16[544,256]{1,0:T(8,128)(2,1)S(1)}, bf16[544,256]{1,0:T(8,128)(2,1)S(1)}, u32[]{:S(2)}, u32[]{:S(2)}) collective-permute-start(bf16[544,256]{1,0:T(8,128)(2,1)S(1)} %get-tuple-element.83), channel_id=1, source_target_pairs={{0,16},{8,24},{16,0},{24,8},{1,17},{9,25},{17,1},{25,9},{2,18},{10... | collective-permute-start | bytes 835592 | tf_op jit(solution)/shard_map/ppermute | solution.py:352
  132.9 11.8 %collective-permute-start.28 = (bf16[544,256]{1,0:T(8,128)(2,1)S(1)}, bf16[544,256]{1,0:T(8,128)(2,1)S(1)}, u32[]{:S(2)}, u32[]{:S(2)}) collective-permute-start(bf16[544,256]{1,0:T(8,128)(2,1)S(1)} %get-tuple-element.84), channel_id=1, source_target_pairs={{0,24},{8,16},{16,8},{24,0},{1,25},{9,17},{17,9},{25,1},{2,26},{10... | collective-permute-start | bytes 835592 | tf_op jit(solution)/shard_map/ppermute | solution.py:352
  (11 other events, 107.8 us)

commit v17 on v16

--- a/solution.py
+++ b/solution.py
@@ -238,7 +238,7 @@
             pltpu.VMEM((batch, 2 * length // BLOCK * per_group, 2 * BLOCK), jnp.bfloat16),
         ],
         compiler_params=pltpu.CompilerParams(vmem_limit_bytes=24 * 2**20),
-        cost_estimate=COST,
+        cost_estimate=pl.CostEstimate(flops=10**10, bytes_accessed=2**12, transcendentals=0),
         name="causal_conv_grads",
     )(plan, turned, lags, *cotangents, *after)
 
@@ -749,14 +749,14 @@
     total = cotangent_products(
         plan, 2 * MIDDLE + 1, blocks, out_weight, total, after=(through,)
     )
+    received = [swapped(part, "tp", 1) for part in (given_near, given_own)]
     grad_query, *grad_parts = last_cotangents(
-        plan, 2 * FAR + 1, far_other, out_weight, total, convolved, query_gate, members, ()
-    )
-    received = (swapped(given_near, "tp", 1), swapped(given_own, "tp", 1))
+        plan, 2 * FAR + 1, far_other, out_weight, total, convolved, query_gate, members, received
+    )
     third, own = product(NEAR, 2, 0, received, (grad_parts[0],))
     grad_parts = traded(grad_parts, "ctx")
 
-    two_a, two_b = held_until([two_a, two_b], tuple(grad_parts[1:]))
+    two_a, two_b = held_until([two_a, two_b], (own,))
     third, second = added(third, two_a), added(second, two_b)
     back_parts = correlate(plan, turned, lags, grad_parts, per_group, scale, (third, second))
     summands = (own, hop(third, OUTWARD + INWARD), hop(second, ACROSS))

time: 149 us -> 148 us (level)
  waiting for transfers between devices: 37.4 us -> 35.9 us
    ppermute x22, waiting for transfers between devices: 28.8 us -> 27.1 us  [swapped(): return lax.ppermute(array, axis, [(i, i ^ step) for i in range(size)])]
  transfers between devices with their start and end apart: 31 -> 31, of which waited for: 12 -> 11; matrix products, arithmetic and copies ran while one was open for 0% -> 0% of each run, Pallas kernels for 46% -> 47%
where the time goes in v17:
time: 148 us
  Pallas kernels  72.2 us (49%)
  starting transfers between devices  38.4 us (26%)
  waiting for transfers between devices  35.9 us (24%)
    ppermute x22, waiting for transfers between devices, swapped(): return lax.ppermute(array, axis, [(i, i ^ step) for i in range(size)])  27.1 us
    pallas_call x6, Pallas kernels, column_products(): pl.pallas_call(functools.partial(product_kernel, steps, [part.shape[1] fo...  23.8 us
    ppermute x9, starting transfers between devices, hop(): lax.ppermute(array, 'tp', [(2 * i + core, 2 * j + core) for i, j in pairs...  21.4 us
    ppermute x22, starting transfers between devices, swapped(): return lax.ppermute(array, axis, [(i, i ^ step) for i in range(size)])  17 us
    pallas_call x3, Pallas kernels, cotangent_products(): pl.pallas_call(functools.partial(cotangent_kernel, count, begin), out_sha...  16.2 us
    pallas_call x1, Pallas kernels, correlate(): pl.pallas_call(functools.partial(backward_kernel, members, batch, per_gro...  8.93 us
    ppermute x9, waiting for transfers between devices, hop(): lax.ppermute(array, 'tp', [(2 * i + core, 2 * j + core) for i, j in pairs...  8.75 us
    pallas_call x1, Pallas kernels, convolve(): pl.pallas_call(functools.partial(forward_kernel, members, per_group, widt...  4.89 us
  transfers between devices with their start and end apart: 31, of which 11 were waited for; matrix products, arithmetic and copies ran while one was open for 0% of the time, Pallas kernels for 47%

profile of v17, /device:TPU:0, one launch (start us, length us, event | category | flops | bytes accessed | tf_op | source)
XLA Modules:
  0.0 147.7 jit_solution(1849377292514327021)
XLA Ops:
  1.9 5.6 %collective-permute-start.4 = (bf16[512,1024]{1,0:T(8,128)(2,1)}, bf16[512,1024]{1,0:T(8,128)(2,1)S(1)}, u32[]{:S(2)}, u32[]{:S(2)}) collective-permute-start(bf16[512,1024]{1,0:T(8,128)(2,1)} %refs_0_.1), channel_id=1, source_target_pairs={{0,2},{1,3},{6,4},{7,5},{2,0},{3,1},{4,6},{5,7},{8,10},{9,11},{14,... | collective-permute-start | bytes 3145736 | tf_op jit(solution)/shard_map/ppermute | solution.py:385
  7.5 2.6 %gated_input.1 = (bf16[544,256]{1,0:T(8,128)(2,1)S(1)}, bf16[544,256]{1,0:T(8,128)(2,1)S(1)}, bf16[544,256]{1,0:T(8,128)(2,1)S(1)}, bf16[544,256]{1,0:T(8,128)(2,1)S(1)}) custom-call(s32[2]{0:T(128)S(1)} %pad_add_fusion.who_ref, bf16[512,1024]{1,0:T(8,128)(2,1)} %refs_4_.3, bf16[512,1024]{1,0:T(8,128)(2,1)} %refs_5_.1, f32[64,512]{1,0:T(8,128)} %bitcast.4), custom_call_target="tpu_custom_call" | custom-call | flops 1048576 | bytes 4096 | tf_op jit(solution)/shard_map/gated_input/pallas_call | solution.py:285
  14.9 5.0 %cotangent_blocks.3.refs_4_.refs_3_ = f32[512,1024]{1,0:T(8,128)S(1)} custom-call(s32[10]{0:T(128)S(1)} %plan.1._.plan_ref, bf16[1024,8192]{1,0:T(8,128)(2,1)} %weight_ref.19, bf16[512,1024]{1,0:T(8,128)(2,1)S(1)} %copy-done.3, bf16[512,1024]{1,0:T(8,128)(2,1)} %collective-permute-done.3.refs_1_), custom_call_target="tpu_custom_call" | custom-call | flops 1048576 | bytes 4096 | tf_op jit(solution)/shard_map/cotangent_blocks/pallas_call | solution.py:650
  19.9 5.8 %collective-permute-done.1.refs_2_ = bf16[544,256]{1,0:T(8,128)(2,1)S(1)} collective-permute-done((bf16[544,256]{1,0:T(8,128)(2,1)S(1)}, bf16[544,256]{1,0:T(8,128)(2,1)S(1)}, u32[]{:S(2)}, u32[]{:S(2)}) %collective-permute-start.1) | collective-permute-done | bytes 278560 | tf_op jit(solution)/shard_map/ppermute | solution.py:352
  25.7 4.9 %causal_conv.1 = (bf16[512,256]{1,0:T(8,128)(2,1)S(1)}, bf16[512,256]{1,0:T(8,128)(2,1)S(1)}, bf16[512,256]{1,0:T(8,128)(2,1)S(1)}, bf16[512,256]{1,0:T(8,128)(2...) custom-call(s32[10]{0:T(128)S(1)} %plan.1._.plan_ref, bf16[544,256]{1,0:T(8,128)(2,1)S(1)} %get-tuple-element.48.refs_0_, ...), custom_call_target="tpu_custom_call" | custom-call | flops 1048576 | bytes 4096 | tf_op jit(solution)/shard_map/causal_conv/pallas_call | solution.py:188
  36.6 3.4 %lag_matrices.1.refs_5_.lag_ref = bf16[16,128,2048]{2,1,0:T(8,128)(2,1)S(1)} custom-call(f32[16,2048]{1,0:T(8,128)S(1)} %get-tuple-element.53.taps_ref), custom_call_target="tpu_custom_call" | custom-call | flops 1048576 | bytes 4096 | tf_op jit(solution)/shard_map/lag_matrices/pallas_call | solution.py:207
  40.3 5.4 %collective-permute-done.9.refs_2_ = bf16[512,256]{1,0:T(8,128)(2,1)S(1)} collective-permute-done((bf16[512,256]{1,0:T(8,128)(2,1)S(1)}, bf16[512,256]{1,0:T(8,128)(2,1)S(1)}, u32[]{:S(2)}, u32[]{:S(2)}) %collective-permute-start.9) | collective-permute-done | bytes 262176 | tf_op jit(solution)/shard_map/ppermute | solution.py:352
  46.5 3.4 %projection_blocks.6 = (bf16[512,768]{1,0:T(8,128)(2,1)S(1)}, bf16[512,256]{1,0:T(8,128)(2,1)S(1)}) custom-call(s32[10]{0:T(128)S(1)} %plan.1._.plan_ref, bf16[512,1024]{1,0:T(8,128)(2,1)S(1)} %get-tuple-element.64.data_ref, bf16[1024,8192]{1,0:T(8,128)(2,1)} %weight_ref.19), custom_call_target="tpu_custom_call" | custom-call | flops 1048576 | bytes 4096 | tf_op jit(solution)/shard_map/projection_blocks/pallas_call | solution.py:551
  52.6 3.5 %projection_blocks.7.refs_2_.end_ref.refs_0_ = bf16[512,1024]{1,0:T(8,128)(2,1)S(1)} custom-call(s32[10]{0:T(128)S(1)} %plan.1._.plan_ref, bf16[512,1024]{1,0:T(8,128)(2,1)S(1)} %get-tuple-element.64.data_ref, bf16[1024,8192]{1,0:T(8,128)(2,1)} %weight_ref.19, bf16[512,768]{1,0:T(8,128)(2,1)S(1)} %collective-permute-done.11.refs_0_, ...), custom_call_target="tpu_custom_call" | custom-call | flops 1048576 | bytes 4096 | tf_op jit(solution)/shard_map/projection_blocks/pallas_call | solution.py:551
  56.1 4.1 %collective-permute-done.7.refs_1_ = bf16[512,1024]{1,0:T(8,128)(2,1)S(1)} collective-permute-done((bf16[512,1024]{1,0:T(8,128)(2,1)S(1)}, bf16[512,1024]{1,0:T(8,128)(2,1)S(1)}, u32[]{:S(2)}, u32[]{:S(2)}) %collective-permute-start.7) | collective-permute-done | bytes 1048608 | tf_op jit(solution)/shard_map/ppermute | solution.py:385
  61.0 3.8 %collective-permute-start.13 = (bf16[512,1024]{1,0:T(8,128)(2,1)S(1)}, bf16[512,1024]{1,0:T(8,128)(2,1)S(1)}, u32[]{:S(2)}, u32[]{:S(2)}) collective-permute-start(bf16[512,1024]{1,0:T(8,128)(2,1)S(1)} %chosen.2.refs_0_), channel_id=1, source_target_pairs={{2,0},{3,1},{4,6},{5,7},{0,2},{1,3},{6,4},{7,5},{10,8},{11,9},{12,... | collective-permute-start | bytes 3145736 | tf_op jit(solution)/shard_map/ppermute | solution.py:385
  65.2 3.4 %projection_blocks.8 = (bf16[512,512]{1,0:T(8,128)(2,1)S(1)}, bf16[512,512]{1,0:T(8,128)(2,1)S(1)}) custom-call(s32[10]{0:T(128)S(1)} %plan.1._.plan_ref, bf16[512,1024]{1,0:T(8,128)(2,1)S(1)} %get-tuple-element.64.data_ref, bf16[1024,8192]{1,0:T(8,128)(2,1)} %weight_ref.19, bf16[512,1024]{1,0:T(8,128)(2,1)S(1)} %chosen.2.refs_0_), custom_call_target="tpu_custom_call" | custom-call | flops 1048576 | bytes 4096 | tf_op jit(solution)/shard_map/projection_blocks/pallas_call | solution.py:551
  71.4 3.5 %projection_blocks.9.refs_4_.refs_0_ = bf16[512,1024]{1,0:T(8,128)(2,1)S(1)} custom-call(s32[10]{0:T(128)S(1)} %plan.1._.plan_ref, bf16[512,1024]{1,0:T(8,128)(2,1)S(1)} %get-tuple-element.64.data_ref, bf16[1024,8192]{1,0:T(8,128)(2,1)} %weight_ref.19, bf16[512,512]{1,0:T(8,128)(2,1)S(1)} %collective-permute-done.15.refs_0_, ...), custom_call_target="tpu_custom_call" | custom-call | flops 1048576 | bytes 4096 | tf_op jit(solution)/shard_map/projection_blocks/pallas_call | solution.py:551
  74.9 4.9 %projection_blocks.10 = (bf16[512,1024]{1,0:T(8,128)(2,1)S(1)}, bf16[512,1024]{1,0:T(8,128)(2,1)S(1)}) custom-call(s32[10]{0:T(128)S(1)} %plan.1._.plan_ref, bf16[512,1024]{1,0:T(8,128)(2,1)S(1)} %get-tuple-element.64.data_ref, bf16[1024,8192]{1,0:T(8,128)(2,1)} %weight_ref.19, bf16[512,1024]{1,0:T(8,128)(2,1)S(1)} %projection_blocks.9.refs_4_.refs_0_), custom_call_target="tpu_custom_call" | custom-call | flops 1048576 | bytes 4096 | tf_op jit(solution)/shard_map/projection_blocks/pallas_call | solution.py:551
  80.4 6.4 %cotangent_blocks.4.refs_1_.refs_2_ = f32[512,1024]{1,0:T(8,128)S(1)} custom-call(s32[10]{0:T(128)S(1)} %plan.1._.plan_ref, bf16[1024,8192]{1,0:T(8,128)(2,1)} %weight_ref.19, bf16[512,1024]{1,0:T(8,128)(2,1)S(1)} %get-tuple-element.58.refs_0_, bf16[512,1024]{1,0:T(8,128)(2,1)S(1)} %collective-permute-done.14.refs_1_, bf16[512,1024]{1,0:T(8,128)(2,1)S(1)} %added.4.refs_2_, ...), custom_call_target="tpu_custom_call" | custom-call | flops 1048576 | bytes 4096 | tf_op jit(solution)/shard_map/cotangent_blocks/pallas_call | solution.py:650
  91.1 4.8 %cotangent_blocks.5.start_ref = f32[512,1024]{1,0:T(8,128)S(1)} custom-call(s32[10]{0:T(128)S(1)} %plan.1._.plan_ref, bf16[1024,8192]{1,0:T(8,128)(2,1)} %weight_ref.19, bf16[512,1024]{1,0:T(8,128)(2,1)S(1)} %collective-permute-done.18.refs_0_, bf16[512,1024]{1,0:T(8,128)(2,1)S(1)} %chosen.3.refs_1_, f32[512,1024]{1,0:T(8,128)S(1)} %cotangent_blocks.4.refs_1_.refs_2_, ...), custom_call_target="tpu_custom_call" | custom-call | flops 1048576 | bytes 4096 | tf_op jit(solution)/shard_map/cotangent_blocks/pallas_call | solution.py:650
  95.9 4.5 %cotangent_last.1 = (bf16[512,1024]{1,0:T(8,128)(2,1)}, bf16[512,256]{1,0:T(8,128)(2,1)S(1)}, bf16[512,256]{1,0:T(8,128)(2,1)S(1)}, bf16[512,256]{1,0:T(8,128)(2,1)S(1)}, bf16[512,256]{1,0:T(8,128)(2,1)S(1)}) custom-call(s32[10]{0:T(128)S(1)} %plan.1._.plan_ref, bf16[1024,8192]{1,0:T(8,128)(2,1)} %weight_ref.19, ...), custom_call_target="tpu_custom_call" | custom-call | flops 1048576 | bytes 4096 | tf_op jit(solution)/shard_map/cotangent_last/pallas_call | solution.py:616
  103.9 5.1 %projection_blocks.11 = (bf16[512,1024]{1,0:T(8,128)(2,1)S(1)}, bf16[512,1024]{1,0:T(8,128)(2,1)S(1)}) custom-call(s32[10]{0:T(128)S(1)} %plan.1._.plan_ref, bf16[512,1024]{1,0:T(8,128)(2,1)S(1)} %get-tuple-element.64.data_ref, bf16[1024,8192]{1,0:T(8,128)(2,1)} %weight_ref.19, bf16[512,1024]{1,0:T(8,128)(2,1)S(1)} %collective-permute-done.19.refs_0_, ...), custom_call_target="tpu_custom_call" | custom-call | flops 1048576 | bytes 4096 | tf_op jit(solution)/shard_map/projection_blocks/pallas_call | solution.py:551
  109.0 4.3 %collective-permute-done.25.refs_1_ = bf16[512,1024]{1,0:T(8,128)(2,1)S(1)} collective-permute-done((bf16[512,1024]{1,0:T(8,128)(2,1)S(1)}, bf16[512,1024]{1,0:T(8,128)(2,1)S(1)}, u32[]{:S(2)}, u32[]{:S(2)}) %collective-permute-start.25) | collective-permute-done | bytes 1048608 | tf_op jit(solution)/shard_map/ppermute | solution.py:385
  114.9 5.5 %collective-permute-start.29 = (bf16[512,1024]{1,0:T(8,128)(2,1)S(1)}, bf16[512,1024]{1,0:T(8,128)(2,1)S(1)}, u32[]{:S(2)}, u32[]{:S(2)}) collective-permute-start(bf16[512,1024]{1,0:T(8,128)(2,1)S(1)} %added.6.refs_4_), channel_id=1, source_target_pairs={{2,0},{3,1},{4,6},{5,7},{0,2},{1,3},{6,4},{7,5},{10,8},{11,9},{12,... | collective-permute-start | bytes 3145736 | tf_op jit(solution)/shard_map/ppermute | solution.py:385
  120.4 8.9 %causal_conv_grads.1 = (bf16[544,256]{1,0:T(8,128)(2,1)S(1)}, bf16[544,256]{1,0:T(8,128)(2,1)S(1)}, bf16[544,256]{1,0:T(8,128)(2,1)S(1)}, bf16[544,256]{1,0:T(8,128)(2,1)S(1)}) custom-call(s32[10]{0:T(128)S(1)} %plan.1._.plan_ref, bf16[4,256,512]{2,1,0:T(8,128)(2,1)S(1)} %get-tuple-element.52.in_scr, bf16[16,128,2048]{2,1,0:T(8,128)(2,1)S(1)} %lag_matrices.1.refs_5_.lag_ref, ...), custom_call_target="tpu_custom_call" | custom-call | flops 10000000000 | bytes 4096 | tf_op jit(solution)/shard_map/causal_conv_grads/pallas_call | solution.py:226
  132.9 6.1 %collective-permute-done.26.refs_1_ = bf16[544,256]{1,0:T(8,128)(2,1)S(1)} collective-permute-done((bf16[544,256]{1,0:T(8,128)(2,1)S(1)}, bf16[544,256]{1,0:T(8,128)(2,1)S(1)}, u32[]{:S(2)}, u32[]{:S(2)}) %collective-permute-start.26) | collective-permute-done | bytes 278560 | tf_op jit(solution)/shard_map/ppermute | solution.py:352
  139.0 5.3 %collective-permute-done.27.refs_2_ = bf16[544,256]{1,0:T(8,128)(2,1)S(1)} collective-permute-done((bf16[544,256]{1,0:T(8,128)(2,1)S(1)}, bf16[544,256]{1,0:T(8,128)(2,1)S(1)}, u32[]{:S(2)}, u32[]{:S(2)}) %collective-permute-start.27) | collective-permute-done | bytes 278560 | tf_op jit(solution)/shard_map/ppermute | solution.py:352
  144.3 3.2 %input_gradients.1 = (bf16[512,1024]{1,0:T(8,128)(2,1)}, bf16[512,1024]{1,0:T(8,128)(2,1)}, bf16[512,1024]{1,0:T(8,128)(2,1)}, f32[64,512]{1,0:T(8,128)}) custom-call(s32[10]{0:T(128)S(1)} %plan.1._.plan_ref, bf16[544,256]{1,0:T(8,128)(2,1)S(1)} %get-tuple-element.82.refs_0_, bf16[544,256]{1,0:T(8,128)(2,1)S(1)} %collective-permute-done.26.refs_1_, ...), custom_call_target="tpu_custom_call" | custom-call | flops 1048576 | bytes 4096 | tf_op jit(solution)/shard_map/input_gradients/pallas_call | solution.py:334
  (75 shorter events, 33.3 us)
Async XLA Ops:
  0.6 12.6 %collective-permute-start.3 = (bf16[512,1024]{1,0:T(8,128)(2,1)}, bf16[512,1024]{1,0:T(8,128)(2,1)}, u32[]{:S(2)}, u32[]{:S(2)}) collective-permute-start(bf16[512,1024]{1,0:T(8,128)(2,1)} %refs_0_.1), channel_id=1, source_target_pairs={{0,1},{1,0},{2,3},{3,2},{4,5},{5,4},{6,7},{7,6},{8,9},{9,8},{10,11... | collective-permute-start | bytes 3145736 | tf_op jit(solution)/shard_map/ppermute | solution.py:352
  1.2 29.5 %collective-permute-start.5 = (bf16[512,1024]{1,0:T(8,128)(2,1)}, bf16[512,1024]{1,0:T(8,128)(2,1)S(1)}, u32[]{:S(2)}, u32[]{:S(2)}) collective-permute-start(bf16[512,1024]{1,0:T(8,128)(2,1)} %refs_0_.1), channel_id=1, source_target_pairs={{2,4},{3,5},{4,2},{5,3},{10,12},{11,13},{12,10},{13,11},{18,20},{1... | collective-permute-start | bytes 3145736 | tf_op jit(solution)/shard_map/ppermute | solution.py:385
  1.9 29.2 %collective-permute-start.4 = (bf16[512,1024]{1,0:T(8,128)(2,1)}, bf16[512,1024]{1,0:T(8,128)(2,1)S(1)}, u32[]{:S(2)}, u32[]{:S(2)}) collective-permute-start(bf16[512,1024]{1,0:T(8,128)(2,1)} %refs_0_.1), channel_id=1, source_target_pairs={{0,2},{1,3},{6,4},{7,5},{2,0},{3,1},{4,6},{5,7},{8,10},{9,11},{14,... | collective-permute-start | bytes 3145736 | tf_op jit(solution)/shard_map/ppermute | solution.py:385
  10.1 9.8 %collective-permute-start = (bf16[544,256]{1,0:T(8,128)(2,1)S(1)}, bf16[544,256]{1,0:T(8,128)(2,1)S(1)}, u32[]{:S(2)}, u32[]{:S(2)}) collective-permute-start(bf16[544,256]{1,0:T(8,128)(2,1)S(1)} %get-tuple-element.49), channel_id=1, source_target_pairs={{0,8},{8,0},{16,24},{24,16},{1,9},{9,1},{17,25},{25,17},{2,10},{10... | collective-permute-start | bytes 835592 | tf_op jit(solution)/shard_map/ppermute | solution.py:352
  11.7 14.0 %collective-permute-start.1 = (bf16[544,256]{1,0:T(8,128)(2,1)S(1)}, bf16[544,256]{1,0:T(8,128)(2,1)S(1)}, u32[]{:S(2)}, u32[]{:S(2)}) collective-permute-start(bf16[544,256]{1,0:T(8,128)(2,1)S(1)} %get-tuple-element.50), channel_id=1, source_target_pairs={{0,16},{8,24},{16,0},{24,8},{1,17},{9,25},{17,1},{25,9},{2,18},{10... | collective-permute-start | bytes 835592 | tf_op jit(solution)/shard_map/ppermute | solution.py:352
  13.2 12.5 %collective-permute-start.2 = (bf16[544,256]{1,0:T(8,128)(2,1)S(1)}, bf16[544,256]{1,0:T(8,128)(2,1)S(1)}, u32[]{:S(2)}, u32[]{:S(2)}) collective-permute-start(bf16[544,256]{1,0:T(8,128)(2,1)S(1)} %get-tuple-element.51), channel_id=1, source_target_pairs={{0,24},{8,16},{16,8},{24,0},{1,25},{9,17},{17,9},{25,1},{2,26},{10... | collective-permute-start | bytes 835592 | tf_op jit(solution)/shard_map/ppermute | solution.py:352
  32.5 13.1 %collective-permute-start.9 = (bf16[512,256]{1,0:T(8,128)(2,1)S(1)}, bf16[512,256]{1,0:T(8,128)(2,1)S(1)}, u32[]{:S(2)}, u32[]{:S(2)}) collective-permute-start(bf16[512,256]{1,0:T(8,128)(2,1)S(1)} %get-tuple-element.62), channel_id=1, source_target_pairs={{0,16},{8,24},{16,0},{24,8},{1,17},{9,25},{17,1},{25,9},{2,18},{10... | collective-permute-start | bytes 786440 | tf_op jit(solution)/shard_map/ppermute | solution.py:352
  34.1 11.6 %collective-permute-start.10 = (bf16[512,256]{1,0:T(8,128)(2,1)S(1)}, bf16[512,256]{1,0:T(8,128)(2,1)S(1)}, u32[]{:S(2)}, u32[]{:S(2)}) collective-permute-start(bf16[512,256]{1,0:T(8,128)(2,1)S(1)} %get-tuple-element.63), channel_id=1, source_target_pairs={{0,24},{8,16},{16,8},{24,0},{1,25},{9,17},{17,9},{25,1},{2,26},{10... | collective-permute-start | bytes 786440 | tf_op jit(solution)/shard_map/ppermute | solution.py:352
  34.5 25.7 %collective-permute-start.7 = (bf16[512,1024]{1,0:T(8,128)(2,1)S(1)}, bf16[512,1024]{1,0:T(8,128)(2,1)S(1)}, u32[]{:S(2)}, u32[]{:S(2)}) collective-permute-start(bf16[512,1024]{1,0:T(8,128)(2,1)S(1)} %get-tuple-element.59.refs_0_), channel_id=1, source_target_pairs={{2,0},{3,1},{4,6},{5,7},{10,8},{11,9},{12,14},{13,15},{18,16},{19,... | collective-permute-start | bytes 3145736 | tf_op jit(solution)/shard_map/ppermute | solution.py:385
  35.8 24.4 %collective-permute-start.6 = (bf16[512,1024]{1,0:T(8,128)(2,1)S(1)}, bf16[512,1024]{1,0:T(8,128)(2,1)S(1)}, u32[]{:S(2)}, u32[]{:S(2)}) collective-permute-start(bf16[512,1024]{1,0:T(8,128)(2,1)S(1)} %get-tuple-element.58.refs_0_), channel_id=1, source_target_pairs={{2,4},{3,5},{4,2},{5,3},{10,12},{11,13},{12,10},{13,11},{18,20},{1... | collective-permute-start | bytes 3145736 | tf_op jit(solution)/shard_map/ppermute | solution.py:385
  50.5 29.9 %collective-permute-start.14 = (bf16[512,1024]{1,0:T(8,128)(2,1)S(1)}, bf16[512,1024]{1,0:T(8,128)(2,1)S(1)}, u32[]{:S(2)}, u32[]{:S(2)}) collective-permute-start(bf16[512,1024]{1,0:T(8,128)(2,1)S(1)} %get-tuple-element.58.refs_0_), channel_id=1, source_target_pairs={{0,1},{1,0},{2,3},{3,2},{4,5},{5,4},{6,7},{7,6},{8,9},{9,8},{10,11... | collective-permute-start | bytes 3145736 | tf_op jit(solution)/shard_map/ppermute | solution.py:352
  61.0 25.7 %collective-permute-start.13 = (bf16[512,1024]{1,0:T(8,128)(2,1)S(1)}, bf16[512,1024]{1,0:T(8,128)(2,1)S(1)}, u32[]{:S(2)}, u32[]{:S(2)}) collective-permute-start(bf16[512,1024]{1,0:T(8,128)(2,1)S(1)} %chosen.2.refs_0_), channel_id=1, source_target_pairs={{2,0},{3,1},{4,6},{5,7},{0,2},{1,3},{6,4},{7,5},{10,8},{11,9},{12,... | collective-permute-start | bytes 3145736 | tf_op jit(solution)/shard_map/ppermute | solution.py:385
  65.1 25.3 %collective-permute-start.18 = (bf16[512,1024]{1,0:T(8,128)(2,1)S(1)}, bf16[512,1024]{1,0:T(8,128)(2,1)S(1)}, u32[]{:S(2)}, u32[]{:S(2)}) collective-permute-start(bf16[512,1024]{1,0:T(8,128)(2,1)S(1)} %added.4.refs_2_), channel_id=1, source_target_pairs={{0,1},{1,0},{2,3},{3,2},{4,5},{5,4},{6,7},{7,6},{8,9},{9,8},{10,11... | collective-permute-start | bytes 3145736 | tf_op jit(solution)/shard_map/ppermute | solution.py:352
  79.8 16.1 %collective-permute-start.20 = (bf16[512,1024]{1,0:T(8,128)(2,1)S(1)}, bf16[512,1024]{1,0:T(8,128)(2,1)S(1)}, u32[]{:S(2)}, u32[]{:S(2)}) collective-permute-start(bf16[512,1024]{1,0:T(8,128)(2,1)S(1)} %get-tuple-element.73), channel_id=1, source_target_pairs={{0,1},{1,0},{2,3},{3,2},{4,5},{5,4},{6,7},{7,6},{8,9},{9,8},{10,11... | collective-permute-start | bytes 3145736 | tf_op jit(solution)/shard_map/ppermute | solution.py:352
  80.2 15.7 %collective-permute-start.19 = (bf16[512,1024]{1,0:T(8,128)(2,1)S(1)}, bf16[512,1024]{1,0:T(8,128)(2,1)S(1)}, u32[]{:S(2)}, u32[]{:S(2)}) collective-permute-start(bf16[512,1024]{1,0:T(8,128)(2,1)S(1)} %get-tuple-element.71.refs_2_), channel_id=1, source_target_pairs={{0,1},{1,0},{2,3},{3,2},{4,5},{5,4},{6,7},{7,6},{8,9},{9,8},{10,11... | collective-permute-start | bytes 3145736 | tf_op jit(solution)/shard_map/ppermute | solution.py:352
  88.1 25.2 %collective-permute-start.25 = (bf16[512,1024]{1,0:T(8,128)(2,1)S(1)}, bf16[512,1024]{1,0:T(8,128)(2,1)S(1)}, u32[]{:S(2)}, u32[]{:S(2)}) collective-permute-start(bf16[512,1024]{1,0:T(8,128)(2,1)S(1)} %held.8.refs_0_), channel_id=1, source_target_pairs={{0,2},{1,3},{6,4},{7,5},{8,10},{9,11},{14,12},{15,13},{16,18},{17,... | collective-permute-start | bytes 3145736 | tf_op jit(solution)/shard_map/ppermute | solution.py:385
  90.4 23.0 %collective-permute-start.24 = (bf16[512,1024]{1,0:T(8,128)(2,1)S(1)}, bf16[512,1024]{1,0:T(8,128)(2,1)S(1)}, u32[]{:S(2)}, u32[]{:S(2)}) collective-permute-start(bf16[512,1024]{1,0:T(8,128)(2,1)S(1)} %added.5.refs_0_.refs_3_), channel_id=1, source_target_pairs={{2,4},{3,5},{4,2},{5,3},{10,12},{11,13},{12,10},{13,11},{18,20},{1... | collective-permute-start | bytes 3145736 | tf_op jit(solution)/shard_map/ppermute | solution.py:385
  100.4 20.0 %collective-permute-start.21 = (bf16[512,256]{1,0:T(8,128)(2,1)S(1)}, bf16[512,256]{1,0:T(8,128)(2,1)S(1)}, u32[]{:S(2)}, u32[]{:S(2)}) collective-permute-start(bf16[512,256]{1,0:T(8,128)(2,1)S(1)} %get-tuple-element.75), channel_id=1, source_target_pairs={{0,8},{8,0},{16,24},{24,16},{1,9},{9,1},{17,25},{25,17},{2,10},{10... | collective-permute-start | bytes 786440 | tf_op jit(solution)/shard_map/ppermute | solution.py:352
  101.9 18.5 %collective-permute-start.22 = (bf16[512,256]{1,0:T(8,128)(2,1)S(1)}, bf16[512,256]{1,0:T(8,128)(2,1)S(1)}, u32[]{:S(2)}, u32[]{:S(2)}) collective-permute-start(bf16[512,256]{1,0:T(8,128)(2,1)S(1)} %get-tuple-element.76), channel_id=1, source_target_pairs={{0,16},{8,24},{16,0},{24,8},{1,17},{9,25},{17,1},{25,9},{2,18},{10... | collective-permute-start | bytes 786440 | tf_op jit(solution)/shard_map/ppermute | solution.py:352
  103.4 17.0 %collective-permute-start.23 = (bf16[512,256]{1,0:T(8,128)(2,1)S(1)}, bf16[512,256]{1,0:T(8,128)(2,1)S(1)}, u32[]{:S(2)}, u32[]{:S(2)}) collective-permute-start(bf16[512,256]{1,0:T(8,128)(2,1)S(1)} %get-tuple-element.77), channel_id=1, source_target_pairs={{0,24},{8,16},{16,8},{24,0},{1,25},{9,17},{17,9},{25,1},{2,26},{10... | collective-permute-start | bytes 786440 | tf_op jit(solution)/shard_map/ppermute | solution.py:352
  113.6 30.7 %collective-permute-start.30 = (bf16[512,1024]{1,0:T(8,128)(2,1)S(1)}, bf16[512,1024]{1,0:T(8,128)(2,1)S(1)}, u32[]{:S(2)}, u32[]{:S(2)}) collective-permute-start(bf16[512,1024]{1,0:T(8,128)(2,1)S(1)} %added.7.refs_5_), channel_id=1, source_target_pairs={{2,4},{3,5},{4,2},{5,3},{10,12},{11,13},{12,10},{13,11},{18,20},{1... | collective-permute-start | bytes 3145736 | tf_op jit(solution)/shard_map/ppermute | solution.py:385
  114.9 29.4 %collective-permute-start.29 = (bf16[512,1024]{1,0:T(8,128)(2,1)S(1)}, bf16[512,1024]{1,0:T(8,128)(2,1)S(1)}, u32[]{:S(2)}, u32[]{:S(2)}) collective-permute-start(bf16[512,1024]{1,0:T(8,128)(2,1)S(1)} %added.6.refs_4_), channel_id=1, source_target_pairs={{2,0},{3,1},{4,6},{5,7},{0,2},{1,3},{6,4},{7,5},{10,8},{11,9},{12,... | collective-permute-start | bytes 3145736 | tf_op jit(solution)/shard_map/ppermute | solution.py:385
  131.0 13.3 %collective-permute-start.27 = (bf16[544,256]{1,0:T(8,128)(2,1)S(1)}, bf16[544,256]{1,0:T(8,128)(2,1)S(1)}, u32[]{:S(2)}, u32[]{:S(2)}) collective-permute-start(bf16[544,256]{1,0:T(8,128)(2,1)S(1)} %get-tuple-element.84), channel_id=1, source_target_pairs={{0,16},{8,24},{16,0},{24,8},{1,17},{9,25},{17,1},{25,9},{2,18},{10... | collective-permute-start | bytes 835592 | tf_op jit(solution)/shard_map/ppermute | solution.py:352
  132.4 11.9 %collective-permute-start.28 = (bf16[544,256]{1,0:T(8,128)(2,1)S(1)}, bf16[544,256]{1,0:T(8,128)(2,1)S(1)}, u32[]{:S(2)}, u32[]{:S(2)}) collective-permute-start(bf16[544,256]{1,0:T(8,128)(2,1)S(1)} %get-tuple-element.85), channel_id=1, source_target_pairs={{0,24},{8,16},{16,8},{24,0},{1,25},{9,17},{17,9},{25,1},{2,26},{10... | collective-permute-start | bytes 835592 | tf_op jit(solution)/shard_map/ppermute | solution.py:352
  (11 other events, 108.0 us)

commit v18 on v17

--- a/solution.py
+++ b/solution.py
@@ -196,7 +196,7 @@
         out_specs=[VMEM] * (members + 2),
         scratch_shapes=[pltpu.VMEM((members, channels, width), jnp.bfloat16)],
         compiler_params=pltpu.CompilerParams(vmem_limit_bytes=24 * 2**20),
-        cost_estimate=COST,
+        cost_estimate=pl.CostEstimate(flops=9*10**9, bytes_accessed=2**12, transcendentals=0),
         name="causal_conv",
     )(plan, *inputs, *after)
     return parts, turned, taps
@@ -714,10 +714,11 @@
     packed = prepare(who, key_gate, value_input, filter_taps, members, scale)
     input_parts = traded(packed, "ctx")
     conv_parts, turned, taps = convolve(plan, input_parts, length, per_group, (total,))
-    *conv_parts, near, cross = held_until([*conv_parts, near, cross], ())
+    conv_parts = traded(conv_parts, "ctx")
+    lags = lag_matrices(taps)
+    gated_out, convolved = gated(plan, conv_parts, query_gate, ())
+    near, cross = held_until([near, cross], (lags,))
     far, skip = hop(near, ACROSS), hop(cross, OUTWARD)
-    lags = lag_matrices(taps)
-    gated_out, convolved = gated(plan, traded(conv_parts, "ctx"), query_gate, (lags,))
 
     def product(first, count, other, more=(), after=(), tiles=1, widths=()):
         return column_products(
@@ -728,27 +729,25 @@
     given_far = product(FAR, 1, 1, tiles=2, widths=(3 * quarter, quarter))
     received = [swapped(part, "tp", 1) for part in given_far]
     (first,) = product(FAR, 1, 0, received, tiles=2)
-    far, skip = held_until([far, skip], (first,))
-    mixed = chosen(plan, far, first)
-    arrived = hop(mixed, OUTWARD + INWARD)
-    given_middle = product(MIDDLE, 1, 1, (), (mixed,), tiles=2, widths=(half, half))
+    one = hop(first, INWARD)
+    far, skip, near = held_until([far, skip, near], (first,))
+    last = hop(far, OUTWARD)
+    given_middle = product(MIDDLE, 1, 1, (), (far,), tiles=2, widths=(half, half))
     received = [swapped(part, "tp", 1) for part in given_middle]
     (second,) = product(MIDDLE, 1, 0, received, tiles=2)
     middle_block = added(cross, skip)
+    given_near, given_own = product(NEAR, 2, 1, (), (second,))
+    (one,) = held_until([one], (given_near,))
+    through = added(first, one)
+    two_a = hop(through, ACROSS)
+    (second,) = held_until([second], (one,))
+    two_b = hop(second, INWARD)
     blocks = [near, swapped(near, "tp", 1), middle_block]
-    total = cotangent_products(plan, 2 * NEAR, blocks, out_weight, total, after=(second,))
-    given_near, given_own = product(NEAR, 2, 1, (), (second,))
-    (arrived,) = held_until([arrived], (total, given_near))
-    through = added(first, arrived)
-    two_a = hop(through, ACROSS)
-    (second,) = held_until([second], (arrived,))
-    two_b = hop(second, INWARD)
-
-    far_block, far_other = both([chosen(plan, far, arrived, (through,))])
+    total = cotangent_products(plan, 2 * NEAR, blocks, out_weight, total, after=(through,))
+    last, middle_block = held_until([last, middle_block], (total,))
+    far_block, far_other = both([added(far, last)])
     blocks = [swapped(middle_block, "tp", 1), far_block]
-    total = cotangent_products(
-        plan, 2 * MIDDLE + 1, blocks, out_weight, total, after=(through,)
-    )
+    total = cotangent_products(plan, 2 * MIDDLE + 1, blocks, out_weight, total)
     received = [swapped(part, "tp", 1) for part in (given_near, given_own)]
     grad_query, *grad_parts = last_cotangents(
         plan, 2 * FAR + 1, far_other, out_weight, total, convolved, query_gate, members, received

time: 148 us -> 152 us (1.027)
  waiting for transfers between devices: 35.9 us -> 39.7 us
    ppermute x9 -> x10, waiting for transfers between devices: 8.75 us -> 20.5 us  [hop(): lax.ppermute(array, 'tp', [(2 * i + core, 2 * j + core) for i, j in pairs...]
    ppermute x22, waiting for transfers between devices: 27.1 us -> 19.2 us  [swapped(): return lax.ppermute(array, axis, [(i, i ^ step) for i in range(size)])]
    ppermute x9 -> x10, starting transfers between devices: 21.4 us -> 22.2 us  [hop(): lax.ppermute(array, 'tp', [(2 * i + core, 2 * j + core) for i, j in pairs...]
  transfers between devices with their start and end apart: 31 -> 32, of which waited for: 11 -> 12; matrix products, arithmetic and copies ran while one was open for 0% -> 0% of each run, Pallas kernels for 47% -> 45%
where the time goes in v18:
time: 152 us; the launch traced here: 151 us
  Pallas kernels  70.7 us (47%)
  starting transfers between devices  39.7 us (26%)
  waiting for transfers between devices  39.7 us (26%)
    pallas_call x6, Pallas kernels, column_products(): pl.pallas_call(functools.partial(product_kernel, steps, [part.shape[1] fo...  23.8 us
    ppermute x10, starting transfers between devices, hop(): lax.ppermute(array, 'tp', [(2 * i + core, 2 * j + core) for i, j in pairs...  22.2 us
    ppermute x10, waiting for transfers between devices, hop(): lax.ppermute(array, 'tp', [(2 * i + core, 2 * j + core) for i, j in pairs...  20.5 us
    ppermute x22, waiting for transfers between devices, swapped(): return lax.ppermute(array, axis, [(i, i ^ step) for i in range(size)])  19.2 us
    ppermute x22, starting transfers between devices, swapped(): return lax.ppermute(array, axis, [(i, i ^ step) for i in range(size)])  17.5 us
    pallas_call x3, Pallas kernels, cotangent_products(): pl.pallas_call(functools.partial(cotangent_kernel, count, begin), out_sha...  15.9 us
    pallas_call x1, Pallas kernels, correlate(): pl.pallas_call(functools.partial(backward_kernel, members, batch, per_gro...  8.93 us
    pallas_call x1, Pallas kernels, convolve(): pl.pallas_call(functools.partial(forward_kernel, members, per_group, widt...  4.89 us
  transfers between devices with their start and end apart: 32, of which 12 were waited for; matrix products, arithmetic and copies ran while one was open for 0% of the time, Pallas kernels for 45%

profile of v18, /device:TPU:0, one launch (start us, length us, event | category | flops | bytes accessed | tf_op | source)
XLA Modules:
  0.0 151.5 jit_solution(13704526660001688931)
XLA Ops:
  8.7 4.9 %collective-permute-start.4 = (bf16[512,1024]{1,0:T(8,128)(2,1)S(1)}, bf16[512,1024]{1,0:T(8,128)(2,1)S(1)}, u32[]{:S(2)}, u32[]{:S(2)}) collective-permute-start(bf16[512,1024]{1,0:T(8,128)(2,1)S(1)} %copy-done.3), channel_id=1, source_target_pairs={{0,2},{1,3},{6,4},{7,5},{2,0},{3,1},{4,6},{5,7},{8,10},{9,11},{14,... | collective-permute-start | bytes 3145736 | tf_op jit(solution)/shard_map/ppermute | solution.py:385
  14.7 4.8 %cotangent_blocks.3.refs_4_.refs_3_ = f32[512,1024]{1,0:T(8,128)S(1)} custom-call(s32[10]{0:T(128)S(1)} %plan.1._.plan_ref, bf16[1024,8192]{1,0:T(8,128)(2,1)} %weight_ref.19, bf16[512,1024]{1,0:T(8,128)(2,1)S(1)} %copy-done.3, bf16[512,1024]{1,0:T(8,128)(2,1)S(1)} %collective-permute-done.3.refs_1_), custom_call_target="tpu_custom_call" | custom-call | flops 1048576 | bytes 4096 | tf_op jit(solution)/shard_map/cotangent_blocks/pallas_call | solution.py:650
  21.2 4.9 %causal_conv.1 = (bf16[512,256]{1,0:T(8,128)(2,1)S(1)}, bf16[512,256]{1,0:T(8,128)(2,1)S(1)}, bf16[512,256]{1,0:T(8,128)(2,1)S(1)}, bf16[512,256]{1,0:T(8,128)(2...) custom-call(s32[10]{0:T(128)S(1)} %plan.1._.plan_ref, bf16[544,256]{1,0:T(8,128)(2,1)S(1)} %get-tuple-element.47.refs_0_, ...), custom_call_target="tpu_custom_call" | custom-call | flops 8999999488 | bytes 4096 | tf_op jit(solution)/shard_map/causal_conv/pallas_call | solution.py:188
  29.6 3.4 %lag_matrices.1.refs_2_.lag_ref = bf16[16,128,2048]{2,1,0:T(8,128)(2,1)S(1)} custom-call(f32[16,2048]{1,0:T(8,128)S(1)} %get-tuple-element.52.taps_ref), custom_call_target="tpu_custom_call" | custom-call | flops 1048576 | bytes 4096 | tf_op jit(solution)/shard_map/lag_matrices/pallas_call | solution.py:207
  33.1 3.2 %collective-permute-done.4.refs_0_ = bf16[512,1024]{1,0:T(8,128)(2,1)S(1)} collective-permute-done((bf16[512,1024]{1,0:T(8,128)(2,1)S(1)}, bf16[512,1024]{1,0:T(8,128)(2,1)S(1)}, u32[]{:S(2)}, u32[]{:S(2)}) %collective-permute-start.4) | collective-permute-done | bytes 1048608 | tf_op jit(solution)/shard_map/ppermute | solution.py:385
  41.5 3.4 %projection_blocks.6 = (bf16[512,768]{1,0:T(8,128)(2,1)S(1)}, bf16[512,256]{1,0:T(8,128)(2,1)S(1)}) custom-call(s32[10]{0:T(128)S(1)} %plan.1._.plan_ref, bf16[512,1024]{1,0:T(8,128)(2,1)S(1)} %get-tuple-element.59.data_ref, bf16[1024,8192]{1,0:T(8,128)(2,1)} %weight_ref.19), custom_call_target="tpu_custom_call" | custom-call | flops 1048576 | bytes 4096 | tf_op jit(solution)/shard_map/projection_blocks/pallas_call | solution.py:551
  47.6 3.5 %projection_blocks.7.refs_3_.refs_0_ = bf16[512,1024]{1,0:T(8,128)(2,1)S(1)} custom-call(s32[10]{0:T(128)S(1)} %plan.1._.plan_ref, bf16[512,1024]{1,0:T(8,128)(2,1)S(1)} %get-tuple-element.59.data_ref, bf16[1024,8192]{1,0:T(8,128)(2,1)} %weight_ref.19, bf16[512,768]{1,0:T(8,128)(2,1)S(1)} %collective-permute-done.11.refs_0_, ...), custom_call_target="tpu_custom_call" | custom-call | flops 1048576 | bytes 4096 | tf_op jit(solution)/shard_map/projection_blocks/pallas_call | solution.py:551
  51.1 3.5 %collective-permute-start.15 = (bf16[512,1024]{1,0:T(8,128)(2,1)S(1)}, bf16[512,1024]{1,0:T(8,128)(2,1)S(1)}, u32[]{:S(2)}, u32[]{:S(2)}) collective-permute-start(bf16[512,1024]{1,0:T(8,128)(2,1)S(1)} %projection_blocks.7.refs_3_.refs_0_), channel_id=1, source_target_pairs={{0,2},{1,3},{6,4},{7,5},{8,10},{9,11},{14,12},{15,13},{16,18},{17,... | collective-permute-start | bytes 3145736 | tf_op jit(solution)/shard_map/ppermute | solution.py:385
  54.7 8.5 %collective-permute-done.7.refs_1_ = bf16[512,1024]{1,0:T(8,128)(2,1)S(1)} collective-permute-done((bf16[512,1024]{1,0:T(8,128)(2,1)S(1)}, bf16[512,1024]{1,0:T(8,128)(2,1)S(1)}, u32[]{:S(2)}, u32[]{:S(2)}) %collective-permute-start.7) | collective-permute-done | bytes 1048608 | tf_op jit(solution)/shard_map/ppermute | solution.py:385
  64.6 3.4 %projection_blocks.8 = (bf16[512,512]{1,0:T(8,128)(2,1)S(1)}, bf16[512,512]{1,0:T(8,128)(2,1)S(1)}) custom-call(s32[10]{0:T(128)S(1)} %plan.1._.plan_ref, bf16[512,1024]{1,0:T(8,128)(2,1)S(1)} %get-tuple-element.59.data_ref, bf16[1024,8192]{1,0:T(8,128)(2,1)} %weight_ref.19, bf16[512,1024]{1,0:T(8,128)(2,1)S(1)} %get-tuple-element.62.refs_0_), custom_call_target="tpu_custom_call" | custom-call | flops 1048576 | bytes 4096 | tf_op jit(solution)/shard_map/projection_blocks/pallas_call | solution.py:551
  70.9 3.5 %projection_blocks.9.refs_0_ = bf16[512,1024]{1,0:T(8,128)(2,1)S(1)} custom-call(s32[10]{0:T(128)S(1)} %plan.1._.plan_ref, bf16[512,1024]{1,0:T(8,128)(2,1)S(1)} %get-tuple-element.59.data_ref, bf16[1024,8192]{1,0:T(8,128)(2,1)} %weight_ref.19, bf16[512,512]{1,0:T(8,128)(2,1)S(1)} %collective-permute-done.16.refs_0_, ...), custom_call_target="tpu_custom_call" | custom-call | flops 1048576 | bytes 4096 | tf_op jit(solution)/shard_map/projection_blocks/pallas_call | solution.py:551
  74.4 4.9 %projection_blocks.10 = (bf16[512,1024]{1,0:T(8,128)(2,1)S(1)}, bf16[512,1024]{1,0:T(8,128)(2,1)S(1)}) custom-call(s32[10]{0:T(128)S(1)} %plan.1._.plan_ref, bf16[512,1024]{1,0:T(8,128)(2,1)S(1)} %get-tuple-element.59.data_ref, bf16[1024,8192]{1,0:T(8,128)(2,1)} %weight_ref.19, bf16[512,1024]{1,0:T(8,128)(2,1)S(1)} %projection_blocks.9.refs_0_), custom_call_target="tpu_custom_call" | custom-call | flops 1048576 | bytes 4096 | tf_op jit(solution)/shard_map/projection_blocks/pallas_call | solution.py:551
  79.6 6.4 %cotangent_blocks.4.refs_2_ = f32[512,1024]{1,0:T(8,128)S(1)} custom-call(s32[10]{0:T(128)S(1)} %plan.1._.plan_ref, bf16[1024,8192]{1,0:T(8,128)(2,1)} %weight_ref.19, bf16[512,1024]{1,0:T(8,128)(2,1)S(1)} %get-tuple-element.64.refs_0_, bf16[512,1024]{1,0:T(8,128)(2,1)S(1)} %collective-permute-done.14.refs_1_, bf16[512,1024]{1,0:T(8,128)(2,1)S(1)} %added.5.refs_2_.refs_1_, ...), custom_call_target="tpu_custom_call" | custom-call | flops 1048576 | bytes 4096 | tf_op jit(solution)/shard_map/cotangent_blocks/pallas_call | solution.py:650
  86.0 4.6 %collective-permute-done.13.refs_0_ = bf16[512,1024]{1,0:T(8,128)(2,1)S(1)} collective-permute-done((bf16[512,1024]{1,0:T(8,128)(2,1)S(1)}, bf16[512,1024]{1,0:T(8,128)(2,1)S(1)}, u32[]{:S(2)}, u32[]{:S(2)}) %collective-permute-start.13) | collective-permute-done | bytes 1048608 | tf_op jit(solution)/shard_map/ppermute | solution.py:385
  93.3 3.7 %collective-permute-start.26 = (bf16[512,1024]{1,0:T(8,128)(2,1)S(1)}, bf16[512,1024]{1,0:T(8,128)(2,1)S(1)}, u32[]{:S(2)}, u32[]{:S(2)}) collective-permute-start(bf16[512,1024]{1,0:T(8,128)(2,1)S(1)} %held.10.refs_0_), channel_id=1, source_target_pairs={{0,2},{1,3},{6,4},{7,5},{8,10},{9,11},{14,12},{15,13},{16,18},{17,... | collective-permute-start | bytes 3145736 | tf_op jit(solution)/shard_map/ppermute | solution.py:385
  97.0 4.8 %cotangent_blocks.5.start_ref = f32[512,1024]{1,0:T(8,128)S(1)} custom-call(s32[10]{0:T(128)S(1)} %plan.1._.plan_ref, bf16[1024,8192]{1,0:T(8,128)(2,1)} %weight_ref.19, bf16[512,1024]{1,0:T(8,128)(2,1)S(1)} %collective-permute-done.19.refs_0_, bf16[512,1024]{1,0:T(8,128)(2,1)S(1)} %added.7.refs_1_, f32[512,1024]{1,0:T(8,128)S(1)} %cotangent_blocks.4.refs_2_), custom_call_target="tpu_custom_call" | custom-call | flops 1048576 | bytes 4096 | tf_op jit(solution)/shard_map/cotangent_blocks/pallas_call | solution.py:650
  101.8 4.5 %cotangent_last.1 = (bf16[512,1024]{1,0:T(8,128)(2,1)}, bf16[512,256]{1,0:T(8,128)(2,1)S(1)}, bf16[512,256]{1,0:T(8,128)(2,1)S(1)}, bf16[512,256]{1,0:T(8,128)(2,1)S(1)}, bf16[512,256]{1,0:T(8,128)(2,1)S(1)}) custom-call(s32[10]{0:T(128)S(1)} %plan.1._.plan_ref, bf16[1024,8192]{1,0:T(8,128)(2,1)} %weight_ref.19, ...), custom_call_target="tpu_custom_call" | custom-call | flops 1048576 | bytes 4096 | tf_op jit(solution)/shard_map/cotangent_last/pallas_call | solution.py:616
  109.8 5.1 %projection_blocks.11 = (bf16[512,1024]{1,0:T(8,128)(2,1)S(1)}, bf16[512,1024]{1,0:T(8,128)(2,1)S(1)}) custom-call(s32[10]{0:T(128)S(1)} %plan.1._.plan_ref, bf16[512,1024]{1,0:T(8,128)(2,1)S(1)} %get-tuple-element.59.data_ref, bf16[1024,8192]{1,0:T(8,128)(2,1)} %weight_ref.19, bf16[512,1024]{1,0:T(8,128)(2,1)S(1)} %collective-permute-done.20.refs_0_, ...), custom_call_target="tpu_custom_call" | custom-call | flops 1048576 | bytes 4096 | tf_op jit(solution)/shard_map/projection_blocks/pallas_call | solution.py:551
  115.0 4.3 %collective-permute-done.26.refs_1_ = bf16[512,1024]{1,0:T(8,128)(2,1)S(1)} collective-permute-done((bf16[512,1024]{1,0:T(8,128)(2,1)S(1)}, bf16[512,1024]{1,0:T(8,128)(2,1)S(1)}, u32[]{:S(2)}, u32[]{:S(2)}) %collective-permute-start.26) | collective-permute-done | bytes 1048608 | tf_op jit(solution)/shard_map/ppermute | solution.py:385
  120.8 4.2 %collective-permute-start.30 = (bf16[512,1024]{1,0:T(8,128)(2,1)S(1)}, bf16[512,1024]{1,0:T(8,128)(2,1)S(1)}, u32[]{:S(2)}, u32[]{:S(2)}) collective-permute-start(bf16[512,1024]{1,0:T(8,128)(2,1)S(1)} %added.8.refs_4_), channel_id=1, source_target_pairs={{2,0},{3,1},{4,6},{5,7},{0,2},{1,3},{6,4},{7,5},{10,8},{11,9},{12,... | collective-permute-start | bytes 3145736 | tf_op jit(solution)/shard_map/ppermute | solution.py:385
  125.1 8.9 %causal_conv_grads.1 = (bf16[544,256]{1,0:T(8,128)(2,1)S(1)}, bf16[544,256]{1,0:T(8,128)(2,1)S(1)}, bf16[544,256]{1,0:T(8,128)(2,1)S(1)}, bf16[544,256]{1,0:T(8,128)(2,1)S(1)}) custom-call(s32[10]{0:T(128)S(1)} %plan.1._.plan_ref, bf16[4,256,512]{2,1,0:T(8,128)(2,1)S(1)} %get-tuple-element.51.in_scr, bf16[16,128,2048]{2,1,0:T(8,128)(2,1)S(1)} %lag_matrices.1.refs_2_.lag_ref, ...), custom_call_target="tpu_custom_call" | custom-call | flops 10000000000 | bytes 4096 | tf_op jit(solution)/shard_map/causal_conv_grads/pallas_call | solution.py:226
  137.6 6.1 %collective-permute-done.27.refs_1_ = bf16[544,256]{1,0:T(8,128)(2,1)S(1)} collective-permute-done((bf16[544,256]{1,0:T(8,128)(2,1)S(1)}, bf16[544,256]{1,0:T(8,128)(2,1)S(1)}, u32[]{:S(2)}, u32[]{:S(2)}) %collective-permute-start.27) | collective-permute-done | bytes 278560 | tf_op jit(solution)/shard_map/ppermute | solution.py:352
  143.7 4.4 %collective-permute-done.28.refs_2_ = bf16[544,256]{1,0:T(8,128)(2,1)S(1)} collective-permute-done((bf16[544,256]{1,0:T(8,128)(2,1)S(1)}, bf16[544,256]{1,0:T(8,128)(2,1)S(1)}, u32[]{:S(2)}, u32[]{:S(2)}) %collective-permute-start.28) | collective-permute-done | bytes 278560 | tf_op jit(solution)/shard_map/ppermute | solution.py:352
  148.1 3.2 %input_gradients.1 = (bf16[512,1024]{1,0:T(8,128)(2,1)}, bf16[512,1024]{1,0:T(8,128)(2,1)}, bf16[512,1024]{1,0:T(8,128)(2,1)}, f32[64,512]{1,0:T(8,128)}) custom-call(s32[10]{0:T(128)S(1)} %plan.1._.plan_ref, bf16[544,256]{1,0:T(8,128)(2,1)S(1)} %get-tuple-element.80.refs_0_, bf16[544,256]{1,0:T(8,128)(2,1)S(1)} %collective-permute-done.27.refs_1_, ...), custom_call_target="tpu_custom_call" | custom-call | flops 1048576 | bytes 4096 | tf_op jit(solution)/shard_map/input_gradients/pallas_call | solution.py:334
  (77 shorter events, 38.3 us)
Async XLA Ops:
  3.9 15.6 %collective-permute-start = (bf16[544,256]{1,0:T(8,128)(2,1)S(1)}, bf16[544,256]{1,0:T(8,128)(2,1)S(1)}, u32[]{:S(2)}, u32[]{:S(2)}) collective-permute-start(bf16[544,256]{1,0:T(8,128)(2,1)S(1)} %get-tuple-element.48), channel_id=1, source_target_pairs={{0,8},{8,0},{16,24},{24,16},{1,9},{9,1},{17,25},{25,17},{2,10},{10... | collective-permute-start | bytes 835592 | tf_op jit(solution)/shard_map/ppermute | solution.py:352
  6.4 14.7 %collective-permute-start.1 = (bf16[544,256]{1,0:T(8,128)(2,1)S(1)}, bf16[544,256]{1,0:T(8,128)(2,1)S(1)}, u32[]{:S(2)}, u32[]{:S(2)}) collective-permute-start(bf16[544,256]{1,0:T(8,128)(2,1)S(1)} %get-tuple-element.49), channel_id=1, source_target_pairs={{0,16},{8,24},{16,0},{24,8},{1,17},{9,25},{17,1},{25,9},{2,18},{10... | collective-permute-start | bytes 835592 | tf_op jit(solution)/shard_map/ppermute | solution.py:352
  8.0 13.2 %collective-permute-start.2 = (bf16[544,256]{1,0:T(8,128)(2,1)S(1)}, bf16[544,256]{1,0:T(8,128)(2,1)S(1)}, u32[]{:S(2)}, u32[]{:S(2)}) collective-permute-start(bf16[544,256]{1,0:T(8,128)(2,1)S(1)} %get-tuple-element.50), channel_id=1, source_target_pairs={{0,24},{8,16},{16,8},{24,0},{1,25},{9,17},{17,9},{25,1},{2,26},{10... | collective-permute-start | bytes 835592 | tf_op jit(solution)/shard_map/ppermute | solution.py:352
  8.0 25.1 %collective-permute-start.5 = (bf16[512,1024]{1,0:T(8,128)(2,1)S(1)}, bf16[512,1024]{1,0:T(8,128)(2,1)S(1)}, u32[]{:S(2)}, u32[]{:S(2)}) collective-permute-start(bf16[512,1024]{1,0:T(8,128)(2,1)S(1)} %copy-done.3), channel_id=1, source_target_pairs={{2,4},{3,5},{4,2},{5,3},{10,12},{11,13},{12,10},{13,11},{18,20},{1... | collective-permute-start | bytes 3145736 | tf_op jit(solution)/shard_map/ppermute | solution.py:385
  8.7 27.5 %collective-permute-start.4 = (bf16[512,1024]{1,0:T(8,128)(2,1)S(1)}, bf16[512,1024]{1,0:T(8,128)(2,1)S(1)}, u32[]{:S(2)}, u32[]{:S(2)}) collective-permute-start(bf16[512,1024]{1,0:T(8,128)(2,1)S(1)} %copy-done.3), channel_id=1, source_target_pairs={{0,2},{1,3},{6,4},{7,5},{2,0},{3,1},{4,6},{5,7},{8,10},{9,11},{14,... | collective-permute-start | bytes 3145736 | tf_op jit(solution)/shard_map/ppermute | solution.py:385
  26.1 12.2 %collective-permute-start.8 = (bf16[512,256]{1,0:T(8,128)(2,1)S(1)}, bf16[512,256]{1,0:T(8,128)(2,1)S(1)}, u32[]{:S(2)}, u32[]{:S(2)}) collective-permute-start(bf16[512,256]{1,0:T(8,128)(2,1)S(1)} %get-tuple-element.56), channel_id=1, source_target_pairs={{0,8},{8,0},{16,24},{24,16},{1,9},{9,1},{17,25},{25,17},{2,10},{10... | collective-permute-start | bytes 786440 | tf_op jit(solution)/shard_map/ppermute | solution.py:352
  27.4 13.3 %collective-permute-start.9 = (bf16[512,256]{1,0:T(8,128)(2,1)S(1)}, bf16[512,256]{1,0:T(8,128)(2,1)S(1)}, u32[]{:S(2)}, u32[]{:S(2)}) collective-permute-start(bf16[512,256]{1,0:T(8,128)(2,1)S(1)} %get-tuple-element.57), channel_id=1, source_target_pairs={{0,16},{8,24},{16,0},{24,8},{1,17},{9,25},{17,1},{25,9},{2,18},{10... | collective-permute-start | bytes 786440 | tf_op jit(solution)/shard_map/ppermute | solution.py:352
  28.2 12.4 %collective-permute-start.10 = (bf16[512,256]{1,0:T(8,128)(2,1)S(1)}, bf16[512,256]{1,0:T(8,128)(2,1)S(1)}, u32[]{:S(2)}, u32[]{:S(2)}) collective-permute-start(bf16[512,256]{1,0:T(8,128)(2,1)S(1)} %get-tuple-element.58), channel_id=1, source_target_pairs={{0,24},{8,16},{16,8},{24,0},{1,25},{9,17},{17,9},{25,1},{2,26},{10... | collective-permute-start | bytes 786440 | tf_op jit(solution)/shard_map/ppermute | solution.py:352
  36.3 18.4 %collective-permute-start.6 = (bf16[512,1024]{1,0:T(8,128)(2,1)S(1)}, bf16[512,1024]{1,0:T(8,128)(2,1)S(1)}, u32[]{:S(2)}, u32[]{:S(2)}) collective-permute-start(bf16[512,1024]{1,0:T(8,128)(2,1)S(1)} %get-tuple-element.53.refs_2_), channel_id=1, source_target_pairs={{2,4},{3,5},{4,2},{5,3},{10,12},{11,13},{12,10},{13,11},{18,20},{1... | collective-permute-start | bytes 3145736 | tf_op jit(solution)/shard_map/ppermute | solution.py:385
  37.0 26.2 %collective-permute-start.7 = (bf16[512,1024]{1,0:T(8,128)(2,1)S(1)}, bf16[512,1024]{1,0:T(8,128)(2,1)S(1)}, u32[]{:S(2)}, u32[]{:S(2)}) collective-permute-start(bf16[512,1024]{1,0:T(8,128)(2,1)S(1)} %get-tuple-element.54.refs_0_), channel_id=1, source_target_pairs={{2,0},{3,1},{4,6},{5,7},{10,8},{11,9},{12,14},{13,15},{18,16},{19,... | collective-permute-start | bytes 3145736 | tf_op jit(solution)/shard_map/ppermute | solution.py:385
  51.1 28.1 %collective-permute-start.15 = (bf16[512,1024]{1,0:T(8,128)(2,1)S(1)}, bf16[512,1024]{1,0:T(8,128)(2,1)S(1)}, u32[]{:S(2)}, u32[]{:S(2)}) collective-permute-start(bf16[512,1024]{1,0:T(8,128)(2,1)S(1)} %projection_blocks.7.refs_3_.refs_0_), channel_id=1, source_target_pairs={{0,2},{1,3},{6,4},{7,5},{8,10},{9,11},{14,12},{15,13},{16,18},{17,... | collective-permute-start | bytes 3145736 | tf_op jit(solution)/shard_map/ppermute | solution.py:385
  63.2 16.4 %collective-permute-start.14 = (bf16[512,1024]{1,0:T(8,128)(2,1)S(1)}, bf16[512,1024]{1,0:T(8,128)(2,1)S(1)}, u32[]{:S(2)}, u32[]{:S(2)}) collective-permute-start(bf16[512,1024]{1,0:T(8,128)(2,1)S(1)} %get-tuple-element.64.refs_0_), channel_id=1, source_target_pairs={{0,1},{1,0},{2,3},{3,2},{4,5},{5,4},{6,7},{7,6},{8,9},{9,8},{10,11... | collective-permute-start | bytes 3145736 | tf_op jit(solution)/shard_map/ppermute | solution.py:352
  63.2 27.5 %collective-permute-start.13 = (bf16[512,1024]{1,0:T(8,128)(2,1)S(1)}, bf16[512,1024]{1,0:T(8,128)(2,1)S(1)}, u32[]{:S(2)}, u32[]{:S(2)}) collective-permute-start(bf16[512,1024]{1,0:T(8,128)(2,1)S(1)} %get-tuple-element.62.refs_0_), channel_id=1, source_target_pairs={{2,0},{3,1},{4,6},{5,7},{10,8},{11,9},{12,14},{13,15},{18,16},{19,... | collective-permute-start | bytes 3145736 | tf_op jit(solution)/shard_map/ppermute | solution.py:385
  90.6 11.2 %collective-permute-start.20 = (bf16[512,1024]{1,0:T(8,128)(2,1)S(1)}, bf16[512,1024]{1,0:T(8,128)(2,1)S(1)}, u32[]{:S(2)}, u32[]{:S(2)}) collective-permute-start(bf16[512,1024]{1,0:T(8,128)(2,1)S(1)} %get-tuple-element.67.refs_1_), channel_id=1, source_target_pairs={{0,1},{1,0},{2,3},{3,2},{4,5},{5,4},{6,7},{7,6},{8,9},{9,8},{10,11... | collective-permute-start | bytes 3145736 | tf_op jit(solution)/shard_map/ppermute | solution.py:352
  91.1 10.7 %collective-permute-start.21 = (bf16[512,1024]{1,0:T(8,128)(2,1)S(1)}, bf16[512,1024]{1,0:T(8,128)(2,1)S(1)}, u32[]{:S(2)}, u32[]{:S(2)}) collective-permute-start(bf16[512,1024]{1,0:T(8,128)(2,1)S(1)} %get-tuple-element.71), channel_id=1, source_target_pairs={{0,1},{1,0},{2,3},{3,2},{4,5},{5,4},{6,7},{7,6},{8,9},{9,8},{10,11... | collective-permute-start | bytes 3145736 | tf_op jit(solution)/shard_map/ppermute | solution.py:352
  92.0 23.0 %collective-permute-start.25 = (bf16[512,1024]{1,0:T(8,128)(2,1)S(1)}, bf16[512,1024]{1,0:T(8,128)(2,1)S(1)}, u32[]{:S(2)}, u32[]{:S(2)}) collective-permute-start(bf16[512,1024]{1,0:T(8,128)(2,1)S(1)} %added.6.refs_4_), channel_id=1, source_target_pairs={{2,4},{3,5},{4,2},{5,3},{10,12},{11,13},{12,10},{13,11},{18,20},{1... | collective-permute-start | bytes 3145736 | tf_op jit(solution)/shard_map/ppermute | solution.py:385
  93.3 26.0 %collective-permute-start.26 = (bf16[512,1024]{1,0:T(8,128)(2,1)S(1)}, bf16[512,1024]{1,0:T(8,128)(2,1)S(1)}, u32[]{:S(2)}, u32[]{:S(2)}) collective-permute-start(bf16[512,1024]{1,0:T(8,128)(2,1)S(1)} %held.10.refs_0_), channel_id=1, source_target_pairs={{0,2},{1,3},{6,4},{7,5},{8,10},{9,11},{14,12},{15,13},{16,18},{17,... | collective-permute-start | bytes 3145736 | tf_op jit(solution)/shard_map/ppermute | solution.py:385
  106.3 18.7 %collective-permute-start.22 = (bf16[512,256]{1,0:T(8,128)(2,1)S(1)}, bf16[512,256]{1,0:T(8,128)(2,1)S(1)}, u32[]{:S(2)}, u32[]{:S(2)}) collective-permute-start(bf16[512,256]{1,0:T(8,128)(2,1)S(1)} %get-tuple-element.73), channel_id=1, source_target_pairs={{0,8},{8,0},{16,24},{24,16},{1,9},{9,1},{17,25},{25,17},{2,10},{10... | collective-permute-start | bytes 786440 | tf_op jit(solution)/shard_map/ppermute | solution.py:352
  107.8 17.2 %collective-permute-start.23 = (bf16[512,256]{1,0:T(8,128)(2,1)S(1)}, bf16[512,256]{1,0:T(8,128)(2,1)S(1)}, u32[]{:S(2)}, u32[]{:S(2)}) collective-permute-start(bf16[512,256]{1,0:T(8,128)(2,1)S(1)} %get-tuple-element.74), channel_id=1, source_target_pairs={{0,16},{8,24},{16,0},{24,8},{1,17},{9,25},{17,1},{25,9},{2,18},{10... | collective-permute-start | bytes 786440 | tf_op jit(solution)/shard_map/ppermute | solution.py:352
  109.3 15.7 %collective-permute-start.24 = (bf16[512,256]{1,0:T(8,128)(2,1)S(1)}, bf16[512,256]{1,0:T(8,128)(2,1)S(1)}, u32[]{:S(2)}, u32[]{:S(2)}) collective-permute-start(bf16[512,256]{1,0:T(8,128)(2,1)S(1)} %get-tuple-element.75), channel_id=1, source_target_pairs={{0,24},{8,16},{16,8},{24,0},{1,25},{9,17},{17,9},{25,1},{2,26},{10... | collective-permute-start | bytes 786440 | tf_op jit(solution)/shard_map/ppermute | solution.py:352
  119.5 28.6 %collective-permute-start.31 = (bf16[512,1024]{1,0:T(8,128)(2,1)S(1)}, bf16[512,1024]{1,0:T(8,128)(2,1)S(1)}, u32[]{:S(2)}, u32[]{:S(2)}) collective-permute-start(bf16[512,1024]{1,0:T(8,128)(2,1)S(1)} %added.9.refs_5_), channel_id=1, source_target_pairs={{2,4},{3,5},{4,2},{5,3},{10,12},{11,13},{12,10},{13,11},{18,20},{1... | collective-permute-start | bytes 3145736 | tf_op jit(solution)/shard_map/ppermute | solution.py:385
  120.8 27.3 %collective-permute-start.30 = (bf16[512,1024]{1,0:T(8,128)(2,1)S(1)}, bf16[512,1024]{1,0:T(8,128)(2,1)S(1)}, u32[]{:S(2)}, u32[]{:S(2)}) collective-permute-start(bf16[512,1024]{1,0:T(8,128)(2,1)S(1)} %added.8.refs_4_), channel_id=1, source_target_pairs={{2,0},{3,1},{4,6},{5,7},{0,2},{1,3},{6,4},{7,5},{10,8},{11,9},{12,... | collective-permute-start | bytes 3145736 | tf_op jit(solution)/shard_map/ppermute | solution.py:385
  135.6 12.5 %collective-permute-start.28 = (bf16[544,256]{1,0:T(8,128)(2,1)S(1)}, bf16[544,256]{1,0:T(8,128)(2,1)S(1)}, u32[]{:S(2)}, u32[]{:S(2)}) collective-permute-start(bf16[544,256]{1,0:T(8,128)(2,1)S(1)} %get-tuple-element.82), channel_id=1, source_target_pairs={{0,16},{8,24},{16,0},{24,8},{1,17},{9,25},{17,1},{25,9},{2,18},{10... | collective-permute-start | bytes 835592 | tf_op jit(solution)/shard_map/ppermute | solution.py:352
  137.1 11.0 %collective-permute-start.29 = (bf16[544,256]{1,0:T(8,128)(2,1)S(1)}, bf16[544,256]{1,0:T(8,128)(2,1)S(1)}, u32[]{:S(2)}, u32[]{:S(2)}) collective-permute-start(bf16[544,256]{1,0:T(8,128)(2,1)S(1)} %get-tuple-element.83), channel_id=1, source_target_pairs={{0,24},{8,16},{16,8},{24,0},{1,25},{9,17},{17,9},{25,1},{2,26},{10... | collective-permute-start | bytes 835592 | tf_op jit(solution)/shard_map/ppermute | solution.py:352
  (12 other events, 101.6 us)

commit v19 on v18

--- a/solution.py
+++ b/solution.py
@@ -717,8 +717,10 @@
     conv_parts = traded(conv_parts, "ctx")
     lags = lag_matrices(taps)
     gated_out, convolved = gated(plan, conv_parts, query_gate, ())
-    near, cross = held_until([near, cross], (lags,))
-    far, skip = hop(near, ACROSS), hop(cross, OUTWARD)
+    (near,) = held_until([near], (lags,))
+    far = hop(near, ACROSS)
+    (cross,) = held_until([cross], (near,))
+    skip = hop(cross, OUTWARD)
 
     def product(first, count, other, more=(), after=(), tiles=1, widths=()):
         return column_products(
@@ -743,8 +745,8 @@
     (second,) = held_until([second], (one,))
     two_b = hop(second, INWARD)
     blocks = [near, swapped(near, "tp", 1), middle_block]
-    total = cotangent_products(plan, 2 * NEAR, blocks, out_weight, total, after=(through,))
-    last, middle_block = held_until([last, middle_block], (total,))
+    total = cotangent_products(plan, 2 * NEAR, blocks, out_weight, total)
+    last, middle_block = held_until([last, middle_block], (through, total))
     far_block, far_other = both([added(far, last)])
     blocks = [swapped(middle_block, "tp", 1), far_block]
     total = cotangent_products(plan, 2 * MIDDLE + 1, blocks, out_weight, total)

time: 152 us -> 151 us (level)
  starting transfers between devices: 39.7 us -> 37.6 us
    ppermute x22, waiting for transfers between devices: 19.2 us -> 25.1 us  [swapped(): return lax.ppermute(array, axis, [(i, i ^ step) for i in range(size)])]
    ppermute x10, waiting for transfers between devices: 20.5 us -> 16.1 us  [hop(): lax.ppermute(array, 'tp', [(2 * i + core, 2 * j + core) for i, j in pairs...]
    ppermute x10, starting transfers between devices: 22.2 us -> 20.1 us  [hop(): lax.ppermute(array, 'tp', [(2 * i + core, 2 * j + core) for i, j in pairs...]
  transfers between devices with their start and end apart: 32 -> 32, of which waited for: 12 -> 13; matrix products, arithmetic and copies ran while one was open for 0% -> 0% of each run, Pallas kernels for 45% -> 45%
where the time goes in v19:
time: 151 us
  Pallas kernels  70.7 us (47%)
  waiting for transfers between devices  41.2 us (27%)
  starting transfers between devices  37.6 us (25%)
    ppermute x22, waiting for transfers between devices, swapped(): return lax.ppermute(array, axis, [(i, i ^ step) for i in range(size)])  25.1 us
    pallas_call x6, Pallas kernels, column_products(): pl.pallas_call(functools.partial(product_kernel, steps, [part.shape[1] fo...  23.8 us
    ppermute x10, starting transfers between devices, hop(): lax.ppermute(array, 'tp', [(2 * i + core, 2 * j + core) for i, j in pairs...  20.1 us
    ppermute x22, starting transfers between devices, swapped(): return lax.ppermute(array, axis, [(i, i ^ step) for i in range(size)])  17.5 us
    ppermute x10, waiting for transfers between devices, hop(): lax.ppermute(array, 'tp', [(2 * i + core, 2 * j + core) for i, j in pairs...  16.1 us
    pallas_call x3, Pallas kernels, cotangent_products(): pl.pallas_call(functools.partial(cotangent_kernel, count, begin), out_sha...  15.9 us
    pallas_call x1, Pallas kernels, correlate(): pl.pallas_call(functools.partial(backward_kernel, members, batch, per_gro...  8.92 us
    pallas_call x1, Pallas kernels, convolve(): pl.pallas_call(functools.partial(forward_kernel, members, per_group, widt...  4.89 us
  transfers between devices with their start and end apart: 32, of which 13 were waited for; matrix products, arithmetic and copies ran while one was open for 0% of the time, Pallas kernels for 45%

profile of v19, /device:TPU:0, one launch (start us, length us, event | category | flops | bytes accessed | tf_op | source)
XLA Modules:
  0.0 150.8 jit_solution(9663244336263829303)
XLA Ops:
  11.9 4.8 %cotangent_blocks.3.refs_4_.refs_3_ = f32[512,1024]{1,0:T(8,128)S(1)} custom-call(s32[10]{0:T(128)S(1)} %plan.1._.plan_ref, bf16[1024,8192]{1,0:T(8,128)(2,1)} %weight_ref.19, bf16[512,1024]{1,0:T(8,128)(2,1)S(1)} %copy-done.3, bf16[512,1024]{1,0:T(8,128)(2,1)S(1)} %collective-permute-done.3.refs_1_), custom_call_target="tpu_custom_call" | custom-call | flops 1048576 | bytes 4096 | tf_op jit(solution)/shard_map/cotangent_blocks/pallas_call | solution.py:650
  16.7 4.5 %collective-permute-done.1.refs_2_ = bf16[544,256]{1,0:T(8,128)(2,1)S(1)} collective-permute-done((bf16[544,256]{1,0:T(8,128)(2,1)S(1)}, bf16[544,256]{1,0:T(8,128)(2,1)S(1)}, u32[]{:S(2)}, u32[]{:S(2)}) %collective-permute-start.1) | collective-permute-done | bytes 278560 | tf_op jit(solution)/shard_map/ppermute | solution.py:352
  21.2 4.9 %causal_conv.1 = (bf16[512,256]{1,0:T(8,128)(2,1)S(1)}, bf16[512,256]{1,0:T(8,128)(2,1)S(1)}, bf16[512,256]{1,0:T(8,128)(2,1)S(1)}, bf16[512,256]{1,0:T(8,128)(2...) custom-call(s32[10]{0:T(128)S(1)} %plan.1._.plan_ref, bf16[544,256]{1,0:T(8,128)(2,1)S(1)} %get-tuple-element.45.refs_0_, ...), custom_call_target="tpu_custom_call" | custom-call | flops 8999999488 | bytes 4096 | tf_op jit(solution)/shard_map/causal_conv/pallas_call | solution.py:188
  29.6 3.4 %lag_matrices.1.refs_1_.lag_ref = bf16[16,128,2048]{2,1,0:T(8,128)(2,1)S(1)} custom-call(f32[16,2048]{1,0:T(8,128)S(1)} %get-tuple-element.50.taps_ref), custom_call_target="tpu_custom_call" | custom-call | flops 1048576 | bytes 4096 | tf_op jit(solution)/shard_map/lag_matrices/pallas_call | solution.py:207
  35.4 5.2 %collective-permute-done.9.refs_2_ = bf16[512,256]{1,0:T(8,128)(2,1)S(1)} collective-permute-done((bf16[512,256]{1,0:T(8,128)(2,1)S(1)}, bf16[512,256]{1,0:T(8,128)(2,1)S(1)}, u32[]{:S(2)}, u32[]{:S(2)}) %collective-permute-start.9) | collective-permute-done | bytes 262176 | tf_op jit(solution)/shard_map/ppermute | solution.py:352
  41.5 3.4 %projection_blocks.6 = (bf16[512,768]{1,0:T(8,128)(2,1)S(1)}, bf16[512,256]{1,0:T(8,128)(2,1)S(1)}) custom-call(s32[10]{0:T(128)S(1)} %plan.1._.plan_ref, bf16[512,1024]{1,0:T(8,128)(2,1)S(1)} %get-tuple-element.55.data_ref, bf16[1024,8192]{1,0:T(8,128)(2,1)} %weight_ref.19), custom_call_target="tpu_custom_call" | custom-call | flops 1048576 | bytes 4096 | tf_op jit(solution)/shard_map/projection_blocks/pallas_call | solution.py:551
  47.6 3.5 %projection_blocks.7.refs_3_.refs_0_ = bf16[512,1024]{1,0:T(8,128)(2,1)S(1)} custom-call(s32[10]{0:T(128)S(1)} %plan.1._.plan_ref, bf16[512,1024]{1,0:T(8,128)(2,1)S(1)} %get-tuple-element.55.data_ref, bf16[1024,8192]{1,0:T(8,128)(2,1)} %weight_ref.19, bf16[512,768]{1,0:T(8,128)(2,1)S(1)} %collective-permute-done.11.refs_0_, ...), custom_call_target="tpu_custom_call" | custom-call | flops 1048576 | bytes 4096 | tf_op jit(solution)/shard_map/projection_blocks/pallas_call | solution.py:551
  51.1 4.1 %collective-permute-start.14 = (bf16[512,1024]{1,0:T(8,128)(2,1)S(1)}, bf16[512,1024]{1,0:T(8,128)(2,1)S(1)}, u32[]{:S(2)}, u32[]{:S(2)}) collective-permute-start(bf16[512,1024]{1,0:T(8,128)(2,1)S(1)} %projection_blocks.7.refs_3_.refs_0_), channel_id=1, source_target_pairs={{0,2},{1,3},{6,4},{7,5},{8,10},{9,11},{14,12},{15,13},{16,18},{17,... | collective-permute-start | bytes 3145736 | tf_op jit(solution)/shard_map/ppermute | solution.py:385
  55.3 5.8 %collective-permute-done.7.refs_1_ = bf16[512,1024]{1,0:T(8,128)(2,1)S(1)} collective-permute-done((bf16[512,1024]{1,0:T(8,128)(2,1)S(1)}, bf16[512,1024]{1,0:T(8,128)(2,1)S(1)}, u32[]{:S(2)}, u32[]{:S(2)}) %collective-permute-start.7) | collective-permute-done | bytes 1048608 | tf_op jit(solution)/shard_map/ppermute | solution.py:385
  62.6 3.4 %projection_blocks.8 = (bf16[512,512]{1,0:T(8,128)(2,1)S(1)}, bf16[512,512]{1,0:T(8,128)(2,1)S(1)}) custom-call(s32[10]{0:T(128)S(1)} %plan.1._.plan_ref, bf16[512,1024]{1,0:T(8,128)(2,1)S(1)} %get-tuple-element.55.data_ref, bf16[1024,8192]{1,0:T(8,128)(2,1)} %weight_ref.19, bf16[512,1024]{1,0:T(8,128)(2,1)S(1)} %get-tuple-element.58.refs_0_), custom_call_target="tpu_custom_call" | custom-call | flops 1048576 | bytes 4096 | tf_op jit(solution)/shard_map/projection_blocks/pallas_call | solution.py:551
  68.8 3.5 %projection_blocks.9.refs_0_ = bf16[512,1024]{1,0:T(8,128)(2,1)S(1)} custom-call(s32[10]{0:T(128)S(1)} %plan.1._.plan_ref, bf16[512,1024]{1,0:T(8,128)(2,1)S(1)} %get-tuple-element.55.data_ref, bf16[1024,8192]{1,0:T(8,128)(2,1)} %weight_ref.19, bf16[512,512]{1,0:T(8,128)(2,1)S(1)} %collective-permute-done.15.refs_0_, ...), custom_call_target="tpu_custom_call" | custom-call | flops 1048576 | bytes 4096 | tf_op jit(solution)/shard_map/projection_blocks/pallas_call | solution.py:551
  72.3 4.9 %projection_blocks.10 = (bf16[512,1024]{1,0:T(8,128)(2,1)S(1)}, bf16[512,1024]{1,0:T(8,128)(2,1)S(1)}) custom-call(s32[10]{0:T(128)S(1)} %plan.1._.plan_ref, bf16[512,1024]{1,0:T(8,128)(2,1)S(1)} %get-tuple-element.55.data_ref, bf16[1024,8192]{1,0:T(8,128)(2,1)} %weight_ref.19, bf16[512,1024]{1,0:T(8,128)(2,1)S(1)} %projection_blocks.9.refs_0_), custom_call_target="tpu_custom_call" | custom-call | flops 1048576 | bytes 4096 | tf_op jit(solution)/shard_map/projection_blocks/pallas_call | solution.py:551
  78.2 6.4 %cotangent_blocks.4.refs_3_.refs_2_ = f32[512,1024]{1,0:T(8,128)S(1)} custom-call(s32[10]{0:T(128)S(1)} %plan.1._.plan_ref, bf16[1024,8192]{1,0:T(8,128)(2,1)} %weight_ref.19, bf16[512,1024]{1,0:T(8,128)(2,1)S(1)} %get-tuple-element.63.refs_0_, bf16[512,1024]{1,0:T(8,128)(2,1)S(1)} %collective-permute-done.17.refs_1_, ...), custom_call_target="tpu_custom_call" | custom-call | flops 1048576 | bytes 4096 | tf_op jit(solution)/shard_map/cotangent_blocks/pallas_call | solution.py:650
  84.6 5.3 %collective-permute-done.13.refs_0_ = bf16[512,1024]{1,0:T(8,128)(2,1)S(1)} collective-permute-done((bf16[512,1024]{1,0:T(8,128)(2,1)S(1)}, bf16[512,1024]{1,0:T(8,128)(2,1)S(1)}, u32[]{:S(2)}, u32[]{:S(2)}) %collective-permute-start.13) | collective-permute-done | bytes 1048608 | tf_op jit(solution)/shard_map/ppermute | solution.py:385
  92.6 3.6 %collective-permute-start.26 = (bf16[512,1024]{1,0:T(8,128)(2,1)S(1)}, bf16[512,1024]{1,0:T(8,128)(2,1)S(1)}, u32[]{:S(2)}, u32[]{:S(2)}) collective-permute-start(bf16[512,1024]{1,0:T(8,128)(2,1)S(1)} %held.12.refs_0_), channel_id=1, source_target_pairs={{0,2},{1,3},{6,4},{7,5},{8,10},{9,11},{14,12},{15,13},{16,18},{17,... | collective-permute-start | bytes 3145736 | tf_op jit(solution)/shard_map/ppermute | solution.py:385
  96.2 4.8 %cotangent_blocks.5.start_ref = f32[512,1024]{1,0:T(8,128)S(1)} custom-call(s32[10]{0:T(128)S(1)} %plan.1._.plan_ref, bf16[1024,8192]{1,0:T(8,128)(2,1)} %weight_ref.19, bf16[512,1024]{1,0:T(8,128)(2,1)S(1)} %collective-permute-done.19.refs_0_, bf16[512,1024]{1,0:T(8,128)(2,1)S(1)} %added.7.refs_1_, f32[512,1024]{1,0:T(8,128)S(1)} %cotangent_blocks.4.refs_3_.refs_2_), custom_call_target="tpu_custom_call" | custom-call | flops 1048576 | bytes 4096 | tf_op jit(solution)/shard_map/cotangent_blocks/pallas_call | solution.py:650
  101.0 4.5 %cotangent_last.1 = (bf16[512,1024]{1,0:T(8,128)(2,1)}, bf16[512,256]{1,0:T(8,128)(2,1)S(1)}, bf16[512,256]{1,0:T(8,128)(2,1)S(1)}, bf16[512,256]{1,0:T(8,128)(2,1)S(1)}, bf16[512,256]{1,0:T(8,128)(2,1)S(1)}) custom-call(s32[10]{0:T(128)S(1)} %plan.1._.plan_ref, bf16[1024,8192]{1,0:T(8,128)(2,1)} %weight_ref.19, ...), custom_call_target="tpu_custom_call" | custom-call | flops 1048576 | bytes 4096 | tf_op jit(solution)/shard_map/cotangent_last/pallas_call | solution.py:616
  109.0 5.1 %projection_blocks.11 = (bf16[512,1024]{1,0:T(8,128)(2,1)S(1)}, bf16[512,1024]{1,0:T(8,128)(2,1)S(1)}) custom-call(s32[10]{0:T(128)S(1)} %plan.1._.plan_ref, bf16[512,1024]{1,0:T(8,128)(2,1)S(1)} %get-tuple-element.55.data_ref, bf16[1024,8192]{1,0:T(8,128)(2,1)} %weight_ref.19, bf16[512,1024]{1,0:T(8,128)(2,1)S(1)} %collective-permute-done.20.refs_0_, ...), custom_call_target="tpu_custom_call" | custom-call | flops 1048576 | bytes 4096 | tf_op jit(solution)/shard_map/projection_blocks/pallas_call | solution.py:551
  114.2 4.3 %collective-permute-done.26.refs_1_ = bf16[512,1024]{1,0:T(8,128)(2,1)S(1)} collective-permute-done((bf16[512,1024]{1,0:T(8,128)(2,1)S(1)}, bf16[512,1024]{1,0:T(8,128)(2,1)S(1)}, u32[]{:S(2)}, u32[]{:S(2)}) %collective-permute-start.26) | collective-permute-done | bytes 1048608 | tf_op jit(solution)/shard_map/ppermute | solution.py:385
  120.0 4.3 %collective-permute-start.30 = (bf16[512,1024]{1,0:T(8,128)(2,1)S(1)}, bf16[512,1024]{1,0:T(8,128)(2,1)S(1)}, u32[]{:S(2)}, u32[]{:S(2)}) collective-permute-start(bf16[512,1024]{1,0:T(8,128)(2,1)S(1)} %added.8.refs_4_), channel_id=1, source_target_pairs={{2,0},{3,1},{4,6},{5,7},{0,2},{1,3},{6,4},{7,5},{10,8},{11,9},{12,... | collective-permute-start | bytes 3145736 | tf_op jit(solution)/shard_map/ppermute | solution.py:385
  124.4 8.9 %causal_conv_grads.1 = (bf16[544,256]{1,0:T(8,128)(2,1)S(1)}, bf16[544,256]{1,0:T(8,128)(2,1)S(1)}, bf16[544,256]{1,0:T(8,128)(2,1)S(1)}, bf16[544,256]{1,0:T(8,128)(2,1)S(1)}) custom-call(s32[10]{0:T(128)S(1)} %plan.1._.plan_ref, bf16[4,256,512]{2,1,0:T(8,128)(2,1)S(1)} %get-tuple-element.49.in_scr, bf16[16,128,2048]{2,1,0:T(8,128)(2,1)S(1)} %lag_matrices.1.refs_1_.lag_ref, ...), custom_call_target="tpu_custom_call" | custom-call | flops 10000000000 | bytes 4096 | tf_op jit(solution)/shard_map/causal_conv_grads/pallas_call | solution.py:226
  136.8 6.1 %collective-permute-done.27.refs_1_ = bf16[544,256]{1,0:T(8,128)(2,1)S(1)} collective-permute-done((bf16[544,256]{1,0:T(8,128)(2,1)S(1)}, bf16[544,256]{1,0:T(8,128)(2,1)S(1)}, u32[]{:S(2)}, u32[]{:S(2)}) %collective-permute-start.27) | collective-permute-done | bytes 278560 | tf_op jit(solution)/shard_map/ppermute | solution.py:352
  142.9 4.5 %collective-permute-done.28.refs_2_ = bf16[544,256]{1,0:T(8,128)(2,1)S(1)} collective-permute-done((bf16[544,256]{1,0:T(8,128)(2,1)S(1)}, bf16[544,256]{1,0:T(8,128)(2,1)S(1)}, u32[]{:S(2)}, u32[]{:S(2)}) %collective-permute-start.28) | collective-permute-done | bytes 278560 | tf_op jit(solution)/shard_map/ppermute | solution.py:352
  147.5 3.2 %input_gradients.1 = (bf16[512,1024]{1,0:T(8,128)(2,1)}, bf16[512,1024]{1,0:T(8,128)(2,1)}, bf16[512,1024]{1,0:T(8,128)(2,1)}, f32[64,512]{1,0:T(8,128)}) custom-call(s32[10]{0:T(128)S(1)} %plan.1._.plan_ref, bf16[544,256]{1,0:T(8,128)(2,1)S(1)} %get-tuple-element.76.refs_0_, bf16[544,256]{1,0:T(8,128)(2,1)S(1)} %collective-permute-done.27.refs_1_, ...), custom_call_target="tpu_custom_call" | custom-call | flops 1048576 | bytes 4096 | tf_op jit(solution)/shard_map/input_gradients/pallas_call | solution.py:334
  (78 shorter events, 37.2 us)
Async XLA Ops:
  3.9 12.8 %collective-permute-start = (bf16[544,256]{1,0:T(8,128)(2,1)S(1)}, bf16[544,256]{1,0:T(8,128)(2,1)S(1)}, u32[]{:S(2)}, u32[]{:S(2)}) collective-permute-start(bf16[544,256]{1,0:T(8,128)(2,1)S(1)} %get-tuple-element.46), channel_id=1, source_target_pairs={{0,8},{8,0},{16,24},{24,16},{1,9},{9,1},{17,25},{25,17},{2,10},{10... | collective-permute-start | bytes 835592 | tf_op jit(solution)/shard_map/ppermute | solution.py:352
  6.4 14.7 %collective-permute-start.1 = (bf16[544,256]{1,0:T(8,128)(2,1)S(1)}, bf16[544,256]{1,0:T(8,128)(2,1)S(1)}, u32[]{:S(2)}, u32[]{:S(2)}) collective-permute-start(bf16[544,256]{1,0:T(8,128)(2,1)S(1)} %get-tuple-element.47), channel_id=1, source_target_pairs={{0,16},{8,24},{16,0},{24,8},{1,17},{9,25},{17,1},{25,9},{2,18},{10... | collective-permute-start | bytes 835592 | tf_op jit(solution)/shard_map/ppermute | solution.py:352
  8.0 13.2 %collective-permute-start.2 = (bf16[544,256]{1,0:T(8,128)(2,1)S(1)}, bf16[544,256]{1,0:T(8,128)(2,1)S(1)}, u32[]{:S(2)}, u32[]{:S(2)}) collective-permute-start(bf16[544,256]{1,0:T(8,128)(2,1)S(1)} %get-tuple-element.48), channel_id=1, source_target_pairs={{0,24},{8,16},{16,8},{24,0},{1,25},{9,17},{17,9},{25,1},{2,26},{10... | collective-permute-start | bytes 835592 | tf_op jit(solution)/shard_map/ppermute | solution.py:352
  8.0 25.1 %collective-permute-start.4 = (bf16[512,1024]{1,0:T(8,128)(2,1)S(1)}, bf16[512,1024]{1,0:T(8,128)(2,1)S(1)}, u32[]{:S(2)}, u32[]{:S(2)}) collective-permute-start(bf16[512,1024]{1,0:T(8,128)(2,1)S(1)} %copy-done.3), channel_id=1, source_target_pairs={{0,2},{1,3},{6,4},{7,5},{2,0},{3,1},{4,6},{5,7},{8,10},{9,11},{14,... | collective-permute-start | bytes 3145736 | tf_op jit(solution)/shard_map/ppermute | solution.py:385
  10.0 23.1 %collective-permute-start.6 = (bf16[512,1024]{1,0:T(8,128)(2,1)S(1)}, bf16[512,1024]{1,0:T(8,128)(2,1)S(1)}, u32[]{:S(2)}, u32[]{:S(2)}) collective-permute-start(bf16[512,1024]{1,0:T(8,128)(2,1)S(1)} %copy-done.3), channel_id=1, source_target_pairs={{2,4},{3,5},{4,2},{5,3},{10,12},{11,13},{12,10},{13,11},{18,20},{1... | collective-permute-start | bytes 3145736 | tf_op jit(solution)/shard_map/ppermute | solution.py:385
  27.4 13.3 %collective-permute-start.9 = (bf16[512,256]{1,0:T(8,128)(2,1)S(1)}, bf16[512,256]{1,0:T(8,128)(2,1)S(1)}, u32[]{:S(2)}, u32[]{:S(2)}) collective-permute-start(bf16[512,256]{1,0:T(8,128)(2,1)S(1)} %get-tuple-element.53), channel_id=1, source_target_pairs={{0,16},{8,24},{16,0},{24,8},{1,17},{9,25},{17,1},{25,9},{2,18},{10... | collective-permute-start | bytes 786440 | tf_op jit(solution)/shard_map/ppermute | solution.py:352
  28.2 12.4 %collective-permute-start.10 = (bf16[512,256]{1,0:T(8,128)(2,1)S(1)}, bf16[512,256]{1,0:T(8,128)(2,1)S(1)}, u32[]{:S(2)}, u32[]{:S(2)}) collective-permute-start(bf16[512,256]{1,0:T(8,128)(2,1)S(1)} %get-tuple-element.54), channel_id=1, source_target_pairs={{0,24},{8,16},{16,8},{24,0},{1,25},{9,17},{17,9},{25,1},{2,26},{10... | collective-permute-start | bytes 786440 | tf_op jit(solution)/shard_map/ppermute | solution.py:352
  33.1 28.0 %collective-permute-start.7 = (bf16[512,1024]{1,0:T(8,128)(2,1)S(1)}, bf16[512,1024]{1,0:T(8,128)(2,1)S(1)}, u32[]{:S(2)}, u32[]{:S(2)}) collective-permute-start(bf16[512,1024]{1,0:T(8,128)(2,1)S(1)} %held.8.refs_0_), channel_id=1, source_target_pairs={{2,0},{3,1},{4,6},{5,7},{10,8},{11,9},{12,14},{13,15},{18,16},{19,... | collective-permute-start | bytes 3145736 | tf_op jit(solution)/shard_map/ppermute | solution.py:385
  34.5 26.5 %collective-permute-start.5 = (bf16[512,1024]{1,0:T(8,128)(2,1)S(1)}, bf16[512,1024]{1,0:T(8,128)(2,1)S(1)}, u32[]{:S(2)}, u32[]{:S(2)}) collective-permute-start(bf16[512,1024]{1,0:T(8,128)(2,1)S(1)} %held.7.refs_1_.refs_2_), channel_id=1, source_target_pairs={{2,4},{3,5},{4,2},{5,3},{10,12},{11,13},{12,10},{13,11},{18,20},{1... | collective-permute-start | bytes 3145736 | tf_op jit(solution)/shard_map/ppermute | solution.py:385
  51.1 26.8 %collective-permute-start.14 = (bf16[512,1024]{1,0:T(8,128)(2,1)S(1)}, bf16[512,1024]{1,0:T(8,128)(2,1)S(1)}, u32[]{:S(2)}, u32[]{:S(2)}) collective-permute-start(bf16[512,1024]{1,0:T(8,128)(2,1)S(1)} %projection_blocks.7.refs_3_.refs_0_), channel_id=1, source_target_pairs={{0,2},{1,3},{6,4},{7,5},{8,10},{9,11},{14,12},{15,13},{16,18},{17,... | collective-permute-start | bytes 3145736 | tf_op jit(solution)/shard_map/ppermute | solution.py:385
  61.1 17.1 %collective-permute-start.17 = (bf16[512,1024]{1,0:T(8,128)(2,1)S(1)}, bf16[512,1024]{1,0:T(8,128)(2,1)S(1)}, u32[]{:S(2)}, u32[]{:S(2)}) collective-permute-start(bf16[512,1024]{1,0:T(8,128)(2,1)S(1)} %get-tuple-element.63.refs_0_), channel_id=1, source_target_pairs={{0,1},{1,0},{2,3},{3,2},{4,5},{5,4},{6,7},{7,6},{8,9},{9,8},{10,11... | collective-permute-start | bytes 3145736 | tf_op jit(solution)/shard_map/ppermute | solution.py:352
  61.1 28.8 %collective-permute-start.13 = (bf16[512,1024]{1,0:T(8,128)(2,1)S(1)}, bf16[512,1024]{1,0:T(8,128)(2,1)S(1)}, u32[]{:S(2)}, u32[]{:S(2)}) collective-permute-start(bf16[512,1024]{1,0:T(8,128)(2,1)S(1)} %get-tuple-element.58.refs_0_), channel_id=1, source_target_pairs={{2,0},{3,1},{4,6},{5,7},{10,8},{11,9},{12,14},{13,15},{18,16},{19,... | collective-permute-start | bytes 3145736 | tf_op jit(solution)/shard_map/ppermute | solution.py:385
  89.9 11.1 %collective-permute-start.20 = (bf16[512,1024]{1,0:T(8,128)(2,1)S(1)}, bf16[512,1024]{1,0:T(8,128)(2,1)S(1)}, u32[]{:S(2)}, u32[]{:S(2)}) collective-permute-start(bf16[512,1024]{1,0:T(8,128)(2,1)S(1)} %get-tuple-element.62.refs_1_), channel_id=1, source_target_pairs={{0,1},{1,0},{2,3},{3,2},{4,5},{5,4},{6,7},{7,6},{8,9},{9,8},{10,11... | collective-permute-start | bytes 3145736 | tf_op jit(solution)/shard_map/ppermute | solution.py:352
  90.4 10.6 %collective-permute-start.21 = (bf16[512,1024]{1,0:T(8,128)(2,1)S(1)}, bf16[512,1024]{1,0:T(8,128)(2,1)S(1)}, u32[]{:S(2)}, u32[]{:S(2)}) collective-permute-start(bf16[512,1024]{1,0:T(8,128)(2,1)S(1)} %get-tuple-element.67), channel_id=1, source_target_pairs={{0,1},{1,0},{2,3},{3,2},{4,5},{5,4},{6,7},{7,6},{8,9},{9,8},{10,11... | collective-permute-start | bytes 3145736 | tf_op jit(solution)/shard_map/ppermute | solution.py:352
  90.7 10.3 %collective-permute-start.18 = (bf16[512,1024]{1,0:T(8,128)(2,1)S(1)}, bf16[512,1024]{1,0:T(8,128)(2,1)S(1)}, u32[]{:S(2)}, u32[]{:S(2)}) collective-permute-start(bf16[512,1024]{1,0:T(8,128)(2,1)S(1)} %added.7.refs_1_), channel_id=1, source_target_pairs={{0,1},{1,0},{2,3},{3,2},{4,5},{5,4},{6,7},{7,6},{8,9},{9,8},{10,11... | collective-permute-start | bytes 3145736 | tf_op jit(solution)/shard_map/ppermute | solution.py:352
  91.3 22.9 %collective-permute-start.25 = (bf16[512,1024]{1,0:T(8,128)(2,1)S(1)}, bf16[512,1024]{1,0:T(8,128)(2,1)S(1)}, u32[]{:S(2)}, u32[]{:S(2)}) collective-permute-start(bf16[512,1024]{1,0:T(8,128)(2,1)S(1)} %added.6.refs_2_), channel_id=1, source_target_pairs={{2,4},{3,5},{4,2},{5,3},{10,12},{11,13},{12,10},{13,11},{18,20},{1... | collective-permute-start | bytes 3145736 | tf_op jit(solution)/shard_map/ppermute | solution.py:385
  92.6 25.8 %collective-permute-start.26 = (bf16[512,1024]{1,0:T(8,128)(2,1)S(1)}, bf16[512,1024]{1,0:T(8,128)(2,1)S(1)}, u32[]{:S(2)}, u32[]{:S(2)}) collective-permute-start(bf16[512,1024]{1,0:T(8,128)(2,1)S(1)} %held.12.refs_0_), channel_id=1, source_target_pairs={{0,2},{1,3},{6,4},{7,5},{8,10},{9,11},{14,12},{15,13},{16,18},{17,... | collective-permute-start | bytes 3145736 | tf_op jit(solution)/shard_map/ppermute | solution.py:385
  105.5 18.8 %collective-permute-start.22 = (bf16[512,256]{1,0:T(8,128)(2,1)S(1)}, bf16[512,256]{1,0:T(8,128)(2,1)S(1)}, u32[]{:S(2)}, u32[]{:S(2)}) collective-permute-start(bf16[512,256]{1,0:T(8,128)(2,1)S(1)} %get-tuple-element.69), channel_id=1, source_target_pairs={{0,8},{8,0},{16,24},{24,16},{1,9},{9,1},{17,25},{25,17},{2,10},{10... | collective-permute-start | bytes 786440 | tf_op jit(solution)/shard_map/ppermute | solution.py:352
  107.0 17.3 %collective-permute-start.23 = (bf16[512,256]{1,0:T(8,128)(2,1)S(1)}, bf16[512,256]{1,0:T(8,128)(2,1)S(1)}, u32[]{:S(2)}, u32[]{:S(2)}) collective-permute-start(bf16[512,256]{1,0:T(8,128)(2,1)S(1)} %get-tuple-element.70), channel_id=1, source_target_pairs={{0,16},{8,24},{16,0},{24,8},{1,17},{9,25},{17,1},{25,9},{2,18},{10... | collective-permute-start | bytes 786440 | tf_op jit(solution)/shard_map/ppermute | solution.py:352
  108.5 15.8 %collective-permute-start.24 = (bf16[512,256]{1,0:T(8,128)(2,1)S(1)}, bf16[512,256]{1,0:T(8,128)(2,1)S(1)}, u32[]{:S(2)}, u32[]{:S(2)}) collective-permute-start(bf16[512,256]{1,0:T(8,128)(2,1)S(1)} %get-tuple-element.71), channel_id=1, source_target_pairs={{0,24},{8,16},{16,8},{24,0},{1,25},{9,17},{17,9},{25,1},{2,26},{10... | collective-permute-start | bytes 786440 | tf_op jit(solution)/shard_map/ppermute | solution.py:352
  118.7 28.7 %collective-permute-start.31 = (bf16[512,1024]{1,0:T(8,128)(2,1)S(1)}, bf16[512,1024]{1,0:T(8,128)(2,1)S(1)}, u32[]{:S(2)}, u32[]{:S(2)}) collective-permute-start(bf16[512,1024]{1,0:T(8,128)(2,1)S(1)} %added.9.refs_5_), channel_id=1, source_target_pairs={{2,4},{3,5},{4,2},{5,3},{10,12},{11,13},{12,10},{13,11},{18,20},{1... | collective-permute-start | bytes 3145736 | tf_op jit(solution)/shard_map/ppermute | solution.py:385
  120.0 27.5 %collective-permute-start.30 = (bf16[512,1024]{1,0:T(8,128)(2,1)S(1)}, bf16[512,1024]{1,0:T(8,128)(2,1)S(1)}, u32[]{:S(2)}, u32[]{:S(2)}) collective-permute-start(bf16[512,1024]{1,0:T(8,128)(2,1)S(1)} %added.8.refs_4_), channel_id=1, source_target_pairs={{2,0},{3,1},{4,6},{5,7},{0,2},{1,3},{6,4},{7,5},{10,8},{11,9},{12,... | collective-permute-start | bytes 3145736 | tf_op jit(solution)/shard_map/ppermute | solution.py:385
  134.8 12.6 %collective-permute-start.28 = (bf16[544,256]{1,0:T(8,128)(2,1)S(1)}, bf16[544,256]{1,0:T(8,128)(2,1)S(1)}, u32[]{:S(2)}, u32[]{:S(2)}) collective-permute-start(bf16[544,256]{1,0:T(8,128)(2,1)S(1)} %get-tuple-element.78), channel_id=1, source_target_pairs={{0,16},{8,24},{16,0},{24,8},{1,17},{9,25},{17,1},{25,9},{2,18},{10... | collective-permute-start | bytes 835592 | tf_op jit(solution)/shard_map/ppermute | solution.py:352
  136.4 11.0 %collective-permute-start.29 = (bf16[544,256]{1,0:T(8,128)(2,1)S(1)}, bf16[544,256]{1,0:T(8,128)(2,1)S(1)}, u32[]{:S(2)}, u32[]{:S(2)}) collective-permute-start(bf16[544,256]{1,0:T(8,128)(2,1)S(1)} %get-tuple-element.79), channel_id=1, source_target_pairs={{0,24},{8,16},{16,8},{24,0},{1,25},{9,17},{17,9},{25,1},{2,26},{10... | collective-permute-start | bytes 835592 | tf_op jit(solution)/shard_map/ppermute | solution.py:352
  (12 other events, 102.0 us)

commit v20 on v17

--- a/solution.py
+++ b/solution.py
@@ -92,7 +92,7 @@
         spread_out(out_scr, start, per_group, value, members, width)
         return carry
 
-    lax.fori_loop(0, groups, one_group, 0, unroll=8)
+    lax.fori_loop(0, groups, one_group, 0, unroll=16)
     for step in range(members):
         outputs[step][...] = out_scr[position ^ step].T
 
@@ -115,7 +115,8 @@
     def _():
         for step in range(members):
             cot_scr[position ^ step] = cotangents[step][...].T
-        pad_scr[...] = jnp.zeros_like(pad_scr)
+        tail = pad_scr.at[:, depth - per_group :, :]
+        tail[...] = jnp.zeros(tail.shape, jnp.bfloat16)
 
     for local_group in range(batch):
         group = pl.program_id(0) * batch + local_group
@@ -221,7 +222,7 @@
     width, channels = cotangents[0].shape
     length = members * width
     groups = channels // per_group
-    batch = 4 if groups % 4 == 0 else 1
+    batch = next(size for size in (8, 4, 1) if groups % size == 0)
     rows = width + padded(groups) * width // channels
     return pl.pallas_call(
         functools.partial(backward_kernel, members, batch, per_group, scale, width),
@@ -237,7 +238,7 @@
             pltpu.VMEM((groups, length), jnp.float32),
             pltpu.VMEM((batch, 2 * length // BLOCK * per_group, 2 * BLOCK), jnp.bfloat16),
         ],
-        compiler_params=pltpu.CompilerParams(vmem_limit_bytes=24 * 2**20),
+        compiler_params=pltpu.CompilerParams(vmem_limit_bytes=32 * 2**20),
         cost_estimate=pl.CostEstimate(flops=10**10, bytes_accessed=2**12, transcendentals=0),
         name="causal_conv_grads",
     )(plan, turned, lags, *cotangents, *after)

time: 148 us -> 148 us (level)
  transfers between devices with their start and end apart: 31 -> 31, of which waited for: 11 -> 11; matrix products, arithmetic and copies ran while one was open for 0% -> 0% of each run, Pallas kernels for 47% -> 46%
where the time goes in v20:
time: 148 us; the launch traced here: 147 us
  Pallas kernels  71.3 us (48%)
  starting transfers between devices  38.4 us (26%)
  waiting for transfers between devices  36.2 us (24%)
    ppermute x22, waiting for transfers between devices, swapped(): return lax.ppermute(array, axis, [(i, i ^ step) for i in range(size)])  27.1 us
    pallas_call x6, Pallas kernels, column_products(): pl.pallas_call(functools.partial(product_kernel, steps, [part.shape[1] fo...  23.8 us
    ppermute x9, starting transfers between devices, hop(): lax.ppermute(array, 'tp', [(2 * i + core, 2 * j + core) for i, j in pairs...  21.4 us
    ppermute x22, starting transfers between devices, swapped(): return lax.ppermute(array, axis, [(i, i ^ step) for i in range(size)])  17 us
    pallas_call x3, Pallas kernels, cotangent_products(): pl.pallas_call(functools.partial(cotangent_kernel, count, begin), out_sha...  16.2 us
    ppermute x9, waiting for transfers between devices, hop(): lax.ppermute(array, 'tp', [(2 * i + core, 2 * j + core) for i, j in pairs...  9.09 us
    pallas_call x1, Pallas kernels, correlate(): pl.pallas_call(functools.partial(backward_kernel, members, batch, per_gro...  8.39 us
    pallas_call x1, Pallas kernels, convolve(): pl.pallas_call(functools.partial(forward_kernel, members, per_group, widt...  4.55 us
  transfers between devices with their start and end apart: 31, of which 11 were waited for; matrix products, arithmetic and copies ran while one was open for 0% of the time, Pallas kernels for 46%

profile of v20, /device:TPU:0, one launch (start us, length us, event | category | flops | bytes accessed | tf_op | source)
XLA Modules:
  0.0 147.2 jit_solution(2140122611121910273)
XLA Ops:
  1.9 5.6 %collective-permute-start.4 = (bf16[512,1024]{1,0:T(8,128)(2,1)}, bf16[512,1024]{1,0:T(8,128)(2,1)S(1)}, u32[]{:S(2)}, u32[]{:S(2)}) collective-permute-start(bf16[512,1024]{1,0:T(8,128)(2,1)} %refs_0_.1), channel_id=1, source_target_pairs={{0,2},{1,3},{6,4},{7,5},{2,0},{3,1},{4,6},{5,7},{8,10},{9,11},{14,... | collective-permute-start | bytes 3145736 | tf_op jit(solution)/shard_map/ppermute | solution.py:386
  7.5 2.6 %gated_input.1 = (bf16[544,256]{1,0:T(8,128)(2,1)S(1)}, bf16[544,256]{1,0:T(8,128)(2,1)S(1)}, bf16[544,256]{1,0:T(8,128)(2,1)S(1)}, bf16[544,256]{1,0:T(8,128)(2,1)S(1)}) custom-call(s32[2]{0:T(128)S(1)} %pad_add_fusion.who_ref, bf16[512,1024]{1,0:T(8,128)(2,1)} %refs_4_.3, bf16[512,1024]{1,0:T(8,128)(2,1)} %refs_5_.1, f32[64,512]{1,0:T(8,128)} %bitcast.4), custom_call_target="tpu_custom_call" | custom-call | flops 1048576 | bytes 4096 | tf_op jit(solution)/shard_map/gated_input/pallas_call | solution.py:286
  14.9 5.0 %cotangent_blocks.3.refs_4_.refs_3_ = f32[512,1024]{1,0:T(8,128)S(1)} custom-call(s32[10]{0:T(128)S(1)} %plan.1._.plan_ref, bf16[1024,8192]{1,0:T(8,128)(2,1)} %weight_ref.19, bf16[512,1024]{1,0:T(8,128)(2,1)S(1)} %copy-done.3, bf16[512,1024]{1,0:T(8,128)(2,1)} %collective-permute-done.3.refs_1_), custom_call_target="tpu_custom_call" | custom-call | flops 1048576 | bytes 4096 | tf_op jit(solution)/shard_map/cotangent_blocks/pallas_call | solution.py:651
  19.9 5.8 %collective-permute-done.1.refs_2_ = bf16[544,256]{1,0:T(8,128)(2,1)S(1)} collective-permute-done((bf16[544,256]{1,0:T(8,128)(2,1)S(1)}, bf16[544,256]{1,0:T(8,128)(2,1)S(1)}, u32[]{:S(2)}, u32[]{:S(2)}) %collective-permute-start.1) | collective-permute-done | bytes 278560 | tf_op jit(solution)/shard_map/ppermute | solution.py:353
  25.7 4.5 %causal_conv.1 = (bf16[512,256]{1,0:T(8,128)(2,1)S(1)}, bf16[512,256]{1,0:T(8,128)(2,1)S(1)}, bf16[512,256]{1,0:T(8,128)(2,1)S(1)}, bf16[512,256]{1,0:T(8,128)(2...) custom-call(s32[10]{0:T(128)S(1)} %plan.1._.plan_ref, bf16[544,256]{1,0:T(8,128)(2,1)S(1)} %get-tuple-element.48.refs_0_, ...), custom_call_target="tpu_custom_call" | custom-call | flops 1048576 | bytes 4096 | tf_op jit(solution)/shard_map/causal_conv/pallas_call | solution.py:189
  36.6 3.4 %lag_matrices.1.refs_5_.lag_ref = bf16[16,128,2048]{2,1,0:T(8,128)(2,1)S(1)} custom-call(f32[16,2048]{1,0:T(8,128)S(1)} %get-tuple-element.53.taps_ref), custom_call_target="tpu_custom_call" | custom-call | flops 1048576 | bytes 4096 | tf_op jit(solution)/shard_map/lag_matrices/pallas_call | solution.py:208
  40.3 5.4 %collective-permute-done.9.refs_2_ = bf16[512,256]{1,0:T(8,128)(2,1)S(1)} collective-permute-done((bf16[512,256]{1,0:T(8,128)(2,1)S(1)}, bf16[512,256]{1,0:T(8,128)(2,1)S(1)}, u32[]{:S(2)}, u32[]{:S(2)}) %collective-permute-start.9) | collective-permute-done | bytes 262176 | tf_op jit(solution)/shard_map/ppermute | solution.py:353
  46.5 3.4 %projection_blocks.6 = (bf16[512,768]{1,0:T(8,128)(2,1)S(1)}, bf16[512,256]{1,0:T(8,128)(2,1)S(1)}) custom-call(s32[10]{0:T(128)S(1)} %plan.1._.plan_ref, bf16[512,1024]{1,0:T(8,128)(2,1)S(1)} %get-tuple-element.64.data_ref, bf16[1024,8192]{1,0:T(8,128)(2,1)} %weight_ref.19), custom_call_target="tpu_custom_call" | custom-call | flops 1048576 | bytes 4096 | tf_op jit(solution)/shard_map/projection_blocks/pallas_call | solution.py:552
  52.6 3.5 %projection_blocks.7.refs_2_.end_ref.refs_0_ = bf16[512,1024]{1,0:T(8,128)(2,1)S(1)} custom-call(s32[10]{0:T(128)S(1)} %plan.1._.plan_ref, bf16[512,1024]{1,0:T(8,128)(2,1)S(1)} %get-tuple-element.64.data_ref, bf16[1024,8192]{1,0:T(8,128)(2,1)} %weight_ref.19, bf16[512,768]{1,0:T(8,128)(2,1)S(1)} %collective-permute-done.11.refs_0_, ...), custom_call_target="tpu_custom_call" | custom-call | flops 1048576 | bytes 4096 | tf_op jit(solution)/shard_map/projection_blocks/pallas_call | solution.py:552
  56.1 4.1 %collective-permute-done.7.refs_1_ = bf16[512,1024]{1,0:T(8,128)(2,1)S(1)} collective-permute-done((bf16[512,1024]{1,0:T(8,128)(2,1)S(1)}, bf16[512,1024]{1,0:T(8,128)(2,1)S(1)}, u32[]{:S(2)}, u32[]{:S(2)}) %collective-permute-start.7) | collective-permute-done | bytes 1048608 | tf_op jit(solution)/shard_map/ppermute | solution.py:386
  61.0 3.8 %collective-permute-start.13 = (bf16[512,1024]{1,0:T(8,128)(2,1)S(1)}, bf16[512,1024]{1,0:T(8,128)(2,1)S(1)}, u32[]{:S(2)}, u32[]{:S(2)}) collective-permute-start(bf16[512,1024]{1,0:T(8,128)(2,1)S(1)} %chosen.2.refs_0_), channel_id=1, source_target_pairs={{2,0},{3,1},{4,6},{5,7},{0,2},{1,3},{6,4},{7,5},{10,8},{11,9},{12,... | collective-permute-start | bytes 3145736 | tf_op jit(solution)/shard_map/ppermute | solution.py:386
  65.2 3.4 %projection_blocks.8 = (bf16[512,512]{1,0:T(8,128)(2,1)S(1)}, bf16[512,512]{1,0:T(8,128)(2,1)S(1)}) custom-call(s32[10]{0:T(128)S(1)} %plan.1._.plan_ref, bf16[512,1024]{1,0:T(8,128)(2,1)S(1)} %get-tuple-element.64.data_ref, bf16[1024,8192]{1,0:T(8,128)(2,1)} %weight_ref.19, bf16[512,1024]{1,0:T(8,128)(2,1)S(1)} %chosen.2.refs_0_), custom_call_target="tpu_custom_call" | custom-call | flops 1048576 | bytes 4096 | tf_op jit(solution)/shard_map/projection_blocks/pallas_call | solution.py:552
  71.4 3.5 %projection_blocks.9.refs_4_.refs_0_ = bf16[512,1024]{1,0:T(8,128)(2,1)S(1)} custom-call(s32[10]{0:T(128)S(1)} %plan.1._.plan_ref, bf16[512,1024]{1,0:T(8,128)(2,1)S(1)} %get-tuple-element.64.data_ref, bf16[1024,8192]{1,0:T(8,128)(2,1)} %weight_ref.19, bf16[512,512]{1,0:T(8,128)(2,1)S(1)} %collective-permute-done.15.refs_0_, ...), custom_call_target="tpu_custom_call" | custom-call | flops 1048576 | bytes 4096 | tf_op jit(solution)/shard_map/projection_blocks/pallas_call | solution.py:552
  74.9 4.9 %projection_blocks.10 = (bf16[512,1024]{1,0:T(8,128)(2,1)S(1)}, bf16[512,1024]{1,0:T(8,128)(2,1)S(1)}) custom-call(s32[10]{0:T(128)S(1)} %plan.1._.plan_ref, bf16[512,1024]{1,0:T(8,128)(2,1)S(1)} %get-tuple-element.64.data_ref, bf16[1024,8192]{1,0:T(8,128)(2,1)} %weight_ref.19, bf16[512,1024]{1,0:T(8,128)(2,1)S(1)} %projection_blocks.9.refs_4_.refs_0_), custom_call_target="tpu_custom_call" | custom-call | flops 1048576 | bytes 4096 | tf_op jit(solution)/shard_map/projection_blocks/pallas_call | solution.py:552
  80.4 6.4 %cotangent_blocks.4.refs_1_.refs_2_ = f32[512,1024]{1,0:T(8,128)S(1)} custom-call(s32[10]{0:T(128)S(1)} %plan.1._.plan_ref, bf16[1024,8192]{1,0:T(8,128)(2,1)} %weight_ref.19, bf16[512,1024]{1,0:T(8,128)(2,1)S(1)} %get-tuple-element.58.refs_0_, bf16[512,1024]{1,0:T(8,128)(2,1)S(1)} %collective-permute-done.14.refs_1_, bf16[512,1024]{1,0:T(8,128)(2,1)S(1)} %added.4.refs_2_, ...), custom_call_target="tpu_custom_call" | custom-call | flops 1048576 | bytes 4096 | tf_op jit(solution)/shard_map/cotangent_blocks/pallas_call | solution.py:651
  91.1 4.8 %cotangent_blocks.5.start_ref = f32[512,1024]{1,0:T(8,128)S(1)} custom-call(s32[10]{0:T(128)S(1)} %plan.1._.plan_ref, bf16[1024,8192]{1,0:T(8,128)(2,1)} %weight_ref.19, bf16[512,1024]{1,0:T(8,128)(2,1)S(1)} %collective-permute-done.18.refs_0_, bf16[512,1024]{1,0:T(8,128)(2,1)S(1)} %chosen.3.refs_1_, f32[512,1024]{1,0:T(8,128)S(1)} %cotangent_blocks.4.refs_1_.refs_2_, ...), custom_call_target="tpu_custom_call" | custom-call | flops 1048576 | bytes 4096 | tf_op jit(solution)/shard_map/cotangent_blocks/pallas_call | solution.py:651
  95.9 4.5 %cotangent_last.1 = (bf16[512,1024]{1,0:T(8,128)(2,1)}, bf16[512,256]{1,0:T(8,128)(2,1)S(1)}, bf16[512,256]{1,0:T(8,128)(2,1)S(1)}, bf16[512,256]{1,0:T(8,128)(2,1)S(1)}, bf16[512,256]{1,0:T(8,128)(2,1)S(1)}) custom-call(s32[10]{0:T(128)S(1)} %plan.1._.plan_ref, bf16[1024,8192]{1,0:T(8,128)(2,1)} %weight_ref.19, ...), custom_call_target="tpu_custom_call" | custom-call | flops 1048576 | bytes 4096 | tf_op jit(solution)/shard_map/cotangent_last/pallas_call | solution.py:617
  103.9 5.1 %projection_blocks.11 = (bf16[512,1024]{1,0:T(8,128)(2,1)S(1)}, bf16[512,1024]{1,0:T(8,128)(2,1)S(1)}) custom-call(s32[10]{0:T(128)S(1)} %plan.1._.plan_ref, bf16[512,1024]{1,0:T(8,128)(2,1)S(1)} %get-tuple-element.64.data_ref, bf16[1024,8192]{1,0:T(8,128)(2,1)} %weight_ref.19, bf16[512,1024]{1,0:T(8,128)(2,1)S(1)} %collective-permute-done.19.refs_0_, ...), custom_call_target="tpu_custom_call" | custom-call | flops 1048576 | bytes 4096 | tf_op jit(solution)/shard_map/projection_blocks/pallas_call | solution.py:552
  109.0 4.3 %collective-permute-done.25.refs_1_ = bf16[512,1024]{1,0:T(8,128)(2,1)S(1)} collective-permute-done((bf16[512,1024]{1,0:T(8,128)(2,1)S(1)}, bf16[512,1024]{1,0:T(8,128)(2,1)S(1)}, u32[]{:S(2)}, u32[]{:S(2)}) %collective-permute-start.25) | collective-permute-done | bytes 1048608 | tf_op jit(solution)/shard_map/ppermute | solution.py:386
  114.9 5.5 %collective-permute-start.29 = (bf16[512,1024]{1,0:T(8,128)(2,1)S(1)}, bf16[512,1024]{1,0:T(8,128)(2,1)S(1)}, u32[]{:S(2)}, u32[]{:S(2)}) collective-permute-start(bf16[512,1024]{1,0:T(8,128)(2,1)S(1)} %added.6.refs_4_), channel_id=1, source_target_pairs={{2,0},{3,1},{4,6},{5,7},{0,2},{1,3},{6,4},{7,5},{10,8},{11,9},{12,... | collective-permute-start | bytes 3145736 | tf_op jit(solution)/shard_map/ppermute | solution.py:386
  120.4 8.4 %causal_conv_grads.1 = (bf16[544,256]{1,0:T(8,128)(2,1)S(1)}, bf16[544,256]{1,0:T(8,128)(2,1)S(1)}, bf16[544,256]{1,0:T(8,128)(2,1)S(1)}, bf16[544,256]{1,0:T(8,128)(2,1)S(1)}) custom-call(s32[10]{0:T(128)S(1)} %plan.1._.plan_ref, bf16[4,256,512]{2,1,0:T(8,128)(2,1)S(1)} %get-tuple-element.52.in_scr, bf16[16,128,2048]{2,1,0:T(8,128)(2,1)S(1)} %lag_matrices.1.refs_5_.lag_ref, ...), custom_call_target="tpu_custom_call" | custom-call | flops 10000000000 | bytes 4096 | tf_op jit(solution)/shard_map/causal_conv_grads/pallas_call | solution.py:227
  132.4 6.1 %collective-permute-done.26.refs_1_ = bf16[544,256]{1,0:T(8,128)(2,1)S(1)} collective-permute-done((bf16[544,256]{1,0:T(8,128)(2,1)S(1)}, bf16[544,256]{1,0:T(8,128)(2,1)S(1)}, u32[]{:S(2)}, u32[]{:S(2)}) %collective-permute-start.26) | collective-permute-done | bytes 278560 | tf_op jit(solution)/shard_map/ppermute | solution.py:353
  138.5 5.3 %collective-permute-done.27.refs_2_ = bf16[544,256]{1,0:T(8,128)(2,1)S(1)} collective-permute-done((bf16[544,256]{1,0:T(8,128)(2,1)S(1)}, bf16[544,256]{1,0:T(8,128)(2,1)S(1)}, u32[]{:S(2)}, u32[]{:S(2)}) %collective-permute-start.27) | collective-permute-done | bytes 278560 | tf_op jit(solution)/shard_map/ppermute | solution.py:353
  143.8 3.2 %input_gradients.1 = (bf16[512,1024]{1,0:T(8,128)(2,1)}, bf16[512,1024]{1,0:T(8,128)(2,1)}, bf16[512,1024]{1,0:T(8,128)(2,1)}, f32[64,512]{1,0:T(8,128)}) custom-call(s32[10]{0:T(128)S(1)} %plan.1._.plan_ref, bf16[544,256]{1,0:T(8,128)(2,1)S(1)} %get-tuple-element.82.refs_0_, bf16[544,256]{1,0:T(8,128)(2,1)S(1)} %collective-permute-done.26.refs_1_, ...), custom_call_target="tpu_custom_call" | custom-call | flops 1048576 | bytes 4096 | tf_op jit(solution)/shard_map/input_gradients/pallas_call | solution.py:335
  (75 shorter events, 33.6 us)
Async XLA Ops:
  0.6 12.6 %collective-permute-start.3 = (bf16[512,1024]{1,0:T(8,128)(2,1)}, bf16[512,1024]{1,0:T(8,128)(2,1)}, u32[]{:S(2)}, u32[]{:S(2)}) collective-permute-start(bf16[512,1024]{1,0:T(8,128)(2,1)} %refs_0_.1), channel_id=1, source_target_pairs={{0,1},{1,0},{2,3},{3,2},{4,5},{5,4},{6,7},{7,6},{8,9},{9,8},{10,11... | collective-permute-start | bytes 3145736 | tf_op jit(solution)/shard_map/ppermute | solution.py:353
  1.2 29.1 %collective-permute-start.5 = (bf16[512,1024]{1,0:T(8,128)(2,1)}, bf16[512,1024]{1,0:T(8,128)(2,1)S(1)}, u32[]{:S(2)}, u32[]{:S(2)}) collective-permute-start(bf16[512,1024]{1,0:T(8,128)(2,1)} %refs_0_.1), channel_id=1, source_target_pairs={{2,4},{3,5},{4,2},{5,3},{10,12},{11,13},{12,10},{13,11},{18,20},{1... | collective-permute-start | bytes 3145736 | tf_op jit(solution)/shard_map/ppermute | solution.py:386
  1.9 29.2 %collective-permute-start.4 = (bf16[512,1024]{1,0:T(8,128)(2,1)}, bf16[512,1024]{1,0:T(8,128)(2,1)S(1)}, u32[]{:S(2)}, u32[]{:S(2)}) collective-permute-start(bf16[512,1024]{1,0:T(8,128)(2,1)} %refs_0_.1), channel_id=1, source_target_pairs={{0,2},{1,3},{6,4},{7,5},{2,0},{3,1},{4,6},{5,7},{8,10},{9,11},{14,... | collective-permute-start | bytes 3145736 | tf_op jit(solution)/shard_map/ppermute | solution.py:386
  10.1 9.8 %collective-permute-start = (bf16[544,256]{1,0:T(8,128)(2,1)S(1)}, bf16[544,256]{1,0:T(8,128)(2,1)S(1)}, u32[]{:S(2)}, u32[]{:S(2)}) collective-permute-start(bf16[544,256]{1,0:T(8,128)(2,1)S(1)} %get-tuple-element.49), channel_id=1, source_target_pairs={{0,8},{8,0},{16,24},{24,16},{1,9},{9,1},{17,25},{25,17},{2,10},{10... | collective-permute-start | bytes 835592 | tf_op jit(solution)/shard_map/ppermute | solution.py:353
  11.7 14.0 %collective-permute-start.1 = (bf16[544,256]{1,0:T(8,128)(2,1)S(1)}, bf16[544,256]{1,0:T(8,128)(2,1)S(1)}, u32[]{:S(2)}, u32[]{:S(2)}) collective-permute-start(bf16[544,256]{1,0:T(8,128)(2,1)S(1)} %get-tuple-element.50), channel_id=1, source_target_pairs={{0,16},{8,24},{16,0},{24,8},{1,17},{9,25},{17,1},{25,9},{2,18},{10... | collective-permute-start | bytes 835592 | tf_op jit(solution)/shard_map/ppermute | solution.py:353
  13.2 12.5 %collective-permute-start.2 = (bf16[544,256]{1,0:T(8,128)(2,1)S(1)}, bf16[544,256]{1,0:T(8,128)(2,1)S(1)}, u32[]{:S(2)}, u32[]{:S(2)}) collective-permute-start(bf16[544,256]{1,0:T(8,128)(2,1)S(1)} %get-tuple-element.51), channel_id=1, source_target_pairs={{0,24},{8,16},{16,8},{24,0},{1,25},{9,17},{17,9},{25,1},{2,26},{10... | collective-permute-start | bytes 835592 | tf_op jit(solution)/shard_map/ppermute | solution.py:353
  32.5 13.1 %collective-permute-start.9 = (bf16[512,256]{1,0:T(8,128)(2,1)S(1)}, bf16[512,256]{1,0:T(8,128)(2,1)S(1)}, u32[]{:S(2)}, u32[]{:S(2)}) collective-permute-start(bf16[512,256]{1,0:T(8,128)(2,1)S(1)} %get-tuple-element.62), channel_id=1, source_target_pairs={{0,16},{8,24},{16,0},{24,8},{1,17},{9,25},{17,1},{25,9},{2,18},{10... | collective-permute-start | bytes 786440 | tf_op jit(solution)/shard_map/ppermute | solution.py:353
  34.1 11.6 %collective-permute-start.10 = (bf16[512,256]{1,0:T(8,128)(2,1)S(1)}, bf16[512,256]{1,0:T(8,128)(2,1)S(1)}, u32[]{:S(2)}, u32[]{:S(2)}) collective-permute-start(bf16[512,256]{1,0:T(8,128)(2,1)S(1)} %get-tuple-element.63), channel_id=1, source_target_pairs={{0,24},{8,16},{16,8},{24,0},{1,25},{9,17},{17,9},{25,1},{2,26},{10... | collective-permute-start | bytes 786440 | tf_op jit(solution)/shard_map/ppermute | solution.py:353
  34.5 25.7 %collective-permute-start.7 = (bf16[512,1024]{1,0:T(8,128)(2,1)S(1)}, bf16[512,1024]{1,0:T(8,128)(2,1)S(1)}, u32[]{:S(2)}, u32[]{:S(2)}) collective-permute-start(bf16[512,1024]{1,0:T(8,128)(2,1)S(1)} %get-tuple-element.59.refs_0_), channel_id=1, source_target_pairs={{2,0},{3,1},{4,6},{5,7},{10,8},{11,9},{12,14},{13,15},{18,16},{19,... | collective-permute-start | bytes 3145736 | tf_op jit(solution)/shard_map/ppermute | solution.py:386
  35.8 24.4 %collective-permute-start.6 = (bf16[512,1024]{1,0:T(8,128)(2,1)S(1)}, bf16[512,1024]{1,0:T(8,128)(2,1)S(1)}, u32[]{:S(2)}, u32[]{:S(2)}) collective-permute-start(bf16[512,1024]{1,0:T(8,128)(2,1)S(1)} %get-tuple-element.58.refs_0_), channel_id=1, source_target_pairs={{2,4},{3,5},{4,2},{5,3},{10,12},{11,13},{12,10},{13,11},{18,20},{1... | collective-permute-start | bytes 3145736 | tf_op jit(solution)/shard_map/ppermute | solution.py:386
  50.5 29.9 %collective-permute-start.14 = (bf16[512,1024]{1,0:T(8,128)(2,1)S(1)}, bf16[512,1024]{1,0:T(8,128)(2,1)S(1)}, u32[]{:S(2)}, u32[]{:S(2)}) collective-permute-start(bf16[512,1024]{1,0:T(8,128)(2,1)S(1)} %get-tuple-element.58.refs_0_), channel_id=1, source_target_pairs={{0,1},{1,0},{2,3},{3,2},{4,5},{5,4},{6,7},{7,6},{8,9},{9,8},{10,11... | collective-permute-start | bytes 3145736 | tf_op jit(solution)/shard_map/ppermute | solution.py:353
  61.0 25.7 %collective-permute-start.13 = (bf16[512,1024]{1,0:T(8,128)(2,1)S(1)}, bf16[512,1024]{1,0:T(8,128)(2,1)S(1)}, u32[]{:S(2)}, u32[]{:S(2)}) collective-permute-start(bf16[512,1024]{1,0:T(8,128)(2,1)S(1)} %chosen.2.refs_0_), channel_id=1, source_target_pairs={{2,0},{3,1},{4,6},{5,7},{0,2},{1,3},{6,4},{7,5},{10,8},{11,9},{12,... | collective-permute-start | bytes 3145736 | tf_op jit(solution)/shard_map/ppermute | solution.py:386
  65.1 25.3 %collective-permute-start.18 = (bf16[512,1024]{1,0:T(8,128)(2,1)S(1)}, bf16[512,1024]{1,0:T(8,128)(2,1)S(1)}, u32[]{:S(2)}, u32[]{:S(2)}) collective-permute-start(bf16[512,1024]{1,0:T(8,128)(2,1)S(1)} %added.4.refs_2_), channel_id=1, source_target_pairs={{0,1},{1,0},{2,3},{3,2},{4,5},{5,4},{6,7},{7,6},{8,9},{9,8},{10,11... | collective-permute-start | bytes 3145736 | tf_op jit(solution)/shard_map/ppermute | solution.py:353
  79.8 16.1 %collective-permute-start.20 = (bf16[512,1024]{1,0:T(8,128)(2,1)S(1)}, bf16[512,1024]{1,0:T(8,128)(2,1)S(1)}, u32[]{:S(2)}, u32[]{:S(2)}) collective-permute-start(bf16[512,1024]{1,0:T(8,128)(2,1)S(1)} %get-tuple-element.73), channel_id=1, source_target_pairs={{0,1},{1,0},{2,3},{3,2},{4,5},{5,4},{6,7},{7,6},{8,9},{9,8},{10,11... | collective-permute-start | bytes 3145736 | tf_op jit(solution)/shard_map/ppermute | solution.py:353
  80.2 15.7 %collective-permute-start.19 = (bf16[512,1024]{1,0:T(8,128)(2,1)S(1)}, bf16[512,1024]{1,0:T(8,128)(2,1)S(1)}, u32[]{:S(2)}, u32[]{:S(2)}) collective-permute-start(bf16[512,1024]{1,0:T(8,128)(2,1)S(1)} %get-tuple-element.71.refs_2_), channel_id=1, source_target_pairs={{0,1},{1,0},{2,3},{3,2},{4,5},{5,4},{6,7},{7,6},{8,9},{9,8},{10,11... | collective-permute-start | bytes 3145736 | tf_op jit(solution)/shard_map/ppermute | solution.py:353
  88.1 25.2 %collective-permute-start.25 = (bf16[512,1024]{1,0:T(8,128)(2,1)S(1)}, bf16[512,1024]{1,0:T(8,128)(2,1)S(1)}, u32[]{:S(2)}, u32[]{:S(2)}) collective-permute-start(bf16[512,1024]{1,0:T(8,128)(2,1)S(1)} %held.8.refs_0_), channel_id=1, source_target_pairs={{0,2},{1,3},{6,4},{7,5},{8,10},{9,11},{14,12},{15,13},{16,18},{17,... | collective-permute-start | bytes 3145736 | tf_op jit(solution)/shard_map/ppermute | solution.py:386
  90.4 23.0 %collective-permute-start.24 = (bf16[512,1024]{1,0:T(8,128)(2,1)S(1)}, bf16[512,1024]{1,0:T(8,128)(2,1)S(1)}, u32[]{:S(2)}, u32[]{:S(2)}) collective-permute-start(bf16[512,1024]{1,0:T(8,128)(2,1)S(1)} %added.5.refs_0_.refs_3_), channel_id=1, source_target_pairs={{2,4},{3,5},{4,2},{5,3},{10,12},{11,13},{12,10},{13,11},{18,20},{1... | collective-permute-start | bytes 3145736 | tf_op jit(solution)/shard_map/ppermute | solution.py:386
  100.4 20.0 %collective-permute-start.21 = (bf16[512,256]{1,0:T(8,128)(2,1)S(1)}, bf16[512,256]{1,0:T(8,128)(2,1)S(1)}, u32[]{:S(2)}, u32[]{:S(2)}) collective-permute-start(bf16[512,256]{1,0:T(8,128)(2,1)S(1)} %get-tuple-element.75), channel_id=1, source_target_pairs={{0,8},{8,0},{16,24},{24,16},{1,9},{9,1},{17,25},{25,17},{2,10},{10... | collective-permute-start | bytes 786440 | tf_op jit(solution)/shard_map/ppermute | solution.py:353
  101.9 18.5 %collective-permute-start.22 = (bf16[512,256]{1,0:T(8,128)(2,1)S(1)}, bf16[512,256]{1,0:T(8,128)(2,1)S(1)}, u32[]{:S(2)}, u32[]{:S(2)}) collective-permute-start(bf16[512,256]{1,0:T(8,128)(2,1)S(1)} %get-tuple-element.76), channel_id=1, source_target_pairs={{0,16},{8,24},{16,0},{24,8},{1,17},{9,25},{17,1},{25,9},{2,18},{10... | collective-permute-start | bytes 786440 | tf_op jit(solution)/shard_map/ppermute | solution.py:353
  103.4 17.0 %collective-permute-start.23 = (bf16[512,256]{1,0:T(8,128)(2,1)S(1)}, bf16[512,256]{1,0:T(8,128)(2,1)S(1)}, u32[]{:S(2)}, u32[]{:S(2)}) collective-permute-start(bf16[512,256]{1,0:T(8,128)(2,1)S(1)} %get-tuple-element.77), channel_id=1, source_target_pairs={{0,24},{8,16},{16,8},{24,0},{1,25},{9,17},{17,9},{25,1},{2,26},{10... | collective-permute-start | bytes 786440 | tf_op jit(solution)/shard_map/ppermute | solution.py:353
  113.6 30.1 %collective-permute-start.30 = (bf16[512,1024]{1,0:T(8,128)(2,1)S(1)}, bf16[512,1024]{1,0:T(8,128)(2,1)S(1)}, u32[]{:S(2)}, u32[]{:S(2)}) collective-permute-start(bf16[512,1024]{1,0:T(8,128)(2,1)S(1)} %added.7.refs_5_), channel_id=1, source_target_pairs={{2,4},{3,5},{4,2},{5,3},{10,12},{11,13},{12,10},{13,11},{18,20},{1... | collective-permute-start | bytes 3145736 | tf_op jit(solution)/shard_map/ppermute | solution.py:386
  114.9 28.9 %collective-permute-start.29 = (bf16[512,1024]{1,0:T(8,128)(2,1)S(1)}, bf16[512,1024]{1,0:T(8,128)(2,1)S(1)}, u32[]{:S(2)}, u32[]{:S(2)}) collective-permute-start(bf16[512,1024]{1,0:T(8,128)(2,1)S(1)} %added.6.refs_4_), channel_id=1, source_target_pairs={{2,0},{3,1},{4,6},{5,7},{0,2},{1,3},{6,4},{7,5},{10,8},{11,9},{12,... | collective-permute-start | bytes 3145736 | tf_op jit(solution)/shard_map/ppermute | solution.py:386
  130.4 13.4 %collective-permute-start.27 = (bf16[544,256]{1,0:T(8,128)(2,1)S(1)}, bf16[544,256]{1,0:T(8,128)(2,1)S(1)}, u32[]{:S(2)}, u32[]{:S(2)}) collective-permute-start(bf16[544,256]{1,0:T(8,128)(2,1)S(1)} %get-tuple-element.84), channel_id=1, source_target_pairs={{0,16},{8,24},{16,0},{24,8},{1,17},{9,25},{17,1},{25,9},{2,18},{10... | collective-permute-start | bytes 835592 | tf_op jit(solution)/shard_map/ppermute | solution.py:353
  131.9 11.9 %collective-permute-start.28 = (bf16[544,256]{1,0:T(8,128)(2,1)S(1)}, bf16[544,256]{1,0:T(8,128)(2,1)S(1)}, u32[]{:S(2)}, u32[]{:S(2)}) collective-permute-start(bf16[544,256]{1,0:T(8,128)(2,1)S(1)} %get-tuple-element.85), channel_id=1, source_target_pairs={{0,24},{8,16},{16,8},{24,0},{1,25},{9,17},{17,9},{25,1},{2,26},{10... | collective-permute-start | bytes 835592 | tf_op jit(solution)/shard_map/ppermute | solution.py:353
  (11 other events, 106.9 us)
